TPU v7x, 32 devices: a whole 2x2x4 slice. The times are simulated.
32 devices in a mesh: section: 8 (over z, core), tm: 4 (over y, x).
Axes of the slice: x: 2, y: 2, z: 4, core: 2. Of those that a mesh axis runs over, the one named last changes fastest.
Arguments:
- act_in: bfloat16 [8, 512, 2048], P('section', 'tm'), may hold values from -6 to 6
- grad_in: bfloat16 [8, 512, 2048], P('section', 'tm'), may hold values from -6 to 6
- saved_inputs: bfloat16 [8, 2, 512, 2048], P('section', None, 'tm'), may hold values from -6 to 6
- kernels: bfloat16 [8, 2, 31, 2048], P('section'), may hold values from -1 to 1
- norm_gains: bfloat16 [8, 2, 2048], P('section'), may hold values from 0.099609375 to 1.8984375
- forward_lengths: int32 [8], replicated, may hold values from 256 to 512
- backward_lengths: int32 [8], replicated, may hold values from 256 to 512
- forward_slots: int32 [8, 2], replicated, may hold values from 0 to 1
- backward_slots: int32 [8, 2], replicated, may hold values from 0 to 1
Outputs:
- act_out: bfloat16 [8, 512, 2048], P('section', 'tm')
- grad_out: bfloat16 [8, 512, 2048], P('section', 'tm')
- tap_grad: float32 [8, 2, 31, 2048], P('section')
- gain_grad: float32 [8, 2, 2048], P('section')
All inputs are finite; a program needn't handle non-finite values.
Results may differ from a plain program's by a relative error of at most 0.0063.
Values may be sent and summed in bfloat16 or wider, within the bound.
No kernel may reach another device: no remote copies, remote signals or barrier semaphores. Data moves between devices by JAX's collectives and lax.ppermute only.
A program may use at most 64 MiB of HBM per device.

v0:
```python
import jax
import jax.numpy as jnp
from jax import lax
from jax.sharding import PartitionSpec as P

epsilon = 1e-05


def padded(cells, sides, width):
    for axis, dim in sides:
        count = lax.axis_size(axis)
        ends = count - 1
        head = lax.slice_in_dim(cells, 0, width, axis=dim)
        tail = lax.slice_in_dim(cells, cells.shape[dim] - width, cells.shape[dim], axis=dim)
        cells = jnp.concatenate(
            [
                lax.ppermute(tail, axis, [(i, (i + 1) % count) for i in range(ends)]),
                cells,
                lax.ppermute(head, axis, [((i + 1) % count, i) for i in range(ends)]),
            ],
            axis=dim,
        )
    return cells


def shifted(x, axis, by):
    count = lax.axis_size(axis)
    return lax.ppermute(x, axis, [(i, (i + by) % count) for i in range(count)])


def normalized(inputs):
    values = inputs.astype(jnp.float32)
    center = values - jnp.mean(values, axis=-1, keepdims=True)
    inverse = lax.rsqrt(jnp.mean(center * center, axis=-1, keepdims=True) + epsilon)
    return (center * inverse, inverse)


def pick_slot(lookup, slot_id):
    onehot = (jnp.arange(lookup.shape[0], dtype=jnp.int32) == slot_id).astype(jnp.float32)
    return jnp.tensordot(onehot, lookup.astype(jnp.float32), axes=1)


def depthwise(inputs, taps):
    channels = inputs.shape[1]
    result = lax.conv_general_dilated(
        inputs[None],
        taps[:, None, :],
        (1,),
        "VALID",
        dimension_numbers=("NWC", "WIO", "NWC"),
        feature_group_count=channels,
        preferred_element_type=jnp.float32,
    )
    return result[0]


def local(
    act_in,
    grad_in,
    saved_inputs,
    kernels,
    norm_gains,
    forward_lengths,
    backward_lengths,
    forward_slots,
    backward_slots,
):
    section_count = lax.axis_size("section")
    section_idx = lax.axis_index("section")
    frames_dev = act_in.shape[1]
    width = act_in.shape[2]
    tap_count = kernels.shape[2]
    half_width = (tap_count - 1) // 2
    tick_count = saved_inputs.shape[1]
    frame_ids = lax.axis_index("tm") * frames_dev + jnp.arange(frames_dev, dtype=jnp.int32)
    slot_range = jnp.arange(kernels.shape[1], dtype=jnp.int32)
    own_stack = jnp.concatenate([kernels[0], norm_gains[0][:, None, :]], axis=1)
    carried = act_in[0]
    returning = grad_in[0]
    tap_total = jnp.zeros(kernels.shape[1:], jnp.float32)
    gain_total = jnp.zeros(norm_gains.shape[1:], jnp.float32)
    for tick_step in range(tick_count):
        ahead_chosen = pick_slot(own_stack, forward_slots[section_idx, tick_step])
        ahead_len = forward_lengths[(section_idx - tick_step) % section_count]
        back_slot = backward_slots[section_idx, tick_step]
        back_chosen = pick_slot(own_stack, back_slot)
        back_len = backward_lengths[(section_idx + tick_step) % section_count]
        back_kernel = back_chosen[:tap_count]
        back_gain = back_chosen[tap_count]
        normed_ahead = normalized(carried)[0]
        mask_ahead = (frame_ids < ahead_len).astype(jnp.float32)[:, None]
        normed_back, inverse_back = normalized(saved_inputs[0, tick_step])
        mask_back = (frame_ids < back_len).astype(jnp.float32)[:, None]
        masked_pair = jnp.concatenate(
            [
                mask_ahead * ahead_chosen[tap_count] * normed_ahead,
                mask_back * back_gain * normed_back,
            ],
            axis=1,
        ).astype(jnp.bfloat16)
        padded_pair = padded(masked_pair, (("tm", 0),), half_width)
        kernel_pair = jnp.concatenate([ahead_chosen[:tap_count], back_kernel], axis=1).astype(
            jnp.bfloat16
        )
        conv_pair = depthwise(padded_pair, kernel_pair)
        conv_ahead = conv_pair[:, :width]
        conv_back = conv_pair[:, width:]
        outputs = (carried.astype(jnp.float32) + conv_ahead * jax.nn.sigmoid(conv_ahead)).astype(
            jnp.bfloat16
        )
        gate_back = jax.nn.sigmoid(conv_back)
        grad_up = returning.astype(jnp.float32)
        grad_mixed = (grad_up * gate_back * (1.0 + conv_back * (1.0 - gate_back))).astype(
            jnp.bfloat16
        )
        grad_wide = padded(grad_mixed, (("tm", 0),), half_width)
        tap_term = depthwise(padded_pair[:, width:], grad_mixed)
        grad_masked = mask_back * depthwise(grad_wide, back_kernel[::-1].astype(jnp.bfloat16))
        gain_term = jnp.sum(grad_masked * normed_back, axis=0)
        scaled = grad_masked * back_gain
        grad_norm = inverse_back * (
            scaled
            - jnp.mean(scaled, axis=-1, keepdims=True)
            - normed_back * jnp.mean(scaled * normed_back, axis=-1, keepdims=True)
        )
        grad_x = (grad_up + grad_norm).astype(jnp.bfloat16)
        onehot = (slot_range == back_slot).astype(jnp.float32)
        tap_total = tap_total + onehot[:, None, None] * tap_term[None]
        gain_total = gain_total + onehot[:, None] * gain_term[None]
        carried = shifted(outputs, "section", 1)
        returning = shifted(grad_x, "section", -1)
    tap_sum, gain_sum = lax.psum((tap_total, gain_total), "tm")
    return (carried[None], returning[None], tap_sum[None], gain_sum[None])


def solution(mesh):
    in_specs = (
        P("section", "tm", None),
        P("section", "tm", None),
        P("section", None, "tm", None),
        P("section", None, None, None),
        P("section", None, None),
        P(),
        P(),
        P(),
        P(),
    )
    out_specs = (
        P("section", "tm", None),
        P("section", "tm", None),
        P("section", None, None, None),
        P("section", None, None),
    )
    return jax.shard_map(local, mesh=mesh, in_specs=in_specs, out_specs=out_specs, check_vma=False)
```

profile of v0, /device:TPU:0, one launch (start us, length us, event | category | flops | bytes accessed | tf_op | source)
XLA Modules:
  0.0 176.0 jit_solution(10085396210604306835)
XLA Ops:
  7.3 1.3 convert_reduce_fusion.3
  8.6 1.3 fusion.21
  10.0 1.4 fusion.98
  14.2 1.1 fusion.76
  15.3 1.1 fusion.78
  18.2 4.8 %collective-permute-start = (bf16[15,4096]{1,0:T(8,128)(2,1)}, bf16[15,4096]{1,0:T(8,128)(2,1)S(1)}, u32[]{:S(2)}, u32[]{:S(2)}) collective-permute-start(bf16[15,4096]{1,0:T(8,128)(2,1)} %get-tuple-element.25), channel_id=1, source_target_pairs={{0,1},{1,2},{2,3},{4,5},{5,6},{6,7},{8,9},{9,10},{10,11},{12,13},{... | collective-permute-start | bytes 368648 | tf_op jit(solution)/shard_map/ppermute | solution.py:17
  23.0 1.3 collective-permute-start.1
  24.3 1.2 compare_convert_fusion.5
  25.5 1.1 compare_convert_fusion.4
  26.7 1.1 fusion.74
  29.6 1.1 compare_convert_fusion.1
  31.4 5.0 %rev.7 = bf16[31,2048]{1,0:T(8,128)(2,1)} reverse(bf16[31,2048]{1,0:T(8,128)(2,1)S(1)} %get-tuple-element.31), dimensions={0} | reverse | bytes 253952 | tf_op jit(solution)/shard_map/rev | solution.py:118
  39.7 1.4 pad_maximum_fusion
  41.0 10.5 %fusion.2 = f32[1,128,4096]{2,0,1:T(1,128)S(1)} fusion(bf16[1,158,4096]{2,1,0:T(8,128)(2,1)S(1)} %get-tuple-element.18, bf16[31,1,2048]{2,1,0:T(2,128)(2,1)S(1)} %copy.23, bf16[31,1,2048]{2,1,0:T(2,128)(2,1)S(1)} %copy.22), kind=kOutput, calls=%fused_computation.2 | convolution fusion | flops 33013760 | bytes 3645440 | tf_op jit(solution)/shard_map/conv_general_dilated | solution.py:45
  51.6 1.6 copy.98
  54.0 4.5 %collective-permute-start.6 = (bf16[15,2048]{1,0:T(8,128)(2,1)S(1)}, bf16[15,2048]{1,0:T(8,128)(2,1)S(1)}, u32[]{:S(2)}, u32[]{:S(2)}) collective-permute-start(bf16[15,2048]{1,0:T(8,128)(2,1)S(1)} %get-tuple-element.29), channel_id=1, source_target_pairs={{0,1},{1,2},{2,3},{4,5},{5,6},{6,7},{8,9},{9,10},{10,11},{12,13},{... | collective-permute-start | bytes 184328 | tf_op jit(solution)/shard_map/ppermute | solution.py:17
  58.6 1.3 collective-permute-start.7
  60.4 4.6 %collective-permute-done.7 = bf16[15,2048]{1,0:T(8,128)(2,1)S(1)} collective-permute-done((bf16[15,2048]{1,0:T(8,128)(2,1)S(1)}, bf16[15,2048]{1,0:T(8,128)(2,1)S(1)}, u32[]{:S(2)}, u32[]{:S(2)}) %collective-permute-start.7) | collective-permute-done | bytes 61472 | tf_op jit(solution)/shard_map/ppermute | solution.py:19
  65.3 5.1 %fusion.12 = f32[1,128,2048]{2,0,1:T(1,128)S(1)} fusion(bf16[1,158,2048]{2,1,0:T(8,128)(2,1)S(1)} %maximum_bitcast_fusion, bf16[31,1,2048]{2,0,1:T(8,128)(2,1)S(1)} %bitcast.222), kind=kOutput, calls=%fused_computation.29 | convolution fusion | flops 16252928 | bytes 1822720 | tf_op jit(solution)/shard_map/conv_general_dilated | solution.py:45
  73.3 4.8 %collective-permute-start.3 = (bf16[15,4096]{1,0:T(8,128)(2,1)S(1)}, bf16[15,4096]{1,0:T(8,128)(2,1)S(1)}, u32[]{:S(2)}, u32[]{:S(2)}) collective-permute-start(bf16[15,4096]{1,0:T(8,128)(2,1)S(1)} %get-tuple-element.23), channel_id=1, source_target_pairs={{0,1},{1,2},{2,3},{4,5},{5,6},{6,7},{8,9},{9,10},{10,11},{12,13},{... | collective-permute-start | bytes 368648 | tf_op jit(solution)/shard_map/ppermute | solution.py:17
  78.2 1.5 collective-permute-start.4
  79.6 4.8 %fusion.8 = f32[1,31,2048]{2,0,1:T(1,128)S(1)} fusion(bf16[1,158,2048]{2,1,0:T(8,128)(2,1)S(1)} %slice_bitcast_fusion.1, bf16[128,1,2048]{2,0,1:T(8,128)(2,1)S(1)} %bitcast.200), kind=kOutput, calls=%fused_computation.25 | convolution fusion | flops 16252928 | bytes 1425408 | tf_op jit(solution)/shard_map/conv_general_dilated | solution.py:45
  85.9 10.5 %fusion = f32[1,128,4096]{2,0,1:T(1,128)S(1)} fusion(bf16[1,158,4096]{2,1,0:T(8,128)(2,1)S(1)} %get-tuple-element.20, bf16[31,1,2048]{2,1,0:T(2,128)(2,1)S(1)} %copy-done.4, bf16[31,1,2048]{2,1,0:T(2,128)(2,1)S(1)} %copy-done.5), kind=kOutput, calls=%fused_computation | convolution fusion | flops 33013760 | bytes 3645440 | tf_op jit(solution)/shard_map/conv_general_dilated | solution.py:45
  96.4 1.6 copy.97
  98.9 4.3 %collective-permute-start.9 = (bf16[15,2048]{1,0:T(8,128)(2,1)S(1)}, bf16[15,2048]{1,0:T(8,128)(2,1)S(1)}, u32[]{:S(2)}, u32[]{:S(2)}) collective-permute-start(bf16[15,2048]{1,0:T(8,128)(2,1)S(1)} %get-tuple-element.27), channel_id=1, source_target_pairs={{0,1},{1,2},{2,3},{4,5},{5,6},{6,7},{8,9},{9,10},{10,11},{12,13},{... | collective-permute-start | bytes 184328 | tf_op jit(solution)/shard_map/ppermute | solution.py:17
  103.1 1.3 collective-permute-start.10
  104.4 4.8 %fusion.6 = f32[1,31,2048]{2,0,1:T(1,128)S(1)} fusion(bf16[1,158,2048]{2,1,0:T(8,128)(2,1)S(1)} %slice_bitcast_fusion, bf16[128,1,2048]{2,0,1:T(8,128)(2,1)S(1)} %bitcast.201), kind=kOutput, calls=%fused_computation.23 | convolution fusion | flops 16252928 | bytes 1425408 | tf_op jit(solution)/shard_map/conv_general_dilated | solution.py:45
  110.2 5.1 %fusion.10 = f32[1,128,2048]{2,0,1:T(1,128)S(1)} fusion(bf16[1,158,2048]{2,1,0:T(8,128)(2,1)S(1)} %maximum_bitcast_fusion.1, bf16[31,1,2048]{2,0,1:T(8,128)(2,1)S(1)} %bitcast.221), kind=kOutput, calls=%fused_computation.27 | convolution fusion | flops 16252928 | bytes 1822720 | tf_op jit(solution)/shard_map/conv_general_dilated | solution.py:45
  116.7 3.1 %collective-permute-start.11 = (bf16[128,2048]{1,0:T(8,128)(2,1)S(1)}, bf16[128,2048]{1,0:T(8,128)(2,1)S(1)}, u32[]{:S(2)}, u32[]{:S(2)}) collective-permute-start(bf16[128,2048]{1,0:T(8,128)(2,1)S(1)} %fusion.53), channel_id=1, source_target_pairs={{0,28},{4,0},{8,4},{12,8},{16,12},{20,16},{24,20},{28,24},{1,29},{... | collective-permute-start | bytes 1572872 | tf_op jit(solution)/shard_map/ppermute | solution.py:28
  119.8 1.2 add_bitcast_fusion
  121.1 16.9 %psum.15 = f32[1,2,2048]{2,1,0:T(2,128)} all-reduce(f32[1,2,2048]{2,1,0:T(2,128)S(1)} %add_bitcast_fusion.1), channel_id=1, replica_groups=mesh['section'=8,'tm'=4] {'tm'}, use_global_device_ids=true, to_apply=%region_15.16 | all-reduce | flops 4096 | bytes 32768 | tf_op jit(solution)/shard_map/psum | solution.py:132
  138.0 28.8 %all-reduce.2.cloned.1.call-done = f32[1,2,31,2048]{3,1,2,0:T(2,128)} async-done(((f32[1,2,31,2048]{3,1,2,0:T(2,128)}), f32[1,2,31,2048]{3,1,2,0:T(2,128)}) %all-reduce.2.cloned.1.call-update) | async-done | bytes 507920 | tf_op jit(solution)/shard_map/psum | solution.py:132
  (123 shorter events, 21.5 us)
Async XLA Ops:
  7.2 5.5 %copy-start = (bf16[1,2,128,2048]{3,2,1,0:T(8,128)(2,1)S(1)}, bf16[1,2,128,2048]{3,2,1,0:T(8,128)(2,1)}, u32[]{:S(2)}) copy-start(bf16[1,2,128,2048]{3,2,1,0:T(8,128)(2,1)} %param.11) | copy-start | bytes 3145732
  7.2 159.6 %all-reduce.2.cloned.1.call-start = ((), (), s32[]{:S(2)}) async-start(), calls=%async_computation | async-start | bytes 1015808 | tf_op jit(solution)/shard_map/psum | solution.py:132
  7.3 5.9 %copy-start.6 = (bf16[1,2,31,2048]{3,1,2,0:T(2,128)(2,1)S(1)}, bf16[1,2,31,2048]{3,1,2,0:T(2,128)(2,1)}, u32[]{:S(2)}) copy-start(bf16[1,2,31,2048]{3,1,2,0:T(2,128)(2,1)} %param.12) | copy-start | bytes 761860
  7.3 5.9 %copy-start.9 = (bf16[1,2,2048]{2,1,0:T(2,128)(2,1)S(1)}, bf16[1,2,2048]{2,1,0:T(2,128)(2,1)}, u32[]{:S(2)}) copy-start(bf16[1,2,2048]{2,1,0:T(2,128)(2,1)} %param.13) | copy-start | bytes 24580
  8.6 5.0 %copy-start.19 = (s32[8,2]{0,1:T(2,128)S(1)}, s32[8,2]{0,1:T(2,128)}, u32[]{:S(2)}) copy-start(s32[8,2]{0,1:T(2,128)} %param.17) | copy-start | bytes 196
  8.6 5.0 %copy-start.20 = (s32[8,2]{0,1:T(2,128)S(1)}, s32[8,2]{0,1:T(2,128)}, u32[]{:S(2)}) copy-start(s32[8,2]{0,1:T(2,128)} %param.16) | copy-start | bytes 196
  12.0 5.0 %copy-start.13 = (f32[128]{0:T(128)}, f32[128]{0:T(128)S(1)}, u32[]{:S(2)}) copy-start(f32[128]{0:T(128)S(1)} %compare_convert_fusion.2) | copy-start | bytes 1540
  12.9 4.1 %copy-start.11 = (f32[128]{0:T(128)}, f32[128]{0:T(128)S(1)}, u32[]{:S(2)}) copy-start(f32[128]{0:T(128)S(1)} %broadcast_multiply_fusion.6) | copy-start | bytes 1540
  13.2 3.8 %copy-start.15 = (f32[128]{0:T(128)}, f32[128]{0:T(128)S(1)}, u32[]{:S(2)}) copy-start(f32[128]{0:T(128)S(1)} %add_rsqrt_fusion.2) | copy-start | bytes 1540
  14.2 2.4 %copy-start.1 = (bf16[1,128,2048]{2,1,0:T(8,128)(2,1)S(1)}, bf16[1,128,2048]{2,1,0:T(8,128)(2,1)}, u32[]{:S(2)}) copy-start(bf16[1,128,2048]{2,1,0:T(8,128)(2,1)} %param.9) | copy-start | bytes 1572868
  18.2 21.5 %collective-permute-start = (bf16[15,4096]{1,0:T(8,128)(2,1)}, bf16[15,4096]{1,0:T(8,128)(2,1)S(1)}, u32[]{:S(2)}, u32[]{:S(2)}) collective-permute-start(bf16[15,4096]{1,0:T(8,128)(2,1)} %get-tuple-element.25), channel_id=1, source_target_pairs={{0,1},{1,2},{2,3},{4,5},{5,6},{6,7},{8,9},{9,10},{10,11},{12,13},{... | collective-permute-start | bytes 368648 | tf_op jit(solution)/shard_map/ppermute | solution.py:17
  23.0 16.6 %collective-permute-start.1 = (bf16[15,4096]{1,0:T(8,128)(2,1)}, bf16[15,4096]{1,0:T(8,128)(2,1)}, u32[]{:S(2)}, u32[]{:S(2)}) collective-permute-start(bf16[15,4096]{1,0:T(8,128)(2,1)} %get-tuple-element.26), channel_id=1, source_target_pairs={{1,0},{2,1},{3,2},{5,4},{6,5},{7,6},{9,8},{10,9},{11,10},{13,12},{... | collective-permute-start | bytes 368648 | tf_op jit(solution)/shard_map/ppermute | solution.py:19
  51.6 1.7 copy-start.2
  54.0 6.4 %collective-permute-start.6 = (bf16[15,2048]{1,0:T(8,128)(2,1)S(1)}, bf16[15,2048]{1,0:T(8,128)(2,1)S(1)}, u32[]{:S(2)}, u32[]{:S(2)}) collective-permute-start(bf16[15,2048]{1,0:T(8,128)(2,1)S(1)} %get-tuple-element.29), channel_id=1, source_target_pairs={{0,1},{1,2},{2,3},{4,5},{5,6},{6,7},{8,9},{9,10},{10,11},{12,13},{... | collective-permute-start | bytes 184328 | tf_op jit(solution)/shard_map/ppermute | solution.py:17
  58.6 6.5 %collective-permute-start.7 = (bf16[15,2048]{1,0:T(8,128)(2,1)S(1)}, bf16[15,2048]{1,0:T(8,128)(2,1)S(1)}, u32[]{:S(2)}, u32[]{:S(2)}) collective-permute-start(bf16[15,2048]{1,0:T(8,128)(2,1)S(1)} %get-tuple-element.30), channel_id=1, source_target_pairs={{1,0},{2,1},{3,2},{5,4},{6,5},{7,6},{9,8},{10,9},{11,10},{13,12},{... | collective-permute-start | bytes 184328 | tf_op jit(solution)/shard_map/ppermute | solution.py:19
  59.9 12.5 %collective-permute-start.2 = (bf16[128,2048]{1,0:T(8,128)(2,1)S(1)}, bf16[128,2048]{1,0:T(8,128)(2,1)S(1)}, u32[]{:S(2)}, u32[]{:S(2)}) collective-permute-start(bf16[128,2048]{1,0:T(8,128)(2,1)S(1)} %get-tuple-element.16), channel_id=1, source_target_pairs={{0,4},{4,8},{8,12},{12,16},{16,20},{20,24},{24,28},{28,0},{1,5},{5... | collective-permute-start | bytes 1572872 | tf_op jit(solution)/shard_map/ppermute | solution.py:28
  65.3 5.2 %copy-start.10 = (f32[128]{0:T(128)S(1)}, f32[128]{0:T(128)}, u32[]{:S(2)}) copy-start(f32[128]{0:T(128)} %broadcast_multiply_fusion.4) | copy-start | bytes 1540
  65.3 5.2 %copy-start.12 = (f32[128]{0:T(128)S(1)}, f32[128]{0:T(128)}, u32[]{:S(2)}) copy-start(f32[128]{0:T(128)} %copy-done.11) | copy-start | bytes 1540
  65.3 5.2 %copy-start.14 = (f32[128]{0:T(128)S(1)}, f32[128]{0:T(128)}, u32[]{:S(2)}) copy-start(f32[128]{0:T(128)} %copy-done.13) | copy-start | bytes 1540
  65.3 5.2 %copy-start.16 = (f32[128]{0:T(128)S(1)}, f32[128]{0:T(128)}, u32[]{:S(2)}) copy-start(f32[128]{0:T(128)} %copy-done.15) | copy-start | bytes 1540
  71.3 1.6 copy-start.8
  71.3 1.6 copy-start.21
  73.3 12.1 %collective-permute-start.3 = (bf16[15,4096]{1,0:T(8,128)(2,1)S(1)}, bf16[15,4096]{1,0:T(8,128)(2,1)S(1)}, u32[]{:S(2)}, u32[]{:S(2)}) collective-permute-start(bf16[15,4096]{1,0:T(8,128)(2,1)S(1)} %get-tuple-element.23), channel_id=1, source_target_pairs={{0,1},{1,2},{2,3},{4,5},{5,6},{6,7},{8,9},{9,10},{10,11},{12,13},{... | collective-permute-start | bytes 368648 | tf_op jit(solution)/shard_map/ppermute | solution.py:17
  78.2 7.2 %collective-permute-start.4 = (bf16[15,4096]{1,0:T(8,128)(2,1)S(1)}, bf16[15,4096]{1,0:T(8,128)(2,1)S(1)}, u32[]{:S(2)}, u32[]{:S(2)}) collective-permute-start(bf16[15,4096]{1,0:T(8,128)(2,1)S(1)} %get-tuple-element.24), channel_id=1, source_target_pairs={{1,0},{2,1},{3,2},{5,4},{6,5},{7,6},{9,8},{10,9},{11,10},{13,12},{... | collective-permute-start | bytes 368648 | tf_op jit(solution)/shard_map/ppermute | solution.py:19
  84.6 13.5 %collective-permute-start.8 = (bf16[128,2048]{1,0:T(8,128)(2,1)S(1)}, bf16[128,2048]{1,0:T(8,128)(2,1)S(1)}, u32[]{:S(2)}, u32[]{:S(2)}) collective-permute-start(bf16[128,2048]{1,0:T(8,128)(2,1)S(1)} %get-tuple-element.21), channel_id=1, source_target_pairs={{0,28},{4,0},{8,4},{12,8},{16,12},{20,16},{24,20},{28,24},{1,29},{... | collective-permute-start | bytes 1572872 | tf_op jit(solution)/shard_map/ppermute | solution.py:28
  98.9 10.6 %collective-permute-start.9 = (bf16[15,2048]{1,0:T(8,128)(2,1)S(1)}, bf16[15,2048]{1,0:T(8,128)(2,1)S(1)}, u32[]{:S(2)}, u32[]{:S(2)}) collective-permute-start(bf16[15,2048]{1,0:T(8,128)(2,1)S(1)} %get-tuple-element.27), channel_id=1, source_target_pairs={{0,1},{1,2},{2,3},{4,5},{5,6},{6,7},{8,9},{9,10},{10,11},{12,13},{... | collective-permute-start | bytes 184328 | tf_op jit(solution)/shard_map/ppermute | solution.py:17
  103.1 6.3 %collective-permute-start.10 = (bf16[15,2048]{1,0:T(8,128)(2,1)S(1)}, bf16[15,2048]{1,0:T(8,128)(2,1)S(1)}, u32[]{:S(2)}, u32[]{:S(2)}) collective-permute-start(bf16[15,2048]{1,0:T(8,128)(2,1)S(1)} %get-tuple-element.28), channel_id=1, source_target_pairs={{1,0},{2,1},{3,2},{5,4},{6,5},{7,6},{9,8},{10,9},{11,10},{13,12},{... | collective-permute-start | bytes 184328 | tf_op jit(solution)/shard_map/ppermute | solution.py:19
  109.4 28.6 %collective-permute-start.5 = (bf16[128,2048]{1,0:T(8,128)(2,1)S(1)}, bf16[128,2048]{1,0:T(8,128)(2,1)S(1)}, u32[]{:S(2)}, u32[]{:S(2)}) collective-permute-start(bf16[128,2048]{1,0:T(8,128)(2,1)S(1)} %get-tuple-element.14), channel_id=1, source_target_pairs={{0,4},{4,8},{8,12},{12,16},{16,20},{20,24},{24,28},{28,0},{1,5},{5... | collective-permute-start | bytes 1572872 | tf_op jit(solution)/shard_map/ppermute | solution.py:28
  115.9 3.9 %copy-start.17 = (f32[2]{0:T(128)S(1)}, f32[2]{0:T(128)}, u32[]{:S(2)}) copy-start(f32[2]{0:T(128)} %compare_convert_fusion.5) | copy-start | bytes 28
  116.0 3.9 %copy-start.18 = (f32[2]{0:T(128)S(1)}, f32[2]{0:T(128)}, u32[]{:S(2)}) copy-start(f32[2]{0:T(128)} %compare_convert_fusion.4) | copy-start | bytes 28
  116.7 21.3 %collective-permute-start.11 = (bf16[128,2048]{1,0:T(8,128)(2,1)S(1)}, bf16[128,2048]{1,0:T(8,128)(2,1)S(1)}, u32[]{:S(2)}, u32[]{:S(2)}) collective-permute-start(bf16[128,2048]{1,0:T(8,128)(2,1)S(1)} %fusion.53), channel_id=1, source_target_pairs={{0,28},{4,0},{8,4},{12,8},{16,12},{20,16},{24,20},{28,24},{1,29},{... | collective-permute-start | bytes 1572872 | tf_op jit(solution)/shard_map/ppermute | solution.py:28
  166.8 1.6 copy-start.3
  (3 other events, 3.5 us)
Sparse Core Ops, SparseCore 0:
  121.1 45.5 all-reduce.1
where the time goes:
time: 176 us
  matrix products  45.1 us (26%)
  waiting for transfers between devices  33.9 us (19%)
  starting transfers between devices  27.9 us (16%)
  other arithmetic  20 us (11%)
  local copies, waits for them, and re-layouts  17.3 us (10%)
  blocking collectives  16.9 us (10%)
  between operations  14.9 us (8%)
    conv_general_dilated x6, matrix products, depthwise(): lax.conv_general_dilated(inputs[None], taps[:, None, :], (1,), 'VALID', d...  40.8 us
    psum x1, waiting for transfers between devices, local(): tap_sum, gain_sum = lax.psum((tap_total, gain_total), 'tm')  28.8 us
    ppermute x4, starting transfers between devices, padded(): lax.ppermute(tail, axis, [(i, (i + 1) % count) for i in range(ends)])  18.5 us
    psum x1, blocking collectives, local(): tap_sum, gain_sum = lax.psum((tap_total, gain_total), 'tm')  16.9 us
    unnamed x51, local copies, waits for them, and re-layouts  6.46 us
    rev x2, local copies, waits for them, and re-layouts, local(): back_kernel[::-1].astype(jnp.bfloat16)  5.47 us
    ppermute x4, starting transfers between devices, padded(): lax.ppermute(head, axis, [((i + 1) % count, i) for i in range(ends)])  5.35 us
    ppermute x4, waiting for transfers between devices, padded(): lax.ppermute(head, axis, [((i + 1) % count, i) for i in range(ends)])  4.65 us
  transfers between devices with their start and end apart: 13, of which 3 were waited for; matrix products, arithmetic and copies ran while one was open for 30% of the time, Pallas kernels for 0%

commit v1 on v0

v1 whole, which is shorter than its diff:
```python
import functools

import jax
import jax.numpy as jnp
import ml_dtypes
import numpy as np
from jax import lax
from jax.experimental import pallas as pl
from jax.experimental.pallas import tpu as pltpu
from jax.sharding import PartitionSpec as P

epsilon = 1e-05
BLOCK = 512
ROWS = 16
F32 = jnp.float32
BF16 = jnp.bfloat16


def split(matrix):
    high = matrix.astype(ml_dtypes.bfloat16)
    low = (matrix - high.astype(np.float64)).astype(ml_dtypes.bfloat16)
    return high, low


def angles(size, times):
    return 2.0 * np.pi / size * np.outer(np.arange(size // 2) + 0.5, np.asarray(times, np.float64))


def to_freq(size, times):
    phase = angles(size, times)
    return np.concatenate([np.cos(phase), -np.sin(phase)], axis=0)


def from_freq(size, times):
    phase = angles(size, times).T
    return 2.0 / size * np.concatenate([np.cos(phase), -np.sin(phase)], axis=1)


def stacked(matrix):
    return np.stack(split(matrix))


def beside(matrix):
    return np.concatenate(split(matrix), axis=1)


def tap_freq(size, taps):
    phase = angles(size, np.arange(taps) - (taps - 1) // 2)
    table = np.concatenate([np.cos(phase), np.sin(phase)], axis=0)
    return beside(np.concatenate([table, np.zeros((size, 1))], axis=1))


def dot(a, b):
    return jnp.dot(a, b, preferred_element_type=F32)


def forward_dft(table, values):
    return dot(table[0], values) + dot(table[1], values)


def inverse_dft(table, values):
    high = values.astype(BF16)
    low = (values - high.astype(F32)).astype(BF16)
    return dot(table[0], high) + (dot(table[1], high) + dot(table[0], low))


def halves(values):
    half = values.shape[0] // 2
    return values[:half], values[half:]


def product(a, b):
    ar, ai = halves(a)
    br, bi = halves(b)
    return jnp.concatenate([ar * br - ai * bi, ar * bi + ai * br], axis=0)


def product_conj(a, b):
    ar, ai = halves(a)
    br, bi = halves(b)
    return jnp.concatenate([ar * br + ai * bi, ai * br - ar * bi], axis=0)


def sigmoid(values):
    return 0.5 * jnp.tanh(0.5 * values) + 0.5


def norm_rows(pieces, gain, first, length, masked_ref, normed_ref, inverse_ref, skip):
    width = masked_ref.shape[1]
    total = sum(piece[2] for piece in pieces)
    at = 0
    for ref, start, count in pieces:
        keep = normed_ref is not None and at + count > skip and at < total - skip

        def step(i, _, ref=ref, start=start, at=at, keep=keep):
            row = pl.multiple_of(i * ROWS, ROWS)
            values = ref[pl.ds(start + row, ROWS), :].astype(F32)
            center = values - jnp.sum(values, axis=1, keepdims=True) * (1.0 / width)
            inverse = lax.rsqrt(jnp.sum(center * center, axis=1, keepdims=True) * (1.0 / width) + epsilon)
            normed = center * inverse
            frame = first + at + row + lax.broadcasted_iota(jnp.int32, (ROWS, 1), 0)
            mask = ((frame >= 0) & (frame < length)).astype(F32)
            masked_ref[pl.ds(at + row, ROWS), :] = (mask * gain * normed).astype(BF16)
            if keep:
                normed_ref[pl.ds(at + row, ROWS), :] = normed
                inverse_ref[pl.ds(at + row, ROWS), :] = jnp.broadcast_to(inverse, (ROWS, 128))
            return 0

        lax.fori_loop(0, count // ROWS, step, 0)
        at += count


def window(pieces, columns):
    parts = [ref[pl.ds(start, count), columns] for ref, start, count in pieces]
    return parts[0] if len(parts) == 1 else jnp.concatenate(parts, axis=0)


def each_block(width, body):
    def step(i, _):
        body(pl.ds(pl.multiple_of(i * BLOCK, BLOCK), BLOCK))
        return 0

    lax.fori_loop(0, width // BLOCK, step, 0)


def tap_spectrum(table, weights):
    return dot(table, jnp.concatenate([weights, weights], axis=0))


def backward_kernel(
    cut, out_rows, scalars, saved, saved_left, saved_right, grads, weights,
    m_table, q_table, c_table, go_table, gh_table, x_table, t_table,
    grad_x, taps, masked, normed, inverse, scaled, sum_a, sum_b,
):
    own, width = saved.shape
    saved_reach, saved_at, grad_reach, grad_pieces = cut(saved, saved_left, saved_right, grads)
    out_reach = (out_rows - own) // 2
    slot, length, first = scalars[0], scalars[1], scalars[2]
    gain = weights[slot, 31:32, :].astype(F32)
    norm_rows(
        saved_at, gain, first - saved_reach, length, masked, normed, inverse, saved_reach - out_reach
    )
    sum_a[...] = jnp.zeros_like(sum_a)
    sum_b[...] = jnp.zeros_like(sum_b)
    lo = saved_reach - out_reach
    frame = first - out_reach + lax.broadcasted_iota(jnp.int32, (out_rows, 1), 0)
    mask = ((frame >= 0) & (frame < length)).astype(F32)

    def block(columns):
        chosen = weights[slot, :, columns]
        q = tap_spectrum(q_table[...], chosen)
        m = forward_dft(m_table, masked[:, columns])
        conv = inverse_dft(c_table, product(m, q))
        gate = sigmoid(conv)
        upstream = window(grad_pieces, columns).astype(F32)
        mixed = (upstream * gate * (1.0 + conv * (1.0 - gate))).astype(BF16)
        inner = mixed[grad_reach : grad_reach + own]
        ends = jnp.concatenate([mixed[:grad_reach], mixed[grad_reach + own :]], axis=0)
        g_own = dot(go_table[...], jnp.concatenate([inner, inner], axis=0))
        g_all = g_own + dot(gh_table[...], jnp.concatenate([ends, ends], axis=0))
        tap = inverse_dft(t_table, product_conj(m, g_own))
        grad_masked = mask * inverse_dft(x_table, product_conj(g_all, q))
        here = normed[lo : lo + out_rows, columns]
        weighted = grad_masked * here
        gain_term = jnp.sum(weighted[out_reach : out_reach + own], axis=0, keepdims=True)
        row = lax.broadcasted_iota(jnp.int32, tap.shape, 0)
        taps[:, columns] = jnp.where(row == tap.shape[0] - 1, gain_term, tap).astype(taps.dtype)
        gain_here = chosen[31:32].astype(F32)
        by_gain = grad_masked * gain_here
        scaled[:, columns] = by_gain
        both = weighted * gain_here
        part_a = by_gain[:, :128]
        part_b = both[:, :128]
        for lane in range(128, BLOCK, 128):
            part_a = part_a + by_gain[:, lane : lane + 128]
            part_b = part_b + both[:, lane : lane + 128]
        sum_a[...] += part_a
        sum_b[...] += part_b

    each_block(width, block)

    at = 0
    skip = grad_reach - out_reach
    for ref, start, count in grad_pieces:
        begin = max(at, skip)
        end = min(at + count, skip + out_rows)

        def step(i, _, ref=ref, source=start + begin - at, begin=begin):
            row = pl.multiple_of(i * ROWS, ROWS)
            out = pl.ds(begin - skip + row, ROWS)
            inside = pl.ds(begin - skip + lo + row, ROWS)
            mean_a = jnp.sum(sum_a[out, :], axis=1, keepdims=True) * (1.0 / width)
            mean_b = jnp.sum(sum_b[out, :], axis=1, keepdims=True) * (1.0 / width)
            inv = inverse[inside, :][:, :1]
            change = inv * (scaled[out, :] - mean_a - normed[inside, :] * mean_b)
            grad_x[out, :] = (ref[pl.ds(source + row, ROWS), :].astype(F32) + change).astype(BF16)
            return 0

        lax.fori_loop(0, (end - begin) // ROWS, step, 0)
        at += count


def forward_kernel(
    offset, reach, scalars, act, left, right, weights, later,
    m0_table, q0_table, c0_table, m1_table, q1_table, c1_table,
    out, masked0, between, masked1,
):
    own, width = act.shape
    middle = reach // 2
    slot, length, first = scalars[0], scalars[1], scalars[2]
    pieces = [(left, offset, reach), (act, 0, own), (right, offset, reach)]
    inner = [(left, offset + middle, middle), (act, 0, own), (right, offset, middle)]
    gain = weights[slot, 31:32, :].astype(F32)
    norm_rows(pieces, gain, first - reach, length, masked0, None, None, 0)

    def first_layer(columns):
        q = tap_spectrum(q0_table[...], weights[slot, :, columns])
        conv = inverse_dft(c0_table, product(forward_dft(m0_table, masked0[:, columns]), q))
        between[:, columns] = (window(inner, columns).astype(F32) + conv * sigmoid(conv)).astype(BF16)

    each_block(width, first_layer)
    gain = later[31:32, :].astype(F32)
    norm_rows([(between, 0, own + 2 * middle)], gain, first - middle, length, masked1, None, None, 0)

    def second_layer(columns):
        q = tap_spectrum(q1_table[...], later[:, columns])
        conv = inverse_dft(c1_table, product(forward_dft(m1_table, masked1[:, columns]), q))
        here = between[middle : middle + own, columns].astype(F32)
        out[:, columns] = (here + conv * sigmoid(conv)).astype(BF16)

    each_block(width, second_layer)


def span(reach, own):
    return np.arange(-reach, own + reach)


VMEM = pl.BlockSpec(memory_space=pltpu.VMEM)
SMEM = pl.BlockSpec(memory_space=pltpu.SMEM)
LIMIT = 56 * 1024 * 1024


def call(kernel, outs, scratch, operands, flops):
    moved = sum(int(np.prod(x.shape)) * x.dtype.itemsize for x in operands)
    return pl.pallas_call(
        kernel,
        out_shape=outs,
        in_specs=[SMEM] + [VMEM] * (len(operands) - 1),
        out_specs=jax.tree.map(lambda _: VMEM, outs),
        scratch_shapes=scratch,
        compiler_params=pltpu.CompilerParams(vmem_limit_bytes=LIMIT),
        cost_estimate=pl.CostEstimate(flops=flops, bytes_accessed=moved, transcendentals=0),
    )(*operands)


def backward(cut, reaches, scalars, saved, left, right, grads, weights):
    saved_reach, grad_reach, out_reach = reaches
    own, width = saved.shape
    taps = weights.shape[1] - 1
    size = own + 2 * saved_reach
    out_rows = own + 2 * out_reach
    ends = np.concatenate([np.arange(-grad_reach, 0), np.arange(own, own + grad_reach)])
    tap_back = np.concatenate([from_freq(size, np.arange(taps) - (taps - 1) // 2), np.zeros((1, size))], axis=0)
    tables = [
        stacked(to_freq(size, span(saved_reach, own))),
        tap_freq(size, taps),
        stacked(from_freq(size, span(grad_reach, own))),
        beside(to_freq(size, np.arange(own))),
        beside(to_freq(size, ends)),
        stacked(from_freq(size, span(out_reach, own))),
        stacked(tap_back),
    ]
    operands = [scalars, saved, left, right, grads, weights] + [jnp.asarray(t) for t in tables]
    outs = (
        jax.ShapeDtypeStruct((out_rows, width), BF16),
        jax.ShapeDtypeStruct((taps + 1, width), BF16),
    )
    scratch = [
        pltpu.VMEM((size, width), BF16),
        pltpu.VMEM((size, width), F32),
        pltpu.VMEM((size, 128), F32),
        pltpu.VMEM((out_rows, width), F32),
        pltpu.VMEM((out_rows, 128), F32),
        pltpu.VMEM((out_rows, 128), F32),
    ]
    kernel = functools.partial(backward_kernel, cut, out_rows)
    return call(kernel, outs, scratch, operands, 12 * 2 * size * size * width)


def forward(offset, reach, scalars, act, left, right, weights, later):
    own, width = act.shape
    taps = weights.shape[1] - 1
    middle = reach // 2
    size0, size1 = own + 2 * reach, own + 2 * middle
    tables = [
        stacked(to_freq(size0, span(reach, own))),
        tap_freq(size0, taps),
        stacked(from_freq(size0, span(middle, own))),
        stacked(to_freq(size1, span(middle, own))),
        tap_freq(size1, taps),
        stacked(from_freq(size1, span(0, own))),
    ]
    operands = [scalars, act, left, right, weights, later] + [jnp.asarray(t) for t in tables]
    scratch = [
        pltpu.VMEM((size0, width), BF16),
        pltpu.VMEM((size1, width), BF16),
        pltpu.VMEM((size1, width), BF16),
    ]
    kernel = functools.partial(forward_kernel, offset, reach)
    return call(kernel, jax.ShapeDtypeStruct((own, width), BF16), scratch, operands, 10 * 2 * size0 * size0 * width)


def up16(count):
    return -(-count // 16) * 16


def local(
    act_in, grad_in, saved_inputs, kernels, norm_gains,
    forward_lengths, backward_lengths, forward_slots, backward_slots,
):
    sections = lax.axis_size("section")
    shards = lax.axis_size("tm")
    section = lax.axis_index("section")
    act, grad, saved = act_in[0], grad_in[0], saved_inputs[0]
    own = act.shape[0]
    tap_count = kernels.shape[2]
    half = (tap_count - 1) // 2
    first = lax.axis_index("tm") * own
    one, two, three = up16(half), up16(2 * half), up16(3 * half)

    def shifted(x, by):
        return lax.ppermute(x, "section", [(i, (i + by) % sections) for i in range(sections)])

    parts = [(saved[0], three), (grad, two), (saved[1], two), (act, two)]
    tail = jnp.concatenate([x[own - n :] for x, n in parts], axis=0)
    head = jnp.concatenate([x[:n] for x, n in parts], axis=0)
    left = lax.ppermute(tail, "tm", [(i, i + 1) for i in range(shards - 1)])
    right = lax.ppermute(head, "tm", [(i + 1, i) for i in range(shards - 1)])
    weights = jnp.concatenate([kernels[0], norm_gains[0][:, None, :]], axis=1)
    later = shifted(lax.dynamic_index_in_dim(weights, forward_slots[section, 1], 0, keepdims=False), -1)

    def scalars(slot, length):
        return jnp.stack([slot, length, first]).astype(jnp.int32)

    def cut0(saved_ref, left_ref, right_ref, grad_ref):
        return (
            three,
            [(left_ref, 0, three), (saved_ref, 0, own), (right_ref, 0, three)],
            two,
            [(left_ref, three, two), (grad_ref, 0, own), (right_ref, three, two)],
        )

    def cut1(saved_ref, left_ref, right_ref, grad_ref):
        at = three + two
        return (
            two,
            [(left_ref, at, two), (saved_ref, 0, own), (right_ref, at, two)],
            one,
            [(grad_ref, 0, own + 2 * one)],
        )

    slot0, slot1 = backward_slots[section, 0], backward_slots[section, 1]
    grad_mid, taps0 = backward(
        cut0, (three, two, one), scalars(slot0, backward_lengths[section]),
        saved[0], left, right, grad, weights,
    )
    grad_mid = shifted(grad_mid, -1)
    act_out = forward(
        three + 2 * two, two, scalars(forward_slots[section, 0], forward_lengths[section]),
        act, left, right, weights, later,
    )
    act_out = shifted(act_out, 2)
    grad_out, taps1 = backward(
        cut1, (two, one, 0), scalars(slot1, backward_lengths[(section + 1) % sections]),
        saved[1], left, right, grad_mid, weights,
    )
    grad_out = shifted(grad_out, -1)

    def summed(x):
        if shards & (shards - 1):
            return lax.psum(x.astype(F32), "tm")
        step = 1
        while step < shards:
            other = lax.ppermute(x, "tm", [(i, i ^ step) for i in range(shards)])
            total = x.astype(F32) + other.astype(F32)
            x = total.astype(BF16)
            step *= 2
        return total

    total0, total1 = summed(taps0), summed(taps1)
    slots = jnp.arange(kernels.shape[1], dtype=jnp.int32)[:, None, None]
    sums = jnp.where(slots == slot0, total0[None], 0.0) + jnp.where(slots == slot1, total1[None], 0.0)
    return act_out[None], grad_out[None], sums[None, :, :tap_count], sums[None, :, tap_count]


def solution(mesh):
    in_specs = (
        P("section", "tm", None),
        P("section", "tm", None),
        P("section", None, "tm", None),
        P("section", None, None, None),
        P("section", None, None),
        P(),
        P(),
        P(),
        P(),
    )
    out_specs = (
        P("section", "tm", None),
        P("section", "tm", None),
        P("section", None, None, None),
        P("section", None, None),
    )
    return jax.shard_map(local, mesh=mesh, in_specs=in_specs, out_specs=out_specs, check_vma=False)
```

time: 176 us -> 104 us (0.59)
  matrix products: 45.1 us -> 0 us
  Pallas kernels: 0 us -> 36.8 us
  waiting for transfers between devices: 33.9 us -> 9.95 us
  blocking collectives: 16.9 us -> 0 us
  between operations: 14.9 us -> 2.83 us
  other arithmetic: 20 us -> 9.05 us
  starting transfers between devices: 27.9 us -> 35.2 us
  local copies, waits for them, and re-layouts: 17.3 us -> 10 us
    conv_general_dilated x6 -> x0, matrix products: 40.8 us -> none  [depthwise(): lax.conv_general_dilated(inputs[None], taps[:, None, :], (1,), 'VALID', d...]
    pallas_call x0 -> x3, Pallas kernels: none -> 36.8 us  [call(): pl.pallas_call(kernel, out_shape=outs, in_specs=[SMEM] + [VMEM] * (len(op...]
    psum x1 -> x0, waiting for transfers between devices: 28.8 us -> none  [local(): tap_sum, gain_sum = lax.psum((tap_total, gain_total), 'tm')]
    psum x1 -> x0, blocking collectives: 16.9 us -> none  [local(): tap_sum, gain_sum = lax.psum((tap_total, gain_total), 'tm')]
    convert_element_type x10 -> x2, other arithmetic: 8.69 us -> 0.97 us  [summed(): x = total.astype(BF16)]
    ppermute x12 -> x10, starting transfers between devices: 27.9 us -> 35.2 us  [the longest x4 20.8 us: summed(): other = lax.ppermute(x, 'tm', [(i, i ^ step) for i in range(shards)])]
    rev x2 -> x0, local copies, waits for them, and re-layouts: 5.47 us -> none  [local(): back_kernel[::-1].astype(jnp.bfloat16)]
    reduce_sum x8 -> x0, other arithmetic: 5.06 us -> none  [the longest x3 1.92 us: normalized(): jnp.mean(center * center, axis=-1, keepdims=True) + epsilon]
  transfers between devices with their start and end apart: 13 -> 10, of which waited for: 3 -> 5; matrix products, arithmetic and copies ran while one was open for 30% -> 13% of each run, Pallas kernels for 0% -> 23%
where the time goes in v1:
time: 104 us
  Pallas kernels  36.8 us (35%)
  starting transfers between devices  35.2 us (34%)
  local copies, waits for them, and re-layouts  10 us (10%)
  waiting for transfers between devices  9.95 us (10%)
  other arithmetic  9.05 us (9%)
  between operations  2.83 us (3%)
    pallas_call x3, Pallas kernels, call(): pl.pallas_call(kernel, out_shape=outs, in_specs=[SMEM] + [VMEM] * (len(op...  36.8 us
    ppermute x4, starting transfers between devices, summed(): other = lax.ppermute(x, 'tm', [(i, i ^ step) for i in range(shards)])  20.8 us
    ppermute x4, starting transfers between devices, shifted(): lax.ppermute(x, 'section', [(i, (i + by) % sections) for i in range(secti...  6.52 us
    ppermute x1, starting transfers between devices, local(): left = lax.ppermute(tail, 'tm', [(i, i + 1) for i in range(shards - 1)])  6.46 us
    another operation x3, other arithmetic, scalars(): return jnp.stack([slot, length, first]).astype(jnp.int32)  5.52 us
    ppermute x1, waiting for transfers between devices, local(): right = lax.ppermute(head, 'tm', [(i + 1, i) for i in range(shards - 1)])  4.08 us
    unnamed x31, local copies, waits for them, and re-layouts  3.48 us
    ppermute x4, waiting for transfers between devices, shifted(): lax.ppermute(x, 'section', [(i, (i + by) % sections) for i in range(secti...  3.07 us
  transfers between devices with their start and end apart: 10, of which 5 were waited for; matrix products, arithmetic and copies ran while one was open for 13% of the time, Pallas kernels for 23%

profile of v1, /device:TPU:0, one launch (start us, length us, event | category | flops | bytes accessed | tf_op | source)
XLA Modules:
  0.0 103.8 jit_solution(11389705159477069704)
XLA Ops:
  0.7 1.1 %slice_bitcast_fusion.3 = (bf16[48,2048]{1,0:T(8,128)(2,1)S(1)}, bf16[48,2048]{1,0:T(8,128)(2,1)S(1)}) fusion(bf16[1,2,128,2048]{3,2,1,0:T(8,128)(2,1)} %param.31), kind=kLoop, calls=%fused_computation.14 | loop fusion | bytes 786432 | tf_op jit(solution)/shard_map/slice | solution.py:336
  1.8 1.0 slice_bitcast_fusion.6
  3.0 1.4 %collective-permute-start.1 = (bf16[144,2048]{1,0:T(8,128)(2,1)S(1)}, bf16[144,2048]{1,0:T(8,128)(2,1)S(1)}, u32[]{:S(2)}, u32[]{:S(2)}) collective-permute-start(bf16[144,2048]{1,0:T(8,128)(2,1)S(1)} %pad_maximum_fusion.1), channel_id=1, source_target_pairs={{1,0},{2,1},{3,2},{5,4},{6,5},{7,6},{9,8},{10,9},{11,10},{13,12},{... | collective-permute-start | bytes 1769480 | tf_op jit(solution)/shard_map/ppermute | solution.py:338
  4.5 6.5 %collective-permute-start = (bf16[144,2048]{1,0:T(8,128)(2,1)S(1)}, bf16[144,2048]{1,0:T(8,128)(2,1)}, u32[]{:S(2)}, u32[]{:S(2)}) collective-permute-start(bf16[144,2048]{1,0:T(8,128)(2,1)S(1)} %pad_maximum_fusion), channel_id=1, source_target_pairs={{0,1},{1,2},{2,3},{4,5},{5,6},{6,7},{8,9},{9,10},{10,11},{12,13},{... | collective-permute-start | bytes 1769480 | tf_op jit(solution)/shard_map/ppermute | solution.py:337
  11.1 0.7 constant_dynamic-slice_fusion
  13.0 0.7 fusion.2
  13.7 0.7 pad_maximum_fusion.2.weights
  15.1 1.9 %add_add_fusion.2.scalars = s32[3]{0:T(128)} fusion(s32[1]{0:T(128)} %get-tuple-element.26, s32[1]{0:T(128)} %bitcast.18, s32[1]{0:T(128)} %bitcast.1), kind=kLoop, calls=%fused_computation.29 | loop fusion | flops 6 | bytes 24 | tf_op jit(solution)/shard_map/stack | solution.py:343
  17.0 1.0 slice_bitcast_fusion
  18.0 4.1 %collective-permute-done.1.right.saved_right = bf16[144,2048]{1,0:T(8,128)(2,1)S(1)} collective-permute-done((bf16[144,2048]{1,0:T(8,128)(2,1)S(1)}, bf16[144,2048]{1,0:T(8,128)(2,1)S(1)}, u32[]{:S(2)}, u32[]{:S(2)}) %collective-permute-start.1) | collective-permute-done | bytes 589856 | tf_op jit(solution)/shard_map/ppermute | solution.py:338
  22.9 12.9 %shard_map.301 = (bf16[160,2048]{1,0:T(8,128)(2,1)}, bf16[32,2048]{1,0:T(8,128)(2,1)}) custom-call(s32[3]{0:T(128)} %add_add_fusion.2.scalars, bf16[128,2048]{1,0:T(8,128)(2,1)} %get-tuple-element.12.saved, bf16[144,2048]{1,0:T(8,128)(2,1)} %collective-permute-done.left.saved_left, bf16[144,2048]{1,0:T(8,128)(2,1)} %copy-done.10, ...), custom_call_target="tpu_custom_call" | custom-call | flops 2466250752 | bytes 3235852 | tf_op jit(solution)/shard_map/pallas_call | solution.py:245
  35.9 1.8 %collective-permute-start.4 = (bf16[160,2048]{1,0:T(8,128)(2,1)}, bf16[160,2048]{1,0:T(8,128)(2,1)S(1)}, u32[]{:S(2)}, u32[]{:S(2)}) collective-permute-start(bf16[160,2048]{1,0:T(8,128)(2,1)} %get-tuple-element.8), channel_id=1, source_target_pairs={{0,28},{4,0},{8,4},{12,8},{16,12},{20,16},{24,20},{28,24},{1,29},{... | collective-permute-start | bytes 1966088 | tf_op jit(solution)/shard_map/ppermute | solution.py:332
  37.7 2.5 %collective-permute-start.2 = (bf16[32,2048]{1,0:T(8,128)(2,1)S(1)}, bf16[32,2048]{1,0:T(8,128)(2,1)S(1)}, u32[]{:S(2)}, u32[]{:S(2)}) collective-permute-start(bf16[32,2048]{1,0:T(8,128)(2,1)S(1)} %fusion.1), channel_id=1, source_target_pairs={{0,28},{4,0},{8,4},{12,8},{16,12},{20,16},{24,20},{28,24},{1,29},{... | collective-permute-start | bytes 393224 | tf_op jit(solution)/shard_map/ppermute | solution.py:332
  40.8 0.7 iota_compare_fusion.1
  41.4 1.8 %add_add_fusion.1.scalars = s32[3]{0:T(128)} fusion(s32[1]{0:T(128)} %get-tuple-element.27, s32[1]{0:T(128)} %bitcast.16, s32[1]{0:T(128)} %bitcast.1), kind=kLoop, calls=%fused_computation.28 | loop fusion | flops 6 | bytes 24 | tf_op jit(solution)/shard_map/stack | solution.py:343
  43.8 1.8 %add_add_fusion.scalars = s32[3]{0:T(128)} fusion(s32[1]{0:T(128)} %dynamic_slice.26, s32[1]{0:T(128)} %bitcast, s32[1]{0:T(128)} %bitcast.1), kind=kLoop, calls=%fused_computation.27 | loop fusion | flops 6 | bytes 24 | tf_op jit(solution)/shard_map/stack | solution.py:343
  45.7 10.2 %collective-permute-start.6 = (bf16[32,2048]{1,0:T(8,128)(2,1)}, bf16[32,2048]{1,0:T(8,128)(2,1)S(1)}, u32[]{:S(2)}, u32[]{:S(2)}) collective-permute-start(bf16[32,2048]{1,0:T(8,128)(2,1)} %get-tuple-element.10), channel_id=1, source_target_pairs={{0,1},{1,0},{2,3},{3,2},{4,5},{5,4},{6,7},{7,6},{8,9},{9,8},{10,11... | collective-permute-start | bytes 393224 | tf_op jit(solution)/shard_map/ppermute | solution.py:384
  55.9 0.6 copy-done.12
  56.5 12.2 %shard_map.300 = bf16[128,2048]{1,0:T(8,128)(2,1)} custom-call(s32[3]{0:T(128)} %add_add_fusion.scalars, bf16[128,2048]{1,0:T(8,128)(2,1)} %bitcast.46, bf16[144,2048]{1,0:T(8,128)(2,1)} %collective-permute-done.left.saved_left, bf16[144,2048]{1,0:T(8,128)(2,1)} %copy-done.10, bf16[2,32,2048]{2,1,0:T(8,128)(2,1)} %pad_maximum_fusion.2.weights, ...), custom_call_target="tpu_custom_call" | custom-call | flops 1509949440 | bytes 2596876 | tf_op jit(solution)/shard_map/pallas_call | solution.py:245
  68.7 0.8 copy-done.9
  69.6 11.6 %shard_map.302 = (bf16[128,2048]{1,0:T(8,128)(2,1)}, bf16[32,2048]{1,0:T(8,128)(2,1)}) custom-call(s32[3]{0:T(128)} %add_add_fusion.1.scalars, bf16[128,2048]{1,0:T(8,128)(2,1)} %get-tuple-element.13.saved, bf16[144,2048]{1,0:T(8,128)(2,1)} %collective-permute-done.left.saved_left, bf16[144,2048]{1,0:T(8,128)(2,1)} %copy-done.10, ...), custom_call_target="tpu_custom_call" | custom-call | flops 1811939328 | bytes 3162124 | tf_op jit(solution)/shard_map/pallas_call | solution.py:245
  81.2 2.7 %collective-permute-start.8 = (bf16[32,2048]{1,0:T(8,128)(2,1)}, bf16[32,2048]{1,0:T(8,128)(2,1)S(1)}, u32[]{:S(2)}, u32[]{:S(2)}) collective-permute-start(bf16[32,2048]{1,0:T(8,128)(2,1)} %get-tuple-element.11), channel_id=1, source_target_pairs={{0,1},{1,0},{2,3},{3,2},{4,5},{5,4},{6,7},{7,6},{8,9},{9,8},{10,11... | collective-permute-start | bytes 393224 | tf_op jit(solution)/shard_map/ppermute | solution.py:384
  83.9 3.6 %collective-permute-start.7 = (bf16[32,2048]{1,0:T(8,128)(2,1)S(1)}, bf16[32,2048]{1,0:T(8,128)(2,1)S(1)}, u32[]{:S(2)}, u32[]{:S(2)}) collective-permute-start(bf16[32,2048]{1,0:T(8,128)(2,1)S(1)} %add_convert_fusion.1), channel_id=1, source_target_pairs={{0,2},{1,3},{2,0},{3,1},{4,6},{5,7},{6,4},{7,5},{8,10},{9,11},{10,... | collective-permute-start | bytes 393224 | tf_op jit(solution)/shard_map/ppermute | solution.py:384
  88.0 0.9 add_convert_fusion
  89.0 4.3 %collective-permute-start.9 = (bf16[32,2048]{1,0:T(8,128)(2,1)S(1)}, bf16[32,2048]{1,0:T(8,128)(2,1)S(1)}, u32[]{:S(2)}, u32[]{:S(2)}) collective-permute-start(bf16[32,2048]{1,0:T(8,128)(2,1)S(1)} %add_convert_fusion), channel_id=1, source_target_pairs={{0,2},{1,3},{2,0},{3,1},{4,6},{5,7},{6,4},{7,5},{8,10},{9,11},{10,... | collective-permute-start | bytes 393224 | tf_op jit(solution)/shard_map/ppermute | solution.py:384
  93.4 2.2 %collective-permute-start.5 = (bf16[128,2048]{1,0:T(8,128)(2,1)S(1)}, bf16[128,2048]{1,0:T(8,128)(2,1)S(1)}, u32[]{:S(2)}, u32[]{:S(2)}) collective-permute-start(bf16[128,2048]{1,0:T(8,128)(2,1)S(1)} %copy-done.11), channel_id=1, source_target_pairs={{0,28},{4,0},{8,4},{12,8},{16,12},{20,16},{24,20},{28,24},{1,29},{... | collective-permute-start | bytes 1572872 | tf_op jit(solution)/shard_map/ppermute | solution.py:332
  95.5 1.7 %collective-permute-done.9 = bf16[32,2048]{1,0:T(8,128)(2,1)S(1)} collective-permute-done((bf16[32,2048]{1,0:T(8,128)(2,1)S(1)}, bf16[32,2048]{1,0:T(8,128)(2,1)S(1)}, u32[]{:S(2)}, u32[]{:S(2)}) %collective-permute-start.9) | collective-permute-done | bytes 131104 | tf_op jit(solution)/shard_map/ppermute | solution.py:384
  97.8 0.6 slice_bitcast_fusion.11
  98.4 0.8 slice_bitcast_fusion.2
  99.2 3.1 %collective-permute-done.5 = bf16[128,2048]{1,0:T(8,128)(2,1)S(1)} collective-permute-done((bf16[128,2048]{1,0:T(8,128)(2,1)S(1)}, bf16[128,2048]{1,0:T(8,128)(2,1)S(1)}, u32[]{:S(2)}, u32[]{:S(2)}) %collective-permute-start.5) | collective-permute-done | bytes 524320 | tf_op jit(solution)/shard_map/ppermute | solution.py:332
  102.2 0.8 copy.40
  103.0 0.8 copy.41
  (46 shorter events, 3.3 us)
Async XLA Ops:
  0.6 2.2 %copy-start.4 = (bf16[1,128,2048]{2,1,0:T(8,128)(2,1)S(1)}, bf16[1,128,2048]{2,1,0:T(8,128)(2,1)}, u32[]{:S(2)}) copy-start(bf16[1,128,2048]{2,1,0:T(8,128)(2,1)} %param.29) | copy-start | bytes 1572868
  0.6 2.2 %copy-start.3 = (bf16[1,128,2048]{2,1,0:T(8,128)(2,1)S(1)}, bf16[1,128,2048]{2,1,0:T(8,128)(2,1)}, u32[]{:S(2)}) copy-start(bf16[1,128,2048]{2,1,0:T(8,128)(2,1)} %param.30) | copy-start | bytes 1572868
  2.9 8.1 %copy-start.1 = (bf16[1,2,31,2048]{3,1,2,0:T(2,128)(2,1)S(1)}, bf16[1,2,31,2048]{3,1,2,0:T(2,128)(2,1)}, u32[]{:S(2)}) copy-start(bf16[1,2,31,2048]{3,1,2,0:T(2,128)(2,1)} %param.32) | copy-start | bytes 761860
  2.9 8.1 %copy-start.5 = (bf16[1,2,2048]{2,1,0:T(2,128)(2,1)S(1)}, bf16[1,2,2048]{2,1,0:T(2,128)(2,1)}, u32[]{:S(2)}) copy-start(bf16[1,2,2048]{2,1,0:T(2,128)(2,1)} %param.33) | copy-start | bytes 24580
  2.9 8.1 %copy-start.7 = (s32[8,2]{0,1:T(2,128)S(1)}, s32[8,2]{0,1:T(2,128)}, u32[]{:S(2)}) copy-start(s32[8,2]{0,1:T(2,128)} %param.37) | copy-start | bytes 196
  2.9 8.1 %copy-start.8 = (s32[8,2]{0,1:T(2,128)S(1)}, s32[8,2]{0,1:T(2,128)}, u32[]{:S(2)}) copy-start(s32[8,2]{0,1:T(2,128)} %param.36) | copy-start | bytes 196
  3.0 10.1 %copy-start.6 = (s32[8]{0:T(128)S(1)}, s32[8]{0:T(128)}, u32[]{:S(2)}) copy-start(s32[8]{0:T(128)} %param.35) | copy-start | bytes 100
  3.0 19.1 %collective-permute-start.1 = (bf16[144,2048]{1,0:T(8,128)(2,1)S(1)}, bf16[144,2048]{1,0:T(8,128)(2,1)S(1)}, u32[]{:S(2)}, u32[]{:S(2)}) collective-permute-start(bf16[144,2048]{1,0:T(8,128)(2,1)S(1)} %pad_maximum_fusion.1), channel_id=1, source_target_pairs={{1,0},{2,1},{3,2},{5,4},{6,5},{7,6},{9,8},{10,9},{11,10},{13,12},{... | collective-permute-start | bytes 1769480 | tf_op jit(solution)/shard_map/ppermute | solution.py:338
  4.4 12.6 %copy-start = (bf16[1,2,128,2048]{3,2,1,0:T(8,128)(2,1)S(1)}, bf16[1,2,128,2048]{3,2,1,0:T(8,128)(2,1)}, u32[]{:S(2)}) copy-start(bf16[1,2,128,2048]{3,2,1,0:T(8,128)(2,1)} %param.31) | copy-start | bytes 3145732
  4.5 18.2 %collective-permute-start = (bf16[144,2048]{1,0:T(8,128)(2,1)S(1)}, bf16[144,2048]{1,0:T(8,128)(2,1)}, u32[]{:S(2)}, u32[]{:S(2)}) collective-permute-start(bf16[144,2048]{1,0:T(8,128)(2,1)S(1)} %pad_maximum_fusion), channel_id=1, source_target_pairs={{0,1},{1,2},{2,3},{4,5},{5,6},{6,7},{8,9},{9,10},{10,11},{12,13},{... | collective-permute-start | bytes 1769480 | tf_op jit(solution)/shard_map/ppermute | solution.py:337
  22.1 0.8 copy-start.10
  22.9 20.3 %copy-start.13 = (s32[8]{0:T(128)S(1)}, s32[8]{0:T(128)}, u32[]{:S(2)}) copy-start(s32[8]{0:T(128)} %param.34) | copy-start | bytes 100
  35.9 32.9 %collective-permute-start.4 = (bf16[160,2048]{1,0:T(8,128)(2,1)}, bf16[160,2048]{1,0:T(8,128)(2,1)S(1)}, u32[]{:S(2)}, u32[]{:S(2)}) collective-permute-start(bf16[160,2048]{1,0:T(8,128)(2,1)} %get-tuple-element.8), channel_id=1, source_target_pairs={{0,28},{4,0},{8,4},{12,8},{16,12},{20,16},{24,20},{28,24},{1,29},{... | collective-permute-start | bytes 1966088 | tf_op jit(solution)/shard_map/ppermute | solution.py:332
  37.7 18.2 %collective-permute-start.2 = (bf16[32,2048]{1,0:T(8,128)(2,1)S(1)}, bf16[32,2048]{1,0:T(8,128)(2,1)S(1)}, u32[]{:S(2)}, u32[]{:S(2)}) collective-permute-start(bf16[32,2048]{1,0:T(8,128)(2,1)S(1)} %fusion.1), channel_id=1, source_target_pairs={{0,28},{4,0},{8,4},{12,8},{16,12},{20,16},{24,20},{28,24},{1,29},{... | collective-permute-start | bytes 393224 | tf_op jit(solution)/shard_map/ppermute | solution.py:332
  45.7 38.2 %collective-permute-start.6 = (bf16[32,2048]{1,0:T(8,128)(2,1)}, bf16[32,2048]{1,0:T(8,128)(2,1)S(1)}, u32[]{:S(2)}, u32[]{:S(2)}) collective-permute-start(bf16[32,2048]{1,0:T(8,128)(2,1)} %get-tuple-element.10), channel_id=1, source_target_pairs={{0,1},{1,0},{2,3},{3,2},{4,5},{5,4},{6,7},{7,6},{8,9},{9,8},{10,11... | collective-permute-start | bytes 393224 | tf_op jit(solution)/shard_map/ppermute | solution.py:384
  55.9 0.6 copy-start.12
  68.7 24.6 %collective-permute-start.3 = (bf16[128,2048]{1,0:T(8,128)(2,1)}, bf16[128,2048]{1,0:T(8,128)(2,1)S(1)}, u32[]{:S(2)}, u32[]{:S(2)}) collective-permute-start(bf16[128,2048]{1,0:T(8,128)(2,1)} %shard_map.300), channel_id=1, source_target_pairs={{0,8},{4,12},{8,16},{12,20},{16,24},{20,28},{24,0},{28,4},{1,9},{5... | collective-permute-start | bytes 1572872 | tf_op jit(solution)/shard_map/ppermute | solution.py:332
  68.7 0.8 copy-start.9
  69.6 14.3 %copy-start.2 = (bf16[32,2048]{1,0:T(8,128)(2,1)S(1)}, bf16[32,2048]{1,0:T(8,128)(2,1)}, u32[]{:S(2)}) copy-start(bf16[32,2048]{1,0:T(8,128)(2,1)} %get-tuple-element.10) | copy-start | bytes 393220
  81.2 12.1 %copy-start.11 = (bf16[128,2048]{1,0:T(8,128)(2,1)S(1)}, bf16[128,2048]{1,0:T(8,128)(2,1)}, u32[]{:S(2)}) copy-start(bf16[128,2048]{1,0:T(8,128)(2,1)} %get-tuple-element.9) | copy-start | bytes 1572868
  81.2 6.8 %collective-permute-start.8 = (bf16[32,2048]{1,0:T(8,128)(2,1)}, bf16[32,2048]{1,0:T(8,128)(2,1)S(1)}, u32[]{:S(2)}, u32[]{:S(2)}) collective-permute-start(bf16[32,2048]{1,0:T(8,128)(2,1)} %get-tuple-element.11), channel_id=1, source_target_pairs={{0,1},{1,0},{2,3},{3,2},{4,5},{5,4},{6,7},{7,6},{8,9},{9,8},{10,11... | collective-permute-start | bytes 393224 | tf_op jit(solution)/shard_map/ppermute | solution.py:384
  83.9 9.4 %collective-permute-start.7 = (bf16[32,2048]{1,0:T(8,128)(2,1)S(1)}, bf16[32,2048]{1,0:T(8,128)(2,1)S(1)}, u32[]{:S(2)}, u32[]{:S(2)}) collective-permute-start(bf16[32,2048]{1,0:T(8,128)(2,1)S(1)} %add_convert_fusion.1), channel_id=1, source_target_pairs={{0,2},{1,3},{2,0},{3,1},{4,6},{5,7},{6,4},{7,5},{8,10},{9,11},{10,... | collective-permute-start | bytes 393224 | tf_op jit(solution)/shard_map/ppermute | solution.py:384
  89.0 8.3 %collective-permute-start.9 = (bf16[32,2048]{1,0:T(8,128)(2,1)S(1)}, bf16[32,2048]{1,0:T(8,128)(2,1)S(1)}, u32[]{:S(2)}, u32[]{:S(2)}) collective-permute-start(bf16[32,2048]{1,0:T(8,128)(2,1)S(1)} %add_convert_fusion), channel_id=1, source_target_pairs={{0,2},{1,3},{2,0},{3,1},{4,6},{5,7},{6,4},{7,5},{8,10},{9,11},{10,... | collective-permute-start | bytes 393224 | tf_op jit(solution)/shard_map/ppermute | solution.py:384
  93.4 8.9 %collective-permute-start.5 = (bf16[128,2048]{1,0:T(8,128)(2,1)S(1)}, bf16[128,2048]{1,0:T(8,128)(2,1)S(1)}, u32[]{:S(2)}, u32[]{:S(2)}) collective-permute-start(bf16[128,2048]{1,0:T(8,128)(2,1)S(1)} %copy-done.11), channel_id=1, source_target_pairs={{0,28},{4,0},{8,4},{12,8},{16,12},{20,16},{24,20},{28,24},{1,29},{... | collective-permute-start | bytes 1572872 | tf_op jit(solution)/shard_map/ppermute | solution.py:332

commit v2 on v1

v2 whole, which is shorter than its diff:
```python
import functools

import jax
import jax.numpy as jnp
import ml_dtypes
import numpy as np
from jax import lax
from jax.experimental import pallas as pl
from jax.experimental.pallas import tpu as pltpu
from jax.sharding import PartitionSpec as P

epsilon = 1e-05
BLOCK = 512
LANES = 128
F32 = jnp.float32
BF16 = jnp.bfloat16


def split(matrix):
    high = matrix.astype(ml_dtypes.bfloat16)
    low = (matrix - high.astype(np.float64)).astype(ml_dtypes.bfloat16)
    return high, low


def angles(size, times):
    return 2.0 * np.pi / size * np.outer(np.arange(size // 2) + 0.5, np.asarray(times, np.float64))


def to_freq(size, times):
    phase = angles(size, times)
    return np.concatenate([np.cos(phase), -np.sin(phase)], axis=0)


def from_freq(size, times):
    phase = angles(size, times).T
    return 2.0 / size * np.concatenate([np.cos(phase), -np.sin(phase)], axis=1)


def stacked(matrix):
    return np.stack(split(matrix))


def beside(matrix):
    return np.concatenate(split(matrix), axis=1)


def tap_freq(size, taps):
    phase = angles(size, np.arange(taps) - (taps - 1) // 2)
    table = np.concatenate([np.cos(phase), np.sin(phase)], axis=0)
    return beside(np.concatenate([table, np.zeros((size, 1))], axis=1))


def dot(a, b):
    return jnp.dot(a, b, preferred_element_type=F32)


def forward_dft(table, values):
    return dot(table[0], values) + dot(table[1], values)


def inverse_dft(table, values):
    high = values.astype(BF16)
    low = (values - high.astype(F32)).astype(BF16)
    return dot(table[0], high) + (dot(table[1], high) + dot(table[0], low))


def halves(values):
    half = values.shape[0] // 2
    return values[:half], values[half:]


def product(a, b):
    ar, ai = halves(a)
    br, bi = halves(b)
    return jnp.concatenate([ar * br - ai * bi, ar * bi + ai * br], axis=0)


def product_conj(a, b):
    ar, ai = halves(a)
    br, bi = halves(b)
    return jnp.concatenate([ar * br + ai * bi, ai * br - ar * bi], axis=0)


def sigmoid(values):
    return 0.5 * jnp.tanh(0.5 * values) + 0.5


def wide(stat, count):
    return jnp.concatenate([stat] * (count // LANES), axis=1)


def norm_rows(ref, start, count, at, gain, first, length, masked_ref, mean_ref, inverse_ref):
    width = masked_ref.shape[1]
    rows = pl.ds(start, count)
    tiles = [pl.ds(i * LANES, LANES) for i in range(width // LANES)]

    def values(tile):
        return ref[rows, tile].astype(F32)

    total = values(tiles[0])
    for tile in tiles[1:]:
        total = total + values(tile)
    mean = jnp.sum(total, axis=1, keepdims=True) * (1.0 / width)
    mean = jnp.broadcast_to(mean, (count, LANES))
    square = jnp.zeros((count, LANES), F32)
    for tile in tiles:
        center = values(tile) - mean
        square = square + center * center
    var = jnp.sum(square, axis=1, keepdims=True) * (1.0 / width)
    inverse = jnp.broadcast_to(lax.rsqrt(var + epsilon), (count, LANES))
    frame = first + at + lax.broadcasted_iota(jnp.int32, (count, LANES), 0)
    mask = ((frame >= 0) & (frame < length)).astype(F32)
    scale = mask * inverse
    out = pl.ds(at, count)
    for tile in tiles:
        masked_ref[out, tile] = ((values(tile) - mean) * scale * gain(tile)).astype(BF16)
    if mean_ref is not None:
        mean_ref[out, :] = mean
        inverse_ref[out, :] = inverse


def norm_pieces(pieces, gain, first, length, masked_ref, mean_ref=None, inverse_ref=None, chunk=64):
    at = 0
    for ref, start, count in pieces:
        for begin in range(0, count, chunk):
            norm_rows(
                ref, start + begin, min(chunk, count - begin), at + begin,
                gain, first, length, masked_ref, mean_ref, inverse_ref,
            )
        at += count


def window(pieces, columns):
    parts = [ref[pl.ds(start, count), columns] for ref, start, count in pieces]
    return parts[0] if len(parts) == 1 else jnp.concatenate(parts, axis=0)


def each_block(width, body):
    def step(i, _):
        body(pl.ds(pl.multiple_of(i * BLOCK, BLOCK), BLOCK))
        return 0

    lax.fori_loop(0, width // BLOCK, step, 0)


def tap_spectrum(table, weights):
    return dot(table, jnp.concatenate([weights, weights], axis=0))


def gate_factor(conv):
    gate = sigmoid(conv)
    return gate * (1.0 + conv * (1.0 - gate))


def place(rows):
    sections = lax.axis_size("section")
    return lax.axis_index("section"), sections, lax.axis_index("tm") * rows


def lane_sum(values):
    total = values[:, :LANES]
    for lane in range(LANES, values.shape[1], LANES):
        total = total + values[:, lane : lane + LANES]
    return total


class Back:
    def __init__(self, own, reach, saved, mean, inverse, gain, mask_row, go_table, gh_table, x_table):
        self.__dict__.update(locals())

    def mixed(self, pieces, factor, columns):
        return (window(pieces, columns).astype(F32) * factor).astype(BF16)

    def spectra(self, mixed):
        own, reach = self.own, self.reach
        inner = mixed[reach : reach + own]
        ends = jnp.concatenate([mixed[:reach], mixed[reach + own :]], axis=0)
        g_own = dot(self.go_table[...], jnp.concatenate([inner, inner], axis=0))
        return g_own, g_own + dot(self.gh_table[...], jnp.concatenate([ends, ends], axis=0))

    def rest(self, g_all, q, columns, scaled, sum_a, sum_b):
        grad_masked = wide(self.mask_row, BLOCK) * inverse_dft(self.x_table, product_conj(g_all, q))
        centered = self.saved[:, columns].astype(F32) - wide(self.mean[...], BLOCK)
        weighted = grad_masked * (centered * wide(self.inverse[...], BLOCK))
        gain = self.gain(columns)
        by_gain = grad_masked * gain
        scaled[:, columns] = by_gain
        sum_a[...] += lane_sum(by_gain)
        sum_b[...] += lane_sum(weighted * gain)
        return jnp.sum(weighted, axis=0, keepdims=True)

    def finish(self, ref, start, scaled, sum_a, sum_b, outs, chunk=64):
        width = self.saved.shape[1]
        for begin in range(0, self.own, chunk):
            rows = pl.ds(begin, chunk)
            mean = self.mean[rows, :]
            inverse = self.inverse[rows, :]
            mean_a = jnp.sum(sum_a[rows, :], axis=1, keepdims=True) * (1.0 / width)
            mean_b = jnp.sum(sum_b[rows, :], axis=1, keepdims=True) * (1.0 / width)
            slope = inverse * jnp.broadcast_to(mean_b, (chunk, LANES)) * inverse
            fixed = inverse * jnp.broadcast_to(mean_a, (chunk, LANES)) - slope * mean
            for lane in range(0, width, LANES):
                tile = pl.ds(lane, LANES)
                change = inverse * scaled[rows, tile] - fixed - slope * self.saved[rows, tile].astype(F32)
                value = ref[pl.ds(start + begin, chunk), tile].astype(F32) + change
                for out, low, high in outs:
                    if low < begin + chunk and high > begin:
                        a, b = max(low, begin), min(high, begin + chunk)
                        out[pl.ds(a - low, b - a), tile] = value[a - begin : b - begin].astype(BF16)


def own_mask(own, first, length):
    frame = first + lax.broadcasted_iota(jnp.int32, (own, LANES), 0)
    return (frame < length).astype(F32)


def slot_row(weights, slot):
    last = weights.shape[1] - 1
    return lambda columns: weights[slot, last : last + 1, columns].astype(F32)


def first_backward_kernel(
    reach, lengths, slots, saved, left, right, grads, weights,
    m_table, q_table, c_table, go_table, gh_table, x_table,
    grad_x, top, bottom, masked, inner, gain_sum, mean, inverse, scaled, sum_a, sum_b,
):
    own = saved.shape[0]
    width = saved.shape[1]
    half = reach // 2
    section, sections, first = place(own)
    slot, length = slots[section, 0], lengths[section]
    gain = slot_row(weights, slot)
    pieces = [(left, 0, reach), (saved, 0, own), (right, 0, reach)]
    norm_pieces(pieces, gain, first - reach, length, masked, mean, inverse)
    grad_pieces = [(left, reach, half), (grads, 0, own), (right, reach, half)]
    middle = pl.ds(reach, own)
    back = Back(
        own, half, saved, mean.at[middle], inverse.at[middle], gain, own_mask(own, first, length),
        go_table, gh_table, x_table,
    )
    sum_a[...] = jnp.zeros_like(sum_a)
    sum_b[...] = jnp.zeros_like(sum_b)

    def block(columns):
        q = tap_spectrum(q_table[...], weights[slot, :, columns])
        m = forward_dft(m_table, masked[:, columns])
        conv = inverse_dft(c_table, product(m, q))
        mixed = back.mixed(grad_pieces, gate_factor(conv), columns)
        inner[:, columns] = mixed[half : half + own]
        gain_sum[:, columns] = back.rest(back.spectra(mixed)[1], q, columns, scaled, sum_a, sum_b)

    each_block(width, block)
    outs = [(grad_x, 0, own), (top, 0, half), (bottom, own - half, own)]
    back.finish(grads, 0, scaled, sum_a, sum_b, outs)


def first_taps_kernel(masked, inner, gain_sum, m_table, go_table, t_table, taps):
    def block(columns):
        m = forward_dft(m_table, masked[:, columns])
        mixed = inner[:, columns]
        g_own = dot(go_table[...], jnp.concatenate([mixed, mixed], axis=0))
        put_taps(taps, inverse_dft(t_table, product_conj(m, g_own)), gain_sum[:, columns], columns)

    each_block(masked.shape[1], block)


def put_taps(taps, tap, gain_sum, columns):
    row = lax.broadcasted_iota(jnp.int32, tap.shape, 0)
    taps[:, columns] = jnp.where(row == tap.shape[0] - 1, gain_sum, tap).astype(taps.dtype)


def prepare_kernel(
    reach, lengths, slots, saved, left, right, weights,
    m_table, q_table, c_table,
    m_out, q_out, factor_out, mean_out, inverse_out, masked, mean, inverse,
):
    own, width = saved.shape
    section, sections, first = place(own)
    slot, length = slots[section, 1], lengths[lax.rem(section + 1, sections)]
    gain = slot_row(weights, slot)
    pieces = [(left, 0, reach), (saved, 0, own), (right, 0, reach)]
    norm_pieces(pieces, gain, first - reach, length, masked, mean, inverse)
    mean_out[...] = mean[pl.ds(reach, own), :]
    inverse_out[...] = inverse[pl.ds(reach, own), :]

    def block(columns):
        q = tap_spectrum(q_table[...], weights[slot, :, columns])
        m = forward_dft(m_table, masked[:, columns])
        q_out[:, columns] = q
        m_out[:, columns] = m
        factor_out[:, columns] = gate_factor(inverse_dft(c_table, product(m, q)))

    each_block(width, block)


def second_backward_kernel(
    lengths, slots, saved, left, grads, right, weights, m, q, factor, mean, inverse,
    go_table, gh_table, x_table, t_table,
    grad_x, taps, scaled, sum_a, sum_b,
):
    own, width = saved.shape
    half = left.shape[0]
    section, sections, first = place(own)
    slot, length = slots[section, 1], lengths[lax.rem(section + 1, sections)]
    pieces = [(left, 0, half), (grads, 0, own), (right, 0, half)]
    back = Back(
        own, half, saved, mean, inverse, slot_row(weights, slot), own_mask(own, first, length),
        go_table, gh_table, x_table,
    )
    sum_a[...] = jnp.zeros_like(sum_a)
    sum_b[...] = jnp.zeros_like(sum_b)

    def block(columns):
        mixed = back.mixed(pieces, factor[:, columns], columns)
        g_own, g_all = back.spectra(mixed)
        tap = inverse_dft(t_table, product_conj(m[:, columns], g_own))
        gain_sum = back.rest(g_all, q[:, columns], columns, scaled, sum_a, sum_b)
        put_taps(taps, tap, gain_sum, columns)

    each_block(width, block)
    back.finish(grads, 0, scaled, sum_a, sum_b, [(grad_x, 0, own)])


def forward_kernel(
    reach, lengths, slots, act, left, right, weights, later,
    m0_table, q0_table, c0_table, m1_table, q1_table, c1_table,
    out, masked0, between, masked1,
):
    own, width = act.shape
    middle = reach // 2
    section, sections, first = place(own)
    slot, length = slots[section, 0], lengths[section]
    at = left.shape[0] - reach
    pieces = [(left, at, reach), (act, 0, own), (right, at, reach)]
    inner = [(left, at + middle, middle), (act, 0, own), (right, at, middle)]
    norm_pieces(pieces, slot_row(weights, slot), first - reach, length, masked0)

    def first_layer(columns):
        q = tap_spectrum(q0_table[...], weights[slot, :, columns])
        conv = inverse_dft(c0_table, product(forward_dft(m0_table, masked0[:, columns]), q))
        between[:, columns] = (window(inner, columns).astype(F32) + conv * sigmoid(conv)).astype(BF16)

    each_block(width, first_layer)
    last = later.shape[0] - 1
    norm_pieces([(between, 0, own + 2 * middle)], lambda tile: later[last : last + 1, tile].astype(F32), first - middle, length, masked1)

    def second_layer(columns):
        q = tap_spectrum(q1_table[...], later[:, columns])
        conv = inverse_dft(c1_table, product(forward_dft(m1_table, masked1[:, columns]), q))
        here = between[middle : middle + own, columns].astype(F32)
        out[:, columns] = (here + conv * sigmoid(conv)).astype(BF16)

    each_block(width, second_layer)


def pack_kernel(count, refs):
    sems = refs[-1]
    copies = [
        pltpu.make_async_copy(refs[a].at[i].at[pl.ds(s, n)], refs[b].at[pl.ds(t, n)], sems.at[k])
        for k, (a, i, s, n, b, t) in enumerate(count)
    ]
    for copy in copies:
        copy.start()
    for copy in copies:
        copy.wait()


def final_kernel(slots, mine0, other0, mine1, other1, act, grad, act_out, grad_out, taps, gains, sems):
    copies = [
        pltpu.make_async_copy(act, act_out, sems.at[0]),
        pltpu.make_async_copy(grad, grad_out, sems.at[1]),
    ]
    for copy in copies:
        copy.start()
    section = lax.axis_index("section")
    count = taps.shape[0]
    total0 = mine0[...].astype(F32) + other0[...].astype(F32)
    total1 = mine1[...].astype(F32) + other1[...].astype(F32)
    for slot in range(taps.shape[1]):
        use0 = (slots[section, 0] == slot).astype(F32)
        use1 = (slots[section, 1] == slot).astype(F32)
        total = use0 * total0 + use1 * total1
        taps[:, slot, :] = total[:count]
        gains[slot : slot + 1, :] = total[count:]
    for copy in copies:
        copy.wait()


def span(reach, own):
    return np.arange(-reach, own + reach)


VMEM = pl.BlockSpec(memory_space=pltpu.VMEM)
SMEM = pl.BlockSpec(memory_space=pltpu.SMEM)
ANY = pl.BlockSpec(memory_space=pl.ANY)
LIMIT = 24 * 1024 * 1024


def call(kernel, outs, scratch, operands, flops, specs=None, out_specs=None):
    moved = sum(int(np.prod(x.shape)) * x.dtype.itemsize for x in operands)
    if specs is None:
        specs = [SMEM if x.dtype == jnp.int32 else VMEM for x in operands]
    return pl.pallas_call(
        kernel,
        out_shape=outs,
        in_specs=specs,
        out_specs=jax.tree.map(lambda _: VMEM, outs) if out_specs is None else out_specs,
        scratch_shapes=scratch,
        compiler_params=pltpu.CompilerParams(vmem_limit_bytes=LIMIT),
        cost_estimate=pl.CostEstimate(flops=flops, bytes_accessed=moved, transcendentals=0),
    )(*operands)


def like(rows, width, dtype):
    return jax.ShapeDtypeStruct((rows, width), dtype)


def up16(count):
    return -(-count // 16) * 16


def local(
    act_in, grad_in, saved_inputs, kernels, norm_gains,
    forward_lengths, backward_lengths, forward_slots, backward_slots,
):
    sections = lax.axis_size("section")
    shards = lax.axis_size("tm")
    section = lax.axis_index("section")
    act, grad, saved = act_in[0], grad_in[0], saved_inputs[0]
    own, width = act.shape
    tap_count = kernels.shape[2]
    half = (tap_count - 1) // 2
    one, two = up16(half), up16(2 * half)
    size = own + 2 * two
    small = own + 2 * one

    def shifted(x, by):
        return lax.ppermute(x, "section", [(i, (i + by) % sections) for i in range(sections)])

    def to_neighbour(x, by, along):
        pairs = [
            (s * shards + t, (s + by) % sections * shards + t + along)
            for s in range(sections)
            for t in range(shards)
            if 0 <= t + along < shards
        ]
        return lax.ppermute(x, ("section", "tm"), pairs)

    end, end2 = own - one, own - two
    plan = [
        (0, 0, end2, two, 3, 0), (1, 0, end, one, 3, two), (0, 0, 0, two, 4, 0), (1, 0, 0, one, 4, two),
        (0, 1, end2, two, 5, 0), (2, 0, end2, two, 5, two), (0, 1, 0, two, 6, 0), (2, 0, 0, two, 6, two),
    ]
    tail0, head0, tail1, head1 = call(
        lambda *refs: pack_kernel(plan, refs),
        tuple(like(n, width, BF16) for n in (two + one, two + one, 2 * two, 2 * two)),
        [pltpu.SemaphoreType.DMA((len(plan),))],
        (saved, grad_in, act_in),
        0, [ANY] * 3, (ANY,) * 4,
    )
    up = [(i, i + 1) for i in range(shards - 1)]
    down = [(i + 1, i) for i in range(shards - 1)]
    left0, right0 = lax.ppermute(tail0, "tm", up), lax.ppermute(head0, "tm", down)
    left1, right1 = lax.ppermute(tail1, "tm", up), lax.ppermute(head1, "tm", down)
    weights = jnp.concatenate([kernels[0], norm_gains[0][:, None, :]], axis=1)
    later = shifted(lax.dynamic_index_in_dim(weights, forward_slots[section, 1], 0, keepdims=False), -1)

    ends = np.concatenate([np.arange(-one, 0), np.arange(own, own + one)])
    tap_back = np.concatenate([from_freq(size, np.arange(tap_count) - half), np.zeros((1, size))], axis=0)
    m_table = stacked(to_freq(size, span(two, own)))
    q_table = tap_freq(size, tap_count)
    c_table = stacked(from_freq(size, span(one, own)))
    go_table = beside(to_freq(size, np.arange(own)))
    gh_table = beside(to_freq(size, ends))
    x_table = stacked(from_freq(size, span(0, own)))
    t_table = stacked(tap_back)
    work = 2 * size * size * width

    def run(kernel, outs, scratch, operands, flops):
        return call(kernel, outs, scratch, [jnp.asarray(x) for x in operands], flops)

    rows = [pltpu.VMEM((own, width), F32)] + [pltpu.VMEM((own, LANES), F32)] * 2
    stats = [pltpu.VMEM((size, LANES), F32)] * 2
    grad_mid, top, bottom, masked0, inner0, gain0 = run(
        functools.partial(first_backward_kernel, two),
        (
            like(own, width, BF16), like(one, width, BF16), like(one, width, BF16),
            like(size, width, BF16), like(own, width, BF16), like(1, width, F32),
        ),
        stats + rows,
        [
            backward_lengths, backward_slots, saved[0], left0, right0, grad, weights,
            m_table, q_table, c_table, go_table, gh_table, x_table,
        ],
        9 * work,
    )
    mid_right = to_neighbour(top, -1, -1)
    mid_left = to_neighbour(bottom, -1, 1)
    grad_mid = shifted(grad_mid, -1)
    taps0 = run(
        first_taps_kernel, like(tap_count + 1, width, BF16), [],
        [masked0, inner0, gain0, m_table, go_table, t_table], 3 * work,
    )
    act_out = run(
        functools.partial(forward_kernel, two),
        like(own, width, BF16),
        [pltpu.VMEM((size, width), BF16), pltpu.VMEM((small, width), BF16), pltpu.VMEM((small, width), BF16)],
        [
            forward_lengths, forward_slots, act, left1, right1, weights, later,
            m_table, q_table, c_table,
            stacked(to_freq(small, span(one, own))), tap_freq(small, tap_count), stacked(from_freq(small, span(0, own))),
        ],
        10 * work,
    )
    act_out = shifted(act_out, 2)
    prepared = run(
        functools.partial(prepare_kernel, two),
        (
            like(size, width, F32), like(size, width, F32), like(small, width, F32),
            like(own, LANES, F32), like(own, LANES, F32),
        ),
        [pltpu.VMEM((size, width), BF16)] + stats,
        [backward_lengths, backward_slots, saved[1], left1, right1, weights, m_table, q_table, c_table],
        6 * work,
    )
    grad_out, taps1 = run(
        second_backward_kernel,
        (like(own, width, BF16), like(tap_count + 1, width, BF16)),
        rows,
        [
            backward_lengths, backward_slots, saved[1], mid_left, grad_mid, mid_right, weights, *prepared,
            go_table, gh_table, x_table, t_table,
        ],
        6 * work,
    )

    def summed(x):
        step = 1
        while True:
            other = lax.ppermute(x, "tm", [(i, i ^ step) for i in range(shards)])
            step *= 2
            if step >= shards:
                return x, other
            x = (x.astype(F32) + other.astype(F32)).astype(BF16)

    grad_out = shifted(grad_out, -1)
    sums = summed(taps0) + summed(taps1)
    slots = kernels.shape[1]
    act_out, grad_out, taps, gains = call(
        final_kernel,
        (
            like(own, width, BF16), like(own, width, BF16),
            jax.ShapeDtypeStruct((tap_count, slots, width), F32), like(slots, width, F32),
        ),
        [pltpu.SemaphoreType.DMA((2,))],
        (backward_slots, *sums, act_out, grad_out),
        0, [SMEM] + [VMEM] * 4 + [ANY] * 2, (ANY, ANY, VMEM, VMEM),
    )
    return act_out[None], grad_out[None], taps.transpose(1, 0, 2)[None], gains[None]


def solution(mesh):
    in_specs = (
        P("section", "tm", None),
        P("section", "tm", None),
        P("section", None, "tm", None),
        P("section", None, None, None),
        P("section", None, None),
        P(),
        P(),
        P(),
        P(),
    )
    out_specs = (
        P("section", "tm", None),
        P("section", "tm", None),
        P("section", None, None, None),
        P("section", None, None),
    )
    return jax.shard_map(local, mesh=mesh, in_specs=in_specs, out_specs=out_specs, check_vma=False)
```

time: 104 us -> 82.7 us (0.80)
  other arithmetic: 9.05 us -> 0.78 us
  Pallas kernels: 36.8 us -> 28.8 us
  waiting for transfers between devices: 9.95 us -> 4.04 us
    ppermute x2 -> x6, starting transfers between devices: 7.88 us -> 18.3 us  [the longest x2 5.44 us: to_neighbour(): return lax.ppermute(x, ('section', 'tm'), pairs)]
    pallas_call x3 -> x7, Pallas kernels: 36.8 us -> 28.8 us  [call(): pl.pallas_call(kernel, out_shape=outs, in_specs=specs, out_specs=jax.tree...]
    ppermute x4, starting transfers between devices: 20.8 us -> 13.1 us  [summed(): other = lax.ppermute(x, 'tm', [(i, i ^ step) for i in range(shards)])]
    unnamed x31 -> x73, local copies, waits for them, and re-layouts: 3.48 us -> 9.49 us
    another operation x3 -> x0, other arithmetic: 5.52 us -> none  [scalars(): return jnp.stack([slot, length, first]).astype(jnp.int32)]
    ppermute x2 -> x6, waiting for transfers between devices: 4.63 us -> 0.02 us  [the longest x2 0.01 us: to_neighbour(): return lax.ppermute(x, ('section', 'tm'), pairs)]
    ppermute x4, waiting for transfers between devices: 3.07 us -> 0.03 us  [shifted(): lax.ppermute(x, 'section', [(i, (i + by) % sections) for i in range(secti...]
    ppermute x4, starting transfers between devices: 6.52 us -> 3.83 us  [shifted(): lax.ppermute(x, 'section', [(i, (i + by) % sections) for i in range(secti...]
  transfers between devices with their start and end apart: 10 -> 14, of which waited for: 5 -> 2; matrix products, arithmetic and copies ran while one was open for 13% -> 2% of each run, Pallas kernels for 23% -> 31%
where the time goes in v2:
time: 82.7 us; the launch traced here: 82 us
  starting transfers between devices  35.1 us (42%)
  Pallas kernels  28.8 us (35%)
  local copies, waits for them, and re-layouts  10.2 us (12%)
  waiting for transfers between devices  4.04 us (5%)
  between operations  3.03 us (4%)
    pallas_call x7, Pallas kernels, call(): pl.pallas_call(kernel, out_shape=outs, in_specs=specs, out_specs=jax.tree...  28.8 us
    ppermute x4, starting transfers between devices, summed(): other = lax.ppermute(x, 'tm', [(i, i ^ step) for i in range(shards)])  13.1 us
    unnamed x73, local copies, waits for them, and re-layouts  9.49 us
    ppermute x2, starting transfers between devices, to_neighbour(): return lax.ppermute(x, ('section', 'tm'), pairs)  5.44 us
    ppermute x1, starting transfers between devices, local(): lax.ppermute(tail1, 'tm', up)  5.25 us
    ppermute x1, starting transfers between devices, local(): lax.ppermute(tail0, 'tm', up)  4.99 us
    ppermute x4, waiting for transfers between devices, summed(): other = lax.ppermute(x, 'tm', [(i, i ^ step) for i in range(shards)])  4 us
    ppermute x4, starting transfers between devices, shifted(): lax.ppermute(x, 'section', [(i, (i + by) % sections) for i in range(secti...  3.83 us
  transfers between devices with their start and end apart: 14, of which 2 were waited for; matrix products, arithmetic and copies ran while one was open for 2% of the time, Pallas kernels for 31%

profile of v2, /device:TPU:0, one launch (start us, length us, event | category | flops | bytes accessed | tf_op | source)
XLA Modules:
  0.0 82.0 jit_solution(16857648010337372831)
XLA Ops:
  0.6 1.2 %copy-done = bf16[1,2,128,2048]{3,2,1,0:T(8,128)(2,1)S(1)} copy-done((bf16[1,2,128,2048]{3,2,1,0:T(8,128)(2,1)S(1)}, bf16[1,2,128,2048]{3,2,1,0:T(8,128)(2,1)}, u32[]{:S(2)}) %copy-start) | copy-done | bytes 1048600
  1.9 1.0 %copy-done.1 = bf16[1,128,2048]{2,1,0:T(8,128)(2,1)S(1)} copy-done((bf16[1,128,2048]{2,1,0:T(8,128)(2,1)S(1)}, bf16[1,128,2048]{2,1,0:T(8,128)(2,1)}, u32[]{:S(2)}) %copy-start.1) | copy-done | bytes 524312
  2.9 1.0 %copy-done.3 = bf16[1,128,2048]{2,1,0:T(8,128)(2,1)S(1)} copy-done((bf16[1,128,2048]{2,1,0:T(8,128)(2,1)S(1)}, bf16[1,128,2048]{2,1,0:T(8,128)(2,1)}, u32[]{:S(2)}) %copy-start.3) | copy-done | bytes 524312
  3.9 1.3 %shard_map.210 = (bf16[48,2048]{1,0:T(8,128)(2,1)S(1)}, bf16[48,2048]{1,0:T(8,128)(2,1)S(1)}, bf16[64,2048]{1,0:T(8,128)(2,1)}, bf16[64,2048]{1,0:T(8,128)(2,1)}) custom-call(bf16[2,128,2048]{2,1,0:T(8,128)(2,1)S(1)} %bitcast.20, bf16[1,128,2048]{2,1,0:T(8,128)(2,1)S(1)} %copy-done.1, bf16[1,128,2048]{2,1,0:T(8,128)(2,1)S(1)} %copy-done.3), custom_call_target="tpu_custom_call" | custom-call | bytes 2097152 | tf_op jit(solution)/shard_map/pallas_call | solution.py:403
  5.3 5.0 %collective-permute-start = (bf16[48,2048]{1,0:T(8,128)(2,1)S(1)}, bf16[48,2048]{1,0:T(8,128)(2,1)S(1)}, u32[]{:S(2)}, u32[]{:S(2)}) collective-permute-start(bf16[48,2048]{1,0:T(8,128)(2,1)S(1)} %get-tuple-element.25), channel_id=1, source_target_pairs={{0,1},{1,2},{2,3},{4,5},{5,6},{6,7},{8,9},{9,10},{10,11},{12,13},{... | collective-permute-start | bytes 589832 | tf_op jit(solution)/shard_map/ppermute | solution.py:463
  10.3 1.3 %collective-permute-start.1 = (bf16[48,2048]{1,0:T(8,128)(2,1)S(1)}, bf16[48,2048]{1,0:T(8,128)(2,1)S(1)}, u32[]{:S(2)}, u32[]{:S(2)}) collective-permute-start(bf16[48,2048]{1,0:T(8,128)(2,1)S(1)} %get-tuple-element.26), channel_id=1, source_target_pairs={{1,0},{2,1},{3,2},{5,4},{6,5},{7,6},{9,8},{10,9},{11,10},{13,12},{... | collective-permute-start | bytes 589832 | tf_op jit(solution)/shard_map/ppermute | solution.py:463
  11.6 5.3 %collective-permute-start.7 = (bf16[64,2048]{1,0:T(8,128)(2,1)}, bf16[64,2048]{1,0:T(8,128)(2,1)}, u32[]{:S(2)}, u32[]{:S(2)}) collective-permute-start(bf16[64,2048]{1,0:T(8,128)(2,1)} %get-tuple-element.33), channel_id=1, source_target_pairs={{0,1},{1,2},{2,3},{4,5},{5,6},{6,7},{8,9},{9,10},{10,11},{12,13},{... | collective-permute-start | bytes 786440 | tf_op jit(solution)/shard_map/ppermute | solution.py:464
  16.9 1.3 %collective-permute-start.8 = (bf16[64,2048]{1,0:T(8,128)(2,1)}, bf16[64,2048]{1,0:T(8,128)(2,1)}, u32[]{:S(2)}, u32[]{:S(2)}) collective-permute-start(bf16[64,2048]{1,0:T(8,128)(2,1)} %get-tuple-element.34), channel_id=1, source_target_pairs={{1,0},{2,1},{3,2},{5,4},{6,5},{7,6},{9,8},{10,9},{11,10},{13,12},{... | collective-permute-start | bytes 786440 | tf_op jit(solution)/shard_map/ppermute | solution.py:464
  18.3 0.6 constant_dynamic-slice_fusion
  21.2 0.7 copy-done.12
  21.8 0.7 copy-done.14
  22.6 0.9 %copy-done.8 = bf16[2,128,192]{2,1,0:T(8,128)(2,1)S(1)} copy-done((bf16[2,128,192]{2,1,0:T(8,128)(2,1)S(1)}, bf16[2,128,192]{2,1,0:T(8,128)(2,1)}, u32[]{:S(2)}) %copy-start.8) | copy-done | bytes 98328
  23.5 0.9 %copy-done.13 = bf16[48,2048]{1,0:T(8,128)(2,1)S(1)} copy-done((bf16[48,2048]{1,0:T(8,128)(2,1)S(1)}, bf16[48,2048]{1,0:T(8,128)(2,1)}, u32[]{:S(2)}) %copy-start.13) | copy-done | bytes 196632
  24.4 0.9 %copy-done.15 = bf16[48,2048]{1,0:T(8,128)(2,1)S(1)} copy-done((bf16[48,2048]{1,0:T(8,128)(2,1)S(1)}, bf16[48,2048]{1,0:T(8,128)(2,1)}, u32[]{:S(2)}) %copy-start.15) | copy-done | bytes 196632
  25.3 0.9 %copy-done.20 = bf16[2,160,192]{2,1,0:T(8,128)(2,1)S(1)} copy-done((bf16[2,160,192]{2,1,0:T(8,128)(2,1)S(1)}, bf16[2,160,192]{2,1,0:T(8,128)(2,1)}, u32[]{:S(2)}) %copy-start.20) | copy-done | bytes 122904
  26.2 0.8 copy-done.24
  27.0 7.4 %shard_map.211 = (bf16[128,2048]{1,0:T(8,128)(2,1)}, bf16[16,2048]{1,0:T(8,128)(2,1)S(1)}, bf16[16,2048]{1,0:T(8,128)(2,1)S(1)}, bf16[192,2048]{1,0:T(8,128)(2,1...) custom-call(s32[8]{0:T(128)S(1)} %copy-done.11, s32[8,2]{1,0:T(8,128)S(1)} %copy.35.slots, ...), custom_call_target="tpu_custom_call" | custom-call | flops 1358954496 | bytes 2220128 | tf_op jit(solution)/shard_map/pallas_call | solution.py:403
  34.4 2.3 %collective-permute-start.5 = (bf16[128,2048]{1,0:T(8,128)(2,1)}, bf16[128,2048]{1,0:T(8,128)(2,1)S(1)}, u32[]{:S(2)}, u32[]{:S(2)}) collective-permute-start(bf16[128,2048]{1,0:T(8,128)(2,1)} %get-tuple-element.31), channel_id=1, source_target_pairs={{0,28},{4,0},{8,4},{12,8},{16,12},{20,16},{24,20},{28,24},{1,29},{... | collective-permute-start | bytes 1572872 | tf_op jit(solution)/shard_map/ppermute | solution.py:438
  36.7 0.7 fusion.1
  37.4 1.5 %collective-permute-start.11 = (bf16[32,2048]{1,0:T(8,128)(2,1)}, bf16[32,2048]{1,0:T(8,128)(2,1)}, u32[]{:S(2)}, u32[]{:S(2)}) collective-permute-start(bf16[32,2048]{1,0:T(8,128)(2,1)} %fusion.1), channel_id=1, source_target_pairs={{0,28},{4,0},{8,4},{12,8},{16,12},{20,16},{24,20},{28,24},{1,29},{... | collective-permute-start | bytes 393224 | tf_op jit(solution)/shard_map/ppermute | solution.py:438
  39.0 4.2 %collective-permute-start.4 = (bf16[16,2048]{1,0:T(8,128)(2,1)}, bf16[16,2048]{1,0:T(8,128)(2,1)S(1)}, u32[]{:S(2)}, u32[]{:S(2)}) collective-permute-start(bf16[16,2048]{1,0:T(8,128)(2,1)} %copy-done.18), channel_id=1, source_target_pairs={{0,29},{1,30},{2,31},{4,1},{5,2},{6,3},{8,5},{9,6},{10,7},{12,9},{... | collective-permute-start | bytes 196616 | tf_op jit(solution)/shard_map/ppermute | solution.py:447
  43.2 2.2 %shard_map.212 = bf16[32,2048]{1,0:T(8,128)(2,1)S(1)} custom-call(bf16[192,2048]{1,0:T(8,128)(2,1)S(1)} %get-tuple-element.27.masked, bf16[128,2048]{1,0:T(8,128)(2,1)S(1)} %get-tuple-element.28.inner, f32[1,2048]{1,0:T(1,128)S(1)} %get-tuple-element.29.gain_sum, bf16[2,192,192]{2,1,0:T(8,128)(2,1)S(1)} %copy-done.6, bf16[192,256]{1,0:T(8,128)(2,1)S(1)} %copy-done.5, ...), custom_call_target="tpu_custom_call" | custom-call | flops 452984832 | bytes 1589248 | tf_op jit(solution)/shard_map/pallas_call | solution.py:403
  45.4 1.3 %collective-permute-start.6 = (bf16[16,2048]{1,0:T(8,128)(2,1)S(1)}, bf16[16,2048]{1,0:T(8,128)(2,1)S(1)}, u32[]{:S(2)}, u32[]{:S(2)}) collective-permute-start(bf16[16,2048]{1,0:T(8,128)(2,1)S(1)} %copy-done.17), channel_id=1, source_target_pairs={{1,28},{2,29},{3,30},{5,0},{6,1},{7,2},{9,4},{10,5},{11,6},{13,8},... | collective-permute-start | bytes 196616 | tf_op jit(solution)/shard_map/ppermute | solution.py:447
  46.7 5.6 %collective-permute-start.2 = (bf16[32,2048]{1,0:T(8,128)(2,1)S(1)}, bf16[32,2048]{1,0:T(8,128)(2,1)S(1)}, u32[]{:S(2)}, u32[]{:S(2)}) collective-permute-start(bf16[32,2048]{1,0:T(8,128)(2,1)S(1)} %shard_map.212), channel_id=1, source_target_pairs={{0,1},{1,0},{2,3},{3,2},{4,5},{5,4},{6,7},{7,6},{8,9},{9,8},{10,11... | collective-permute-start | bytes 393224 | tf_op jit(solution)/shard_map/ppermute | solution.py:540
  52.3 7.3 %shard_map.215 = bf16[128,2048]{1,0:T(8,128)(2,1)S(1)} custom-call(s32[8]{0:T(128)S(1)} %copy-done.19, s32[8,2]{1,0:T(8,128)S(1)} %copy.34.slots, bf16[128,2048]{1,0:T(8,128)(2,1)S(1)} %bitcast.22, bf16[64,2048]{1,0:T(8,128)(2,1)} %collective-permute-done.7.left, bf16[64,2048]{1,0:T(8,128)(2,1)} %collective-permute-done.8.right, ...), custom_call_target="tpu_custom_call" | custom-call | flops 1509949440 | bytes 1941600 | tf_op jit(solution)/shard_map/pallas_call | solution.py:403
  59.7 4.5 %shard_map.213 = (f32[192,2048]{1,0:T(8,128)S(1)}, f32[192,2048]{1,0:T(8,128)S(1)}, f32[160,2048]{1,0:T(8,128)S(1)}, f32[128,128]{1,0:T(8,128)S(1)}, f32[128,128]{1,0:T(8,128)S(1)}) custom-call(s32[8]{0:T(128)S(1)} %copy-done.11, s32[8,2]{1,0:T(8,128)S(1)} %copy.35.slots, bf16[128,2048]{1,0:T(8,128)(2,1)S(1)} %get-tuple-element.46.saved, ...), custom_call_target="tpu_custom_call" | custom-call | flops 905969664 | bytes 1605728 | tf_op jit(solution)/shard_map/pallas_call | solution.py:403
  64.2 3.9 %shard_map.214 = (bf16[128,2048]{1,0:T(8,128)(2,1)S(1)}, bf16[32,2048]{1,0:T(8,128)(2,1)S(1)}) custom-call(s32[8]{0:T(128)S(1)} %copy-done.11, s32[8,2]{1,0:T(8,128)S(1)} %copy.35.slots, bf16[128,2048]{1,0:T(8,128)(2,1)S(1)} %get-tuple-element.46.saved, bf16[16,2048]{1,0:T(8,128)(2,1)S(1)} %collective-permute-done.4.left, ...), custom_call_target="tpu_custom_call" | custom-call | flops 905969664 | bytes 6275168 | tf_op jit(solution)/shard_map/pallas_call | solution.py:403
  68.2 3.8 %collective-permute-start.3 = (bf16[32,2048]{1,0:T(8,128)(2,1)S(1)}, bf16[32,2048]{1,0:T(8,128)(2,1)S(1)}, u32[]{:S(2)}, u32[]{:S(2)}) collective-permute-start(bf16[32,2048]{1,0:T(8,128)(2,1)S(1)} %add_convert_fusion.1.mine0), channel_id=1, source_target_pairs={{0,2},{1,3},{2,0},{3,1},{4,6},{5,7},{6,4},{7,5},{8,10},{9,11},{10,... | collective-permute-start | bytes 393224 | tf_op jit(solution)/shard_map/ppermute | solution.py:540
  72.1 1.1 %collective-permute-done.9 = bf16[32,2048]{1,0:T(8,128)(2,1)S(1)} collective-permute-done((bf16[32,2048]{1,0:T(8,128)(2,1)S(1)}, bf16[32,2048]{1,0:T(8,128)(2,1)S(1)}, u32[]{:S(2)}, u32[]{:S(2)}) %collective-permute-start.9) | collective-permute-done | bytes 131104 | tf_op jit(solution)/shard_map/ppermute | solution.py:540
  73.1 3.5 %collective-permute-start.10 = (bf16[32,2048]{1,0:T(8,128)(2,1)S(1)}, bf16[32,2048]{1,0:T(8,128)(2,1)S(1)}, u32[]{:S(2)}, u32[]{:S(2)}) collective-permute-start(bf16[32,2048]{1,0:T(8,128)(2,1)S(1)} %add_convert_fusion.mine1), channel_id=1, source_target_pairs={{0,2},{1,3},{2,0},{3,1},{4,6},{5,7},{6,4},{7,5},{8,10},{9,11},{10,... | collective-permute-start | bytes 393224 | tf_op jit(solution)/shard_map/ppermute | solution.py:540
  76.7 2.9 %collective-permute-done.10.other1 = bf16[32,2048]{1,0:T(8,128)(2,1)S(1)} collective-permute-done((bf16[32,2048]{1,0:T(8,128)(2,1)S(1)}, bf16[32,2048]{1,0:T(8,128)(2,1)S(1)}, u32[]{:S(2)}, u32[]{:S(2)}) %collective-permute-start.10) | collective-permute-done | bytes 131104 | tf_op jit(solution)/shard_map/ppermute | solution.py:540
  79.6 2.4 %shard_map.216 = (bf16[128,2048]{1,0:T(8,128)(2,1)}, bf16[128,2048]{1,0:T(8,128)(2,1)}, f32[31,2,2048]{2,1,0:T(2,128)}, f32[2,2048]{1,0:T(2,128)}) custom-call(s32[8,2]{1,0:T(8,128)S(1)} %copy.35.slots, bf16[32,2048]{1,0:T(8,128)(2,1)S(1)} %add_convert_fusion.1.mine0, bf16[32,2048]{1,0:T(8,128)(2,1)S(1)} %collective-permute-done.3.other0, ...), custom_call_target="tpu_custom_call" | custom-call | bytes 1572928 | tf_op jit(solution)/shard_map/pallas_call | solution.py:403
  (83 shorter events, 0.8 us)
Async XLA Ops:
  5.3 13.0 %copy-start.34 = (s32[8,2]{0,1:T(2,128)S(1)}, s32[8,2]{0,1:T(2,128)}, u32[]{:S(2)}) copy-start(s32[8,2]{0,1:T(2,128)} %param.26) | copy-start | bytes 196
  5.3 14.9 %copy-start.33 = (s32[8,2]{0,1:T(2,128)S(1)}, s32[8,2]{0,1:T(2,128)}, u32[]{:S(2)}) copy-start(s32[8,2]{0,1:T(2,128)} %param.27) | copy-start | bytes 196
  5.3 15.0 %copy-start.32 = (bf16[1,2,2048]{2,1,0:T(2,128)(2,1)S(1)}, bf16[1,2,2048]{2,1,0:T(2,128)(2,1)}, u32[]{:S(2)}) copy-start(bf16[1,2,2048]{2,1,0:T(2,128)(2,1)} %param.23) | copy-start | bytes 24580
  5.3 15.0 %copy-start.29 = (bf16[1,2,31,2048]{3,1,2,0:T(2,128)(2,1)S(1)}, bf16[1,2,31,2048]{3,1,2,0:T(2,128)(2,1)}, u32[]{:S(2)}) copy-start(bf16[1,2,31,2048]{3,1,2,0:T(2,128)(2,1)} %param.22) | copy-start | bytes 761860
  5.3 15.8 %collective-permute-start = (bf16[48,2048]{1,0:T(8,128)(2,1)S(1)}, bf16[48,2048]{1,0:T(8,128)(2,1)S(1)}, u32[]{:S(2)}, u32[]{:S(2)}) collective-permute-start(bf16[48,2048]{1,0:T(8,128)(2,1)S(1)} %get-tuple-element.25), channel_id=1, source_target_pairs={{0,1},{1,2},{2,3},{4,5},{5,6},{6,7},{8,9},{9,10},{10,11},{12,13},{... | collective-permute-start | bytes 589832 | tf_op jit(solution)/shard_map/ppermute | solution.py:463
  10.3 11.5 %collective-permute-start.1 = (bf16[48,2048]{1,0:T(8,128)(2,1)S(1)}, bf16[48,2048]{1,0:T(8,128)(2,1)S(1)}, u32[]{:S(2)}, u32[]{:S(2)}) collective-permute-start(bf16[48,2048]{1,0:T(8,128)(2,1)S(1)} %get-tuple-element.26), channel_id=1, source_target_pairs={{1,0},{2,1},{3,2},{5,4},{6,5},{7,6},{9,8},{10,9},{11,10},{13,12},{... | collective-permute-start | bytes 589832 | tf_op jit(solution)/shard_map/ppermute | solution.py:463
  11.6 35.1 %collective-permute-start.7 = (bf16[64,2048]{1,0:T(8,128)(2,1)}, bf16[64,2048]{1,0:T(8,128)(2,1)}, u32[]{:S(2)}, u32[]{:S(2)}) collective-permute-start(bf16[64,2048]{1,0:T(8,128)(2,1)} %get-tuple-element.33), channel_id=1, source_target_pairs={{0,1},{1,2},{2,3},{4,5},{5,6},{6,7},{8,9},{9,10},{10,11},{12,13},{... | collective-permute-start | bytes 786440 | tf_op jit(solution)/shard_map/ppermute | solution.py:464
  16.9 35.4 %collective-permute-start.8 = (bf16[64,2048]{1,0:T(8,128)(2,1)}, bf16[64,2048]{1,0:T(8,128)(2,1)}, u32[]{:S(2)}, u32[]{:S(2)}) collective-permute-start(bf16[64,2048]{1,0:T(8,128)(2,1)} %get-tuple-element.34), channel_id=1, source_target_pairs={{1,0},{2,1},{3,2},{5,4},{6,5},{7,6},{9,8},{10,9},{11,10},{13,12},{... | collective-permute-start | bytes 786440 | tf_op jit(solution)/shard_map/ppermute | solution.py:464
  18.2 4.3 %copy-start.2 = (bf16[1,128,2048]{2,1,0:T(8,128)(2,1)S(1)}, bf16[1,128,2048]{2,1,0:T(8,128)(2,1)}, u32[]{:S(2)}) copy-start(bf16[1,128,2048]{2,1,0:T(8,128)(2,1)} %refs_1_.1) | copy-start | bytes 1572868
  18.2 4.3 %copy-start.5 = (bf16[192,256]{1,0:T(8,128)(2,1)S(1)}, bf16[192,256]{1,0:T(8,128)(2,1)}, u32[]{:S(2)}) copy-start(bf16[192,256]{1,0:T(8,128)(2,1)} %constant.40.clone.go_table) | copy-start | bytes 294916
  27.0 9.7 %copy-start.28 = (bf16[1,2,31,2048]{3,2,1,0:T(8,128)(2,1)S(1)}, bf16[1,2,31,2048]{3,2,1,0:T(8,128)(2,1)}, u32[]{:S(2)}) copy-start(bf16[1,2,31,2048]{3,2,1,0:T(8,128)(2,1)} %copy-done.27) | copy-start | bytes 761860
  27.0 9.7 %copy-start.31 = (bf16[2,1,2048]{2,1,0:T(2,128)(2,1)S(1)}, bf16[2,1,2048]{2,1,0:T(2,128)(2,1)}, u32[]{:S(2)}) copy-start(bf16[2,1,2048]{2,1,0:T(2,128)(2,1)} %copy-done.30) | copy-start | bytes 24580
  27.0 16.1 %copy-start.7 = (bf16[2,32,192]{2,1,0:T(8,128)(2,1)S(1)}, bf16[2,32,192]{2,1,0:T(8,128)(2,1)}, u32[]{:S(2)}) copy-start(bf16[2,32,192]{2,1,0:T(8,128)(2,1)} %constant.43.clone.t_table) | copy-start | bytes 73732
  34.4 17.9 %copy-start.4 = (bf16[1,128,2048]{2,1,0:T(8,128)(2,1)S(1)}, bf16[1,128,2048]{2,1,0:T(8,128)(2,1)}, u32[]{:S(2)}) copy-start(bf16[1,128,2048]{2,1,0:T(8,128)(2,1)} %refs_2_.1) | copy-start | bytes 1572868
  34.4 17.9 %copy-start.19 = (s32[8]{0:T(128)S(1)}, s32[8]{0:T(128)}, u32[]{:S(2)}) copy-start(s32[8]{0:T(128)} %lengths.7) | copy-start | bytes 100
  34.4 29.7 %collective-permute-start.5 = (bf16[128,2048]{1,0:T(8,128)(2,1)}, bf16[128,2048]{1,0:T(8,128)(2,1)S(1)}, u32[]{:S(2)}, u32[]{:S(2)}) collective-permute-start(bf16[128,2048]{1,0:T(8,128)(2,1)} %get-tuple-element.31), channel_id=1, source_target_pairs={{0,28},{4,0},{8,4},{12,8},{16,12},{20,16},{24,20},{28,24},{1,29},{... | collective-permute-start | bytes 1572872 | tf_op jit(solution)/shard_map/ppermute | solution.py:438
  37.4 8.0 %collective-permute-start.11 = (bf16[32,2048]{1,0:T(8,128)(2,1)}, bf16[32,2048]{1,0:T(8,128)(2,1)}, u32[]{:S(2)}, u32[]{:S(2)}) collective-permute-start(bf16[32,2048]{1,0:T(8,128)(2,1)} %fusion.1), channel_id=1, source_target_pairs={{0,28},{4,0},{8,4},{12,8},{16,12},{20,16},{24,20},{28,24},{1,29},{... | collective-permute-start | bytes 393224 | tf_op jit(solution)/shard_map/ppermute | solution.py:438
  39.0 6.4 %copy-start.17 = (bf16[16,2048]{1,0:T(8,128)(2,1)S(1)}, bf16[16,2048]{1,0:T(8,128)(2,1)}, u32[]{:S(2)}) copy-start(bf16[16,2048]{1,0:T(8,128)(2,1)} %copy-done.16) | copy-start | bytes 196612
  39.0 13.3 %copy-start.21 = (bf16[2,160,192]{2,1,0:T(8,128)(2,1)S(1)}, bf16[2,160,192]{2,1,0:T(8,128)(2,1)}, u32[]{:S(2)}) copy-start(bf16[2,160,192]{2,1,0:T(8,128)(2,1)} %constant.39.clone.c_table.c0_table) | copy-start | bytes 368644
  39.0 13.3 %copy-start.22 = (bf16[2,160,160]{2,1,0:T(8,128)(2,1)S(1)}, bf16[2,160,160]{2,1,0:T(8,128)(2,1)}, u32[]{:S(2)}) copy-start(bf16[2,160,160]{2,1,0:T(8,128)(2,1)} %constant.44.clone.m1_table) | copy-start | bytes 307204
  39.0 13.3 %copy-start.23 = (bf16[2,128,160]{2,1,0:T(8,128)(2,1)S(1)}, bf16[2,128,160]{2,1,0:T(8,128)(2,1)}, u32[]{:S(2)}) copy-start(bf16[2,128,160]{2,1,0:T(8,128)(2,1)} %constant.46.clone.c1_table) | copy-start | bytes 245764
  39.0 13.3 %copy-start.25 = (bf16[192,64]{1,0:T(8,128)(2,1)S(1)}, bf16[192,64]{1,0:T(8,128)(2,1)}, u32[]{:S(2)}) copy-start(bf16[192,64]{1,0:T(8,128)(2,1)} %constant.38.clone.q_table.q0_table) | copy-start | bytes 73732
  39.0 13.3 %copy-start.26 = (bf16[160,64]{1,0:T(8,128)(2,1)S(1)}, bf16[160,64]{1,0:T(8,128)(2,1)}, u32[]{:S(2)}) copy-start(bf16[160,64]{1,0:T(8,128)(2,1)} %constant.45.clone.q1_table) | copy-start | bytes 61444
  39.0 25.2 %collective-permute-start.4 = (bf16[16,2048]{1,0:T(8,128)(2,1)}, bf16[16,2048]{1,0:T(8,128)(2,1)S(1)}, u32[]{:S(2)}, u32[]{:S(2)}) collective-permute-start(bf16[16,2048]{1,0:T(8,128)(2,1)} %copy-done.18), channel_id=1, source_target_pairs={{0,29},{1,30},{2,31},{4,1},{5,2},{6,3},{8,5},{9,6},{10,7},{12,9},{... | collective-permute-start | bytes 196616 | tf_op jit(solution)/shard_map/ppermute | solution.py:447
  45.4 18.8 %collective-permute-start.6 = (bf16[16,2048]{1,0:T(8,128)(2,1)S(1)}, bf16[16,2048]{1,0:T(8,128)(2,1)S(1)}, u32[]{:S(2)}, u32[]{:S(2)}) collective-permute-start(bf16[16,2048]{1,0:T(8,128)(2,1)S(1)} %copy-done.17), channel_id=1, source_target_pairs={{1,28},{2,29},{3,30},{5,0},{6,1},{7,2},{9,4},{10,5},{11,6},{13,8},... | collective-permute-start | bytes 196616 | tf_op jit(solution)/shard_map/ppermute | solution.py:447
  46.7 21.5 %collective-permute-start.2 = (bf16[32,2048]{1,0:T(8,128)(2,1)S(1)}, bf16[32,2048]{1,0:T(8,128)(2,1)S(1)}, u32[]{:S(2)}, u32[]{:S(2)}) collective-permute-start(bf16[32,2048]{1,0:T(8,128)(2,1)S(1)} %shard_map.212), channel_id=1, source_target_pairs={{0,1},{1,0},{2,3},{3,2},{4,5},{5,4},{6,7},{7,6},{8,9},{9,8},{10,11... | collective-permute-start | bytes 393224 | tf_op jit(solution)/shard_map/ppermute | solution.py:540
  59.6 17.1 %collective-permute-start.12 = (bf16[128,2048]{1,0:T(8,128)(2,1)S(1)}, bf16[128,2048]{1,0:T(8,128)(2,1)S(1)}, u32[]{:S(2)}, u32[]{:S(2)}) collective-permute-start(bf16[128,2048]{1,0:T(8,128)(2,1)S(1)} %shard_map.215), channel_id=1, source_target_pairs={{0,8},{4,12},{8,16},{12,20},{16,24},{20,28},{24,0},{28,4},{1,9},{5... | collective-permute-start | bytes 1572872 | tf_op jit(solution)/shard_map/ppermute | solution.py:438
  59.7 4.5 %copy-start.9 = (bf16[2,128,192]{2,1,0:T(8,128)(2,1)S(1)}, bf16[2,128,192]{2,1,0:T(8,128)(2,1)}, u32[]{:S(2)}) copy-start(bf16[2,128,192]{2,1,0:T(8,128)(2,1)} %constant.42.clone.x_table) | copy-start | bytes 294916
  68.1 5.0 %collective-permute-start.9 = (bf16[32,2048]{1,0:T(8,128)(2,1)S(1)}, bf16[32,2048]{1,0:T(8,128)(2,1)S(1)}, u32[]{:S(2)}, u32[]{:S(2)}) collective-permute-start(bf16[32,2048]{1,0:T(8,128)(2,1)S(1)} %get-tuple-element.40), channel_id=1, source_target_pairs={{0,1},{1,0},{2,3},{3,2},{4,5},{5,4},{6,7},{7,6},{8,9},{9,8},{10,11... | collective-permute-start | bytes 393224 | tf_op jit(solution)/shard_map/ppermute | solution.py:540
  68.2 8.5 %collective-permute-start.3 = (bf16[32,2048]{1,0:T(8,128)(2,1)S(1)}, bf16[32,2048]{1,0:T(8,128)(2,1)S(1)}, u32[]{:S(2)}, u32[]{:S(2)}) collective-permute-start(bf16[32,2048]{1,0:T(8,128)(2,1)S(1)} %add_convert_fusion.1.mine0), channel_id=1, source_target_pairs={{0,2},{1,3},{2,0},{3,1},{4,6},{5,7},{6,4},{7,5},{8,10},{9,11},{10,... | collective-permute-start | bytes 393224 | tf_op jit(solution)/shard_map/ppermute | solution.py:540
  72.0 7.6 %collective-permute-start.13 = (bf16[128,2048]{1,0:T(8,128)(2,1)S(1)}, bf16[128,2048]{1,0:T(8,128)(2,1)S(1)}, u32[]{:S(2)}, u32[]{:S(2)}) collective-permute-start(bf16[128,2048]{1,0:T(8,128)(2,1)S(1)} %get-tuple-element.41), channel_id=1, source_target_pairs={{0,28},{4,0},{8,4},{12,8},{16,12},{20,16},{24,20},{28,24},{1,29},{... | collective-permute-start | bytes 1572872 | tf_op jit(solution)/shard_map/ppermute | solution.py:438
  73.1 6.5 %collective-permute-start.10 = (bf16[32,2048]{1,0:T(8,128)(2,1)S(1)}, bf16[32,2048]{1,0:T(8,128)(2,1)S(1)}, u32[]{:S(2)}, u32[]{:S(2)}) collective-permute-start(bf16[32,2048]{1,0:T(8,128)(2,1)S(1)} %add_convert_fusion.mine1), channel_id=1, source_target_pairs={{0,2},{1,3},{2,0},{3,1},{4,6},{5,7},{6,4},{7,5},{8,10},{9,11},{10,... | collective-permute-start | bytes 393224 | tf_op jit(solution)/shard_map/ppermute | solution.py:540
  (17 other events, 32.3 us)

commit v3 on v2

--- a/solution.py
+++ b/solution.py
@@ -37,7 +37,7 @@
 
 
 def stacked(matrix):
-    return np.stack(split(matrix))
+    return np.concatenate(split(matrix), axis=0)
 
 
 def beside(matrix):
@@ -54,14 +54,8 @@
     return jnp.dot(a, b, preferred_element_type=F32)
 
 
-def forward_dft(table, values):
-    return dot(table[0], values) + dot(table[1], values)
-
-
-def inverse_dft(table, values):
-    high = values.astype(BF16)
-    low = (values - high.astype(F32)).astype(BF16)
-    return dot(table[0], high) + (dot(table[1], high) + dot(table[0], low))
+def transform(table, values):
+    return sum(halves(dot(table[...], values.astype(BF16))))
 
 
 def halves(values):
@@ -179,7 +173,7 @@
         return g_own, g_own + dot(self.gh_table[...], jnp.concatenate([ends, ends], axis=0))
 
     def rest(self, g_all, q, columns, scaled, sum_a, sum_b):
-        grad_masked = wide(self.mask_row, BLOCK) * inverse_dft(self.x_table, product_conj(g_all, q))
+        grad_masked = wide(self.mask_row, BLOCK) * transform(self.x_table, product_conj(g_all, q))
         centered = self.saved[:, columns].astype(F32) - wide(self.mean[...], BLOCK)
         weighted = grad_masked * (centered * wide(self.inverse[...], BLOCK))
         gain = self.gain(columns)
@@ -219,49 +213,75 @@
     return lambda columns: weights[slot, last : last + 1, columns].astype(F32)
 
 
+def prepare_kernel(
+    reach, lengths, slots, later_slots, kernels, gains, saved, q_table,
+    weights, later, masked, mean, inverse, q,
+):
+    own, width = saved.shape[1:]
+    count = kernels.shape[0]
+    for slot in range(kernels.shape[1]):
+        weights[slot, :count, :] = kernels[:, slot, :]
+        weights[slot, count:, :] = gains[slot : slot + 1, :]
+    section, sections, first = place(own)
+    later[...] = weights[later_slots[1, section]]
+    slot = slots[0, section]
+    gain = slot_row(weights, slot)
+    norm_pieces([(saved.at[0], 0, own)], gain, first, lengths[section], masked, mean, inverse)
+
+    def block(columns):
+        q[:, columns] = tap_spectrum(q_table[...], weights[slot, :, columns])
+
+    each_block(width, block)
+
+
+def joined(halo, own, columns):
+    reach = halo.shape[0] // 2
+    return jnp.concatenate([halo[:reach, columns], own[:, columns], halo[reach:, columns]], axis=0)
+
+
 def first_backward_kernel(
-    reach, lengths, slots, saved, left, right, grads, weights,
-    m_table, q_table, c_table, go_table, gh_table, x_table,
-    grad_x, top, bottom, masked, inner, gain_sum, mean, inverse, scaled, sum_a, sum_b,
+    reach, lengths, slots, saved, left, right, grads, weights, later, masked, mean, inverse, q,
+    m_table, c_table, go_table, gh_table, x_table,
+    grad_x, top, bottom, halo, inner, gain_sum, scaled, sum_a, sum_b,
 ):
-    own = saved.shape[0]
-    width = saved.shape[1]
+    own, width = saved.shape[1:]
     half = reach // 2
     section, sections, first = place(own)
-    slot, length = slots[section, 0], lengths[section]
+    slot, length = slots[0, section], lengths[section]
     gain = slot_row(weights, slot)
-    pieces = [(left, 0, reach), (saved, 0, own), (right, 0, reach)]
-    norm_pieces(pieces, gain, first - reach, length, masked, mean, inverse)
+    norm_pieces([(left, 0, reach)], gain, first - reach, length, halo)
+    norm_pieces([(right, 0, reach)], gain, first + own, length, halo.at[pl.ds(reach, reach)])
     grad_pieces = [(left, reach, half), (grads, 0, own), (right, reach, half)]
-    middle = pl.ds(reach, own)
     back = Back(
-        own, half, saved, mean.at[middle], inverse.at[middle], gain, own_mask(own, first, length),
-        go_table, gh_table, x_table,
+        own, half, saved.at[0], mean, inverse, gain, own_mask(own, first, length), go_table, gh_table, x_table
     )
     sum_a[...] = jnp.zeros_like(sum_a)
     sum_b[...] = jnp.zeros_like(sum_b)
 
     def block(columns):
-        q = tap_spectrum(q_table[...], weights[slot, :, columns])
-        m = forward_dft(m_table, masked[:, columns])
-        conv = inverse_dft(c_table, product(m, q))
+        m = transform(m_table, joined(halo, masked, columns))
+        conv = transform(c_table, product(m, q[:, columns]))
         mixed = back.mixed(grad_pieces, gate_factor(conv), columns)
         inner[:, columns] = mixed[half : half + own]
-        gain_sum[:, columns] = back.rest(back.spectra(mixed)[1], q, columns, scaled, sum_a, sum_b)
+        gain_sum[:, columns] = back.rest(back.spectra(mixed)[1], q[:, columns], columns, scaled, sum_a, sum_b)
 
     each_block(width, block)
     outs = [(grad_x, 0, own), (top, 0, half), (bottom, own - half, own)]
     back.finish(grads, 0, scaled, sum_a, sum_b, outs)
 
 
-def first_taps_kernel(masked, inner, gain_sum, m_table, go_table, t_table, taps):
+def first_taps_kernel(halo, masked, inner, gain_sum, m_table, go_table, t_table, taps):
     def block(columns):
-        m = forward_dft(m_table, masked[:, columns])
+        m = transform(m_table, joined(halo, masked, columns))
         mixed = inner[:, columns]
         g_own = dot(go_table[...], jnp.concatenate([mixed, mixed], axis=0))
-        put_taps(taps, inverse_dft(t_table, product_conj(m, g_own)), gain_sum[:, columns], columns)
+        put_taps(taps, transform(t_table, product_conj(m, g_own)), gain_sum[:, columns], columns)
 
     each_block(masked.shape[1], block)
+
+
+def add_kernel(mine, other, out):
+    out[...] = (mine[...].astype(F32) + other[...].astype(F32)).astype(out.dtype)
 
 
 def put_taps(taps, tap, gain_sum, columns):
@@ -269,42 +289,42 @@
     taps[:, columns] = jnp.where(row == tap.shape[0] - 1, gain_sum, tap).astype(taps.dtype)
 
 
-def prepare_kernel(
+def second_ready_kernel(
     reach, lengths, slots, saved, left, right, weights,
     m_table, q_table, c_table,
     m_out, q_out, factor_out, mean_out, inverse_out, masked, mean, inverse,
 ):
-    own, width = saved.shape
+    own, width = saved.shape[1:]
     section, sections, first = place(own)
-    slot, length = slots[section, 1], lengths[lax.rem(section + 1, sections)]
+    slot, length = slots[1, section], lengths[lax.rem(section + 1, sections)]
     gain = slot_row(weights, slot)
-    pieces = [(left, 0, reach), (saved, 0, own), (right, 0, reach)]
+    pieces = [(left, 0, reach), (saved.at[1], 0, own), (right, 0, reach)]
     norm_pieces(pieces, gain, first - reach, length, masked, mean, inverse)
     mean_out[...] = mean[pl.ds(reach, own), :]
     inverse_out[...] = inverse[pl.ds(reach, own), :]
 
     def block(columns):
         q = tap_spectrum(q_table[...], weights[slot, :, columns])
-        m = forward_dft(m_table, masked[:, columns])
+        m = transform(m_table, masked[:, columns])
         q_out[:, columns] = q
         m_out[:, columns] = m
-        factor_out[:, columns] = gate_factor(inverse_dft(c_table, product(m, q)))
+        factor_out[:, columns] = gate_factor(transform(c_table, product(m, q)))
 
     each_block(width, block)
 
 
 def second_backward_kernel(
-    lengths, slots, saved, left, grads, right, weights, m, q, factor, mean, inverse,
+    lengths, slots, saved, left, grads, right, weights, m, q, factor, mean, inverse, ready,
     go_table, gh_table, x_table, t_table,
     grad_x, taps, scaled, sum_a, sum_b,
 ):
-    own, width = saved.shape
+    own, width = saved.shape[1:]
     half = left.shape[0]
     section, sections, first = place(own)
-    slot, length = slots[section, 1], lengths[lax.rem(section + 1, sections)]
+    slot, length = slots[1, section], lengths[lax.rem(section + 1, sections)]
     pieces = [(left, 0, half), (grads, 0, own), (right, 0, half)]
     back = Back(
-        own, half, saved, mean, inverse, slot_row(weights, slot), own_mask(own, first, length),
+        own, half, saved.at[1], mean, inverse, slot_row(weights, slot), own_mask(own, first, length),
         go_table, gh_table, x_table,
     )
     sum_a[...] = jnp.zeros_like(sum_a)
@@ -313,7 +333,7 @@
     def block(columns):
         mixed = back.mixed(pieces, factor[:, columns], columns)
         g_own, g_all = back.spectra(mixed)
-        tap = inverse_dft(t_table, product_conj(m[:, columns], g_own))
+        tap = transform(t_table, product_conj(m[:, columns], g_own))
         gain_sum = back.rest(g_all, q[:, columns], columns, scaled, sum_a, sum_b)
         put_taps(taps, tap, gain_sum, columns)
 
@@ -329,7 +349,7 @@
     own, width = act.shape
     middle = reach // 2
     section, sections, first = place(own)
-    slot, length = slots[section, 0], lengths[section]
+    slot, length = slots[0, section], lengths[section]
     at = left.shape[0] - reach
     pieces = [(left, at, reach), (act, 0, own), (right, at, reach)]
     inner = [(left, at + middle, middle), (act, 0, own), (right, at, middle)]
@@ -337,7 +357,7 @@
 
     def first_layer(columns):
         q = tap_spectrum(q0_table[...], weights[slot, :, columns])
-        conv = inverse_dft(c0_table, product(forward_dft(m0_table, masked0[:, columns]), q))
+        conv = transform(c0_table, product(transform(m0_table, masked0[:, columns]), q))
         between[:, columns] = (window(inner, columns).astype(F32) + conv * sigmoid(conv)).astype(BF16)
 
     each_block(width, first_layer)
@@ -346,7 +366,7 @@
 
     def second_layer(columns):
         q = tap_spectrum(q1_table[...], later[:, columns])
-        conv = inverse_dft(c1_table, product(forward_dft(m1_table, masked1[:, columns]), q))
+        conv = transform(c1_table, product(transform(m1_table, masked1[:, columns]), q))
         here = between[middle : middle + own, columns].astype(F32)
         out[:, columns] = (here + conv * sigmoid(conv)).astype(BF16)
 
@@ -377,8 +397,8 @@
     total0 = mine0[...].astype(F32) + other0[...].astype(F32)
     total1 = mine1[...].astype(F32) + other1[...].astype(F32)
     for slot in range(taps.shape[1]):
-        use0 = (slots[section, 0] == slot).astype(F32)
-        use1 = (slots[section, 1] == slot).astype(F32)
+        use0 = (slots[0, section] == slot).astype(F32)
+        use1 = (slots[1, section] == slot).astype(F32)
         total = use0 * total0 + use1 * total1
         taps[:, slot, :] = total[:count]
         gains[slot : slot + 1, :] = total[count:]
@@ -393,10 +413,12 @@
 VMEM = pl.BlockSpec(memory_space=pltpu.VMEM)
 SMEM = pl.BlockSpec(memory_space=pltpu.SMEM)
 ANY = pl.BlockSpec(memory_space=pl.ANY)
+HBM = pl.BlockSpec(memory_space=pltpu.HBM)
 LIMIT = 24 * 1024 * 1024
-
-
-def call(kernel, outs, scratch, operands, flops, specs=None, out_specs=None):
+FULL = 127 * 512 * 1024
+
+
+def call(kernel, outs, scratch, operands, flops, specs=None, out_specs=None, limit=LIMIT):
     moved = sum(int(np.prod(x.shape)) * x.dtype.itemsize for x in operands)
     if specs is None:
         specs = [SMEM if x.dtype == jnp.int32 else VMEM for x in operands]
@@ -406,7 +428,7 @@
         in_specs=specs,
         out_specs=jax.tree.map(lambda _: VMEM, outs) if out_specs is None else out_specs,
         scratch_shapes=scratch,
-        compiler_params=pltpu.CompilerParams(vmem_limit_bytes=LIMIT),
+        compiler_params=pltpu.CompilerParams(vmem_limit_bytes=limit),
         cost_estimate=pl.CostEstimate(flops=flops, bytes_accessed=moved, transcendentals=0),
     )(*operands)
 
@@ -425,7 +447,6 @@
 ):
     sections = lax.axis_size("section")
     shards = lax.axis_size("tm")
-    section = lax.axis_index("section")
     act, grad, saved = act_in[0], grad_in[0], saved_inputs[0]
     own, width = act.shape
     tap_count = kernels.shape[2]
@@ -456,15 +477,12 @@
         tuple(like(n, width, BF16) for n in (two + one, two + one, 2 * two, 2 * two)),
         [pltpu.SemaphoreType.DMA((len(plan),))],
         (saved, grad_in, act_in),
-        0, [ANY] * 3, (ANY,) * 4,
+        0, [HBM] * 3, (ANY,) * 4, FULL,
     )
     up = [(i, i + 1) for i in range(shards - 1)]
     down = [(i + 1, i) for i in range(shards - 1)]
     left0, right0 = lax.ppermute(tail0, "tm", up), lax.ppermute(head0, "tm", down)
     left1, right1 = lax.ppermute(tail1, "tm", up), lax.ppermute(head1, "tm", down)
-    weights = jnp.concatenate([kernels[0], norm_gains[0][:, None, :]], axis=1)
-    later = shifted(lax.dynamic_index_in_dim(weights, forward_slots[section, 1], 0, keepdims=False), -1)
-
     ends = np.concatenate([np.arange(-one, 0), np.arange(own, own + one)])
     tap_back = np.concatenate([from_freq(size, np.arange(tap_count) - half), np.zeros((1, size))], axis=0)
     m_table = stacked(to_freq(size, span(two, own)))
@@ -481,16 +499,31 @@
 
     rows = [pltpu.VMEM((own, width), F32)] + [pltpu.VMEM((own, LANES), F32)] * 2
     stats = [pltpu.VMEM((size, LANES), F32)] * 2
-    grad_mid, top, bottom, masked0, inner0, gain0 = run(
+    forward_slots, backward_slots = forward_slots.T, backward_slots.T
+    weights, later, masked0, mean0, inverse0, q0 = run(
+        functools.partial(prepare_kernel, two),
+        (
+            jax.ShapeDtypeStruct((kernels.shape[1], tap_count + 1, width), BF16), like(tap_count + 1, width, BF16),
+            like(own, width, BF16), like(own, LANES, F32), like(own, LANES, F32), like(size, width, F32),
+        ),
+        [],
+        [
+            backward_lengths, backward_slots, forward_slots,
+            kernels[0].transpose(1, 0, 2), norm_gains[0], saved, q_table,
+        ],
+        work,
+    )
+    later = shifted(later, -1)
+    grad_mid, top, bottom, halo0, inner0, gain0 = run(
         functools.partial(first_backward_kernel, two),
         (
             like(own, width, BF16), like(one, width, BF16), like(one, width, BF16),
-            like(size, width, BF16), like(own, width, BF16), like(1, width, F32),
+            like(2 * two, width, BF16), like(own, width, BF16), like(1, width, F32),
         ),
-        stats + rows,
+        rows,
         [
-            backward_lengths, backward_slots, saved[0], left0, right0, grad, weights,
-            m_table, q_table, c_table, go_table, gh_table, x_table,
+            backward_lengths, backward_slots, saved, left0, right0, grad, weights, later, masked0, mean0, inverse0, q0,
+            m_table, c_table, go_table, gh_table, x_table,
         ],
         9 * work,
     )
@@ -499,7 +532,7 @@
     grad_mid = shifted(grad_mid, -1)
     taps0 = run(
         first_taps_kernel, like(tap_count + 1, width, BF16), [],
-        [masked0, inner0, gain0, m_table, go_table, t_table], 3 * work,
+        [halo0, masked0, inner0, gain0, m_table, go_table, t_table], 3 * work,
     )
     act_out = run(
         functools.partial(forward_kernel, two),
@@ -514,26 +547,15 @@
     )
     act_out = shifted(act_out, 2)
     prepared = run(
-        functools.partial(prepare_kernel, two),
+        functools.partial(second_ready_kernel, two),
         (
             like(size, width, F32), like(size, width, F32), like(small, width, F32),
             like(own, LANES, F32), like(own, LANES, F32),
         ),
         [pltpu.VMEM((size, width), BF16)] + stats,
-        [backward_lengths, backward_slots, saved[1], left1, right1, weights, m_table, q_table, c_table],
+        [backward_lengths, backward_slots, saved, left1, right1, weights, m_table, q_table, c_table],
         6 * work,
     )
-    grad_out, taps1 = run(
-        second_backward_kernel,
-        (like(own, width, BF16), like(tap_count + 1, width, BF16)),
-        rows,
-        [
-            backward_lengths, backward_slots, saved[1], mid_left, grad_mid, mid_right, weights, *prepared,
-            go_table, gh_table, x_table, t_table,
-        ],
-        6 * work,
-    )
-
     def summed(x):
         step = 1
         while True:
@@ -541,10 +563,22 @@
             step *= 2
             if step >= shards:
                 return x, other
-            x = (x.astype(F32) + other.astype(F32)).astype(BF16)
+            x = call(add_kernel, like(*x.shape, BF16), [], (x, other), 0)
+
+    mine0, other0 = summed(taps0)
+    grad_out, taps1 = run(
+        second_backward_kernel,
+        (like(own, width, BF16), like(tap_count + 1, width, BF16)),
+        rows,
+        [
+            backward_lengths, backward_slots, saved, mid_left, grad_mid, mid_right, weights, *prepared, mine0,
+            go_table, gh_table, x_table, t_table,
+        ],
+        6 * work,
+    )
 
     grad_out = shifted(grad_out, -1)
-    sums = summed(taps0) + summed(taps1)
+    sums = (mine0, other0) + summed(taps1)
     slots = kernels.shape[1]
     act_out, grad_out, taps, gains = call(
         final_kernel,

time: 82.7 us -> 105 us (1.27)
  Pallas kernels: 28.8 us -> 54.5 us
  waiting for transfers between devices: 4.04 us -> 10.4 us
  local copies, waits for them, and re-layouts: 10.2 us -> 4.79 us
  between operations: 3.03 us -> 1.05 us
  starting transfers between devices: 35.1 us -> 33.3 us
    pallas_call x7 -> x10, Pallas kernels: 28.8 us -> 54.5 us  [call(): pl.pallas_call(kernel, out_shape=outs, in_specs=specs, out_specs=jax.tree...]
    ppermute x4, starting transfers between devices: 13.1 us -> 6.78 us  [summed(): other = lax.ppermute(x, 'tm', [(i, i ^ step) for i in range(shards)])]
    ppermute x4, starting transfers between devices: 3.83 us -> 9.3 us  [shifted(): lax.ppermute(x, 'section', [(i, (i + by) % sections) for i in range(secti...]
    unnamed x73 -> x50, local copies, waits for them, and re-layouts: 9.49 us -> 4.79 us
    ppermute x4, waiting for transfers between devices: 4 us -> 6.55 us  [summed(): other = lax.ppermute(x, 'tm', [(i, i ^ step) for i in range(shards)])]
    ppermute x4, waiting for transfers between devices: 0.03 us -> 2.53 us  [shifted(): lax.ppermute(x, 'section', [(i, (i + by) % sections) for i in range(secti...]
    ppermute x1, waiting for transfers between devices: 0.01 us -> 1.31 us  [local(): lax.ppermute(head1, 'tm', down)]
  transfers between devices with their start and end apart: 14 -> 14, of which waited for: 2 -> 4; matrix products, arithmetic and copies ran while one was open for 2% -> 0% of each run, Pallas kernels for 31% -> 17%
where the time goes in v3:
time: 105 us; the launch traced here: 104 us
  Pallas kernels  54.5 us (52%)
  starting transfers between devices  33.3 us (32%)
  waiting for transfers between devices  10.4 us (10%)
  local copies, waits for them, and re-layouts  4.79 us (5%)
  between operations  1.05 us (1%)
    pallas_call x10, Pallas kernels, call(): pl.pallas_call(kernel, out_shape=outs, in_specs=specs, out_specs=jax.tree...  54.5 us
    ppermute x4, starting transfers between devices, shifted(): lax.ppermute(x, 'section', [(i, (i + by) % sections) for i in range(secti...  9.3 us
    ppermute x4, starting transfers between devices, summed(): other = lax.ppermute(x, 'tm', [(i, i ^ step) for i in range(shards)])  6.78 us
    ppermute x4, waiting for transfers between devices, summed(): other = lax.ppermute(x, 'tm', [(i, i ^ step) for i in range(shards)])  6.55 us
    ppermute x2, starting transfers between devices, to_neighbour(): return lax.ppermute(x, ('section', 'tm'), pairs)  5.51 us
    ppermute x1, starting transfers between devices, local(): lax.ppermute(tail0, 'tm', up)  4.85 us
    unnamed x50, local copies, waits for them, and re-layouts  4.79 us
    ppermute x1, starting transfers between devices, local(): lax.ppermute(tail1, 'tm', up)  4.26 us
  transfers between devices with their start and end apart: 14, of which 4 were waited for; matrix products, arithmetic and copies ran while one was open for 0% of the time, Pallas kernels for 17%

profile of v3, /device:TPU:0, one launch (start us, length us, event | category | flops | bytes accessed | tf_op | source)
XLA Modules:
  0.0 104.0 jit_solution(5705462617424283315)
XLA Ops:
  0.7 0.0 copy-start.3
  0.7 29.0 %shard_map.210 = (bf16[48,2048]{1,0:T(8,128)(2,1)}, bf16[48,2048]{1,0:T(8,128)(2,1)}, bf16[64,2048]{1,0:T(8,128)(2,1)}, bf16[64,2048]{1,0:T(8,128)(2,1)}) custom-call(bf16[2,128,2048]{2,1,0:T(8,128)(2,1)} %bitcast.15, bf16[1,128,2048]{2,1,0:T(8,128)(2,1)} %refs_1_.1, bf16[1,128,2048]{2,1,0:T(8,128)(2,1)} %refs_2_.1), custom_call_target="tpu_custom_call" | custom-call | bytes 2097152 | tf_op jit(solution)/shard_map/pallas_call | solution.py:425
  29.7 4.9 %collective-permute-start = (bf16[48,2048]{1,0:T(8,128)(2,1)}, bf16[48,2048]{1,0:T(8,128)(2,1)S(1)}, u32[]{:S(2)}, u32[]{:S(2)}) collective-permute-start(bf16[48,2048]{1,0:T(8,128)(2,1)} %get-tuple-element.31), channel_id=1, source_target_pairs={{0,1},{1,2},{2,3},{4,5},{5,6},{6,7},{8,9},{9,10},{10,11},{12,13},{... | collective-permute-start | bytes 589832 | tf_op jit(solution)/shard_map/ppermute | solution.py:484
  34.5 1.3 %collective-permute-start.1 = (bf16[48,2048]{1,0:T(8,128)(2,1)}, bf16[48,2048]{1,0:T(8,128)(2,1)S(1)}, u32[]{:S(2)}, u32[]{:S(2)}) collective-permute-start(bf16[48,2048]{1,0:T(8,128)(2,1)} %get-tuple-element.32), channel_id=1, source_target_pairs={{1,0},{2,1},{3,2},{5,4},{6,5},{7,6},{9,8},{10,9},{11,10},{13,12},{... | collective-permute-start | bytes 589832 | tf_op jit(solution)/shard_map/ppermute | solution.py:484
  35.9 1.2 %copy-done = bf16[1,2,128,2048]{3,2,1,0:T(8,128)(2,1)S(1)} copy-done((bf16[1,2,128,2048]{3,2,1,0:T(8,128)(2,1)S(1)}, bf16[1,2,128,2048]{3,2,1,0:T(8,128)(2,1)}, u32[]{:S(2)}) %copy-start) | copy-done | bytes 1048600
  37.1 0.9 copy-done.7
  38.1 0.8 copy-done.13
  38.9 2.4 %shard_map.211 = (bf16[2,32,2048]{2,1,0:T(8,128)(2,1)S(1)}, bf16[32,2048]{1,0:T(8,128)(2,1)S(1)}, bf16[128,2048]{1,0:T(8,128)(2,1)S(1)}, f32[128,128]{1,0:T(8,12...) custom-call(s32[8]{0:T(128)S(1)} %copy-done.17, s32[2,8]{1,0:T(2,128)S(1)} %bitcast.23, s32[2,8]{1,0:T(2,128)S(1)} %bitcast.29, ...), custom_call_target="tpu_custom_call" | custom-call | flops 150994944 | bytes 1335456 | tf_op jit(solution)/shard_map/pallas_call | solution.py:425
  41.2 2.8 %collective-permute-start.2 = (bf16[32,2048]{1,0:T(8,128)(2,1)S(1)}, bf16[32,2048]{1,0:T(8,128)(2,1)S(1)}, u32[]{:S(2)}, u32[]{:S(2)}) collective-permute-start(bf16[32,2048]{1,0:T(8,128)(2,1)S(1)} %get-tuple-element.34), channel_id=1, source_target_pairs={{0,28},{4,0},{8,4},{12,8},{16,12},{20,16},{24,20},{28,24},{1,29},{... | collective-permute-start | bytes 393224 | tf_op jit(solution)/shard_map/ppermute | solution.py:459
  44.0 2.5 %collective-permute-done.2.later = bf16[32,2048]{1,0:T(8,128)(2,1)S(1)} collective-permute-done((bf16[32,2048]{1,0:T(8,128)(2,1)S(1)}, bf16[32,2048]{1,0:T(8,128)(2,1)S(1)}, u32[]{:S(2)}, u32[]{:S(2)}) %collective-permute-start.2) | collective-permute-done | bytes 131104 | tf_op jit(solution)/shard_map/ppermute | solution.py:459
  46.6 0.8 copy-done.8
  47.4 0.9 copy-done.10
  48.3 5.6 %shard_map.212 = (bf16[128,2048]{1,0:T(8,128)(2,1)S(1)}, bf16[16,2048]{1,0:T(8,128)(2,1)S(1)}, bf16[16,2048]{1,0:T(8,128)(2,1)S(1)}, bf16[64,2048]{1,0:T(8,128)(...) custom-call(s32[8]{0:T(128)S(1)} %copy-done.17, s32[2,8]{1,0:T(2,128)S(1)} %bitcast.24, ...), custom_call_target="tpu_custom_call" | custom-call | flops 1358954496 | bytes 5079136 | tf_op jit(solution)/shard_map/pallas_call | solution.py:425
  54.0 3.7 %collective-permute-start.6 = (bf16[128,2048]{1,0:T(8,128)(2,1)S(1)}, bf16[128,2048]{1,0:T(8,128)(2,1)S(1)}, u32[]{:S(2)}, u32[]{:S(2)}) collective-permute-start(bf16[128,2048]{1,0:T(8,128)(2,1)S(1)} %get-tuple-element.43), channel_id=1, source_target_pairs={{0,28},{4,0},{8,4},{12,8},{16,12},{20,16},{24,20},{28,24},{1,29},{... | collective-permute-start | bytes 1572872 | tf_op jit(solution)/shard_map/ppermute | solution.py:459
  57.8 4.3 %collective-permute-start.8 = (bf16[64,2048]{1,0:T(8,128)(2,1)S(1)}, bf16[64,2048]{1,0:T(8,128)(2,1)S(1)}, u32[]{:S(2)}, u32[]{:S(2)}) collective-permute-start(bf16[64,2048]{1,0:T(8,128)(2,1)S(1)} %copy-done.24), channel_id=1, source_target_pairs={{0,1},{1,2},{2,3},{4,5},{5,6},{6,7},{8,9},{9,10},{10,11},{12,13},{... | collective-permute-start | bytes 786440 | tf_op jit(solution)/shard_map/ppermute | solution.py:485
  62.0 1.3 %collective-permute-start.9 = (bf16[64,2048]{1,0:T(8,128)(2,1)S(1)}, bf16[64,2048]{1,0:T(8,128)(2,1)S(1)}, u32[]{:S(2)}, u32[]{:S(2)}) collective-permute-start(bf16[64,2048]{1,0:T(8,128)(2,1)S(1)} %copy-done.23), channel_id=1, source_target_pairs={{1,0},{2,1},{3,2},{5,4},{6,5},{7,6},{9,8},{10,9},{11,10},{13,12},{... | collective-permute-start | bytes 786440 | tf_op jit(solution)/shard_map/ppermute | solution.py:485
  63.3 4.2 %collective-permute-start.5 = (bf16[16,2048]{1,0:T(8,128)(2,1)S(1)}, bf16[16,2048]{1,0:T(8,128)(2,1)S(1)}, u32[]{:S(2)}, u32[]{:S(2)}) collective-permute-start(bf16[16,2048]{1,0:T(8,128)(2,1)S(1)} %get-tuple-element.42), channel_id=1, source_target_pairs={{0,29},{1,30},{2,31},{4,1},{5,2},{6,3},{8,5},{9,6},{10,7},{12,9},{... | collective-permute-start | bytes 196616 | tf_op jit(solution)/shard_map/ppermute | solution.py:468
  67.6 1.3 %collective-permute-start.7 = (bf16[16,2048]{1,0:T(8,128)(2,1)S(1)}, bf16[16,2048]{1,0:T(8,128)(2,1)S(1)}, u32[]{:S(2)}, u32[]{:S(2)}) collective-permute-start(bf16[16,2048]{1,0:T(8,128)(2,1)S(1)} %get-tuple-element.44), channel_id=1, source_target_pairs={{1,28},{2,29},{3,30},{5,0},{6,1},{7,2},{9,4},{10,5},{11,6},{13,8},... | collective-permute-start | bytes 196616 | tf_op jit(solution)/shard_map/ppermute | solution.py:468
  68.9 1.9 %shard_map.213.mine = bf16[32,2048]{1,0:T(8,128)(2,1)S(1)} custom-call(bf16[64,2048]{1,0:T(8,128)(2,1)S(1)} %get-tuple-element.39.halo, bf16[128,2048]{1,0:T(8,128)(2,1)S(1)} %get-tuple-element.35.masked, bf16[128,2048]{1,0:T(8,128)(2,1)S(1)} %get-tuple-element.40.inner, f32[1,2048]{1,0:T(1,128)S(1)} %get-tuple-element.41.gain_sum, ...), custom_call_target="tpu_custom_call" | custom-call | flops 452984832 | bytes 1589248 | tf_op jit(solution)/shard_map/pallas_call | solution.py:425
  70.8 3.3 %collective-permute-start.3 = (bf16[32,2048]{1,0:T(8,128)(2,1)S(1)}, bf16[32,2048]{1,0:T(8,128)(2,1)S(1)}, u32[]{:S(2)}, u32[]{:S(2)}) collective-permute-start(bf16[32,2048]{1,0:T(8,128)(2,1)S(1)} %shard_map.213.mine), channel_id=1, source_target_pairs={{0,1},{1,0},{2,3},{3,2},{4,5},{5,4},{6,7},{7,6},{8,9},{9,8},{10,11... | collective-permute-start | bytes 393224 | tf_op jit(solution)/shard_map/ppermute | solution.py:562
  74.1 1.3 %collective-permute-done.9.right = bf16[64,2048]{1,0:T(8,128)(2,1)S(1)} collective-permute-done((bf16[64,2048]{1,0:T(8,128)(2,1)S(1)}, bf16[64,2048]{1,0:T(8,128)(2,1)S(1)}, u32[]{:S(2)}, u32[]{:S(2)}) %collective-permute-start.9) | collective-permute-done | bytes 262176 | tf_op jit(solution)/shard_map/ppermute | solution.py:485
  75.5 6.2 %shard_map.218 = bf16[128,2048]{1,0:T(8,128)(2,1)S(1)} custom-call(s32[8]{0:T(128)S(1)} %copy-done.19, s32[2,8]{1,0:T(2,128)S(1)} %bitcast.30, bf16[128,2048]{1,0:T(8,128)(2,1)S(1)} %bitcast.21, bf16[64,2048]{1,0:T(8,128)(2,1)S(1)} %collective-permute-done.8.left, bf16[64,2048]{1,0:T(8,128)(2,1)S(1)} %collective-permute-done.9.right, ...), custom_call_target="tpu_custom_call" | custom-call | flops 1509949440 | bytes 1941600 | tf_op jit(solution)/shard_map/pallas_call | solution.py:425
  81.8 0.5 collective-permute-start.12
  82.2 3.6 %shard_map.215 = (f32[192,2048]{1,0:T(8,128)S(1)}, f32[192,2048]{1,0:T(8,128)S(1)}, f32[160,2048]{1,0:T(8,128)S(1)}, f32[128,128]{1,0:T(8,128)S(1)}, f32[128,128]{1,0:T(8,128)S(1)}) custom-call(s32[8]{0:T(128)S(1)} %copy-done.17, s32[2,8]{1,0:T(2,128)S(1)} %bitcast.25, bf16[2,128,2048]{2,1,0:T(8,128)(2,1)S(1)} %bitcast.18, ...), custom_call_target="tpu_custom_call" | custom-call | flops 905969664 | bytes 2130016 | tf_op jit(solution)/shard_map/pallas_call | solution.py:425
  86.0 3.4 %shard_map.216 = (bf16[128,2048]{1,0:T(8,128)(2,1)S(1)}, bf16[32,2048]{1,0:T(8,128)(2,1)S(1)}) custom-call(s32[8]{0:T(128)S(1)} %copy-done.17, s32[2,8]{1,0:T(2,128)S(1)} %bitcast.26, bf16[2,128,2048]{2,1,0:T(8,128)(2,1)S(1)} %bitcast.19, bf16[16,2048]{1,0:T(8,128)(2,1)S(1)} %collective-permute-done.5.left, ...), custom_call_target="tpu_custom_call" | custom-call | flops 905969664 | bytes 6930528 | tf_op jit(solution)/shard_map/pallas_call | solution.py:425
  89.4 2.3 %collective-permute-start.13 = (bf16[128,2048]{1,0:T(8,128)(2,1)S(1)}, bf16[128,2048]{1,0:T(8,128)(2,1)S(1)}, u32[]{:S(2)}, u32[]{:S(2)}) collective-permute-start(bf16[128,2048]{1,0:T(8,128)(2,1)S(1)} %get-tuple-element.53), channel_id=1, source_target_pairs={{0,28},{4,0},{8,4},{12,8},{16,12},{20,16},{24,20},{28,24},{1,29},{... | collective-permute-start | bytes 1572872 | tf_op jit(solution)/shard_map/ppermute | solution.py:459
  91.7 0.3 collective-permute-start.10
  92.0 2.2 %collective-permute-start.4 = (bf16[32,2048]{1,0:T(8,128)(2,1)S(1)}, bf16[32,2048]{1,0:T(8,128)(2,1)S(1)}, u32[]{:S(2)}, u32[]{:S(2)}) collective-permute-start(bf16[32,2048]{1,0:T(8,128)(2,1)S(1)} %shard_map.214.ready.mine0), channel_id=1, source_target_pairs={{0,2},{1,3},{2,0},{3,1},{4,6},{5,7},{6,4},{7,5},{8,10},{9,11},{10,... | collective-permute-start | bytes 393224 | tf_op jit(solution)/shard_map/ppermute | solution.py:562
  94.2 2.5 %collective-permute-done.10.other = bf16[32,2048]{1,0:T(8,128)(2,1)S(1)} collective-permute-done((bf16[32,2048]{1,0:T(8,128)(2,1)S(1)}, bf16[32,2048]{1,0:T(8,128)(2,1)S(1)}, u32[]{:S(2)}, u32[]{:S(2)}) %collective-permute-start.10) | collective-permute-done | bytes 131104 | tf_op jit(solution)/shard_map/ppermute | solution.py:562
  96.7 0.9 collective-permute-start.11
  97.6 4.1 %collective-permute-done.11.other1 = bf16[32,2048]{1,0:T(8,128)(2,1)S(1)} collective-permute-done((bf16[32,2048]{1,0:T(8,128)(2,1)S(1)}, bf16[32,2048]{1,0:T(8,128)(2,1)S(1)}, u32[]{:S(2)}, u32[]{:S(2)}) %collective-permute-start.11) | collective-permute-done | bytes 131104 | tf_op jit(solution)/shard_map/ppermute | solution.py:562
  101.7 2.3 %shard_map.219 = (bf16[128,2048]{1,0:T(8,128)(2,1)}, bf16[128,2048]{1,0:T(8,128)(2,1)}, f32[31,2,2048]{2,1,0:T(2,128)}, f32[2,2048]{1,0:T(2,128)}) custom-call(s32[2,8]{1,0:T(2,128)S(1)} %bitcast.27, bf16[32,2048]{1,0:T(8,128)(2,1)S(1)} %shard_map.214.ready.mine0, bf16[32,2048]{1,0:T(8,128)(2,1)S(1)} %collective-permute-done.4.other0, ...), custom_call_target="tpu_custom_call" | custom-call | bytes 1572928 | tf_op jit(solution)/shard_map/pallas_call | solution.py:425
  (56 shorter events, 0.2 us)
Async XLA Ops:
  0.6 35.2 %copy-start.17 = (s32[8]{0:T(128)S(1)}, s32[8]{0:T(128)}, u32[]{:S(2)}) copy-start(s32[8]{0:T(128)} %lengths.8) | copy-start | bytes 100
  0.6 35.2 %copy-start.15 = (s32[8,2]{0,1:T(2,128)S(1)}, s32[8,2]{0,1:T(2,128)}, u32[]{:S(2)}) copy-start(s32[8,2]{0,1:T(2,128)} %param.27) | copy-start | bytes 196
  0.7 35.2 %copy-start.18 = (s32[8,2]{0,1:T(2,128)S(1)}, s32[8,2]{0,1:T(2,128)}, u32[]{:S(2)}) copy-start(s32[8,2]{0,1:T(2,128)} %param.26) | copy-start | bytes 196
  0.7 35.2 %copy-start.16 = (bf16[1,2,2048]{2,1,0:T(2,128)(2,1)S(1)}, bf16[1,2,2048]{2,1,0:T(2,128)(2,1)}, u32[]{:S(2)}) copy-start(bf16[1,2,2048]{2,1,0:T(2,128)(2,1)} %param.23) | copy-start | bytes 24580
  0.7 45.9 %copy-start.3 = (bf16[192,256]{1,0:T(8,128)(2,1)S(1)}, bf16[192,256]{1,0:T(8,128)(2,1)}, u32[]{:S(2)}) copy-start(bf16[192,256]{1,0:T(8,128)(2,1)} %constant.23.clone.go_table) | copy-start | bytes 294916
  0.7 45.9 %copy-start.4 = (bf16[384,192]{1,0:T(8,128)(2,1)S(1)}, bf16[384,192]{1,0:T(8,128)(2,1)}, u32[]{:S(2)}) copy-start(bf16[384,192]{1,0:T(8,128)(2,1)} %constant.21.clone.m_table.m0_table) | copy-start | bytes 442372
  0.7 45.9 %copy-start.5 = (bf16[256,192]{1,0:T(8,128)(2,1)S(1)}, bf16[256,192]{1,0:T(8,128)(2,1)}, u32[]{:S(2)}) copy-start(bf16[256,192]{1,0:T(8,128)(2,1)} %constant.25.clone.x_table) | copy-start | bytes 294916
  29.7 16.9 %collective-permute-start = (bf16[48,2048]{1,0:T(8,128)(2,1)}, bf16[48,2048]{1,0:T(8,128)(2,1)S(1)}, u32[]{:S(2)}, u32[]{:S(2)}) collective-permute-start(bf16[48,2048]{1,0:T(8,128)(2,1)} %get-tuple-element.31), channel_id=1, source_target_pairs={{0,1},{1,2},{2,3},{4,5},{5,6},{6,7},{8,9},{9,10},{10,11},{12,13},{... | collective-permute-start | bytes 589832 | tf_op jit(solution)/shard_map/ppermute | solution.py:484
  34.5 12.0 %collective-permute-start.1 = (bf16[48,2048]{1,0:T(8,128)(2,1)}, bf16[48,2048]{1,0:T(8,128)(2,1)S(1)}, u32[]{:S(2)}, u32[]{:S(2)}) collective-permute-start(bf16[48,2048]{1,0:T(8,128)(2,1)} %get-tuple-element.32), channel_id=1, source_target_pairs={{1,0},{2,1},{3,2},{5,4},{6,5},{7,6},{9,8},{10,9},{11,10},{13,12},{... | collective-permute-start | bytes 589832 | tf_op jit(solution)/shard_map/ppermute | solution.py:484
  38.9 7.7 %copy-start.2 = (bf16[1,128,2048]{2,1,0:T(8,128)(2,1)S(1)}, bf16[1,128,2048]{2,1,0:T(8,128)(2,1)}, u32[]{:S(2)}) copy-start(bf16[1,128,2048]{2,1,0:T(8,128)(2,1)} %refs_1_.1) | copy-start | bytes 1572868
  41.2 5.3 %collective-permute-start.2 = (bf16[32,2048]{1,0:T(8,128)(2,1)S(1)}, bf16[32,2048]{1,0:T(8,128)(2,1)S(1)}, u32[]{:S(2)}, u32[]{:S(2)}) collective-permute-start(bf16[32,2048]{1,0:T(8,128)(2,1)S(1)} %get-tuple-element.34), channel_id=1, source_target_pairs={{0,28},{4,0},{8,4},{12,8},{16,12},{20,16},{24,20},{28,24},{1,29},{... | collective-permute-start | bytes 393224 | tf_op jit(solution)/shard_map/ppermute | solution.py:459
  48.3 9.4 %copy-start.24 = (bf16[64,2048]{1,0:T(8,128)(2,1)S(1)}, bf16[64,2048]{1,0:T(8,128)(2,1)}, u32[]{:S(2)}) copy-start(bf16[64,2048]{1,0:T(8,128)(2,1)} %get-tuple-element.45) | copy-start | bytes 786436
  48.3 13.7 %copy-start.23 = (bf16[64,2048]{1,0:T(8,128)(2,1)S(1)}, bf16[64,2048]{1,0:T(8,128)(2,1)}, u32[]{:S(2)}) copy-start(bf16[64,2048]{1,0:T(8,128)(2,1)} %get-tuple-element.46) | copy-start | bytes 786436
  48.3 20.5 %copy-start.12 = (bf16[64,192]{1,0:T(8,128)(2,1)S(1)}, bf16[64,192]{1,0:T(8,128)(2,1)}, u32[]{:S(2)}) copy-start(bf16[64,192]{1,0:T(8,128)(2,1)} %constant.26.clone.t_table) | copy-start | bytes 73732
  53.9 21.5 %copy-start.6 = (bf16[1,128,2048]{2,1,0:T(8,128)(2,1)S(1)}, bf16[1,128,2048]{2,1,0:T(8,128)(2,1)}, u32[]{:S(2)}) copy-start(bf16[1,128,2048]{2,1,0:T(8,128)(2,1)} %refs_2_.1) | copy-start | bytes 1572868
  54.0 21.5 %copy-start.14 = (bf16[192,64]{1,0:T(8,128)(2,1)S(1)}, bf16[192,64]{1,0:T(8,128)(2,1)}, u32[]{:S(2)}) copy-start(bf16[192,64]{1,0:T(8,128)(2,1)} %constant.20.clone.q_table.q0_table) | copy-start | bytes 73732
  54.0 21.5 %copy-start.19 = (s32[8]{0:T(128)S(1)}, s32[8]{0:T(128)}, u32[]{:S(2)}) copy-start(s32[8]{0:T(128)} %lengths.9) | copy-start | bytes 100
  54.0 21.5 %copy-start.20 = (bf16[320,160]{1,0:T(8,128)(2,1)S(1)}, bf16[320,160]{1,0:T(8,128)(2,1)}, u32[]{:S(2)}) copy-start(bf16[320,160]{1,0:T(8,128)(2,1)} %constant.27.clone.m1_table) | copy-start | bytes 307204
  54.0 21.5 %copy-start.21 = (bf16[256,160]{1,0:T(8,128)(2,1)S(1)}, bf16[256,160]{1,0:T(8,128)(2,1)}, u32[]{:S(2)}) copy-start(bf16[256,160]{1,0:T(8,128)(2,1)} %constant.29.clone.c1_table) | copy-start | bytes 245764
  54.0 21.5 %copy-start.22 = (bf16[160,64]{1,0:T(8,128)(2,1)S(1)}, bf16[160,64]{1,0:T(8,128)(2,1)}, u32[]{:S(2)}) copy-start(bf16[160,64]{1,0:T(8,128)(2,1)} %constant.28.clone.q1_table) | copy-start | bytes 61444
  54.0 31.9 %collective-permute-start.6 = (bf16[128,2048]{1,0:T(8,128)(2,1)S(1)}, bf16[128,2048]{1,0:T(8,128)(2,1)S(1)}, u32[]{:S(2)}, u32[]{:S(2)}) collective-permute-start(bf16[128,2048]{1,0:T(8,128)(2,1)S(1)} %get-tuple-element.43), channel_id=1, source_target_pairs={{0,28},{4,0},{8,4},{12,8},{16,12},{20,16},{24,20},{28,24},{1,29},{... | collective-permute-start | bytes 1572872 | tf_op jit(solution)/shard_map/ppermute | solution.py:459
  57.8 13.0 %collective-permute-start.8 = (bf16[64,2048]{1,0:T(8,128)(2,1)S(1)}, bf16[64,2048]{1,0:T(8,128)(2,1)S(1)}, u32[]{:S(2)}, u32[]{:S(2)}) collective-permute-start(bf16[64,2048]{1,0:T(8,128)(2,1)S(1)} %copy-done.24), channel_id=1, source_target_pairs={{0,1},{1,2},{2,3},{4,5},{5,6},{6,7},{8,9},{9,10},{10,11},{12,13},{... | collective-permute-start | bytes 786440 | tf_op jit(solution)/shard_map/ppermute | solution.py:485
  62.0 13.4 %collective-permute-start.9 = (bf16[64,2048]{1,0:T(8,128)(2,1)S(1)}, bf16[64,2048]{1,0:T(8,128)(2,1)S(1)}, u32[]{:S(2)}, u32[]{:S(2)}) collective-permute-start(bf16[64,2048]{1,0:T(8,128)(2,1)S(1)} %copy-done.23), channel_id=1, source_target_pairs={{1,0},{2,1},{3,2},{5,4},{6,5},{7,6},{9,8},{10,9},{11,10},{13,12},{... | collective-permute-start | bytes 786440 | tf_op jit(solution)/shard_map/ppermute | solution.py:485
  63.3 22.6 %collective-permute-start.5 = (bf16[16,2048]{1,0:T(8,128)(2,1)S(1)}, bf16[16,2048]{1,0:T(8,128)(2,1)S(1)}, u32[]{:S(2)}, u32[]{:S(2)}) collective-permute-start(bf16[16,2048]{1,0:T(8,128)(2,1)S(1)} %get-tuple-element.42), channel_id=1, source_target_pairs={{0,29},{1,30},{2,31},{4,1},{5,2},{6,3},{8,5},{9,6},{10,7},{12,9},{... | collective-permute-start | bytes 196616 | tf_op jit(solution)/shard_map/ppermute | solution.py:468
  67.6 18.4 %collective-permute-start.7 = (bf16[16,2048]{1,0:T(8,128)(2,1)S(1)}, bf16[16,2048]{1,0:T(8,128)(2,1)S(1)}, u32[]{:S(2)}, u32[]{:S(2)}) collective-permute-start(bf16[16,2048]{1,0:T(8,128)(2,1)S(1)} %get-tuple-element.44), channel_id=1, source_target_pairs={{1,28},{2,29},{3,30},{5,0},{6,1},{7,2},{9,4},{10,5},{11,6},{13,8},... | collective-permute-start | bytes 196616 | tf_op jit(solution)/shard_map/ppermute | solution.py:468
  70.8 15.1 %collective-permute-start.3 = (bf16[32,2048]{1,0:T(8,128)(2,1)S(1)}, bf16[32,2048]{1,0:T(8,128)(2,1)S(1)}, u32[]{:S(2)}, u32[]{:S(2)}) collective-permute-start(bf16[32,2048]{1,0:T(8,128)(2,1)S(1)} %shard_map.213.mine), channel_id=1, source_target_pairs={{0,1},{1,0},{2,3},{3,2},{4,5},{5,4},{6,7},{7,6},{8,9},{9,8},{10,11... | collective-permute-start | bytes 393224 | tf_op jit(solution)/shard_map/ppermute | solution.py:562
  75.5 6.8 %copy-start.1 = (bf16[1,2,128,2048]{3,2,1,0:T(8,128)(2,1)S(1)}, bf16[1,2,128,2048]{3,2,1,0:T(8,128)(2,1)}, u32[]{:S(2)}) copy-start(bf16[1,2,128,2048]{3,2,1,0:T(8,128)(2,1)} %param.21) | copy-start | bytes 3145732
  81.8 15.8 %collective-permute-start.12 = (bf16[128,2048]{1,0:T(8,128)(2,1)S(1)}, bf16[128,2048]{1,0:T(8,128)(2,1)S(1)}, u32[]{:S(2)}, u32[]{:S(2)}) collective-permute-start(bf16[128,2048]{1,0:T(8,128)(2,1)S(1)} %shard_map.218), channel_id=1, source_target_pairs={{0,8},{4,12},{8,16},{12,20},{16,24},{20,28},{24,0},{28,4},{1,9},{5... | collective-permute-start | bytes 1572872 | tf_op jit(solution)/shard_map/ppermute | solution.py:459
  89.4 12.3 %collective-permute-start.13 = (bf16[128,2048]{1,0:T(8,128)(2,1)S(1)}, bf16[128,2048]{1,0:T(8,128)(2,1)S(1)}, u32[]{:S(2)}, u32[]{:S(2)}) collective-permute-start(bf16[128,2048]{1,0:T(8,128)(2,1)S(1)} %get-tuple-element.53), channel_id=1, source_target_pairs={{0,28},{4,0},{8,4},{12,8},{16,12},{20,16},{24,20},{28,24},{1,29},{... | collective-permute-start | bytes 1572872 | tf_op jit(solution)/shard_map/ppermute | solution.py:459
  91.7 5.0 %collective-permute-start.10 = (bf16[32,2048]{1,0:T(8,128)(2,1)S(1)}, bf16[32,2048]{1,0:T(8,128)(2,1)S(1)}, u32[]{:S(2)}, u32[]{:S(2)}) collective-permute-start(bf16[32,2048]{1,0:T(8,128)(2,1)S(1)} %get-tuple-element.52.mine), channel_id=1, source_target_pairs={{0,1},{1,0},{2,3},{3,2},{4,5},{5,4},{6,7},{7,6},{8,9},{9,8},{10,11... | collective-permute-start | bytes 393224 | tf_op jit(solution)/shard_map/ppermute | solution.py:562
  92.0 5.6 %collective-permute-start.4 = (bf16[32,2048]{1,0:T(8,128)(2,1)S(1)}, bf16[32,2048]{1,0:T(8,128)(2,1)S(1)}, u32[]{:S(2)}, u32[]{:S(2)}) collective-permute-start(bf16[32,2048]{1,0:T(8,128)(2,1)S(1)} %shard_map.214.ready.mine0), channel_id=1, source_target_pairs={{0,2},{1,3},{2,0},{3,1},{4,6},{5,7},{6,4},{7,5},{8,10},{9,11},{10,... | collective-permute-start | bytes 393224 | tf_op jit(solution)/shard_map/ppermute | solution.py:562
  96.7 5.0 %collective-permute-start.11 = (bf16[32,2048]{1,0:T(8,128)(2,1)S(1)}, bf16[32,2048]{1,0:T(8,128)(2,1)S(1)}, u32[]{:S(2)}, u32[]{:S(2)}) collective-permute-start(bf16[32,2048]{1,0:T(8,128)(2,1)S(1)} %shard_map.217.mine1), channel_id=1, source_target_pairs={{0,2},{1,3},{2,0},{3,1},{4,6},{5,7},{6,4},{7,5},{8,10},{9,11},{10,... | collective-permute-start | bytes 393224 | tf_op jit(solution)/shard_map/ppermute | solution.py:562
  (7 other events, 15.7 us)

commit v4 on v3

--- a/solution.py
+++ b/solution.py
@@ -159,21 +159,13 @@
 
 
 class Back:
-    def __init__(self, own, reach, saved, mean, inverse, gain, mask_row, go_table, gh_table, x_table):
+    def __init__(self, own, saved, mean, inverse, gain, mask_row, g_table, x_table):
         self.__dict__.update(locals())
 
-    def mixed(self, pieces, factor, columns):
-        return (window(pieces, columns).astype(F32) * factor).astype(BF16)
-
-    def spectra(self, mixed):
-        own, reach = self.own, self.reach
-        inner = mixed[reach : reach + own]
-        ends = jnp.concatenate([mixed[:reach], mixed[reach + own :]], axis=0)
-        g_own = dot(self.go_table[...], jnp.concatenate([inner, inner], axis=0))
-        return g_own, g_own + dot(self.gh_table[...], jnp.concatenate([ends, ends], axis=0))
-
-    def rest(self, g_all, q, columns, scaled, sum_a, sum_b):
-        grad_masked = wide(self.mask_row, BLOCK) * transform(self.x_table, product_conj(g_all, q))
+    def rest(self, mixed, q, columns, scaled, sum_a, sum_b):
+        grad_masked = wide(self.mask_row, BLOCK) * transform(
+            self.x_table, product_conj(transform(self.g_table, mixed), q)
+        )
         centered = self.saved[:, columns].astype(F32) - wide(self.mean[...], BLOCK)
         weighted = grad_masked * (centered * wide(self.inverse[...], BLOCK))
         gain = self.gain(columns)
@@ -214,24 +206,36 @@
 
 
 def prepare_kernel(
-    reach, lengths, slots, later_slots, kernels, gains, saved, q_table,
-    weights, later, masked, mean, inverse, q,
+    reach, back_lengths, ahead_lengths, back_slots, ahead_slots, kernels, gains, saved, act, ready, q_table,
+    weights, later, tail, head, *outs,
 ):
-    own, width = saved.shape[1:]
+    own, width = act.shape
+    for x, at in ((saved.at[1], 0), (act, reach)):
+        tail[pl.ds(at, reach), :] = x[pl.ds(own - reach, reach), :]
+        head[pl.ds(at, reach), :] = x[pl.ds(0, reach), :]
     count = kernels.shape[0]
     for slot in range(kernels.shape[1]):
         weights[slot, :count, :] = kernels[:, slot, :]
         weights[slot, count:, :] = gains[slot : slot + 1, :]
     section, sections, first = place(own)
-    later[...] = weights[later_slots[1, section]]
-    slot = slots[0, section]
-    gain = slot_row(weights, slot)
-    norm_pieces([(saved.at[0], 0, own)], gain, first, lengths[section], masked, mean, inverse)
-
-    def block(columns):
-        q[:, columns] = tap_spectrum(q_table[...], weights[slot, :, columns])
-
-    each_block(width, block)
+    later[...] = weights[ahead_slots[1, section]]
+    layers = [
+        (saved.at[0], back_slots[0, section], back_lengths[section]),
+        (saved.at[1], back_slots[1, section], back_lengths[lax.rem(section + 1, sections)]),
+        (act, ahead_slots[0, section], ahead_lengths[section]),
+    ]
+    for (x, slot, length), (masked, mean, inverse, q) in zip(layers, (outs[:4], outs[4:8], outs[8:])):
+        norm_pieces([(x, 0, own)], slot_row(weights, slot), first, length, masked, mean, inverse)
+
+        def block(columns, slot=slot, q=q):
+            q[:, columns] = tap_spectrum(q_table[...], weights[slot, :, columns])
+
+        each_block(width, block)
+
+
+def norm_halo(left, right, at, reach, own, gain, first, length, halo):
+    norm_pieces([(left, at, reach)], gain, first - reach, length, halo)
+    norm_pieces([(right, at, reach)], gain, first + own, length, halo.at[pl.ds(reach, reach)])
 
 
 def joined(halo, own, columns):
@@ -241,41 +245,47 @@
 
 def first_backward_kernel(
     reach, lengths, slots, saved, left, right, grads, weights, later, masked, mean, inverse, q,
-    m_table, c_table, go_table, gh_table, x_table,
+    m_table, c_table, g_table, x_table,
     grad_x, top, bottom, halo, inner, gain_sum, scaled, sum_a, sum_b,
 ):
-    own, width = saved.shape[1:]
+    own, width = grads.shape
     half = reach // 2
     section, sections, first = place(own)
     slot, length = slots[0, section], lengths[section]
     gain = slot_row(weights, slot)
-    norm_pieces([(left, 0, reach)], gain, first - reach, length, halo)
-    norm_pieces([(right, 0, reach)], gain, first + own, length, halo.at[pl.ds(reach, reach)])
+    norm_halo(left, right, 0, reach, own, gain, first, length, halo)
     grad_pieces = [(left, reach, half), (grads, 0, own), (right, reach, half)]
-    back = Back(
-        own, half, saved.at[0], mean, inverse, gain, own_mask(own, first, length), go_table, gh_table, x_table
-    )
+    back = Back(own, saved.at[0], mean, inverse, gain, own_mask(own, first, length), g_table, x_table)
     sum_a[...] = jnp.zeros_like(sum_a)
     sum_b[...] = jnp.zeros_like(sum_b)
+    grad_x[pl.ds(own, later.shape[0]), :] = later[...]
 
     def block(columns):
         m = transform(m_table, joined(halo, masked, columns))
         conv = transform(c_table, product(m, q[:, columns]))
-        mixed = back.mixed(grad_pieces, gate_factor(conv), columns)
+        mixed = (window(grad_pieces, columns).astype(F32) * gate_factor(conv)).astype(BF16)
         inner[:, columns] = mixed[half : half + own]
-        gain_sum[:, columns] = back.rest(back.spectra(mixed)[1], q[:, columns], columns, scaled, sum_a, sum_b)
+        gain_sum[:, columns] = back.rest(mixed, q[:, columns], columns, scaled, sum_a, sum_b)
 
     each_block(width, block)
     outs = [(grad_x, 0, own), (top, 0, half), (bottom, own - half, own)]
     back.finish(grads, 0, scaled, sum_a, sum_b, outs)
 
 
+def tap_term(go_table, t_table, m, mixed):
+    g_own = dot(go_table[...], jnp.concatenate([mixed, mixed], axis=0))
+    return transform(t_table, product_conj(m, g_own))
+
+
+def put_taps(taps, tap, gain_sum, columns):
+    row = lax.broadcasted_iota(jnp.int32, tap.shape, 0)
+    taps[:, columns] = jnp.where(row == tap.shape[0] - 1, gain_sum, tap).astype(taps.dtype)
+
+
 def first_taps_kernel(halo, masked, inner, gain_sum, m_table, go_table, t_table, taps):
     def block(columns):
         m = transform(m_table, joined(halo, masked, columns))
-        mixed = inner[:, columns]
-        g_own = dot(go_table[...], jnp.concatenate([mixed, mixed], axis=0))
-        put_taps(taps, transform(t_table, product_conj(m, g_own)), gain_sum[:, columns], columns)
+        put_taps(taps, tap_term(go_table, t_table, m, inner[:, columns]), gain_sum[:, columns], columns)
 
     each_block(masked.shape[1], block)
 
@@ -284,93 +294,95 @@
     out[...] = (mine[...].astype(F32) + other[...].astype(F32)).astype(out.dtype)
 
 
-def put_taps(taps, tap, gain_sum, columns):
-    row = lax.broadcasted_iota(jnp.int32, tap.shape, 0)
-    taps[:, columns] = jnp.where(row == tap.shape[0] - 1, gain_sum, tap).astype(taps.dtype)
-
-
 def second_ready_kernel(
-    reach, lengths, slots, saved, left, right, weights,
-    m_table, q_table, c_table,
-    m_out, q_out, factor_out, mean_out, inverse_out, masked, mean, inverse,
+    reach, lengths, slots, left, right, weights, masked, q, m_table, c_table, m_out, factor, conv_out, halo
 ):
-    own, width = saved.shape[1:]
+    own, width = masked.shape
     section, sections, first = place(own)
     slot, length = slots[1, section], lengths[lax.rem(section + 1, sections)]
-    gain = slot_row(weights, slot)
-    pieces = [(left, 0, reach), (saved.at[1], 0, own), (right, 0, reach)]
-    norm_pieces(pieces, gain, first - reach, length, masked, mean, inverse)
-    mean_out[...] = mean[pl.ds(reach, own), :]
-    inverse_out[...] = inverse[pl.ds(reach, own), :]
+    norm_halo(left, right, 0, reach, own, slot_row(weights, slot), first, length, halo)
 
     def block(columns):
-        q = tap_spectrum(q_table[...], weights[slot, :, columns])
-        m = transform(m_table, masked[:, columns])
-        q_out[:, columns] = q
+        m = transform(m_table, joined(halo, masked, columns))
+        conv = transform(c_table, product(m, q[:, columns]))
         m_out[:, columns] = m
-        factor_out[:, columns] = gate_factor(transform(c_table, product(m, q)))
+        factor[:, columns] = gate_factor(conv)
+        edge = (conv.shape[0] - own) // 2
+        conv_out[:, columns] = conv[edge : edge + own]
 
     each_block(width, block)
 
 
-def second_backward_kernel(
-    lengths, slots, saved, left, grads, right, weights, m, q, factor, mean, inverse, ready,
-    go_table, gh_table, x_table, t_table,
-    grad_x, taps, scaled, sum_a, sum_b,
-):
-    own, width = saved.shape[1:]
+def second_taps_kernel(slots, left, grads, right, weights, m, factor, conv, ready, go_table, t_table, mixed_out, taps):
+    own, width = conv.shape
     half = left.shape[0]
     section, sections, first = place(own)
+    gain = slot_row(weights, slots[1, section])
+    pieces = [(left, 0, half), (grads, 0, own), (right, 0, half)]
+
+    def block(columns):
+        mixed = (window(pieces, columns).astype(F32) * factor[:, columns]).astype(BF16)
+        mixed_out[:, columns] = mixed
+        inner = mixed[half : half + own]
+        gain_sum = jnp.sum(inner.astype(F32) * conv[:, columns], axis=0, keepdims=True) / gain(columns)
+        put_taps(taps, tap_term(go_table, t_table, m[:, columns], inner), gain_sum, columns)
+
+    each_block(width, block)
+
+
+def second_backward_kernel(
+    lengths, slots, saved, grads, weights, mixed, q, mean, inverse, g_table, x_table, grad_x, scaled, sum_a, sum_b
+):
+    own, width = grad_x.shape
+    section, sections, first = place(own)
     slot, length = slots[1, section], lengths[lax.rem(section + 1, sections)]
-    pieces = [(left, 0, half), (grads, 0, own), (right, 0, half)]
     back = Back(
-        own, half, saved.at[1], mean, inverse, slot_row(weights, slot), own_mask(own, first, length),
-        go_table, gh_table, x_table,
+        own, saved.at[1], mean, inverse, slot_row(weights, slot), own_mask(own, first, length), g_table, x_table
     )
     sum_a[...] = jnp.zeros_like(sum_a)
     sum_b[...] = jnp.zeros_like(sum_b)
 
     def block(columns):
-        mixed = back.mixed(pieces, factor[:, columns], columns)
-        g_own, g_all = back.spectra(mixed)
-        tap = transform(t_table, product_conj(m[:, columns], g_own))
-        gain_sum = back.rest(g_all, q[:, columns], columns, scaled, sum_a, sum_b)
-        put_taps(taps, tap, gain_sum, columns)
+        back.rest(mixed[:, columns], q[:, columns], columns, scaled, sum_a, sum_b)
 
     each_block(width, block)
     back.finish(grads, 0, scaled, sum_a, sum_b, [(grad_x, 0, own)])
 
 
-def forward_kernel(
-    reach, lengths, slots, act, left, right, weights, later,
-    m0_table, q0_table, c0_table, m1_table, q1_table, c1_table,
-    out, masked0, between, masked1,
+def first_forward_kernel(
+    reach, lengths, slots, act, left, right, weights, masked, q, m_table, c_table, out, halo
 ):
     own, width = act.shape
     middle = reach // 2
     section, sections, first = place(own)
     slot, length = slots[0, section], lengths[section]
-    at = left.shape[0] - reach
-    pieces = [(left, at, reach), (act, 0, own), (right, at, reach)]
-    inner = [(left, at + middle, middle), (act, 0, own), (right, at, middle)]
-    norm_pieces(pieces, slot_row(weights, slot), first - reach, length, masked0)
-
-    def first_layer(columns):
-        q = tap_spectrum(q0_table[...], weights[slot, :, columns])
-        conv = transform(c0_table, product(transform(m0_table, masked0[:, columns]), q))
-        between[:, columns] = (window(inner, columns).astype(F32) + conv * sigmoid(conv)).astype(BF16)
-
-    each_block(width, first_layer)
-    last = later.shape[0] - 1
-    norm_pieces([(between, 0, own + 2 * middle)], lambda tile: later[last : last + 1, tile].astype(F32), first - middle, length, masked1)
-
-    def second_layer(columns):
-        q = tap_spectrum(q1_table[...], later[:, columns])
-        conv = transform(c1_table, product(transform(m1_table, masked1[:, columns]), q))
-        here = between[middle : middle + own, columns].astype(F32)
-        out[:, columns] = (here + conv * sigmoid(conv)).astype(BF16)
-
-    each_block(width, second_layer)
+    inner = [(left, reach + middle, middle), (act, 0, own), (right, reach, middle)]
+    norm_halo(left, right, reach, reach, own, slot_row(weights, slot), first, length, halo)
+
+    def block(columns):
+        conv = transform(c_table, product(transform(m_table, joined(halo, masked, columns)), q[:, columns]))
+        out[:, columns] = (window(inner, columns).astype(F32) + conv * sigmoid(conv)).astype(BF16)
+
+    each_block(width, block)
+
+
+def second_forward_kernel(lengths, between, received, m_table, q_table, c_table, out, masked):
+    own, width = out.shape
+    edge = (between.shape[0] - own) // 2
+    section, sections, first = place(own)
+    last = received.shape[0] - 1
+
+    def gain(columns):
+        return received[last : last + 1, columns].astype(F32)
+
+    norm_pieces([(between, 0, own + 2 * edge)], gain, first - edge, lengths[section], masked)
+
+    def block(columns):
+        q = tap_spectrum(q_table[...], received[own:, columns])
+        conv = transform(c_table, product(transform(m_table, masked[:, columns]), q))
+        out[:, columns] = (between[edge : edge + own, columns].astype(F32) + conv * sigmoid(conv)).astype(BF16)
+
+    each_block(width, block)
 
 
 def pack_kernel(count, refs):
@@ -418,8 +430,7 @@
 FULL = 127 * 512 * 1024
 
 
-def call(kernel, outs, scratch, operands, flops, specs=None, out_specs=None, limit=LIMIT):
-    moved = sum(int(np.prod(x.shape)) * x.dtype.itemsize for x in operands)
+def call(kernel, outs, scratch, operands, micros, specs=None, out_specs=None, limit=LIMIT):
     if specs is None:
         specs = [SMEM if x.dtype == jnp.int32 else VMEM for x in operands]
     return pl.pallas_call(
@@ -429,7 +440,7 @@
         out_specs=jax.tree.map(lambda _: VMEM, outs) if out_specs is None else out_specs,
         scratch_shapes=scratch,
         compiler_params=pltpu.CompilerParams(vmem_limit_bytes=limit),
-        cost_estimate=pl.CostEstimate(flops=flops, bytes_accessed=moved, transcendentals=0),
+        cost_estimate=pl.CostEstimate(flops=int(micros * 1e9), bytes_accessed=0, transcendentals=0),
     )(*operands)
 
 
@@ -468,117 +479,122 @@
         return lax.ppermute(x, ("section", "tm"), pairs)
 
     end, end2 = own - one, own - two
-    plan = [
-        (0, 0, end2, two, 3, 0), (1, 0, end, one, 3, two), (0, 0, 0, two, 4, 0), (1, 0, 0, one, 4, two),
-        (0, 1, end2, two, 5, 0), (2, 0, end2, two, 5, two), (0, 1, 0, two, 6, 0), (2, 0, 0, two, 6, two),
-    ]
-    tail0, head0, tail1, head1 = call(
+    plan = [(0, 0, end2, two, 2, 0), (1, 0, end, one, 2, two), (0, 0, 0, two, 3, 0), (1, 0, 0, one, 3, two)]
+    tail0, head0 = call(
         lambda *refs: pack_kernel(plan, refs),
-        tuple(like(n, width, BF16) for n in (two + one, two + one, 2 * two, 2 * two)),
+        (like(two + one, width, BF16),) * 2,
         [pltpu.SemaphoreType.DMA((len(plan),))],
-        (saved, grad_in, act_in),
-        0, [HBM] * 3, (ANY,) * 4, FULL,
+        (saved, grad_in),
+        0, [HBM] * 2, None, FULL,
     )
     up = [(i, i + 1) for i in range(shards - 1)]
     down = [(i + 1, i) for i in range(shards - 1)]
     left0, right0 = lax.ppermute(tail0, "tm", up), lax.ppermute(head0, "tm", down)
-    left1, right1 = lax.ppermute(tail1, "tm", up), lax.ppermute(head1, "tm", down)
-    ends = np.concatenate([np.arange(-one, 0), np.arange(own, own + one)])
     tap_back = np.concatenate([from_freq(size, np.arange(tap_count) - half), np.zeros((1, size))], axis=0)
     m_table = stacked(to_freq(size, span(two, own)))
     q_table = tap_freq(size, tap_count)
     c_table = stacked(from_freq(size, span(one, own)))
     go_table = beside(to_freq(size, np.arange(own)))
-    gh_table = beside(to_freq(size, ends))
+    g_table = stacked(to_freq(size, span(one, own)))
     x_table = stacked(from_freq(size, span(0, own)))
     t_table = stacked(tap_back)
-    work = 2 * size * size * width
-
-    def run(kernel, outs, scratch, operands, flops):
-        return call(kernel, outs, scratch, [jnp.asarray(x) for x in operands], flops)
+
+    def run(kernel, outs, scratch, operands, micros=0):
+        return call(kernel, outs, scratch, [jnp.asarray(x) for x in operands], micros)
 
     rows = [pltpu.VMEM((own, width), F32)] + [pltpu.VMEM((own, LANES), F32)] * 2
-    stats = [pltpu.VMEM((size, LANES), F32)] * 2
     forward_slots, backward_slots = forward_slots.T, backward_slots.T
-    weights, later, masked0, mean0, inverse0, q0 = run(
+    layer = (like(own, width, BF16), like(own, LANES, F32), like(own, LANES, F32), like(size, width, F32))
+    weights, later, tail1, head1, *layers = run(
         functools.partial(prepare_kernel, two),
         (
             jax.ShapeDtypeStruct((kernels.shape[1], tap_count + 1, width), BF16), like(tap_count + 1, width, BF16),
-            like(own, width, BF16), like(own, LANES, F32), like(own, LANES, F32), like(size, width, F32),
+            like(2 * two, width, BF16), like(2 * two, width, BF16), *layer, *layer, *layer,
         ),
         [],
         [
-            backward_lengths, backward_slots, forward_slots,
-            kernels[0].transpose(1, 0, 2), norm_gains[0], saved, q_table,
+            backward_lengths, forward_lengths, backward_slots, forward_slots,
+            kernels[0].transpose(1, 0, 2), norm_gains[0], saved, act, tail0, q_table,
         ],
-        work,
-    )
-    later = shifted(later, -1)
+    )
+    masked0, mean0, inverse0, q0, masked1, mean1, inverse1, q1, masked2, _, _, q2 = layers
+    left1, right1 = lax.ppermute(tail1, "tm", up), lax.ppermute(head1, "tm", down)
     grad_mid, top, bottom, halo0, inner0, gain0 = run(
         functools.partial(first_backward_kernel, two),
         (
-            like(own, width, BF16), like(one, width, BF16), like(one, width, BF16),
+            like(own + tap_count + 1, width, BF16), like(one, width, BF16), like(one, width, BF16),
             like(2 * two, width, BF16), like(own, width, BF16), like(1, width, F32),
         ),
         rows,
         [
             backward_lengths, backward_slots, saved, left0, right0, grad, weights, later, masked0, mean0, inverse0, q0,
-            m_table, c_table, go_table, gh_table, x_table,
+            m_table, c_table, g_table, x_table,
         ],
-        9 * work,
-    )
+        4,
+    )
+    grad_mid = shifted(grad_mid, -1)
     mid_right = to_neighbour(top, -1, -1)
     mid_left = to_neighbour(bottom, -1, 1)
-    grad_mid = shifted(grad_mid, -1)
     taps0 = run(
         first_taps_kernel, like(tap_count + 1, width, BF16), [],
-        [halo0, masked0, inner0, gain0, m_table, go_table, t_table], 3 * work,
+        [halo0, masked0, inner0, gain0, m_table, go_table, t_table],
+        0,
+    )
+    between = run(
+        functools.partial(first_forward_kernel, two),
+        like(small, width, BF16),
+        [pltpu.VMEM((2 * two, width), BF16)],
+        [forward_lengths, forward_slots, act, left1, right1, weights, masked2, q2, m_table, c_table],
+        3,
+    )
+    m1, factor1, conv1 = run(
+        functools.partial(second_ready_kernel, two),
+        (like(size, width, F32), like(small, width, F32), like(own, width, F32)),
+        [pltpu.VMEM((2 * two, width), BF16)],
+        [backward_lengths, backward_slots, left1, right1, weights, masked1, q1, m_table, c_table],
+        3,
     )
     act_out = run(
-        functools.partial(forward_kernel, two),
+        second_forward_kernel,
         like(own, width, BF16),
-        [pltpu.VMEM((size, width), BF16), pltpu.VMEM((small, width), BF16), pltpu.VMEM((small, width), BF16)],
+        [pltpu.VMEM((small, width), BF16)],
         [
-            forward_lengths, forward_slots, act, left1, right1, weights, later,
-            m_table, q_table, c_table,
+            forward_lengths, between, grad_mid,
             stacked(to_freq(small, span(one, own))), tap_freq(small, tap_count), stacked(from_freq(small, span(0, own))),
         ],
-        10 * work,
+        3,
     )
     act_out = shifted(act_out, 2)
-    prepared = run(
-        functools.partial(second_ready_kernel, two),
-        (
-            like(size, width, F32), like(size, width, F32), like(small, width, F32),
-            like(own, LANES, F32), like(own, LANES, F32),
-        ),
-        [pltpu.VMEM((size, width), BF16)] + stats,
-        [backward_lengths, backward_slots, saved, left1, right1, weights, m_table, q_table, c_table],
-        6 * work,
-    )
-    def summed(x):
+
+    def summed(x, micros):
         step = 1
         while True:
             other = lax.ppermute(x, "tm", [(i, i ^ step) for i in range(shards)])
             step *= 2
             if step >= shards:
                 return x, other
-            x = call(add_kernel, like(*x.shape, BF16), [], (x, other), 0)
-
-    mine0, other0 = summed(taps0)
-    grad_out, taps1 = run(
+            x = call(add_kernel, like(*x.shape, BF16), [], (x, other), micros)
+
+    mine0, other0 = summed(taps0, 0)
+    mixed1, taps1 = run(
+        second_taps_kernel,
+        (like(small, width, BF16), like(tap_count + 1, width, BF16)),
+        [],
+        [backward_slots, mid_left, grad_mid, mid_right, weights, m1, factor1, conv1, other0, go_table, t_table],
+        2,
+    )
+    grad_out = run(
         second_backward_kernel,
-        (like(own, width, BF16), like(tap_count + 1, width, BF16)),
+        like(own, width, BF16),
         rows,
         [
-            backward_lengths, backward_slots, saved, mid_left, grad_mid, mid_right, weights, *prepared, mine0,
-            go_table, gh_table, x_table, t_table,
+            backward_lengths, backward_slots, saved, grad_mid, weights, mixed1, q1, mean1, inverse1,
+            g_table, x_table,
         ],
-        6 * work,
-    )
-
+        6,
+    )
     grad_out = shifted(grad_out, -1)
-    sums = (mine0, other0) + summed(taps1)
+    sums = (mine0, other0) + summed(taps1, 6)
     slots = kernels.shape[1]
     act_out, grad_out, taps, gains = call(
         final_kernel,

time: 105 us -> 80.8 us (0.77)
  the two profiles are of different devices: /device:TPU:0 before, /device:TPU:1 now
where the time goes in v4:
time: 80.8 us; the launch traced here: 80.3 us
  Pallas kernels  31.7 us (39%)
  starting transfers between devices  29.2 us (36%)
  waiting for transfers between devices  11.6 us (14%)
  local copies, waits for them, and re-layouts  6.73 us (8%)
  between operations  0.99 us (1%)
    pallas_call x12, Pallas kernels, call(): pl.pallas_call(kernel, out_shape=outs, in_specs=specs, out_specs=jax.tree...  31.7 us
    ppermute x3, waiting for transfers between devices, shifted(): lax.ppermute(x, 'section', [(i, (i + by) % sections) for i in range(secti...  8.62 us
    ppermute x4, starting transfers between devices, summed(): other = lax.ppermute(x, 'tm', [(i, i ^ step) for i in range(shards)])  7.55 us
    ppermute x2, starting transfers between devices, to_neighbour(): return lax.ppermute(x, ('section', 'tm'), pairs)  7.32 us
    unnamed x44, local copies, waits for them, and re-layouts  6.73 us
    ppermute x1, starting transfers between devices, local(): lax.ppermute(tail0, 'tm', up)  4.58 us
    ppermute x1, starting transfers between devices, local(): lax.ppermute(tail1, 'tm', up)  4.3 us
    ppermute x4, waiting for transfers between devices, summed(): other = lax.ppermute(x, 'tm', [(i, i ^ step) for i in range(shards)])  2.98 us
  transfers between devices with their start and end apart: 13, of which 4 were waited for; matrix products, arithmetic and copies ran while one was open for 0% of the time, Pallas kernels for 34%

profile of v4, /device:TPU:1, one launch (start us, length us, event | category | flops | bytes accessed | tf_op | source)
XLA Modules:
  0.0 80.3 jit_solution(5700150447960573605)
XLA Ops:
  0.7 1.8 %shard_map.210 = (bf16[48,2048]{1,0:T(8,128)(2,1)}, bf16[48,2048]{1,0:T(8,128)(2,1)}) custom-call(bf16[2,128,2048]{2,1,0:T(8,128)(2,1)} %bitcast.15, bf16[1,128,2048]{2,1,0:T(8,128)(2,1)} %refs_1_.1), custom_call_target="tpu_custom_call" | custom-call | tf_op jit(solution)/shard_map/pallas_call | solution.py:436
  2.5 1.3 %collective-permute-start.1 = (bf16[48,2048]{1,0:T(8,128)(2,1)}, bf16[48,2048]{1,0:T(8,128)(2,1)S(1)}, u32[]{:S(2)}, u32[]{:S(2)}) collective-permute-start(bf16[48,2048]{1,0:T(8,128)(2,1)} %get-tuple-element.36), channel_id=1, source_target_pairs={{1,0},{2,1},{3,2},{5,4},{6,5},{7,6},{9,8},{10,9},{11,10},{13,12},{... | collective-permute-start | bytes 589832 | tf_op jit(solution)/shard_map/ppermute | solution.py:492
  3.8 4.6 %collective-permute-start = (bf16[48,2048]{1,0:T(8,128)(2,1)}, bf16[48,2048]{1,0:T(8,128)(2,1)S(1)}, u32[]{:S(2)}, u32[]{:S(2)}) collective-permute-start(bf16[48,2048]{1,0:T(8,128)(2,1)} %get-tuple-element.35.ready), channel_id=1, source_target_pairs={{0,1},{1,2},{2,3},{4,5},{5,6},{6,7},{8,9},{9,10},{10,11},{12,13},{... | collective-permute-start | bytes 589832 | tf_op jit(solution)/shard_map/ppermute | solution.py:492
  8.4 1.2 %copy-done = bf16[1,2,128,2048]{3,2,1,0:T(8,128)(2,1)S(1)} copy-done((bf16[1,2,128,2048]{3,2,1,0:T(8,128)(2,1)S(1)}, bf16[1,2,128,2048]{3,2,1,0:T(8,128)(2,1)}, u32[]{:S(2)}) %copy-start) | copy-done | bytes 1048600
  9.6 1.0 %copy-done.3 = bf16[1,128,2048]{2,1,0:T(8,128)(2,1)S(1)} copy-done((bf16[1,128,2048]{2,1,0:T(8,128)(2,1)S(1)}, bf16[1,128,2048]{2,1,0:T(8,128)(2,1)}, u32[]{:S(2)}) %copy-start.3) | copy-done | bytes 524312
  10.7 0.9 %copy-done.7 = bf16[48,2048]{1,0:T(8,128)(2,1)S(1)} copy-done((bf16[48,2048]{1,0:T(8,128)(2,1)S(1)}, bf16[48,2048]{1,0:T(8,128)(2,1)}, u32[]{:S(2)}) %copy-start.7) | copy-done | bytes 196632
  11.6 0.8 copy-done.9
  12.4 0.7 copy-done.12
  13.1 0.7 copy-done.13
  13.8 0.7 copy-done.14
  15.1 5.2 %shard_map.211 = (bf16[2,32,2048]{2,1,0:T(8,128)(2,1)S(1)}, bf16[32,2048]{1,0:T(8,128)(2,1)S(1)}, bf16[64,2048]{1,0:T(8,128)(2,1)S(1)}, bf16[64,2048]{1,0:T(8,12...) custom-call(s32[8]{0:T(128)S(1)} %copy-done.15, ...), custom_call_target="tpu_custom_call" | custom-call | tf_op jit(solution)/shard_map/pallas_call | solution.py:436
  20.3 4.3 %collective-permute-start.7 = (bf16[64,2048]{1,0:T(8,128)(2,1)S(1)}, bf16[64,2048]{1,0:T(8,128)(2,1)S(1)}, u32[]{:S(2)}, u32[]{:S(2)}) collective-permute-start(bf16[64,2048]{1,0:T(8,128)(2,1)S(1)} %get-tuple-element.49), channel_id=1, source_target_pairs={{0,1},{1,2},{2,3},{4,5},{5,6},{6,7},{8,9},{9,10},{10,11},{12,13},{... | collective-permute-start | bytes 786440 | tf_op jit(solution)/shard_map/ppermute | solution.py:521
  24.6 1.3 %collective-permute-start.8 = (bf16[64,2048]{1,0:T(8,128)(2,1)S(1)}, bf16[64,2048]{1,0:T(8,128)(2,1)S(1)}, u32[]{:S(2)}, u32[]{:S(2)}) collective-permute-start(bf16[64,2048]{1,0:T(8,128)(2,1)S(1)} %get-tuple-element.50), channel_id=1, source_target_pairs={{1,0},{2,1},{3,2},{5,4},{6,5},{7,6},{9,8},{10,9},{11,10},{13,12},{... | collective-permute-start | bytes 786440 | tf_op jit(solution)/shard_map/ppermute | solution.py:521
  26.0 5.6 %shard_map.212 = (bf16[160,2048]{1,0:T(8,128)(2,1)S(1)}, bf16[16,2048]{1,0:T(8,128)(2,1)S(1)}, bf16[16,2048]{1,0:T(8,128)(2,1)S(1)}, bf16[64,2048]{1,0:T(8,128)(...) custom-call(s32[8]{0:T(128)S(1)} %copy-done.15, s32[2,8]{1,0:T(2,128)S(1)} %bitcast.25, ...), custom_call_target="tpu_custom_call" | custom-call | flops 4000000000 | tf_op jit(solution)/shard_map/pallas_call | solution.py:436
  31.6 1.6 %collective-permute-start.5 = (bf16[160,2048]{1,0:T(8,128)(2,1)S(1)}, bf16[160,2048]{1,0:T(8,128)(2,1)S(1)}, u32[]{:S(2)}, u32[]{:S(2)}) collective-permute-start(bf16[160,2048]{1,0:T(8,128)(2,1)S(1)} %get-tuple-element.47), channel_id=1, source_target_pairs={{0,28},{4,0},{8,4},{12,8},{16,12},{20,16},{24,20},{28,24},{1,29},{... | collective-permute-start | bytes 1966088 | tf_op jit(solution)/shard_map/ppermute | solution.py:470
  33.2 6.0 %collective-permute-start.4 = (bf16[16,2048]{1,0:T(8,128)(2,1)S(1)}, bf16[16,2048]{1,0:T(8,128)(2,1)S(1)}, u32[]{:S(2)}, u32[]{:S(2)}) collective-permute-start(bf16[16,2048]{1,0:T(8,128)(2,1)S(1)} %get-tuple-element.46), channel_id=1, source_target_pairs={{0,29},{1,30},{2,31},{4,1},{5,2},{6,3},{8,5},{9,6},{10,7},{12,9},{... | collective-permute-start | bytes 196616 | tf_op jit(solution)/shard_map/ppermute | solution.py:479
  39.2 1.3 %collective-permute-start.6 = (bf16[16,2048]{1,0:T(8,128)(2,1)S(1)}, bf16[16,2048]{1,0:T(8,128)(2,1)S(1)}, u32[]{:S(2)}, u32[]{:S(2)}) collective-permute-start(bf16[16,2048]{1,0:T(8,128)(2,1)S(1)} %get-tuple-element.48), channel_id=1, source_target_pairs={{1,28},{2,29},{3,30},{5,0},{6,1},{7,2},{9,4},{10,5},{11,6},{13,8},... | collective-permute-start | bytes 196616 | tf_op jit(solution)/shard_map/ppermute | solution.py:479
  40.5 1.9 %shard_map.213.mine = bf16[32,2048]{1,0:T(8,128)(2,1)S(1)} custom-call(bf16[64,2048]{1,0:T(8,128)(2,1)S(1)} %get-tuple-element.43.halo, bf16[128,2048]{1,0:T(8,128)(2,1)S(1)} %get-tuple-element.39.masked, bf16[128,2048]{1,0:T(8,128)(2,1)S(1)} %get-tuple-element.44.inner, f32[1,2048]{1,0:T(1,128)S(1)} %get-tuple-element.45.gain_sum, ...), custom_call_target="tpu_custom_call" | custom-call | tf_op jit(solution)/shard_map/pallas_call | solution.py:436
  42.5 3.7 %collective-permute-start.2 = (bf16[32,2048]{1,0:T(8,128)(2,1)S(1)}, bf16[32,2048]{1,0:T(8,128)(2,1)S(1)}, u32[]{:S(2)}, u32[]{:S(2)}) collective-permute-start(bf16[32,2048]{1,0:T(8,128)(2,1)S(1)} %shard_map.213.mine), channel_id=1, source_target_pairs={{0,1},{1,0},{2,3},{3,2},{4,5},{5,4},{6,7},{7,6},{8,9},{9,8},{10,11... | collective-permute-start | bytes 393224 | tf_op jit(solution)/shard_map/ppermute | solution.py:572
  46.2 3.1 %shard_map.218.between = bf16[160,2048]{1,0:T(8,128)(2,1)S(1)} custom-call(s32[8]{0:T(128)S(1)} %copy-done.14, s32[2,8]{1,0:T(2,128)S(1)} %bitcast.31, bf16[128,2048]{1,0:T(8,128)(2,1)S(1)} %bitcast.21, bf16[64,2048]{1,0:T(8,128)(2,1)S(1)} %collective-permute-done.7.left, bf16[64,2048]{1,0:T(8,128)(2,1)S(1)} %collective-permute-done.8.right, ...), custom_call_target="tpu_custom_call" | custom-call | flops 3000000000 | tf_op jit(solution)/shard_map/pallas_call | solution.py:436
  49.3 3.2 %shard_map.215 = (f32[192,2048]{1,0:T(8,128)S(1)}, f32[160,2048]{1,0:T(8,128)S(1)}, f32[128,2048]{1,0:T(8,128)S(1)}) custom-call(s32[8]{0:T(128)S(1)} %copy-done.15, s32[2,8]{1,0:T(2,128)S(1)} %bitcast.26, bf16[64,2048]{1,0:T(8,128)(2,1)S(1)} %collective-permute-done.7.left, bf16[64,2048]{1,0:T(8,128)(2,1)S(1)} %collective-permute-done.8.right, ...), custom_call_target="tpu_custom_call" | custom-call | flops 3000000000 | tf_op jit(solution)/shard_map/pallas_call | solution.py:436
  52.5 1.0 %collective-permute-start.3 = (bf16[32,2048]{1,0:T(8,128)(2,1)S(1)}, bf16[32,2048]{1,0:T(8,128)(2,1)S(1)}, u32[]{:S(2)}, u32[]{:S(2)}) collective-permute-start(bf16[32,2048]{1,0:T(8,128)(2,1)S(1)} %shard_map.214.mine0), channel_id=1, source_target_pairs={{0,2},{1,3},{2,0},{3,1},{4,6},{5,7},{6,4},{7,5},{8,10},{9,11},{10,... | collective-permute-start | bytes 393224 | tf_op jit(solution)/shard_map/ppermute | solution.py:572
  53.6 3.2 %shard_map.219 = bf16[128,2048]{1,0:T(8,128)(2,1)S(1)} custom-call(s32[8]{0:T(128)S(1)} %copy-done.14, bf16[160,2048]{1,0:T(8,128)(2,1)S(1)} %shard_map.218.between, bf16[160,2048]{1,0:T(8,128)(2,1)S(1)} %collective-permute-done.5.grads.received, bf16[320,160]{1,0:T(8,128)(2,1)S(1)} %copy-done.17, bf16[160,64]{1,0:T(8,128)(2,1)S(1)} %copy-done.21, ...), custom_call_target="tpu_custom_call" | custom-call | flops 3000000000 | tf_op jit(solution)/shard_map/pallas_call | solution.py:436
  57.2 2.3 %shard_map.216 = (bf16[160,2048]{1,0:T(8,128)(2,1)S(1)}, bf16[32,2048]{1,0:T(8,128)(2,1)S(1)}) custom-call(s32[2,8]{1,0:T(2,128)S(1)} %bitcast.27, bf16[16,2048]{1,0:T(8,128)(2,1)S(1)} %collective-permute-done.4.left, bf16[160,2048]{1,0:T(8,128)(2,1)S(1)} %collective-permute-done.5.grads.received, bf16[16,2048]{1,0:T(8,128)(2,1)S(1)} %collective-permute-done.6.right, ...), custom_call_target="tpu_custom_call" | custom-call | flops 2000000000 | tf_op jit(solution)/shard_map/pallas_call | solution.py:436
  59.5 1.3 %collective-permute-start.9 = (bf16[32,2048]{1,0:T(8,128)(2,1)S(1)}, bf16[32,2048]{1,0:T(8,128)(2,1)S(1)}, u32[]{:S(2)}, u32[]{:S(2)}) collective-permute-start(bf16[32,2048]{1,0:T(8,128)(2,1)S(1)} %get-tuple-element.56.mine), channel_id=1, source_target_pairs={{0,1},{1,0},{2,3},{3,2},{4,5},{5,4},{6,7},{7,6},{8,9},{9,8},{10,11... | collective-permute-start | bytes 393224 | tf_op jit(solution)/shard_map/ppermute | solution.py:572
  60.8 3.0 %shard_map.220 = bf16[128,2048]{1,0:T(8,128)(2,1)S(1)} custom-call(s32[8]{0:T(128)S(1)} %copy-done.15, s32[2,8]{1,0:T(2,128)S(1)} %bitcast.28, bf16[2,128,2048]{2,1,0:T(8,128)(2,1)S(1)} %bitcast.18, bf16[160,2048]{1,0:T(8,128)(2,1)S(1)} %collective-permute-done.5.grads.received, bf16[2,32,2048]{2,1,0:T(8,128)(2,1)S(1)} %get-tuple-element.37.weights, ...), custom_call_target="tpu_custom_call" | custom-call | flops 6000000000 | tf_op jit(solution)/shard_map/pallas_call | solution.py:436
  63.8 1.3 %collective-permute-start.12 = (bf16[128,2048]{1,0:T(8,128)(2,1)S(1)}, bf16[128,2048]{1,0:T(8,128)(2,1)S(1)}, u32[]{:S(2)}, u32[]{:S(2)}) collective-permute-start(bf16[128,2048]{1,0:T(8,128)(2,1)S(1)} %shard_map.220), channel_id=1, source_target_pairs={{0,28},{4,0},{8,4},{12,8},{16,12},{20,16},{24,20},{28,24},{1,29},{... | collective-permute-start | bytes 1572872 | tf_op jit(solution)/shard_map/ppermute | solution.py:470
  65.2 1.5 %collective-permute-start.10 = (bf16[32,2048]{1,0:T(8,128)(2,1)S(1)}, bf16[32,2048]{1,0:T(8,128)(2,1)S(1)}, u32[]{:S(2)}, u32[]{:S(2)}) collective-permute-start(bf16[32,2048]{1,0:T(8,128)(2,1)S(1)} %shard_map.217.mine1), channel_id=1, source_target_pairs={{0,2},{1,3},{2,0},{3,1},{4,6},{5,7},{6,4},{7,5},{8,10},{9,11},{10,... | collective-permute-start | bytes 393224 | tf_op jit(solution)/shard_map/ppermute | solution.py:572
  66.7 2.7 %collective-permute-done.10.other1 = bf16[32,2048]{1,0:T(8,128)(2,1)S(1)} collective-permute-done((bf16[32,2048]{1,0:T(8,128)(2,1)S(1)}, bf16[32,2048]{1,0:T(8,128)(2,1)S(1)}, u32[]{:S(2)}, u32[]{:S(2)}) %collective-permute-start.10) | collective-permute-done | bytes 131104 | tf_op jit(solution)/shard_map/ppermute | solution.py:572
  69.3 2.4 %collective-permute-done.11.act = bf16[128,2048]{1,0:T(8,128)(2,1)S(1)} collective-permute-done((bf16[128,2048]{1,0:T(8,128)(2,1)S(1)}, bf16[128,2048]{1,0:T(8,128)(2,1)S(1)}, u32[]{:S(2)}, u32[]{:S(2)}) %collective-permute-start.11) | collective-permute-done | bytes 524320 | tf_op jit(solution)/shard_map/ppermute | solution.py:470
  71.8 6.2 %collective-permute-done.12.grad = bf16[128,2048]{1,0:T(8,128)(2,1)S(1)} collective-permute-done((bf16[128,2048]{1,0:T(8,128)(2,1)S(1)}, bf16[128,2048]{1,0:T(8,128)(2,1)S(1)}, u32[]{:S(2)}, u32[]{:S(2)}) %collective-permute-start.12) | collective-permute-done | bytes 524320 | tf_op jit(solution)/shard_map/ppermute | solution.py:470
  78.0 2.3 %shard_map.221 = (bf16[128,2048]{1,0:T(8,128)(2,1)}, bf16[128,2048]{1,0:T(8,128)(2,1)}, f32[31,2,2048]{2,1,0:T(2,128)}, f32[2,2048]{1,0:T(2,128)}) custom-call(s32[2,8]{1,0:T(2,128)S(1)} %bitcast.29, bf16[32,2048]{1,0:T(8,128)(2,1)S(1)} %shard_map.214.mine0, bf16[32,2048]{1,0:T(8,128)(2,1)S(1)} %collective-permute-done.3.ready.other0, ...), custom_call_target="tpu_custom_call" | custom-call | tf_op jit(solution)/shard_map/pallas_call | solution.py:436
  (50 shorter events, 1.2 us)
Async XLA Ops:
  0.6 7.8 %copy-start.11 = (bf16[1,2,2048]{2,1,0:T(2,128)(2,1)S(1)}, bf16[1,2,2048]{2,1,0:T(2,128)(2,1)}, u32[]{:S(2)}) copy-start(bf16[1,2,2048]{2,1,0:T(2,128)(2,1)} %param.23) | copy-start | bytes 24580
  0.6 7.8 %copy-start.5 = (bf16[1,2,31,2048]{3,1,2,0:T(2,128)(2,1)S(1)}, bf16[1,2,31,2048]{3,1,2,0:T(2,128)(2,1)}, u32[]{:S(2)}) copy-start(bf16[1,2,31,2048]{3,1,2,0:T(2,128)(2,1)} %param.22) | copy-start | bytes 761860
  0.7 25.3 %copy-start.6 = (bf16[384,192]{1,0:T(8,128)(2,1)S(1)}, bf16[384,192]{1,0:T(8,128)(2,1)}, u32[]{:S(2)}) copy-start(bf16[384,192]{1,0:T(8,128)(2,1)} %constant.21.clone.m_table) | copy-start | bytes 442372
  2.5 23.4 %collective-permute-start.1 = (bf16[48,2048]{1,0:T(8,128)(2,1)}, bf16[48,2048]{1,0:T(8,128)(2,1)S(1)}, u32[]{:S(2)}, u32[]{:S(2)}) collective-permute-start(bf16[48,2048]{1,0:T(8,128)(2,1)} %get-tuple-element.36), channel_id=1, source_target_pairs={{1,0},{2,1},{3,2},{5,4},{6,5},{7,6},{9,8},{10,9},{11,10},{13,12},{... | collective-permute-start | bytes 589832 | tf_op jit(solution)/shard_map/ppermute | solution.py:492
  3.8 22.1 %collective-permute-start = (bf16[48,2048]{1,0:T(8,128)(2,1)}, bf16[48,2048]{1,0:T(8,128)(2,1)S(1)}, u32[]{:S(2)}, u32[]{:S(2)}) collective-permute-start(bf16[48,2048]{1,0:T(8,128)(2,1)} %get-tuple-element.35.ready), channel_id=1, source_target_pairs={{0,1},{1,2},{2,3},{4,5},{5,6},{6,7},{8,9},{9,10},{10,11},{12,13},{... | collective-permute-start | bytes 589832 | tf_op jit(solution)/shard_map/ppermute | solution.py:492
  8.4 1.2 %copy-start = (bf16[1,2,128,2048]{3,2,1,0:T(8,128)(2,1)S(1)}, bf16[1,2,128,2048]{3,2,1,0:T(8,128)(2,1)}, u32[]{:S(2)}) copy-start(bf16[1,2,128,2048]{3,2,1,0:T(8,128)(2,1)} %param.21) | copy-start | bytes 3145732
  9.6 1.0 %copy-start.3 = (bf16[1,128,2048]{2,1,0:T(8,128)(2,1)S(1)}, bf16[1,128,2048]{2,1,0:T(8,128)(2,1)}, u32[]{:S(2)}) copy-start(bf16[1,128,2048]{2,1,0:T(8,128)(2,1)} %param.19) | copy-start | bytes 1572868
  10.7 0.9 %copy-start.7 = (bf16[48,2048]{1,0:T(8,128)(2,1)S(1)}, bf16[48,2048]{1,0:T(8,128)(2,1)}, u32[]{:S(2)}) copy-start(bf16[48,2048]{1,0:T(8,128)(2,1)} %get-tuple-element.35.ready) | copy-start | bytes 589828
  11.6 0.8 copy-start.9
  12.4 0.7 copy-start.12
  15.1 10.9 %copy-start.2 = (bf16[1,128,2048]{2,1,0:T(8,128)(2,1)S(1)}, bf16[1,128,2048]{2,1,0:T(8,128)(2,1)}, u32[]{:S(2)}) copy-start(bf16[1,128,2048]{2,1,0:T(8,128)(2,1)} %refs_1_.1) | copy-start | bytes 1572868
  15.1 10.9 %copy-start.16 = (bf16[384,160]{1,0:T(8,128)(2,1)S(1)}, bf16[384,160]{1,0:T(8,128)(2,1)}, u32[]{:S(2)}) copy-start(bf16[384,160]{1,0:T(8,128)(2,1)} %constant.23.clone.g_table) | copy-start | bytes 368644
  15.1 10.9 %copy-start.18 = (bf16[320,192]{1,0:T(8,128)(2,1)S(1)}, bf16[320,192]{1,0:T(8,128)(2,1)}, u32[]{:S(2)}) copy-start(bf16[320,192]{1,0:T(8,128)(2,1)} %constant.22.clone.c_table) | copy-start | bytes 368644
  15.1 10.9 %copy-start.19 = (bf16[256,192]{1,0:T(8,128)(2,1)S(1)}, bf16[256,192]{1,0:T(8,128)(2,1)}, u32[]{:S(2)}) copy-start(bf16[256,192]{1,0:T(8,128)(2,1)} %constant.24.clone.x_table) | copy-start | bytes 294916
  20.3 22.2 %collective-permute-start.7 = (bf16[64,2048]{1,0:T(8,128)(2,1)S(1)}, bf16[64,2048]{1,0:T(8,128)(2,1)S(1)}, u32[]{:S(2)}, u32[]{:S(2)}) collective-permute-start(bf16[64,2048]{1,0:T(8,128)(2,1)S(1)} %get-tuple-element.49), channel_id=1, source_target_pairs={{0,1},{1,2},{2,3},{4,5},{5,6},{6,7},{8,9},{9,10},{10,11},{12,13},{... | collective-permute-start | bytes 786440 | tf_op jit(solution)/shard_map/ppermute | solution.py:521
  24.6 21.6 %collective-permute-start.8 = (bf16[64,2048]{1,0:T(8,128)(2,1)S(1)}, bf16[64,2048]{1,0:T(8,128)(2,1)S(1)}, u32[]{:S(2)}, u32[]{:S(2)}) collective-permute-start(bf16[64,2048]{1,0:T(8,128)(2,1)S(1)} %get-tuple-element.50), channel_id=1, source_target_pairs={{1,0},{2,1},{3,2},{5,4},{6,5},{7,6},{9,8},{10,9},{11,10},{13,12},{... | collective-permute-start | bytes 786440 | tf_op jit(solution)/shard_map/ppermute | solution.py:521
  26.0 14.6 %copy-start.8 = (bf16[192,256]{1,0:T(8,128)(2,1)S(1)}, bf16[192,256]{1,0:T(8,128)(2,1)}, u32[]{:S(2)}) copy-start(bf16[192,256]{1,0:T(8,128)(2,1)} %constant.25.clone.go_table) | copy-start | bytes 294916
  26.0 14.6 %copy-start.10 = (bf16[64,192]{1,0:T(8,128)(2,1)S(1)}, bf16[64,192]{1,0:T(8,128)(2,1)}, u32[]{:S(2)}) copy-start(bf16[64,192]{1,0:T(8,128)(2,1)} %constant.26.clone.t_table) | copy-start | bytes 73732
  31.6 14.5 %copy-start.4 = (bf16[1,128,2048]{2,1,0:T(8,128)(2,1)S(1)}, bf16[1,128,2048]{2,1,0:T(8,128)(2,1)}, u32[]{:S(2)}) copy-start(bf16[1,128,2048]{2,1,0:T(8,128)(2,1)} %param.19) | copy-start | bytes 1572868
  31.6 21.9 %collective-permute-start.5 = (bf16[160,2048]{1,0:T(8,128)(2,1)S(1)}, bf16[160,2048]{1,0:T(8,128)(2,1)S(1)}, u32[]{:S(2)}, u32[]{:S(2)}) collective-permute-start(bf16[160,2048]{1,0:T(8,128)(2,1)S(1)} %get-tuple-element.47), channel_id=1, source_target_pairs={{0,28},{4,0},{8,4},{12,8},{16,12},{20,16},{24,20},{28,24},{1,29},{... | collective-permute-start | bytes 1966088 | tf_op jit(solution)/shard_map/ppermute | solution.py:470
  33.2 23.7 %collective-permute-start.4 = (bf16[16,2048]{1,0:T(8,128)(2,1)S(1)}, bf16[16,2048]{1,0:T(8,128)(2,1)S(1)}, u32[]{:S(2)}, u32[]{:S(2)}) collective-permute-start(bf16[16,2048]{1,0:T(8,128)(2,1)S(1)} %get-tuple-element.46), channel_id=1, source_target_pairs={{0,29},{1,30},{2,31},{4,1},{5,2},{6,3},{8,5},{9,6},{10,7},{12,9},{... | collective-permute-start | bytes 196616 | tf_op jit(solution)/shard_map/ppermute | solution.py:479
  39.2 17.7 %collective-permute-start.6 = (bf16[16,2048]{1,0:T(8,128)(2,1)S(1)}, bf16[16,2048]{1,0:T(8,128)(2,1)S(1)}, u32[]{:S(2)}, u32[]{:S(2)}) collective-permute-start(bf16[16,2048]{1,0:T(8,128)(2,1)S(1)} %get-tuple-element.48), channel_id=1, source_target_pairs={{1,28},{2,29},{3,30},{5,0},{6,1},{7,2},{9,4},{10,5},{11,6},{13,8},... | collective-permute-start | bytes 196616 | tf_op jit(solution)/shard_map/ppermute | solution.py:479
  42.5 10.0 %collective-permute-start.2 = (bf16[32,2048]{1,0:T(8,128)(2,1)S(1)}, bf16[32,2048]{1,0:T(8,128)(2,1)S(1)}, u32[]{:S(2)}, u32[]{:S(2)}) collective-permute-start(bf16[32,2048]{1,0:T(8,128)(2,1)S(1)} %shard_map.213.mine), channel_id=1, source_target_pairs={{0,1},{1,0},{2,3},{3,2},{4,5},{5,4},{6,7},{7,6},{8,9},{9,8},{10,11... | collective-permute-start | bytes 393224 | tf_op jit(solution)/shard_map/ppermute | solution.py:572
  49.3 4.3 %copy-start.17 = (bf16[320,160]{1,0:T(8,128)(2,1)S(1)}, bf16[320,160]{1,0:T(8,128)(2,1)}, u32[]{:S(2)}) copy-start(bf16[320,160]{1,0:T(8,128)(2,1)} %constant.27.clone.m_table) | copy-start | bytes 307204
  49.3 4.3 %copy-start.20 = (bf16[256,160]{1,0:T(8,128)(2,1)S(1)}, bf16[256,160]{1,0:T(8,128)(2,1)}, u32[]{:S(2)}) copy-start(bf16[256,160]{1,0:T(8,128)(2,1)} %constant.29.clone.c_table) | copy-start | bytes 245764
  49.3 4.3 %copy-start.21 = (bf16[160,64]{1,0:T(8,128)(2,1)S(1)}, bf16[160,64]{1,0:T(8,128)(2,1)}, u32[]{:S(2)}) copy-start(bf16[160,64]{1,0:T(8,128)(2,1)} %constant.28.clone.q_table) | copy-start | bytes 61444
  52.5 4.7 %collective-permute-start.3 = (bf16[32,2048]{1,0:T(8,128)(2,1)S(1)}, bf16[32,2048]{1,0:T(8,128)(2,1)S(1)}, u32[]{:S(2)}, u32[]{:S(2)}) collective-permute-start(bf16[32,2048]{1,0:T(8,128)(2,1)S(1)} %shard_map.214.mine0), channel_id=1, source_target_pairs={{0,2},{1,3},{2,0},{3,1},{4,6},{5,7},{6,4},{7,5},{8,10},{9,11},{10,... | collective-permute-start | bytes 393224 | tf_op jit(solution)/shard_map/ppermute | solution.py:572
  56.8 15.0 %collective-permute-start.11 = (bf16[128,2048]{1,0:T(8,128)(2,1)S(1)}, bf16[128,2048]{1,0:T(8,128)(2,1)S(1)}, u32[]{:S(2)}, u32[]{:S(2)}) collective-permute-start(bf16[128,2048]{1,0:T(8,128)(2,1)S(1)} %shard_map.219), channel_id=1, source_target_pairs={{0,8},{4,12},{8,16},{12,20},{16,24},{20,28},{24,0},{28,4},{1,9},{5... | collective-permute-start | bytes 1572872 | tf_op jit(solution)/shard_map/ppermute | solution.py:470
  57.2 3.6 %copy-start.1 = (bf16[1,2,128,2048]{3,2,1,0:T(8,128)(2,1)S(1)}, bf16[1,2,128,2048]{3,2,1,0:T(8,128)(2,1)}, u32[]{:S(2)}) copy-start(bf16[1,2,128,2048]{3,2,1,0:T(8,128)(2,1)} %param.21) | copy-start | bytes 3145732
  59.5 5.6 %collective-permute-start.9 = (bf16[32,2048]{1,0:T(8,128)(2,1)S(1)}, bf16[32,2048]{1,0:T(8,128)(2,1)S(1)}, u32[]{:S(2)}, u32[]{:S(2)}) collective-permute-start(bf16[32,2048]{1,0:T(8,128)(2,1)S(1)} %get-tuple-element.56.mine), channel_id=1, source_target_pairs={{0,1},{1,0},{2,3},{3,2},{4,5},{5,4},{6,7},{7,6},{8,9},{9,8},{10,11... | collective-permute-start | bytes 393224 | tf_op jit(solution)/shard_map/ppermute | solution.py:572
  63.8 14.1 %collective-permute-start.12 = (bf16[128,2048]{1,0:T(8,128)(2,1)S(1)}, bf16[128,2048]{1,0:T(8,128)(2,1)S(1)}, u32[]{:S(2)}, u32[]{:S(2)}) collective-permute-start(bf16[128,2048]{1,0:T(8,128)(2,1)S(1)} %shard_map.220), channel_id=1, source_target_pairs={{0,28},{4,0},{8,4},{12,8},{16,12},{20,16},{24,20},{28,24},{1,29},{... | collective-permute-start | bytes 1572872 | tf_op jit(solution)/shard_map/ppermute | solution.py:470
  65.2 4.2 %collective-permute-start.10 = (bf16[32,2048]{1,0:T(8,128)(2,1)S(1)}, bf16[32,2048]{1,0:T(8,128)(2,1)S(1)}, u32[]{:S(2)}, u32[]{:S(2)}) collective-permute-start(bf16[32,2048]{1,0:T(8,128)(2,1)S(1)} %shard_map.217.mine1), channel_id=1, source_target_pairs={{0,2},{1,3},{2,0},{3,1},{4,6},{5,7},{6,4},{7,5},{8,10},{9,11},{10,... | collective-permute-start | bytes 393224 | tf_op jit(solution)/shard_map/ppermute | solution.py:572
  (3 other events, 2.0 us)

commit v5 on v4

v5 whole, which is shorter than its diff:
```python
import functools

import jax
import jax.numpy as jnp
import ml_dtypes
import numpy as np
from jax import lax
from jax.experimental import pallas as pl
from jax.experimental.pallas import tpu as pltpu
from jax.sharding import PartitionSpec as P

epsilon = 1e-05
BLOCK = 512
LANES = 128
F32 = jnp.float32
BF16 = jnp.bfloat16


def split(matrix):
    high = matrix.astype(ml_dtypes.bfloat16)
    low = (matrix - high.astype(np.float64)).astype(ml_dtypes.bfloat16)
    return high, low


def angles(size, times):
    return 2.0 * np.pi / size * np.outer(np.arange(size // 2) + 0.5, np.asarray(times, np.float64))


def to_freq(size, times):
    phase = angles(size, times)
    return np.concatenate([np.cos(phase), -np.sin(phase)], axis=0)


def from_freq(size, times):
    phase = angles(size, times).T
    return 2.0 / size * np.concatenate([np.cos(phase), -np.sin(phase)], axis=1)


def stacked(matrix):
    return np.concatenate(split(matrix), axis=0)


def beside(matrix):
    return np.concatenate(split(matrix), axis=1)


def tap_freq(size, taps):
    phase = angles(size, np.arange(taps) - (taps - 1) // 2)
    table = np.concatenate([np.cos(phase), np.sin(phase)], axis=0)
    return beside(np.concatenate([table, np.zeros((size, 1))], axis=1))


def dot(a, b):
    return jnp.dot(a, b, preferred_element_type=F32)


def transform(table, values):
    return sum(halves(dot(table[...], values.astype(BF16))))


def halves(values):
    half = values.shape[0] // 2
    return values[:half], values[half:]


def product(a, b):
    ar, ai = halves(a)
    br, bi = halves(b)
    return jnp.concatenate([ar * br - ai * bi, ar * bi + ai * br], axis=0)


def product_conj(a, b):
    ar, ai = halves(a)
    br, bi = halves(b)
    return jnp.concatenate([ar * br + ai * bi, ai * br - ar * bi], axis=0)


def sigmoid(values):
    return 0.5 * jnp.tanh(0.5 * values) + 0.5


def wide(stat, count):
    return jnp.concatenate([stat] * (count // LANES), axis=1)


def norm_rows(ref, start, count, at, gain, first, length, masked_ref, mean_ref, inverse_ref):
    width = masked_ref.shape[1]
    rows = pl.ds(start, count)
    tiles = [pl.ds(i * LANES, LANES) for i in range(width // LANES)]

    def values(tile):
        return ref[rows, tile].astype(F32)

    total = values(tiles[0])
    for tile in tiles[1:]:
        total = total + values(tile)
    mean = jnp.sum(total, axis=1, keepdims=True) * (1.0 / width)
    mean = jnp.broadcast_to(mean, (count, LANES))
    square = jnp.zeros((count, LANES), F32)
    for tile in tiles:
        center = values(tile) - mean
        square = square + center * center
    var = jnp.sum(square, axis=1, keepdims=True) * (1.0 / width)
    inverse = jnp.broadcast_to(lax.rsqrt(var + epsilon), (count, LANES))
    frame = first + at + lax.broadcasted_iota(jnp.int32, (count, LANES), 0)
    mask = ((frame >= 0) & (frame < length)).astype(F32)
    scale = mask * inverse
    out = pl.ds(at, count)
    for tile in tiles:
        masked_ref[out, tile] = ((values(tile) - mean) * scale * gain(tile)).astype(BF16)
    if mean_ref is not None:
        mean_ref[out, :] = mean
        inverse_ref[out, :] = inverse


def norm_pieces(pieces, gain, first, length, masked_ref, mean_ref=None, inverse_ref=None, chunk=64):
    at = 0
    for ref, start, count in pieces:
        for begin in range(0, count, chunk):
            norm_rows(
                ref, start + begin, min(chunk, count - begin), at + begin,
                gain, first, length, masked_ref, mean_ref, inverse_ref,
            )
        at += count


def window(pieces, columns):
    parts = [ref[pl.ds(start, count), columns] for ref, start, count in pieces]
    return parts[0] if len(parts) == 1 else jnp.concatenate(parts, axis=0)


def each_block(width, body):
    def step(i, _):
        body(pl.ds(pl.multiple_of(i * BLOCK, BLOCK), BLOCK))
        return 0

    lax.fori_loop(0, width // BLOCK, step, 0)


def tap_spectrum(table, weights):
    return dot(table, jnp.concatenate([weights, weights], axis=0))


def gate_factor(conv):
    gate = sigmoid(conv)
    return gate * (1.0 + conv * (1.0 - gate))


FIRST, BACK0, BACK1, AHEAD0 = range(0, 8, 2)


def looked_up(notes, layer):
    return notes[layer], notes[layer + 1], notes[FIRST]


def sorted_halos(near, far, at, halos):
    even = lax.rem(lax.axis_index("tm") + 1, 2)
    rows = pl.ds(at, halos.shape[1])
    halos[even] = near[rows, :]
    halos[1 - even] = far[rows, :]
    return halos.at[0], halos.at[1]


def lane_sum(values):
    total = values[:, :LANES]
    for lane in range(LANES, values.shape[1], LANES):
        total = total + values[:, lane : lane + LANES]
    return total


def first_pass(pieces, mean, inverse, gain, mask, tables, mixed, q, columns, scaled, sum_a, sum_b):
    g_table, x_table = tables
    grad_masked = wide(mask, BLOCK) * transform(x_table, product_conj(transform(g_table, mixed), q))
    centered = window(pieces, columns).astype(F32) - wide(mean[...], BLOCK)
    weighted = grad_masked * (centered * wide(inverse[...], BLOCK))
    gain = gain(columns)
    by_gain = grad_masked * gain
    scaled[:, columns] = by_gain
    sum_a[...] += lane_sum(by_gain)
    sum_b[...] += lane_sum(weighted * gain)
    return weighted


def last_pass(grad_pieces, pieces, mean, inverse, scaled, sum_a, sum_b, grad_x, chunk=64):
    width = scaled.shape[1]
    at = 0
    for (ref, start, count), (saved, base, _) in zip(grad_pieces, pieces):
        for begin in range(0, count, chunk):
            here = min(chunk, count - begin)
            rows = pl.ds(at + begin, here)
            inv = inverse[rows, :]
            mean_a = jnp.sum(sum_a[rows, :], axis=1, keepdims=True) * (1.0 / width)
            mean_b = jnp.sum(sum_b[rows, :], axis=1, keepdims=True) * (1.0 / width)
            slope = inv * jnp.broadcast_to(mean_b, (here, LANES)) * inv
            fixed = inv * jnp.broadcast_to(mean_a, (here, LANES)) - slope * mean[rows, :]
            for lane in range(0, width, LANES):
                tile = pl.ds(lane, LANES)
                x = saved[pl.ds(base + begin, here), tile].astype(F32)
                change = inv * scaled[rows, tile] - fixed - slope * x
                grad_x[rows, tile] = (ref[pl.ds(start + begin, here), tile].astype(F32) + change).astype(BF16)
        at += count


def frame_mask(rows, first, length):
    frame = first + lax.broadcasted_iota(jnp.int32, (rows, LANES), 0)
    return ((frame >= 0) & (frame < length)).astype(F32)


def slot_row(weights, slot):
    last = weights.shape[1] - 1
    return lambda columns: weights[slot, last : last + 1, columns].astype(F32)


def prepare_kernel(
    reach, back_lengths, ahead_lengths, back_slots, ahead_slots, kernels, gains, saved, act, ready, q_table,
    weights, later, near, far, notes, masked, mean, inverse, q,
):
    own, width = act.shape
    section, sections = lax.axis_index("section"), lax.axis_size("section")
    for even in range(2):

        @pl.when(lax.rem(lax.axis_index("tm") + 1, 2) == even)
        def _():
            for x, at in ((saved.at[1], 0), (act, reach)):
                tail, head = (near, far) if even else (far, near)
                tail[pl.ds(at, reach), :] = x[pl.ds(own - reach, reach), :]
                head[pl.ds(at, reach), :] = x[pl.ds(0, reach), :]

    count = kernels.shape[0]
    for slot in range(kernels.shape[1]):
        weights[slot, :count, :] = kernels[:, slot, :]
        weights[slot, count:, :] = gains[slot : slot + 1, :]
    later[...] = weights[ahead_slots[1, section]]
    slot, length, first = back_slots[0, section], back_lengths[section], lax.axis_index("tm") * own
    notes[FIRST] = first
    notes[BACK0] = slot
    notes[BACK0 + 1] = length
    notes[BACK1] = back_slots[1, section]
    notes[BACK1 + 1] = back_lengths[lax.rem(section + 1, sections)]
    notes[AHEAD0] = ahead_slots[0, section]
    notes[AHEAD0 + 1] = ahead_lengths[section]
    norm_pieces([(saved.at[0], 0, own)], slot_row(weights, slot), first, length, masked, mean, inverse)

    def block(columns):
        q[:, columns] = tap_spectrum(q_table[...], weights[slot, :, columns])

    each_block(width, block)


def prepare_later_kernel(notes, saved, act, weights, q_table, *outs):
    own, width = act.shape
    for x, layer, (masked, mean, inverse, q) in ((saved.at[1], BACK1, outs[:4]), (act, AHEAD0, outs[4:])):
        slot, length, first = looked_up(notes, layer)
        norm_pieces([(x, 0, own)], slot_row(weights, slot), first, length, masked, mean, inverse)

        def block(columns, slot=slot, q=q):
            q[:, columns] = tap_spectrum(q_table[...], weights[slot, :, columns])

        each_block(width, block)


def norm_halo(left, right, own, gain, first, length, halo):
    reach = left.shape[0]
    norm_pieces([(left, 0, reach)], gain, first - reach, length, halo)
    norm_pieces([(right, 0, reach)], gain, first + own, length, halo.at[pl.ds(reach, reach)])


def joined(halo, own, columns):
    reach = halo.shape[0] // 2
    return jnp.concatenate([halo[:reach, columns], own[:, columns], halo[reach:, columns]], axis=0)


def first_backward_kernel(
    reaches, notes, saved, near, far, grads, weights, later, own_masked, own_mean, own_inverse, q,
    m_table, c_table, g_table, x_table,
    grad_x, halo, inner, gain_sum, halos, grad_halos, all_mean, all_inverse, scaled, sum_a, sum_b,
):
    own, width = grads.shape
    reach, grad_reach, out_reach = reaches
    slot, length, first = looked_up(notes, BACK0)
    gain = slot_row(weights, slot)
    left, right = sorted_halos(near, far, 0, halos)
    grad_left, grad_right = sorted_halos(near, far, reach, grad_halos)
    edge = reach - out_reach
    low, middle, high = pl.ds(0, out_reach), pl.ds(out_reach, own), pl.ds(out_reach + own, out_reach)
    bounds = ((left, first - reach, 0, edge, low), (right, first + own, reach, 0, high))
    for x, begin, at, skip, rows in bounds:
        norm_rows(x, 0, reach, 0, gain, begin, length, halo.at[pl.ds(at, reach)], sum_a, sum_b)
        all_mean[rows, :] = sum_a[pl.ds(skip, out_reach), :]
        all_inverse[rows, :] = sum_b[pl.ds(skip, out_reach), :]
    all_mean[middle, :] = own_mean[...]
    all_inverse[middle, :] = own_inverse[...]
    grad_pieces = [(grad_left, 0, grad_reach), (grads, 0, own), (grad_right, 0, grad_reach)]
    pieces = [(left, edge, out_reach), (saved.at[0], 0, own), (right, 0, out_reach)]
    out_pieces = [(grad_left, grad_reach - out_reach, out_reach), (grads, 0, own), (grad_right, 0, out_reach)]
    mask = frame_mask(own + 2 * out_reach, first - out_reach, length)
    sum_a[...] = jnp.zeros_like(sum_a)
    sum_b[...] = jnp.zeros_like(sum_b)
    grad_x[pl.ds(own + 2 * out_reach, later.shape[0]), :] = later[...]

    def block(columns):
        m = transform(m_table, joined(halo, own_masked, columns))
        conv = transform(c_table, product(m, q[:, columns]))
        mixed = (window(grad_pieces, columns).astype(F32) * gate_factor(conv)).astype(BF16)
        inner[:, columns] = mixed[grad_reach : grad_reach + own]
        weighted = first_pass(
            pieces, all_mean, all_inverse, gain, mask, (g_table, x_table), mixed, q[:, columns], columns,
            scaled, sum_a, sum_b,
        )
        gain_sum[:, columns] = jnp.sum(weighted[out_reach : out_reach + own], axis=0, keepdims=True)

    each_block(width, block)
    last_pass(out_pieces, pieces, all_mean, all_inverse, scaled, sum_a, sum_b, grad_x)


def tap_term(go_table, t_table, m, mixed):
    g_own = dot(go_table[...], jnp.concatenate([mixed, mixed], axis=0))
    return transform(t_table, product_conj(m, g_own))


def put_taps(taps, tap, gain_sum, columns):
    row = lax.broadcasted_iota(jnp.int32, tap.shape, 0)
    taps[:, columns] = jnp.where(row == tap.shape[0] - 1, gain_sum, tap).astype(taps.dtype)


def first_taps_kernel(reach, halo, masked, inner, gain_sum, m_table, go_table, t_table, taps):
    wide_reach = halo.shape[0] // 2
    own, width = masked.shape
    pieces = [(halo, wide_reach - reach, reach), (masked, 0, own), (halo, wide_reach, reach)]

    def block(columns):
        m = transform(m_table, window(pieces, columns))
        put_taps(taps, tap_term(go_table, t_table, m, inner[:, columns]), gain_sum[:, columns], columns)

    each_block(width, block)


def add_kernel(mine, other, out):
    out[...] = (mine[...].astype(F32) + other[...].astype(F32)).astype(out.dtype)


def second_ready_kernel(
    reach, notes, near, far, weights, masked, q, m_table, c_table, m_out, factor, conv_out, halo, halos
):
    own, width = masked.shape
    slot, length, first = looked_up(notes, BACK1)
    left, right = sorted_halos(near, far, 0, halos)
    norm_halo(left, right, own, slot_row(weights, slot), first, length, halo)

    def block(columns):
        m = transform(m_table, joined(halo, masked, columns))
        conv = transform(c_table, product(m, q[:, columns]))
        m_out[:, columns] = m
        factor[:, columns] = gate_factor(conv)
        edge = (conv.shape[0] - own) // 2
        conv_out[:, columns] = conv[edge : edge + own]

    each_block(width, block)


def second_taps_kernel(notes, received, weights, m, factor, conv, ready, go_table, t_table, mixed_out, taps):
    own, width = conv.shape
    rows = factor.shape[0]
    edge = (rows - own) // 2
    gain = slot_row(weights, notes[BACK1])

    def block(columns):
        mixed = (received[:rows, columns].astype(F32) * factor[:, columns]).astype(BF16)
        mixed_out[:, columns] = mixed
        inner = mixed[edge : edge + own]
        gain_sum = jnp.sum(inner.astype(F32) * conv[:, columns], axis=0, keepdims=True) / gain(columns)
        put_taps(taps, tap_term(go_table, t_table, m[:, columns], inner), gain_sum, columns)

    each_block(width, block)


def second_backward_kernel(
    notes, saved, received, weights, mixed, q, mean, inverse, g_table, x_table, grad_x, scaled, sum_a, sum_b
):
    own, width = grad_x.shape
    slot, length, first = looked_up(notes, BACK1)
    pieces = [(saved.at[1], 0, own)]
    edge = (mixed.shape[0] - own) // 2
    mask = frame_mask(own, first, length)
    sum_a[...] = jnp.zeros_like(sum_a)
    sum_b[...] = jnp.zeros_like(sum_b)

    def block(columns):
        first_pass(
            pieces, mean, inverse, slot_row(weights, slot), mask, (g_table, x_table), mixed[:, columns], q[:, columns],
            columns, scaled, sum_a, sum_b,
        )

    each_block(width, block)
    last_pass([(received, edge, own)], pieces, mean, inverse, scaled, sum_a, sum_b, grad_x)


def first_forward_kernel(reach, notes, act, near, far, weights, masked, q, m_table, c_table, out, halo, halos):
    own, width = act.shape
    middle = reach // 2
    slot, length, first = looked_up(notes, AHEAD0)
    left, right = sorted_halos(near, far, reach, halos)
    inner = [(left, middle, middle), (act, 0, own), (right, 0, middle)]
    norm_halo(left, right, own, slot_row(weights, slot), first, length, halo)

    def block(columns):
        conv = transform(c_table, product(transform(m_table, joined(halo, masked, columns)), q[:, columns]))
        out[:, columns] = (window(inner, columns).astype(F32) + conv * sigmoid(conv)).astype(BF16)

    each_block(width, block)


def second_forward_kernel(notes, between, received, m_table, q_table, c_table, out, masked):
    own, width = out.shape
    rows = between.shape[0]
    edge = (rows - own) // 2
    slot, length, first = looked_up(notes, AHEAD0)
    last = received.shape[0] - 1

    def gain(columns):
        return received[last : last + 1, columns].astype(F32)

    norm_pieces([(between, 0, rows)], gain, first - edge, length, masked)

    def block(columns):
        q = tap_spectrum(q_table[...], received[rows:, columns])
        conv = transform(c_table, product(transform(m_table, masked[:, columns]), q))
        out[:, columns] = (between[edge : edge + own, columns].astype(F32) + conv * sigmoid(conv)).astype(BF16)

    each_block(width, block)


def pack_kernel(reaches, saved, grad, near, far, ready, sems):
    own = grad.shape[1]
    even = lax.rem(lax.axis_index("tm") + 1, 2)
    copies = []
    at = 0
    for x, reach in zip((saved, grad), reaches):
        for out, tail in ((near, even), (far, 1 - even)):
            start = pl.multiple_of(tail * (own - reach), 16)
            copies.append(
                pltpu.make_async_copy(
                    x.at[0, pl.ds(start, reach)], out.at[pl.ds(at, reach)], sems.at[len(copies)]
                )
            )
        at += reach
    ready[...] = jnp.zeros_like(ready)
    for copy in copies:
        copy.start()
    for copy in copies:
        copy.wait()


def final_kernel(slots, mine0, other0, mine1, other1, act, grad, act_out, grad_out, taps, gains, sems):
    copies = [
        pltpu.make_async_copy(act, act_out, sems.at[0]),
        pltpu.make_async_copy(grad, grad_out, sems.at[1]),
    ]
    for copy in copies:
        copy.start()
    section = lax.axis_index("section")
    count = taps.shape[0]
    total0 = mine0[...].astype(F32) + other0[...].astype(F32)
    total1 = mine1[...].astype(F32) + other1[...].astype(F32)
    for slot in range(taps.shape[1]):
        use0 = (slots[0, section] == slot).astype(F32)
        use1 = (slots[1, section] == slot).astype(F32)
        total = use0 * total0 + use1 * total1
        taps[:, slot, :] = total[:count]
        gains[slot : slot + 1, :] = total[count:]
    for copy in copies:
        copy.wait()


def span(reach, own):
    return np.arange(-reach, own + reach)


VMEM = pl.BlockSpec(memory_space=pltpu.VMEM)
SMEM = pl.BlockSpec(memory_space=pltpu.SMEM)
ANY = pl.BlockSpec(memory_space=pl.ANY)
HBM = pl.BlockSpec(memory_space=pltpu.HBM)
LIMIT = 24 * 1024 * 1024
FULL = 127 * 512 * 1024


def call(kernel, outs, scratch, operands, micros, specs=None, out_specs=None, limit=LIMIT):
    if specs is None:
        specs = [SMEM if x.dtype == jnp.int32 else VMEM for x in operands]
    return pl.pallas_call(
        kernel,
        out_shape=outs,
        in_specs=specs,
        out_specs=jax.tree.map(lambda _: VMEM, outs) if out_specs is None else out_specs,
        scratch_shapes=scratch,
        compiler_params=pltpu.CompilerParams(vmem_limit_bytes=limit),
        cost_estimate=pl.CostEstimate(flops=int(micros * 1e9), bytes_accessed=0, transcendentals=0),
    )(*operands)


def like(rows, width, dtype):
    return jax.ShapeDtypeStruct((rows, width), dtype)


def up16(count):
    return -(-count // 16) * 16


def local(
    act_in, grad_in, saved_inputs, kernels, norm_gains,
    forward_lengths, backward_lengths, forward_slots, backward_slots,
):
    sections = lax.axis_size("section")
    shards = lax.axis_size("tm")
    act, grad, saved = act_in[0], grad_in[0], saved_inputs[0]
    own, width = act.shape
    tap_count = kernels.shape[2]
    half = (tap_count - 1) // 2
    one, two, three = up16(half), up16(2 * half), up16(3 * half)
    large, size, small = own + 2 * three, own + 2 * two, own + 2 * one

    def shifted(x, by):
        return lax.ppermute(x, "section", [(i, (i + by) % sections) for i in range(sections)])

    def swapped(near, far):
        results = []
        for x, begin in ((near, 0), (far, 1)):
            pairs = [(i, i + 1) for i in range(begin, shards - 1, 2)]
            results.append(lax.ppermute(x, "tm", pairs + [(b, a) for a, b in pairs]))
        return results

    near0, far0, ready = call(
        functools.partial(pack_kernel, (three, two)),
        (like(three + two, width, BF16), like(three + two, width, BF16), like(8, LANES, F32)),
        [pltpu.SemaphoreType.DMA((4,))],
        (saved, grad_in),
        0, [HBM] * 2, None, FULL,
    )
    near0, far0 = swapped(near0, far0)
    tap_back = np.concatenate([from_freq(size, np.arange(tap_count) - half), np.zeros((1, size))], axis=0)
    m_table = stacked(to_freq(size, span(two, own)))
    q_table = tap_freq(size, tap_count)
    c_table = stacked(from_freq(size, span(one, own)))
    go_table = beside(to_freq(size, np.arange(own)))
    t_table = stacked(tap_back)

    def run(kernel, outs, scratch, operands, micros=0):
        return call(kernel, outs, scratch, [jnp.asarray(x) for x in operands], micros)

    rows = [pltpu.VMEM((own, width), F32)] + [pltpu.VMEM((own, LANES), F32)] * 2
    forward_slots, backward_slots = forward_slots.T, backward_slots.T

    def layer(size):
        return like(own, width, BF16), like(own, LANES, F32), like(own, LANES, F32), like(size, width, F32)

    weights, later, near1, far1, notes, *layer0 = call(
        functools.partial(prepare_kernel, two),
        (
            jax.ShapeDtypeStruct((kernels.shape[1], tap_count + 1, width), BF16), like(tap_count + 1, width, BF16),
            like(2 * two, width, BF16), like(2 * two, width, BF16), jax.ShapeDtypeStruct((8,), jnp.int32), *layer(large),
        ),
        [],
        [
            backward_lengths, forward_lengths, backward_slots, forward_slots,
            kernels[0].transpose(1, 0, 2), norm_gains[0], saved, act, ready, jnp.asarray(tap_freq(large, tap_count)),
        ],
        0,
        None, (VMEM,) * 4 + (SMEM,) + (VMEM,) * 4,
    )
    near1, far1 = swapped(near1, far1)
    grad_mid, halo0, inner0, gain0 = run(
        functools.partial(first_backward_kernel, (three, two, one)),
        (
            like(small + tap_count + 1, width, BF16),
            like(2 * three, width, BF16), like(own, width, BF16), like(1, width, F32),
        ),
        [
            pltpu.VMEM((2, three, width), BF16), pltpu.VMEM((2, two, width), BF16),
            pltpu.VMEM((small, LANES), F32), pltpu.VMEM((small, LANES), F32),
            pltpu.VMEM((small, width), F32), pltpu.VMEM((small, LANES), F32), pltpu.VMEM((small, LANES), F32),
        ],
        [
            notes, saved, near0, far0, grad, weights, later, *layer0,
            stacked(to_freq(large, span(three, own))), stacked(from_freq(large, span(two, own))),
            stacked(to_freq(large, span(two, own))), stacked(from_freq(large, span(one, own))),
        ],
        4,
    )
    grad_mid = shifted(grad_mid, -1)
    layers = run(
        prepare_later_kernel, (*layer(size), *layer(size)), [], [notes, saved, act, weights, q_table], 0
    )
    masked1, mean1, inverse1, q1, masked2, _, _, q2 = layers
    taps0 = run(
        functools.partial(first_taps_kernel, two), like(tap_count + 1, width, BF16), [],
        [halo0, layer0[0], inner0, gain0, m_table, go_table, t_table],
        0,
    )
    halo_scratch = [pltpu.VMEM((2 * two, width), BF16), pltpu.VMEM((2, two, width), BF16)]
    between = run(
        functools.partial(first_forward_kernel, two),
        like(small, width, BF16),
        halo_scratch,
        [notes, act, near1, far1, weights, masked2, q2, m_table, c_table],
        5,
    )
    m1, factor1, conv1 = run(
        functools.partial(second_ready_kernel, two),
        (like(size, width, F32), like(small, width, F32), like(own, width, F32)),
        halo_scratch,
        [notes, near1, far1, weights, masked1, q1, m_table, c_table],
        1,
    )
    act_out = run(
        second_forward_kernel,
        like(own, width, BF16),
        [pltpu.VMEM((small, width), BF16)],
        [
            notes, between, grad_mid,
            stacked(to_freq(small, span(one, own))), tap_freq(small, tap_count), stacked(from_freq(small, span(0, own))),
        ],
        3,
    )
    act_out = shifted(act_out, 2)

    def summed(x, micros):
        step = 1
        while True:
            other = lax.ppermute(x, "tm", [(i, i ^ step) for i in range(shards)])
            step *= 2
            if step >= shards:
                return x, other
            x = call(add_kernel, like(*x.shape, BF16), [], (x, other), micros)

    mine0, other0 = summed(taps0, 0)
    mixed1, taps1 = run(
        second_taps_kernel,
        (like(small, width, BF16), like(tap_count + 1, width, BF16)),
        [],
        [notes, grad_mid, weights, m1, factor1, conv1, other0, go_table, t_table],
        2,
    )
    grad_out = run(
        second_backward_kernel,
        like(own, width, BF16),
        rows,
        [
            notes, saved, grad_mid, weights, mixed1, q1, mean1, inverse1,
            stacked(to_freq(size, span(one, own))), stacked(from_freq(size, span(0, own))),
        ],
        6,
    )
    grad_out = shifted(grad_out, -1)
    sums = (mine0, other0) + summed(taps1, 6)
    slots = kernels.shape[1]
    act_out, grad_out, taps, gains = call(
        final_kernel,
        (
            like(own, width, BF16), like(own, width, BF16),
            jax.ShapeDtypeStruct((tap_count, slots, width), F32), like(slots, width, F32),
        ),
        [pltpu.SemaphoreType.DMA((2,))],
        (backward_slots, *sums, act_out, grad_out),
        0, [SMEM] + [VMEM] * 4 + [ANY] * 2, (ANY, ANY, VMEM, VMEM),
    )
    return act_out[None], grad_out[None], taps.transpose(1, 0, 2)[None], gains[None]


def solution(mesh):
    in_specs = (
        P("section", "tm", None),
        P("section", "tm", None),
        P("section", None, "tm", None),
        P("section", None, None, None),
        P("section", None, None),
        P(),
        P(),
        P(),
        P(),
    )
    out_specs = (
        P("section", "tm", None),
        P("section", "tm", None),
        P("section", None, None, None),
        P("section", None, None),
    )
    return jax.shard_map(local, mesh=mesh, in_specs=in_specs, out_specs=out_specs, check_vma=False)
```

time: 80.8 us -> 69.7 us (0.86)
  starting transfers between devices: 29.2 us -> 19.8 us
  local copies, waits for them, and re-layouts: 6.73 us -> 3.07 us
  Pallas kernels: 31.7 us -> 33.7 us
    ppermute x6 -> x4, starting transfers between devices: 18.8 us -> 7.14 us  [swapped(): results.append(lax.ppermute(x, 'tm', pairs + [(b, a) for a, b in pairs]))]
    unnamed x44 -> x54, local copies, waits for them, and re-layouts: 6.73 us -> 3.07 us
    pallas_call x12 -> x13, Pallas kernels: 31.7 us -> 33.7 us  [call(): pl.pallas_call(kernel, out_shape=outs, in_specs=specs, out_specs=jax.tree...]
    ppermute x3, starting transfers between devices: 2.92 us -> 4.18 us  [shifted(): lax.ppermute(x, 'section', [(i, (i + by) % sections) for i in range(secti...]
    ppermute x4, starting transfers between devices: 7.55 us -> 8.48 us  [summed(): other = lax.ppermute(x, 'tm', [(i, i ^ step) for i in range(shards)])]
  transfers between devices with their start and end apart: 13 -> 11, of which waited for: 4 -> 3; matrix products, arithmetic and copies ran while one was open for 0% -> 0% of each run, Pallas kernels for 34% -> 42%
where the time goes in v5:
time: 69.7 us; the launch traced here: 69.4 us
  Pallas kernels  33.7 us (48%)
  starting transfers between devices  19.8 us (28%)
  waiting for transfers between devices  11.8 us (17%)
  local copies, waits for them, and re-layouts  3.07 us (4%)
  between operations  1.06 us (2%)
    pallas_call x13, Pallas kernels, call(): pl.pallas_call(kernel, out_shape=outs, in_specs=specs, out_specs=jax.tree...  33.7 us
    ppermute x3, waiting for transfers between devices, shifted(): lax.ppermute(x, 'section', [(i, (i + by) % sections) for i in range(secti...  8.53 us
    ppermute x4, starting transfers between devices, summed(): other = lax.ppermute(x, 'tm', [(i, i ^ step) for i in range(shards)])  8.48 us
    ppermute x4, starting transfers between devices, swapped(): results.append(lax.ppermute(x, 'tm', pairs + [(b, a) for a, b in pairs]))  7.14 us
    ppermute x3, starting transfers between devices, shifted(): lax.ppermute(x, 'section', [(i, (i + by) % sections) for i in range(secti...  4.18 us
    ppermute x4, waiting for transfers between devices, summed(): other = lax.ppermute(x, 'tm', [(i, i ^ step) for i in range(shards)])  3.26 us
    unnamed x54, local copies, waits for them, and re-layouts  3.07 us
  transfers between devices with their start and end apart: 11, of which 3 were waited for; matrix products, arithmetic and copies ran while one was open for 0% of the time, Pallas kernels for 42%

profile of v5, /device:TPU:1, one launch (start us, length us, event | category | flops | bytes accessed | tf_op | source)
XLA Modules:
  0.0 69.4 jit_solution(17748415987788009851)
XLA Ops:
  0.6 0.0 copy-start.8
  0.7 2.1 %shard_map.255 = (bf16[80,2048]{1,0:T(8,128)(2,1)}, bf16[80,2048]{1,0:T(8,128)(2,1)}, f32[8,128]{1,0:T(8,128)}) custom-call(bf16[2,128,2048]{2,1,0:T(8,128)(2,1)} %bitcast.15, bf16[1,128,2048]{2,1,0:T(8,128)(2,1)} %grad.1), custom_call_target="tpu_custom_call" | custom-call | tf_op jit(solution)/shard_map/pallas_call | solution.py:490
  2.8 2.1 %collective-permute-start = (bf16[80,2048]{1,0:T(8,128)(2,1)}, bf16[80,2048]{1,0:T(8,128)(2,1)S(1)}, u32[]{:S(2)}, u32[]{:S(2)}) collective-permute-start(bf16[80,2048]{1,0:T(8,128)(2,1)} %get-tuple-element.37), channel_id=1, source_target_pairs={{0,1},{2,3},{1,0},{3,2},{4,5},{6,7},{5,4},{7,6},{8,9},{10,11},{9,8... | collective-permute-start | bytes 983048 | tf_op jit(solution)/shard_map/ppermute | solution.py:529
  4.9 0.7 collective-permute-start.1
  5.7 1.2 %copy-done = bf16[1,2,128,2048]{3,2,1,0:T(8,128)(2,1)S(1)} copy-done((bf16[1,2,128,2048]{3,2,1,0:T(8,128)(2,1)S(1)}, bf16[1,2,128,2048]{3,2,1,0:T(8,128)(2,1)}, u32[]{:S(2)}) %copy-start) | copy-done | bytes 1048600
  6.9 1.0 %copy-done.2 = bf16[1,128,2048]{2,1,0:T(8,128)(2,1)S(1)} copy-done((bf16[1,128,2048]{2,1,0:T(8,128)(2,1)S(1)}, bf16[1,128,2048]{2,1,0:T(8,128)(2,1)}, u32[]{:S(2)}) %copy-start.2) | copy-done | bytes 524312
  8.0 0.7 copy-done.12
  8.7 0.0 copy-start.23
  8.7 2.9 %shard_map.256 = (bf16[2,32,2048]{2,1,0:T(8,128)(2,1)S(1)}, bf16[32,2048]{1,0:T(8,128)(2,1)S(1)}, bf16[64,2048]{1,0:T(8,128)(2,1)S(1)}, bf16[64,2048]{1,0:T(8,12...) custom-call(s32[8]{0:T(128)S(1)} %copy-done.15, ...), custom_call_target="tpu_custom_call" | custom-call | tf_op jit(solution)/shard_map/pallas_call | solution.py:490
  11.5 3.7 %collective-permute-start.5 = (bf16[64,2048]{1,0:T(8,128)(2,1)S(1)}, bf16[64,2048]{1,0:T(8,128)(2,1)S(1)}, u32[]{:S(2)}, u32[]{:S(2)}) collective-permute-start(bf16[64,2048]{1,0:T(8,128)(2,1)S(1)} %get-tuple-element.49), channel_id=1, source_target_pairs={{0,1},{2,3},{1,0},{3,2},{4,5},{6,7},{5,4},{7,6},{8,9},{10,11},{9,8... | collective-permute-start | bytes 786440 | tf_op jit(solution)/shard_map/ppermute | solution.py:529
  15.2 0.7 collective-permute-start.6
  16.0 0.0 copy-start.9
  16.0 6.2 %shard_map.257 = (bf16[192,2048]{1,0:T(8,128)(2,1)S(1)}, bf16[96,2048]{1,0:T(8,128)(2,1)S(1)}, bf16[128,2048]{1,0:T(8,128)(2,1)S(1)}, f32[1,2048]{1,0:T(1,128)S(1)}) custom-call(s32[8]{0:T(128)S(1)} %get-tuple-element.36.notes, bf16[2,128,2048]{2,1,0:T(8,128)(2,1)S(1)} %bitcast.17, bf16[80,2048]{1,0:T(8,128)(2,1)S(1)} %collective-permute-done.near, ...), custom_call_target="tpu_custom_call" | custom-call | flops 4000000000 | tf_op jit(solution)/shard_map/pallas_call | solution.py:490
  22.2 0.0 copy-start.7
  22.3 1.6 %collective-permute-start.4 = (bf16[192,2048]{1,0:T(8,128)(2,1)S(1)}, bf16[192,2048]{1,0:T(8,128)(2,1)S(1)}, u32[]{:S(2)}, u32[]{:S(2)}) collective-permute-start(bf16[192,2048]{1,0:T(8,128)(2,1)S(1)} %get-tuple-element.48), channel_id=1, source_target_pairs={{0,28},{4,0},{8,4},{12,8},{16,12},{20,16},{24,20},{28,24},{1,29},{... | collective-permute-start | bytes 2359304 | tf_op jit(solution)/shard_map/ppermute | solution.py:523
  23.9 3.4 %shard_map.260 = (bf16[128,2048]{1,0:T(8,128)(2,1)S(1)}, f32[128,128]{1,0:T(8,128)S(1)}, f32[128,128]{1,0:T(8,128)S(1)}, f32[192,2048]{1,0:T(8,128)S(1)}, bf16[1...) custom-call(s32[8]{0:T(128)S(1)} %get-tuple-element.36.notes, ...), custom_call_target="tpu_custom_call" | custom-call | tf_op jit(solution)/shard_map/pallas_call | solution.py:490
  27.3 1.9 %shard_map.258.mine = bf16[32,2048]{1,0:T(8,128)(2,1)S(1)} custom-call(bf16[96,2048]{1,0:T(8,128)(2,1)S(1)} %get-tuple-element.45.halo, bf16[128,2048]{1,0:T(8,128)(2,1)S(1)} %get-tuple-element.41.own_masked.masked, bf16[128,2048]{1,0:T(8,128)(2,1)S(1)} %get-tuple-element.46.inner, f32[1,2048]{1,0:T(1,128)S(1)} %get-tuple-element.47.gain_sum, ...), custom_call_target="tpu_custom_call" | custom-call | tf_op jit(solution)/shard_map/pallas_call | solution.py:490
  29.2 7.0 %collective-permute-start.2 = (bf16[32,2048]{1,0:T(8,128)(2,1)S(1)}, bf16[32,2048]{1,0:T(8,128)(2,1)S(1)}, u32[]{:S(2)}, u32[]{:S(2)}) collective-permute-start(bf16[32,2048]{1,0:T(8,128)(2,1)S(1)} %shard_map.258.mine), channel_id=1, source_target_pairs={{0,1},{1,0},{2,3},{3,2},{4,5},{5,4},{6,7},{7,6},{8,9},{9,8},{10,11... | collective-permute-start | bytes 393224 | tf_op jit(solution)/shard_map/ppermute | solution.py:629
  36.2 3.1 %shard_map.264.between = bf16[160,2048]{1,0:T(8,128)(2,1)S(1)} custom-call(s32[8]{0:T(128)S(1)} %get-tuple-element.36.notes, bf16[128,2048]{1,0:T(8,128)(2,1)S(1)} %bitcast.22, bf16[64,2048]{1,0:T(8,128)(2,1)S(1)} %collective-permute-done.5.near, bf16[64,2048]{1,0:T(8,128)(2,1)S(1)} %collective-permute-done.6.far, ...), custom_call_target="tpu_custom_call" | custom-call | flops 5000000000 | tf_op jit(solution)/shard_map/pallas_call | solution.py:490
  39.3 3.2 %shard_map.261 = (f32[192,2048]{1,0:T(8,128)S(1)}, f32[160,2048]{1,0:T(8,128)S(1)}, f32[128,2048]{1,0:T(8,128)S(1)}) custom-call(s32[8]{0:T(128)S(1)} %get-tuple-element.36.notes, bf16[64,2048]{1,0:T(8,128)(2,1)S(1)} %collective-permute-done.5.near, bf16[64,2048]{1,0:T(8,128)(2,1)S(1)} %collective-permute-done.6.far, ...), custom_call_target="tpu_custom_call" | custom-call | flops 1000000000 | tf_op jit(solution)/shard_map/pallas_call | solution.py:490
  42.5 0.1 collective-permute-start.3
  42.7 3.2 %shard_map.265 = bf16[128,2048]{1,0:T(8,128)(2,1)S(1)} custom-call(s32[8]{0:T(128)S(1)} %get-tuple-element.36.notes, bf16[160,2048]{1,0:T(8,128)(2,1)S(1)} %shard_map.264.between, bf16[192,2048]{1,0:T(8,128)(2,1)S(1)} %collective-permute-done.4.received, bf16[320,160]{1,0:T(8,128)(2,1)S(1)} %copy-done.21, bf16[160,64]{1,0:T(8,128)(2,1)S(1)} %copy-done.26, ...), custom_call_target="tpu_custom_call" | custom-call | flops 3000000000 | tf_op jit(solution)/shard_map/pallas_call | solution.py:490
  45.9 1.4 %collective-permute-start.9 = (bf16[128,2048]{1,0:T(8,128)(2,1)S(1)}, bf16[128,2048]{1,0:T(8,128)(2,1)S(1)}, u32[]{:S(2)}, u32[]{:S(2)}) collective-permute-start(bf16[128,2048]{1,0:T(8,128)(2,1)S(1)} %shard_map.265), channel_id=1, source_target_pairs={{0,8},{4,12},{8,16},{12,20},{16,24},{20,28},{24,0},{28,4},{1,9},{5... | collective-permute-start | bytes 1572872 | tf_op jit(solution)/shard_map/ppermute | solution.py:523
  47.3 2.3 %shard_map.262 = (bf16[160,2048]{1,0:T(8,128)(2,1)S(1)}, bf16[32,2048]{1,0:T(8,128)(2,1)S(1)}) custom-call(s32[8]{0:T(128)S(1)} %get-tuple-element.36.notes, bf16[192,2048]{1,0:T(8,128)(2,1)S(1)} %collective-permute-done.4.received, bf16[2,32,2048]{2,1,0:T(8,128)(2,1)S(1)} %get-tuple-element.39.weights, f32[192,2048]{1,0:T(8,128)S(1)} %get-tuple-element.53.m, ...), custom_call_target="tpu_custom_call" | custom-call | flops 2000000000 | tf_op jit(solution)/shard_map/pallas_call | solution.py:490
  49.6 0.5 collective-permute-start.7
  50.1 3.0 %shard_map.266 = bf16[128,2048]{1,0:T(8,128)(2,1)S(1)} custom-call(s32[8]{0:T(128)S(1)} %get-tuple-element.36.notes, bf16[2,128,2048]{2,1,0:T(8,128)(2,1)S(1)} %bitcast.19, bf16[192,2048]{1,0:T(8,128)(2,1)S(1)} %collective-permute-done.4.received, bf16[2,32,2048]{2,1,0:T(8,128)(2,1)S(1)} %get-tuple-element.39.weights, ...), custom_call_target="tpu_custom_call" | custom-call | flops 6000000000 | tf_op jit(solution)/shard_map/pallas_call | solution.py:490
  53.1 1.2 %collective-permute-start.10 = (bf16[128,2048]{1,0:T(8,128)(2,1)S(1)}, bf16[128,2048]{1,0:T(8,128)(2,1)S(1)}, u32[]{:S(2)}, u32[]{:S(2)}) collective-permute-start(bf16[128,2048]{1,0:T(8,128)(2,1)S(1)} %shard_map.266), channel_id=1, source_target_pairs={{0,28},{4,0},{8,4},{12,8},{16,12},{20,16},{24,20},{28,24},{1,29},{... | collective-permute-start | bytes 1572872 | tf_op jit(solution)/shard_map/ppermute | solution.py:523
  54.4 0.9 %collective-permute-start.8 = (bf16[32,2048]{1,0:T(8,128)(2,1)S(1)}, bf16[32,2048]{1,0:T(8,128)(2,1)S(1)}, u32[]{:S(2)}, u32[]{:S(2)}) collective-permute-start(bf16[32,2048]{1,0:T(8,128)(2,1)S(1)} %shard_map.263.mine1), channel_id=1, source_target_pairs={{0,2},{1,3},{2,0},{3,1},{4,6},{5,7},{6,4},{7,5},{8,10},{9,11},{10,... | collective-permute-start | bytes 393224 | tf_op jit(solution)/shard_map/ppermute | solution.py:629
  55.3 3.3 %collective-permute-done.8.other1 = bf16[32,2048]{1,0:T(8,128)(2,1)S(1)} collective-permute-done((bf16[32,2048]{1,0:T(8,128)(2,1)S(1)}, bf16[32,2048]{1,0:T(8,128)(2,1)S(1)}, u32[]{:S(2)}, u32[]{:S(2)}) %collective-permute-start.8) | collective-permute-done | bytes 131104 | tf_op jit(solution)/shard_map/ppermute | solution.py:629
  58.6 1.5 %collective-permute-done.9.act = bf16[128,2048]{1,0:T(8,128)(2,1)S(1)} collective-permute-done((bf16[128,2048]{1,0:T(8,128)(2,1)S(1)}, bf16[128,2048]{1,0:T(8,128)(2,1)S(1)}, u32[]{:S(2)}, u32[]{:S(2)}) %collective-permute-start.9) | collective-permute-done | bytes 524320 | tf_op jit(solution)/shard_map/ppermute | solution.py:523
  60.0 7.1 %collective-permute-done.10.grad = bf16[128,2048]{1,0:T(8,128)(2,1)S(1)} collective-permute-done((bf16[128,2048]{1,0:T(8,128)(2,1)S(1)}, bf16[128,2048]{1,0:T(8,128)(2,1)S(1)}, u32[]{:S(2)}, u32[]{:S(2)}) %collective-permute-start.10) | collective-permute-done | bytes 524320 | tf_op jit(solution)/shard_map/ppermute | solution.py:523
  67.1 2.3 %shard_map.267 = (bf16[128,2048]{1,0:T(8,128)(2,1)}, bf16[128,2048]{1,0:T(8,128)(2,1)}, f32[31,2,2048]{2,1,0:T(2,128)}, f32[2,2048]{1,0:T(2,128)}) custom-call(s32[2,8]{1,0:T(2,128)S(1)} %bitcast.27, bf16[32,2048]{1,0:T(8,128)(2,1)S(1)} %shard_map.259.mine0, bf16[32,2048]{1,0:T(8,128)(2,1)S(1)} %collective-permute-done.3.ready.other0, ...), custom_call_target="tpu_custom_call" | custom-call | tf_op jit(solution)/shard_map/pallas_call | solution.py:490
  (57 shorter events, 0.2 us)
Async XLA Ops:
  0.6 5.0 %copy-start.8 = (bf16[224,64]{1,0:T(8,128)(2,1)S(1)}, bf16[224,64]{1,0:T(8,128)(2,1)}, u32[]{:S(2)}) copy-start(bf16[224,64]{1,0:T(8,128)(2,1)} %constant.30.clone.q_table) | copy-start | bytes 86020
  0.6 5.0 %copy-start.13 = (s32[8,2]{0,1:T(2,128)S(1)}, s32[8,2]{0,1:T(2,128)}, u32[]{:S(2)}) copy-start(s32[8,2]{0,1:T(2,128)} %param.32) | copy-start | bytes 196
  0.7 5.0 %copy-start.14 = (s32[8,2]{0,1:T(2,128)S(1)}, s32[8,2]{0,1:T(2,128)}, u32[]{:S(2)}) copy-start(s32[8,2]{0,1:T(2,128)} %param.31) | copy-start | bytes 196
  0.7 5.0 %copy-start.15 = (s32[8]{0:T(128)S(1)}, s32[8]{0:T(128)}, u32[]{:S(2)}) copy-start(s32[8]{0:T(128)} %back_lengths.1) | copy-start | bytes 100
  0.7 5.0 %copy-start.16 = (s32[8]{0:T(128)S(1)}, s32[8]{0:T(128)}, u32[]{:S(2)}) copy-start(s32[8]{0:T(128)} %ahead_lengths.1) | copy-start | bytes 100
  0.7 5.0 %copy-start.11 = (bf16[1,2,2048]{2,1,0:T(2,128)(2,1)S(1)}, bf16[1,2,2048]{2,1,0:T(2,128)(2,1)}, u32[]{:S(2)}) copy-start(bf16[1,2,2048]{2,1,0:T(2,128)(2,1)} %param.28) | copy-start | bytes 24580
  0.7 5.0 %copy-start.5 = (bf16[1,2,31,2048]{3,1,2,0:T(2,128)(2,1)S(1)}, bf16[1,2,31,2048]{3,1,2,0:T(2,128)(2,1)}, u32[]{:S(2)}) copy-start(bf16[1,2,31,2048]{3,1,2,0:T(2,128)(2,1)} %param.27) | copy-start | bytes 761860
  2.8 13.1 %collective-permute-start = (bf16[80,2048]{1,0:T(8,128)(2,1)}, bf16[80,2048]{1,0:T(8,128)(2,1)S(1)}, u32[]{:S(2)}, u32[]{:S(2)}) collective-permute-start(bf16[80,2048]{1,0:T(8,128)(2,1)} %get-tuple-element.37), channel_id=1, source_target_pairs={{0,1},{2,3},{1,0},{3,2},{4,5},{6,7},{5,4},{7,6},{8,9},{10,11},{9,8... | collective-permute-start | bytes 983048 | tf_op jit(solution)/shard_map/ppermute | solution.py:529
  4.9 11.0 %collective-permute-start.1 = (bf16[80,2048]{1,0:T(8,128)(2,1)}, bf16[80,2048]{1,0:T(8,128)(2,1)S(1)}, u32[]{:S(2)}, u32[]{:S(2)}) collective-permute-start(bf16[80,2048]{1,0:T(8,128)(2,1)} %get-tuple-element.38), channel_id=1, source_target_pairs={{1,2},{2,1},{5,6},{6,5},{9,10},{10,9},{13,14},{14,13},{17,18},{18,... | collective-permute-start | bytes 983048 | tf_op jit(solution)/shard_map/ppermute | solution.py:529
  8.6 7.3 %copy-start.4 = (bf16[1,128,2048]{2,1,0:T(8,128)(2,1)S(1)}, bf16[1,128,2048]{2,1,0:T(8,128)(2,1)}, u32[]{:S(2)}) copy-start(bf16[1,128,2048]{2,1,0:T(8,128)(2,1)} %grad.1) | copy-start | bytes 1572868
  8.6 7.3 %copy-start.17 = (bf16[448,192]{1,0:T(8,128)(2,1)S(1)}, bf16[448,192]{1,0:T(8,128)(2,1)}, u32[]{:S(2)}) copy-start(bf16[448,192]{1,0:T(8,128)(2,1)} %constant.33.clone.g_table) | copy-start | bytes 516100
  8.6 7.3 %copy-start.18 = (bf16[448,224]{1,0:T(8,128)(2,1)S(1)}, bf16[448,224]{1,0:T(8,128)(2,1)}, u32[]{:S(2)}) copy-start(bf16[448,224]{1,0:T(8,128)(2,1)} %constant.31.clone.m_table) | copy-start | bytes 602116
  8.6 7.3 %copy-start.20 = (bf16[384,224]{1,0:T(8,128)(2,1)S(1)}, bf16[384,224]{1,0:T(8,128)(2,1)}, u32[]{:S(2)}) copy-start(bf16[384,224]{1,0:T(8,128)(2,1)} %constant.32.clone.c_table) | copy-start | bytes 516100
  8.7 7.3 %copy-start.23 = (bf16[320,224]{1,0:T(8,128)(2,1)S(1)}, bf16[320,224]{1,0:T(8,128)(2,1)}, u32[]{:S(2)}) copy-start(bf16[320,224]{1,0:T(8,128)(2,1)} %constant.34.clone.x_table) | copy-start | bytes 430084
  11.5 24.6 %collective-permute-start.5 = (bf16[64,2048]{1,0:T(8,128)(2,1)S(1)}, bf16[64,2048]{1,0:T(8,128)(2,1)S(1)}, u32[]{:S(2)}, u32[]{:S(2)}) collective-permute-start(bf16[64,2048]{1,0:T(8,128)(2,1)S(1)} %get-tuple-element.49), channel_id=1, source_target_pairs={{0,1},{2,3},{1,0},{3,2},{4,5},{6,7},{5,4},{7,6},{8,9},{10,11},{9,8... | collective-permute-start | bytes 786440 | tf_op jit(solution)/shard_map/ppermute | solution.py:529
  15.2 20.9 %collective-permute-start.6 = (bf16[64,2048]{1,0:T(8,128)(2,1)S(1)}, bf16[64,2048]{1,0:T(8,128)(2,1)S(1)}, u32[]{:S(2)}, u32[]{:S(2)}) collective-permute-start(bf16[64,2048]{1,0:T(8,128)(2,1)S(1)} %get-tuple-element.50), channel_id=1, source_target_pairs={{1,2},{2,1},{5,6},{6,5},{9,10},{10,9},{13,14},{14,13},{17,18},{18,... | collective-permute-start | bytes 786440 | tf_op jit(solution)/shard_map/ppermute | solution.py:529
  16.0 7.9 %copy-start.3 = (bf16[1,128,2048]{2,1,0:T(8,128)(2,1)S(1)}, bf16[1,128,2048]{2,1,0:T(8,128)(2,1)}, u32[]{:S(2)}) copy-start(bf16[1,128,2048]{2,1,0:T(8,128)(2,1)} %param.24) | copy-start | bytes 1572868
  16.0 7.9 %copy-start.9 = (bf16[192,64]{1,0:T(8,128)(2,1)S(1)}, bf16[192,64]{1,0:T(8,128)(2,1)}, u32[]{:S(2)}) copy-start(bf16[192,64]{1,0:T(8,128)(2,1)} %constant.35.clone.q_table) | copy-start | bytes 73732
  22.2 5.0 %copy-start.6 = (bf16[384,192]{1,0:T(8,128)(2,1)S(1)}, bf16[384,192]{1,0:T(8,128)(2,1)}, u32[]{:S(2)}) copy-start(bf16[384,192]{1,0:T(8,128)(2,1)} %constant.36.clone.m_table) | copy-start | bytes 442372
  22.2 5.0 %copy-start.7 = (bf16[192,256]{1,0:T(8,128)(2,1)S(1)}, bf16[192,256]{1,0:T(8,128)(2,1)}, u32[]{:S(2)}) copy-start(bf16[192,256]{1,0:T(8,128)(2,1)} %constant.37.clone.go_table) | copy-start | bytes 294916
  22.2 5.0 %copy-start.10 = (bf16[64,192]{1,0:T(8,128)(2,1)S(1)}, bf16[64,192]{1,0:T(8,128)(2,1)}, u32[]{:S(2)}) copy-start(bf16[64,192]{1,0:T(8,128)(2,1)} %constant.38.clone.t_table) | copy-start | bytes 73732
  22.3 13.9 %copy-start.22 = (bf16[320,192]{1,0:T(8,128)(2,1)S(1)}, bf16[320,192]{1,0:T(8,128)(2,1)}, u32[]{:S(2)}) copy-start(bf16[320,192]{1,0:T(8,128)(2,1)} %constant.39.clone.c_table) | copy-start | bytes 368644
  22.3 20.4 %collective-permute-start.4 = (bf16[192,2048]{1,0:T(8,128)(2,1)S(1)}, bf16[192,2048]{1,0:T(8,128)(2,1)S(1)}, u32[]{:S(2)}, u32[]{:S(2)}) collective-permute-start(bf16[192,2048]{1,0:T(8,128)(2,1)S(1)} %get-tuple-element.48), channel_id=1, source_target_pairs={{0,28},{4,0},{8,4},{12,8},{16,12},{20,16},{24,20},{28,24},{1,29},{... | collective-permute-start | bytes 2359304 | tf_op jit(solution)/shard_map/ppermute | solution.py:523
  29.2 13.3 %collective-permute-start.2 = (bf16[32,2048]{1,0:T(8,128)(2,1)S(1)}, bf16[32,2048]{1,0:T(8,128)(2,1)S(1)}, u32[]{:S(2)}, u32[]{:S(2)}) collective-permute-start(bf16[32,2048]{1,0:T(8,128)(2,1)S(1)} %shard_map.258.mine), channel_id=1, source_target_pairs={{0,1},{1,0},{2,3},{3,2},{4,5},{5,4},{6,7},{7,6},{8,9},{9,8},{10,11... | collective-permute-start | bytes 393224 | tf_op jit(solution)/shard_map/ppermute | solution.py:629
  39.3 3.4 %copy-start.21 = (bf16[320,160]{1,0:T(8,128)(2,1)S(1)}, bf16[320,160]{1,0:T(8,128)(2,1)}, u32[]{:S(2)}) copy-start(bf16[320,160]{1,0:T(8,128)(2,1)} %constant.40.clone.m_table) | copy-start | bytes 307204
  39.3 3.4 %copy-start.25 = (bf16[256,160]{1,0:T(8,128)(2,1)S(1)}, bf16[256,160]{1,0:T(8,128)(2,1)}, u32[]{:S(2)}) copy-start(bf16[256,160]{1,0:T(8,128)(2,1)} %constant.42.clone.c_table) | copy-start | bytes 245764
  39.3 3.4 %copy-start.26 = (bf16[160,64]{1,0:T(8,128)(2,1)S(1)}, bf16[160,64]{1,0:T(8,128)(2,1)}, u32[]{:S(2)}) copy-start(bf16[160,64]{1,0:T(8,128)(2,1)} %constant.41.clone.q_table) | copy-start | bytes 61444
  42.5 4.7 %collective-permute-start.3 = (bf16[32,2048]{1,0:T(8,128)(2,1)S(1)}, bf16[32,2048]{1,0:T(8,128)(2,1)S(1)}, u32[]{:S(2)}, u32[]{:S(2)}) collective-permute-start(bf16[32,2048]{1,0:T(8,128)(2,1)S(1)} %shard_map.259.mine0), channel_id=1, source_target_pairs={{0,2},{1,3},{2,0},{3,1},{4,6},{5,7},{6,4},{7,5},{8,10},{9,11},{10,... | collective-permute-start | bytes 393224 | tf_op jit(solution)/shard_map/ppermute | solution.py:629
  45.9 14.1 %collective-permute-start.9 = (bf16[128,2048]{1,0:T(8,128)(2,1)S(1)}, bf16[128,2048]{1,0:T(8,128)(2,1)S(1)}, u32[]{:S(2)}, u32[]{:S(2)}) collective-permute-start(bf16[128,2048]{1,0:T(8,128)(2,1)S(1)} %shard_map.265), channel_id=1, source_target_pairs={{0,8},{4,12},{8,16},{12,20},{16,24},{20,28},{24,0},{28,4},{1,9},{5... | collective-permute-start | bytes 1572872 | tf_op jit(solution)/shard_map/ppermute | solution.py:523
  49.6 4.8 %collective-permute-start.7 = (bf16[32,2048]{1,0:T(8,128)(2,1)S(1)}, bf16[32,2048]{1,0:T(8,128)(2,1)S(1)}, u32[]{:S(2)}, u32[]{:S(2)}) collective-permute-start(bf16[32,2048]{1,0:T(8,128)(2,1)S(1)} %get-tuple-element.56.mine), channel_id=1, source_target_pairs={{0,1},{1,0},{2,3},{3,2},{4,5},{5,4},{6,7},{7,6},{8,9},{9,8},{10,11... | collective-permute-start | bytes 393224 | tf_op jit(solution)/shard_map/ppermute | solution.py:629
  53.1 14.0 %collective-permute-start.10 = (bf16[128,2048]{1,0:T(8,128)(2,1)S(1)}, bf16[128,2048]{1,0:T(8,128)(2,1)S(1)}, u32[]{:S(2)}, u32[]{:S(2)}) collective-permute-start(bf16[128,2048]{1,0:T(8,128)(2,1)S(1)} %shard_map.266), channel_id=1, source_target_pairs={{0,28},{4,0},{8,4},{12,8},{16,12},{20,16},{24,20},{28,24},{1,29},{... | collective-permute-start | bytes 1572872 | tf_op jit(solution)/shard_map/ppermute | solution.py:523
  54.4 4.2 %collective-permute-start.8 = (bf16[32,2048]{1,0:T(8,128)(2,1)S(1)}, bf16[32,2048]{1,0:T(8,128)(2,1)S(1)}, u32[]{:S(2)}, u32[]{:S(2)}) collective-permute-start(bf16[32,2048]{1,0:T(8,128)(2,1)S(1)} %shard_map.263.mine1), channel_id=1, source_target_pairs={{0,2},{1,3},{2,0},{3,1},{4,6},{5,7},{6,4},{7,5},{8,10},{9,11},{10,... | collective-permute-start | bytes 393224 | tf_op jit(solution)/shard_map/ppermute | solution.py:629
  (6 other events, 11.4 us)

commit v6 on v5

--- a/solution.py
+++ b/solution.py
@@ -113,7 +113,7 @@
         inverse_ref[out, :] = inverse
 
 
-def norm_pieces(pieces, gain, first, length, masked_ref, mean_ref=None, inverse_ref=None, chunk=64):
+def norm_pieces(pieces, gain, first, length, masked_ref, mean_ref=None, inverse_ref=None, chunk=128):
     at = 0
     for ref, start, count in pieces:
         for begin in range(0, count, chunk):
@@ -130,11 +130,8 @@
 
 
 def each_block(width, body):
-    def step(i, _):
-        body(pl.ds(pl.multiple_of(i * BLOCK, BLOCK), BLOCK))
-        return 0
-
-    lax.fori_loop(0, width // BLOCK, step, 0)
+    for begin in range(0, width, BLOCK):
+        body(pl.ds(begin, BLOCK))
 
 
 def tap_spectrum(table, weights):
@@ -181,7 +178,7 @@
     return weighted
 
 
-def last_pass(grad_pieces, pieces, mean, inverse, scaled, sum_a, sum_b, grad_x, chunk=64):
+def last_pass(grad_pieces, pieces, mean, inverse, scaled, sum_a, sum_b, grad_x, chunk=128):
     width = scaled.shape[1]
     at = 0
     for (ref, start, count), (saved, base, _) in zip(grad_pieces, pieces):
@@ -247,11 +244,14 @@
     each_block(width, block)
 
 
-def prepare_later_kernel(notes, saved, act, weights, q_table, *outs):
+def prepare_later_kernel(notes, saved, act, weights, ready, q_table, *outs):
     own, width = act.shape
-    for x, layer, (masked, mean, inverse, q) in ((saved.at[1], BACK1, outs[:4]), (act, AHEAD0, outs[4:])):
+    layers = ((saved.at[1], BACK1, outs[:4]), (act, AHEAD0, outs[4:]))
+    for x, layer, (masked, mean, inverse, _) in layers:
         slot, length, first = looked_up(notes, layer)
         norm_pieces([(x, 0, own)], slot_row(weights, slot), first, length, masked, mean, inverse)
+    for _, layer, (_, _, _, q) in layers:
+        slot = notes[layer]
 
         def block(columns, slot=slot, q=q):
             q[:, columns] = tap_spectrum(q_table[...], weights[slot, :, columns])
@@ -271,7 +271,7 @@
 
 
 def first_backward_kernel(
-    reaches, notes, saved, near, far, grads, weights, later, own_masked, own_mean, own_inverse, q,
+    reaches, notes, saved, near, far, grads, weights, own_masked, own_mean, own_inverse, q,
     m_table, c_table, g_table, x_table,
     grad_x, halo, inner, gain_sum, halos, grad_halos, all_mean, all_inverse, scaled, sum_a, sum_b,
 ):
@@ -296,7 +296,6 @@
     mask = frame_mask(own + 2 * out_reach, first - out_reach, length)
     sum_a[...] = jnp.zeros_like(sum_a)
     sum_b[...] = jnp.zeros_like(sum_b)
-    grad_x[pl.ds(own + 2 * out_reach, later.shape[0]), :] = later[...]
 
     def block(columns):
         m = transform(m_table, joined(halo, own_masked, columns))
@@ -358,9 +357,12 @@
     each_block(width, block)
 
 
-def second_taps_kernel(notes, received, weights, m, factor, conv, ready, go_table, t_table, mixed_out, taps):
+def second_taps_kernel(notes, received, weights, m, factor, conv, taps0, go_table, t_table, mixed_out, taps):
     own, width = conv.shape
     rows = factor.shape[0]
+    count = taps0.shape[0]
+    taps[pl.ds(0, count), :] = taps0[...]
+    taps1 = taps.at[pl.ds(count, count)]
     edge = (rows - own) // 2
     gain = slot_row(weights, notes[BACK1])
 
@@ -369,7 +371,7 @@
         mixed_out[:, columns] = mixed
         inner = mixed[edge : edge + own]
         gain_sum = jnp.sum(inner.astype(F32) * conv[:, columns], axis=0, keepdims=True) / gain(columns)
-        put_taps(taps, tap_term(go_table, t_table, m[:, columns], inner), gain_sum, columns)
+        put_taps(taps1, tap_term(go_table, t_table, m[:, columns], inner), gain_sum, columns)
 
     each_block(width, block)
 
@@ -410,20 +412,20 @@
     each_block(width, block)
 
 
-def second_forward_kernel(notes, between, received, m_table, q_table, c_table, out, masked):
+def second_forward_kernel(notes, between, later, m_table, q_table, c_table, out, masked):
     own, width = out.shape
     rows = between.shape[0]
     edge = (rows - own) // 2
     slot, length, first = looked_up(notes, AHEAD0)
-    last = received.shape[0] - 1
+    last = later.shape[0] - 1
 
     def gain(columns):
-        return received[last : last + 1, columns].astype(F32)
-
-    norm_pieces([(between, 0, rows)], gain, first - edge, length, masked)
-
-    def block(columns):
-        q = tap_spectrum(q_table[...], received[rows:, columns])
+        return later[last : last + 1, columns].astype(F32)
+
+    norm_pieces([(between, 0, rows)], gain, first - edge, length, masked, chunk=rows // 2)
+
+    def block(columns):
+        q = tap_spectrum(q_table[...], later[:, columns])
         conv = transform(c_table, product(transform(m_table, masked[:, columns]), q))
         out[:, columns] = (between[edge : edge + own, columns].astype(F32) + conv * sigmoid(conv)).astype(BF16)
 
@@ -451,25 +453,19 @@
         copy.wait()
 
 
-def final_kernel(slots, mine0, other0, mine1, other1, act, grad, act_out, grad_out, taps, gains, sems):
-    copies = [
-        pltpu.make_async_copy(act, act_out, sems.at[0]),
-        pltpu.make_async_copy(grad, grad_out, sems.at[1]),
-    ]
-    for copy in copies:
-        copy.start()
+def final_kernel(slots, mine, other, act, act_out, taps, gains, sem):
+    copy = pltpu.make_async_copy(act, act_out, sem)
+    copy.start()
     section = lax.axis_index("section")
     count = taps.shape[0]
-    total0 = mine0[...].astype(F32) + other0[...].astype(F32)
-    total1 = mine1[...].astype(F32) + other1[...].astype(F32)
+    total = mine[...].astype(F32) + other[...].astype(F32)
+    ticks = total[: count + 1], total[count + 1 :]
     for slot in range(taps.shape[1]):
-        use0 = (slots[0, section] == slot).astype(F32)
-        use1 = (slots[1, section] == slot).astype(F32)
-        total = use0 * total0 + use1 * total1
-        taps[:, slot, :] = total[:count]
-        gains[slot : slot + 1, :] = total[count:]
-    for copy in copies:
-        copy.wait()
+        use = [(slots[tick, section] == slot).astype(F32) for tick in range(2)]
+        both = use[0] * ticks[0] + use[1] * ticks[1]
+        taps[:, slot, :] = both[:count]
+        gains[slot : slot + 1, :] = both[count:]
+    copy.wait()
 
 
 def span(reach, own):
@@ -567,11 +563,12 @@
         0,
         None, (VMEM,) * 4 + (SMEM,) + (VMEM,) * 4,
     )
+    later = shifted(later, -1)
     near1, far1 = swapped(near1, far1)
     grad_mid, halo0, inner0, gain0 = run(
         functools.partial(first_backward_kernel, (three, two, one)),
         (
-            like(small + tap_count + 1, width, BF16),
+            like(small, width, BF16),
             like(2 * three, width, BF16), like(own, width, BF16), like(1, width, F32),
         ),
         [
@@ -580,7 +577,7 @@
             pltpu.VMEM((small, width), F32), pltpu.VMEM((small, LANES), F32), pltpu.VMEM((small, LANES), F32),
         ],
         [
-            notes, saved, near0, far0, grad, weights, later, *layer0,
+            notes, saved, near0, far0, grad, weights, *layer0,
             stacked(to_freq(large, span(three, own))), stacked(from_freq(large, span(two, own))),
             stacked(to_freq(large, span(two, own))), stacked(from_freq(large, span(one, own))),
         ],
@@ -588,7 +585,7 @@
     )
     grad_mid = shifted(grad_mid, -1)
     layers = run(
-        prepare_later_kernel, (*layer(size), *layer(size)), [], [notes, saved, act, weights, q_table], 0
+        prepare_later_kernel, (*layer(size), *layer(size)), [], [notes, saved, act, weights, gain0, q_table], 0
     )
     masked1, mean1, inverse1, q1, masked2, _, _, q2 = layers
     taps0 = run(
@@ -602,21 +599,21 @@
         like(small, width, BF16),
         halo_scratch,
         [notes, act, near1, far1, weights, masked2, q2, m_table, c_table],
-        5,
+        3,
     )
     m1, factor1, conv1 = run(
         functools.partial(second_ready_kernel, two),
         (like(size, width, F32), like(small, width, F32), like(own, width, F32)),
         halo_scratch,
         [notes, near1, far1, weights, masked1, q1, m_table, c_table],
-        1,
+        3,
     )
     act_out = run(
         second_forward_kernel,
         like(own, width, BF16),
         [pltpu.VMEM((small, width), BF16)],
         [
-            notes, between, grad_mid,
+            notes, between, later,
             stacked(to_freq(small, span(one, own))), tap_freq(small, tap_count), stacked(from_freq(small, span(0, own))),
         ],
         3,
@@ -632,12 +629,11 @@
                 return x, other
             x = call(add_kernel, like(*x.shape, BF16), [], (x, other), micros)
 
-    mine0, other0 = summed(taps0, 0)
-    mixed1, taps1 = run(
+    mixed1, sums = run(
         second_taps_kernel,
-        (like(small, width, BF16), like(tap_count + 1, width, BF16)),
+        (like(small, width, BF16), like(2 * (tap_count + 1), width, BF16)),
         [],
-        [notes, grad_mid, weights, m1, factor1, conv1, other0, go_table, t_table],
+        [notes, grad_mid, weights, m1, factor1, conv1, taps0, go_table, t_table],
         2,
     )
     grad_out = run(
@@ -651,17 +647,17 @@
         6,
     )
     grad_out = shifted(grad_out, -1)
-    sums = (mine0, other0) + summed(taps1, 6)
+    sums = summed(sums, 6)
     slots = kernels.shape[1]
-    act_out, grad_out, taps, gains = call(
+    act_out, taps, gains = call(
         final_kernel,
         (
-            like(own, width, BF16), like(own, width, BF16),
+            like(own, width, BF16),
             jax.ShapeDtypeStruct((tap_count, slots, width), F32), like(slots, width, F32),
         ),
-        [pltpu.SemaphoreType.DMA((2,))],
-        (backward_slots, *sums, act_out, grad_out),
-        0, [SMEM] + [VMEM] * 4 + [ANY] * 2, (ANY, ANY, VMEM, VMEM),
+        [pltpu.SemaphoreType.DMA],
+        (backward_slots, *sums, act_out),
+        0, [SMEM] + [VMEM] * 2 + [ANY], (ANY, VMEM, VMEM),
     )
     return act_out[None], grad_out[None], taps.transpose(1, 0, 2)[None], gains[None]
 

time: 69.7 us -> 62.4 us (0.90)
  the two profiles are of different devices: /device:TPU:1 before, /device:TPU:0 now
where the time goes in v6:
time: 62.4 us; the launch traced here: 62.1 us
  Pallas kernels  27.3 us (44%)
  starting transfers between devices  21.8 us (35%)
  waiting for transfers between devices  8.01 us (13%)
  local copies, waits for them, and re-layouts  3.88 us (6%)
  between operations  1.07 us (2%)
    pallas_call x12, Pallas kernels, call(): pl.pallas_call(kernel, out_shape=outs, in_specs=specs, out_specs=jax.tree...  27.3 us
    ppermute x4, starting transfers between devices, swapped(): results.append(lax.ppermute(x, 'tm', pairs + [(b, a) for a, b in pairs]))  8.27 us
    ppermute x2, starting transfers between devices, summed(): other = lax.ppermute(x, 'tm', [(i, i ^ step) for i in range(shards)])  7.76 us
    ppermute x4, starting transfers between devices, shifted(): lax.ppermute(x, 'section', [(i, (i + by) % sections) for i in range(secti...  5.82 us
    ppermute x2, waiting for transfers between devices, summed(): other = lax.ppermute(x, 'tm', [(i, i ^ step) for i in range(shards)])  4.55 us
    unnamed x55, local copies, waits for them, and re-layouts  3.88 us
    ppermute x4, waiting for transfers between devices, shifted(): lax.ppermute(x, 'section', [(i, (i + by) % sections) for i in range(secti...  3.45 us
  transfers between devices with their start and end apart: 10, of which 3 were waited for; matrix products, arithmetic and copies ran while one was open for 0% of the time, Pallas kernels for 37%

profile of v6, /device:TPU:0, one launch (start us, length us, event | category | flops | bytes accessed | tf_op | source)
XLA Modules:
  0.0 62.1 jit_solution(790736193137914031)
XLA Ops:
  0.6 0.0 copy-start.8
  0.7 2.1 %shard_map.255 = (bf16[80,2048]{1,0:T(8,128)(2,1)}, bf16[80,2048]{1,0:T(8,128)(2,1)}, f32[8,128]{1,0:T(8,128)}) custom-call(bf16[2,128,2048]{2,1,0:T(8,128)(2,1)} %bitcast.15, bf16[1,128,2048]{2,1,0:T(8,128)(2,1)} %grad.1), custom_call_target="tpu_custom_call" | custom-call | tf_op jit(solution)/shard_map/pallas_call | solution.py:486
  2.8 3.0 %collective-permute-start = (bf16[80,2048]{1,0:T(8,128)(2,1)}, bf16[80,2048]{1,0:T(8,128)(2,1)S(1)}, u32[]{:S(2)}, u32[]{:S(2)}) collective-permute-start(bf16[80,2048]{1,0:T(8,128)(2,1)} %get-tuple-element.36), channel_id=1, source_target_pairs={{0,1},{2,3},{1,0},{3,2},{4,5},{6,7},{5,4},{7,6},{8,9},{10,11},{9,8... | collective-permute-start | bytes 983048 | tf_op jit(solution)/shard_map/ppermute | solution.py:525
  5.8 0.7 %collective-permute-start.1 = (bf16[80,2048]{1,0:T(8,128)(2,1)}, bf16[80,2048]{1,0:T(8,128)(2,1)S(1)}, u32[]{:S(2)}, u32[]{:S(2)}) collective-permute-start(bf16[80,2048]{1,0:T(8,128)(2,1)} %get-tuple-element.37), channel_id=1, source_target_pairs={{1,2},{2,1},{5,6},{6,5},{9,10},{10,9},{13,14},{14,13},{17,18},{18,... | collective-permute-start | bytes 983048 | tf_op jit(solution)/shard_map/ppermute | solution.py:525
  6.6 1.2 %copy-done = bf16[1,2,128,2048]{3,2,1,0:T(8,128)(2,1)S(1)} copy-done((bf16[1,2,128,2048]{3,2,1,0:T(8,128)(2,1)S(1)}, bf16[1,2,128,2048]{3,2,1,0:T(8,128)(2,1)}, u32[]{:S(2)}) %copy-start) | copy-done | bytes 1048600
  7.8 1.0 %copy-done.2 = bf16[1,128,2048]{2,1,0:T(8,128)(2,1)S(1)} copy-done((bf16[1,128,2048]{2,1,0:T(8,128)(2,1)S(1)}, bf16[1,128,2048]{2,1,0:T(8,128)(2,1)}, u32[]{:S(2)}) %copy-start.2) | copy-done | bytes 524312
  8.9 0.7 %copy-done.12 = f32[8,128]{1,0:T(8,128)S(1)} copy-done((f32[8,128]{1,0:T(8,128)S(1)}, f32[8,128]{1,0:T(8,128)}, u32[]{:S(2)}) %copy-start.12) | copy-done | bytes 4120
  9.5 0.0 copy-start.23
  9.6 2.2 %shard_map.256 = (bf16[2,32,2048]{2,1,0:T(8,128)(2,1)S(1)}, bf16[32,2048]{1,0:T(8,128)(2,1)S(1)}, bf16[64,2048]{1,0:T(8,128)(2,1)S(1)}, bf16[64,2048]{1,0:T(8,12...) custom-call(s32[8]{0:T(128)S(1)} %copy-done.15, ...), custom_call_target="tpu_custom_call" | custom-call | tf_op jit(solution)/shard_map/pallas_call | solution.py:486
  11.8 2.8 %collective-permute-start.7 = (bf16[32,2048]{1,0:T(8,128)(2,1)S(1)}, bf16[32,2048]{1,0:T(8,128)(2,1)S(1)}, u32[]{:S(2)}, u32[]{:S(2)}) collective-permute-start(bf16[32,2048]{1,0:T(8,128)(2,1)S(1)} %get-tuple-element.57), channel_id=1, source_target_pairs={{0,28},{4,0},{8,4},{12,8},{16,12},{20,16},{24,20},{28,24},{1,29},{... | collective-permute-start | bytes 393224 | tf_op jit(solution)/shard_map/ppermute | solution.py:519
  14.6 3.9 %collective-permute-start.3 = (bf16[64,2048]{1,0:T(8,128)(2,1)S(1)}, bf16[64,2048]{1,0:T(8,128)(2,1)S(1)}, u32[]{:S(2)}, u32[]{:S(2)}) collective-permute-start(bf16[64,2048]{1,0:T(8,128)(2,1)S(1)} %get-tuple-element.44), channel_id=1, source_target_pairs={{0,1},{2,3},{1,0},{3,2},{4,5},{6,7},{5,4},{7,6},{8,9},{10,11},{9,8... | collective-permute-start | bytes 786440 | tf_op jit(solution)/shard_map/ppermute | solution.py:525
  18.5 0.7 %collective-permute-start.4 = (bf16[64,2048]{1,0:T(8,128)(2,1)S(1)}, bf16[64,2048]{1,0:T(8,128)(2,1)S(1)}, u32[]{:S(2)}, u32[]{:S(2)}) collective-permute-start(bf16[64,2048]{1,0:T(8,128)(2,1)S(1)} %get-tuple-element.45), channel_id=1, source_target_pairs={{1,2},{2,1},{5,6},{6,5},{9,10},{10,9},{13,14},{14,13},{17,18},{18,... | collective-permute-start | bytes 786440 | tf_op jit(solution)/shard_map/ppermute | solution.py:525
  19.3 0.0 copy-start.9
  19.3 5.4 %shard_map.257 = (bf16[160,2048]{1,0:T(8,128)(2,1)S(1)}, bf16[96,2048]{1,0:T(8,128)(2,1)S(1)}, bf16[128,2048]{1,0:T(8,128)(2,1)S(1)}, f32[1,2048]{1,0:T(1,128)S(1)}) custom-call(s32[8]{0:T(128)S(1)} %get-tuple-element.35.notes, bf16[2,128,2048]{2,1,0:T(8,128)(2,1)S(1)} %bitcast.17, bf16[80,2048]{1,0:T(8,128)(2,1)S(1)} %collective-permute-done.near, ...), custom_call_target="tpu_custom_call" | custom-call | flops 4000000000 | tf_op jit(solution)/shard_map/pallas_call | solution.py:486
  24.8 1.0 %collective-permute-start.2 = (bf16[160,2048]{1,0:T(8,128)(2,1)S(1)}, bf16[160,2048]{1,0:T(8,128)(2,1)S(1)}, u32[]{:S(2)}, u32[]{:S(2)}) collective-permute-start(bf16[160,2048]{1,0:T(8,128)(2,1)S(1)} %get-tuple-element.43), channel_id=1, source_target_pairs={{0,28},{4,0},{8,4},{12,8},{16,12},{20,16},{24,20},{28,24},{1,29},{... | collective-permute-start | bytes 1966088 | tf_op jit(solution)/shard_map/ppermute | solution.py:519
  25.8 2.2 %shard_map.258 = (bf16[128,2048]{1,0:T(8,128)(2,1)S(1)}, f32[128,128]{1,0:T(8,128)S(1)}, f32[128,128]{1,0:T(8,128)S(1)}, f32[192,2048]{1,0:T(8,128)S(1)}, bf16[1...) custom-call(s32[8]{0:T(128)S(1)} %get-tuple-element.35.notes, ...), custom_call_target="tpu_custom_call" | custom-call | tf_op jit(solution)/shard_map/pallas_call | solution.py:486
  28.1 2.4 %shard_map.263.between = bf16[160,2048]{1,0:T(8,128)(2,1)S(1)} custom-call(s32[8]{0:T(128)S(1)} %get-tuple-element.35.notes, bf16[128,2048]{1,0:T(8,128)(2,1)S(1)} %bitcast.22, bf16[64,2048]{1,0:T(8,128)(2,1)S(1)} %collective-permute-done.3.near, bf16[64,2048]{1,0:T(8,128)(2,1)S(1)} %collective-permute-done.4.far, ...), custom_call_target="tpu_custom_call" | custom-call | flops 3000000000 | tf_op jit(solution)/shard_map/pallas_call | solution.py:486
  30.6 2.5 %shard_map.264 = bf16[128,2048]{1,0:T(8,128)(2,1)S(1)} custom-call(s32[8]{0:T(128)S(1)} %get-tuple-element.35.notes, bf16[160,2048]{1,0:T(8,128)(2,1)S(1)} %shard_map.263.between, bf16[32,2048]{1,0:T(8,128)(2,1)S(1)} %collective-permute-done.7.later, bf16[320,160]{1,0:T(8,128)(2,1)S(1)} %copy-done.22, bf16[160,64]{1,0:T(8,128)(2,1)S(1)} %copy-done.26, ...), custom_call_target="tpu_custom_call" | custom-call | flops 3000000000 | tf_op jit(solution)/shard_map/pallas_call | solution.py:486
  33.1 1.6 %collective-permute-start.8 = (bf16[128,2048]{1,0:T(8,128)(2,1)S(1)}, bf16[128,2048]{1,0:T(8,128)(2,1)S(1)}, u32[]{:S(2)}, u32[]{:S(2)}) collective-permute-start(bf16[128,2048]{1,0:T(8,128)(2,1)S(1)} %shard_map.264), channel_id=1, source_target_pairs={{0,8},{4,12},{8,16},{12,20},{16,24},{20,28},{24,0},{28,4},{1,9},{5... | collective-permute-start | bytes 1572872 | tf_op jit(solution)/shard_map/ppermute | solution.py:519
  34.7 1.5 %shard_map.260.taps0 = bf16[32,2048]{1,0:T(8,128)(2,1)S(1)} custom-call(bf16[96,2048]{1,0:T(8,128)(2,1)S(1)} %get-tuple-element.52.halo, bf16[128,2048]{1,0:T(8,128)(2,1)S(1)} %get-tuple-element.39.own_masked.masked, bf16[128,2048]{1,0:T(8,128)(2,1)S(1)} %get-tuple-element.53.inner, f32[1,2048]{1,0:T(1,128)S(1)} %get-tuple-element.46.ready.gain_sum, ...), custom_call_target="tpu_custom_call" | custom-call | tf_op jit(solution)/shard_map/pallas_call | solution.py:486
  36.2 2.5 %shard_map.259 = (f32[192,2048]{1,0:T(8,128)S(1)}, f32[160,2048]{1,0:T(8,128)S(1)}, f32[128,2048]{1,0:T(8,128)S(1)}) custom-call(s32[8]{0:T(128)S(1)} %get-tuple-element.35.notes, bf16[64,2048]{1,0:T(8,128)(2,1)S(1)} %collective-permute-done.3.near, bf16[64,2048]{1,0:T(8,128)(2,1)S(1)} %collective-permute-done.4.far, ...), custom_call_target="tpu_custom_call" | custom-call | flops 3000000000 | tf_op jit(solution)/shard_map/pallas_call | solution.py:486
  38.8 1.8 %shard_map.261 = (bf16[160,2048]{1,0:T(8,128)(2,1)S(1)}, bf16[64,2048]{1,0:T(8,128)(2,1)S(1)}) custom-call(s32[8]{0:T(128)S(1)} %get-tuple-element.35.notes, bf16[160,2048]{1,0:T(8,128)(2,1)S(1)} %collective-permute-done.2.received, bf16[2,32,2048]{2,1,0:T(8,128)(2,1)S(1)} %get-tuple-element.38.weights, f32[192,2048]{1,0:T(8,128)S(1)} %get-tuple-element.49.m, ...), custom_call_target="tpu_custom_call" | custom-call | flops 2000000000 | tf_op jit(solution)/shard_map/pallas_call | solution.py:486
  40.5 6.9 %collective-permute-start.5 = (bf16[64,2048]{1,0:T(8,128)(2,1)S(1)}, bf16[64,2048]{1,0:T(8,128)(2,1)S(1)}, u32[]{:S(2)}, u32[]{:S(2)}) collective-permute-start(bf16[64,2048]{1,0:T(8,128)(2,1)S(1)} %get-tuple-element.54.mine), channel_id=1, source_target_pairs={{0,1},{1,0},{2,3},{3,2},{4,5},{5,4},{6,7},{7,6},{8,9},{9,8},{10,11... | collective-permute-start | bytes 786440 | tf_op jit(solution)/shard_map/ppermute | solution.py:626
  47.5 2.4 %shard_map.266 = bf16[128,2048]{1,0:T(8,128)(2,1)S(1)} custom-call(s32[8]{0:T(128)S(1)} %get-tuple-element.35.notes, bf16[2,128,2048]{2,1,0:T(8,128)(2,1)S(1)} %bitcast.19, bf16[160,2048]{1,0:T(8,128)(2,1)S(1)} %collective-permute-done.2.received, bf16[2,32,2048]{2,1,0:T(8,128)(2,1)S(1)} %get-tuple-element.38.weights, ...), custom_call_target="tpu_custom_call" | custom-call | flops 6000000000 | tf_op jit(solution)/shard_map/pallas_call | solution.py:486
  49.9 0.4 collective-permute-start.9
  50.3 2.4 %collective-permute-done.5.other = bf16[64,2048]{1,0:T(8,128)(2,1)S(1)} collective-permute-done((bf16[64,2048]{1,0:T(8,128)(2,1)S(1)}, bf16[64,2048]{1,0:T(8,128)(2,1)S(1)}, u32[]{:S(2)}, u32[]{:S(2)}) %collective-permute-start.5) | collective-permute-done | bytes 262176 | tf_op jit(solution)/shard_map/ppermute | solution.py:626
  52.6 0.1 shard_map.262.mine
  52.7 0.8 %collective-permute-start.6 = (bf16[64,2048]{1,0:T(8,128)(2,1)S(1)}, bf16[64,2048]{1,0:T(8,128)(2,1)S(1)}, u32[]{:S(2)}, u32[]{:S(2)}) collective-permute-start(bf16[64,2048]{1,0:T(8,128)(2,1)S(1)} %shard_map.262.mine), channel_id=1, source_target_pairs={{0,2},{1,3},{2,0},{3,1},{4,6},{5,7},{6,4},{7,5},{8,10},{9,11},{10,... | collective-permute-start | bytes 786440 | tf_op jit(solution)/shard_map/ppermute | solution.py:626
  53.5 3.4 %collective-permute-done.9 = bf16[128,2048]{1,0:T(8,128)(2,1)S(1)} collective-permute-done((bf16[128,2048]{1,0:T(8,128)(2,1)S(1)}, bf16[128,2048]{1,0:T(8,128)(2,1)S(1)}, u32[]{:S(2)}, u32[]{:S(2)}) %collective-permute-start.9) | collective-permute-done | bytes 524320 | tf_op jit(solution)/shard_map/ppermute | solution.py:519
  57.0 2.2 %collective-permute-done.6.other = bf16[64,2048]{1,0:T(8,128)(2,1)S(1)} collective-permute-done((bf16[64,2048]{1,0:T(8,128)(2,1)S(1)}, bf16[64,2048]{1,0:T(8,128)(2,1)S(1)}, u32[]{:S(2)}, u32[]{:S(2)}) %collective-permute-start.6) | collective-permute-done | bytes 262176 | tf_op jit(solution)/shard_map/ppermute | solution.py:626
  59.1 2.1 %shard_map.265 = (bf16[128,2048]{1,0:T(8,128)(2,1)}, f32[31,2,2048]{2,1,0:T(2,128)}, f32[2,2048]{1,0:T(2,128)}) custom-call(s32[2,8]{1,0:T(2,128)S(1)} %bitcast.27, bf16[64,2048]{1,0:T(8,128)(2,1)S(1)} %shard_map.262.mine, bf16[64,2048]{1,0:T(8,128)(2,1)S(1)} %collective-permute-done.6.other, bf16[128,2048]{1,0:T(8,128)(2,1)S(1)} %collective-permute-done.8.act), custom_call_target="tpu_custom_call" | custom-call | tf_op jit(solution)/shard_map/pallas_call | solution.py:486
  61.3 0.8 %copy.29 = bf16[1,128,2048]{2,1,0:T(8,128)(2,1)} copy(bf16[1,128,2048]{2,1,0:T(8,128)(2,1)S(1)} %bitcast.29) | data formatting | bytes 1048576
  (55 shorter events, 0.1 us)
Async XLA Ops:
  0.6 5.9 %copy-start.8 = (bf16[224,64]{1,0:T(8,128)(2,1)S(1)}, bf16[224,64]{1,0:T(8,128)(2,1)}, u32[]{:S(2)}) copy-start(bf16[224,64]{1,0:T(8,128)(2,1)} %constant.30.clone.q_table) | copy-start | bytes 86020
  0.6 5.9 %copy-start.13 = (s32[8,2]{0,1:T(2,128)S(1)}, s32[8,2]{0,1:T(2,128)}, u32[]{:S(2)}) copy-start(s32[8,2]{0,1:T(2,128)} %param.32) | copy-start | bytes 196
  0.7 5.9 %copy-start.14 = (s32[8,2]{0,1:T(2,128)S(1)}, s32[8,2]{0,1:T(2,128)}, u32[]{:S(2)}) copy-start(s32[8,2]{0,1:T(2,128)} %param.31) | copy-start | bytes 196
  0.7 5.9 %copy-start.15 = (s32[8]{0:T(128)S(1)}, s32[8]{0:T(128)}, u32[]{:S(2)}) copy-start(s32[8]{0:T(128)} %back_lengths.1) | copy-start | bytes 100
  0.7 5.9 %copy-start.16 = (s32[8]{0:T(128)S(1)}, s32[8]{0:T(128)}, u32[]{:S(2)}) copy-start(s32[8]{0:T(128)} %ahead_lengths.1) | copy-start | bytes 100
  0.7 5.9 %copy-start.11 = (bf16[1,2,2048]{2,1,0:T(2,128)(2,1)S(1)}, bf16[1,2,2048]{2,1,0:T(2,128)(2,1)}, u32[]{:S(2)}) copy-start(bf16[1,2,2048]{2,1,0:T(2,128)(2,1)} %param.28) | copy-start | bytes 24580
  0.7 5.9 %copy-start.5 = (bf16[1,2,31,2048]{3,1,2,0:T(2,128)(2,1)S(1)}, bf16[1,2,31,2048]{3,1,2,0:T(2,128)(2,1)}, u32[]{:S(2)}) copy-start(bf16[1,2,31,2048]{3,1,2,0:T(2,128)(2,1)} %param.27) | copy-start | bytes 761860
  2.8 16.4 %collective-permute-start = (bf16[80,2048]{1,0:T(8,128)(2,1)}, bf16[80,2048]{1,0:T(8,128)(2,1)S(1)}, u32[]{:S(2)}, u32[]{:S(2)}) collective-permute-start(bf16[80,2048]{1,0:T(8,128)(2,1)} %get-tuple-element.36), channel_id=1, source_target_pairs={{0,1},{2,3},{1,0},{3,2},{4,5},{6,7},{5,4},{7,6},{8,9},{10,11},{9,8... | collective-permute-start | bytes 983048 | tf_op jit(solution)/shard_map/ppermute | solution.py:525
  5.8 13.4 %collective-permute-start.1 = (bf16[80,2048]{1,0:T(8,128)(2,1)}, bf16[80,2048]{1,0:T(8,128)(2,1)S(1)}, u32[]{:S(2)}, u32[]{:S(2)}) collective-permute-start(bf16[80,2048]{1,0:T(8,128)(2,1)} %get-tuple-element.37), channel_id=1, source_target_pairs={{1,2},{2,1},{5,6},{6,5},{9,10},{10,9},{13,14},{14,13},{17,18},{18,... | collective-permute-start | bytes 983048 | tf_op jit(solution)/shard_map/ppermute | solution.py:525
  9.5 9.7 %copy-start.4 = (bf16[1,128,2048]{2,1,0:T(8,128)(2,1)S(1)}, bf16[1,128,2048]{2,1,0:T(8,128)(2,1)}, u32[]{:S(2)}) copy-start(bf16[1,128,2048]{2,1,0:T(8,128)(2,1)} %grad.1) | copy-start | bytes 1572868
  9.5 9.7 %copy-start.17 = (bf16[448,192]{1,0:T(8,128)(2,1)S(1)}, bf16[448,192]{1,0:T(8,128)(2,1)}, u32[]{:S(2)}) copy-start(bf16[448,192]{1,0:T(8,128)(2,1)} %constant.33.clone.g_table) | copy-start | bytes 516100
  9.5 9.7 %copy-start.18 = (bf16[448,224]{1,0:T(8,128)(2,1)S(1)}, bf16[448,224]{1,0:T(8,128)(2,1)}, u32[]{:S(2)}) copy-start(bf16[448,224]{1,0:T(8,128)(2,1)} %constant.31.clone.m_table) | copy-start | bytes 602116
  9.5 9.7 %copy-start.20 = (bf16[384,224]{1,0:T(8,128)(2,1)S(1)}, bf16[384,224]{1,0:T(8,128)(2,1)}, u32[]{:S(2)}) copy-start(bf16[384,224]{1,0:T(8,128)(2,1)} %constant.32.clone.c_table) | copy-start | bytes 516100
  9.5 9.7 %copy-start.23 = (bf16[320,224]{1,0:T(8,128)(2,1)S(1)}, bf16[320,224]{1,0:T(8,128)(2,1)}, u32[]{:S(2)}) copy-start(bf16[320,224]{1,0:T(8,128)(2,1)} %constant.34.clone.x_table) | copy-start | bytes 430084
  11.8 18.7 %collective-permute-start.7 = (bf16[32,2048]{1,0:T(8,128)(2,1)S(1)}, bf16[32,2048]{1,0:T(8,128)(2,1)S(1)}, u32[]{:S(2)}, u32[]{:S(2)}) collective-permute-start(bf16[32,2048]{1,0:T(8,128)(2,1)S(1)} %get-tuple-element.57), channel_id=1, source_target_pairs={{0,28},{4,0},{8,4},{12,8},{16,12},{20,16},{24,20},{28,24},{1,29},{... | collective-permute-start | bytes 393224 | tf_op jit(solution)/shard_map/ppermute | solution.py:519
  14.6 13.4 %collective-permute-start.3 = (bf16[64,2048]{1,0:T(8,128)(2,1)S(1)}, bf16[64,2048]{1,0:T(8,128)(2,1)S(1)}, u32[]{:S(2)}, u32[]{:S(2)}) collective-permute-start(bf16[64,2048]{1,0:T(8,128)(2,1)S(1)} %get-tuple-element.44), channel_id=1, source_target_pairs={{0,1},{2,3},{1,0},{3,2},{4,5},{6,7},{5,4},{7,6},{8,9},{10,11},{9,8... | collective-permute-start | bytes 786440 | tf_op jit(solution)/shard_map/ppermute | solution.py:525
  18.5 9.5 %collective-permute-start.4 = (bf16[64,2048]{1,0:T(8,128)(2,1)S(1)}, bf16[64,2048]{1,0:T(8,128)(2,1)S(1)}, u32[]{:S(2)}, u32[]{:S(2)}) collective-permute-start(bf16[64,2048]{1,0:T(8,128)(2,1)S(1)} %get-tuple-element.45), channel_id=1, source_target_pairs={{1,2},{2,1},{5,6},{6,5},{9,10},{10,9},{13,14},{14,13},{17,18},{18,... | collective-permute-start | bytes 786440 | tf_op jit(solution)/shard_map/ppermute | solution.py:525
  19.3 6.5 %copy-start.3 = (bf16[1,128,2048]{2,1,0:T(8,128)(2,1)S(1)}, bf16[1,128,2048]{2,1,0:T(8,128)(2,1)}, u32[]{:S(2)}) copy-start(bf16[1,128,2048]{2,1,0:T(8,128)(2,1)} %param.24) | copy-start | bytes 1572868
  19.3 6.5 %copy-start.9 = (bf16[192,64]{1,0:T(8,128)(2,1)S(1)}, bf16[192,64]{1,0:T(8,128)(2,1)}, u32[]{:S(2)}) copy-start(bf16[192,64]{1,0:T(8,128)(2,1)} %constant.35.clone.q_table) | copy-start | bytes 73732
  24.7 3.3 %copy-start.6 = (bf16[384,192]{1,0:T(8,128)(2,1)S(1)}, bf16[384,192]{1,0:T(8,128)(2,1)}, u32[]{:S(2)}) copy-start(bf16[384,192]{1,0:T(8,128)(2,1)} %constant.36.clone.m_table) | copy-start | bytes 442372
  24.7 3.3 %copy-start.21 = (bf16[320,192]{1,0:T(8,128)(2,1)S(1)}, bf16[320,192]{1,0:T(8,128)(2,1)}, u32[]{:S(2)}) copy-start(bf16[320,192]{1,0:T(8,128)(2,1)} %constant.39.clone.c_table) | copy-start | bytes 368644
  24.8 13.9 %collective-permute-start.2 = (bf16[160,2048]{1,0:T(8,128)(2,1)S(1)}, bf16[160,2048]{1,0:T(8,128)(2,1)S(1)}, u32[]{:S(2)}, u32[]{:S(2)}) collective-permute-start(bf16[160,2048]{1,0:T(8,128)(2,1)S(1)} %get-tuple-element.43), channel_id=1, source_target_pairs={{0,28},{4,0},{8,4},{12,8},{16,12},{20,16},{24,20},{28,24},{1,29},{... | collective-permute-start | bytes 1966088 | tf_op jit(solution)/shard_map/ppermute | solution.py:519
  28.0 2.5 %copy-start.22 = (bf16[320,160]{1,0:T(8,128)(2,1)S(1)}, bf16[320,160]{1,0:T(8,128)(2,1)}, u32[]{:S(2)}) copy-start(bf16[320,160]{1,0:T(8,128)(2,1)} %constant.40.clone.m_table) | copy-start | bytes 307204
  30.5 4.2 %copy-start.7 = (bf16[192,256]{1,0:T(8,128)(2,1)S(1)}, bf16[192,256]{1,0:T(8,128)(2,1)}, u32[]{:S(2)}) copy-start(bf16[192,256]{1,0:T(8,128)(2,1)} %constant.37.clone.go_table) | copy-start | bytes 294916
  30.5 4.2 %copy-start.10 = (bf16[64,192]{1,0:T(8,128)(2,1)S(1)}, bf16[64,192]{1,0:T(8,128)(2,1)}, u32[]{:S(2)}) copy-start(bf16[64,192]{1,0:T(8,128)(2,1)} %constant.38.clone.t_table) | copy-start | bytes 73732
  33.1 23.9 %collective-permute-start.8 = (bf16[128,2048]{1,0:T(8,128)(2,1)S(1)}, bf16[128,2048]{1,0:T(8,128)(2,1)S(1)}, u32[]{:S(2)}, u32[]{:S(2)}) collective-permute-start(bf16[128,2048]{1,0:T(8,128)(2,1)S(1)} %shard_map.264), channel_id=1, source_target_pairs={{0,8},{4,12},{8,16},{12,20},{16,24},{20,28},{24,0},{28,4},{1,9},{5... | collective-permute-start | bytes 1572872 | tf_op jit(solution)/shard_map/ppermute | solution.py:519
  38.7 8.8 %copy-start.1 = (bf16[1,2,128,2048]{3,2,1,0:T(8,128)(2,1)S(1)}, bf16[1,2,128,2048]{3,2,1,0:T(8,128)(2,1)}, u32[]{:S(2)}) copy-start(bf16[1,2,128,2048]{3,2,1,0:T(8,128)(2,1)} %param.26) | copy-start | bytes 3145732
  38.7 8.8 %copy-start.19 = (bf16[384,160]{1,0:T(8,128)(2,1)S(1)}, bf16[384,160]{1,0:T(8,128)(2,1)}, u32[]{:S(2)}) copy-start(bf16[384,160]{1,0:T(8,128)(2,1)} %constant.43.clone.g_table) | copy-start | bytes 368644
  38.7 8.7 %copy-start.24 = (bf16[256,192]{1,0:T(8,128)(2,1)S(1)}, bf16[256,192]{1,0:T(8,128)(2,1)}, u32[]{:S(2)}) copy-start(bf16[256,192]{1,0:T(8,128)(2,1)} %constant.44.clone.x_table) | copy-start | bytes 294916
  40.5 12.1 %collective-permute-start.5 = (bf16[64,2048]{1,0:T(8,128)(2,1)S(1)}, bf16[64,2048]{1,0:T(8,128)(2,1)S(1)}, u32[]{:S(2)}, u32[]{:S(2)}) collective-permute-start(bf16[64,2048]{1,0:T(8,128)(2,1)S(1)} %get-tuple-element.54.mine), channel_id=1, source_target_pairs={{0,1},{1,0},{2,3},{3,2},{4,5},{5,4},{6,7},{7,6},{8,9},{9,8},{10,11... | collective-permute-start | bytes 786440 | tf_op jit(solution)/shard_map/ppermute | solution.py:626
  49.9 7.1 %collective-permute-start.9 = (bf16[128,2048]{1,0:T(8,128)(2,1)S(1)}, bf16[128,2048]{1,0:T(8,128)(2,1)S(1)}, u32[]{:S(2)}, u32[]{:S(2)}) collective-permute-start(bf16[128,2048]{1,0:T(8,128)(2,1)S(1)} %shard_map.266), channel_id=1, source_target_pairs={{0,28},{4,0},{8,4},{12,8},{16,12},{20,16},{24,20},{28,24},{1,29},{... | collective-permute-start | bytes 1572872 | tf_op jit(solution)/shard_map/ppermute | solution.py:519
  52.7 6.4 %collective-permute-start.6 = (bf16[64,2048]{1,0:T(8,128)(2,1)S(1)}, bf16[64,2048]{1,0:T(8,128)(2,1)S(1)}, u32[]{:S(2)}, u32[]{:S(2)}) collective-permute-start(bf16[64,2048]{1,0:T(8,128)(2,1)S(1)} %shard_map.262.mine), channel_id=1, source_target_pairs={{0,2},{1,3},{2,0},{3,1},{4,6},{5,7},{6,4},{7,5},{8,10},{9,11},{10,... | collective-permute-start | bytes 786440 | tf_op jit(solution)/shard_map/ppermute | solution.py:626
  (5 other events, 7.9 us)

commit v7 on v6

--- a/solution.py
+++ b/solution.py
@@ -10,7 +10,7 @@
 from jax.sharding import PartitionSpec as P
 
 epsilon = 1e-05
-BLOCK = 512
+BLOCK = 256
 LANES = 128
 F32 = jnp.float32
 BF16 = jnp.bfloat16
@@ -453,9 +453,13 @@
         copy.wait()
 
 
-def final_kernel(slots, mine, other, act, act_out, taps, gains, sem):
-    copy = pltpu.make_async_copy(act, act_out, sem)
-    copy.start()
+def final_kernel(slots, mine, other, act, grad, act_out, grad_out, taps, gains, sems):
+    copies = [
+        pltpu.make_async_copy(act, act_out, sems.at[0]),
+        pltpu.make_async_copy(grad, grad_out, sems.at[1]),
+    ]
+    for copy in copies:
+        copy.start()
     section = lax.axis_index("section")
     count = taps.shape[0]
     total = mine[...].astype(F32) + other[...].astype(F32)
@@ -465,7 +469,8 @@
         both = use[0] * ticks[0] + use[1] * ticks[1]
         taps[:, slot, :] = both[:count]
         gains[slot : slot + 1, :] = both[count:]
-    copy.wait()
+    for copy in copies:
+        copy.wait()
 
 
 def span(reach, own):
@@ -649,15 +654,15 @@
     grad_out = shifted(grad_out, -1)
     sums = summed(sums, 6)
     slots = kernels.shape[1]
-    act_out, taps, gains = call(
+    act_out, grad_out, taps, gains = call(
         final_kernel,
         (
-            like(own, width, BF16),
+            like(own, width, BF16), like(own, width, BF16),
             jax.ShapeDtypeStruct((tap_count, slots, width), F32), like(slots, width, F32),
         ),
-        [pltpu.SemaphoreType.DMA],
-        (backward_slots, *sums, act_out),
-        0, [SMEM] + [VMEM] * 2 + [ANY], (ANY, VMEM, VMEM),
+        [pltpu.SemaphoreType.DMA((2,))],
+        (backward_slots, *sums, act_out, grad_out),
+        0, [SMEM] + [VMEM] * 2 + [ANY] * 2, (ANY, ANY, VMEM, VMEM),
     )
     return act_out[None], grad_out[None], taps.transpose(1, 0, 2)[None], gains[None]
 

time: 62.4 us -> 69.4 us (1.11)
  Pallas kernels: 27.3 us -> 35.3 us
  local copies, waits for them, and re-layouts: 3.88 us -> 3.08 us
  starting transfers between devices: 21.8 us -> 21.1 us
    pallas_call x12, Pallas kernels: 27.3 us -> 35.3 us  [call(): pl.pallas_call(kernel, out_shape=outs, in_specs=specs, out_specs=jax.tree...]
    ppermute x2, waiting for transfers between devices: 4.55 us -> 8.42 us  [summed(): other = lax.ppermute(x, 'tm', [(i, i ^ step) for i in range(shards)])]
    ppermute x4, waiting for transfers between devices: 3.45 us -> 0.01 us  [shifted(): lax.ppermute(x, 'section', [(i, (i + by) % sections) for i in range(secti...]
    ppermute x2, starting transfers between devices: 7.76 us -> 6.8 us  [summed(): other = lax.ppermute(x, 'tm', [(i, i ^ step) for i in range(shards)])]
    unnamed x55 -> x54, local copies, waits for them, and re-layouts: 3.88 us -> 3.08 us
  transfers between devices with their start and end apart: 10 -> 10, of which waited for: 3 -> 2; matrix products, arithmetic and copies ran while one was open for 0% -> 0% of each run, Pallas kernels for 37% -> 45%
where the time goes in v7:
time: 69.4 us; the launch traced here: 69.1 us
  Pallas kernels  35.3 us (51%)
  starting transfers between devices  21.1 us (30%)
  waiting for transfers between devices  8.45 us (12%)
  local copies, waits for them, and re-layouts  3.08 us (4%)
  between operations  1.23 us (2%)
    pallas_call x12, Pallas kernels, call(): pl.pallas_call(kernel, out_shape=outs, in_specs=specs, out_specs=jax.tree...  35.3 us
    ppermute x2, waiting for transfers between devices, summed(): other = lax.ppermute(x, 'tm', [(i, i ^ step) for i in range(shards)])  8.42 us
    ppermute x4, starting transfers between devices, swapped(): results.append(lax.ppermute(x, 'tm', pairs + [(b, a) for a, b in pairs]))  8.27 us
    ppermute x2, starting transfers between devices, summed(): other = lax.ppermute(x, 'tm', [(i, i ^ step) for i in range(shards)])  6.8 us
    ppermute x4, starting transfers between devices, shifted(): lax.ppermute(x, 'section', [(i, (i + by) % sections) for i in range(secti...  5.98 us
    unnamed x54, local copies, waits for them, and re-layouts  3.08 us
  transfers between devices with their start and end apart: 10, of which 2 were waited for; matrix products, arithmetic and copies ran while one was open for 0% of the time, Pallas kernels for 45%

profile of v7, /device:TPU:0, one launch (start us, length us, event | category | flops | bytes accessed | tf_op | source)
XLA Modules:
  0.0 69.1 jit_solution(10884964096128236994)
XLA Ops:
  0.7 2.1 %shard_map.255 = (bf16[80,2048]{1,0:T(8,128)(2,1)}, bf16[80,2048]{1,0:T(8,128)(2,1)}, f32[8,128]{1,0:T(8,128)}) custom-call(bf16[2,128,2048]{2,1,0:T(8,128)(2,1)} %bitcast.15, bf16[1,128,2048]{2,1,0:T(8,128)(2,1)} %grad.1), custom_call_target="tpu_custom_call" | custom-call | tf_op jit(solution)/shard_map/pallas_call | solution.py:491
  2.8 3.0 %collective-permute-start = (bf16[80,2048]{1,0:T(8,128)(2,1)}, bf16[80,2048]{1,0:T(8,128)(2,1)S(1)}, u32[]{:S(2)}, u32[]{:S(2)}) collective-permute-start(bf16[80,2048]{1,0:T(8,128)(2,1)} %get-tuple-element.37), channel_id=1, source_target_pairs={{0,1},{2,3},{1,0},{3,2},{4,5},{6,7},{5,4},{7,6},{8,9},{10,11},{9,8... | collective-permute-start | bytes 983048 | tf_op jit(solution)/shard_map/ppermute | solution.py:530
  5.8 0.7 collective-permute-start.1
  6.6 1.2 %copy-done = bf16[1,2,128,2048]{3,2,1,0:T(8,128)(2,1)S(1)} copy-done((bf16[1,2,128,2048]{3,2,1,0:T(8,128)(2,1)S(1)}, bf16[1,2,128,2048]{3,2,1,0:T(8,128)(2,1)}, u32[]{:S(2)}) %copy-start) | copy-done | bytes 1048600
  7.8 1.0 %copy-done.2 = bf16[1,128,2048]{2,1,0:T(8,128)(2,1)S(1)} copy-done((bf16[1,128,2048]{2,1,0:T(8,128)(2,1)S(1)}, bf16[1,128,2048]{2,1,0:T(8,128)(2,1)}, u32[]{:S(2)}) %copy-start.2) | copy-done | bytes 524312
  8.9 0.7 copy-done.12
  9.5 0.0 copy-start.23
  9.6 2.2 %shard_map.256 = (bf16[2,32,2048]{2,1,0:T(8,128)(2,1)S(1)}, bf16[32,2048]{1,0:T(8,128)(2,1)S(1)}, bf16[64,2048]{1,0:T(8,128)(2,1)S(1)}, bf16[64,2048]{1,0:T(8,12...) custom-call(s32[8]{0:T(128)S(1)} %copy-done.15, ...), custom_call_target="tpu_custom_call" | custom-call | tf_op jit(solution)/shard_map/pallas_call | solution.py:491
  11.8 2.8 %collective-permute-start.7 = (bf16[32,2048]{1,0:T(8,128)(2,1)S(1)}, bf16[32,2048]{1,0:T(8,128)(2,1)S(1)}, u32[]{:S(2)}, u32[]{:S(2)}) collective-permute-start(bf16[32,2048]{1,0:T(8,128)(2,1)S(1)} %get-tuple-element.58), channel_id=1, source_target_pairs={{0,28},{4,0},{8,4},{12,8},{16,12},{20,16},{24,20},{28,24},{1,29},{... | collective-permute-start | bytes 393224 | tf_op jit(solution)/shard_map/ppermute | solution.py:524
  14.6 3.9 %collective-permute-start.3 = (bf16[64,2048]{1,0:T(8,128)(2,1)S(1)}, bf16[64,2048]{1,0:T(8,128)(2,1)S(1)}, u32[]{:S(2)}, u32[]{:S(2)}) collective-permute-start(bf16[64,2048]{1,0:T(8,128)(2,1)S(1)} %get-tuple-element.45), channel_id=1, source_target_pairs={{0,1},{2,3},{1,0},{3,2},{4,5},{6,7},{5,4},{7,6},{8,9},{10,11},{9,8... | collective-permute-start | bytes 786440 | tf_op jit(solution)/shard_map/ppermute | solution.py:530
  18.5 0.7 collective-permute-start.4
  19.3 0.0 copy-start.9
  19.3 8.1 %shard_map.257 = (bf16[160,2048]{1,0:T(8,128)(2,1)S(1)}, bf16[96,2048]{1,0:T(8,128)(2,1)S(1)}, bf16[128,2048]{1,0:T(8,128)(2,1)S(1)}, f32[1,2048]{1,0:T(1,128)S(1)}) custom-call(s32[8]{0:T(128)S(1)} %get-tuple-element.36.notes, bf16[2,128,2048]{2,1,0:T(8,128)(2,1)S(1)} %bitcast.17, bf16[80,2048]{1,0:T(8,128)(2,1)S(1)} %collective-permute-done.near, ...), custom_call_target="tpu_custom_call" | custom-call | flops 4000000000 | tf_op jit(solution)/shard_map/pallas_call | solution.py:491
  27.4 0.0 copy-start.6
  27.5 1.0 %collective-permute-start.2 = (bf16[160,2048]{1,0:T(8,128)(2,1)S(1)}, bf16[160,2048]{1,0:T(8,128)(2,1)S(1)}, u32[]{:S(2)}, u32[]{:S(2)}) collective-permute-start(bf16[160,2048]{1,0:T(8,128)(2,1)S(1)} %get-tuple-element.44), channel_id=1, source_target_pairs={{0,28},{4,0},{8,4},{12,8},{16,12},{20,16},{24,20},{28,24},{1,29},{... | collective-permute-start | bytes 1966088 | tf_op jit(solution)/shard_map/ppermute | solution.py:524
  28.5 2.2 %shard_map.258 = (bf16[128,2048]{1,0:T(8,128)(2,1)S(1)}, f32[128,128]{1,0:T(8,128)S(1)}, f32[128,128]{1,0:T(8,128)S(1)}, f32[192,2048]{1,0:T(8,128)S(1)}, bf16[1...) custom-call(s32[8]{0:T(128)S(1)} %get-tuple-element.36.notes, ...), custom_call_target="tpu_custom_call" | custom-call | tf_op jit(solution)/shard_map/pallas_call | solution.py:491
  30.7 0.0 copy-start.22
  30.8 0.0 copy-start.25
  30.8 3.5 %shard_map.263.between = bf16[160,2048]{1,0:T(8,128)(2,1)S(1)} custom-call(s32[8]{0:T(128)S(1)} %get-tuple-element.36.notes, bf16[128,2048]{1,0:T(8,128)(2,1)S(1)} %bitcast.22, bf16[64,2048]{1,0:T(8,128)(2,1)S(1)} %collective-permute-done.3.near, bf16[64,2048]{1,0:T(8,128)(2,1)S(1)} %collective-permute-done.4.far, ...), custom_call_target="tpu_custom_call" | custom-call | flops 3000000000 | tf_op jit(solution)/shard_map/pallas_call | solution.py:491
  34.4 3.5 %shard_map.264 = bf16[128,2048]{1,0:T(8,128)(2,1)S(1)} custom-call(s32[8]{0:T(128)S(1)} %get-tuple-element.36.notes, bf16[160,2048]{1,0:T(8,128)(2,1)S(1)} %shard_map.263.between, bf16[32,2048]{1,0:T(8,128)(2,1)S(1)} %collective-permute-done.7.later, bf16[320,160]{1,0:T(8,128)(2,1)S(1)} %copy-done.22, bf16[160,64]{1,0:T(8,128)(2,1)S(1)} %copy-done.26, ...), custom_call_target="tpu_custom_call" | custom-call | flops 3000000000 | tf_op jit(solution)/shard_map/pallas_call | solution.py:491
  37.8 0.2 collective-permute-start.8
  38.1 2.2 %shard_map.260.taps0 = bf16[32,2048]{1,0:T(8,128)(2,1)S(1)} custom-call(bf16[96,2048]{1,0:T(8,128)(2,1)S(1)} %get-tuple-element.53.halo, bf16[128,2048]{1,0:T(8,128)(2,1)S(1)} %get-tuple-element.40.own_masked.masked, bf16[128,2048]{1,0:T(8,128)(2,1)S(1)} %get-tuple-element.54.inner, f32[1,2048]{1,0:T(1,128)S(1)} %get-tuple-element.47.ready.gain_sum, ...), custom_call_target="tpu_custom_call" | custom-call | tf_op jit(solution)/shard_map/pallas_call | solution.py:491
  40.3 3.6 %shard_map.259 = (f32[192,2048]{1,0:T(8,128)S(1)}, f32[160,2048]{1,0:T(8,128)S(1)}, f32[128,2048]{1,0:T(8,128)S(1)}) custom-call(s32[8]{0:T(128)S(1)} %get-tuple-element.36.notes, bf16[64,2048]{1,0:T(8,128)(2,1)S(1)} %collective-permute-done.3.near, bf16[64,2048]{1,0:T(8,128)(2,1)S(1)} %collective-permute-done.4.far, ...), custom_call_target="tpu_custom_call" | custom-call | flops 3000000000 | tf_op jit(solution)/shard_map/pallas_call | solution.py:491
  43.9 2.0 %shard_map.261 = (bf16[160,2048]{1,0:T(8,128)(2,1)S(1)}, bf16[64,2048]{1,0:T(8,128)(2,1)S(1)}) custom-call(s32[8]{0:T(128)S(1)} %get-tuple-element.36.notes, bf16[160,2048]{1,0:T(8,128)(2,1)S(1)} %collective-permute-done.2.received, bf16[2,32,2048]{2,1,0:T(8,128)(2,1)S(1)} %get-tuple-element.39.weights, f32[192,2048]{1,0:T(8,128)S(1)} %get-tuple-element.50.m, ...), custom_call_target="tpu_custom_call" | custom-call | flops 2000000000 | tf_op jit(solution)/shard_map/pallas_call | solution.py:491
  45.9 6.0 %collective-permute-start.5 = (bf16[64,2048]{1,0:T(8,128)(2,1)S(1)}, bf16[64,2048]{1,0:T(8,128)(2,1)S(1)}, u32[]{:S(2)}, u32[]{:S(2)}) collective-permute-start(bf16[64,2048]{1,0:T(8,128)(2,1)S(1)} %get-tuple-element.55.mine), channel_id=1, source_target_pairs={{0,1},{1,0},{2,3},{3,2},{4,5},{5,4},{6,7},{7,6},{8,9},{9,8},{10,11... | collective-permute-start | bytes 786440 | tf_op jit(solution)/shard_map/ppermute | solution.py:631
  51.9 3.5 %shard_map.265 = bf16[128,2048]{1,0:T(8,128)(2,1)S(1)} custom-call(s32[8]{0:T(128)S(1)} %get-tuple-element.36.notes, bf16[2,128,2048]{2,1,0:T(8,128)(2,1)S(1)} %bitcast.19, bf16[160,2048]{1,0:T(8,128)(2,1)S(1)} %collective-permute-done.2.received, bf16[2,32,2048]{2,1,0:T(8,128)(2,1)S(1)} %get-tuple-element.39.weights, ...), custom_call_target="tpu_custom_call" | custom-call | flops 6000000000 | tf_op jit(solution)/shard_map/pallas_call | solution.py:491
  55.4 1.9 %collective-permute-start.9 = (bf16[128,2048]{1,0:T(8,128)(2,1)S(1)}, bf16[128,2048]{1,0:T(8,128)(2,1)S(1)}, u32[]{:S(2)}, u32[]{:S(2)}) collective-permute-start(bf16[128,2048]{1,0:T(8,128)(2,1)S(1)} %shard_map.265), channel_id=1, source_target_pairs={{0,28},{4,0},{8,4},{12,8},{16,12},{20,16},{24,20},{28,24},{1,29},{... | collective-permute-start | bytes 1572872 | tf_op jit(solution)/shard_map/ppermute | solution.py:524
  57.3 1.3 %collective-permute-done.5.other = bf16[64,2048]{1,0:T(8,128)(2,1)S(1)} collective-permute-done((bf16[64,2048]{1,0:T(8,128)(2,1)S(1)}, bf16[64,2048]{1,0:T(8,128)(2,1)S(1)}, u32[]{:S(2)}, u32[]{:S(2)}) %collective-permute-start.5) | collective-permute-done | bytes 262176 | tf_op jit(solution)/shard_map/ppermute | solution.py:631
  58.6 0.1 shard_map.262.mine
  58.6 0.8 %collective-permute-start.6 = (bf16[64,2048]{1,0:T(8,128)(2,1)S(1)}, bf16[64,2048]{1,0:T(8,128)(2,1)S(1)}, u32[]{:S(2)}, u32[]{:S(2)}) collective-permute-start(bf16[64,2048]{1,0:T(8,128)(2,1)S(1)} %shard_map.262.mine), channel_id=1, source_target_pairs={{0,2},{1,3},{2,0},{3,1},{4,6},{5,7},{6,4},{7,5},{8,10},{9,11},{10,... | collective-permute-start | bytes 786440 | tf_op jit(solution)/shard_map/ppermute | solution.py:631
  59.5 7.1 %collective-permute-done.6.other = bf16[64,2048]{1,0:T(8,128)(2,1)S(1)} collective-permute-done((bf16[64,2048]{1,0:T(8,128)(2,1)S(1)}, bf16[64,2048]{1,0:T(8,128)(2,1)S(1)}, u32[]{:S(2)}, u32[]{:S(2)}) %collective-permute-start.6) | collective-permute-done | bytes 262176 | tf_op jit(solution)/shard_map/ppermute | solution.py:631
  66.6 2.3 %shard_map.266 = (bf16[128,2048]{1,0:T(8,128)(2,1)}, bf16[128,2048]{1,0:T(8,128)(2,1)}, f32[31,2,2048]{2,1,0:T(2,128)}, f32[2,2048]{1,0:T(2,128)}) custom-call(s32[2,8]{1,0:T(2,128)S(1)} %bitcast.27, bf16[64,2048]{1,0:T(8,128)(2,1)S(1)} %shard_map.262.mine, bf16[64,2048]{1,0:T(8,128)(2,1)S(1)} %collective-permute-done.6.other, ...), custom_call_target="tpu_custom_call" | custom-call | tf_op jit(solution)/shard_map/pallas_call | solution.py:491
  (54 shorter events, 0.1 us)
Async XLA Ops:
  0.6 5.9 %copy-start.8 = (bf16[224,64]{1,0:T(8,128)(2,1)S(1)}, bf16[224,64]{1,0:T(8,128)(2,1)}, u32[]{:S(2)}) copy-start(bf16[224,64]{1,0:T(8,128)(2,1)} %constant.30.clone.q_table) | copy-start | bytes 86020
  0.6 5.9 %copy-start.13 = (s32[8,2]{0,1:T(2,128)S(1)}, s32[8,2]{0,1:T(2,128)}, u32[]{:S(2)}) copy-start(s32[8,2]{0,1:T(2,128)} %param.32) | copy-start | bytes 196
  0.7 5.9 %copy-start.14 = (s32[8,2]{0,1:T(2,128)S(1)}, s32[8,2]{0,1:T(2,128)}, u32[]{:S(2)}) copy-start(s32[8,2]{0,1:T(2,128)} %param.31) | copy-start | bytes 196
  0.7 5.9 %copy-start.15 = (s32[8]{0:T(128)S(1)}, s32[8]{0:T(128)}, u32[]{:S(2)}) copy-start(s32[8]{0:T(128)} %back_lengths.1) | copy-start | bytes 100
  0.7 5.9 %copy-start.16 = (s32[8]{0:T(128)S(1)}, s32[8]{0:T(128)}, u32[]{:S(2)}) copy-start(s32[8]{0:T(128)} %ahead_lengths.1) | copy-start | bytes 100
  0.7 5.9 %copy-start.11 = (bf16[1,2,2048]{2,1,0:T(2,128)(2,1)S(1)}, bf16[1,2,2048]{2,1,0:T(2,128)(2,1)}, u32[]{:S(2)}) copy-start(bf16[1,2,2048]{2,1,0:T(2,128)(2,1)} %param.28) | copy-start | bytes 24580
  0.7 5.9 %copy-start.5 = (bf16[1,2,31,2048]{3,1,2,0:T(2,128)(2,1)S(1)}, bf16[1,2,31,2048]{3,1,2,0:T(2,128)(2,1)}, u32[]{:S(2)}) copy-start(bf16[1,2,31,2048]{3,1,2,0:T(2,128)(2,1)} %param.27) | copy-start | bytes 761860
  2.8 16.4 %collective-permute-start = (bf16[80,2048]{1,0:T(8,128)(2,1)}, bf16[80,2048]{1,0:T(8,128)(2,1)S(1)}, u32[]{:S(2)}, u32[]{:S(2)}) collective-permute-start(bf16[80,2048]{1,0:T(8,128)(2,1)} %get-tuple-element.37), channel_id=1, source_target_pairs={{0,1},{2,3},{1,0},{3,2},{4,5},{6,7},{5,4},{7,6},{8,9},{10,11},{9,8... | collective-permute-start | bytes 983048 | tf_op jit(solution)/shard_map/ppermute | solution.py:530
  5.8 13.4 %collective-permute-start.1 = (bf16[80,2048]{1,0:T(8,128)(2,1)}, bf16[80,2048]{1,0:T(8,128)(2,1)S(1)}, u32[]{:S(2)}, u32[]{:S(2)}) collective-permute-start(bf16[80,2048]{1,0:T(8,128)(2,1)} %get-tuple-element.38), channel_id=1, source_target_pairs={{1,2},{2,1},{5,6},{6,5},{9,10},{10,9},{13,14},{14,13},{17,18},{18,... | collective-permute-start | bytes 983048 | tf_op jit(solution)/shard_map/ppermute | solution.py:530
  9.5 9.7 %copy-start.4 = (bf16[1,128,2048]{2,1,0:T(8,128)(2,1)S(1)}, bf16[1,128,2048]{2,1,0:T(8,128)(2,1)}, u32[]{:S(2)}) copy-start(bf16[1,128,2048]{2,1,0:T(8,128)(2,1)} %grad.1) | copy-start | bytes 1572868
  9.5 9.7 %copy-start.17 = (bf16[448,192]{1,0:T(8,128)(2,1)S(1)}, bf16[448,192]{1,0:T(8,128)(2,1)}, u32[]{:S(2)}) copy-start(bf16[448,192]{1,0:T(8,128)(2,1)} %constant.33.clone.g_table) | copy-start | bytes 516100
  9.5 9.7 %copy-start.18 = (bf16[448,224]{1,0:T(8,128)(2,1)S(1)}, bf16[448,224]{1,0:T(8,128)(2,1)}, u32[]{:S(2)}) copy-start(bf16[448,224]{1,0:T(8,128)(2,1)} %constant.31.clone.m_table) | copy-start | bytes 602116
  9.5 9.7 %copy-start.20 = (bf16[384,224]{1,0:T(8,128)(2,1)S(1)}, bf16[384,224]{1,0:T(8,128)(2,1)}, u32[]{:S(2)}) copy-start(bf16[384,224]{1,0:T(8,128)(2,1)} %constant.32.clone.c_table) | copy-start | bytes 516100
  9.5 9.7 %copy-start.23 = (bf16[320,224]{1,0:T(8,128)(2,1)S(1)}, bf16[320,224]{1,0:T(8,128)(2,1)}, u32[]{:S(2)}) copy-start(bf16[320,224]{1,0:T(8,128)(2,1)} %constant.34.clone.x_table) | copy-start | bytes 430084
  11.8 22.5 %collective-permute-start.7 = (bf16[32,2048]{1,0:T(8,128)(2,1)S(1)}, bf16[32,2048]{1,0:T(8,128)(2,1)S(1)}, u32[]{:S(2)}, u32[]{:S(2)}) collective-permute-start(bf16[32,2048]{1,0:T(8,128)(2,1)S(1)} %get-tuple-element.58), channel_id=1, source_target_pairs={{0,28},{4,0},{8,4},{12,8},{16,12},{20,16},{24,20},{28,24},{1,29},{... | collective-permute-start | bytes 393224 | tf_op jit(solution)/shard_map/ppermute | solution.py:524
  14.6 16.1 %collective-permute-start.3 = (bf16[64,2048]{1,0:T(8,128)(2,1)S(1)}, bf16[64,2048]{1,0:T(8,128)(2,1)S(1)}, u32[]{:S(2)}, u32[]{:S(2)}) collective-permute-start(bf16[64,2048]{1,0:T(8,128)(2,1)S(1)} %get-tuple-element.45), channel_id=1, source_target_pairs={{0,1},{2,3},{1,0},{3,2},{4,5},{6,7},{5,4},{7,6},{8,9},{10,11},{9,8... | collective-permute-start | bytes 786440 | tf_op jit(solution)/shard_map/ppermute | solution.py:530
  18.5 12.2 %collective-permute-start.4 = (bf16[64,2048]{1,0:T(8,128)(2,1)S(1)}, bf16[64,2048]{1,0:T(8,128)(2,1)S(1)}, u32[]{:S(2)}, u32[]{:S(2)}) collective-permute-start(bf16[64,2048]{1,0:T(8,128)(2,1)S(1)} %get-tuple-element.46), channel_id=1, source_target_pairs={{1,2},{2,1},{5,6},{6,5},{9,10},{10,9},{13,14},{14,13},{17,18},{18,... | collective-permute-start | bytes 786440 | tf_op jit(solution)/shard_map/ppermute | solution.py:530
  19.3 9.2 %copy-start.3 = (bf16[1,128,2048]{2,1,0:T(8,128)(2,1)S(1)}, bf16[1,128,2048]{2,1,0:T(8,128)(2,1)}, u32[]{:S(2)}) copy-start(bf16[1,128,2048]{2,1,0:T(8,128)(2,1)} %param.24) | copy-start | bytes 1572868
  19.3 9.2 %copy-start.9 = (bf16[192,64]{1,0:T(8,128)(2,1)S(1)}, bf16[192,64]{1,0:T(8,128)(2,1)}, u32[]{:S(2)}) copy-start(bf16[192,64]{1,0:T(8,128)(2,1)} %constant.35.clone.q_table) | copy-start | bytes 73732
  27.5 16.4 %collective-permute-start.2 = (bf16[160,2048]{1,0:T(8,128)(2,1)S(1)}, bf16[160,2048]{1,0:T(8,128)(2,1)S(1)}, u32[]{:S(2)}, u32[]{:S(2)}) collective-permute-start(bf16[160,2048]{1,0:T(8,128)(2,1)S(1)} %get-tuple-element.44), channel_id=1, source_target_pairs={{0,28},{4,0},{8,4},{12,8},{16,12},{20,16},{24,20},{28,24},{1,29},{... | collective-permute-start | bytes 1966088 | tf_op jit(solution)/shard_map/ppermute | solution.py:524
  30.7 3.6 %copy-start.22 = (bf16[320,160]{1,0:T(8,128)(2,1)S(1)}, bf16[320,160]{1,0:T(8,128)(2,1)}, u32[]{:S(2)}) copy-start(bf16[320,160]{1,0:T(8,128)(2,1)} %constant.40.clone.m_table) | copy-start | bytes 307204
  30.8 3.6 %copy-start.25 = (bf16[256,160]{1,0:T(8,128)(2,1)S(1)}, bf16[256,160]{1,0:T(8,128)(2,1)}, u32[]{:S(2)}) copy-start(bf16[256,160]{1,0:T(8,128)(2,1)} %constant.42.clone.c_table) | copy-start | bytes 245764
  30.8 3.6 %copy-start.26 = (bf16[160,64]{1,0:T(8,128)(2,1)S(1)}, bf16[160,64]{1,0:T(8,128)(2,1)}, u32[]{:S(2)}) copy-start(bf16[160,64]{1,0:T(8,128)(2,1)} %constant.41.clone.q_table) | copy-start | bytes 61444
  34.3 3.8 %copy-start.7 = (bf16[192,256]{1,0:T(8,128)(2,1)S(1)}, bf16[192,256]{1,0:T(8,128)(2,1)}, u32[]{:S(2)}) copy-start(bf16[192,256]{1,0:T(8,128)(2,1)} %constant.37.clone.go_table) | copy-start | bytes 294916
  34.3 3.8 %copy-start.10 = (bf16[64,192]{1,0:T(8,128)(2,1)S(1)}, bf16[64,192]{1,0:T(8,128)(2,1)}, u32[]{:S(2)}) copy-start(bf16[64,192]{1,0:T(8,128)(2,1)} %constant.38.clone.t_table) | copy-start | bytes 73732
  37.8 21.6 %collective-permute-start.8 = (bf16[128,2048]{1,0:T(8,128)(2,1)S(1)}, bf16[128,2048]{1,0:T(8,128)(2,1)S(1)}, u32[]{:S(2)}, u32[]{:S(2)}) collective-permute-start(bf16[128,2048]{1,0:T(8,128)(2,1)S(1)} %shard_map.264), channel_id=1, source_target_pairs={{0,8},{4,12},{8,16},{12,20},{16,24},{20,28},{24,0},{28,4},{1,9},{5... | collective-permute-start | bytes 1572872 | tf_op jit(solution)/shard_map/ppermute | solution.py:524
  43.9 8.0 %copy-start.1 = (bf16[1,2,128,2048]{3,2,1,0:T(8,128)(2,1)S(1)}, bf16[1,2,128,2048]{3,2,1,0:T(8,128)(2,1)}, u32[]{:S(2)}) copy-start(bf16[1,2,128,2048]{3,2,1,0:T(8,128)(2,1)} %param.26) | copy-start | bytes 3145732
  43.9 8.0 %copy-start.19 = (bf16[384,160]{1,0:T(8,128)(2,1)S(1)}, bf16[384,160]{1,0:T(8,128)(2,1)}, u32[]{:S(2)}) copy-start(bf16[384,160]{1,0:T(8,128)(2,1)} %constant.43.clone.g_table) | copy-start | bytes 368644
  43.9 8.0 %copy-start.24 = (bf16[256,192]{1,0:T(8,128)(2,1)S(1)}, bf16[256,192]{1,0:T(8,128)(2,1)}, u32[]{:S(2)}) copy-start(bf16[256,192]{1,0:T(8,128)(2,1)} %constant.44.clone.x_table) | copy-start | bytes 294916
  45.9 12.6 %collective-permute-start.5 = (bf16[64,2048]{1,0:T(8,128)(2,1)S(1)}, bf16[64,2048]{1,0:T(8,128)(2,1)S(1)}, u32[]{:S(2)}, u32[]{:S(2)}) collective-permute-start(bf16[64,2048]{1,0:T(8,128)(2,1)S(1)} %get-tuple-element.55.mine), channel_id=1, source_target_pairs={{0,1},{1,0},{2,3},{3,2},{4,5},{5,4},{6,7},{7,6},{8,9},{9,8},{10,11... | collective-permute-start | bytes 786440 | tf_op jit(solution)/shard_map/ppermute | solution.py:631
  55.4 11.2 %collective-permute-start.9 = (bf16[128,2048]{1,0:T(8,128)(2,1)S(1)}, bf16[128,2048]{1,0:T(8,128)(2,1)S(1)}, u32[]{:S(2)}, u32[]{:S(2)}) collective-permute-start(bf16[128,2048]{1,0:T(8,128)(2,1)S(1)} %shard_map.265), channel_id=1, source_target_pairs={{0,28},{4,0},{8,4},{12,8},{16,12},{20,16},{24,20},{28,24},{1,29},{... | collective-permute-start | bytes 1572872 | tf_op jit(solution)/shard_map/ppermute | solution.py:524
  58.6 8.0 %collective-permute-start.6 = (bf16[64,2048]{1,0:T(8,128)(2,1)S(1)}, bf16[64,2048]{1,0:T(8,128)(2,1)S(1)}, u32[]{:S(2)}, u32[]{:S(2)}) collective-permute-start(bf16[64,2048]{1,0:T(8,128)(2,1)S(1)} %shard_map.262.mine), channel_id=1, source_target_pairs={{0,2},{1,3},{2,0},{3,1},{4,6},{5,7},{6,4},{7,5},{8,10},{9,11},{10,... | collective-permute-start | bytes 786440 | tf_op jit(solution)/shard_map/ppermute | solution.py:631
  (5 other events, 9.5 us)

commit v8 on v7

--- a/solution.py
+++ b/solution.py
@@ -10,7 +10,7 @@
 from jax.sharding import PartitionSpec as P
 
 epsilon = 1e-05
-BLOCK = 256
+BLOCK = 1024
 LANES = 128
 F32 = jnp.float32
 BF16 = jnp.bfloat16
@@ -271,45 +271,44 @@
 
 
 def first_backward_kernel(
-    reaches, notes, saved, near, far, grads, weights, own_masked, own_mean, own_inverse, q,
+    reach, notes, saved, near, far, grads, weights, later, masked, mean, inverse, q,
     m_table, c_table, g_table, x_table,
-    grad_x, halo, inner, gain_sum, halos, grad_halos, all_mean, all_inverse, scaled, sum_a, sum_b,
+    grad_x, near_edge, far_edge, halo, inner, gain_sum, halos, grad_halos, scaled, sum_a, sum_b,
 ):
     own, width = grads.shape
-    reach, grad_reach, out_reach = reaches
+    edge = near_edge.shape[0]
     slot, length, first = looked_up(notes, BACK0)
     gain = slot_row(weights, slot)
     left, right = sorted_halos(near, far, 0, halos)
     grad_left, grad_right = sorted_halos(near, far, reach, grad_halos)
-    edge = reach - out_reach
-    low, middle, high = pl.ds(0, out_reach), pl.ds(out_reach, own), pl.ds(out_reach + own, out_reach)
-    bounds = ((left, first - reach, 0, edge, low), (right, first + own, reach, 0, high))
-    for x, begin, at, skip, rows in bounds:
-        norm_rows(x, 0, reach, 0, gain, begin, length, halo.at[pl.ds(at, reach)], sum_a, sum_b)
-        all_mean[rows, :] = sum_a[pl.ds(skip, out_reach), :]
-        all_inverse[rows, :] = sum_b[pl.ds(skip, out_reach), :]
-    all_mean[middle, :] = own_mean[...]
-    all_inverse[middle, :] = own_inverse[...]
-    grad_pieces = [(grad_left, 0, grad_reach), (grads, 0, own), (grad_right, 0, grad_reach)]
-    pieces = [(left, edge, out_reach), (saved.at[0], 0, own), (right, 0, out_reach)]
-    out_pieces = [(grad_left, grad_reach - out_reach, out_reach), (grads, 0, own), (grad_right, 0, out_reach)]
-    mask = frame_mask(own + 2 * out_reach, first - out_reach, length)
+    norm_halo(left, right, own, gain, first, length, halo)
+    grad_pieces = [(grad_left, 0, edge), (grads, 0, own), (grad_right, 0, edge)]
+    pieces = [(saved.at[0], 0, own)]
+    mask = frame_mask(own, first, length)
     sum_a[...] = jnp.zeros_like(sum_a)
     sum_b[...] = jnp.zeros_like(sum_b)
-
-    def block(columns):
-        m = transform(m_table, joined(halo, own_masked, columns))
+    grad_x[pl.ds(own, later.shape[0]), :] = later[...]
+
+    def block(columns):
+        m = transform(m_table, joined(halo, masked, columns))
         conv = transform(c_table, product(m, q[:, columns]))
         mixed = (window(grad_pieces, columns).astype(F32) * gate_factor(conv)).astype(BF16)
-        inner[:, columns] = mixed[grad_reach : grad_reach + own]
+        inner[:, columns] = mixed[edge : edge + own]
         weighted = first_pass(
-            pieces, all_mean, all_inverse, gain, mask, (g_table, x_table), mixed, q[:, columns], columns,
+            pieces, mean, inverse, gain, mask, (g_table, x_table), mixed, q[:, columns], columns,
             scaled, sum_a, sum_b,
         )
-        gain_sum[:, columns] = jnp.sum(weighted[out_reach : out_reach + own], axis=0, keepdims=True)
+        gain_sum[:, columns] = jnp.sum(weighted, axis=0, keepdims=True)
 
     each_block(width, block)
-    last_pass(out_pieces, pieces, all_mean, all_inverse, scaled, sum_a, sum_b, grad_x)
+    last_pass([(grads, 0, own)], pieces, mean, inverse, scaled, sum_a, sum_b, grad_x)
+    for even in range(2):
+
+        @pl.when(lax.rem(lax.axis_index("tm") + 1, 2) == even)
+        def _():
+            top, bottom = (far_edge, near_edge) if even else (near_edge, far_edge)
+            top[...] = grad_x[pl.ds(0, edge), :]
+            bottom[...] = grad_x[pl.ds(own - edge, edge), :]
 
 
 def tap_term(go_table, t_table, m, mixed):
@@ -322,16 +321,12 @@
     taps[:, columns] = jnp.where(row == tap.shape[0] - 1, gain_sum, tap).astype(taps.dtype)
 
 
-def first_taps_kernel(reach, halo, masked, inner, gain_sum, m_table, go_table, t_table, taps):
-    wide_reach = halo.shape[0] // 2
-    own, width = masked.shape
-    pieces = [(halo, wide_reach - reach, reach), (masked, 0, own), (halo, wide_reach, reach)]
-
-    def block(columns):
-        m = transform(m_table, window(pieces, columns))
+def first_taps_kernel(halo, masked, inner, gain_sum, m_table, go_table, t_table, taps):
+    def block(columns):
+        m = transform(m_table, joined(halo, masked, columns))
         put_taps(taps, tap_term(go_table, t_table, m, inner[:, columns]), gain_sum[:, columns], columns)
 
-    each_block(width, block)
+    each_block(masked.shape[1], block)
 
 
 def add_kernel(mine, other, out):
@@ -357,7 +352,9 @@
     each_block(width, block)
 
 
-def second_taps_kernel(notes, received, weights, m, factor, conv, taps0, go_table, t_table, mixed_out, taps):
+def second_taps_kernel(
+    notes, received, near, far, weights, m, factor, conv, taps0, go_table, t_table, mixed_out, taps, halos
+):
     own, width = conv.shape
     rows = factor.shape[0]
     count = taps0.shape[0]
@@ -365,9 +362,11 @@
     taps1 = taps.at[pl.ds(count, count)]
     edge = (rows - own) // 2
     gain = slot_row(weights, notes[BACK1])
-
-    def block(columns):
-        mixed = (received[:rows, columns].astype(F32) * factor[:, columns]).astype(BF16)
+    left, right = sorted_halos(near, far, 0, halos)
+    pieces = [(left, 0, edge), (received, 0, own), (right, 0, edge)]
+
+    def block(columns):
+        mixed = (window(pieces, columns).astype(F32) * factor[:, columns]).astype(BF16)
         mixed_out[:, columns] = mixed
         inner = mixed[edge : edge + own]
         gain_sum = jnp.sum(inner.astype(F32) * conv[:, columns], axis=0, keepdims=True) / gain(columns)
@@ -382,7 +381,6 @@
     own, width = grad_x.shape
     slot, length, first = looked_up(notes, BACK1)
     pieces = [(saved.at[1], 0, own)]
-    edge = (mixed.shape[0] - own) // 2
     mask = frame_mask(own, first, length)
     sum_a[...] = jnp.zeros_like(sum_a)
     sum_b[...] = jnp.zeros_like(sum_b)
@@ -394,7 +392,7 @@
         )
 
     each_block(width, block)
-    last_pass([(received, edge, own)], pieces, mean, inverse, scaled, sum_a, sum_b, grad_x)
+    last_pass([(received, 0, own)], pieces, mean, inverse, scaled, sum_a, sum_b, grad_x)
 
 
 def first_forward_kernel(reach, notes, act, near, far, weights, masked, q, m_table, c_table, out, halo, halos):
@@ -412,20 +410,20 @@
     each_block(width, block)
 
 
-def second_forward_kernel(notes, between, later, m_table, q_table, c_table, out, masked):
+def second_forward_kernel(notes, between, received, m_table, q_table, c_table, out, masked):
     own, width = out.shape
     rows = between.shape[0]
     edge = (rows - own) // 2
     slot, length, first = looked_up(notes, AHEAD0)
-    last = later.shape[0] - 1
+    last = received.shape[0] - 1
 
     def gain(columns):
-        return later[last : last + 1, columns].astype(F32)
+        return received[last : last + 1, columns].astype(F32)
 
     norm_pieces([(between, 0, rows)], gain, first - edge, length, masked, chunk=rows // 2)
 
     def block(columns):
-        q = tap_spectrum(q_table[...], later[:, columns])
+        q = tap_spectrum(q_table[...], received[own:, columns])
         conv = transform(c_table, product(transform(m_table, masked[:, columns]), q))
         out[:, columns] = (between[edge : edge + own, columns].astype(F32) + conv * sigmoid(conv)).astype(BF16)
 
@@ -517,22 +515,28 @@
     own, width = act.shape
     tap_count = kernels.shape[2]
     half = (tap_count - 1) // 2
-    one, two, three = up16(half), up16(2 * half), up16(3 * half)
-    large, size, small = own + 2 * three, own + 2 * two, own + 2 * one
+    one, two = up16(half), up16(2 * half)
+    size, small = own + 2 * two, own + 2 * one
 
     def shifted(x, by):
         return lax.ppermute(x, "section", [(i, (i + by) % sections) for i in range(sections)])
 
-    def swapped(near, far):
+    def swapped(near, far, by=0):
         results = []
         for x, begin in ((near, 0), (far, 1)):
             pairs = [(i, i + 1) for i in range(begin, shards - 1, 2)]
-            results.append(lax.ppermute(x, "tm", pairs + [(b, a) for a, b in pairs]))
+            pairs = [
+                (s * shards + i, (s + by) % sections * shards + j)
+                for s in range(sections)
+                for a, b in pairs
+                for i, j in ((a, b), (b, a))
+            ]
+            results.append(lax.ppermute(x, ("section", "tm"), pairs))
         return results
 
     near0, far0, ready = call(
-        functools.partial(pack_kernel, (three, two)),
-        (like(three + two, width, BF16), like(three + two, width, BF16), like(8, LANES, F32)),
+        functools.partial(pack_kernel, (two, one)),
+        (like(two + one, width, BF16), like(two + one, width, BF16), like(8, LANES, F32)),
         [pltpu.SemaphoreType.DMA((4,))],
         (saved, grad_in),
         0, [HBM] * 2, None, FULL,
@@ -558,43 +562,39 @@
         functools.partial(prepare_kernel, two),
         (
             jax.ShapeDtypeStruct((kernels.shape[1], tap_count + 1, width), BF16), like(tap_count + 1, width, BF16),
-            like(2 * two, width, BF16), like(2 * two, width, BF16), jax.ShapeDtypeStruct((8,), jnp.int32), *layer(large),
+            like(2 * two, width, BF16), like(2 * two, width, BF16), jax.ShapeDtypeStruct((8,), jnp.int32), *layer(size),
         ),
         [],
         [
             backward_lengths, forward_lengths, backward_slots, forward_slots,
-            kernels[0].transpose(1, 0, 2), norm_gains[0], saved, act, ready, jnp.asarray(tap_freq(large, tap_count)),
+            kernels[0].transpose(1, 0, 2), norm_gains[0], saved, act, ready, jnp.asarray(q_table),
         ],
         0,
         None, (VMEM,) * 4 + (SMEM,) + (VMEM,) * 4,
     )
-    later = shifted(later, -1)
     near1, far1 = swapped(near1, far1)
-    grad_mid, halo0, inner0, gain0 = run(
-        functools.partial(first_backward_kernel, (three, two, one)),
+    g_table, x_table = stacked(to_freq(size, span(one, own))), stacked(from_freq(size, span(0, own)))
+    grad_mid, near2, far2, halo0, inner0, gain0 = run(
+        functools.partial(first_backward_kernel, two),
         (
-            like(small, width, BF16),
-            like(2 * three, width, BF16), like(own, width, BF16), like(1, width, F32),
+            like(own + tap_count + 1, width, BF16), like(one, width, BF16), like(one, width, BF16),
+            like(2 * two, width, BF16), like(own, width, BF16), like(1, width, F32),
         ),
+        [pltpu.VMEM((2, two, width), BF16), pltpu.VMEM((2, one, width), BF16), *rows],
         [
-            pltpu.VMEM((2, three, width), BF16), pltpu.VMEM((2, two, width), BF16),
-            pltpu.VMEM((small, LANES), F32), pltpu.VMEM((small, LANES), F32),
-            pltpu.VMEM((small, width), F32), pltpu.VMEM((small, LANES), F32), pltpu.VMEM((small, LANES), F32),
-        ],
-        [
-            notes, saved, near0, far0, grad, weights, *layer0,
-            stacked(to_freq(large, span(three, own))), stacked(from_freq(large, span(two, own))),
-            stacked(to_freq(large, span(two, own))), stacked(from_freq(large, span(one, own))),
+            notes, saved, near0, far0, grad, weights, later, *layer0,
+            m_table, c_table, g_table, x_table,
         ],
         4,
     )
     grad_mid = shifted(grad_mid, -1)
+    near2, far2 = swapped(near2, far2, -1)
     layers = run(
         prepare_later_kernel, (*layer(size), *layer(size)), [], [notes, saved, act, weights, gain0, q_table], 0
     )
     masked1, mean1, inverse1, q1, masked2, _, _, q2 = layers
     taps0 = run(
-        functools.partial(first_taps_kernel, two), like(tap_count + 1, width, BF16), [],
+        first_taps_kernel, like(tap_count + 1, width, BF16), [],
         [halo0, layer0[0], inner0, gain0, m_table, go_table, t_table],
         0,
     )
@@ -618,7 +618,7 @@
         like(own, width, BF16),
         [pltpu.VMEM((small, width), BF16)],
         [
-            notes, between, later,
+            notes, between, grad_mid,
             stacked(to_freq(small, span(one, own))), tap_freq(small, tap_count), stacked(from_freq(small, span(0, own))),
         ],
         3,
@@ -637,8 +637,8 @@
     mixed1, sums = run(
         second_taps_kernel,
         (like(small, width, BF16), like(2 * (tap_count + 1), width, BF16)),
-        [],
-        [notes, grad_mid, weights, m1, factor1, conv1, taps0, go_table, t_table],
+        [pltpu.VMEM((2, one, width), BF16)],
+        [notes, grad_mid, near2, far2, weights, m1, factor1, conv1, taps0, go_table, t_table],
         2,
     )
     grad_out = run(
@@ -647,7 +647,7 @@
         rows,
         [
             notes, saved, grad_mid, weights, mixed1, q1, mean1, inverse1,
-            stacked(to_freq(size, span(one, own))), stacked(from_freq(size, span(0, own))),
+            g_table, x_table,
         ],
         6,
     )

time: 69.4 us -> 63.6 us (0.916)
  the two profiles are of different devices: /device:TPU:0 before, /device:TPU:5 now
where the time goes in v8:
time: 63.6 us; the launch traced here: 63.2 us
  Pallas kernels  23.3 us (37%)
  waiting for transfers between devices  16.7 us (26%)
  starting transfers between devices  15.5 us (24%)
  local copies, waits for them, and re-layouts  6.5 us (10%)
  between operations  1.2 us (2%)
    pallas_call x12, Pallas kernels, call(): pl.pallas_call(kernel, out_shape=outs, in_specs=specs, out_specs=jax.tree...  23.3 us
    ppermute x6, starting transfers between devices, swapped(): results.append(lax.ppermute(x, ('section', 'tm'), pairs))  13 us
    ppermute x3, waiting for transfers between devices, shifted(): lax.ppermute(x, 'section', [(i, (i + by) % sections) for i in range(secti...  12 us
    unnamed x48, local copies, waits for them, and re-layouts  6.5 us
    ppermute x2, waiting for transfers between devices, summed(): other = lax.ppermute(x, 'tm', [(i, i ^ step) for i in range(shards)])  4.62 us
    ppermute x3, starting transfers between devices, shifted(): lax.ppermute(x, 'section', [(i, (i + by) % sections) for i in range(secti...  2.42 us
  transfers between devices with their start and end apart: 11, of which 4 were waited for; matrix products, arithmetic and copies ran while one was open for 0% of the time, Pallas kernels for 30%

profile of v8, /device:TPU:5, one launch (start us, length us, event | category | flops | bytes accessed | tf_op | source)
XLA Modules:
  0.0 63.2 jit_solution(15054727580515733884)
XLA Ops:
  0.7 1.8 %shard_map.210 = (bf16[48,2048]{1,0:T(8,128)(2,1)}, bf16[48,2048]{1,0:T(8,128)(2,1)}, f32[8,128]{1,0:T(8,128)}) custom-call(bf16[2,128,2048]{2,1,0:T(8,128)(2,1)} %bitcast.15, bf16[1,128,2048]{2,1,0:T(8,128)(2,1)} %grad.1), custom_call_target="tpu_custom_call" | custom-call | tf_op jit(solution)/shard_map/pallas_call | solution.py:489
  2.5 1.3 %collective-permute-start = (bf16[48,2048]{1,0:T(8,128)(2,1)}, bf16[48,2048]{1,0:T(8,128)(2,1)S(1)}, u32[]{:S(2)}, u32[]{:S(2)}) collective-permute-start(bf16[48,2048]{1,0:T(8,128)(2,1)} %get-tuple-element.39), channel_id=1, source_target_pairs={{0,1},{1,0},{2,3},{3,2},{4,5},{5,4},{6,7},{7,6},{8,9},{9,8},{10,11... | collective-permute-start | bytes 589832 | tf_op jit(solution)/shard_map/ppermute | solution.py:534
  3.8 1.9 %collective-permute-start.1 = (bf16[48,2048]{1,0:T(8,128)(2,1)}, bf16[48,2048]{1,0:T(8,128)(2,1)S(1)}, u32[]{:S(2)}, u32[]{:S(2)}) collective-permute-start(bf16[48,2048]{1,0:T(8,128)(2,1)} %get-tuple-element.40), channel_id=1, source_target_pairs={{1,2},{2,1},{5,6},{6,5},{9,10},{10,9},{13,14},{14,13},{17,18},{18,... | collective-permute-start | bytes 589832 | tf_op jit(solution)/shard_map/ppermute | solution.py:534
  5.7 1.2 %copy-done = bf16[1,2,128,2048]{3,2,1,0:T(8,128)(2,1)S(1)} copy-done((bf16[1,2,128,2048]{3,2,1,0:T(8,128)(2,1)S(1)}, bf16[1,2,128,2048]{3,2,1,0:T(8,128)(2,1)}, u32[]{:S(2)}) %copy-start) | copy-done | bytes 1048600
  7.0 1.0 %copy-done.2 = bf16[1,128,2048]{2,1,0:T(8,128)(2,1)S(1)} copy-done((bf16[1,128,2048]{2,1,0:T(8,128)(2,1)S(1)}, bf16[1,128,2048]{2,1,0:T(8,128)(2,1)}, u32[]{:S(2)}) %copy-start.2) | copy-done | bytes 524312
  8.0 0.8 %copy-done.7 = bf16[192,64]{1,0:T(8,128)(2,1)S(1)} copy-done((bf16[192,64]{1,0:T(8,128)(2,1)S(1)}, bf16[192,64]{1,0:T(8,128)(2,1)}, u32[]{:S(2)}) %copy-start.7) | copy-done | bytes 24600
  8.8 0.7 %copy-done.12 = f32[8,128]{1,0:T(8,128)S(1)} copy-done((f32[8,128]{1,0:T(8,128)S(1)}, f32[8,128]{1,0:T(8,128)}, u32[]{:S(2)}) %copy-start.12) | copy-done | bytes 4120
  9.5 0.7 %copy-done.13 = s32[8,2]{0,1:T(2,128)S(1)} copy-done((s32[8,2]{0,1:T(2,128)S(1)}, s32[8,2]{0,1:T(2,128)}, u32[]{:S(2)}) %copy-start.13) | copy-done | bytes 88
  10.2 0.7 %copy-done.15 = s32[8,2]{0,1:T(2,128)S(1)} copy-done((s32[8,2]{0,1:T(2,128)S(1)}, s32[8,2]{0,1:T(2,128)}, u32[]{:S(2)}) %copy-start.15) | copy-done | bytes 88
  10.8 0.7 %copy-done.16 = s32[8]{0:T(128)S(1)} copy-done((s32[8]{0:T(128)S(1)}, s32[8]{0:T(128)}, u32[]{:S(2)}) %copy-start.16) | copy-done | bytes 56
  11.5 0.7 %copy-done.17 = s32[8]{0:T(128)S(1)} copy-done((s32[8]{0:T(128)S(1)}, s32[8]{0:T(128)}, u32[]{:S(2)}) %copy-start.17) | copy-done | bytes 56
  12.2 2.1 %shard_map.211 = (bf16[2,32,2048]{2,1,0:T(8,128)(2,1)S(1)}, bf16[32,2048]{1,0:T(8,128)(2,1)S(1)}, bf16[64,2048]{1,0:T(8,128)(2,1)S(1)}, bf16[64,2048]{1,0:T(8,12...) custom-call(s32[8]{0:T(128)S(1)} %copy-done.16, ...), custom_call_target="tpu_custom_call" | custom-call | tf_op jit(solution)/shard_map/pallas_call | solution.py:489
  14.3 0.1 collective-permute-start.5
  14.4 4.3 %collective-permute-start.6 = (bf16[64,2048]{1,0:T(8,128)(2,1)S(1)}, bf16[64,2048]{1,0:T(8,128)(2,1)S(1)}, u32[]{:S(2)}, u32[]{:S(2)}) collective-permute-start(bf16[64,2048]{1,0:T(8,128)(2,1)S(1)} %get-tuple-element.51), channel_id=1, source_target_pairs={{1,2},{2,1},{5,6},{6,5},{9,10},{10,9},{13,14},{14,13},{17,18},{18,... | collective-permute-start | bytes 786440 | tf_op jit(solution)/shard_map/ppermute | solution.py:534
  18.7 3.7 %shard_map.212 = (bf16[160,2048]{1,0:T(8,128)(2,1)S(1)}, bf16[16,2048]{1,0:T(8,128)(2,1)S(1)}, bf16[16,2048]{1,0:T(8,128)(2,1)S(1)}, bf16[64,2048]{1,0:T(8,128)(...) custom-call(s32[8]{0:T(128)S(1)} %get-tuple-element.38.notes, bf16[2,128,2048]{2,1,0:T(8,128)(2,1)S(1)} %bitcast.17, ...), custom_call_target="tpu_custom_call" | custom-call | flops 4000000000 | tf_op jit(solution)/shard_map/pallas_call | solution.py:489
  22.5 1.6 %collective-permute-start.2 = (bf16[160,2048]{1,0:T(8,128)(2,1)S(1)}, bf16[160,2048]{1,0:T(8,128)(2,1)S(1)}, u32[]{:S(2)}, u32[]{:S(2)}) collective-permute-start(bf16[160,2048]{1,0:T(8,128)(2,1)S(1)} %get-tuple-element.47), channel_id=1, source_target_pairs={{0,28},{4,0},{8,4},{12,8},{16,12},{20,16},{24,20},{28,24},{1,29},{... | collective-permute-start | bytes 1966088 | tf_op jit(solution)/shard_map/ppermute | solution.py:522
  24.0 0.1 collective-permute-start.3
  24.2 5.3 %collective-permute-start.4 = (bf16[16,2048]{1,0:T(8,128)(2,1)S(1)}, bf16[16,2048]{1,0:T(8,128)(2,1)S(1)}, u32[]{:S(2)}, u32[]{:S(2)}) collective-permute-start(bf16[16,2048]{1,0:T(8,128)(2,1)S(1)} %get-tuple-element.49), channel_id=1, source_target_pairs={{1,30},{2,29},{5,2},{6,1},{9,6},{10,5},{13,10},{14,9},{17,14},{18,... | collective-permute-start | bytes 196616 | tf_op jit(solution)/shard_map/ppermute | solution.py:534
  29.5 2.3 %shard_map.213 = (bf16[128,2048]{1,0:T(8,128)(2,1)S(1)}, f32[128,128]{1,0:T(8,128)S(1)}, f32[128,128]{1,0:T(8,128)S(1)}, f32[192,2048]{1,0:T(8,128)S(1)}, bf16[1...) custom-call(s32[8]{0:T(128)S(1)} %get-tuple-element.38.notes, ...), custom_call_target="tpu_custom_call" | custom-call | tf_op jit(solution)/shard_map/pallas_call | solution.py:489
  31.8 1.1 %shard_map.215.taps0 = bf16[32,2048]{1,0:T(8,128)(2,1)S(1)} custom-call(bf16[64,2048]{1,0:T(8,128)(2,1)S(1)} %get-tuple-element.58.halo, bf16[128,2048]{1,0:T(8,128)(2,1)S(1)} %get-tuple-element.43.masked, bf16[128,2048]{1,0:T(8,128)(2,1)S(1)} %get-tuple-element.59.inner, f32[1,2048]{1,0:T(1,128)S(1)} %get-tuple-element.52.ready.gain_sum, ...), custom_call_target="tpu_custom_call" | custom-call | tf_op jit(solution)/shard_map/pallas_call | solution.py:489
  32.9 2.1 %shard_map.218.between = bf16[160,2048]{1,0:T(8,128)(2,1)S(1)} custom-call(s32[8]{0:T(128)S(1)} %get-tuple-element.38.notes, bf16[128,2048]{1,0:T(8,128)(2,1)S(1)} %bitcast.22, bf16[64,2048]{1,0:T(8,128)(2,1)S(1)} %collective-permute-done.5.near, bf16[64,2048]{1,0:T(8,128)(2,1)S(1)} %collective-permute-done.6.far, ...), custom_call_target="tpu_custom_call" | custom-call | flops 3000000000 | tf_op jit(solution)/shard_map/pallas_call | solution.py:489
  35.1 2.1 %shard_map.214 = (f32[192,2048]{1,0:T(8,128)S(1)}, f32[160,2048]{1,0:T(8,128)S(1)}, f32[128,2048]{1,0:T(8,128)S(1)}) custom-call(s32[8]{0:T(128)S(1)} %get-tuple-element.38.notes, bf16[64,2048]{1,0:T(8,128)(2,1)S(1)} %collective-permute-done.5.near, bf16[64,2048]{1,0:T(8,128)(2,1)S(1)} %collective-permute-done.6.far, ...), custom_call_target="tpu_custom_call" | custom-call | flops 3000000000 | tf_op jit(solution)/shard_map/pallas_call | solution.py:489
  37.2 2.1 %shard_map.219 = bf16[128,2048]{1,0:T(8,128)(2,1)S(1)} custom-call(s32[8]{0:T(128)S(1)} %get-tuple-element.38.notes, bf16[160,2048]{1,0:T(8,128)(2,1)S(1)} %shard_map.218.between, bf16[160,2048]{1,0:T(8,128)(2,1)S(1)} %collective-permute-done.2.received, bf16[320,160]{1,0:T(8,128)(2,1)S(1)} %copy-done.19, bf16[160,64]{1,0:T(8,128)(2,1)S(1)} %copy-done.23, ...), custom_call_target="tpu_custom_call" | custom-call | flops 3000000000 | tf_op jit(solution)/shard_map/pallas_call | solution.py:489
  39.4 0.2 collective-permute-start.9
  39.7 1.5 %shard_map.216 = (bf16[160,2048]{1,0:T(8,128)(2,1)S(1)}, bf16[64,2048]{1,0:T(8,128)(2,1)S(1)}) custom-call(s32[8]{0:T(128)S(1)} %get-tuple-element.38.notes, bf16[160,2048]{1,0:T(8,128)(2,1)S(1)} %collective-permute-done.2.received, bf16[16,2048]{1,0:T(8,128)(2,1)S(1)} %collective-permute-done.3.near, bf16[16,2048]{1,0:T(8,128)(2,1)S(1)} %collective-permute-done.4.far, ...), custom_call_target="tpu_custom_call" | custom-call | flops 2000000000 | tf_op jit(solution)/shard_map/pallas_call | solution.py:489
  41.2 2.1 %shard_map.220 = bf16[128,2048]{1,0:T(8,128)(2,1)S(1)} custom-call(s32[8]{0:T(128)S(1)} %get-tuple-element.38.notes, bf16[2,128,2048]{2,1,0:T(8,128)(2,1)S(1)} %bitcast.19, bf16[160,2048]{1,0:T(8,128)(2,1)S(1)} %collective-permute-done.2.received, bf16[2,32,2048]{2,1,0:T(8,128)(2,1)S(1)} %get-tuple-element.41.weights, ...), custom_call_target="tpu_custom_call" | custom-call | flops 6000000000 | tf_op jit(solution)/shard_map/pallas_call | solution.py:489
  43.3 0.6 collective-permute-start.10
  43.9 4.6 %collective-permute-done.7.other = bf16[64,2048]{1,0:T(8,128)(2,1)S(1)} collective-permute-done((bf16[64,2048]{1,0:T(8,128)(2,1)S(1)}, bf16[64,2048]{1,0:T(8,128)(2,1)S(1)}, u32[]{:S(2)}, u32[]{:S(2)}) %collective-permute-start.7) | collective-permute-done | bytes 262176 | tf_op jit(solution)/shard_map/ppermute | solution.py:631
  48.6 0.1 collective-permute-start.8
  48.6 6.3 %collective-permute-done.9.act = bf16[128,2048]{1,0:T(8,128)(2,1)S(1)} collective-permute-done((bf16[128,2048]{1,0:T(8,128)(2,1)S(1)}, bf16[128,2048]{1,0:T(8,128)(2,1)S(1)}, u32[]{:S(2)}, u32[]{:S(2)}) %collective-permute-start.9) | collective-permute-done | bytes 524320 | tf_op jit(solution)/shard_map/ppermute | solution.py:522
  55.0 5.7 %collective-permute-done.10.grad = bf16[128,2048]{1,0:T(8,128)(2,1)S(1)} collective-permute-done((bf16[128,2048]{1,0:T(8,128)(2,1)S(1)}, bf16[128,2048]{1,0:T(8,128)(2,1)S(1)}, u32[]{:S(2)}, u32[]{:S(2)}) %collective-permute-start.10) | collective-permute-done | bytes 524320 | tf_op jit(solution)/shard_map/ppermute | solution.py:522
  60.7 2.3 %shard_map.221 = (bf16[128,2048]{1,0:T(8,128)(2,1)}, bf16[128,2048]{1,0:T(8,128)(2,1)}, f32[31,2,2048]{2,1,0:T(2,128)}, f32[2,2048]{1,0:T(2,128)}) custom-call(s32[2,8]{1,0:T(2,128)S(1)} %bitcast.27, bf16[64,2048]{1,0:T(8,128)(2,1)S(1)} %shard_map.217.mine, bf16[64,2048]{1,0:T(8,128)(2,1)S(1)} %collective-permute-done.8.other, ...), custom_call_target="tpu_custom_call" | custom-call | tf_op jit(solution)/shard_map/pallas_call | solution.py:489
  (50 shorter events, 0.3 us)
Async XLA Ops:
  0.6 5.1 %copy-start.11 = (bf16[1,2,2048]{2,1,0:T(2,128)(2,1)S(1)}, bf16[1,2,2048]{2,1,0:T(2,128)(2,1)}, u32[]{:S(2)}) copy-start(bf16[1,2,2048]{2,1,0:T(2,128)(2,1)} %param.23) | copy-start | bytes 24580
  0.6 5.1 %copy-start.5 = (bf16[1,2,31,2048]{3,1,2,0:T(2,128)(2,1)S(1)}, bf16[1,2,31,2048]{3,1,2,0:T(2,128)(2,1)}, u32[]{:S(2)}) copy-start(bf16[1,2,31,2048]{3,1,2,0:T(2,128)(2,1)} %param.22) | copy-start | bytes 761860
  0.7 18.0 %copy-start.6 = (bf16[384,192]{1,0:T(8,128)(2,1)S(1)}, bf16[384,192]{1,0:T(8,128)(2,1)}, u32[]{:S(2)}) copy-start(bf16[384,192]{1,0:T(8,128)(2,1)} %constant.21.clone.m_table) | copy-start | bytes 442372
  2.5 16.1 %collective-permute-start = (bf16[48,2048]{1,0:T(8,128)(2,1)}, bf16[48,2048]{1,0:T(8,128)(2,1)S(1)}, u32[]{:S(2)}, u32[]{:S(2)}) collective-permute-start(bf16[48,2048]{1,0:T(8,128)(2,1)} %get-tuple-element.39), channel_id=1, source_target_pairs={{0,1},{1,0},{2,3},{3,2},{4,5},{5,4},{6,7},{7,6},{8,9},{9,8},{10,11... | collective-permute-start | bytes 589832 | tf_op jit(solution)/shard_map/ppermute | solution.py:534
  3.8 14.9 %collective-permute-start.1 = (bf16[48,2048]{1,0:T(8,128)(2,1)}, bf16[48,2048]{1,0:T(8,128)(2,1)S(1)}, u32[]{:S(2)}, u32[]{:S(2)}) collective-permute-start(bf16[48,2048]{1,0:T(8,128)(2,1)} %get-tuple-element.40), channel_id=1, source_target_pairs={{1,2},{2,1},{5,6},{6,5},{9,10},{10,9},{13,14},{14,13},{17,18},{18,... | collective-permute-start | bytes 589832 | tf_op jit(solution)/shard_map/ppermute | solution.py:534
  5.7 1.2 %copy-start = (bf16[1,2,128,2048]{3,2,1,0:T(8,128)(2,1)S(1)}, bf16[1,2,128,2048]{3,2,1,0:T(8,128)(2,1)}, u32[]{:S(2)}) copy-start(bf16[1,2,128,2048]{3,2,1,0:T(8,128)(2,1)} %param.21) | copy-start | bytes 3145732
  7.0 1.0 %copy-start.2 = (bf16[1,128,2048]{2,1,0:T(8,128)(2,1)S(1)}, bf16[1,128,2048]{2,1,0:T(8,128)(2,1)}, u32[]{:S(2)}) copy-start(bf16[1,128,2048]{2,1,0:T(8,128)(2,1)} %param.19) | copy-start | bytes 1572868
  8.0 0.8 %copy-start.7 = (bf16[192,64]{1,0:T(8,128)(2,1)S(1)}, bf16[192,64]{1,0:T(8,128)(2,1)}, u32[]{:S(2)}) copy-start(bf16[192,64]{1,0:T(8,128)(2,1)} %constant.20.clone.q_table) | copy-start | bytes 73732
  8.8 0.7 %copy-start.12 = (f32[8,128]{1,0:T(8,128)S(1)}, f32[8,128]{1,0:T(8,128)}, u32[]{:S(2)}) copy-start(f32[8,128]{1,0:T(8,128)} %get-tuple-element.37.ready) | copy-start | bytes 12292
  9.5 0.7 %copy-start.13 = (s32[8,2]{0,1:T(2,128)S(1)}, s32[8,2]{0,1:T(2,128)}, u32[]{:S(2)}) copy-start(s32[8,2]{0,1:T(2,128)} %param.27) | copy-start | bytes 196
  12.2 6.5 %copy-start.4 = (bf16[1,128,2048]{2,1,0:T(8,128)(2,1)S(1)}, bf16[1,128,2048]{2,1,0:T(8,128)(2,1)}, u32[]{:S(2)}) copy-start(bf16[1,128,2048]{2,1,0:T(8,128)(2,1)} %grad.1) | copy-start | bytes 1572868
  12.2 6.5 %copy-start.18 = (bf16[384,160]{1,0:T(8,128)(2,1)S(1)}, bf16[384,160]{1,0:T(8,128)(2,1)}, u32[]{:S(2)}) copy-start(bf16[384,160]{1,0:T(8,128)(2,1)} %constant.23.clone.g_table) | copy-start | bytes 368644
  12.2 6.5 %copy-start.20 = (bf16[320,192]{1,0:T(8,128)(2,1)S(1)}, bf16[320,192]{1,0:T(8,128)(2,1)}, u32[]{:S(2)}) copy-start(bf16[320,192]{1,0:T(8,128)(2,1)} %constant.22.clone.c_table) | copy-start | bytes 368644
  12.2 6.6 %copy-start.21 = (bf16[256,192]{1,0:T(8,128)(2,1)S(1)}, bf16[256,192]{1,0:T(8,128)(2,1)}, u32[]{:S(2)}) copy-start(bf16[256,192]{1,0:T(8,128)(2,1)} %constant.24.clone.x_table) | copy-start | bytes 294916
  14.3 18.6 %collective-permute-start.5 = (bf16[64,2048]{1,0:T(8,128)(2,1)S(1)}, bf16[64,2048]{1,0:T(8,128)(2,1)S(1)}, u32[]{:S(2)}, u32[]{:S(2)}) collective-permute-start(bf16[64,2048]{1,0:T(8,128)(2,1)S(1)} %get-tuple-element.50), channel_id=1, source_target_pairs={{0,1},{1,0},{2,3},{3,2},{4,5},{5,4},{6,7},{7,6},{8,9},{9,8},{10,11... | collective-permute-start | bytes 786440 | tf_op jit(solution)/shard_map/ppermute | solution.py:534
  14.4 18.5 %collective-permute-start.6 = (bf16[64,2048]{1,0:T(8,128)(2,1)S(1)}, bf16[64,2048]{1,0:T(8,128)(2,1)S(1)}, u32[]{:S(2)}, u32[]{:S(2)}) collective-permute-start(bf16[64,2048]{1,0:T(8,128)(2,1)S(1)} %get-tuple-element.51), channel_id=1, source_target_pairs={{1,2},{2,1},{5,6},{6,5},{9,10},{10,9},{13,14},{14,13},{17,18},{18,... | collective-permute-start | bytes 786440 | tf_op jit(solution)/shard_map/ppermute | solution.py:534
  18.7 10.8 %copy-start.3 = (bf16[1,128,2048]{2,1,0:T(8,128)(2,1)S(1)}, bf16[1,128,2048]{2,1,0:T(8,128)(2,1)}, u32[]{:S(2)}) copy-start(bf16[1,128,2048]{2,1,0:T(8,128)(2,1)} %param.19) | copy-start | bytes 1572868
  18.7 10.8 %copy-start.8 = (bf16[192,64]{1,0:T(8,128)(2,1)S(1)}, bf16[192,64]{1,0:T(8,128)(2,1)}, u32[]{:S(2)}) copy-start(bf16[192,64]{1,0:T(8,128)(2,1)} %constant.20.clone.q_table) | copy-start | bytes 73732
  22.4 9.3 %copy-start.9 = (bf16[192,256]{1,0:T(8,128)(2,1)S(1)}, bf16[192,256]{1,0:T(8,128)(2,1)}, u32[]{:S(2)}) copy-start(bf16[192,256]{1,0:T(8,128)(2,1)} %constant.25.clone.go_table) | copy-start | bytes 294916
  22.5 9.3 %copy-start.10 = (bf16[64,192]{1,0:T(8,128)(2,1)S(1)}, bf16[64,192]{1,0:T(8,128)(2,1)}, u32[]{:S(2)}) copy-start(bf16[64,192]{1,0:T(8,128)(2,1)} %constant.26.clone.t_table) | copy-start | bytes 73732
  22.5 14.7 %collective-permute-start.2 = (bf16[160,2048]{1,0:T(8,128)(2,1)S(1)}, bf16[160,2048]{1,0:T(8,128)(2,1)S(1)}, u32[]{:S(2)}, u32[]{:S(2)}) collective-permute-start(bf16[160,2048]{1,0:T(8,128)(2,1)S(1)} %get-tuple-element.47), channel_id=1, source_target_pairs={{0,28},{4,0},{8,4},{12,8},{16,12},{20,16},{24,20},{28,24},{1,29},{... | collective-permute-start | bytes 1966088 | tf_op jit(solution)/shard_map/ppermute | solution.py:522
  24.0 15.6 %collective-permute-start.3 = (bf16[16,2048]{1,0:T(8,128)(2,1)S(1)}, bf16[16,2048]{1,0:T(8,128)(2,1)S(1)}, u32[]{:S(2)}, u32[]{:S(2)}) collective-permute-start(bf16[16,2048]{1,0:T(8,128)(2,1)S(1)} %get-tuple-element.48), channel_id=1, source_target_pairs={{0,29},{1,28},{2,31},{3,30},{4,1},{5,0},{6,3},{7,2},{8,5},{9,4},{1... | collective-permute-start | bytes 196616 | tf_op jit(solution)/shard_map/ppermute | solution.py:534
  24.2 15.5 %collective-permute-start.4 = (bf16[16,2048]{1,0:T(8,128)(2,1)S(1)}, bf16[16,2048]{1,0:T(8,128)(2,1)S(1)}, u32[]{:S(2)}, u32[]{:S(2)}) collective-permute-start(bf16[16,2048]{1,0:T(8,128)(2,1)S(1)} %get-tuple-element.49), channel_id=1, source_target_pairs={{1,30},{2,29},{5,2},{6,1},{9,6},{10,5},{13,10},{14,9},{17,14},{18,... | collective-permute-start | bytes 196616 | tf_op jit(solution)/shard_map/ppermute | solution.py:534
  35.0 2.2 %copy-start.19 = (bf16[320,160]{1,0:T(8,128)(2,1)S(1)}, bf16[320,160]{1,0:T(8,128)(2,1)}, u32[]{:S(2)}) copy-start(bf16[320,160]{1,0:T(8,128)(2,1)} %constant.27.clone.m_table) | copy-start | bytes 307204
  35.0 2.2 %copy-start.22 = (bf16[256,160]{1,0:T(8,128)(2,1)S(1)}, bf16[256,160]{1,0:T(8,128)(2,1)}, u32[]{:S(2)}) copy-start(bf16[256,160]{1,0:T(8,128)(2,1)} %constant.29.clone.c_table) | copy-start | bytes 245764
  35.1 2.2 %copy-start.23 = (bf16[160,64]{1,0:T(8,128)(2,1)S(1)}, bf16[160,64]{1,0:T(8,128)(2,1)}, u32[]{:S(2)}) copy-start(bf16[160,64]{1,0:T(8,128)(2,1)} %constant.28.clone.q_table) | copy-start | bytes 61444
  39.4 15.6 %collective-permute-start.9 = (bf16[128,2048]{1,0:T(8,128)(2,1)S(1)}, bf16[128,2048]{1,0:T(8,128)(2,1)S(1)}, u32[]{:S(2)}, u32[]{:S(2)}) collective-permute-start(bf16[128,2048]{1,0:T(8,128)(2,1)S(1)} %shard_map.219), channel_id=1, source_target_pairs={{0,8},{4,12},{8,16},{12,20},{16,24},{20,28},{24,0},{28,4},{1,9},{5... | collective-permute-start | bytes 1572872 | tf_op jit(solution)/shard_map/ppermute | solution.py:522
  39.7 1.6 %copy-start.1 = (bf16[1,2,128,2048]{3,2,1,0:T(8,128)(2,1)S(1)}, bf16[1,2,128,2048]{3,2,1,0:T(8,128)(2,1)}, u32[]{:S(2)}) copy-start(bf16[1,2,128,2048]{3,2,1,0:T(8,128)(2,1)} %param.21) | copy-start | bytes 3145732
  41.2 7.3 %collective-permute-start.7 = (bf16[64,2048]{1,0:T(8,128)(2,1)S(1)}, bf16[64,2048]{1,0:T(8,128)(2,1)S(1)}, u32[]{:S(2)}, u32[]{:S(2)}) collective-permute-start(bf16[64,2048]{1,0:T(8,128)(2,1)S(1)} %get-tuple-element.60.mine), channel_id=1, source_target_pairs={{0,1},{1,0},{2,3},{3,2},{4,5},{5,4},{6,7},{7,6},{8,9},{9,8},{10,11... | collective-permute-start | bytes 786440 | tf_op jit(solution)/shard_map/ppermute | solution.py:631
  43.3 17.4 %copy-start.14 = (s32[8,2]{0,1:T(2,128)S(1)}, s32[8,2]{0,1:T(2,128)}, u32[]{:S(2)}) copy-start(s32[8,2]{0,1:T(2,128)} %param.27) | copy-start | bytes 196
  43.3 17.4 %collective-permute-start.10 = (bf16[128,2048]{1,0:T(8,128)(2,1)S(1)}, bf16[128,2048]{1,0:T(8,128)(2,1)S(1)}, u32[]{:S(2)}, u32[]{:S(2)}) collective-permute-start(bf16[128,2048]{1,0:T(8,128)(2,1)S(1)} %shard_map.220), channel_id=1, source_target_pairs={{0,28},{4,0},{8,4},{12,8},{16,12},{20,16},{24,20},{28,24},{1,29},{... | collective-permute-start | bytes 1572872 | tf_op jit(solution)/shard_map/ppermute | solution.py:522
  48.6 6.4 %collective-permute-start.8 = (bf16[64,2048]{1,0:T(8,128)(2,1)S(1)}, bf16[64,2048]{1,0:T(8,128)(2,1)S(1)}, u32[]{:S(2)}, u32[]{:S(2)}) collective-permute-start(bf16[64,2048]{1,0:T(8,128)(2,1)S(1)} %shard_map.217.mine), channel_id=1, source_target_pairs={{0,2},{1,3},{2,0},{3,1},{4,6},{5,7},{6,4},{7,5},{8,10},{9,11},{10,... | collective-permute-start | bytes 786440 | tf_op jit(solution)/shard_map/ppermute | solution.py:631
  (3 other events, 2.0 us)

commit v9 on v8

--- a/solution.py
+++ b/solution.py
@@ -209,11 +209,9 @@
 
 
 def prepare_kernel(
-    reach, back_lengths, ahead_lengths, back_slots, ahead_slots, kernels, gains, saved, act, ready, q_table,
-    weights, later, near, far, notes, masked, mean, inverse, q,
+    reach, notes, kernels, gains, saved, act, q_table, weights, later, near, far, masked, mean, inverse, q
 ):
     own, width = act.shape
-    section, sections = lax.axis_index("section"), lax.axis_size("section")
     for even in range(2):
 
         @pl.when(lax.rem(lax.axis_index("tm") + 1, 2) == even)
@@ -227,36 +225,14 @@
     for slot in range(kernels.shape[1]):
         weights[slot, :count, :] = kernels[:, slot, :]
         weights[slot, count:, :] = gains[slot : slot + 1, :]
-    later[...] = weights[ahead_slots[1, section]]
-    slot, length, first = back_slots[0, section], back_lengths[section], lax.axis_index("tm") * own
-    notes[FIRST] = first
-    notes[BACK0] = slot
-    notes[BACK0 + 1] = length
-    notes[BACK1] = back_slots[1, section]
-    notes[BACK1 + 1] = back_lengths[lax.rem(section + 1, sections)]
-    notes[AHEAD0] = ahead_slots[0, section]
-    notes[AHEAD0 + 1] = ahead_lengths[section]
+    later[...] = weights[notes[FIRST + 1]]
+    slot, length, first = looked_up(notes, BACK0)
     norm_pieces([(saved.at[0], 0, own)], slot_row(weights, slot), first, length, masked, mean, inverse)
 
     def block(columns):
         q[:, columns] = tap_spectrum(q_table[...], weights[slot, :, columns])
 
     each_block(width, block)
-
-
-def prepare_later_kernel(notes, saved, act, weights, ready, q_table, *outs):
-    own, width = act.shape
-    layers = ((saved.at[1], BACK1, outs[:4]), (act, AHEAD0, outs[4:]))
-    for x, layer, (masked, mean, inverse, _) in layers:
-        slot, length, first = looked_up(notes, layer)
-        norm_pieces([(x, 0, own)], slot_row(weights, slot), first, length, masked, mean, inverse)
-    for _, layer, (_, _, _, q) in layers:
-        slot = notes[layer]
-
-        def block(columns, slot=slot, q=q):
-            q[:, columns] = tap_spectrum(q_table[...], weights[slot, :, columns])
-
-        each_block(width, block)
 
 
 def norm_halo(left, right, own, gain, first, length, halo):
@@ -329,22 +305,37 @@
     each_block(masked.shape[1], block)
 
 
+def added(mine, other):
+    return (mine[...].astype(F32) + other[...].astype(F32)).astype(BF16)
+
+
 def add_kernel(mine, other, out):
-    out[...] = (mine[...].astype(F32) + other[...].astype(F32)).astype(out.dtype)
+    out[...] = added(mine, other)
+
+
+def below_kernel(mine0, other0, mine1, other1, out):
+    count = mine0.shape[0]
+    out[pl.ds(0, count), :] = added(mine0, other0)
+    out[pl.ds(count, count), :] = added(mine1, other1)
 
 
 def second_ready_kernel(
-    reach, notes, near, far, weights, masked, q, m_table, c_table, m_out, factor, conv_out, halo, halos
+    reach, notes, saved, near, far, weights, m_table, q_table, c_table,
+    m_out, q_out, factor, conv_out, mean, inverse, halo, halos, masked,
 ):
     own, width = masked.shape
     slot, length, first = looked_up(notes, BACK1)
+    gain = slot_row(weights, slot)
     left, right = sorted_halos(near, far, 0, halos)
-    norm_halo(left, right, own, slot_row(weights, slot), first, length, halo)
+    norm_pieces([(saved.at[1], 0, own)], gain, first, length, masked, mean, inverse)
+    norm_halo(left, right, own, gain, first, length, halo)
 
     def block(columns):
         m = transform(m_table, joined(halo, masked, columns))
-        conv = transform(c_table, product(m, q[:, columns]))
+        q = tap_spectrum(q_table[...], weights[slot, :, columns])
+        conv = transform(c_table, product(m, q))
         m_out[:, columns] = m
+        q_out[:, columns] = q
         factor[:, columns] = gate_factor(conv)
         edge = (conv.shape[0] - own) // 2
         conv_out[:, columns] = conv[edge : edge + own]
@@ -353,13 +344,10 @@
 
 
 def second_taps_kernel(
-    notes, received, near, far, weights, m, factor, conv, taps0, go_table, t_table, mixed_out, taps, halos
+    notes, received, near, far, weights, m, factor, conv, go_table, t_table, mixed_out, taps, halos
 ):
     own, width = conv.shape
     rows = factor.shape[0]
-    count = taps0.shape[0]
-    taps[pl.ds(0, count), :] = taps0[...]
-    taps1 = taps.at[pl.ds(count, count)]
     edge = (rows - own) // 2
     gain = slot_row(weights, notes[BACK1])
     left, right = sorted_halos(near, far, 0, halos)
@@ -370,7 +358,7 @@
         mixed_out[:, columns] = mixed
         inner = mixed[edge : edge + own]
         gain_sum = jnp.sum(inner.astype(F32) * conv[:, columns], axis=0, keepdims=True) / gain(columns)
-        put_taps(taps1, tap_term(go_table, t_table, m[:, columns], inner), gain_sum, columns)
+        put_taps(taps, tap_term(go_table, t_table, m[:, columns], inner), gain_sum, columns)
 
     each_block(width, block)
 
@@ -395,16 +383,19 @@
     last_pass([(received, 0, own)], pieces, mean, inverse, scaled, sum_a, sum_b, grad_x)
 
 
-def first_forward_kernel(reach, notes, act, near, far, weights, masked, q, m_table, c_table, out, halo, halos):
+def first_forward_kernel(reach, notes, act, near, far, weights, m_table, q_table, c_table, out, halo, halos, masked):
     own, width = act.shape
     middle = reach // 2
     slot, length, first = looked_up(notes, AHEAD0)
+    gain = slot_row(weights, slot)
     left, right = sorted_halos(near, far, reach, halos)
     inner = [(left, middle, middle), (act, 0, own), (right, 0, middle)]
-    norm_halo(left, right, own, slot_row(weights, slot), first, length, halo)
-
-    def block(columns):
-        conv = transform(c_table, product(transform(m_table, joined(halo, masked, columns)), q[:, columns]))
+    norm_pieces([(act, 0, own)], gain, first, length, masked)
+    norm_halo(left, right, own, gain, first, length, halo)
+
+    def block(columns):
+        q = tap_spectrum(q_table[...], weights[slot, :, columns])
+        conv = transform(c_table, product(transform(m_table, joined(halo, masked, columns)), q))
         out[:, columns] = (window(inner, columns).astype(F32) + conv * sigmoid(conv)).astype(BF16)
 
     each_block(width, block)
@@ -430,7 +421,10 @@
     each_block(width, block)
 
 
-def pack_kernel(reaches, saved, grad, near, far, ready, sems):
+def pack_kernel(
+    reaches, saved, grad, back_lengths, ahead_lengths, back_slots, ahead_slots,
+    near, far, notes, back_len, ahead_len, back_slot, ahead_slot, sems,
+):
     own = grad.shape[1]
     even = lax.rem(lax.axis_index("tm") + 1, 2)
     copies = []
@@ -438,32 +432,37 @@
     for x, reach in zip((saved, grad), reaches):
         for out, tail in ((near, even), (far, 1 - even)):
             start = pl.multiple_of(tail * (own - reach), 16)
-            copies.append(
-                pltpu.make_async_copy(
-                    x.at[0, pl.ds(start, reach)], out.at[pl.ds(at, reach)], sems.at[len(copies)]
-                )
-            )
+            copies.append((x.at[0, pl.ds(start, reach)], out.at[pl.ds(at, reach)]))
         at += reach
-    ready[...] = jnp.zeros_like(ready)
+    small = [(back_lengths, back_len), (ahead_lengths, ahead_len), (back_slots, back_slot), (ahead_slots, ahead_slot)]
+    copies = [pltpu.make_async_copy(a, b, sems.at[k]) for k, (a, b) in enumerate(small + copies)]
     for copy in copies:
         copy.start()
     for copy in copies:
         copy.wait()
-
-
-def final_kernel(slots, mine, other, act, grad, act_out, grad_out, taps, gains, sems):
+    section, sections = lax.axis_index("section"), lax.axis_size("section")
+    notes[FIRST] = lax.axis_index("tm") * own
+    notes[FIRST + 1] = ahead_slot[1, section]
+    notes[BACK0] = back_slot[0, section]
+    notes[BACK0 + 1] = back_len[section]
+    notes[BACK1] = back_slot[1, section]
+    notes[BACK1 + 1] = back_len[lax.rem(section + 1, sections)]
+    notes[AHEAD0] = ahead_slot[0, section]
+    notes[AHEAD0 + 1] = ahead_len[section]
+
+
+def final_kernel(notes, mine, other, act, grad, act_out, grad_out, taps, gains, sems):
     copies = [
         pltpu.make_async_copy(act, act_out, sems.at[0]),
         pltpu.make_async_copy(grad, grad_out, sems.at[1]),
     ]
     for copy in copies:
         copy.start()
-    section = lax.axis_index("section")
     count = taps.shape[0]
     total = mine[...].astype(F32) + other[...].astype(F32)
     ticks = total[: count + 1], total[count + 1 :]
     for slot in range(taps.shape[1]):
-        use = [(slots[tick, section] == slot).astype(F32) for tick in range(2)]
+        use = [(notes[layer] == slot).astype(F32) for layer in (BACK0, BACK1)]
         both = use[0] * ticks[0] + use[1] * ticks[1]
         taps[:, slot, :] = both[:count]
         gains[slot : slot + 1, :] = both[count:]
@@ -483,9 +482,16 @@
 FULL = 127 * 512 * 1024
 
 
-def call(kernel, outs, scratch, operands, micros, specs=None, out_specs=None, limit=LIMIT):
+def call(kernel, outs, scratch, operands, micros, specs=None, out_specs=None, limit=LIMIT, after=None):
     if specs is None:
         specs = [SMEM if x.dtype == jnp.int32 else VMEM for x in operands]
+    if after is not None:
+        operands, specs = [*operands, after], [*specs, ANY]
+        inner, place = kernel, len(operands) - 1
+
+        def kernel(*refs):
+            return inner(*refs[:place], *refs[place + 1 :])
+
     return pl.pallas_call(
         kernel,
         out_shape=outs,
@@ -523,7 +529,7 @@
 
     def swapped(near, far, by=0):
         results = []
-        for x, begin in ((near, 0), (far, 1)):
+        for x, begin in ((far, 1), (near, 0)):
             pairs = [(i, i + 1) for i in range(begin, shards - 1, 2)]
             pairs = [
                 (s * shards + i, (s + by) % sections * shards + j)
@@ -532,14 +538,17 @@
                 for i, j in ((a, b), (b, a))
             ]
             results.append(lax.ppermute(x, ("section", "tm"), pairs))
-        return results
-
-    near0, far0, ready = call(
+        return results[::-1]
+
+    lengths = pltpu.SMEM(backward_lengths.shape, jnp.int32)
+    forward_slots, backward_slots = forward_slots.T, backward_slots.T
+    slots = pltpu.SMEM(backward_slots.shape, jnp.int32)
+    near0, far0, notes = call(
         functools.partial(pack_kernel, (two, one)),
-        (like(two + one, width, BF16), like(two + one, width, BF16), like(8, LANES, F32)),
-        [pltpu.SemaphoreType.DMA((4,))],
-        (saved, grad_in),
-        0, [HBM] * 2, None, FULL,
+        (like(two + one, width, BF16), like(two + one, width, BF16), jax.ShapeDtypeStruct((8,), jnp.int32)),
+        [lengths, lengths, slots, slots, pltpu.SemaphoreType.DMA((8,))],
+        (saved, grad_in, backward_lengths, forward_lengths, backward_slots, forward_slots),
+        0, [HBM] * 6, (VMEM, VMEM, SMEM), FULL,
     )
     near0, far0 = swapped(near0, far0)
     tap_back = np.concatenate([from_freq(size, np.arange(tap_count) - half), np.zeros((1, size))], axis=0)
@@ -549,28 +558,20 @@
     go_table = beside(to_freq(size, np.arange(own)))
     t_table = stacked(tap_back)
 
-    def run(kernel, outs, scratch, operands, micros=0):
-        return call(kernel, outs, scratch, [jnp.asarray(x) for x in operands], micros)
+    def run(kernel, outs, scratch, operands, micros=0, after=None):
+        return call(kernel, outs, scratch, [jnp.asarray(x) for x in operands], micros, after=after)
 
     rows = [pltpu.VMEM((own, width), F32)] + [pltpu.VMEM((own, LANES), F32)] * 2
-    forward_slots, backward_slots = forward_slots.T, backward_slots.T
-
-    def layer(size):
-        return like(own, width, BF16), like(own, LANES, F32), like(own, LANES, F32), like(size, width, F32)
-
-    weights, later, near1, far1, notes, *layer0 = call(
+    layer = like(own, width, BF16), like(own, LANES, F32), like(own, LANES, F32), like(size, width, F32)
+    weights, later, near1, far1, *layer0 = run(
         functools.partial(prepare_kernel, two),
         (
             jax.ShapeDtypeStruct((kernels.shape[1], tap_count + 1, width), BF16), like(tap_count + 1, width, BF16),
-            like(2 * two, width, BF16), like(2 * two, width, BF16), jax.ShapeDtypeStruct((8,), jnp.int32), *layer(size),
+            like(2 * two, width, BF16), like(2 * two, width, BF16), *layer,
         ),
         [],
-        [
-            backward_lengths, forward_lengths, backward_slots, forward_slots,
-            kernels[0].transpose(1, 0, 2), norm_gains[0], saved, act, ready, jnp.asarray(q_table),
-        ],
+        [notes, kernels[0].transpose(1, 0, 2), norm_gains[0], saved, act, q_table],
         0,
-        None, (VMEM,) * 4 + (SMEM,) + (VMEM,) * 4,
     )
     near1, far1 = swapped(near1, far1)
     g_table, x_table = stacked(to_freq(size, span(one, own))), stacked(from_freq(size, span(0, own)))
@@ -589,31 +590,17 @@
     )
     grad_mid = shifted(grad_mid, -1)
     near2, far2 = swapped(near2, far2, -1)
-    layers = run(
-        prepare_later_kernel, (*layer(size), *layer(size)), [], [notes, saved, act, weights, gain0, q_table], 0
-    )
-    masked1, mean1, inverse1, q1, masked2, _, _, q2 = layers
-    taps0 = run(
-        first_taps_kernel, like(tap_count + 1, width, BF16), [],
-        [halo0, layer0[0], inner0, gain0, m_table, go_table, t_table],
-        0,
-    )
-    halo_scratch = [pltpu.VMEM((2 * two, width), BF16), pltpu.VMEM((2, two, width), BF16)]
+    halo_scratch = [
+        pltpu.VMEM((2 * two, width), BF16), pltpu.VMEM((2, two, width), BF16), pltpu.VMEM((own, width), BF16)
+    ]
     between = run(
         functools.partial(first_forward_kernel, two),
         like(small, width, BF16),
         halo_scratch,
-        [notes, act, near1, far1, weights, masked2, q2, m_table, c_table],
-        3,
-    )
-    m1, factor1, conv1 = run(
-        functools.partial(second_ready_kernel, two),
-        (like(size, width, F32), like(small, width, F32), like(own, width, F32)),
-        halo_scratch,
-        [notes, near1, far1, weights, masked1, q1, m_table, c_table],
-        3,
-    )
-    act_out = run(
+        [notes, act, near1, far1, weights, m_table, q_table, c_table],
+        20,
+    )
+    act_ahead = run(
         second_forward_kernel,
         like(own, width, BF16),
         [pltpu.VMEM((small, width), BF16)],
@@ -623,22 +610,34 @@
         ],
         3,
     )
-    act_out = shifted(act_out, 2)
-
-    def summed(x, micros):
-        step = 1
-        while True:
-            other = lax.ppermute(x, "tm", [(i, i ^ step) for i in range(shards)])
-            step *= 2
-            if step >= shards:
-                return x, other
-            x = call(add_kernel, like(*x.shape, BF16), [], (x, other), micros)
-
-    mixed1, sums = run(
+    act_out = shifted(act_ahead, 2)
+    taps0 = run(
+        first_taps_kernel, like(tap_count + 1, width, BF16), [],
+        [halo0, layer0[0], inner0, gain0, m_table, go_table, t_table],
+        0,
+        act_ahead,
+    )
+    m1, q1, factor1, conv1, mean1, inverse1 = run(
+        functools.partial(second_ready_kernel, two),
+        (
+            like(size, width, F32), like(size, width, F32), like(small, width, F32), like(own, width, F32),
+            like(own, LANES, F32), like(own, LANES, F32),
+        ),
+        halo_scratch,
+        [notes, saved, near1, far1, weights, m_table, q_table, c_table],
+        3,
+        act_ahead,
+    )
+
+    def partner(x, step):
+        return lax.ppermute(x, "tm", [(i, i ^ step) for i in range(shards)])
+
+    other0 = partner(taps0, 1)
+    mixed1, taps1 = run(
         second_taps_kernel,
-        (like(small, width, BF16), like(2 * (tap_count + 1), width, BF16)),
+        (like(small, width, BF16), like(tap_count + 1, width, BF16)),
         [pltpu.VMEM((2, one, width), BF16)],
-        [notes, grad_mid, near2, far2, weights, m1, factor1, conv1, taps0, go_table, t_table],
+        [notes, grad_mid, near2, far2, weights, m1, factor1, conv1, go_table, t_table],
         2,
     )
     grad_out = run(
@@ -652,7 +651,15 @@
         6,
     )
     grad_out = shifted(grad_out, -1)
-    sums = summed(sums, 6)
+    other1 = partner(taps1, 1)
+    mine = call(below_kernel, like(2 * (tap_count + 1), width, BF16), [], (taps0, other0, taps1, other1), 6)
+    step = 2
+    while True:
+        other = partner(mine, step)
+        step *= 2
+        if step >= shards:
+            break
+        mine = call(add_kernel, like(*mine.shape, BF16), [], (mine, other), 0)
     slots = kernels.shape[1]
     act_out, grad_out, taps, gains = call(
         final_kernel,
@@ -661,7 +668,7 @@
             jax.ShapeDtypeStruct((tap_count, slots, width), F32), like(slots, width, F32),
         ),
         [pltpu.SemaphoreType.DMA((2,))],
-        (backward_slots, *sums, act_out, grad_out),
+        (notes, mine, other, act_out, grad_out),
         0, [SMEM] + [VMEM] * 2 + [ANY] * 2, (ANY, ANY, VMEM, VMEM),
     )
     return act_out[None], grad_out[None], taps.transpose(1, 0, 2)[None], gains[None]

time: 63.6 us -> 57.6 us (0.906)
  the two profiles are of different devices: /device:TPU:5 before, /device:TPU:0 now
where the time goes in v9:
time: 57.6 us; the launch traced here: 56.8 us
  starting transfers between devices  22.2 us (39%)
  Pallas kernels  21.6 us (38%)
  waiting for transfers between devices  8.05 us (14%)
  local copies, waits for them, and re-layouts  3.79 us (7%)
  between operations  1.14 us (2%)
    pallas_call x11, Pallas kernels, call(): pl.pallas_call(kernel, out_shape=outs, in_specs=specs, out_specs=jax.tree...  21.6 us
    ppermute x6, starting transfers between devices, swapped(): results.append(lax.ppermute(x, ('section', 'tm'), pairs))  12.2 us
    ppermute x3, waiting for transfers between devices, partner(): return lax.ppermute(x, 'tm', [(i, i ^ step) for i in range(shards)])  6 us
    ppermute x3, starting transfers between devices, partner(): return lax.ppermute(x, 'tm', [(i, i ^ step) for i in range(shards)])  5.27 us
    ppermute x3, starting transfers between devices, shifted(): lax.ppermute(x, 'section', [(i, (i + by) % sections) for i in range(secti...  4.79 us
    unnamed x40, local copies, waits for them, and re-layouts  3.79 us
    ppermute x3, waiting for transfers between devices, shifted(): lax.ppermute(x, 'section', [(i, (i + by) % sections) for i in range(secti...  2.03 us
  transfers between devices with their start and end apart: 12, of which 3 were waited for; matrix products, arithmetic and copies ran while one was open for 0% of the time, Pallas kernels for 31%

profile of v9, /device:TPU:0, one launch (start us, length us, event | category | flops | bytes accessed | tf_op | source)
XLA Modules:
  0.0 56.8 jit_solution(17415784779735472086)
XLA Ops:
  0.7 0.0 copy-start.6
  0.7 1.9 %shard_map.210 = (bf16[48,2048]{1,0:T(8,128)(2,1)}, bf16[48,2048]{1,0:T(8,128)(2,1)}, s32[8]{0:T(128)}) custom-call(bf16[2,128,2048]{2,1,0:T(8,128)(2,1)} %bitcast.15, bf16[1,128,2048]{2,1,0:T(8,128)(2,1)} %grad.1, s32[8]{0:T(128)} %back_lengths.1, s32[8]{0:T(128)} %ahead_lengths.1, s32[2,8]{1,0:T(2,128)} %bitcast.25, s32[2,8]{1,0:T(2,128)} %bitcast.26), custom_call_target="tpu_custom_call" | custom-call | tf_op jit(solution)/shard_map/pallas_call | solution.py:495
  2.6 3.0 %collective-permute-start = (bf16[48,2048]{1,0:T(8,128)(2,1)}, bf16[48,2048]{1,0:T(8,128)(2,1)S(1)}, u32[]{:S(2)}, u32[]{:S(2)}) collective-permute-start(bf16[48,2048]{1,0:T(8,128)(2,1)} %get-tuple-element.34), channel_id=1, source_target_pairs={{0,1},{1,0},{2,3},{3,2},{4,5},{5,4},{6,7},{7,6},{8,9},{9,8},{10,11... | collective-permute-start | bytes 589832 | tf_op jit(solution)/shard_map/ppermute | solution.py:540
  5.6 0.7 %collective-permute-start.1 = (bf16[48,2048]{1,0:T(8,128)(2,1)}, bf16[48,2048]{1,0:T(8,128)(2,1)S(1)}, u32[]{:S(2)}, u32[]{:S(2)}) collective-permute-start(bf16[48,2048]{1,0:T(8,128)(2,1)} %get-tuple-element.35), channel_id=1, source_target_pairs={{1,2},{2,1},{5,6},{6,5},{9,10},{10,9},{13,14},{14,13},{17,18},{18,... | collective-permute-start | bytes 589832 | tf_op jit(solution)/shard_map/ppermute | solution.py:540
  6.3 1.2 %copy-done = bf16[1,2,128,2048]{3,2,1,0:T(8,128)(2,1)S(1)} copy-done((bf16[1,2,128,2048]{3,2,1,0:T(8,128)(2,1)S(1)}, bf16[1,2,128,2048]{3,2,1,0:T(8,128)(2,1)}, u32[]{:S(2)}) %copy-start) | copy-done | bytes 1048600
  7.5 1.0 %copy-done.3 = bf16[1,128,2048]{2,1,0:T(8,128)(2,1)S(1)} copy-done((bf16[1,128,2048]{2,1,0:T(8,128)(2,1)S(1)}, bf16[1,128,2048]{2,1,0:T(8,128)(2,1)}, u32[]{:S(2)}) %copy-start.3) | copy-done | bytes 524312
  8.5 0.8 %copy-done.8 = bf16[192,64]{1,0:T(8,128)(2,1)S(1)} copy-done((bf16[192,64]{1,0:T(8,128)(2,1)S(1)}, bf16[192,64]{1,0:T(8,128)(2,1)}, u32[]{:S(2)}) %copy-start.8) | copy-done | bytes 24600
  9.3 0.7 %copy-done.12 = s32[8]{0:T(128)S(1)} copy-done((s32[8]{0:T(128)S(1)}, s32[8]{0:T(128)}, u32[]{:S(2)}) %copy-start.12) | copy-done | bytes 56
  10.0 1.7 %shard_map.211 = (bf16[2,32,2048]{2,1,0:T(8,128)(2,1)S(1)}, bf16[32,2048]{1,0:T(8,128)(2,1)S(1)}, bf16[64,2048]{1,0:T(8,128)(2,1)S(1)}, bf16[64,2048]{1,0:T(8,12...) custom-call(s32[8]{0:T(128)S(1)} %copy-done.12, ...), custom_call_target="tpu_custom_call" | custom-call | tf_op jit(solution)/shard_map/pallas_call | solution.py:495
  11.7 4.3 %collective-permute-start.2 = (bf16[64,2048]{1,0:T(8,128)(2,1)S(1)}, bf16[64,2048]{1,0:T(8,128)(2,1)S(1)}, u32[]{:S(2)}, u32[]{:S(2)}) collective-permute-start(bf16[64,2048]{1,0:T(8,128)(2,1)S(1)} %get-tuple-element.45), channel_id=1, source_target_pairs={{0,1},{1,0},{2,3},{3,2},{4,5},{5,4},{6,7},{7,6},{8,9},{9,8},{10,11... | collective-permute-start | bytes 786440 | tf_op jit(solution)/shard_map/ppermute | solution.py:540
  16.0 0.7 %collective-permute-start.3 = (bf16[64,2048]{1,0:T(8,128)(2,1)S(1)}, bf16[64,2048]{1,0:T(8,128)(2,1)S(1)}, u32[]{:S(2)}, u32[]{:S(2)}) collective-permute-start(bf16[64,2048]{1,0:T(8,128)(2,1)S(1)} %get-tuple-element.46), channel_id=1, source_target_pairs={{1,2},{2,1},{5,6},{6,5},{9,10},{10,9},{13,14},{14,13},{17,18},{18,... | collective-permute-start | bytes 786440 | tf_op jit(solution)/shard_map/ppermute | solution.py:540
  16.8 0.0 copy-start.9
  16.8 3.7 %shard_map.212 = (bf16[160,2048]{1,0:T(8,128)(2,1)S(1)}, bf16[16,2048]{1,0:T(8,128)(2,1)S(1)}, bf16[16,2048]{1,0:T(8,128)(2,1)S(1)}, bf16[64,2048]{1,0:T(8,128)(...) custom-call(s32[8]{0:T(128)S(1)} %copy-done.12, bf16[2,128,2048]{2,1,0:T(8,128)(2,1)S(1)} %bitcast.17, ...), custom_call_target="tpu_custom_call" | custom-call | flops 4000000000 | tf_op jit(solution)/shard_map/pallas_call | solution.py:495
  20.5 2.3 %collective-permute-start.4 = (bf16[160,2048]{1,0:T(8,128)(2,1)S(1)}, bf16[160,2048]{1,0:T(8,128)(2,1)S(1)}, u32[]{:S(2)}, u32[]{:S(2)}) collective-permute-start(bf16[160,2048]{1,0:T(8,128)(2,1)S(1)} %get-tuple-element.47), channel_id=1, source_target_pairs={{0,28},{4,0},{8,4},{12,8},{16,12},{20,16},{24,20},{28,24},{1,29},{... | collective-permute-start | bytes 1966088 | tf_op jit(solution)/shard_map/ppermute | solution.py:528
  22.8 2.8 %collective-permute-start.6 = (bf16[16,2048]{1,0:T(8,128)(2,1)S(1)}, bf16[16,2048]{1,0:T(8,128)(2,1)S(1)}, u32[]{:S(2)}, u32[]{:S(2)}) collective-permute-start(bf16[16,2048]{1,0:T(8,128)(2,1)S(1)} %get-tuple-element.48), channel_id=1, source_target_pairs={{0,29},{1,28},{2,31},{3,30},{4,1},{5,0},{6,3},{7,2},{8,5},{9,4},{1... | collective-permute-start | bytes 196616 | tf_op jit(solution)/shard_map/ppermute | solution.py:540
  25.5 0.8 %collective-permute-start.7 = (bf16[16,2048]{1,0:T(8,128)(2,1)S(1)}, bf16[16,2048]{1,0:T(8,128)(2,1)S(1)}, u32[]{:S(2)}, u32[]{:S(2)}) collective-permute-start(bf16[16,2048]{1,0:T(8,128)(2,1)S(1)} %get-tuple-element.49), channel_id=1, source_target_pairs={{1,30},{2,29},{5,2},{6,1},{9,6},{10,5},{13,10},{14,9},{17,14},{18,... | collective-permute-start | bytes 196616 | tf_op jit(solution)/shard_map/ppermute | solution.py:540
  26.4 2.4 %shard_map.213.between = bf16[160,2048]{1,0:T(8,128)(2,1)S(1)} custom-call(s32[8]{0:T(128)S(1)} %copy-done.13, bf16[128,2048]{1,0:T(8,128)(2,1)S(1)} %bitcast.22, bf16[64,2048]{1,0:T(8,128)(2,1)S(1)} %collective-permute-done.2.near.refs_2_, bf16[64,2048]{1,0:T(8,128)(2,1)S(1)} %collective-permute-done.3.far.refs_3_, ...), custom_call_target="tpu_custom_call" | custom-call | flops 20000000000 | tf_op jit(solution)/shard_map/pallas_call | solution.py:495
  28.9 2.0 %collective-permute-done.4.received = bf16[160,2048]{1,0:T(8,128)(2,1)S(1)} collective-permute-done((bf16[160,2048]{1,0:T(8,128)(2,1)S(1)}, bf16[160,2048]{1,0:T(8,128)(2,1)S(1)}, u32[]{:S(2)}, u32[]{:S(2)}) %collective-permute-start.4) | collective-permute-done | bytes 655392 | tf_op jit(solution)/shard_map/ppermute | solution.py:528
  30.9 2.1 %shard_map.214.refs_7_.refs_8_ = bf16[128,2048]{1,0:T(8,128)(2,1)S(1)} custom-call(s32[8]{0:T(128)S(1)} %copy-done.13, bf16[160,2048]{1,0:T(8,128)(2,1)S(1)} %shard_map.213.between, bf16[160,2048]{1,0:T(8,128)(2,1)S(1)} %collective-permute-done.4.received, bf16[320,160]{1,0:T(8,128)(2,1)S(1)} %copy-done.16, bf16[160,64]{1,0:T(8,128)(2,1)S(1)} %copy-done.19, ...), custom_call_target="tpu_custom_call" | custom-call | flops 3000000000 | tf_op jit(solution)/shard_map/pallas_call | solution.py:495
  33.0 0.2 collective-permute-start.10
  33.3 1.1 %shard_map.215.mine0 = bf16[32,2048]{1,0:T(8,128)(2,1)S(1)} custom-call(bf16[64,2048]{1,0:T(8,128)(2,1)S(1)} %get-tuple-element.42.refs_0_, bf16[128,2048]{1,0:T(8,128)(2,1)S(1)} %get-tuple-element.38.masked.refs_1_, bf16[128,2048]{1,0:T(8,128)(2,1)S(1)} %get-tuple-element.43.refs_2_, f32[1,2048]{1,0:T(1,128)S(1)} %get-tuple-element.44.refs_3_, ...), custom_call_target="tpu_custom_call" | custom-call | tf_op jit(solution)/shard_map/pallas_call | solution.py:495
  34.5 3.0 %collective-permute-start.5 = (bf16[32,2048]{1,0:T(8,128)(2,1)S(1)}, bf16[32,2048]{1,0:T(8,128)(2,1)S(1)}, u32[]{:S(2)}, u32[]{:S(2)}) collective-permute-start(bf16[32,2048]{1,0:T(8,128)(2,1)S(1)} %shard_map.215.mine0), channel_id=1, source_target_pairs={{0,1},{1,0},{2,3},{3,2},{4,5},{5,4},{6,7},{7,6},{8,9},{9,8},{10,11... | collective-permute-start | bytes 393224 | tf_op jit(solution)/shard_map/ppermute | solution.py:633
  37.5 2.6 %shard_map.216 = (f32[192,2048]{1,0:T(8,128)S(1)}, f32[192,2048]{1,0:T(8,128)S(1)}, f32[160,2048]{1,0:T(8,128)S(1)}, f32[128,2048]{1,0:T(8,128)S(1)}, f32[128,128]{1,0:T(8,128)S(1)}, /*index=5*/f32[128,128]{1,0:T(8,128)S(1)}) custom-call(s32[8]{0:T(128)S(1)} %copy-done.13, bf16[2,128,2048]{2,1,0:T(8,128)(2,1)S(1)} %bitcast.18, ...), custom_call_target="tpu_custom_call" | custom-call | flops 3000000000 | tf_op jit(solution)/shard_map/pallas_call | solution.py:495
  40.1 1.5 %shard_map.217 = (bf16[160,2048]{1,0:T(8,128)(2,1)S(1)}, bf16[32,2048]{1,0:T(8,128)(2,1)S(1)}) custom-call(s32[8]{0:T(128)S(1)} %copy-done.13, bf16[160,2048]{1,0:T(8,128)(2,1)S(1)} %collective-permute-done.4.received, bf16[16,2048]{1,0:T(8,128)(2,1)S(1)} %collective-permute-done.6.near, bf16[16,2048]{1,0:T(8,128)(2,1)S(1)} %collective-permute-done.7.far, ...), custom_call_target="tpu_custom_call" | custom-call | flops 2000000000 | tf_op jit(solution)/shard_map/pallas_call | solution.py:495
  41.6 0.1 collective-permute-start.8
  41.6 2.1 %shard_map.219 = bf16[128,2048]{1,0:T(8,128)(2,1)S(1)} custom-call(s32[8]{0:T(128)S(1)} %copy-done.13, bf16[2,128,2048]{2,1,0:T(8,128)(2,1)S(1)} %bitcast.19, bf16[160,2048]{1,0:T(8,128)(2,1)S(1)} %collective-permute-done.4.received, bf16[2,32,2048]{2,1,0:T(8,128)(2,1)S(1)} %get-tuple-element.36.weights.refs_4_, ...), custom_call_target="tpu_custom_call" | custom-call | flops 6000000000 | tf_op jit(solution)/shard_map/pallas_call | solution.py:495
  43.7 2.3 %collective-permute-start.11 = (bf16[128,2048]{1,0:T(8,128)(2,1)S(1)}, bf16[128,2048]{1,0:T(8,128)(2,1)S(1)}, u32[]{:S(2)}, u32[]{:S(2)}) collective-permute-start(bf16[128,2048]{1,0:T(8,128)(2,1)S(1)} %shard_map.219), channel_id=1, source_target_pairs={{0,28},{4,0},{8,4},{12,8},{16,12},{20,16},{24,20},{28,24},{1,29},{... | collective-permute-start | bytes 1572872 | tf_op jit(solution)/shard_map/ppermute | solution.py:528
  46.0 0.6 collective-permute-done.8.other1
  46.6 0.1 shard_map.218.mine
  46.6 2.2 %collective-permute-start.9 = (bf16[64,2048]{1,0:T(8,128)(2,1)S(1)}, bf16[64,2048]{1,0:T(8,128)(2,1)S(1)}, u32[]{:S(2)}, u32[]{:S(2)}) collective-permute-start(bf16[64,2048]{1,0:T(8,128)(2,1)S(1)} %shard_map.218.mine), channel_id=1, source_target_pairs={{0,2},{1,3},{2,0},{3,1},{4,6},{5,7},{6,4},{7,5},{8,10},{9,11},{10,... | collective-permute-start | bytes 786440 | tf_op jit(solution)/shard_map/ppermute | solution.py:633
  48.9 5.4 %collective-permute-done.9.other = bf16[64,2048]{1,0:T(8,128)(2,1)S(1)} collective-permute-done((bf16[64,2048]{1,0:T(8,128)(2,1)S(1)}, bf16[64,2048]{1,0:T(8,128)(2,1)S(1)}, u32[]{:S(2)}, u32[]{:S(2)}) %collective-permute-start.9) | collective-permute-done | bytes 262176 | tf_op jit(solution)/shard_map/ppermute | solution.py:633
  54.3 2.3 %shard_map.220 = (bf16[128,2048]{1,0:T(8,128)(2,1)}, bf16[128,2048]{1,0:T(8,128)(2,1)}, f32[31,2,2048]{2,1,0:T(2,128)}, f32[2,2048]{1,0:T(2,128)}) custom-call(s32[8]{0:T(128)S(1)} %copy-done.13, bf16[64,2048]{1,0:T(8,128)(2,1)S(1)} %shard_map.218.mine, bf16[64,2048]{1,0:T(8,128)(2,1)S(1)} %collective-permute-done.9.other, ...), custom_call_target="tpu_custom_call" | custom-call | tf_op jit(solution)/shard_map/pallas_call | solution.py:495
  (43 shorter events, 0.1 us)
Async XLA Ops:
  0.6 5.6 %copy-start.5 = (bf16[1,2,31,2048]{3,1,2,0:T(2,128)(2,1)S(1)}, bf16[1,2,31,2048]{3,1,2,0:T(2,128)(2,1)}, u32[]{:S(2)}) copy-start(bf16[1,2,31,2048]{3,1,2,0:T(2,128)(2,1)} %param.22) | copy-start | bytes 761860
  0.6 5.6 %copy-start.11 = (bf16[1,2,2048]{2,1,0:T(2,128)(2,1)S(1)}, bf16[1,2,2048]{2,1,0:T(2,128)(2,1)}, u32[]{:S(2)}) copy-start(bf16[1,2,2048]{2,1,0:T(2,128)(2,1)} %param.23) | copy-start | bytes 24580
  0.7 16.0 %copy-start.6 = (bf16[384,192]{1,0:T(8,128)(2,1)S(1)}, bf16[384,192]{1,0:T(8,128)(2,1)}, u32[]{:S(2)}) copy-start(bf16[384,192]{1,0:T(8,128)(2,1)} %constant.21.clone.m_table.refs_4_.refs_5_) | copy-start | bytes 442372
  2.6 14.1 %collective-permute-start = (bf16[48,2048]{1,0:T(8,128)(2,1)}, bf16[48,2048]{1,0:T(8,128)(2,1)S(1)}, u32[]{:S(2)}, u32[]{:S(2)}) collective-permute-start(bf16[48,2048]{1,0:T(8,128)(2,1)} %get-tuple-element.34), channel_id=1, source_target_pairs={{0,1},{1,0},{2,3},{3,2},{4,5},{5,4},{6,7},{7,6},{8,9},{9,8},{10,11... | collective-permute-start | bytes 589832 | tf_op jit(solution)/shard_map/ppermute | solution.py:540
  5.6 11.1 %collective-permute-start.1 = (bf16[48,2048]{1,0:T(8,128)(2,1)}, bf16[48,2048]{1,0:T(8,128)(2,1)S(1)}, u32[]{:S(2)}, u32[]{:S(2)}) collective-permute-start(bf16[48,2048]{1,0:T(8,128)(2,1)} %get-tuple-element.35), channel_id=1, source_target_pairs={{1,2},{2,1},{5,6},{6,5},{9,10},{10,9},{13,14},{14,13},{17,18},{18,... | collective-permute-start | bytes 589832 | tf_op jit(solution)/shard_map/ppermute | solution.py:540
  6.3 1.2 %copy-start = (bf16[1,2,128,2048]{3,2,1,0:T(8,128)(2,1)S(1)}, bf16[1,2,128,2048]{3,2,1,0:T(8,128)(2,1)}, u32[]{:S(2)}) copy-start(bf16[1,2,128,2048]{3,2,1,0:T(8,128)(2,1)} %param.21) | copy-start | bytes 3145732
  7.5 1.0 %copy-start.3 = (bf16[1,128,2048]{2,1,0:T(8,128)(2,1)S(1)}, bf16[1,128,2048]{2,1,0:T(8,128)(2,1)}, u32[]{:S(2)}) copy-start(bf16[1,128,2048]{2,1,0:T(8,128)(2,1)} %param.19) | copy-start | bytes 1572868
  8.5 0.8 %copy-start.8 = (bf16[192,64]{1,0:T(8,128)(2,1)S(1)}, bf16[192,64]{1,0:T(8,128)(2,1)}, u32[]{:S(2)}) copy-start(bf16[192,64]{1,0:T(8,128)(2,1)} %constant.20.clone.q_table.refs_6_) | copy-start | bytes 73732
  9.3 0.7 %copy-start.12 = (s32[8]{0:T(128)S(1)}, s32[8]{0:T(128)}, u32[]{:S(2)}) copy-start(s32[8]{0:T(128)} %get-tuple-element.33.notes.refs_0_) | copy-start | bytes 100
  10.0 6.7 %copy-start.2 = (bf16[1,128,2048]{2,1,0:T(8,128)(2,1)S(1)}, bf16[1,128,2048]{2,1,0:T(8,128)(2,1)}, u32[]{:S(2)}) copy-start(bf16[1,128,2048]{2,1,0:T(8,128)(2,1)} %grad.1) | copy-start | bytes 1572868
  10.0 6.7 %copy-start.14 = (bf16[384,160]{1,0:T(8,128)(2,1)S(1)}, bf16[384,160]{1,0:T(8,128)(2,1)}, u32[]{:S(2)}) copy-start(bf16[384,160]{1,0:T(8,128)(2,1)} %constant.23.clone.g_table) | copy-start | bytes 368644
  10.0 6.7 %copy-start.15 = (bf16[320,192]{1,0:T(8,128)(2,1)S(1)}, bf16[320,192]{1,0:T(8,128)(2,1)}, u32[]{:S(2)}) copy-start(bf16[320,192]{1,0:T(8,128)(2,1)} %constant.22.clone.c_table.refs_7_) | copy-start | bytes 368644
  10.0 6.7 %copy-start.17 = (bf16[256,192]{1,0:T(8,128)(2,1)S(1)}, bf16[256,192]{1,0:T(8,128)(2,1)}, u32[]{:S(2)}) copy-start(bf16[256,192]{1,0:T(8,128)(2,1)} %constant.24.clone.x_table) | copy-start | bytes 294916
  11.7 14.6 %collective-permute-start.2 = (bf16[64,2048]{1,0:T(8,128)(2,1)S(1)}, bf16[64,2048]{1,0:T(8,128)(2,1)S(1)}, u32[]{:S(2)}, u32[]{:S(2)}) collective-permute-start(bf16[64,2048]{1,0:T(8,128)(2,1)S(1)} %get-tuple-element.45), channel_id=1, source_target_pairs={{0,1},{1,0},{2,3},{3,2},{4,5},{5,4},{6,7},{7,6},{8,9},{9,8},{10,11... | collective-permute-start | bytes 786440 | tf_op jit(solution)/shard_map/ppermute | solution.py:540
  16.0 10.4 %collective-permute-start.3 = (bf16[64,2048]{1,0:T(8,128)(2,1)S(1)}, bf16[64,2048]{1,0:T(8,128)(2,1)S(1)}, u32[]{:S(2)}, u32[]{:S(2)}) collective-permute-start(bf16[64,2048]{1,0:T(8,128)(2,1)S(1)} %get-tuple-element.46), channel_id=1, source_target_pairs={{1,2},{2,1},{5,6},{6,5},{9,10},{10,9},{13,14},{14,13},{17,18},{18,... | collective-permute-start | bytes 786440 | tf_op jit(solution)/shard_map/ppermute | solution.py:540
  16.7 9.6 %copy-start.4 = (bf16[1,128,2048]{2,1,0:T(8,128)(2,1)S(1)}, bf16[1,128,2048]{2,1,0:T(8,128)(2,1)}, u32[]{:S(2)}) copy-start(bf16[1,128,2048]{2,1,0:T(8,128)(2,1)} %param.19) | copy-start | bytes 1572868
  16.8 9.6 %copy-start.9 = (bf16[192,64]{1,0:T(8,128)(2,1)S(1)}, bf16[192,64]{1,0:T(8,128)(2,1)}, u32[]{:S(2)}) copy-start(bf16[192,64]{1,0:T(8,128)(2,1)} %constant.20.clone.q_table.refs_6_) | copy-start | bytes 73732
  16.8 9.6 %copy-start.13 = (s32[8]{0:T(128)S(1)}, s32[8]{0:T(128)}, u32[]{:S(2)}) copy-start(s32[8]{0:T(128)} %get-tuple-element.33.notes.refs_0_) | copy-start | bytes 100
  20.5 10.4 %collective-permute-start.4 = (bf16[160,2048]{1,0:T(8,128)(2,1)S(1)}, bf16[160,2048]{1,0:T(8,128)(2,1)S(1)}, u32[]{:S(2)}, u32[]{:S(2)}) collective-permute-start(bf16[160,2048]{1,0:T(8,128)(2,1)S(1)} %get-tuple-element.47), channel_id=1, source_target_pairs={{0,28},{4,0},{8,4},{12,8},{16,12},{20,16},{24,20},{28,24},{1,29},{... | collective-permute-start | bytes 1966088 | tf_op jit(solution)/shard_map/ppermute | solution.py:528
  22.8 17.3 %collective-permute-start.6 = (bf16[16,2048]{1,0:T(8,128)(2,1)S(1)}, bf16[16,2048]{1,0:T(8,128)(2,1)S(1)}, u32[]{:S(2)}, u32[]{:S(2)}) collective-permute-start(bf16[16,2048]{1,0:T(8,128)(2,1)S(1)} %get-tuple-element.48), channel_id=1, source_target_pairs={{0,29},{1,28},{2,31},{3,30},{4,1},{5,0},{6,3},{7,2},{8,5},{9,4},{1... | collective-permute-start | bytes 196616 | tf_op jit(solution)/shard_map/ppermute | solution.py:540
  25.5 5.4 %copy-start.16 = (bf16[320,160]{1,0:T(8,128)(2,1)S(1)}, bf16[320,160]{1,0:T(8,128)(2,1)}, u32[]{:S(2)}) copy-start(bf16[320,160]{1,0:T(8,128)(2,1)} %constant.25.clone.m_table) | copy-start | bytes 307204
  25.5 5.4 %copy-start.18 = (bf16[256,160]{1,0:T(8,128)(2,1)S(1)}, bf16[256,160]{1,0:T(8,128)(2,1)}, u32[]{:S(2)}) copy-start(bf16[256,160]{1,0:T(8,128)(2,1)} %constant.27.clone.c_table) | copy-start | bytes 245764
  25.5 5.4 %copy-start.19 = (bf16[160,64]{1,0:T(8,128)(2,1)S(1)}, bf16[160,64]{1,0:T(8,128)(2,1)}, u32[]{:S(2)}) copy-start(bf16[160,64]{1,0:T(8,128)(2,1)} %constant.26.clone.q_table) | copy-start | bytes 61444
  25.5 14.5 %collective-permute-start.7 = (bf16[16,2048]{1,0:T(8,128)(2,1)S(1)}, bf16[16,2048]{1,0:T(8,128)(2,1)S(1)}, u32[]{:S(2)}, u32[]{:S(2)}) collective-permute-start(bf16[16,2048]{1,0:T(8,128)(2,1)S(1)} %get-tuple-element.49), channel_id=1, source_target_pairs={{1,30},{2,29},{5,2},{6,1},{9,6},{10,5},{13,10},{14,9},{17,14},{18,... | collective-permute-start | bytes 196616 | tf_op jit(solution)/shard_map/ppermute | solution.py:540
  28.8 4.5 %copy-start.7 = (bf16[192,256]{1,0:T(8,128)(2,1)S(1)}, bf16[192,256]{1,0:T(8,128)(2,1)}, u32[]{:S(2)}) copy-start(bf16[192,256]{1,0:T(8,128)(2,1)} %constant.28.clone.refs_5_.go_table) | copy-start | bytes 294916
  28.8 4.5 %copy-start.10 = (bf16[64,192]{1,0:T(8,128)(2,1)S(1)}, bf16[64,192]{1,0:T(8,128)(2,1)}, u32[]{:S(2)}) copy-start(bf16[64,192]{1,0:T(8,128)(2,1)} %constant.29.clone.refs_6_.t_table) | copy-start | bytes 73732
  33.0 4.4 %copy-start.1 = (bf16[1,2,128,2048]{3,2,1,0:T(8,128)(2,1)S(1)}, bf16[1,2,128,2048]{3,2,1,0:T(8,128)(2,1)}, u32[]{:S(2)}) copy-start(bf16[1,2,128,2048]{3,2,1,0:T(8,128)(2,1)} %param.21) | copy-start | bytes 3145732
  33.0 21.2 %collective-permute-start.10 = (bf16[128,2048]{1,0:T(8,128)(2,1)S(1)}, bf16[128,2048]{1,0:T(8,128)(2,1)S(1)}, u32[]{:S(2)}, u32[]{:S(2)}) collective-permute-start(bf16[128,2048]{1,0:T(8,128)(2,1)S(1)} %shard_map.214.refs_7_.refs_8_), channel_id=1, source_target_pairs={{0,8},{4,12},{8,16},{12,20},{16,24},{20,28},{24,0},{28,4},{1,9},{5... | collective-permute-start | bytes 1572872 | tf_op jit(solution)/shard_map/ppermute | solution.py:528
  34.5 11.5 %collective-permute-start.5 = (bf16[32,2048]{1,0:T(8,128)(2,1)S(1)}, bf16[32,2048]{1,0:T(8,128)(2,1)S(1)}, u32[]{:S(2)}, u32[]{:S(2)}) collective-permute-start(bf16[32,2048]{1,0:T(8,128)(2,1)S(1)} %shard_map.215.mine0), channel_id=1, source_target_pairs={{0,1},{1,0},{2,3},{3,2},{4,5},{5,4},{6,7},{7,6},{8,9},{9,8},{10,11... | collective-permute-start | bytes 393224 | tf_op jit(solution)/shard_map/ppermute | solution.py:633
  41.6 5.0 %collective-permute-start.8 = (bf16[32,2048]{1,0:T(8,128)(2,1)S(1)}, bf16[32,2048]{1,0:T(8,128)(2,1)S(1)}, u32[]{:S(2)}, u32[]{:S(2)}) collective-permute-start(bf16[32,2048]{1,0:T(8,128)(2,1)S(1)} %get-tuple-element.53.mine1), channel_id=1, source_target_pairs={{0,1},{1,0},{2,3},{3,2},{4,5},{5,4},{6,7},{7,6},{8,9},{9,8},{10,11... | collective-permute-start | bytes 393224 | tf_op jit(solution)/shard_map/ppermute | solution.py:633
  43.7 10.6 %collective-permute-start.11 = (bf16[128,2048]{1,0:T(8,128)(2,1)S(1)}, bf16[128,2048]{1,0:T(8,128)(2,1)S(1)}, u32[]{:S(2)}, u32[]{:S(2)}) collective-permute-start(bf16[128,2048]{1,0:T(8,128)(2,1)S(1)} %shard_map.219), channel_id=1, source_target_pairs={{0,28},{4,0},{8,4},{12,8},{16,12},{20,16},{24,20},{28,24},{1,29},{... | collective-permute-start | bytes 1572872 | tf_op jit(solution)/shard_map/ppermute | solution.py:528
  46.6 7.6 %collective-permute-start.9 = (bf16[64,2048]{1,0:T(8,128)(2,1)S(1)}, bf16[64,2048]{1,0:T(8,128)(2,1)S(1)}, u32[]{:S(2)}, u32[]{:S(2)}) collective-permute-start(bf16[64,2048]{1,0:T(8,128)(2,1)S(1)} %shard_map.218.mine), channel_id=1, source_target_pairs={{0,2},{1,3},{2,0},{3,1},{4,6},{5,7},{6,4},{7,5},{8,10},{9,11},{10,... | collective-permute-start | bytes 786440 | tf_op jit(solution)/shard_map/ppermute | solution.py:633

commit v10 on v9

--- a/solution.py
+++ b/solution.py
@@ -209,7 +209,7 @@
 
 
 def prepare_kernel(
-    reach, notes, kernels, gains, saved, act, q_table, weights, later, near, far, masked, mean, inverse, q
+    reach, notes, kernels, gains, saved, act, weights, later, near, far, masked, mean, inverse
 ):
     own, width = act.shape
     for even in range(2):
@@ -229,11 +229,6 @@
     slot, length, first = looked_up(notes, BACK0)
     norm_pieces([(saved.at[0], 0, own)], slot_row(weights, slot), first, length, masked, mean, inverse)
 
-    def block(columns):
-        q[:, columns] = tap_spectrum(q_table[...], weights[slot, :, columns])
-
-    each_block(width, block)
-
 
 def norm_halo(left, right, own, gain, first, length, halo):
     reach = left.shape[0]
@@ -247,8 +242,8 @@
 
 
 def first_backward_kernel(
-    reach, notes, saved, near, far, grads, weights, later, masked, mean, inverse, q,
-    m_table, c_table, g_table, x_table,
+    reach, notes, saved, far, near, grads, weights, later, masked, mean, inverse,
+    m_table, q_table, c_table, g_table, x_table,
     grad_x, near_edge, far_edge, halo, inner, gain_sum, halos, grad_halos, scaled, sum_a, sum_b,
 ):
     own, width = grads.shape
@@ -267,12 +262,12 @@
 
     def block(columns):
         m = transform(m_table, joined(halo, masked, columns))
-        conv = transform(c_table, product(m, q[:, columns]))
+        q = tap_spectrum(q_table[...], weights[slot, :, columns])
+        conv = transform(c_table, product(m, q))
         mixed = (window(grad_pieces, columns).astype(F32) * gate_factor(conv)).astype(BF16)
         inner[:, columns] = mixed[edge : edge + own]
         weighted = first_pass(
-            pieces, mean, inverse, gain, mask, (g_table, x_table), mixed, q[:, columns], columns,
-            scaled, sum_a, sum_b,
+            pieces, mean, inverse, gain, mask, (g_table, x_table), mixed, q, columns, scaled, sum_a, sum_b
         )
         gain_sum[:, columns] = jnp.sum(weighted, axis=0, keepdims=True)
 
@@ -320,7 +315,7 @@
 
 
 def second_ready_kernel(
-    reach, notes, saved, near, far, weights, m_table, q_table, c_table,
+    reach, notes, saved, far, near, weights, m_table, q_table, c_table,
     m_out, q_out, factor, conv_out, mean, inverse, halo, halos, masked,
 ):
     own, width = masked.shape
@@ -344,7 +339,7 @@
 
 
 def second_taps_kernel(
-    notes, received, near, far, weights, m, factor, conv, go_table, t_table, mixed_out, taps, halos
+    notes, received, far, near, weights, m, factor, conv, go_table, t_table, mixed_out, taps, halos
 ):
     own, width = conv.shape
     rows = factor.shape[0]
@@ -383,7 +378,7 @@
     last_pass([(received, 0, own)], pieces, mean, inverse, scaled, sum_a, sum_b, grad_x)
 
 
-def first_forward_kernel(reach, notes, act, near, far, weights, m_table, q_table, c_table, out, halo, halos, masked):
+def first_forward_kernel(reach, notes, act, far, near, weights, m_table, q_table, c_table, out, halo, halos, masked):
     own, width = act.shape
     middle = reach // 2
     slot, length, first = looked_up(notes, AHEAD0)
@@ -562,7 +557,7 @@
         return call(kernel, outs, scratch, [jnp.asarray(x) for x in operands], micros, after=after)
 
     rows = [pltpu.VMEM((own, width), F32)] + [pltpu.VMEM((own, LANES), F32)] * 2
-    layer = like(own, width, BF16), like(own, LANES, F32), like(own, LANES, F32), like(size, width, F32)
+    layer = like(own, width, BF16), like(own, LANES, F32), like(own, LANES, F32)
     weights, later, near1, far1, *layer0 = run(
         functools.partial(prepare_kernel, two),
         (
@@ -570,7 +565,7 @@
             like(2 * two, width, BF16), like(2 * two, width, BF16), *layer,
         ),
         [],
-        [notes, kernels[0].transpose(1, 0, 2), norm_gains[0], saved, act, q_table],
+        [notes, kernels[0].transpose(1, 0, 2), norm_gains[0], saved, act],
         0,
     )
     near1, far1 = swapped(near1, far1)
@@ -583,13 +578,18 @@
         ),
         [pltpu.VMEM((2, two, width), BF16), pltpu.VMEM((2, one, width), BF16), *rows],
         [
-            notes, saved, near0, far0, grad, weights, later, *layer0,
-            m_table, c_table, g_table, x_table,
+            notes, saved, far0, near0, grad, weights, later, *layer0,
+            m_table, q_table, c_table, g_table, x_table,
         ],
         4,
     )
     grad_mid = shifted(grad_mid, -1)
     near2, far2 = swapped(near2, far2, -1)
+    taps0 = run(
+        first_taps_kernel, like(tap_count + 1, width, BF16), [],
+        [halo0, layer0[0], inner0, gain0, m_table, go_table, t_table],
+        0,
+    )
     halo_scratch = [
         pltpu.VMEM((2 * two, width), BF16), pltpu.VMEM((2, two, width), BF16), pltpu.VMEM((own, width), BF16)
     ]
@@ -597,8 +597,9 @@
         functools.partial(first_forward_kernel, two),
         like(small, width, BF16),
         halo_scratch,
-        [notes, act, near1, far1, weights, m_table, q_table, c_table],
+        [notes, act, far1, near1, weights, m_table, q_table, c_table],
         20,
+        taps0,
     )
     act_ahead = run(
         second_forward_kernel,
@@ -611,12 +612,6 @@
         3,
     )
     act_out = shifted(act_ahead, 2)
-    taps0 = run(
-        first_taps_kernel, like(tap_count + 1, width, BF16), [],
-        [halo0, layer0[0], inner0, gain0, m_table, go_table, t_table],
-        0,
-        act_ahead,
-    )
     m1, q1, factor1, conv1, mean1, inverse1 = run(
         functools.partial(second_ready_kernel, two),
         (
@@ -624,7 +619,7 @@
             like(own, LANES, F32), like(own, LANES, F32),
         ),
         halo_scratch,
-        [notes, saved, near1, far1, weights, m_table, q_table, c_table],
+        [notes, saved, far1, near1, weights, m_table, q_table, c_table],
         3,
         act_ahead,
     )
@@ -637,7 +632,7 @@
         second_taps_kernel,
         (like(small, width, BF16), like(tap_count + 1, width, BF16)),
         [pltpu.VMEM((2, one, width), BF16)],
-        [notes, grad_mid, near2, far2, weights, m1, factor1, conv1, go_table, t_table],
+        [notes, grad_mid, far2, near2, weights, m1, factor1, conv1, go_table, t_table],
         2,
     )
     grad_out = run(

time: 57.6 us -> 58.6 us (1.017)
  the two profiles are of different devices: /device:TPU:0 before, /device:TPU:1 now
where the time goes in v10:
time: 58.6 us; the launch traced here: 58.3 us
  Pallas kernels  21.8 us (37%)
  starting transfers between devices  19.1 us (33%)
  waiting for transfers between devices  13.3 us (23%)
  local copies, waits for them, and re-layouts  3.01 us (5%)
  between operations  1.13 us (2%)
    pallas_call x11, Pallas kernels, call(): pl.pallas_call(kernel, out_shape=outs, in_specs=specs, out_specs=jax.tree...  21.8 us
    ppermute x6, starting transfers between devices, swapped(): results.append(lax.ppermute(x, ('section', 'tm'), pairs))  14.1 us
    ppermute x3, waiting for transfers between devices, partner(): return lax.ppermute(x, 'tm', [(i, i ^ step) for i in range(shards)])  8.87 us
    ppermute x3, starting transfers between devices, shifted(): lax.ppermute(x, 'section', [(i, (i + by) % sections) for i in range(secti...  4.81 us
    ppermute x3, waiting for transfers between devices, shifted(): lax.ppermute(x, 'section', [(i, (i + by) % sections) for i in range(secti...  3.59 us
    unnamed x38, local copies, waits for them, and re-layouts  3.01 us
  transfers between devices with their start and end apart: 12, of which 4 were waited for; matrix products, arithmetic and copies ran while one was open for 0% of the time, Pallas kernels for 30%

profile of v10, /device:TPU:1, one launch (start us, length us, event | category | flops | bytes accessed | tf_op | source)
XLA Modules:
  0.0 58.3 jit_solution(7332527449256642242)
XLA Ops:
  0.7 0.0 copy-start.6
  0.7 1.9 %shard_map.210 = (bf16[48,2048]{1,0:T(8,128)(2,1)}, bf16[48,2048]{1,0:T(8,128)(2,1)}, s32[8]{0:T(128)}) custom-call(bf16[2,128,2048]{2,1,0:T(8,128)(2,1)} %bitcast.15, bf16[1,128,2048]{2,1,0:T(8,128)(2,1)} %grad.1, s32[8]{0:T(128)} %back_lengths.1, s32[8]{0:T(128)} %ahead_lengths.1, s32[2,8]{1,0:T(2,128)} %bitcast.25, s32[2,8]{1,0:T(2,128)} %bitcast.26), custom_call_target="tpu_custom_call" | custom-call | tf_op jit(solution)/shard_map/pallas_call | solution.py:490
  2.6 0.7 %collective-permute-start = (bf16[48,2048]{1,0:T(8,128)(2,1)}, bf16[48,2048]{1,0:T(8,128)(2,1)S(1)}, u32[]{:S(2)}, u32[]{:S(2)}) collective-permute-start(bf16[48,2048]{1,0:T(8,128)(2,1)} %get-tuple-element.33), channel_id=1, source_target_pairs={{1,2},{2,1},{5,6},{6,5},{9,10},{10,9},{13,14},{14,13},{17,18},{18,... | collective-permute-start | bytes 589832 | tf_op jit(solution)/shard_map/ppermute | solution.py:535
  3.3 4.6 %collective-permute-start.1 = (bf16[48,2048]{1,0:T(8,128)(2,1)}, bf16[48,2048]{1,0:T(8,128)(2,1)S(1)}, u32[]{:S(2)}, u32[]{:S(2)}) collective-permute-start(bf16[48,2048]{1,0:T(8,128)(2,1)} %get-tuple-element.34), channel_id=1, source_target_pairs={{0,1},{1,0},{2,3},{3,2},{4,5},{5,4},{6,7},{7,6},{8,9},{9,8},{10,11... | collective-permute-start | bytes 589832 | tf_op jit(solution)/shard_map/ppermute | solution.py:535
  7.8 1.2 %copy-done = bf16[1,2,128,2048]{3,2,1,0:T(8,128)(2,1)S(1)} copy-done((bf16[1,2,128,2048]{3,2,1,0:T(8,128)(2,1)S(1)}, bf16[1,2,128,2048]{3,2,1,0:T(8,128)(2,1)}, u32[]{:S(2)}) %copy-start) | copy-done | bytes 1048600
  9.1 1.0 %copy-done.3 = bf16[1,128,2048]{2,1,0:T(8,128)(2,1)S(1)} copy-done((bf16[1,128,2048]{2,1,0:T(8,128)(2,1)S(1)}, bf16[1,128,2048]{2,1,0:T(8,128)(2,1)}, u32[]{:S(2)}) %copy-start.3) | copy-done | bytes 524312
  10.1 0.7 %copy-done.10 = s32[8]{0:T(128)S(1)} copy-done((s32[8]{0:T(128)S(1)}, s32[8]{0:T(128)}, u32[]{:S(2)}) %copy-start.10) | copy-done | bytes 56
  10.8 1.7 %shard_map.211 = (bf16[2,32,2048]{2,1,0:T(8,128)(2,1)S(1)}, bf16[32,2048]{1,0:T(8,128)(2,1)S(1)}, bf16[64,2048]{1,0:T(8,128)(2,1)S(1)}, bf16[64,2048]{1,0:T(8,12...) custom-call(s32[8]{0:T(128)S(1)} %copy-done.10, ...), custom_call_target="tpu_custom_call" | custom-call | tf_op jit(solution)/shard_map/pallas_call | solution.py:490
  12.5 0.7 %collective-permute-start.6 = (bf16[64,2048]{1,0:T(8,128)(2,1)S(1)}, bf16[64,2048]{1,0:T(8,128)(2,1)S(1)}, u32[]{:S(2)}, u32[]{:S(2)}) collective-permute-start(bf16[64,2048]{1,0:T(8,128)(2,1)S(1)} %get-tuple-element.46), channel_id=1, source_target_pairs={{1,2},{2,1},{5,6},{6,5},{9,10},{10,9},{13,14},{14,13},{17,18},{18,... | collective-permute-start | bytes 786440 | tf_op jit(solution)/shard_map/ppermute | solution.py:535
  13.2 2.5 %collective-permute-start.7 = (bf16[64,2048]{1,0:T(8,128)(2,1)S(1)}, bf16[64,2048]{1,0:T(8,128)(2,1)S(1)}, u32[]{:S(2)}, u32[]{:S(2)}) collective-permute-start(bf16[64,2048]{1,0:T(8,128)(2,1)S(1)} %get-tuple-element.47), channel_id=1, source_target_pairs={{0,1},{1,0},{2,3},{3,2},{4,5},{5,4},{6,7},{7,6},{8,9},{9,8},{10,11... | collective-permute-start | bytes 786440 | tf_op jit(solution)/shard_map/ppermute | solution.py:535
  15.6 0.8 %collective-permute-done.1.near = bf16[48,2048]{1,0:T(8,128)(2,1)S(1)} collective-permute-done((bf16[48,2048]{1,0:T(8,128)(2,1)}, bf16[48,2048]{1,0:T(8,128)(2,1)S(1)}, u32[]{:S(2)}, u32[]{:S(2)}) %collective-permute-start.1) | collective-permute-done | bytes 196640 | tf_op jit(solution)/shard_map/ppermute | solution.py:535
  16.5 3.9 %shard_map.212 = (bf16[160,2048]{1,0:T(8,128)(2,1)S(1)}, bf16[16,2048]{1,0:T(8,128)(2,1)S(1)}, bf16[16,2048]{1,0:T(8,128)(2,1)S(1)}, bf16[64,2048]{1,0:T(8,128)(...) custom-call(s32[8]{0:T(128)S(1)} %copy-done.11, bf16[2,128,2048]{2,1,0:T(8,128)(2,1)S(1)} %bitcast.17, ...), custom_call_target="tpu_custom_call" | custom-call | flops 4000000000 | tf_op jit(solution)/shard_map/pallas_call | solution.py:490
  20.5 2.4 %collective-permute-start.3 = (bf16[160,2048]{1,0:T(8,128)(2,1)S(1)}, bf16[160,2048]{1,0:T(8,128)(2,1)S(1)}, u32[]{:S(2)}, u32[]{:S(2)}) collective-permute-start(bf16[160,2048]{1,0:T(8,128)(2,1)S(1)} %get-tuple-element.43), channel_id=1, source_target_pairs={{0,28},{4,0},{8,4},{12,8},{16,12},{20,16},{24,20},{28,24},{1,29},{... | collective-permute-start | bytes 1966088 | tf_op jit(solution)/shard_map/ppermute | solution.py:523
  22.9 0.7 %collective-permute-start.4 = (bf16[16,2048]{1,0:T(8,128)(2,1)S(1)}, bf16[16,2048]{1,0:T(8,128)(2,1)S(1)}, u32[]{:S(2)}, u32[]{:S(2)}) collective-permute-start(bf16[16,2048]{1,0:T(8,128)(2,1)S(1)} %get-tuple-element.44), channel_id=1, source_target_pairs={{1,30},{2,29},{5,2},{6,1},{9,6},{10,5},{13,10},{14,9},{17,14},{18,... | collective-permute-start | bytes 196616 | tf_op jit(solution)/shard_map/ppermute | solution.py:535
  23.5 5.1 %collective-permute-start.5 = (bf16[16,2048]{1,0:T(8,128)(2,1)S(1)}, bf16[16,2048]{1,0:T(8,128)(2,1)S(1)}, u32[]{:S(2)}, u32[]{:S(2)}) collective-permute-start(bf16[16,2048]{1,0:T(8,128)(2,1)S(1)} %get-tuple-element.45), channel_id=1, source_target_pairs={{0,29},{1,28},{2,31},{3,30},{4,1},{5,0},{6,3},{7,2},{8,5},{9,4},{1... | collective-permute-start | bytes 196616 | tf_op jit(solution)/shard_map/ppermute | solution.py:535
  28.6 1.1 %shard_map.213.refs_8_.mine0 = bf16[32,2048]{1,0:T(8,128)(2,1)S(1)} custom-call(bf16[64,2048]{1,0:T(8,128)(2,1)S(1)} %get-tuple-element.40.halo, bf16[128,2048]{1,0:T(8,128)(2,1)S(1)} %get-tuple-element.37.masked, bf16[128,2048]{1,0:T(8,128)(2,1)S(1)} %get-tuple-element.41.inner, f32[1,2048]{1,0:T(1,128)S(1)} %get-tuple-element.42.gain_sum, ...), custom_call_target="tpu_custom_call" | custom-call | tf_op jit(solution)/shard_map/pallas_call | solution.py:490
  29.8 0.0 copy-start.14
  29.8 0.1 collective-permute-start.2
  29.9 2.4 %shard_map.214.between = bf16[160,2048]{1,0:T(8,128)(2,1)S(1)} custom-call(s32[8]{0:T(128)S(1)} %copy-done.11, bf16[128,2048]{1,0:T(8,128)(2,1)S(1)} %bitcast.22, bf16[64,2048]{1,0:T(8,128)(2,1)S(1)} %collective-permute-done.6.refs_2_, bf16[64,2048]{1,0:T(8,128)(2,1)S(1)} %collective-permute-done.7.refs_3_, ...), custom_call_target="tpu_custom_call" | custom-call | flops 20000000000 | tf_op jit(solution)/shard_map/pallas_call | solution.py:490
  32.4 2.1 %shard_map.215.refs_8_ = bf16[128,2048]{1,0:T(8,128)(2,1)S(1)} custom-call(s32[8]{0:T(128)S(1)} %copy-done.11, bf16[160,2048]{1,0:T(8,128)(2,1)S(1)} %shard_map.214.between, bf16[160,2048]{1,0:T(8,128)(2,1)S(1)} %collective-permute-done.3.received, bf16[320,160]{1,0:T(8,128)(2,1)S(1)} %copy-done.14, bf16[160,64]{1,0:T(8,128)(2,1)S(1)} %copy-done.18, ...), custom_call_target="tpu_custom_call" | custom-call | flops 3000000000 | tf_op jit(solution)/shard_map/pallas_call | solution.py:490
  34.5 1.7 %collective-permute-start.10 = (bf16[128,2048]{1,0:T(8,128)(2,1)S(1)}, bf16[128,2048]{1,0:T(8,128)(2,1)S(1)}, u32[]{:S(2)}, u32[]{:S(2)}) collective-permute-start(bf16[128,2048]{1,0:T(8,128)(2,1)S(1)} %shard_map.215.refs_8_), channel_id=1, source_target_pairs={{0,8},{4,12},{8,16},{12,20},{16,24},{20,28},{24,0},{28,4},{1,9},{5... | collective-permute-start | bytes 1572872 | tf_op jit(solution)/shard_map/ppermute | solution.py:523
  36.3 2.6 %shard_map.216 = (f32[192,2048]{1,0:T(8,128)S(1)}, f32[192,2048]{1,0:T(8,128)S(1)}, f32[160,2048]{1,0:T(8,128)S(1)}, f32[128,2048]{1,0:T(8,128)S(1)}, f32[128,128]{1,0:T(8,128)S(1)}, /*index=5*/f32[128,128]{1,0:T(8,128)S(1)}) custom-call(s32[8]{0:T(128)S(1)} %copy-done.11, bf16[2,128,2048]{2,1,0:T(8,128)(2,1)S(1)} %bitcast.18, ...), custom_call_target="tpu_custom_call" | custom-call | flops 3000000000 | tf_op jit(solution)/shard_map/pallas_call | solution.py:490
  38.9 1.5 %shard_map.217 = (bf16[160,2048]{1,0:T(8,128)(2,1)S(1)}, bf16[32,2048]{1,0:T(8,128)(2,1)S(1)}) custom-call(s32[8]{0:T(128)S(1)} %copy-done.11, bf16[160,2048]{1,0:T(8,128)(2,1)S(1)} %collective-permute-done.3.received, bf16[16,2048]{1,0:T(8,128)(2,1)S(1)} %collective-permute-done.4.far, bf16[16,2048]{1,0:T(8,128)(2,1)S(1)} %collective-permute-done.5.near, ...), custom_call_target="tpu_custom_call" | custom-call | flops 2000000000 | tf_op jit(solution)/shard_map/pallas_call | solution.py:490
  40.4 0.1 collective-permute-start.8
  40.4 2.1 %shard_map.219 = bf16[128,2048]{1,0:T(8,128)(2,1)S(1)} custom-call(s32[8]{0:T(128)S(1)} %copy-done.11, bf16[2,128,2048]{2,1,0:T(8,128)(2,1)S(1)} %bitcast.19, bf16[160,2048]{1,0:T(8,128)(2,1)S(1)} %collective-permute-done.3.received, bf16[2,32,2048]{2,1,0:T(8,128)(2,1)S(1)} %get-tuple-element.35.weights.refs_4_, ...), custom_call_target="tpu_custom_call" | custom-call | flops 6000000000 | tf_op jit(solution)/shard_map/pallas_call | solution.py:490
  42.5 0.7 %collective-permute-start.11 = (bf16[128,2048]{1,0:T(8,128)(2,1)S(1)}, bf16[128,2048]{1,0:T(8,128)(2,1)S(1)}, u32[]{:S(2)}, u32[]{:S(2)}) collective-permute-start(bf16[128,2048]{1,0:T(8,128)(2,1)S(1)} %shard_map.219), channel_id=1, source_target_pairs={{0,28},{4,0},{8,4},{12,8},{16,12},{20,16},{24,20},{28,24},{1,29},{... | collective-permute-start | bytes 1572872 | tf_op jit(solution)/shard_map/ppermute | solution.py:523
  43.3 2.1 %collective-permute-done.8.other1 = bf16[32,2048]{1,0:T(8,128)(2,1)S(1)} collective-permute-done((bf16[32,2048]{1,0:T(8,128)(2,1)S(1)}, bf16[32,2048]{1,0:T(8,128)(2,1)S(1)}, u32[]{:S(2)}, u32[]{:S(2)}) %collective-permute-start.8) | collective-permute-done | bytes 131104 | tf_op jit(solution)/shard_map/ppermute | solution.py:628
  45.3 0.1 shard_map.218.mine
  45.4 0.1 collective-permute-start.9
  45.5 6.8 %collective-permute-done.9.other = bf16[64,2048]{1,0:T(8,128)(2,1)S(1)} collective-permute-done((bf16[64,2048]{1,0:T(8,128)(2,1)S(1)}, bf16[64,2048]{1,0:T(8,128)(2,1)S(1)}, u32[]{:S(2)}, u32[]{:S(2)}) %collective-permute-start.9) | collective-permute-done | bytes 262176 | tf_op jit(solution)/shard_map/ppermute | solution.py:628
  52.3 3.6 %collective-permute-done.11.grad = bf16[128,2048]{1,0:T(8,128)(2,1)S(1)} collective-permute-done((bf16[128,2048]{1,0:T(8,128)(2,1)S(1)}, bf16[128,2048]{1,0:T(8,128)(2,1)S(1)}, u32[]{:S(2)}, u32[]{:S(2)}) %collective-permute-start.11) | collective-permute-done | bytes 524320 | tf_op jit(solution)/shard_map/ppermute | solution.py:523
  55.9 2.3 %shard_map.220 = (bf16[128,2048]{1,0:T(8,128)(2,1)}, bf16[128,2048]{1,0:T(8,128)(2,1)}, f32[31,2,2048]{2,1,0:T(2,128)}, f32[2,2048]{1,0:T(2,128)}) custom-call(s32[8]{0:T(128)S(1)} %copy-done.11, bf16[64,2048]{1,0:T(8,128)(2,1)S(1)} %shard_map.218.mine, bf16[64,2048]{1,0:T(8,128)(2,1)S(1)} %collective-permute-done.9.other, ...), custom_call_target="tpu_custom_call" | custom-call | tf_op jit(solution)/shard_map/pallas_call | solution.py:490
  (41 shorter events, 0.1 us)
Async XLA Ops:
  0.6 7.2 %copy-start.5 = (bf16[1,2,31,2048]{3,1,2,0:T(2,128)(2,1)S(1)}, bf16[1,2,31,2048]{3,1,2,0:T(2,128)(2,1)}, u32[]{:S(2)}) copy-start(bf16[1,2,31,2048]{3,1,2,0:T(2,128)(2,1)} %param.22) | copy-start | bytes 761860
  0.6 7.2 %copy-start.9 = (bf16[1,2,2048]{2,1,0:T(2,128)(2,1)S(1)}, bf16[1,2,2048]{2,1,0:T(2,128)(2,1)}, u32[]{:S(2)}) copy-start(bf16[1,2,2048]{2,1,0:T(2,128)(2,1)} %param.23) | copy-start | bytes 24580
  0.7 15.8 %copy-start.6 = (bf16[384,192]{1,0:T(8,128)(2,1)S(1)}, bf16[384,192]{1,0:T(8,128)(2,1)}, u32[]{:S(2)}) copy-start(bf16[384,192]{1,0:T(8,128)(2,1)} %constant.20.clone.m_table.refs_5_) | copy-start | bytes 442372
  2.6 13.9 %copy-start.11 = (s32[8]{0:T(128)S(1)}, s32[8]{0:T(128)}, u32[]{:S(2)}) copy-start(s32[8]{0:T(128)} %get-tuple-element.32.notes.refs_0_) | copy-start | bytes 100
  2.6 13.0 %collective-permute-start = (bf16[48,2048]{1,0:T(8,128)(2,1)}, bf16[48,2048]{1,0:T(8,128)(2,1)S(1)}, u32[]{:S(2)}, u32[]{:S(2)}) collective-permute-start(bf16[48,2048]{1,0:T(8,128)(2,1)} %get-tuple-element.33), channel_id=1, source_target_pairs={{1,2},{2,1},{5,6},{6,5},{9,10},{10,9},{13,14},{14,13},{17,18},{18,... | collective-permute-start | bytes 589832 | tf_op jit(solution)/shard_map/ppermute | solution.py:535
  3.3 13.2 %collective-permute-start.1 = (bf16[48,2048]{1,0:T(8,128)(2,1)}, bf16[48,2048]{1,0:T(8,128)(2,1)S(1)}, u32[]{:S(2)}, u32[]{:S(2)}) collective-permute-start(bf16[48,2048]{1,0:T(8,128)(2,1)} %get-tuple-element.34), channel_id=1, source_target_pairs={{0,1},{1,0},{2,3},{3,2},{4,5},{5,4},{6,7},{7,6},{8,9},{9,8},{10,11... | collective-permute-start | bytes 589832 | tf_op jit(solution)/shard_map/ppermute | solution.py:535
  7.8 1.2 %copy-start = (bf16[1,2,128,2048]{3,2,1,0:T(8,128)(2,1)S(1)}, bf16[1,2,128,2048]{3,2,1,0:T(8,128)(2,1)}, u32[]{:S(2)}) copy-start(bf16[1,2,128,2048]{3,2,1,0:T(8,128)(2,1)} %param.21) | copy-start | bytes 3145732
  9.1 1.0 %copy-start.3 = (bf16[1,128,2048]{2,1,0:T(8,128)(2,1)S(1)}, bf16[1,128,2048]{2,1,0:T(8,128)(2,1)}, u32[]{:S(2)}) copy-start(bf16[1,128,2048]{2,1,0:T(8,128)(2,1)} %param.19) | copy-start | bytes 1572868
  10.1 0.7 %copy-start.10 = (s32[8]{0:T(128)S(1)}, s32[8]{0:T(128)}, u32[]{:S(2)}) copy-start(s32[8]{0:T(128)} %get-tuple-element.32.notes.refs_0_) | copy-start | bytes 100
  10.8 5.7 %copy-start.2 = (bf16[1,128,2048]{2,1,0:T(8,128)(2,1)S(1)}, bf16[1,128,2048]{2,1,0:T(8,128)(2,1)}, u32[]{:S(2)}) copy-start(bf16[1,128,2048]{2,1,0:T(8,128)(2,1)} %grad.1) | copy-start | bytes 1572868
  10.8 5.7 %copy-start.12 = (bf16[384,160]{1,0:T(8,128)(2,1)S(1)}, bf16[384,160]{1,0:T(8,128)(2,1)}, u32[]{:S(2)}) copy-start(bf16[384,160]{1,0:T(8,128)(2,1)} %constant.23.clone.g_table) | copy-start | bytes 368644
  10.8 5.7 %copy-start.13 = (bf16[320,192]{1,0:T(8,128)(2,1)S(1)}, bf16[320,192]{1,0:T(8,128)(2,1)}, u32[]{:S(2)}) copy-start(bf16[320,192]{1,0:T(8,128)(2,1)} %constant.22.clone.c_table.refs_7_) | copy-start | bytes 368644
  10.8 5.7 %copy-start.15 = (bf16[256,192]{1,0:T(8,128)(2,1)S(1)}, bf16[256,192]{1,0:T(8,128)(2,1)}, u32[]{:S(2)}) copy-start(bf16[256,192]{1,0:T(8,128)(2,1)} %constant.24.clone.x_table) | copy-start | bytes 294916
  10.8 5.7 %copy-start.17 = (bf16[192,64]{1,0:T(8,128)(2,1)S(1)}, bf16[192,64]{1,0:T(8,128)(2,1)}, u32[]{:S(2)}) copy-start(bf16[192,64]{1,0:T(8,128)(2,1)} %constant.21.clone.q_table.refs_6_) | copy-start | bytes 73732
  12.5 17.3 %collective-permute-start.6 = (bf16[64,2048]{1,0:T(8,128)(2,1)S(1)}, bf16[64,2048]{1,0:T(8,128)(2,1)S(1)}, u32[]{:S(2)}, u32[]{:S(2)}) collective-permute-start(bf16[64,2048]{1,0:T(8,128)(2,1)S(1)} %get-tuple-element.46), channel_id=1, source_target_pairs={{1,2},{2,1},{5,6},{6,5},{9,10},{10,9},{13,14},{14,13},{17,18},{18,... | collective-permute-start | bytes 786440 | tf_op jit(solution)/shard_map/ppermute | solution.py:535
  13.2 16.7 %collective-permute-start.7 = (bf16[64,2048]{1,0:T(8,128)(2,1)S(1)}, bf16[64,2048]{1,0:T(8,128)(2,1)S(1)}, u32[]{:S(2)}, u32[]{:S(2)}) collective-permute-start(bf16[64,2048]{1,0:T(8,128)(2,1)S(1)} %get-tuple-element.47), channel_id=1, source_target_pairs={{0,1},{1,0},{2,3},{3,2},{4,5},{5,4},{6,7},{7,6},{8,9},{9,8},{10,11... | collective-permute-start | bytes 786440 | tf_op jit(solution)/shard_map/ppermute | solution.py:535
  16.5 12.1 %copy-start.7 = (bf16[192,256]{1,0:T(8,128)(2,1)S(1)}, bf16[192,256]{1,0:T(8,128)(2,1)}, u32[]{:S(2)}) copy-start(bf16[192,256]{1,0:T(8,128)(2,1)} %constant.25.clone.go_table) | copy-start | bytes 294916
  16.5 12.1 %copy-start.8 = (bf16[64,192]{1,0:T(8,128)(2,1)S(1)}, bf16[64,192]{1,0:T(8,128)(2,1)}, u32[]{:S(2)}) copy-start(bf16[64,192]{1,0:T(8,128)(2,1)} %constant.26.clone.t_table) | copy-start | bytes 73732
  20.5 9.4 %copy-start.4 = (bf16[1,128,2048]{2,1,0:T(8,128)(2,1)S(1)}, bf16[1,128,2048]{2,1,0:T(8,128)(2,1)}, u32[]{:S(2)}) copy-start(bf16[1,128,2048]{2,1,0:T(8,128)(2,1)} %param.19) | copy-start | bytes 1572868
  20.5 11.9 %collective-permute-start.3 = (bf16[160,2048]{1,0:T(8,128)(2,1)S(1)}, bf16[160,2048]{1,0:T(8,128)(2,1)S(1)}, u32[]{:S(2)}, u32[]{:S(2)}) collective-permute-start(bf16[160,2048]{1,0:T(8,128)(2,1)S(1)} %get-tuple-element.43), channel_id=1, source_target_pairs={{0,28},{4,0},{8,4},{12,8},{16,12},{20,16},{24,20},{28,24},{1,29},{... | collective-permute-start | bytes 1966088 | tf_op jit(solution)/shard_map/ppermute | solution.py:523
  22.9 16.0 %collective-permute-start.4 = (bf16[16,2048]{1,0:T(8,128)(2,1)S(1)}, bf16[16,2048]{1,0:T(8,128)(2,1)S(1)}, u32[]{:S(2)}, u32[]{:S(2)}) collective-permute-start(bf16[16,2048]{1,0:T(8,128)(2,1)S(1)} %get-tuple-element.44), channel_id=1, source_target_pairs={{1,30},{2,29},{5,2},{6,1},{9,6},{10,5},{13,10},{14,9},{17,14},{18,... | collective-permute-start | bytes 196616 | tf_op jit(solution)/shard_map/ppermute | solution.py:535
  23.5 15.4 %collective-permute-start.5 = (bf16[16,2048]{1,0:T(8,128)(2,1)S(1)}, bf16[16,2048]{1,0:T(8,128)(2,1)S(1)}, u32[]{:S(2)}, u32[]{:S(2)}) collective-permute-start(bf16[16,2048]{1,0:T(8,128)(2,1)S(1)} %get-tuple-element.45), channel_id=1, source_target_pairs={{0,29},{1,28},{2,31},{3,30},{4,1},{5,0},{6,3},{7,2},{8,5},{9,4},{1... | collective-permute-start | bytes 196616 | tf_op jit(solution)/shard_map/ppermute | solution.py:535
  29.8 2.6 %copy-start.14 = (bf16[320,160]{1,0:T(8,128)(2,1)S(1)}, bf16[320,160]{1,0:T(8,128)(2,1)}, u32[]{:S(2)}) copy-start(bf16[320,160]{1,0:T(8,128)(2,1)} %constant.27.clone.m_table) | copy-start | bytes 307204
  29.8 2.6 %copy-start.16 = (bf16[256,160]{1,0:T(8,128)(2,1)S(1)}, bf16[256,160]{1,0:T(8,128)(2,1)}, u32[]{:S(2)}) copy-start(bf16[256,160]{1,0:T(8,128)(2,1)} %constant.29.clone.c_table) | copy-start | bytes 245764
  29.8 2.6 %copy-start.18 = (bf16[160,64]{1,0:T(8,128)(2,1)S(1)}, bf16[160,64]{1,0:T(8,128)(2,1)}, u32[]{:S(2)}) copy-start(bf16[160,64]{1,0:T(8,128)(2,1)} %constant.28.clone.q_table) | copy-start | bytes 61444
  29.8 13.5 %collective-permute-start.2 = (bf16[32,2048]{1,0:T(8,128)(2,1)S(1)}, bf16[32,2048]{1,0:T(8,128)(2,1)S(1)}, u32[]{:S(2)}, u32[]{:S(2)}) collective-permute-start(bf16[32,2048]{1,0:T(8,128)(2,1)S(1)} %shard_map.213.refs_8_.mine0), channel_id=1, source_target_pairs={{0,1},{1,0},{2,3},{3,2},{4,5},{5,4},{6,7},{7,6},{8,9},{9,8},{10,11... | collective-permute-start | bytes 393224 | tf_op jit(solution)/shard_map/ppermute | solution.py:628
  32.4 3.9 %copy-start.1 = (bf16[1,2,128,2048]{3,2,1,0:T(8,128)(2,1)S(1)}, bf16[1,2,128,2048]{3,2,1,0:T(8,128)(2,1)}, u32[]{:S(2)}) copy-start(bf16[1,2,128,2048]{3,2,1,0:T(8,128)(2,1)} %param.21) | copy-start | bytes 3145732
  34.5 21.3 %collective-permute-start.10 = (bf16[128,2048]{1,0:T(8,128)(2,1)S(1)}, bf16[128,2048]{1,0:T(8,128)(2,1)S(1)}, u32[]{:S(2)}, u32[]{:S(2)}) collective-permute-start(bf16[128,2048]{1,0:T(8,128)(2,1)S(1)} %shard_map.215.refs_8_), channel_id=1, source_target_pairs={{0,8},{4,12},{8,16},{12,20},{16,24},{20,28},{24,0},{28,4},{1,9},{5... | collective-permute-start | bytes 1572872 | tf_op jit(solution)/shard_map/ppermute | solution.py:523
  40.4 5.0 %collective-permute-start.8 = (bf16[32,2048]{1,0:T(8,128)(2,1)S(1)}, bf16[32,2048]{1,0:T(8,128)(2,1)S(1)}, u32[]{:S(2)}, u32[]{:S(2)}) collective-permute-start(bf16[32,2048]{1,0:T(8,128)(2,1)S(1)} %get-tuple-element.51.mine1), channel_id=1, source_target_pairs={{0,1},{1,0},{2,3},{3,2},{4,5},{5,4},{6,7},{7,6},{8,9},{9,8},{10,11... | collective-permute-start | bytes 393224 | tf_op jit(solution)/shard_map/ppermute | solution.py:628
  42.5 13.3 %collective-permute-start.11 = (bf16[128,2048]{1,0:T(8,128)(2,1)S(1)}, bf16[128,2048]{1,0:T(8,128)(2,1)S(1)}, u32[]{:S(2)}, u32[]{:S(2)}) collective-permute-start(bf16[128,2048]{1,0:T(8,128)(2,1)S(1)} %shard_map.219), channel_id=1, source_target_pairs={{0,28},{4,0},{8,4},{12,8},{16,12},{20,16},{24,20},{28,24},{1,29},{... | collective-permute-start | bytes 1572872 | tf_op jit(solution)/shard_map/ppermute | solution.py:523
  45.4 6.9 %collective-permute-start.9 = (bf16[64,2048]{1,0:T(8,128)(2,1)S(1)}, bf16[64,2048]{1,0:T(8,128)(2,1)S(1)}, u32[]{:S(2)}, u32[]{:S(2)}) collective-permute-start(bf16[64,2048]{1,0:T(8,128)(2,1)S(1)} %shard_map.218.mine), channel_id=1, source_target_pairs={{0,2},{1,3},{2,0},{3,1},{4,6},{5,7},{6,4},{7,5},{8,10},{9,11},{10,... | collective-permute-start | bytes 786440 | tf_op jit(solution)/shard_map/ppermute | solution.py:628

commit v11 on v10

--- a/solution.py
+++ b/solution.py
@@ -10,7 +10,7 @@
 from jax.sharding import PartitionSpec as P
 
 epsilon = 1e-05
-BLOCK = 1024
+BLOCK = 2048
 LANES = 128
 F32 = jnp.float32
 BF16 = jnp.bfloat16
@@ -230,6 +230,21 @@
     norm_pieces([(saved.at[0], 0, own)], slot_row(weights, slot), first, length, masked, mean, inverse)
 
 
+def prepare_later_kernel(notes, saved, act, weights, q_table, *outs):
+    own, width = act.shape
+    layers = ((saved.at[1], BACK1, outs[:4]), (act, AHEAD0, outs[4:]))
+    for x, layer, (masked, mean, inverse, _) in layers:
+        slot, length, first = looked_up(notes, layer)
+        norm_pieces([(x, 0, own)], slot_row(weights, slot), first, length, masked, mean, inverse)
+    for _, layer, (_, _, _, q) in layers:
+        slot = notes[layer]
+
+        def block(columns, slot=slot, q=q):
+            q[:, columns] = tap_spectrum(q_table[...], weights[slot, :, columns])
+
+        each_block(width, block)
+
+
 def norm_halo(left, right, own, gain, first, length, halo):
     reach = left.shape[0]
     norm_pieces([(left, 0, reach)], gain, first - reach, length, halo)
@@ -315,22 +330,17 @@
 
 
 def second_ready_kernel(
-    reach, notes, saved, far, near, weights, m_table, q_table, c_table,
-    m_out, q_out, factor, conv_out, mean, inverse, halo, halos, masked,
+    reach, notes, far, near, weights, masked, q, m_table, c_table, m_out, factor, conv_out, halo, halos
 ):
     own, width = masked.shape
     slot, length, first = looked_up(notes, BACK1)
-    gain = slot_row(weights, slot)
     left, right = sorted_halos(near, far, 0, halos)
-    norm_pieces([(saved.at[1], 0, own)], gain, first, length, masked, mean, inverse)
-    norm_halo(left, right, own, gain, first, length, halo)
+    norm_halo(left, right, own, slot_row(weights, slot), first, length, halo)
 
     def block(columns):
         m = transform(m_table, joined(halo, masked, columns))
-        q = tap_spectrum(q_table[...], weights[slot, :, columns])
-        conv = transform(c_table, product(m, q))
+        conv = transform(c_table, product(m, q[:, columns]))
         m_out[:, columns] = m
-        q_out[:, columns] = q
         factor[:, columns] = gate_factor(conv)
         edge = (conv.shape[0] - own) // 2
         conv_out[:, columns] = conv[edge : edge + own]
@@ -378,19 +388,16 @@
     last_pass([(received, 0, own)], pieces, mean, inverse, scaled, sum_a, sum_b, grad_x)
 
 
-def first_forward_kernel(reach, notes, act, far, near, weights, m_table, q_table, c_table, out, halo, halos, masked):
+def first_forward_kernel(reach, notes, act, far, near, weights, masked, q, m_table, c_table, out, halo, halos):
     own, width = act.shape
     middle = reach // 2
     slot, length, first = looked_up(notes, AHEAD0)
-    gain = slot_row(weights, slot)
     left, right = sorted_halos(near, far, reach, halos)
     inner = [(left, middle, middle), (act, 0, own), (right, 0, middle)]
-    norm_pieces([(act, 0, own)], gain, first, length, masked)
-    norm_halo(left, right, own, gain, first, length, halo)
+    norm_halo(left, right, own, slot_row(weights, slot), first, length, halo)
 
     def block(columns):
-        q = tap_spectrum(q_table[...], weights[slot, :, columns])
-        conv = transform(c_table, product(transform(m_table, joined(halo, masked, columns)), q))
+        conv = transform(c_table, product(transform(m_table, joined(halo, masked, columns)), q[:, columns]))
         out[:, columns] = (window(inner, columns).astype(F32) + conv * sigmoid(conv)).astype(BF16)
 
     each_block(width, block)
@@ -585,21 +592,17 @@
     )
     grad_mid = shifted(grad_mid, -1)
     near2, far2 = swapped(near2, far2, -1)
-    taps0 = run(
-        first_taps_kernel, like(tap_count + 1, width, BF16), [],
-        [halo0, layer0[0], inner0, gain0, m_table, go_table, t_table],
-        0,
-    )
-    halo_scratch = [
-        pltpu.VMEM((2 * two, width), BF16), pltpu.VMEM((2, two, width), BF16), pltpu.VMEM((own, width), BF16)
-    ]
+    layer = (*layer, like(size, width, F32))
+    masked1, mean1, inverse1, q1, masked2, _, _, q2 = run(
+        prepare_later_kernel, (*layer, *layer), [], [notes, saved, act, weights, q_table], 0, gain0
+    )
+    halo_scratch = [pltpu.VMEM((2 * two, width), BF16), pltpu.VMEM((2, two, width), BF16)]
     between = run(
         functools.partial(first_forward_kernel, two),
         like(small, width, BF16),
         halo_scratch,
-        [notes, act, far1, near1, weights, m_table, q_table, c_table],
+        [notes, act, far1, near1, weights, masked2, q2, m_table, c_table],
         20,
-        taps0,
     )
     act_ahead = run(
         second_forward_kernel,
@@ -612,14 +615,17 @@
         3,
     )
     act_out = shifted(act_ahead, 2)
-    m1, q1, factor1, conv1, mean1, inverse1 = run(
+    taps0 = run(
+        first_taps_kernel, like(tap_count + 1, width, BF16), [],
+        [halo0, layer0[0], inner0, gain0, m_table, go_table, t_table],
+        0,
+        act_ahead,
+    )
+    m1, factor1, conv1 = run(
         functools.partial(second_ready_kernel, two),
-        (
-            like(size, width, F32), like(size, width, F32), like(small, width, F32), like(own, width, F32),
-            like(own, LANES, F32), like(own, LANES, F32),
-        ),
+        (like(size, width, F32), like(small, width, F32), like(own, width, F32)),
         halo_scratch,
-        [notes, saved, far1, near1, weights, m_table, q_table, c_table],
+        [notes, far1, near1, weights, masked1, q1, m_table, c_table],
         3,
         act_ahead,
     )

time: 58.6 us -> 60.1 us (1.026)
  starting transfers between devices: 19.1 us -> 21.3 us
  waiting for transfers between devices: 13.3 us -> 12.5 us
    ppermute x3, starting transfers between devices: 0.19 us -> 3.27 us  [partner(): return lax.ppermute(x, 'tm', [(i, i ^ step) for i in range(shards)])]
    ppermute x3, waiting for transfers between devices: 8.87 us -> 7.11 us  [partner(): return lax.ppermute(x, 'tm', [(i, i ^ step) for i in range(shards)])]
    ppermute x3, waiting for transfers between devices: 3.59 us -> 4.58 us  [shifted(): lax.ppermute(x, 'section', [(i, (i + by) % sections) for i in range(secti...]
    ppermute x3, starting transfers between devices: 4.81 us -> 3.89 us  [shifted(): lax.ppermute(x, 'section', [(i, (i + by) % sections) for i in range(secti...]
    pallas_call x11 -> x12, Pallas kernels: 21.8 us -> 21.9 us  [call(): pl.pallas_call(kernel, out_shape=outs, in_specs=specs, out_specs=jax.tree...]
  transfers between devices with their start and end apart: 12 -> 12, of which waited for: 4 -> 5; matrix products, arithmetic and copies ran while one was open for 0% -> 0% of each run, Pallas kernels for 30% -> 30%
where the time goes in v11:
time: 60.1 us; the launch traced here: 59.8 us
  Pallas kernels  21.9 us (36%)
  starting transfers between devices  21.3 us (35%)
  waiting for transfers between devices  12.5 us (21%)
  local copies, waits for them, and re-layouts  3.01 us (5%)
  between operations  1.08 us (2%)
    pallas_call x12, Pallas kernels, call(): pl.pallas_call(kernel, out_shape=outs, in_specs=specs, out_specs=jax.tree...  21.9 us
    ppermute x6, starting transfers between devices, swapped(): results.append(lax.ppermute(x, ('section', 'tm'), pairs))  14.1 us
    ppermute x3, waiting for transfers between devices, partner(): return lax.ppermute(x, 'tm', [(i, i ^ step) for i in range(shards)])  7.11 us
    ppermute x3, waiting for transfers between devices, shifted(): lax.ppermute(x, 'section', [(i, (i + by) % sections) for i in range(secti...  4.58 us
    ppermute x3, starting transfers between devices, shifted(): lax.ppermute(x, 'section', [(i, (i + by) % sections) for i in range(secti...  3.89 us
    ppermute x3, starting transfers between devices, partner(): return lax.ppermute(x, 'tm', [(i, i ^ step) for i in range(shards)])  3.27 us
    unnamed x38, local copies, waits for them, and re-layouts  3.01 us
  transfers between devices with their start and end apart: 12, of which 5 were waited for; matrix products, arithmetic and copies ran while one was open for 0% of the time, Pallas kernels for 30%

profile of v11, /device:TPU:1, one launch (start us, length us, event | category | flops | bytes accessed | tf_op | source)
XLA Modules:
  0.0 59.8 jit_solution(17263484124452892754)
XLA Ops:
  0.7 1.9 %shard_map.210 = (bf16[48,2048]{1,0:T(8,128)(2,1)}, bf16[48,2048]{1,0:T(8,128)(2,1)}, s32[8]{0:T(128)}) custom-call(bf16[2,128,2048]{2,1,0:T(8,128)(2,1)} %bitcast.15, bf16[1,128,2048]{2,1,0:T(8,128)(2,1)} %grad.1, s32[8]{0:T(128)} %back_lengths.1, s32[8]{0:T(128)} %ahead_lengths.1, s32[2,8]{1,0:T(2,128)} %bitcast.26, s32[2,8]{1,0:T(2,128)} %bitcast.27), custom_call_target="tpu_custom_call" | custom-call | tf_op jit(solution)/shard_map/pallas_call | solution.py:497
  2.6 0.7 %collective-permute-start = (bf16[48,2048]{1,0:T(8,128)(2,1)}, bf16[48,2048]{1,0:T(8,128)(2,1)S(1)}, u32[]{:S(2)}, u32[]{:S(2)}) collective-permute-start(bf16[48,2048]{1,0:T(8,128)(2,1)} %get-tuple-element.36), channel_id=1, source_target_pairs={{1,2},{2,1},{5,6},{6,5},{9,10},{10,9},{13,14},{14,13},{17,18},{18,... | collective-permute-start | bytes 589832 | tf_op jit(solution)/shard_map/ppermute | solution.py:542
  3.3 4.6 %collective-permute-start.1 = (bf16[48,2048]{1,0:T(8,128)(2,1)}, bf16[48,2048]{1,0:T(8,128)(2,1)S(1)}, u32[]{:S(2)}, u32[]{:S(2)}) collective-permute-start(bf16[48,2048]{1,0:T(8,128)(2,1)} %get-tuple-element.37), channel_id=1, source_target_pairs={{0,1},{1,0},{2,3},{3,2},{4,5},{5,4},{6,7},{7,6},{8,9},{9,8},{10,11... | collective-permute-start | bytes 589832 | tf_op jit(solution)/shard_map/ppermute | solution.py:542
  7.8 1.2 %copy-done = bf16[1,2,128,2048]{3,2,1,0:T(8,128)(2,1)S(1)} copy-done((bf16[1,2,128,2048]{3,2,1,0:T(8,128)(2,1)S(1)}, bf16[1,2,128,2048]{3,2,1,0:T(8,128)(2,1)}, u32[]{:S(2)}) %copy-start) | copy-done | bytes 1048600
  9.0 1.0 %copy-done.2 = bf16[1,128,2048]{2,1,0:T(8,128)(2,1)S(1)} copy-done((bf16[1,128,2048]{2,1,0:T(8,128)(2,1)S(1)}, bf16[1,128,2048]{2,1,0:T(8,128)(2,1)}, u32[]{:S(2)}) %copy-start.2) | copy-done | bytes 524312
  10.1 0.7 %copy-done.11 = s32[8]{0:T(128)S(1)} copy-done((s32[8]{0:T(128)S(1)}, s32[8]{0:T(128)}, u32[]{:S(2)}) %copy-start.11) | copy-done | bytes 56
  10.8 1.7 %shard_map.211 = (bf16[2,32,2048]{2,1,0:T(8,128)(2,1)S(1)}, bf16[32,2048]{1,0:T(8,128)(2,1)S(1)}, bf16[64,2048]{1,0:T(8,128)(2,1)S(1)}, bf16[64,2048]{1,0:T(8,12...) custom-call(s32[8]{0:T(128)S(1)} %copy-done.11, ...), custom_call_target="tpu_custom_call" | custom-call | tf_op jit(solution)/shard_map/pallas_call | solution.py:497
  12.5 0.7 %collective-permute-start.2 = (bf16[64,2048]{1,0:T(8,128)(2,1)S(1)}, bf16[64,2048]{1,0:T(8,128)(2,1)S(1)}, u32[]{:S(2)}, u32[]{:S(2)}) collective-permute-start(bf16[64,2048]{1,0:T(8,128)(2,1)S(1)} %get-tuple-element.46), channel_id=1, source_target_pairs={{1,2},{2,1},{5,6},{6,5},{9,10},{10,9},{13,14},{14,13},{17,18},{18,... | collective-permute-start | bytes 786440 | tf_op jit(solution)/shard_map/ppermute | solution.py:542
  13.1 2.5 %collective-permute-start.3 = (bf16[64,2048]{1,0:T(8,128)(2,1)S(1)}, bf16[64,2048]{1,0:T(8,128)(2,1)S(1)}, u32[]{:S(2)}, u32[]{:S(2)}) collective-permute-start(bf16[64,2048]{1,0:T(8,128)(2,1)S(1)} %get-tuple-element.47), channel_id=1, source_target_pairs={{0,1},{1,0},{2,3},{3,2},{4,5},{5,4},{6,7},{7,6},{8,9},{9,8},{10,11... | collective-permute-start | bytes 786440 | tf_op jit(solution)/shard_map/ppermute | solution.py:542
  15.6 0.8 %collective-permute-done.1.near = bf16[48,2048]{1,0:T(8,128)(2,1)S(1)} collective-permute-done((bf16[48,2048]{1,0:T(8,128)(2,1)}, bf16[48,2048]{1,0:T(8,128)(2,1)S(1)}, u32[]{:S(2)}, u32[]{:S(2)}) %collective-permute-start.1) | collective-permute-done | bytes 196640 | tf_op jit(solution)/shard_map/ppermute | solution.py:542
  16.5 3.5 %shard_map.212 = (bf16[160,2048]{1,0:T(8,128)(2,1)S(1)}, bf16[16,2048]{1,0:T(8,128)(2,1)S(1)}, bf16[16,2048]{1,0:T(8,128)(2,1)S(1)}, bf16[64,2048]{1,0:T(8,128)(...) custom-call(s32[8]{0:T(128)S(1)} %copy-done.11, bf16[2,128,2048]{2,1,0:T(8,128)(2,1)S(1)} %bitcast.17, ...), custom_call_target="tpu_custom_call" | custom-call | flops 4000000000 | tf_op jit(solution)/shard_map/pallas_call | solution.py:497
  20.0 2.2 %shard_map.213 = (bf16[128,2048]{1,0:T(8,128)(2,1)S(1)}, f32[128,128]{1,0:T(8,128)S(1)}, f32[128,128]{1,0:T(8,128)S(1)}, f32[192,2048]{1,0:T(8,128)S(1)}, bf16[1...) custom-call(s32[8]{0:T(128)S(1)} %copy-done.11, ...), custom_call_target="tpu_custom_call" | custom-call | tf_op jit(solution)/shard_map/pallas_call | solution.py:497
  22.2 2.3 %collective-permute-start.4 = (bf16[160,2048]{1,0:T(8,128)(2,1)S(1)}, bf16[160,2048]{1,0:T(8,128)(2,1)S(1)}, u32[]{:S(2)}, u32[]{:S(2)}) collective-permute-start(bf16[160,2048]{1,0:T(8,128)(2,1)S(1)} %get-tuple-element.50), channel_id=1, source_target_pairs={{0,28},{4,0},{8,4},{12,8},{16,12},{20,16},{24,20},{28,24},{1,29},{... | collective-permute-start | bytes 1966088 | tf_op jit(solution)/shard_map/ppermute | solution.py:530
  24.5 0.7 %collective-permute-start.6 = (bf16[16,2048]{1,0:T(8,128)(2,1)S(1)}, bf16[16,2048]{1,0:T(8,128)(2,1)S(1)}, u32[]{:S(2)}, u32[]{:S(2)}) collective-permute-start(bf16[16,2048]{1,0:T(8,128)(2,1)S(1)} %get-tuple-element.51), channel_id=1, source_target_pairs={{1,30},{2,29},{5,2},{6,1},{9,6},{10,5},{13,10},{14,9},{17,14},{18,... | collective-permute-start | bytes 196616 | tf_op jit(solution)/shard_map/ppermute | solution.py:542
  25.2 5.1 %collective-permute-start.7 = (bf16[16,2048]{1,0:T(8,128)(2,1)S(1)}, bf16[16,2048]{1,0:T(8,128)(2,1)S(1)}, u32[]{:S(2)}, u32[]{:S(2)}) collective-permute-start(bf16[16,2048]{1,0:T(8,128)(2,1)S(1)} %get-tuple-element.52), channel_id=1, source_target_pairs={{0,29},{1,28},{2,31},{3,30},{4,1},{5,0},{6,3},{7,2},{8,5},{9,4},{1... | collective-permute-start | bytes 196616 | tf_op jit(solution)/shard_map/ppermute | solution.py:542
  30.3 2.0 %shard_map.214.between = bf16[160,2048]{1,0:T(8,128)(2,1)S(1)} custom-call(s32[8]{0:T(128)S(1)} %copy-done.12, bf16[128,2048]{1,0:T(8,128)(2,1)S(1)} %bitcast.22, bf16[64,2048]{1,0:T(8,128)(2,1)S(1)} %collective-permute-done.2.far.refs_1_, bf16[64,2048]{1,0:T(8,128)(2,1)S(1)} %collective-permute-done.3.near.refs_2_, ...), custom_call_target="tpu_custom_call" | custom-call | flops 20000000000 | tf_op jit(solution)/shard_map/pallas_call | solution.py:497
  32.3 1.7 %collective-permute-done.4.received = bf16[160,2048]{1,0:T(8,128)(2,1)S(1)} collective-permute-done((bf16[160,2048]{1,0:T(8,128)(2,1)S(1)}, bf16[160,2048]{1,0:T(8,128)(2,1)S(1)}, u32[]{:S(2)}, u32[]{:S(2)}) %collective-permute-start.4) | collective-permute-done | bytes 655392 | tf_op jit(solution)/shard_map/ppermute | solution.py:530
  34.0 2.0 %shard_map.215.refs_7_.refs_8_ = bf16[128,2048]{1,0:T(8,128)(2,1)S(1)} custom-call(s32[8]{0:T(128)S(1)} %copy-done.12, bf16[160,2048]{1,0:T(8,128)(2,1)S(1)} %shard_map.214.between, bf16[160,2048]{1,0:T(8,128)(2,1)S(1)} %collective-permute-done.4.received, bf16[320,160]{1,0:T(8,128)(2,1)S(1)} %copy-done.15, bf16[160,64]{1,0:T(8,128)(2,1)S(1)} %copy-done.18, ...), custom_call_target="tpu_custom_call" | custom-call | flops 3000000000 | tf_op jit(solution)/shard_map/pallas_call | solution.py:497
  36.0 1.5 %collective-permute-start.10 = (bf16[128,2048]{1,0:T(8,128)(2,1)S(1)}, bf16[128,2048]{1,0:T(8,128)(2,1)S(1)}, u32[]{:S(2)}, u32[]{:S(2)}) collective-permute-start(bf16[128,2048]{1,0:T(8,128)(2,1)S(1)} %shard_map.215.refs_7_.refs_8_), channel_id=1, source_target_pairs={{0,8},{4,12},{8,16},{12,20},{16,24},{20,28},{24,0},{28,4},{1,9},{5... | collective-permute-start | bytes 1572872 | tf_op jit(solution)/shard_map/ppermute | solution.py:530
  37.5 1.0 %shard_map.216.mine0 = bf16[32,2048]{1,0:T(8,128)(2,1)S(1)} custom-call(bf16[64,2048]{1,0:T(8,128)(2,1)S(1)} %get-tuple-element.43.refs_0_, bf16[128,2048]{1,0:T(8,128)(2,1)S(1)} %get-tuple-element.40.masked.refs_1_, bf16[128,2048]{1,0:T(8,128)(2,1)S(1)} %get-tuple-element.44.refs_2_, f32[1,2048]{1,0:T(1,128)S(1)} %get-tuple-element.45.refs_5_.refs_3_, ...), custom_call_target="tpu_custom_call" | custom-call | tf_op jit(solution)/shard_map/pallas_call | solution.py:497
  38.5 0.1 collective-permute-start.5
  38.6 2.0 %shard_map.217 = (f32[192,2048]{1,0:T(8,128)S(1)}, f32[160,2048]{1,0:T(8,128)S(1)}, f32[128,2048]{1,0:T(8,128)S(1)}) custom-call(s32[8]{0:T(128)S(1)} %copy-done.12, bf16[64,2048]{1,0:T(8,128)(2,1)S(1)} %collective-permute-done.2.far.refs_1_, bf16[64,2048]{1,0:T(8,128)(2,1)S(1)} %collective-permute-done.3.near.refs_2_, ...), custom_call_target="tpu_custom_call" | custom-call | flops 3000000000 | tf_op jit(solution)/shard_map/pallas_call | solution.py:497
  40.6 1.4 %shard_map.218 = (bf16[160,2048]{1,0:T(8,128)(2,1)S(1)}, bf16[32,2048]{1,0:T(8,128)(2,1)S(1)}) custom-call(s32[8]{0:T(128)S(1)} %copy-done.12, bf16[160,2048]{1,0:T(8,128)(2,1)S(1)} %collective-permute-done.4.received, bf16[16,2048]{1,0:T(8,128)(2,1)S(1)} %collective-permute-done.6.far, bf16[16,2048]{1,0:T(8,128)(2,1)S(1)} %collective-permute-done.7.near, ...), custom_call_target="tpu_custom_call" | custom-call | flops 2000000000 | tf_op jit(solution)/shard_map/pallas_call | solution.py:497
  42.0 1.5 %collective-permute-start.8 = (bf16[32,2048]{1,0:T(8,128)(2,1)S(1)}, bf16[32,2048]{1,0:T(8,128)(2,1)S(1)}, u32[]{:S(2)}, u32[]{:S(2)}) collective-permute-start(bf16[32,2048]{1,0:T(8,128)(2,1)S(1)} %get-tuple-element.58.mine1), channel_id=1, source_target_pairs={{0,1},{1,0},{2,3},{3,2},{4,5},{5,4},{6,7},{7,6},{8,9},{9,8},{10,11... | collective-permute-start | bytes 393224 | tf_op jit(solution)/shard_map/ppermute | solution.py:634
  43.5 1.9 %shard_map.220 = bf16[128,2048]{1,0:T(8,128)(2,1)S(1)} custom-call(s32[8]{0:T(128)S(1)} %copy-done.12, bf16[2,128,2048]{2,1,0:T(8,128)(2,1)S(1)} %bitcast.19, bf16[160,2048]{1,0:T(8,128)(2,1)S(1)} %collective-permute-done.4.received, bf16[2,32,2048]{2,1,0:T(8,128)(2,1)S(1)} %get-tuple-element.38.weights.refs_3_, ...), custom_call_target="tpu_custom_call" | custom-call | flops 6000000000 | tf_op jit(solution)/shard_map/pallas_call | solution.py:497
  45.5 0.1 collective-permute-start.11
  45.6 1.4 %collective-permute-done.8.other1 = bf16[32,2048]{1,0:T(8,128)(2,1)S(1)} collective-permute-done((bf16[32,2048]{1,0:T(8,128)(2,1)S(1)}, bf16[32,2048]{1,0:T(8,128)(2,1)S(1)}, u32[]{:S(2)}, u32[]{:S(2)}) %collective-permute-start.8) | collective-permute-done | bytes 131104 | tf_op jit(solution)/shard_map/ppermute | solution.py:634
  47.0 0.1 shard_map.219.mine
  47.1 1.7 %collective-permute-start.9 = (bf16[64,2048]{1,0:T(8,128)(2,1)S(1)}, bf16[64,2048]{1,0:T(8,128)(2,1)S(1)}, u32[]{:S(2)}, u32[]{:S(2)}) collective-permute-start(bf16[64,2048]{1,0:T(8,128)(2,1)S(1)} %shard_map.219.mine), channel_id=1, source_target_pairs={{0,2},{1,3},{2,0},{3,1},{4,6},{5,7},{6,4},{7,5},{8,10},{9,11},{10,... | collective-permute-start | bytes 786440 | tf_op jit(solution)/shard_map/ppermute | solution.py:634
  48.8 5.7 %collective-permute-done.9.other = bf16[64,2048]{1,0:T(8,128)(2,1)S(1)} collective-permute-done((bf16[64,2048]{1,0:T(8,128)(2,1)S(1)}, bf16[64,2048]{1,0:T(8,128)(2,1)S(1)}, u32[]{:S(2)}, u32[]{:S(2)}) %collective-permute-start.9) | collective-permute-done | bytes 262176 | tf_op jit(solution)/shard_map/ppermute | solution.py:634
  54.5 2.9 %collective-permute-done.11.grad = bf16[128,2048]{1,0:T(8,128)(2,1)S(1)} collective-permute-done((bf16[128,2048]{1,0:T(8,128)(2,1)S(1)}, bf16[128,2048]{1,0:T(8,128)(2,1)S(1)}, u32[]{:S(2)}, u32[]{:S(2)}) %collective-permute-start.11) | collective-permute-done | bytes 524320 | tf_op jit(solution)/shard_map/ppermute | solution.py:530
  57.4 2.3 %shard_map.221 = (bf16[128,2048]{1,0:T(8,128)(2,1)}, bf16[128,2048]{1,0:T(8,128)(2,1)}, f32[31,2,2048]{2,1,0:T(2,128)}, f32[2,2048]{1,0:T(2,128)}) custom-call(s32[8]{0:T(128)S(1)} %copy-done.12, bf16[64,2048]{1,0:T(8,128)(2,1)S(1)} %shard_map.219.mine, bf16[64,2048]{1,0:T(8,128)(2,1)S(1)} %collective-permute-done.9.other, ...), custom_call_target="tpu_custom_call" | custom-call | tf_op jit(solution)/shard_map/pallas_call | solution.py:497
  (42 shorter events, 0.1 us)
Async XLA Ops:
  0.6 7.2 %copy-start.5 = (bf16[1,2,31,2048]{3,1,2,0:T(2,128)(2,1)S(1)}, bf16[1,2,31,2048]{3,1,2,0:T(2,128)(2,1)}, u32[]{:S(2)}) copy-start(bf16[1,2,31,2048]{3,1,2,0:T(2,128)(2,1)} %param.22) | copy-start | bytes 761860
  0.6 7.2 %copy-start.10 = (bf16[1,2,2048]{2,1,0:T(2,128)(2,1)S(1)}, bf16[1,2,2048]{2,1,0:T(2,128)(2,1)}, u32[]{:S(2)}) copy-start(bf16[1,2,2048]{2,1,0:T(2,128)(2,1)} %param.23) | copy-start | bytes 24580
  0.7 15.8 %copy-start.6 = (bf16[384,192]{1,0:T(8,128)(2,1)S(1)}, bf16[384,192]{1,0:T(8,128)(2,1)}, u32[]{:S(2)}) copy-start(bf16[384,192]{1,0:T(8,128)(2,1)} %constant.20.clone.m_table.refs_4_.refs_6_) | copy-start | bytes 442372
  2.6 13.0 %collective-permute-start = (bf16[48,2048]{1,0:T(8,128)(2,1)}, bf16[48,2048]{1,0:T(8,128)(2,1)S(1)}, u32[]{:S(2)}, u32[]{:S(2)}) collective-permute-start(bf16[48,2048]{1,0:T(8,128)(2,1)} %get-tuple-element.36), channel_id=1, source_target_pairs={{1,2},{2,1},{5,6},{6,5},{9,10},{10,9},{13,14},{14,13},{17,18},{18,... | collective-permute-start | bytes 589832 | tf_op jit(solution)/shard_map/ppermute | solution.py:542
  3.3 13.2 %collective-permute-start.1 = (bf16[48,2048]{1,0:T(8,128)(2,1)}, bf16[48,2048]{1,0:T(8,128)(2,1)S(1)}, u32[]{:S(2)}, u32[]{:S(2)}) collective-permute-start(bf16[48,2048]{1,0:T(8,128)(2,1)} %get-tuple-element.37), channel_id=1, source_target_pairs={{0,1},{1,0},{2,3},{3,2},{4,5},{5,4},{6,7},{7,6},{8,9},{9,8},{10,11... | collective-permute-start | bytes 589832 | tf_op jit(solution)/shard_map/ppermute | solution.py:542
  7.8 1.2 %copy-start = (bf16[1,2,128,2048]{3,2,1,0:T(8,128)(2,1)S(1)}, bf16[1,2,128,2048]{3,2,1,0:T(8,128)(2,1)}, u32[]{:S(2)}) copy-start(bf16[1,2,128,2048]{3,2,1,0:T(8,128)(2,1)} %param.21) | copy-start | bytes 3145732
  9.0 1.0 %copy-start.2 = (bf16[1,128,2048]{2,1,0:T(8,128)(2,1)S(1)}, bf16[1,128,2048]{2,1,0:T(8,128)(2,1)}, u32[]{:S(2)}) copy-start(bf16[1,128,2048]{2,1,0:T(8,128)(2,1)} %param.19) | copy-start | bytes 1572868
  10.1 0.7 %copy-start.11 = (s32[8]{0:T(128)S(1)}, s32[8]{0:T(128)}, u32[]{:S(2)}) copy-start(s32[8]{0:T(128)} %get-tuple-element.35.notes.refs_0_) | copy-start | bytes 100
  10.7 5.7 %copy-start.4 = (bf16[1,128,2048]{2,1,0:T(8,128)(2,1)S(1)}, bf16[1,128,2048]{2,1,0:T(8,128)(2,1)}, u32[]{:S(2)}) copy-start(bf16[1,128,2048]{2,1,0:T(8,128)(2,1)} %grad.1) | copy-start | bytes 1572868
  10.7 5.7 %copy-start.8 = (bf16[192,64]{1,0:T(8,128)(2,1)S(1)}, bf16[192,64]{1,0:T(8,128)(2,1)}, u32[]{:S(2)}) copy-start(bf16[192,64]{1,0:T(8,128)(2,1)} %constant.21.clone.q_table.refs_4_) | copy-start | bytes 73732
  10.7 5.7 %copy-start.13 = (bf16[384,160]{1,0:T(8,128)(2,1)S(1)}, bf16[384,160]{1,0:T(8,128)(2,1)}, u32[]{:S(2)}) copy-start(bf16[384,160]{1,0:T(8,128)(2,1)} %constant.23.clone.g_table) | copy-start | bytes 368644
  10.7 5.7 %copy-start.14 = (bf16[320,192]{1,0:T(8,128)(2,1)S(1)}, bf16[320,192]{1,0:T(8,128)(2,1)}, u32[]{:S(2)}) copy-start(bf16[320,192]{1,0:T(8,128)(2,1)} %constant.22.clone.c_table.refs_7_) | copy-start | bytes 368644
  10.8 5.7 %copy-start.16 = (bf16[256,192]{1,0:T(8,128)(2,1)S(1)}, bf16[256,192]{1,0:T(8,128)(2,1)}, u32[]{:S(2)}) copy-start(bf16[256,192]{1,0:T(8,128)(2,1)} %constant.24.clone.x_table) | copy-start | bytes 294916
  12.5 17.8 %collective-permute-start.2 = (bf16[64,2048]{1,0:T(8,128)(2,1)S(1)}, bf16[64,2048]{1,0:T(8,128)(2,1)S(1)}, u32[]{:S(2)}, u32[]{:S(2)}) collective-permute-start(bf16[64,2048]{1,0:T(8,128)(2,1)S(1)} %get-tuple-element.46), channel_id=1, source_target_pairs={{1,2},{2,1},{5,6},{6,5},{9,10},{10,9},{13,14},{14,13},{17,18},{18,... | collective-permute-start | bytes 786440 | tf_op jit(solution)/shard_map/ppermute | solution.py:542
  13.1 17.1 %collective-permute-start.3 = (bf16[64,2048]{1,0:T(8,128)(2,1)S(1)}, bf16[64,2048]{1,0:T(8,128)(2,1)S(1)}, u32[]{:S(2)}, u32[]{:S(2)}) collective-permute-start(bf16[64,2048]{1,0:T(8,128)(2,1)S(1)} %get-tuple-element.47), channel_id=1, source_target_pairs={{0,1},{1,0},{2,3},{3,2},{4,5},{5,4},{6,7},{7,6},{8,9},{9,8},{10,11... | collective-permute-start | bytes 786440 | tf_op jit(solution)/shard_map/ppermute | solution.py:542
  16.5 3.5 %copy-start.3 = (bf16[1,128,2048]{2,1,0:T(8,128)(2,1)S(1)}, bf16[1,128,2048]{2,1,0:T(8,128)(2,1)}, u32[]{:S(2)}) copy-start(bf16[1,128,2048]{2,1,0:T(8,128)(2,1)} %param.19) | copy-start | bytes 1572868
  20.0 10.3 %copy-start.12 = (s32[8]{0:T(128)S(1)}, s32[8]{0:T(128)}, u32[]{:S(2)}) copy-start(s32[8]{0:T(128)} %get-tuple-element.35.notes.refs_0_) | copy-start | bytes 100
  22.2 11.7 %collective-permute-start.4 = (bf16[160,2048]{1,0:T(8,128)(2,1)S(1)}, bf16[160,2048]{1,0:T(8,128)(2,1)S(1)}, u32[]{:S(2)}, u32[]{:S(2)}) collective-permute-start(bf16[160,2048]{1,0:T(8,128)(2,1)S(1)} %get-tuple-element.50), channel_id=1, source_target_pairs={{0,28},{4,0},{8,4},{12,8},{16,12},{20,16},{24,20},{28,24},{1,29},{... | collective-permute-start | bytes 1966088 | tf_op jit(solution)/shard_map/ppermute | solution.py:530
  24.5 16.1 %collective-permute-start.6 = (bf16[16,2048]{1,0:T(8,128)(2,1)S(1)}, bf16[16,2048]{1,0:T(8,128)(2,1)S(1)}, u32[]{:S(2)}, u32[]{:S(2)}) collective-permute-start(bf16[16,2048]{1,0:T(8,128)(2,1)S(1)} %get-tuple-element.51), channel_id=1, source_target_pairs={{1,30},{2,29},{5,2},{6,1},{9,6},{10,5},{13,10},{14,9},{17,14},{18,... | collective-permute-start | bytes 196616 | tf_op jit(solution)/shard_map/ppermute | solution.py:542
  25.2 15.4 %collective-permute-start.7 = (bf16[16,2048]{1,0:T(8,128)(2,1)S(1)}, bf16[16,2048]{1,0:T(8,128)(2,1)S(1)}, u32[]{:S(2)}, u32[]{:S(2)}) collective-permute-start(bf16[16,2048]{1,0:T(8,128)(2,1)S(1)} %get-tuple-element.52), channel_id=1, source_target_pairs={{0,29},{1,28},{2,31},{3,30},{4,1},{5,0},{6,3},{7,2},{8,5},{9,4},{1... | collective-permute-start | bytes 196616 | tf_op jit(solution)/shard_map/ppermute | solution.py:542
  30.3 3.7 %copy-start.15 = (bf16[320,160]{1,0:T(8,128)(2,1)S(1)}, bf16[320,160]{1,0:T(8,128)(2,1)}, u32[]{:S(2)}) copy-start(bf16[320,160]{1,0:T(8,128)(2,1)} %constant.25.clone.m_table) | copy-start | bytes 307204
  30.3 3.7 %copy-start.17 = (bf16[256,160]{1,0:T(8,128)(2,1)S(1)}, bf16[256,160]{1,0:T(8,128)(2,1)}, u32[]{:S(2)}) copy-start(bf16[256,160]{1,0:T(8,128)(2,1)} %constant.27.clone.c_table) | copy-start | bytes 245764
  30.3 3.7 %copy-start.18 = (bf16[160,64]{1,0:T(8,128)(2,1)S(1)}, bf16[160,64]{1,0:T(8,128)(2,1)}, u32[]{:S(2)}) copy-start(bf16[160,64]{1,0:T(8,128)(2,1)} %constant.26.clone.q_table) | copy-start | bytes 61444
  32.3 5.2 %copy-start.7 = (bf16[192,256]{1,0:T(8,128)(2,1)S(1)}, bf16[192,256]{1,0:T(8,128)(2,1)}, u32[]{:S(2)}) copy-start(bf16[192,256]{1,0:T(8,128)(2,1)} %constant.28.clone.refs_5_.go_table) | copy-start | bytes 294916
  32.3 5.2 %copy-start.9 = (bf16[64,192]{1,0:T(8,128)(2,1)S(1)}, bf16[64,192]{1,0:T(8,128)(2,1)}, u32[]{:S(2)}) copy-start(bf16[64,192]{1,0:T(8,128)(2,1)} %constant.29.clone.refs_6_.t_table) | copy-start | bytes 73732
  36.0 18.5 %collective-permute-start.10 = (bf16[128,2048]{1,0:T(8,128)(2,1)S(1)}, bf16[128,2048]{1,0:T(8,128)(2,1)S(1)}, u32[]{:S(2)}, u32[]{:S(2)}) collective-permute-start(bf16[128,2048]{1,0:T(8,128)(2,1)S(1)} %shard_map.215.refs_7_.refs_8_), channel_id=1, source_target_pairs={{0,8},{4,12},{8,16},{12,20},{16,24},{20,28},{24,0},{28,4},{1,9},{5... | collective-permute-start | bytes 1572872 | tf_op jit(solution)/shard_map/ppermute | solution.py:530
  38.5 7.1 %collective-permute-start.5 = (bf16[32,2048]{1,0:T(8,128)(2,1)S(1)}, bf16[32,2048]{1,0:T(8,128)(2,1)S(1)}, u32[]{:S(2)}, u32[]{:S(2)}) collective-permute-start(bf16[32,2048]{1,0:T(8,128)(2,1)S(1)} %shard_map.216.mine0), channel_id=1, source_target_pairs={{0,1},{1,0},{2,3},{3,2},{4,5},{5,4},{6,7},{7,6},{8,9},{9,8},{10,11... | collective-permute-start | bytes 393224 | tf_op jit(solution)/shard_map/ppermute | solution.py:634
  40.6 2.9 %copy-start.1 = (bf16[1,2,128,2048]{3,2,1,0:T(8,128)(2,1)S(1)}, bf16[1,2,128,2048]{3,2,1,0:T(8,128)(2,1)}, u32[]{:S(2)}) copy-start(bf16[1,2,128,2048]{3,2,1,0:T(8,128)(2,1)} %param.21) | copy-start | bytes 3145732
  42.0 5.0 %collective-permute-start.8 = (bf16[32,2048]{1,0:T(8,128)(2,1)S(1)}, bf16[32,2048]{1,0:T(8,128)(2,1)S(1)}, u32[]{:S(2)}, u32[]{:S(2)}) collective-permute-start(bf16[32,2048]{1,0:T(8,128)(2,1)S(1)} %get-tuple-element.58.mine1), channel_id=1, source_target_pairs={{0,1},{1,0},{2,3},{3,2},{4,5},{5,4},{6,7},{7,6},{8,9},{9,8},{10,11... | collective-permute-start | bytes 393224 | tf_op jit(solution)/shard_map/ppermute | solution.py:634
  45.5 11.9 %collective-permute-start.11 = (bf16[128,2048]{1,0:T(8,128)(2,1)S(1)}, bf16[128,2048]{1,0:T(8,128)(2,1)S(1)}, u32[]{:S(2)}, u32[]{:S(2)}) collective-permute-start(bf16[128,2048]{1,0:T(8,128)(2,1)S(1)} %shard_map.220), channel_id=1, source_target_pairs={{0,28},{4,0},{8,4},{12,8},{16,12},{20,16},{24,20},{28,24},{1,29},{... | collective-permute-start | bytes 1572872 | tf_op jit(solution)/shard_map/ppermute | solution.py:530
  47.1 7.4 %collective-permute-start.9 = (bf16[64,2048]{1,0:T(8,128)(2,1)S(1)}, bf16[64,2048]{1,0:T(8,128)(2,1)S(1)}, u32[]{:S(2)}, u32[]{:S(2)}) collective-permute-start(bf16[64,2048]{1,0:T(8,128)(2,1)S(1)} %shard_map.219.mine), channel_id=1, source_target_pairs={{0,2},{1,3},{2,0},{3,1},{4,6},{5,7},{6,4},{7,5},{8,10},{9,11},{10,... | collective-permute-start | bytes 786440 | tf_op jit(solution)/shard_map/ppermute | solution.py:634

commit v12 on v10

--- a/solution.py
+++ b/solution.py
@@ -10,7 +10,7 @@
 from jax.sharding import PartitionSpec as P
 
 epsilon = 1e-05
-BLOCK = 1024
+BLOCK = 2048
 LANES = 128
 F32 = jnp.float32
 BF16 = jnp.bfloat16
@@ -208,10 +208,20 @@
     return lambda columns: weights[slot, last : last + 1, columns].astype(F32)
 
 
-def prepare_kernel(
-    reach, notes, kernels, gains, saved, act, weights, later, near, far, masked, mean, inverse
-):
-    own, width = act.shape
+def prepare_kernel(notes, kernels, gains, saved, weights, ahead0, ahead1, masked, mean, inverse):
+    own = saved.shape[1]
+    count = kernels.shape[0]
+    for slot in range(kernels.shape[1]):
+        weights[slot, :count, :] = kernels[:, slot, :]
+        weights[slot, count:, :] = gains[slot : slot + 1, :]
+    ahead0[...] = weights[notes[AHEAD0]]
+    ahead1[...] = weights[notes[FIRST + 1]]
+    slot, length, first = looked_up(notes, BACK0)
+    norm_pieces([(saved.at[0], 0, own)], slot_row(weights, slot), first, length, masked, mean, inverse)
+
+
+def second_pack_kernel(reach, saved, act, near, far):
+    own = act.shape[0]
     for even in range(2):
 
         @pl.when(lax.rem(lax.axis_index("tm") + 1, 2) == even)
@@ -221,14 +231,6 @@
                 tail[pl.ds(at, reach), :] = x[pl.ds(own - reach, reach), :]
                 head[pl.ds(at, reach), :] = x[pl.ds(0, reach), :]
 
-    count = kernels.shape[0]
-    for slot in range(kernels.shape[1]):
-        weights[slot, :count, :] = kernels[:, slot, :]
-        weights[slot, count:, :] = gains[slot : slot + 1, :]
-    later[...] = weights[notes[FIRST + 1]]
-    slot, length, first = looked_up(notes, BACK0)
-    norm_pieces([(saved.at[0], 0, own)], slot_row(weights, slot), first, length, masked, mean, inverse)
-
 
 def norm_halo(left, right, own, gain, first, length, halo):
     reach = left.shape[0]
@@ -242,7 +244,7 @@
 
 
 def first_backward_kernel(
-    reach, notes, saved, far, near, grads, weights, later, masked, mean, inverse,
+    reach, notes, saved, far, near, grads, weights, masked, mean, inverse,
     m_table, q_table, c_table, g_table, x_table,
     grad_x, near_edge, far_edge, halo, inner, gain_sum, halos, grad_halos, scaled, sum_a, sum_b,
 ):
@@ -258,7 +260,6 @@
     mask = frame_mask(own, first, length)
     sum_a[...] = jnp.zeros_like(sum_a)
     sum_b[...] = jnp.zeros_like(sum_b)
-    grad_x[pl.ds(own, later.shape[0]), :] = later[...]
 
     def block(columns):
         m = transform(m_table, joined(halo, masked, columns))
@@ -315,7 +316,7 @@
 
 
 def second_ready_kernel(
-    reach, notes, saved, far, near, weights, m_table, q_table, c_table,
+    reach, notes, saved, near, far, weights, m_table, q_table, c_table,
     m_out, q_out, factor, conv_out, mean, inverse, halo, halos, masked,
 ):
     own, width = masked.shape
@@ -378,38 +379,37 @@
     last_pass([(received, 0, own)], pieces, mean, inverse, scaled, sum_a, sum_b, grad_x)
 
 
-def first_forward_kernel(reach, notes, act, far, near, weights, m_table, q_table, c_table, out, halo, halos, masked):
+def row_gain(layer):
+    last = layer.shape[0] - 1
+    return lambda columns: layer[last : last + 1, columns].astype(F32)
+
+
+def first_forward_kernel(reach, notes, act, far, near, layer, m_table, q_table, c_table, out, halo, halos, masked):
     own, width = act.shape
     middle = reach // 2
-    slot, length, first = looked_up(notes, AHEAD0)
-    gain = slot_row(weights, slot)
+    _, length, first = looked_up(notes, AHEAD0)
     left, right = sorted_halos(near, far, reach, halos)
     inner = [(left, middle, middle), (act, 0, own), (right, 0, middle)]
-    norm_pieces([(act, 0, own)], gain, first, length, masked)
-    norm_halo(left, right, own, gain, first, length, halo)
+    norm_pieces([(act, 0, own)], row_gain(layer), first, length, masked)
+    norm_halo(left, right, own, row_gain(layer), first, length, halo)
 
     def block(columns):
-        q = tap_spectrum(q_table[...], weights[slot, :, columns])
+        q = tap_spectrum(q_table[...], layer[:, columns])
         conv = transform(c_table, product(transform(m_table, joined(halo, masked, columns)), q))
         out[:, columns] = (window(inner, columns).astype(F32) + conv * sigmoid(conv)).astype(BF16)
 
     each_block(width, block)
 
 
-def second_forward_kernel(notes, between, received, m_table, q_table, c_table, out, masked):
+def second_forward_kernel(notes, between, layer, m_table, q_table, c_table, out, masked):
     own, width = out.shape
     rows = between.shape[0]
     edge = (rows - own) // 2
-    slot, length, first = looked_up(notes, AHEAD0)
-    last = received.shape[0] - 1
-
-    def gain(columns):
-        return received[last : last + 1, columns].astype(F32)
-
-    norm_pieces([(between, 0, rows)], gain, first - edge, length, masked, chunk=rows // 2)
+    _, length, first = looked_up(notes, AHEAD0)
+    norm_pieces([(between, 0, rows)], row_gain(layer), first - edge, length, masked, chunk=rows // 2)
 
     def block(columns):
-        q = tap_spectrum(q_table[...], received[own:, columns])
+        q = tap_spectrum(q_table[...], layer[:, columns])
         conv = transform(c_table, product(transform(m_table, masked[:, columns]), q))
         out[:, columns] = (between[edge : edge + own, columns].astype(F32) + conv * sigmoid(conv)).astype(BF16)
 
@@ -443,7 +443,7 @@
     notes[BACK1] = back_slot[1, section]
     notes[BACK1 + 1] = back_len[lax.rem(section + 1, sections)]
     notes[AHEAD0] = ahead_slot[0, section]
-    notes[AHEAD0 + 1] = ahead_len[section]
+    notes[AHEAD0 + 1] = ahead_len[lax.rem(section + sections - 2, sections)]
 
 
 def final_kernel(notes, mine, other, act, grad, act_out, grad_out, taps, gains, sems):
@@ -477,15 +477,15 @@
 FULL = 127 * 512 * 1024
 
 
-def call(kernel, outs, scratch, operands, micros, specs=None, out_specs=None, limit=LIMIT, after=None):
+def call(kernel, outs, scratch, operands, micros, specs=None, out_specs=None, limit=LIMIT, after=()):
     if specs is None:
         specs = [SMEM if x.dtype == jnp.int32 else VMEM for x in operands]
-    if after is not None:
-        operands, specs = [*operands, after], [*specs, ANY]
-        inner, place = kernel, len(operands) - 1
+    if after:
+        inner, place = kernel, len(operands)
+        operands, specs = [*operands, *after], [*specs, *[ANY] * len(after)]
 
         def kernel(*refs):
-            return inner(*refs[:place], *refs[place + 1 :])
+            return inner(*refs[:place], *refs[place + len(after) :])
 
     return pl.pallas_call(
         kernel,
@@ -535,6 +535,7 @@
             results.append(lax.ppermute(x, ("section", "tm"), pairs))
         return results[::-1]
 
+    act = shifted(act, 2)
     lengths = pltpu.SMEM(backward_lengths.shape, jnp.int32)
     forward_slots, backward_slots = forward_slots.T, backward_slots.T
     slots = pltpu.SMEM(backward_slots.shape, jnp.int32)
@@ -553,35 +554,40 @@
     go_table = beside(to_freq(size, np.arange(own)))
     t_table = stacked(tap_back)
 
-    def run(kernel, outs, scratch, operands, micros=0, after=None):
+    def run(kernel, outs, scratch, operands, micros=0, *after):
         return call(kernel, outs, scratch, [jnp.asarray(x) for x in operands], micros, after=after)
 
     rows = [pltpu.VMEM((own, width), F32)] + [pltpu.VMEM((own, LANES), F32)] * 2
     layer = like(own, width, BF16), like(own, LANES, F32), like(own, LANES, F32)
-    weights, later, near1, far1, *layer0 = run(
-        functools.partial(prepare_kernel, two),
+    weights, ahead0, ahead1, *layer0 = run(
+        prepare_kernel,
         (
             jax.ShapeDtypeStruct((kernels.shape[1], tap_count + 1, width), BF16), like(tap_count + 1, width, BF16),
-            like(2 * two, width, BF16), like(2 * two, width, BF16), *layer,
+            like(tap_count + 1, width, BF16), *layer,
         ),
         [],
-        [notes, kernels[0].transpose(1, 0, 2), norm_gains[0], saved, act],
+        [notes, kernels[0].transpose(1, 0, 2), norm_gains[0], saved],
         0,
     )
-    near1, far1 = swapped(near1, far1)
+    packed1 = run(
+        functools.partial(second_pack_kernel, two), (like(2 * two, width, BF16),) * 2, [], [saved, act], 0, weights
+    )
+    near1, far1 = swapped(*packed1)
+    ahead0, ahead1 = shifted(ahead0, 2), shifted(ahead1, 1)
     g_table, x_table = stacked(to_freq(size, span(one, own))), stacked(from_freq(size, span(0, own)))
     grad_mid, near2, far2, halo0, inner0, gain0 = run(
         functools.partial(first_backward_kernel, two),
         (
-            like(own + tap_count + 1, width, BF16), like(one, width, BF16), like(one, width, BF16),
+            like(own, width, BF16), like(one, width, BF16), like(one, width, BF16),
             like(2 * two, width, BF16), like(own, width, BF16), like(1, width, F32),
         ),
         [pltpu.VMEM((2, two, width), BF16), pltpu.VMEM((2, one, width), BF16), *rows],
         [
-            notes, saved, far0, near0, grad, weights, later, *layer0,
+            notes, saved, far0, near0, grad, weights, *layer0,
             m_table, q_table, c_table, g_table, x_table,
         ],
         4,
+        packed1[0], ahead0, ahead1,
     )
     grad_mid = shifted(grad_mid, -1)
     near2, far2 = swapped(near2, far2, -1)
@@ -593,25 +599,6 @@
     halo_scratch = [
         pltpu.VMEM((2 * two, width), BF16), pltpu.VMEM((2, two, width), BF16), pltpu.VMEM((own, width), BF16)
     ]
-    between = run(
-        functools.partial(first_forward_kernel, two),
-        like(small, width, BF16),
-        halo_scratch,
-        [notes, act, far1, near1, weights, m_table, q_table, c_table],
-        20,
-        taps0,
-    )
-    act_ahead = run(
-        second_forward_kernel,
-        like(own, width, BF16),
-        [pltpu.VMEM((small, width), BF16)],
-        [
-            notes, between, grad_mid,
-            stacked(to_freq(small, span(one, own))), tap_freq(small, tap_count), stacked(from_freq(small, span(0, own))),
-        ],
-        3,
-    )
-    act_out = shifted(act_ahead, 2)
     m1, q1, factor1, conv1, mean1, inverse1 = run(
         functools.partial(second_ready_kernel, two),
         (
@@ -619,11 +606,10 @@
             like(own, LANES, F32), like(own, LANES, F32),
         ),
         halo_scratch,
-        [notes, saved, far1, near1, weights, m_table, q_table, c_table],
-        3,
-        act_ahead,
-    )
-
+        [notes, saved, near1, far1, weights, m_table, q_table, c_table],
+        20,
+        taps0,
+    )
     def partner(x, step):
         return lax.ppermute(x, "tm", [(i, i ^ step) for i in range(shards)])
 
@@ -648,6 +634,24 @@
     grad_out = shifted(grad_out, -1)
     other1 = partner(taps1, 1)
     mine = call(below_kernel, like(2 * (tap_count + 1), width, BF16), [], (taps0, other0, taps1, other1), 6)
+    between = run(
+        functools.partial(first_forward_kernel, two),
+        like(small, width, BF16),
+        halo_scratch,
+        [notes, act, far1, near1, ahead0, m_table, q_table, c_table],
+        10,
+        mine,
+    )
+    act_out = run(
+        second_forward_kernel,
+        like(own, width, BF16),
+        [pltpu.VMEM((small, width), BF16)],
+        [
+            notes, between, ahead1,
+            stacked(to_freq(small, span(one, own))), tap_freq(small, tap_count), stacked(from_freq(small, span(0, own))),
+        ],
+        10,
+    )
     step = 2
     while True:
         other = partner(mine, step)

time: 58.6 us -> 56.2 us (0.959)
  the two profiles are of different devices: /device:TPU:1 before, /device:TPU:0 now
where the time goes in v12:
time: 56.2 us; the launch traced here: 55.9 us
  starting transfers between devices  27.2 us (48%)
  Pallas kernels  22.1 us (39%)
  waiting for transfers between devices  3.5 us (6%)
  local copies, waits for them, and re-layouts  1.96 us (3%)
  between operations  1.14 us (2%)
    pallas_call x12, Pallas kernels, call(): pl.pallas_call(kernel, out_shape=outs, in_specs=specs, out_specs=jax.tree...  22.1 us
    ppermute x6, starting transfers between devices, swapped(): results.append(lax.ppermute(x, ('section', 'tm'), pairs))  16.7 us
    ppermute x5, starting transfers between devices, shifted(): lax.ppermute(x, 'section', [(i, (i + by) % sections) for i in range(secti...  6.63 us
    ppermute x3, starting transfers between devices, partner(): return lax.ppermute(x, 'tm', [(i, i ^ step) for i in range(shards)])  3.85 us
    ppermute x5, waiting for transfers between devices, shifted(): lax.ppermute(x, 'section', [(i, (i + by) % sections) for i in range(secti...  2.55 us
    unnamed x34, local copies, waits for them, and re-layouts  1.96 us
  transfers between devices with their start and end apart: 14, of which 2 were waited for; matrix products, arithmetic and copies ran while one was open for 0% of the time, Pallas kernels for 35%

profile of v12, /device:TPU:0, one launch (start us, length us, event | category | flops | bytes accessed | tf_op | source)
XLA Modules:
  0.0 55.9 jit_solution(2191487326141509880)
XLA Ops:
  0.7 3.1 %collective-permute-start.2 = (bf16[128,2048]{1,0:T(8,128)(2,1)}, bf16[128,2048]{1,0:T(8,128)(2,1)}, u32[]{:S(2)}, u32[]{:S(2)}) collective-permute-start(bf16[128,2048]{1,0:T(8,128)(2,1)} %bitcast.26), channel_id=1, source_target_pairs={{0,8},{4,12},{8,16},{12,20},{16,24},{20,28},{24,0},{28,4},{1,9},{5... | collective-permute-start | bytes 1572872 | tf_op jit(solution)/shard_map/ppermute | solution.py:523
  3.7 1.8 %shard_map.210 = (bf16[48,2048]{1,0:T(8,128)(2,1)}, bf16[48,2048]{1,0:T(8,128)(2,1)}, s32[8]{0:T(128)}) custom-call(bf16[2,128,2048]{2,1,0:T(8,128)(2,1)} %bitcast.15, bf16[1,128,2048]{2,1,0:T(8,128)(2,1)} %grad.1, s32[8]{0:T(128)} %back_lengths.1, s32[8]{0:T(128)} %ahead_lengths.1, s32[2,8]{1,0:T(2,128)} %bitcast.24, s32[2,8]{1,0:T(2,128)} %bitcast.25), custom_call_target="tpu_custom_call" | custom-call | tf_op jit(solution)/shard_map/pallas_call | solution.py:490
  5.6 0.7 %collective-permute-start = (bf16[48,2048]{1,0:T(8,128)(2,1)}, bf16[48,2048]{1,0:T(8,128)(2,1)S(1)}, u32[]{:S(2)}, u32[]{:S(2)}) collective-permute-start(bf16[48,2048]{1,0:T(8,128)(2,1)} %get-tuple-element.34), channel_id=1, source_target_pairs={{1,2},{2,1},{5,6},{6,5},{9,10},{10,9},{13,14},{14,13},{17,18},{18,... | collective-permute-start | bytes 589832 | tf_op jit(solution)/shard_map/ppermute | solution.py:535
  6.2 4.3 %collective-permute-start.1 = (bf16[48,2048]{1,0:T(8,128)(2,1)}, bf16[48,2048]{1,0:T(8,128)(2,1)S(1)}, u32[]{:S(2)}, u32[]{:S(2)}) collective-permute-start(bf16[48,2048]{1,0:T(8,128)(2,1)} %get-tuple-element.35), channel_id=1, source_target_pairs={{0,1},{1,0},{2,3},{3,2},{4,5},{5,4},{6,7},{7,6},{8,9},{9,8},{10,11... | collective-permute-start | bytes 589832 | tf_op jit(solution)/shard_map/ppermute | solution.py:535
  10.5 1.2 %copy-done = bf16[1,2,128,2048]{3,2,1,0:T(8,128)(2,1)S(1)} copy-done((bf16[1,2,128,2048]{3,2,1,0:T(8,128)(2,1)S(1)}, bf16[1,2,128,2048]{3,2,1,0:T(8,128)(2,1)}, u32[]{:S(2)}) %copy-start) | copy-done | bytes 1048600
  11.8 0.7 %copy-done.8 = s32[8]{0:T(128)S(1)} copy-done((s32[8]{0:T(128)S(1)}, s32[8]{0:T(128)}, u32[]{:S(2)}) %copy-start.8) | copy-done | bytes 56
  12.4 0.0 copy-start.12
  12.4 0.0 copy-start.14
  12.4 0.0 copy-start.15
  12.5 1.6 %shard_map.211 = (bf16[2,32,2048]{2,1,0:T(8,128)(2,1)S(1)}, bf16[32,2048]{1,0:T(8,128)(2,1)S(1)}, bf16[32,2048]{1,0:T(8,128)(2,1)S(1)}, bf16[128,2048]{1,0:T(8,1...) custom-call(s32[8]{0:T(128)S(1)} %copy-done.8, bf16[31,2,2048]{2,1,0:T(2,128)(2,1)S(1)} %bitcast.22, ...), custom_call_target="tpu_custom_call" | custom-call | tf_op jit(solution)/shard_map/pallas_call | solution.py:490
  14.1 1.6 %collective-permute-start.3 = (bf16[32,2048]{1,0:T(8,128)(2,1)S(1)}, bf16[32,2048]{1,0:T(8,128)(2,1)S(1)}, u32[]{:S(2)}, u32[]{:S(2)}) collective-permute-start(bf16[32,2048]{1,0:T(8,128)(2,1)S(1)} %get-tuple-element.41), channel_id=1, source_target_pairs={{0,8},{4,12},{8,16},{12,20},{16,24},{20,28},{24,0},{28,4},{1,9},{5... | collective-permute-start | bytes 393224 | tf_op jit(solution)/shard_map/ppermute | solution.py:523
  15.7 2.5 %collective-permute-done.2.refs_1_ = bf16[128,2048]{1,0:T(8,128)(2,1)} collective-permute-done((bf16[128,2048]{1,0:T(8,128)(2,1)}, bf16[128,2048]{1,0:T(8,128)(2,1)}, u32[]{:S(2)}, u32[]{:S(2)}) %collective-permute-start.2) | collective-permute-done | bytes 524320 | tf_op jit(solution)/shard_map/ppermute | solution.py:523
  18.3 1.1 %shard_map.212 = (bf16[64,2048]{1,0:T(8,128)(2,1)S(1)}, bf16[64,2048]{1,0:T(8,128)(2,1)S(1)}) custom-call(bf16[2,128,2048]{2,1,0:T(8,128)(2,1)S(1)} %bitcast.17, bf16[128,2048]{1,0:T(8,128)(2,1)} %collective-permute-done.2.refs_1_, bf16[2,32,2048]{2,1,0:T(8,128)(2,1)S(1)} %get-tuple-element.36.refs_2_.refs_5_.refs_4_.weights), custom_call_target="tpu_custom_call" | custom-call | tf_op jit(solution)/shard_map/pallas_call | solution.py:490
  19.4 2.4 %collective-permute-start.9 = (bf16[64,2048]{1,0:T(8,128)(2,1)S(1)}, bf16[64,2048]{1,0:T(8,128)(2,1)S(1)}, u32[]{:S(2)}, u32[]{:S(2)}) collective-permute-start(bf16[64,2048]{1,0:T(8,128)(2,1)S(1)} %get-tuple-element.40.refs_14_), channel_id=1, source_target_pairs={{0,1},{1,0},{2,3},{3,2},{4,5},{5,4},{6,7},{7,6},{8,9},{9,8},{10,11... | collective-permute-start | bytes 786440 | tf_op jit(solution)/shard_map/ppermute | solution.py:535
  21.7 0.7 %collective-permute-start.10 = (bf16[64,2048]{1,0:T(8,128)(2,1)S(1)}, bf16[64,2048]{1,0:T(8,128)(2,1)S(1)}, u32[]{:S(2)}, u32[]{:S(2)}) collective-permute-start(bf16[64,2048]{1,0:T(8,128)(2,1)S(1)} %get-tuple-element.49), channel_id=1, source_target_pairs={{1,2},{2,1},{5,6},{6,5},{9,10},{10,9},{13,14},{14,13},{17,18},{18,... | collective-permute-start | bytes 786440 | tf_op jit(solution)/shard_map/ppermute | solution.py:535
  22.5 3.5 %shard_map.213 = (bf16[128,2048]{1,0:T(8,128)(2,1)S(1)}, bf16[16,2048]{1,0:T(8,128)(2,1)S(1)}, bf16[16,2048]{1,0:T(8,128)(2,1)S(1)}, bf16[64,2048]{1,0:T(8,128)(...) custom-call(s32[8]{0:T(128)S(1)} %copy-done.9, bf16[2,128,2048]{2,1,0:T(8,128)(2,1)S(1)} %bitcast.18, ...), custom_call_target="tpu_custom_call" | custom-call | flops 4000000000 | tf_op jit(solution)/shard_map/pallas_call | solution.py:490
  26.0 0.1 collective-permute-start.6
  26.1 0.8 %collective-permute-start.7 = (bf16[16,2048]{1,0:T(8,128)(2,1)S(1)}, bf16[16,2048]{1,0:T(8,128)(2,1)S(1)}, u32[]{:S(2)}, u32[]{:S(2)}) collective-permute-start(bf16[16,2048]{1,0:T(8,128)(2,1)S(1)} %get-tuple-element.47), channel_id=1, source_target_pairs={{1,30},{2,29},{5,2},{6,1},{9,6},{10,5},{13,10},{14,9},{17,14},{18,... | collective-permute-start | bytes 196616 | tf_op jit(solution)/shard_map/ppermute | solution.py:535
  26.9 8.0 %collective-permute-start.8 = (bf16[16,2048]{1,0:T(8,128)(2,1)S(1)}, bf16[16,2048]{1,0:T(8,128)(2,1)S(1)}, u32[]{:S(2)}, u32[]{:S(2)}) collective-permute-start(bf16[16,2048]{1,0:T(8,128)(2,1)S(1)} %get-tuple-element.48), channel_id=1, source_target_pairs={{0,29},{1,28},{2,31},{3,30},{4,1},{5,0},{6,3},{7,2},{8,5},{9,4},{1... | collective-permute-start | bytes 196616 | tf_op jit(solution)/shard_map/ppermute | solution.py:535
  34.9 1.0 %shard_map.214.refs_8_.mine0 = bf16[32,2048]{1,0:T(8,128)(2,1)S(1)} custom-call(bf16[64,2048]{1,0:T(8,128)(2,1)S(1)} %get-tuple-element.43.halo, bf16[128,2048]{1,0:T(8,128)(2,1)S(1)} %get-tuple-element.37.refs_6_.masked, bf16[128,2048]{1,0:T(8,128)(2,1)S(1)} %get-tuple-element.44.inner, f32[1,2048]{1,0:T(1,128)S(1)} %get-tuple-element.45.gain_sum, ...), custom_call_target="tpu_custom_call" | custom-call | tf_op jit(solution)/shard_map/pallas_call | solution.py:490
  35.9 0.3 collective-permute-start.5
  36.2 2.5 %shard_map.215 = (f32[192,2048]{1,0:T(8,128)S(1)}, f32[192,2048]{1,0:T(8,128)S(1)}, f32[160,2048]{1,0:T(8,128)S(1)}, f32[128,2048]{1,0:T(8,128)S(1)}, f32[128,128]{1,0:T(8,128)S(1)}, /*index=5*/f32[128,128]{1,0:T(8,128)S(1)}) custom-call(s32[8]{0:T(128)S(1)} %copy-done.9, bf16[2,128,2048]{2,1,0:T(8,128)(2,1)S(1)} %bitcast.19, ...), custom_call_target="tpu_custom_call" | custom-call | flops 20000000000 | tf_op jit(solution)/shard_map/pallas_call | solution.py:490
  38.8 1.4 %shard_map.216 = (bf16[160,2048]{1,0:T(8,128)(2,1)S(1)}, bf16[32,2048]{1,0:T(8,128)(2,1)S(1)}) custom-call(s32[8]{0:T(128)S(1)} %copy-done.9, bf16[128,2048]{1,0:T(8,128)(2,1)S(1)} %collective-permute-done.6.received, bf16[16,2048]{1,0:T(8,128)(2,1)S(1)} %collective-permute-done.7.far, bf16[16,2048]{1,0:T(8,128)(2,1)S(1)} %collective-permute-done.8.near, ...), custom_call_target="tpu_custom_call" | custom-call | flops 2000000000 | tf_op jit(solution)/shard_map/pallas_call | solution.py:490
  40.2 1.8 %collective-permute-start.11 = (bf16[32,2048]{1,0:T(8,128)(2,1)S(1)}, bf16[32,2048]{1,0:T(8,128)(2,1)S(1)}, u32[]{:S(2)}, u32[]{:S(2)}) collective-permute-start(bf16[32,2048]{1,0:T(8,128)(2,1)S(1)} %get-tuple-element.53.mine1), channel_id=1, source_target_pairs={{0,1},{1,0},{2,3},{3,2},{4,5},{5,4},{6,7},{7,6},{8,9},{9,8},{10,11... | collective-permute-start | bytes 393224 | tf_op jit(solution)/shard_map/ppermute | solution.py:614
  42.0 2.0 %shard_map.220 = bf16[128,2048]{1,0:T(8,128)(2,1)S(1)} custom-call(s32[8]{0:T(128)S(1)} %copy-done.9, bf16[2,128,2048]{2,1,0:T(8,128)(2,1)S(1)} %bitcast.20, bf16[128,2048]{1,0:T(8,128)(2,1)S(1)} %collective-permute-done.6.received, bf16[2,32,2048]{2,1,0:T(8,128)(2,1)S(1)} %get-tuple-element.36.refs_2_.refs_5_.refs_4_.weights, ...), custom_call_target="tpu_custom_call" | custom-call | flops 6000000000 | tf_op jit(solution)/shard_map/pallas_call | solution.py:490
  44.0 1.9 %collective-permute-start.13 = (bf16[128,2048]{1,0:T(8,128)(2,1)S(1)}, bf16[128,2048]{1,0:T(8,128)(2,1)S(1)}, u32[]{:S(2)}, u32[]{:S(2)}) collective-permute-start(bf16[128,2048]{1,0:T(8,128)(2,1)S(1)} %shard_map.220), channel_id=1, source_target_pairs={{0,28},{4,0},{8,4},{12,8},{16,12},{20,16},{24,20},{28,24},{1,29},{... | collective-permute-start | bytes 1572872 | tf_op jit(solution)/shard_map/ppermute | solution.py:523
  45.8 0.1 shard_map.217.refs_8_.mine
  45.9 1.7 %collective-permute-start.12 = (bf16[64,2048]{1,0:T(8,128)(2,1)S(1)}, bf16[64,2048]{1,0:T(8,128)(2,1)S(1)}, u32[]{:S(2)}, u32[]{:S(2)}) collective-permute-start(bf16[64,2048]{1,0:T(8,128)(2,1)S(1)} %shard_map.217.refs_8_.mine), channel_id=1, source_target_pairs={{0,2},{1,3},{2,0},{3,1},{4,6},{5,7},{6,4},{7,5},{8,10},{9,11},{10,... | collective-permute-start | bytes 786440 | tf_op jit(solution)/shard_map/ppermute | solution.py:614
  47.7 2.8 %shard_map.218.between = bf16[160,2048]{1,0:T(8,128)(2,1)S(1)} custom-call(s32[8]{0:T(128)S(1)} %copy-done.9, bf16[128,2048]{1,0:T(8,128)(2,1)} %collective-permute-done.2.refs_1_, bf16[64,2048]{1,0:T(8,128)(2,1)S(1)} %collective-permute-done.10.refs_3_.refs_2_, bf16[64,2048]{1,0:T(8,128)(2,1)S(1)} %collective-permute-done.9.refs_2_.refs_3_, ...), custom_call_target="tpu_custom_call" | custom-call | flops 10000000000 | tf_op jit(solution)/shard_map/pallas_call | solution.py:490
  50.5 2.0 %shard_map.219.act = bf16[128,2048]{1,0:T(8,128)(2,1)S(1)} custom-call(s32[8]{0:T(128)S(1)} %copy-done.9, bf16[160,2048]{1,0:T(8,128)(2,1)S(1)} %shard_map.218.between, bf16[32,2048]{1,0:T(8,128)(2,1)S(1)} %collective-permute-done.4.refs_16_.layer, bf16[320,160]{1,0:T(8,128)(2,1)S(1)} %copy-done.11, bf16[160,64]{1,0:T(8,128)(2,1)S(1)} %copy-done.16, ...), custom_call_target="tpu_custom_call" | custom-call | flops 10000000000 | tf_op jit(solution)/shard_map/pallas_call | solution.py:490
  52.5 0.9 %collective-permute-done.12.other = bf16[64,2048]{1,0:T(8,128)(2,1)S(1)} collective-permute-done((bf16[64,2048]{1,0:T(8,128)(2,1)S(1)}, bf16[64,2048]{1,0:T(8,128)(2,1)S(1)}, u32[]{:S(2)}, u32[]{:S(2)}) %collective-permute-start.12) | collective-permute-done | bytes 262176 | tf_op jit(solution)/shard_map/ppermute | solution.py:614
  53.4 2.3 %shard_map.221 = (bf16[128,2048]{1,0:T(8,128)(2,1)}, bf16[128,2048]{1,0:T(8,128)(2,1)}, f32[31,2,2048]{2,1,0:T(2,128)}, f32[2,2048]{1,0:T(2,128)}) custom-call(s32[8]{0:T(128)S(1)} %copy-done.9, bf16[64,2048]{1,0:T(8,128)(2,1)S(1)} %shard_map.217.refs_8_.mine, bf16[64,2048]{1,0:T(8,128)(2,1)S(1)} %collective-permute-done.12.other, ...), custom_call_target="tpu_custom_call" | custom-call | tf_op jit(solution)/shard_map/pallas_call | solution.py:490
  (42 shorter events, 0.1 us)
Async XLA Ops:
  0.6 9.9 %copy-start.3 = (bf16[1,2,31,2048]{3,1,2,0:T(2,128)(2,1)S(1)}, bf16[1,2,31,2048]{3,1,2,0:T(2,128)(2,1)}, u32[]{:S(2)}) copy-start(bf16[1,2,31,2048]{3,1,2,0:T(2,128)(2,1)} %param.22) | copy-start | bytes 761860
  0.6 9.9 %copy-start.7 = (bf16[1,2,2048]{2,1,0:T(2,128)(2,1)S(1)}, bf16[1,2,2048]{2,1,0:T(2,128)(2,1)}, u32[]{:S(2)}) copy-start(bf16[1,2,2048]{2,1,0:T(2,128)(2,1)} %param.23) | copy-start | bytes 24580
  0.7 17.6 %collective-permute-start.2 = (bf16[128,2048]{1,0:T(8,128)(2,1)}, bf16[128,2048]{1,0:T(8,128)(2,1)}, u32[]{:S(2)}, u32[]{:S(2)}) collective-permute-start(bf16[128,2048]{1,0:T(8,128)(2,1)} %bitcast.26), channel_id=1, source_target_pairs={{0,8},{4,12},{8,16},{12,20},{16,24},{20,28},{24,0},{28,4},{1,9},{5... | collective-permute-start | bytes 1572872 | tf_op jit(solution)/shard_map/ppermute | solution.py:523
  5.6 16.8 %collective-permute-start = (bf16[48,2048]{1,0:T(8,128)(2,1)}, bf16[48,2048]{1,0:T(8,128)(2,1)S(1)}, u32[]{:S(2)}, u32[]{:S(2)}) collective-permute-start(bf16[48,2048]{1,0:T(8,128)(2,1)} %get-tuple-element.34), channel_id=1, source_target_pairs={{1,2},{2,1},{5,6},{6,5},{9,10},{10,9},{13,14},{14,13},{17,18},{18,... | collective-permute-start | bytes 589832 | tf_op jit(solution)/shard_map/ppermute | solution.py:535
  6.2 16.2 %collective-permute-start.1 = (bf16[48,2048]{1,0:T(8,128)(2,1)}, bf16[48,2048]{1,0:T(8,128)(2,1)S(1)}, u32[]{:S(2)}, u32[]{:S(2)}) collective-permute-start(bf16[48,2048]{1,0:T(8,128)(2,1)} %get-tuple-element.35), channel_id=1, source_target_pairs={{0,1},{1,0},{2,3},{3,2},{4,5},{5,4},{6,7},{7,6},{8,9},{9,8},{10,11... | collective-permute-start | bytes 589832 | tf_op jit(solution)/shard_map/ppermute | solution.py:535
  10.5 1.2 %copy-start = (bf16[1,2,128,2048]{3,2,1,0:T(8,128)(2,1)S(1)}, bf16[1,2,128,2048]{3,2,1,0:T(8,128)(2,1)}, u32[]{:S(2)}) copy-start(bf16[1,2,128,2048]{3,2,1,0:T(8,128)(2,1)} %param.21) | copy-start | bytes 3145732
  11.8 0.7 %copy-start.8 = (s32[8]{0:T(128)S(1)}, s32[8]{0:T(128)}, u32[]{:S(2)}) copy-start(s32[8]{0:T(128)} %get-tuple-element.33.notes.refs_0_) | copy-start | bytes 100
  12.4 10.0 %copy-start.2 = (bf16[1,128,2048]{2,1,0:T(8,128)(2,1)S(1)}, bf16[1,128,2048]{2,1,0:T(8,128)(2,1)}, u32[]{:S(2)}) copy-start(bf16[1,128,2048]{2,1,0:T(8,128)(2,1)} %grad.1) | copy-start | bytes 1572868
  12.4 10.0 %copy-start.4 = (bf16[384,192]{1,0:T(8,128)(2,1)S(1)}, bf16[384,192]{1,0:T(8,128)(2,1)}, u32[]{:S(2)}) copy-start(bf16[384,192]{1,0:T(8,128)(2,1)} %constant.20.clone.refs_9_.m_table.refs_5_) | copy-start | bytes 442372
  12.4 10.0 %copy-start.9 = (s32[8]{0:T(128)S(1)}, s32[8]{0:T(128)}, u32[]{:S(2)}) copy-start(s32[8]{0:T(128)} %get-tuple-element.33.notes.refs_0_) | copy-start | bytes 100
  12.4 10.0 %copy-start.10 = (bf16[384,160]{1,0:T(8,128)(2,1)S(1)}, bf16[384,160]{1,0:T(8,128)(2,1)}, u32[]{:S(2)}) copy-start(bf16[384,160]{1,0:T(8,128)(2,1)} %constant.23.clone.refs_12_.g_table) | copy-start | bytes 368644
  12.4 10.0 %copy-start.12 = (bf16[320,192]{1,0:T(8,128)(2,1)S(1)}, bf16[320,192]{1,0:T(8,128)(2,1)}, u32[]{:S(2)}) copy-start(bf16[320,192]{1,0:T(8,128)(2,1)} %constant.22.clone.refs_11_.refs_7_) | copy-start | bytes 368644
  12.4 10.0 %copy-start.14 = (bf16[256,192]{1,0:T(8,128)(2,1)S(1)}, bf16[256,192]{1,0:T(8,128)(2,1)}, u32[]{:S(2)}) copy-start(bf16[256,192]{1,0:T(8,128)(2,1)} %constant.24.clone.refs_13_.x_table) | copy-start | bytes 294916
  12.4 10.0 %copy-start.15 = (bf16[192,64]{1,0:T(8,128)(2,1)S(1)}, bf16[192,64]{1,0:T(8,128)(2,1)}, u32[]{:S(2)}) copy-start(bf16[192,64]{1,0:T(8,128)(2,1)} %constant.21.clone.refs_10_.refs_6_) | copy-start | bytes 73732
  14.1 7.6 %collective-permute-start.3 = (bf16[32,2048]{1,0:T(8,128)(2,1)S(1)}, bf16[32,2048]{1,0:T(8,128)(2,1)S(1)}, u32[]{:S(2)}, u32[]{:S(2)}) collective-permute-start(bf16[32,2048]{1,0:T(8,128)(2,1)S(1)} %get-tuple-element.41), channel_id=1, source_target_pairs={{0,8},{4,12},{8,16},{12,20},{16,24},{20,28},{24,0},{28,4},{1,9},{5... | collective-permute-start | bytes 393224 | tf_op jit(solution)/shard_map/ppermute | solution.py:523
  15.7 6.7 %collective-permute-start.4 = (bf16[32,2048]{1,0:T(8,128)(2,1)S(1)}, bf16[32,2048]{1,0:T(8,128)(2,1)S(1)}, u32[]{:S(2)}, u32[]{:S(2)}) collective-permute-start(bf16[32,2048]{1,0:T(8,128)(2,1)S(1)} %get-tuple-element.42), channel_id=1, source_target_pairs={{0,4},{4,8},{8,12},{12,16},{16,20},{20,24},{24,28},{28,0},{1,5},{5... | collective-permute-start | bytes 393224 | tf_op jit(solution)/shard_map/ppermute | solution.py:523
  19.4 16.5 %collective-permute-start.9 = (bf16[64,2048]{1,0:T(8,128)(2,1)S(1)}, bf16[64,2048]{1,0:T(8,128)(2,1)S(1)}, u32[]{:S(2)}, u32[]{:S(2)}) collective-permute-start(bf16[64,2048]{1,0:T(8,128)(2,1)S(1)} %get-tuple-element.40.refs_14_), channel_id=1, source_target_pairs={{0,1},{1,0},{2,3},{3,2},{4,5},{5,4},{6,7},{7,6},{8,9},{9,8},{10,11... | collective-permute-start | bytes 786440 | tf_op jit(solution)/shard_map/ppermute | solution.py:535
  21.7 14.5 %collective-permute-start.10 = (bf16[64,2048]{1,0:T(8,128)(2,1)S(1)}, bf16[64,2048]{1,0:T(8,128)(2,1)S(1)}, u32[]{:S(2)}, u32[]{:S(2)}) collective-permute-start(bf16[64,2048]{1,0:T(8,128)(2,1)S(1)} %get-tuple-element.49), channel_id=1, source_target_pairs={{1,2},{2,1},{5,6},{6,5},{9,10},{10,9},{13,14},{14,13},{17,18},{18,... | collective-permute-start | bytes 786440 | tf_op jit(solution)/shard_map/ppermute | solution.py:535
  22.5 12.4 %copy-start.5 = (bf16[192,256]{1,0:T(8,128)(2,1)S(1)}, bf16[192,256]{1,0:T(8,128)(2,1)}, u32[]{:S(2)}) copy-start(bf16[192,256]{1,0:T(8,128)(2,1)} %constant.25.clone.go_table) | copy-start | bytes 294916
  22.5 12.4 %copy-start.6 = (bf16[64,192]{1,0:T(8,128)(2,1)S(1)}, bf16[64,192]{1,0:T(8,128)(2,1)}, u32[]{:S(2)}) copy-start(bf16[64,192]{1,0:T(8,128)(2,1)} %constant.26.clone.t_table) | copy-start | bytes 73732
  26.0 10.2 %copy-start.1 = (bf16[1,2,128,2048]{3,2,1,0:T(8,128)(2,1)S(1)}, bf16[1,2,128,2048]{3,2,1,0:T(8,128)(2,1)}, u32[]{:S(2)}) copy-start(bf16[1,2,128,2048]{3,2,1,0:T(8,128)(2,1)} %param.21) | copy-start | bytes 3145732
  26.0 12.7 %collective-permute-start.6 = (bf16[128,2048]{1,0:T(8,128)(2,1)S(1)}, bf16[128,2048]{1,0:T(8,128)(2,1)S(1)}, u32[]{:S(2)}, u32[]{:S(2)}) collective-permute-start(bf16[128,2048]{1,0:T(8,128)(2,1)S(1)} %get-tuple-element.46), channel_id=1, source_target_pairs={{0,28},{4,0},{8,4},{12,8},{16,12},{20,16},{24,20},{28,24},{1,29},{... | collective-permute-start | bytes 1572872 | tf_op jit(solution)/shard_map/ppermute | solution.py:523
  26.1 12.6 %collective-permute-start.7 = (bf16[16,2048]{1,0:T(8,128)(2,1)S(1)}, bf16[16,2048]{1,0:T(8,128)(2,1)S(1)}, u32[]{:S(2)}, u32[]{:S(2)}) collective-permute-start(bf16[16,2048]{1,0:T(8,128)(2,1)S(1)} %get-tuple-element.47), channel_id=1, source_target_pairs={{1,30},{2,29},{5,2},{6,1},{9,6},{10,5},{13,10},{14,9},{17,14},{18,... | collective-permute-start | bytes 196616 | tf_op jit(solution)/shard_map/ppermute | solution.py:535
  26.9 11.8 %collective-permute-start.8 = (bf16[16,2048]{1,0:T(8,128)(2,1)S(1)}, bf16[16,2048]{1,0:T(8,128)(2,1)S(1)}, u32[]{:S(2)}, u32[]{:S(2)}) collective-permute-start(bf16[16,2048]{1,0:T(8,128)(2,1)S(1)} %get-tuple-element.48), channel_id=1, source_target_pairs={{0,29},{1,28},{2,31},{3,30},{4,1},{5,0},{6,3},{7,2},{8,5},{9,4},{1... | collective-permute-start | bytes 196616 | tf_op jit(solution)/shard_map/ppermute | solution.py:535
  35.9 9.9 %collective-permute-start.5 = (bf16[32,2048]{1,0:T(8,128)(2,1)S(1)}, bf16[32,2048]{1,0:T(8,128)(2,1)S(1)}, u32[]{:S(2)}, u32[]{:S(2)}) collective-permute-start(bf16[32,2048]{1,0:T(8,128)(2,1)S(1)} %shard_map.214.refs_8_.mine0), channel_id=1, source_target_pairs={{0,1},{1,0},{2,3},{3,2},{4,5},{5,4},{6,7},{7,6},{8,9},{9,8},{10,11... | collective-permute-start | bytes 393224 | tf_op jit(solution)/shard_map/ppermute | solution.py:614
  40.2 5.7 %collective-permute-start.11 = (bf16[32,2048]{1,0:T(8,128)(2,1)S(1)}, bf16[32,2048]{1,0:T(8,128)(2,1)S(1)}, u32[]{:S(2)}, u32[]{:S(2)}) collective-permute-start(bf16[32,2048]{1,0:T(8,128)(2,1)S(1)} %get-tuple-element.53.mine1), channel_id=1, source_target_pairs={{0,1},{1,0},{2,3},{3,2},{4,5},{5,4},{6,7},{7,6},{8,9},{9,8},{10,11... | collective-permute-start | bytes 393224 | tf_op jit(solution)/shard_map/ppermute | solution.py:614
  44.0 9.4 %collective-permute-start.13 = (bf16[128,2048]{1,0:T(8,128)(2,1)S(1)}, bf16[128,2048]{1,0:T(8,128)(2,1)S(1)}, u32[]{:S(2)}, u32[]{:S(2)}) collective-permute-start(bf16[128,2048]{1,0:T(8,128)(2,1)S(1)} %shard_map.220), channel_id=1, source_target_pairs={{0,28},{4,0},{8,4},{12,8},{16,12},{20,16},{24,20},{28,24},{1,29},{... | collective-permute-start | bytes 1572872 | tf_op jit(solution)/shard_map/ppermute | solution.py:523
  45.9 4.6 %copy-start.11 = (bf16[320,160]{1,0:T(8,128)(2,1)S(1)}, bf16[320,160]{1,0:T(8,128)(2,1)}, u32[]{:S(2)}) copy-start(bf16[320,160]{1,0:T(8,128)(2,1)} %constant.27.clone.m_table) | copy-start | bytes 307204
  45.9 4.6 %copy-start.13 = (bf16[256,160]{1,0:T(8,128)(2,1)S(1)}, bf16[256,160]{1,0:T(8,128)(2,1)}, u32[]{:S(2)}) copy-start(bf16[256,160]{1,0:T(8,128)(2,1)} %constant.29.clone.c_table) | copy-start | bytes 245764
  45.9 4.6 %copy-start.16 = (bf16[160,64]{1,0:T(8,128)(2,1)S(1)}, bf16[160,64]{1,0:T(8,128)(2,1)}, u32[]{:S(2)}) copy-start(bf16[160,64]{1,0:T(8,128)(2,1)} %constant.28.clone.q_table) | copy-start | bytes 61444
  45.9 7.5 %collective-permute-start.12 = (bf16[64,2048]{1,0:T(8,128)(2,1)S(1)}, bf16[64,2048]{1,0:T(8,128)(2,1)S(1)}, u32[]{:S(2)}, u32[]{:S(2)}) collective-permute-start(bf16[64,2048]{1,0:T(8,128)(2,1)S(1)} %shard_map.217.refs_8_.mine), channel_id=1, source_target_pairs={{0,2},{1,3},{2,0},{3,1},{4,6},{5,7},{6,4},{7,5},{8,10},{9,11},{10,... | collective-permute-start | bytes 786440 | tf_op jit(solution)/shard_map/ppermute | solution.py:614

commit v13 on v12

--- a/solution.py
+++ b/solution.py
@@ -208,8 +208,19 @@
     return lambda columns: weights[slot, last : last + 1, columns].astype(F32)
 
 
-def prepare_kernel(notes, kernels, gains, saved, weights, ahead0, ahead1, masked, mean, inverse):
-    own = saved.shape[1]
+def prepare_kernel(
+    reach, notes, kernels, gains, saved, act, weights, ahead0, ahead1, near, far, masked, mean, inverse
+):
+    own = act.shape[0]
+    for even in range(2):
+
+        @pl.when(lax.rem(lax.axis_index("tm") + 1, 2) == even)
+        def _():
+            for x, at in ((saved.at[1], 0), (act, reach)):
+                tail, head = (near, far) if even else (far, near)
+                tail[pl.ds(at, reach), :] = x[pl.ds(own - reach, reach), :]
+                head[pl.ds(at, reach), :] = x[pl.ds(0, reach), :]
+
     count = kernels.shape[0]
     for slot in range(kernels.shape[1]):
         weights[slot, :count, :] = kernels[:, slot, :]
@@ -218,18 +229,6 @@
     ahead1[...] = weights[notes[FIRST + 1]]
     slot, length, first = looked_up(notes, BACK0)
     norm_pieces([(saved.at[0], 0, own)], slot_row(weights, slot), first, length, masked, mean, inverse)
-
-
-def second_pack_kernel(reach, saved, act, near, far):
-    own = act.shape[0]
-    for even in range(2):
-
-        @pl.when(lax.rem(lax.axis_index("tm") + 1, 2) == even)
-        def _():
-            for x, at in ((saved.at[1], 0), (act, reach)):
-                tail, head = (near, far) if even else (far, near)
-                tail[pl.ds(at, reach), :] = x[pl.ds(own - reach, reach), :]
-                head[pl.ds(at, reach), :] = x[pl.ds(0, reach), :]
 
 
 def norm_halo(left, right, own, gain, first, length, halo):
@@ -316,9 +315,13 @@
 
 
 def second_ready_kernel(
-    reach, notes, saved, near, far, weights, m_table, q_table, c_table,
-    m_out, q_out, factor, conv_out, mean, inverse, halo, halos, masked,
+    reach, notes, saved, far, near, weights, ahead0, m_table, q_table, c_table,
+    m_out, q_out, factor, conv_out, mean, inverse, ahead, halo, halos, masked,
 ):
+    left, right = sorted_halos(near, far, reach, halos)
+    ahead[pl.ds(0, reach), :] = left[...]
+    ahead[pl.ds(reach, reach), :] = right[...]
+    ahead[pl.ds(2 * reach, ahead0.shape[0]), :] = ahead0[...]
     own, width = masked.shape
     slot, length, first = looked_up(notes, BACK1)
     gain = slot_row(weights, slot)
@@ -384,11 +387,12 @@
     return lambda columns: layer[last : last + 1, columns].astype(F32)
 
 
-def first_forward_kernel(reach, notes, act, far, near, layer, m_table, q_table, c_table, out, halo, halos, masked):
+def first_forward_kernel(reach, notes, act, ahead, m_table, q_table, c_table, out, halo, masked):
     own, width = act.shape
     middle = reach // 2
     _, length, first = looked_up(notes, AHEAD0)
-    left, right = sorted_halos(near, far, reach, halos)
+    left, right = ahead.at[pl.ds(0, reach)], ahead.at[pl.ds(reach, reach)]
+    layer = ahead.at[pl.ds(2 * reach, ahead.shape[0] - 2 * reach)]
     inner = [(left, middle, middle), (act, 0, own), (right, 0, middle)]
     norm_pieces([(act, 0, own)], row_gain(layer), first, length, masked)
     norm_halo(left, right, own, row_gain(layer), first, length, halo)
@@ -535,7 +539,7 @@
             results.append(lax.ppermute(x, ("section", "tm"), pairs))
         return results[::-1]
 
-    act = shifted(act, 2)
+    act_ahead = shifted(act, 2)
     lengths = pltpu.SMEM(backward_lengths.shape, jnp.int32)
     forward_slots, backward_slots = forward_slots.T, backward_slots.T
     slots = pltpu.SMEM(backward_slots.shape, jnp.int32)
@@ -559,21 +563,18 @@
 
     rows = [pltpu.VMEM((own, width), F32)] + [pltpu.VMEM((own, LANES), F32)] * 2
     layer = like(own, width, BF16), like(own, LANES, F32), like(own, LANES, F32)
-    weights, ahead0, ahead1, *layer0 = run(
-        prepare_kernel,
+    weights, ahead0, ahead1, near1, far1, *layer0 = run(
+        functools.partial(prepare_kernel, two),
         (
             jax.ShapeDtypeStruct((kernels.shape[1], tap_count + 1, width), BF16), like(tap_count + 1, width, BF16),
-            like(tap_count + 1, width, BF16), *layer,
+            like(tap_count + 1, width, BF16), like(2 * two, width, BF16), like(2 * two, width, BF16), *layer,
         ),
         [],
-        [notes, kernels[0].transpose(1, 0, 2), norm_gains[0], saved],
+        [notes, kernels[0].transpose(1, 0, 2), norm_gains[0], saved, act],
         0,
     )
-    packed1 = run(
-        functools.partial(second_pack_kernel, two), (like(2 * two, width, BF16),) * 2, [], [saved, act], 0, weights
-    )
-    near1, far1 = swapped(*packed1)
-    ahead0, ahead1 = shifted(ahead0, 2), shifted(ahead1, 1)
+    near1, far1 = swapped(near1, far1)
+    ahead1 = shifted(ahead1, 1)
     g_table, x_table = stacked(to_freq(size, span(one, own))), stacked(from_freq(size, span(0, own)))
     grad_mid, near2, far2, halo0, inner0, gain0 = run(
         functools.partial(first_backward_kernel, two),
@@ -587,7 +588,7 @@
             m_table, q_table, c_table, g_table, x_table,
         ],
         4,
-        packed1[0], ahead0, ahead1,
+        act_ahead,
     )
     grad_mid = shifted(grad_mid, -1)
     near2, far2 = swapped(near2, far2, -1)
@@ -599,17 +600,18 @@
     halo_scratch = [
         pltpu.VMEM((2 * two, width), BF16), pltpu.VMEM((2, two, width), BF16), pltpu.VMEM((own, width), BF16)
     ]
-    m1, q1, factor1, conv1, mean1, inverse1 = run(
+    m1, q1, factor1, conv1, mean1, inverse1, ahead0 = run(
         functools.partial(second_ready_kernel, two),
         (
             like(size, width, F32), like(size, width, F32), like(small, width, F32), like(own, width, F32),
-            like(own, LANES, F32), like(own, LANES, F32),
+            like(own, LANES, F32), like(own, LANES, F32), like(2 * two + tap_count + 1, width, BF16),
         ),
         halo_scratch,
-        [notes, saved, near1, far1, weights, m_table, q_table, c_table],
-        20,
-        taps0,
-    )
+        [notes, saved, far1, near1, weights, ahead0, m_table, q_table, c_table],
+        5,
+        taps0, near2, far2,
+    )
+    ahead0 = shifted(ahead0, 2)
     def partner(x, step):
         return lax.ppermute(x, "tm", [(i, i ^ step) for i in range(shards)])
 
@@ -637,8 +639,8 @@
     between = run(
         functools.partial(first_forward_kernel, two),
         like(small, width, BF16),
-        halo_scratch,
-        [notes, act, far1, near1, ahead0, m_table, q_table, c_table],
+        [pltpu.VMEM((2 * two, width), BF16), pltpu.VMEM((own, width), BF16)],
+        [notes, act_ahead, ahead0, m_table, q_table, c_table],
         10,
         mine,
     )

time: 56.2 us -> 55.9 us (level)
  starting transfers between devices: 27.2 us -> 24.4 us
  waiting for transfers between devices: 3.5 us -> 5.93 us
  local copies, waits for them, and re-layouts: 1.96 us -> 3 us
  Pallas kernels: 22.1 us -> 21.1 us
    ppermute x6, waiting for transfers between devices: 0.02 us -> 4.75 us  [swapped(): results.append(lax.ppermute(x, ('section', 'tm'), pairs))]
    ppermute x6, starting transfers between devices: 16.7 us -> 13.1 us  [swapped(): results.append(lax.ppermute(x, ('section', 'tm'), pairs))]
    ppermute x5, starting transfers between devices: 6.63 us -> 8.81 us  [shifted(): lax.ppermute(x, 'section', [(i, (i + by) % sections) for i in range(secti...]
    ppermute x5, waiting for transfers between devices: 2.55 us -> 1.17 us  [shifted(): lax.ppermute(x, 'section', [(i, (i + by) % sections) for i in range(secti...]
    ppermute x3, starting transfers between devices: 3.85 us -> 2.52 us  [partner(): return lax.ppermute(x, 'tm', [(i, i ^ step) for i in range(shards)])]
    unnamed x34 -> x36, local copies, waits for them, and re-layouts: 1.96 us -> 3 us
    pallas_call x12 -> x11, Pallas kernels: 22.1 us -> 21.1 us  [call(): pl.pallas_call(kernel, out_shape=outs, in_specs=specs, out_specs=jax.tree...]
    ppermute x3, waiting for transfers between devices: 0.93 us -> 0.01 us  [partner(): return lax.ppermute(x, 'tm', [(i, i ^ step) for i in range(shards)])]
  transfers between devices with their start and end apart: 14 -> 14, of which waited for: 2 -> 4; matrix products, arithmetic and copies ran while one was open for 0% -> 0% of each run, Pallas kernels for 35% -> 34%
where the time goes in v13:
time: 55.9 us; the launch traced here: 55.5 us
  starting transfers between devices  24.4 us (44%)
  Pallas kernels  21.1 us (38%)
  waiting for transfers between devices  5.93 us (11%)
  local copies, waits for them, and re-layouts  3 us (5%)
  between operations  1.09 us (2%)
    pallas_call x11, Pallas kernels, call(): pl.pallas_call(kernel, out_shape=outs, in_specs=specs, out_specs=jax.tree...  21.1 us
    ppermute x6, starting transfers between devices, swapped(): results.append(lax.ppermute(x, ('section', 'tm'), pairs))  13.1 us
    ppermute x5, starting transfers between devices, shifted(): lax.ppermute(x, 'section', [(i, (i + by) % sections) for i in range(secti...  8.81 us
    ppermute x6, waiting for transfers between devices, swapped(): results.append(lax.ppermute(x, ('section', 'tm'), pairs))  4.75 us
    unnamed x36, local copies, waits for them, and re-layouts  3 us
    ppermute x3, starting transfers between devices, partner(): return lax.ppermute(x, 'tm', [(i, i ^ step) for i in range(shards)])  2.52 us
    ppermute x5, waiting for transfers between devices, shifted(): lax.ppermute(x, 'section', [(i, (i + by) % sections) for i in range(secti...  1.17 us
  transfers between devices with their start and end apart: 14, of which 4 were waited for; matrix products, arithmetic and copies ran while one was open for 0% of the time, Pallas kernels for 34%

profile of v13, /device:TPU:0, one launch (start us, length us, event | category | flops | bytes accessed | tf_op | source)
XLA Modules:
  0.0 55.5 jit_solution(4764089990510956532)
XLA Ops:
  0.7 3.1 %collective-permute-start.2 = (bf16[128,2048]{1,0:T(8,128)(2,1)}, bf16[128,2048]{1,0:T(8,128)(2,1)}, u32[]{:S(2)}, u32[]{:S(2)}) collective-permute-start(bf16[128,2048]{1,0:T(8,128)(2,1)} %bitcast.21), channel_id=1, source_target_pairs={{0,8},{4,12},{8,16},{12,20},{16,24},{20,28},{24,0},{28,4},{1,9},{5... | collective-permute-start | bytes 1572872 | tf_op jit(solution)/shard_map/ppermute | solution.py:527
  3.7 1.9 %shard_map.210 = (bf16[48,2048]{1,0:T(8,128)(2,1)}, bf16[48,2048]{1,0:T(8,128)(2,1)}, s32[8]{0:T(128)}) custom-call(bf16[2,128,2048]{2,1,0:T(8,128)(2,1)} %bitcast.15, bf16[1,128,2048]{2,1,0:T(8,128)(2,1)} %grad.1, s32[8]{0:T(128)} %back_lengths.1, s32[8]{0:T(128)} %ahead_lengths.1, s32[2,8]{1,0:T(2,128)} %bitcast.25, s32[2,8]{1,0:T(2,128)} %bitcast.26), custom_call_target="tpu_custom_call" | custom-call | tf_op jit(solution)/shard_map/pallas_call | solution.py:494
  5.6 0.7 %collective-permute-start = (bf16[48,2048]{1,0:T(8,128)(2,1)}, bf16[48,2048]{1,0:T(8,128)(2,1)S(1)}, u32[]{:S(2)}, u32[]{:S(2)}) collective-permute-start(bf16[48,2048]{1,0:T(8,128)(2,1)} %get-tuple-element.35), channel_id=1, source_target_pairs={{1,2},{2,1},{5,6},{6,5},{9,10},{10,9},{13,14},{14,13},{17,18},{18,... | collective-permute-start | bytes 589832 | tf_op jit(solution)/shard_map/ppermute | solution.py:539
  6.3 4.3 %collective-permute-start.1 = (bf16[48,2048]{1,0:T(8,128)(2,1)}, bf16[48,2048]{1,0:T(8,128)(2,1)S(1)}, u32[]{:S(2)}, u32[]{:S(2)}) collective-permute-start(bf16[48,2048]{1,0:T(8,128)(2,1)} %get-tuple-element.36), channel_id=1, source_target_pairs={{0,1},{1,0},{2,3},{3,2},{4,5},{5,4},{6,7},{7,6},{8,9},{9,8},{10,11... | collective-permute-start | bytes 589832 | tf_op jit(solution)/shard_map/ppermute | solution.py:539
  10.6 1.2 %copy-done = bf16[1,2,128,2048]{3,2,1,0:T(8,128)(2,1)S(1)} copy-done((bf16[1,2,128,2048]{3,2,1,0:T(8,128)(2,1)S(1)}, bf16[1,2,128,2048]{3,2,1,0:T(8,128)(2,1)}, u32[]{:S(2)}) %copy-start) | copy-done | bytes 1048600
  11.8 1.0 %copy-done.3 = bf16[1,128,2048]{2,1,0:T(8,128)(2,1)S(1)} copy-done((bf16[1,128,2048]{2,1,0:T(8,128)(2,1)S(1)}, bf16[1,128,2048]{2,1,0:T(8,128)(2,1)}, u32[]{:S(2)}) %copy-start.3) | copy-done | bytes 524312
  12.8 0.7 %copy-done.9 = s32[8]{0:T(128)S(1)} copy-done((s32[8]{0:T(128)S(1)}, s32[8]{0:T(128)}, u32[]{:S(2)}) %copy-start.9) | copy-done | bytes 56
  13.5 0.0 copy-start.16
  13.5 1.7 %shard_map.211 = (bf16[2,32,2048]{2,1,0:T(8,128)(2,1)S(1)}, bf16[32,2048]{1,0:T(8,128)(2,1)S(1)}, bf16[32,2048]{1,0:T(8,128)(2,1)S(1)}, bf16[64,2048]{1,0:T(8,12...) custom-call(s32[8]{0:T(128)S(1)} %copy-done.9, ...), custom_call_target="tpu_custom_call" | custom-call | tf_op jit(solution)/shard_map/pallas_call | solution.py:494
  15.2 0.7 %collective-permute-start.7 = (bf16[64,2048]{1,0:T(8,128)(2,1)S(1)}, bf16[64,2048]{1,0:T(8,128)(2,1)S(1)}, u32[]{:S(2)}, u32[]{:S(2)}) collective-permute-start(bf16[64,2048]{1,0:T(8,128)(2,1)S(1)} %get-tuple-element.47), channel_id=1, source_target_pairs={{1,2},{2,1},{5,6},{6,5},{9,10},{10,9},{13,14},{14,13},{17,18},{18,... | collective-permute-start | bytes 786440 | tf_op jit(solution)/shard_map/ppermute | solution.py:539
  15.9 2.8 %collective-permute-start.8 = (bf16[64,2048]{1,0:T(8,128)(2,1)S(1)}, bf16[64,2048]{1,0:T(8,128)(2,1)S(1)}, u32[]{:S(2)}, u32[]{:S(2)}) collective-permute-start(bf16[64,2048]{1,0:T(8,128)(2,1)S(1)} %get-tuple-element.48), channel_id=1, source_target_pairs={{0,1},{1,0},{2,3},{3,2},{4,5},{5,4},{6,7},{7,6},{8,9},{9,8},{10,11... | collective-permute-start | bytes 786440 | tf_op jit(solution)/shard_map/ppermute | solution.py:539
  18.7 1.3 %collective-permute-done.1.refs_3_ = bf16[48,2048]{1,0:T(8,128)(2,1)S(1)} collective-permute-done((bf16[48,2048]{1,0:T(8,128)(2,1)}, bf16[48,2048]{1,0:T(8,128)(2,1)S(1)}, u32[]{:S(2)}, u32[]{:S(2)}) %collective-permute-start.1) | collective-permute-done | bytes 196640 | tf_op jit(solution)/shard_map/ppermute | solution.py:539
  20.1 0.0 copy-start.6
  20.1 3.5 %shard_map.212 = (bf16[128,2048]{1,0:T(8,128)(2,1)S(1)}, bf16[16,2048]{1,0:T(8,128)(2,1)S(1)}, bf16[16,2048]{1,0:T(8,128)(2,1)S(1)}, bf16[64,2048]{1,0:T(8,128)(...) custom-call(s32[8]{0:T(128)S(1)} %copy-done.10, bf16[2,128,2048]{2,1,0:T(8,128)(2,1)S(1)} %bitcast.17, ...), custom_call_target="tpu_custom_call" | custom-call | flops 4000000000 | tf_op jit(solution)/shard_map/pallas_call | solution.py:494
  23.6 0.8 %collective-permute-start.5 = (bf16[16,2048]{1,0:T(8,128)(2,1)S(1)}, bf16[16,2048]{1,0:T(8,128)(2,1)S(1)}, u32[]{:S(2)}, u32[]{:S(2)}) collective-permute-start(bf16[16,2048]{1,0:T(8,128)(2,1)S(1)} %get-tuple-element.45), channel_id=1, source_target_pairs={{1,30},{2,29},{5,2},{6,1},{9,6},{10,5},{13,10},{14,9},{17,14},{18,... | collective-permute-start | bytes 196616 | tf_op jit(solution)/shard_map/ppermute | solution.py:539
  24.4 3.9 %collective-permute-start.6 = (bf16[16,2048]{1,0:T(8,128)(2,1)S(1)}, bf16[16,2048]{1,0:T(8,128)(2,1)S(1)}, u32[]{:S(2)}, u32[]{:S(2)}) collective-permute-start(bf16[16,2048]{1,0:T(8,128)(2,1)S(1)} %get-tuple-element.46), channel_id=1, source_target_pairs={{0,29},{1,28},{2,31},{3,30},{4,1},{5,0},{6,3},{7,2},{8,5},{9,4},{1... | collective-permute-start | bytes 196616 | tf_op jit(solution)/shard_map/ppermute | solution.py:539
  28.3 1.0 %shard_map.213.refs_9_.mine0 = bf16[32,2048]{1,0:T(8,128)(2,1)S(1)} custom-call(bf16[64,2048]{1,0:T(8,128)(2,1)S(1)} %get-tuple-element.41.halo, bf16[128,2048]{1,0:T(8,128)(2,1)S(1)} %get-tuple-element.38.refs_6_.masked, bf16[128,2048]{1,0:T(8,128)(2,1)S(1)} %get-tuple-element.42.inner, f32[1,2048]{1,0:T(1,128)S(1)} %get-tuple-element.43.gain_sum, ...), custom_call_target="tpu_custom_call" | custom-call | tf_op jit(solution)/shard_map/pallas_call | solution.py:494
  29.3 0.6 %collective-permute-start.12 = (bf16[32,2048]{1,0:T(8,128)(2,1)S(1)}, bf16[32,2048]{1,0:T(8,128)(2,1)S(1)}, u32[]{:S(2)}, u32[]{:S(2)}) collective-permute-start(bf16[32,2048]{1,0:T(8,128)(2,1)S(1)} %get-tuple-element.55), channel_id=1, source_target_pairs={{0,4},{4,8},{8,12},{12,16},{16,20},{20,24},{24,28},{28,0},{1,5},{5... | collective-permute-start | bytes 393224 | tf_op jit(solution)/shard_map/ppermute | solution.py:527
  29.9 3.0 %collective-permute-done.8.refs_3_ = bf16[64,2048]{1,0:T(8,128)(2,1)S(1)} collective-permute-done((bf16[64,2048]{1,0:T(8,128)(2,1)S(1)}, bf16[64,2048]{1,0:T(8,128)(2,1)S(1)}, u32[]{:S(2)}, u32[]{:S(2)}) %collective-permute-start.8) | collective-permute-done | bytes 262176 | tf_op jit(solution)/shard_map/ppermute | solution.py:539
  32.8 0.5 collective-permute-done.6.refs_10_.near
  33.3 2.6 %shard_map.214 = (f32[192,2048]{1,0:T(8,128)S(1)}, f32[192,2048]{1,0:T(8,128)S(1)}, f32[160,2048]{1,0:T(8,128)S(1)}, f32[128,2048]{1,0:T(8,128)S(1)}, f32[128,12...) custom-call(s32[8]{0:T(128)S(1)} %copy-done.10, bf16[2,128,2048]{2,1,0:T(8,128)(2,1)S(1)} %bitcast.18, ...), custom_call_target="tpu_custom_call" | custom-call | flops 5000000000 | tf_op jit(solution)/shard_map/pallas_call | solution.py:494
  35.9 1.6 %collective-permute-start.11 = (bf16[96,2048]{1,0:T(8,128)(2,1)S(1)}, bf16[96,2048]{1,0:T(8,128)(2,1)S(1)}, u32[]{:S(2)}, u32[]{:S(2)}) collective-permute-start(bf16[96,2048]{1,0:T(8,128)(2,1)S(1)} %get-tuple-element.54), channel_id=1, source_target_pairs={{0,8},{4,12},{8,16},{12,20},{16,24},{20,28},{24,0},{28,4},{1,9},{5... | collective-permute-start | bytes 1179656 | tf_op jit(solution)/shard_map/ppermute | solution.py:527
  37.5 1.2 %collective-permute-done.4.received = bf16[128,2048]{1,0:T(8,128)(2,1)S(1)} collective-permute-done((bf16[128,2048]{1,0:T(8,128)(2,1)S(1)}, bf16[128,2048]{1,0:T(8,128)(2,1)S(1)}, u32[]{:S(2)}, u32[]{:S(2)}) %collective-permute-start.4) | collective-permute-done | bytes 524320 | tf_op jit(solution)/shard_map/ppermute | solution.py:527
  38.7 1.4 %shard_map.215 = (bf16[160,2048]{1,0:T(8,128)(2,1)S(1)}, bf16[32,2048]{1,0:T(8,128)(2,1)S(1)}) custom-call(s32[8]{0:T(128)S(1)} %copy-done.10, bf16[128,2048]{1,0:T(8,128)(2,1)S(1)} %collective-permute-done.4.received, bf16[16,2048]{1,0:T(8,128)(2,1)S(1)} %collective-permute-done.5.refs_11_.far, bf16[16,2048]{1,0:T(8,128)(2,1)S(1)} %collective-permute-done.6.refs_10_.near, ...), custom_call_target="tpu_custom_call" | custom-call | flops 2000000000 | tf_op jit(solution)/shard_map/pallas_call | solution.py:494
  40.1 0.5 collective-permute-start.9
  40.5 2.0 %shard_map.219 = bf16[128,2048]{1,0:T(8,128)(2,1)S(1)} custom-call(s32[8]{0:T(128)S(1)} %copy-done.10, bf16[2,128,2048]{2,1,0:T(8,128)(2,1)S(1)} %bitcast.19, bf16[128,2048]{1,0:T(8,128)(2,1)S(1)} %collective-permute-done.4.received, bf16[2,32,2048]{2,1,0:T(8,128)(2,1)S(1)} %get-tuple-element.37.refs_5_.refs_4_.weights, ...), custom_call_target="tpu_custom_call" | custom-call | flops 6000000000 | tf_op jit(solution)/shard_map/pallas_call | solution.py:494
  42.5 3.5 %collective-permute-start.13 = (bf16[128,2048]{1,0:T(8,128)(2,1)S(1)}, bf16[128,2048]{1,0:T(8,128)(2,1)S(1)}, u32[]{:S(2)}, u32[]{:S(2)}) collective-permute-start(bf16[128,2048]{1,0:T(8,128)(2,1)S(1)} %shard_map.219), channel_id=1, source_target_pairs={{0,28},{4,0},{8,4},{12,8},{16,12},{20,16},{24,20},{28,24},{1,29},{... | collective-permute-start | bytes 1572872 | tf_op jit(solution)/shard_map/ppermute | solution.py:527
  46.1 0.1 shard_map.216.refs_6_.mine
  46.2 2.1 %collective-permute-start.10 = (bf16[64,2048]{1,0:T(8,128)(2,1)S(1)}, bf16[64,2048]{1,0:T(8,128)(2,1)S(1)}, u32[]{:S(2)}, u32[]{:S(2)}) collective-permute-start(bf16[64,2048]{1,0:T(8,128)(2,1)S(1)} %shard_map.216.refs_6_.mine), channel_id=1, source_target_pairs={{0,2},{1,3},{2,0},{3,1},{4,6},{5,7},{6,4},{7,5},{8,10},{9,11},{10,... | collective-permute-start | bytes 786440 | tf_op jit(solution)/shard_map/ppermute | solution.py:616
  48.2 2.8 %shard_map.217.between = bf16[160,2048]{1,0:T(8,128)(2,1)S(1)} custom-call(s32[8]{0:T(128)S(1)} %copy-done.10, bf16[128,2048]{1,0:T(8,128)(2,1)} %collective-permute-done.2.refs_14_.refs_1_, bf16[96,2048]{1,0:T(8,128)(2,1)S(1)} %collective-permute-done.11.refs_2_, bf16[384,192]{1,0:T(8,128)(2,1)S(1)} %copy-done.5, bf16[192,64]{1,0:T(8,128)(2,1)S(1)} %copy-done.16, ...), custom_call_target="tpu_custom_call" | custom-call | flops 10000000000 | tf_op jit(solution)/shard_map/pallas_call | solution.py:494
  51.1 2.0 %shard_map.218.act = bf16[128,2048]{1,0:T(8,128)(2,1)S(1)} custom-call(s32[8]{0:T(128)S(1)} %copy-done.10, bf16[160,2048]{1,0:T(8,128)(2,1)S(1)} %shard_map.217.between, bf16[32,2048]{1,0:T(8,128)(2,1)S(1)} %collective-permute-done.12.layer, bf16[320,160]{1,0:T(8,128)(2,1)S(1)} %copy-done.12, bf16[160,64]{1,0:T(8,128)(2,1)S(1)} %copy-done.17, ...), custom_call_target="tpu_custom_call" | custom-call | flops 10000000000 | tf_op jit(solution)/shard_map/pallas_call | solution.py:494
  53.1 2.3 %shard_map.220 = (bf16[128,2048]{1,0:T(8,128)(2,1)}, bf16[128,2048]{1,0:T(8,128)(2,1)}, f32[31,2,2048]{2,1,0:T(2,128)}, f32[2,2048]{1,0:T(2,128)}) custom-call(s32[8]{0:T(128)S(1)} %copy-done.10, bf16[64,2048]{1,0:T(8,128)(2,1)S(1)} %shard_map.216.refs_6_.mine, bf16[64,2048]{1,0:T(8,128)(2,1)S(1)} %collective-permute-done.10.other, ...), custom_call_target="tpu_custom_call" | custom-call | tf_op jit(solution)/shard_map/pallas_call | solution.py:494
  (43 shorter events, 0.1 us)
Async XLA Ops:
  0.6 9.9 %copy-start.4 = (bf16[1,2,31,2048]{3,1,2,0:T(2,128)(2,1)S(1)}, bf16[1,2,31,2048]{3,1,2,0:T(2,128)(2,1)}, u32[]{:S(2)}) copy-start(bf16[1,2,31,2048]{3,1,2,0:T(2,128)(2,1)} %param.22) | copy-start | bytes 761860
  0.6 9.9 %copy-start.8 = (bf16[1,2,2048]{2,1,0:T(2,128)(2,1)S(1)}, bf16[1,2,2048]{2,1,0:T(2,128)(2,1)}, u32[]{:S(2)}) copy-start(bf16[1,2,2048]{2,1,0:T(2,128)(2,1)} %param.23) | copy-start | bytes 24580
  0.7 19.3 %collective-permute-start.2 = (bf16[128,2048]{1,0:T(8,128)(2,1)}, bf16[128,2048]{1,0:T(8,128)(2,1)}, u32[]{:S(2)}, u32[]{:S(2)}) collective-permute-start(bf16[128,2048]{1,0:T(8,128)(2,1)} %bitcast.21), channel_id=1, source_target_pairs={{0,8},{4,12},{8,16},{12,20},{16,24},{20,28},{24,0},{28,4},{1,9},{5... | collective-permute-start | bytes 1572872 | tf_op jit(solution)/shard_map/ppermute | solution.py:527
  3.7 16.3 %copy-start.5 = (bf16[384,192]{1,0:T(8,128)(2,1)S(1)}, bf16[384,192]{1,0:T(8,128)(2,1)}, u32[]{:S(2)}) copy-start(bf16[384,192]{1,0:T(8,128)(2,1)} %constant.20.clone.refs_9_.m_table.refs_6_.refs_3_) | copy-start | bytes 442372
  5.6 14.4 %copy-start.10 = (s32[8]{0:T(128)S(1)}, s32[8]{0:T(128)}, u32[]{:S(2)}) copy-start(s32[8]{0:T(128)} %get-tuple-element.34.notes.refs_0_) | copy-start | bytes 100
  5.6 13.1 %collective-permute-start = (bf16[48,2048]{1,0:T(8,128)(2,1)}, bf16[48,2048]{1,0:T(8,128)(2,1)S(1)}, u32[]{:S(2)}, u32[]{:S(2)}) collective-permute-start(bf16[48,2048]{1,0:T(8,128)(2,1)} %get-tuple-element.35), channel_id=1, source_target_pairs={{1,2},{2,1},{5,6},{6,5},{9,10},{10,9},{13,14},{14,13},{17,18},{18,... | collective-permute-start | bytes 589832 | tf_op jit(solution)/shard_map/ppermute | solution.py:539
  6.3 13.7 %collective-permute-start.1 = (bf16[48,2048]{1,0:T(8,128)(2,1)}, bf16[48,2048]{1,0:T(8,128)(2,1)S(1)}, u32[]{:S(2)}, u32[]{:S(2)}) collective-permute-start(bf16[48,2048]{1,0:T(8,128)(2,1)} %get-tuple-element.36), channel_id=1, source_target_pairs={{0,1},{1,0},{2,3},{3,2},{4,5},{5,4},{6,7},{7,6},{8,9},{9,8},{10,11... | collective-permute-start | bytes 589832 | tf_op jit(solution)/shard_map/ppermute | solution.py:539
  10.6 1.2 %copy-start = (bf16[1,2,128,2048]{3,2,1,0:T(8,128)(2,1)S(1)}, bf16[1,2,128,2048]{3,2,1,0:T(8,128)(2,1)}, u32[]{:S(2)}) copy-start(bf16[1,2,128,2048]{3,2,1,0:T(8,128)(2,1)} %param.21) | copy-start | bytes 3145732
  11.8 1.0 %copy-start.3 = (bf16[1,128,2048]{2,1,0:T(8,128)(2,1)S(1)}, bf16[1,128,2048]{2,1,0:T(8,128)(2,1)}, u32[]{:S(2)}) copy-start(bf16[1,128,2048]{2,1,0:T(8,128)(2,1)} %param.19) | copy-start | bytes 1572868
  12.8 0.7 %copy-start.9 = (s32[8]{0:T(128)S(1)}, s32[8]{0:T(128)}, u32[]{:S(2)}) copy-start(s32[8]{0:T(128)} %get-tuple-element.34.notes.refs_0_) | copy-start | bytes 100
  13.5 6.5 %copy-start.2 = (bf16[1,128,2048]{2,1,0:T(8,128)(2,1)S(1)}, bf16[1,128,2048]{2,1,0:T(8,128)(2,1)}, u32[]{:S(2)}) copy-start(bf16[1,128,2048]{2,1,0:T(8,128)(2,1)} %grad.1) | copy-start | bytes 1572868
  13.5 6.5 %copy-start.11 = (bf16[384,160]{1,0:T(8,128)(2,1)S(1)}, bf16[384,160]{1,0:T(8,128)(2,1)}, u32[]{:S(2)}) copy-start(bf16[384,160]{1,0:T(8,128)(2,1)} %constant.23.clone.refs_12_.g_table) | copy-start | bytes 368644
  13.5 6.5 %copy-start.13 = (bf16[320,192]{1,0:T(8,128)(2,1)S(1)}, bf16[320,192]{1,0:T(8,128)(2,1)}, u32[]{:S(2)}) copy-start(bf16[320,192]{1,0:T(8,128)(2,1)} %constant.22.clone.refs_11_.refs_8_.refs_5_) | copy-start | bytes 368644
  13.5 6.5 %copy-start.15 = (bf16[256,192]{1,0:T(8,128)(2,1)S(1)}, bf16[256,192]{1,0:T(8,128)(2,1)}, u32[]{:S(2)}) copy-start(bf16[256,192]{1,0:T(8,128)(2,1)} %constant.24.clone.refs_13_.x_table) | copy-start | bytes 294916
  13.5 6.5 %copy-start.16 = (bf16[192,64]{1,0:T(8,128)(2,1)S(1)}, bf16[192,64]{1,0:T(8,128)(2,1)}, u32[]{:S(2)}) copy-start(bf16[192,64]{1,0:T(8,128)(2,1)} %constant.21.clone.refs_10_.refs_7_.refs_4_) | copy-start | bytes 73732
  15.2 14.1 %collective-permute-start.7 = (bf16[64,2048]{1,0:T(8,128)(2,1)S(1)}, bf16[64,2048]{1,0:T(8,128)(2,1)S(1)}, u32[]{:S(2)}, u32[]{:S(2)}) collective-permute-start(bf16[64,2048]{1,0:T(8,128)(2,1)S(1)} %get-tuple-element.47), channel_id=1, source_target_pairs={{1,2},{2,1},{5,6},{6,5},{9,10},{10,9},{13,14},{14,13},{17,18},{18,... | collective-permute-start | bytes 786440 | tf_op jit(solution)/shard_map/ppermute | solution.py:539
  15.9 16.9 %collective-permute-start.8 = (bf16[64,2048]{1,0:T(8,128)(2,1)S(1)}, bf16[64,2048]{1,0:T(8,128)(2,1)S(1)}, u32[]{:S(2)}, u32[]{:S(2)}) collective-permute-start(bf16[64,2048]{1,0:T(8,128)(2,1)S(1)} %get-tuple-element.48), channel_id=1, source_target_pairs={{0,1},{1,0},{2,3},{3,2},{4,5},{5,4},{6,7},{7,6},{8,9},{9,8},{10,11... | collective-permute-start | bytes 786440 | tf_op jit(solution)/shard_map/ppermute | solution.py:539
  20.1 8.2 %copy-start.6 = (bf16[192,256]{1,0:T(8,128)(2,1)S(1)}, bf16[192,256]{1,0:T(8,128)(2,1)}, u32[]{:S(2)}) copy-start(bf16[192,256]{1,0:T(8,128)(2,1)} %constant.25.clone.go_table) | copy-start | bytes 294916
  20.1 8.2 %copy-start.7 = (bf16[64,192]{1,0:T(8,128)(2,1)S(1)}, bf16[64,192]{1,0:T(8,128)(2,1)}, u32[]{:S(2)}) copy-start(bf16[64,192]{1,0:T(8,128)(2,1)} %constant.26.clone.t_table) | copy-start | bytes 73732
  23.6 9.7 %copy-start.1 = (bf16[1,2,128,2048]{3,2,1,0:T(8,128)(2,1)S(1)}, bf16[1,2,128,2048]{3,2,1,0:T(8,128)(2,1)}, u32[]{:S(2)}) copy-start(bf16[1,2,128,2048]{3,2,1,0:T(8,128)(2,1)} %param.21) | copy-start | bytes 3145732
  23.6 9.2 %collective-permute-start.5 = (bf16[16,2048]{1,0:T(8,128)(2,1)S(1)}, bf16[16,2048]{1,0:T(8,128)(2,1)S(1)}, u32[]{:S(2)}, u32[]{:S(2)}) collective-permute-start(bf16[16,2048]{1,0:T(8,128)(2,1)S(1)} %get-tuple-element.45), channel_id=1, source_target_pairs={{1,30},{2,29},{5,2},{6,1},{9,6},{10,5},{13,10},{14,9},{17,14},{18,... | collective-permute-start | bytes 196616 | tf_op jit(solution)/shard_map/ppermute | solution.py:539
  24.4 8.9 %collective-permute-start.6 = (bf16[16,2048]{1,0:T(8,128)(2,1)S(1)}, bf16[16,2048]{1,0:T(8,128)(2,1)S(1)}, u32[]{:S(2)}, u32[]{:S(2)}) collective-permute-start(bf16[16,2048]{1,0:T(8,128)(2,1)S(1)} %get-tuple-element.46), channel_id=1, source_target_pairs={{0,29},{1,28},{2,31},{3,30},{4,1},{5,0},{6,3},{7,2},{8,5},{9,4},{1... | collective-permute-start | bytes 196616 | tf_op jit(solution)/shard_map/ppermute | solution.py:539
  28.3 10.4 %collective-permute-start.4 = (bf16[128,2048]{1,0:T(8,128)(2,1)S(1)}, bf16[128,2048]{1,0:T(8,128)(2,1)S(1)}, u32[]{:S(2)}, u32[]{:S(2)}) collective-permute-start(bf16[128,2048]{1,0:T(8,128)(2,1)S(1)} %get-tuple-element.44), channel_id=1, source_target_pairs={{0,28},{4,0},{8,4},{12,8},{16,12},{20,16},{24,20},{28,24},{1,29},{... | collective-permute-start | bytes 1572872 | tf_op jit(solution)/shard_map/ppermute | solution.py:527
  29.3 21.7 %collective-permute-start.12 = (bf16[32,2048]{1,0:T(8,128)(2,1)S(1)}, bf16[32,2048]{1,0:T(8,128)(2,1)S(1)}, u32[]{:S(2)}, u32[]{:S(2)}) collective-permute-start(bf16[32,2048]{1,0:T(8,128)(2,1)S(1)} %get-tuple-element.55), channel_id=1, source_target_pairs={{0,4},{4,8},{8,12},{12,16},{16,20},{20,24},{24,28},{28,0},{1,5},{5... | collective-permute-start | bytes 393224 | tf_op jit(solution)/shard_map/ppermute | solution.py:527
  32.8 13.2 %collective-permute-start.3 = (bf16[32,2048]{1,0:T(8,128)(2,1)S(1)}, bf16[32,2048]{1,0:T(8,128)(2,1)S(1)}, u32[]{:S(2)}, u32[]{:S(2)}) collective-permute-start(bf16[32,2048]{1,0:T(8,128)(2,1)S(1)} %shard_map.213.refs_9_.mine0), channel_id=1, source_target_pairs={{0,1},{1,0},{2,3},{3,2},{4,5},{5,4},{6,7},{7,6},{8,9},{9,8},{10,11... | collective-permute-start | bytes 393224 | tf_op jit(solution)/shard_map/ppermute | solution.py:616
  35.9 12.3 %collective-permute-start.11 = (bf16[96,2048]{1,0:T(8,128)(2,1)S(1)}, bf16[96,2048]{1,0:T(8,128)(2,1)S(1)}, u32[]{:S(2)}, u32[]{:S(2)}) collective-permute-start(bf16[96,2048]{1,0:T(8,128)(2,1)S(1)} %get-tuple-element.54), channel_id=1, source_target_pairs={{0,8},{4,12},{8,16},{12,20},{16,24},{20,28},{24,0},{28,4},{1,9},{5... | collective-permute-start | bytes 1179656 | tf_op jit(solution)/shard_map/ppermute | solution.py:527
  40.1 6.0 %collective-permute-start.9 = (bf16[32,2048]{1,0:T(8,128)(2,1)S(1)}, bf16[32,2048]{1,0:T(8,128)(2,1)S(1)}, u32[]{:S(2)}, u32[]{:S(2)}) collective-permute-start(bf16[32,2048]{1,0:T(8,128)(2,1)S(1)} %get-tuple-element.53.mine1), channel_id=1, source_target_pairs={{0,1},{1,0},{2,3},{3,2},{4,5},{5,4},{6,7},{7,6},{8,9},{9,8},{10,11... | collective-permute-start | bytes 393224 | tf_op jit(solution)/shard_map/ppermute | solution.py:616
  42.5 10.5 %collective-permute-start.13 = (bf16[128,2048]{1,0:T(8,128)(2,1)S(1)}, bf16[128,2048]{1,0:T(8,128)(2,1)S(1)}, u32[]{:S(2)}, u32[]{:S(2)}) collective-permute-start(bf16[128,2048]{1,0:T(8,128)(2,1)S(1)} %shard_map.219), channel_id=1, source_target_pairs={{0,28},{4,0},{8,4},{12,8},{16,12},{20,16},{24,20},{28,24},{1,29},{... | collective-permute-start | bytes 1572872 | tf_op jit(solution)/shard_map/ppermute | solution.py:527
  46.1 4.9 %copy-start.12 = (bf16[320,160]{1,0:T(8,128)(2,1)S(1)}, bf16[320,160]{1,0:T(8,128)(2,1)}, u32[]{:S(2)}) copy-start(bf16[320,160]{1,0:T(8,128)(2,1)} %constant.27.clone.m_table) | copy-start | bytes 307204
  46.1 4.9 %copy-start.14 = (bf16[256,160]{1,0:T(8,128)(2,1)S(1)}, bf16[256,160]{1,0:T(8,128)(2,1)}, u32[]{:S(2)}) copy-start(bf16[256,160]{1,0:T(8,128)(2,1)} %constant.29.clone.c_table) | copy-start | bytes 245764
  46.1 4.9 %copy-start.17 = (bf16[160,64]{1,0:T(8,128)(2,1)S(1)}, bf16[160,64]{1,0:T(8,128)(2,1)}, u32[]{:S(2)}) copy-start(bf16[160,64]{1,0:T(8,128)(2,1)} %constant.28.clone.q_table) | copy-start | bytes 61444
  46.2 6.9 %collective-permute-start.10 = (bf16[64,2048]{1,0:T(8,128)(2,1)S(1)}, bf16[64,2048]{1,0:T(8,128)(2,1)S(1)}, u32[]{:S(2)}, u32[]{:S(2)}) collective-permute-start(bf16[64,2048]{1,0:T(8,128)(2,1)S(1)} %shard_map.216.refs_6_.mine), channel_id=1, source_target_pairs={{0,2},{1,3},{2,0},{3,1},{4,6},{5,7},{6,4},{7,5},{8,10},{9,11},{10,... | collective-permute-start | bytes 786440 | tf_op jit(solution)/shard_map/ppermute | solution.py:616

commit v14 on v13

--- a/solution.py
+++ b/solution.py
@@ -315,13 +315,14 @@
 
 
 def second_ready_kernel(
-    reach, notes, saved, far, near, weights, ahead0, m_table, q_table, c_table,
-    m_out, q_out, factor, conv_out, mean, inverse, ahead, halo, halos, masked,
+    reach, notes, saved, far, near, weights, ahead0, ahead1, m_table, q_table, c_table,
+    m_out, q_out, factor, conv_out, mean, inverse, ahead, next_layer, halo, halos, masked,
 ):
     left, right = sorted_halos(near, far, reach, halos)
     ahead[pl.ds(0, reach), :] = left[...]
     ahead[pl.ds(reach, reach), :] = right[...]
     ahead[pl.ds(2 * reach, ahead0.shape[0]), :] = ahead0[...]
+    next_layer[...] = ahead1[...]
     own, width = masked.shape
     slot, length, first = looked_up(notes, BACK1)
     gain = slot_row(weights, slot)
@@ -450,21 +451,29 @@
     notes[AHEAD0 + 1] = ahead_len[lax.rem(section + sections - 2, sections)]
 
 
-def final_kernel(notes, mine, other, act, grad, act_out, grad_out, taps, gains, sems):
+def final_kernel(notes, mine, other, act, grad, act_out, grad_out, taps_out, gains_out, taps, gains, sems):
     copies = [
         pltpu.make_async_copy(act, act_out, sems.at[0]),
         pltpu.make_async_copy(grad, grad_out, sems.at[1]),
     ]
     for copy in copies:
         copy.start()
-    count = taps.shape[0]
-    total = mine[...].astype(F32) + other[...].astype(F32)
-    ticks = total[: count + 1], total[count + 1 :]
-    for slot in range(taps.shape[1]):
-        use = [(notes[layer] == slot).astype(F32) for layer in (BACK0, BACK1)]
-        both = use[0] * ticks[0] + use[1] * ticks[1]
-        taps[:, slot, :] = both[:count]
-        gains[slot : slot + 1, :] = both[count:]
+    count, slots, width = taps.shape
+    step = width // 4
+    for begin in range(0, width, step):
+        columns = pl.ds(begin, step)
+        total = mine[:, columns].astype(F32) + other[:, columns].astype(F32)
+        ticks = total[: count + 1], total[count + 1 :]
+        for slot in range(slots):
+            use = [(notes[layer] == slot).astype(F32) for layer in (BACK0, BACK1)]
+            both = use[0] * ticks[0] + use[1] * ticks[1]
+            taps[:, slot, columns] = both[:count]
+            gains[slot : slot + 1, columns] = both[count:]
+        for source, target in ((taps.at[:, :, columns], taps_out.at[:, :, columns]),):
+            copies.append(pltpu.make_async_copy(source, target, sems.at[len(copies)]))
+            copies[-1].start()
+    copies.append(pltpu.make_async_copy(gains, gains_out, sems.at[len(copies)]))
+    copies[-1].start()
     for copy in copies:
         copy.wait()
 
@@ -574,7 +583,6 @@
         0,
     )
     near1, far1 = swapped(near1, far1)
-    ahead1 = shifted(ahead1, 1)
     g_table, x_table = stacked(to_freq(size, span(one, own))), stacked(from_freq(size, span(0, own)))
     grad_mid, near2, far2, halo0, inner0, gain0 = run(
         functools.partial(first_backward_kernel, two),
@@ -600,18 +608,19 @@
     halo_scratch = [
         pltpu.VMEM((2 * two, width), BF16), pltpu.VMEM((2, two, width), BF16), pltpu.VMEM((own, width), BF16)
     ]
-    m1, q1, factor1, conv1, mean1, inverse1, ahead0 = run(
+    m1, q1, factor1, conv1, mean1, inverse1, ahead0, ahead1 = run(
         functools.partial(second_ready_kernel, two),
         (
             like(size, width, F32), like(size, width, F32), like(small, width, F32), like(own, width, F32),
             like(own, LANES, F32), like(own, LANES, F32), like(2 * two + tap_count + 1, width, BF16),
+            like(tap_count + 1, width, BF16),
         ),
         halo_scratch,
-        [notes, saved, far1, near1, weights, ahead0, m_table, q_table, c_table],
+        [notes, saved, far1, near1, weights, ahead0, ahead1, m_table, q_table, c_table],
         5,
         taps0, near2, far2,
     )
-    ahead0 = shifted(ahead0, 2)
+    ahead0, ahead1 = shifted(ahead0, 2), shifted(ahead1, 1)
     def partner(x, step):
         return lax.ppermute(x, "tm", [(i, i ^ step) for i in range(shards)])
 
@@ -668,9 +677,12 @@
             like(own, width, BF16), like(own, width, BF16),
             jax.ShapeDtypeStruct((tap_count, slots, width), F32), like(slots, width, F32),
         ),
-        [pltpu.SemaphoreType.DMA((2,))],
+        [
+            pltpu.VMEM((tap_count, slots, width), F32), pltpu.VMEM((slots, width), F32),
+            pltpu.SemaphoreType.DMA((7,)),
+        ],
         (notes, mine, other, act_out, grad_out),
-        0, [SMEM] + [VMEM] * 2 + [ANY] * 2, (ANY, ANY, VMEM, VMEM),
+        0, [SMEM] + [VMEM] * 2 + [ANY] * 2, (ANY,) * 4,
     )
     return act_out[None], grad_out[None], taps.transpose(1, 0, 2)[None], gains[None]
 

time: 55.9 us -> 56.5 us (1.011)
  waiting for transfers between devices: 5.93 us -> 7.41 us
  Pallas kernels: 21.1 us -> 20.5 us
    ppermute x3, waiting for transfers between devices: 0.01 us -> 1.38 us  [partner(): return lax.ppermute(x, 'tm', [(i, i ^ step) for i in range(shards)])]
    pallas_call x11, Pallas kernels: 21.1 us -> 20.5 us  [call(): pl.pallas_call(kernel, out_shape=outs, in_specs=specs, out_specs=jax.tree...]
  transfers between devices with their start and end apart: 14 -> 14, of which waited for: 4 -> 5; matrix products, arithmetic and copies ran while one was open for 0% -> 0% of each run, Pallas kernels for 34% -> 33%
where the time goes in v14:
time: 56.5 us; the launch traced here: 56.2 us
  starting transfers between devices  24.1 us (43%)
  Pallas kernels  20.5 us (36%)
  waiting for transfers between devices  7.41 us (13%)
  local copies, waits for them, and re-layouts  3 us (5%)
  between operations  1.08 us (2%)
    pallas_call x11, Pallas kernels, call(): pl.pallas_call(kernel, out_shape=outs, in_specs=specs, out_specs=jax.tree...  20.5 us
    ppermute x6, starting transfers between devices, swapped(): results.append(lax.ppermute(x, ('section', 'tm'), pairs))  13.1 us
    ppermute x5, starting transfers between devices, shifted(): lax.ppermute(x, 'section', [(i, (i + by) % sections) for i in range(secti...  8.65 us
    ppermute x6, waiting for transfers between devices, swapped(): results.append(lax.ppermute(x, ('section', 'tm'), pairs))  4.92 us
    unnamed x36, local copies, waits for them, and re-layouts  3 us
    ppermute x3, starting transfers between devices, partner(): return lax.ppermute(x, 'tm', [(i, i ^ step) for i in range(shards)])  2.44 us
    ppermute x3, waiting for transfers between devices, partner(): return lax.ppermute(x, 'tm', [(i, i ^ step) for i in range(shards)])  1.38 us
  transfers between devices with their start and end apart: 14, of which 5 were waited for; matrix products, arithmetic and copies ran while one was open for 0% of the time, Pallas kernels for 33%

profile of v14, /device:TPU:0, one launch (start us, length us, event | category | flops | bytes accessed | tf_op | source)
XLA Modules:
  0.0 56.2 jit_solution(17374009460918291229)
XLA Ops:
  0.7 3.1 %collective-permute-start.2 = (bf16[128,2048]{1,0:T(8,128)(2,1)}, bf16[128,2048]{1,0:T(8,128)(2,1)}, u32[]{:S(2)}, u32[]{:S(2)}) collective-permute-start(bf16[128,2048]{1,0:T(8,128)(2,1)} %bitcast.21), channel_id=1, source_target_pairs={{0,8},{4,12},{8,16},{12,20},{16,24},{20,28},{24,0},{28,4},{1,9},{5... | collective-permute-start | bytes 1572872 | tf_op jit(solution)/shard_map/ppermute | solution.py:536
  3.7 1.9 %shard_map.210 = (bf16[48,2048]{1,0:T(8,128)(2,1)}, bf16[48,2048]{1,0:T(8,128)(2,1)}, s32[8]{0:T(128)}) custom-call(bf16[2,128,2048]{2,1,0:T(8,128)(2,1)} %bitcast.15, bf16[1,128,2048]{2,1,0:T(8,128)(2,1)} %grad.1, s32[8]{0:T(128)} %back_lengths.1, s32[8]{0:T(128)} %ahead_lengths.1, s32[2,8]{1,0:T(2,128)} %bitcast.25, s32[2,8]{1,0:T(2,128)} %bitcast.26), custom_call_target="tpu_custom_call" | custom-call | tf_op jit(solution)/shard_map/pallas_call | solution.py:503
  5.6 0.7 %collective-permute-start = (bf16[48,2048]{1,0:T(8,128)(2,1)}, bf16[48,2048]{1,0:T(8,128)(2,1)S(1)}, u32[]{:S(2)}, u32[]{:S(2)}) collective-permute-start(bf16[48,2048]{1,0:T(8,128)(2,1)} %get-tuple-element.36), channel_id=1, source_target_pairs={{1,2},{2,1},{5,6},{6,5},{9,10},{10,9},{13,14},{14,13},{17,18},{18,... | collective-permute-start | bytes 589832 | tf_op jit(solution)/shard_map/ppermute | solution.py:548
  6.3 4.3 %collective-permute-start.1 = (bf16[48,2048]{1,0:T(8,128)(2,1)}, bf16[48,2048]{1,0:T(8,128)(2,1)S(1)}, u32[]{:S(2)}, u32[]{:S(2)}) collective-permute-start(bf16[48,2048]{1,0:T(8,128)(2,1)} %get-tuple-element.37), channel_id=1, source_target_pairs={{0,1},{1,0},{2,3},{3,2},{4,5},{5,4},{6,7},{7,6},{8,9},{9,8},{10,11... | collective-permute-start | bytes 589832 | tf_op jit(solution)/shard_map/ppermute | solution.py:548
  10.6 1.2 %copy-done = bf16[1,2,128,2048]{3,2,1,0:T(8,128)(2,1)S(1)} copy-done((bf16[1,2,128,2048]{3,2,1,0:T(8,128)(2,1)S(1)}, bf16[1,2,128,2048]{3,2,1,0:T(8,128)(2,1)}, u32[]{:S(2)}) %copy-start) | copy-done | bytes 1048600
  11.8 1.0 %copy-done.3 = bf16[1,128,2048]{2,1,0:T(8,128)(2,1)S(1)} copy-done((bf16[1,128,2048]{2,1,0:T(8,128)(2,1)S(1)}, bf16[1,128,2048]{2,1,0:T(8,128)(2,1)}, u32[]{:S(2)}) %copy-start.3) | copy-done | bytes 524312
  12.8 0.7 %copy-done.9 = s32[8]{0:T(128)S(1)} copy-done((s32[8]{0:T(128)S(1)}, s32[8]{0:T(128)}, u32[]{:S(2)}) %copy-start.9) | copy-done | bytes 56
  13.5 0.0 copy-start.16
  13.5 1.7 %shard_map.211 = (bf16[2,32,2048]{2,1,0:T(8,128)(2,1)S(1)}, bf16[32,2048]{1,0:T(8,128)(2,1)S(1)}, bf16[32,2048]{1,0:T(8,128)(2,1)S(1)}, bf16[64,2048]{1,0:T(8,12...) custom-call(s32[8]{0:T(128)S(1)} %copy-done.9, ...), custom_call_target="tpu_custom_call" | custom-call | tf_op jit(solution)/shard_map/pallas_call | solution.py:503
  15.2 0.7 %collective-permute-start.7 = (bf16[64,2048]{1,0:T(8,128)(2,1)S(1)}, bf16[64,2048]{1,0:T(8,128)(2,1)S(1)}, u32[]{:S(2)}, u32[]{:S(2)}) collective-permute-start(bf16[64,2048]{1,0:T(8,128)(2,1)S(1)} %get-tuple-element.48), channel_id=1, source_target_pairs={{1,2},{2,1},{5,6},{6,5},{9,10},{10,9},{13,14},{14,13},{17,18},{18,... | collective-permute-start | bytes 786440 | tf_op jit(solution)/shard_map/ppermute | solution.py:548
  15.9 2.8 %collective-permute-start.8 = (bf16[64,2048]{1,0:T(8,128)(2,1)S(1)}, bf16[64,2048]{1,0:T(8,128)(2,1)S(1)}, u32[]{:S(2)}, u32[]{:S(2)}) collective-permute-start(bf16[64,2048]{1,0:T(8,128)(2,1)S(1)} %get-tuple-element.49), channel_id=1, source_target_pairs={{0,1},{1,0},{2,3},{3,2},{4,5},{5,4},{6,7},{7,6},{8,9},{9,8},{10,11... | collective-permute-start | bytes 786440 | tf_op jit(solution)/shard_map/ppermute | solution.py:548
  18.7 1.3 %collective-permute-done.1.refs_3_ = bf16[48,2048]{1,0:T(8,128)(2,1)S(1)} collective-permute-done((bf16[48,2048]{1,0:T(8,128)(2,1)}, bf16[48,2048]{1,0:T(8,128)(2,1)S(1)}, u32[]{:S(2)}, u32[]{:S(2)}) %collective-permute-start.1) | collective-permute-done | bytes 196640 | tf_op jit(solution)/shard_map/ppermute | solution.py:548
  20.1 3.5 %shard_map.212 = (bf16[128,2048]{1,0:T(8,128)(2,1)S(1)}, bf16[16,2048]{1,0:T(8,128)(2,1)S(1)}, bf16[16,2048]{1,0:T(8,128)(2,1)S(1)}, bf16[64,2048]{1,0:T(8,128)(...) custom-call(s32[8]{0:T(128)S(1)} %copy-done.10, bf16[2,128,2048]{2,1,0:T(8,128)(2,1)S(1)} %bitcast.17, ...), custom_call_target="tpu_custom_call" | custom-call | flops 4000000000 | tf_op jit(solution)/shard_map/pallas_call | solution.py:503
  23.6 0.8 %collective-permute-start.5 = (bf16[16,2048]{1,0:T(8,128)(2,1)S(1)}, bf16[16,2048]{1,0:T(8,128)(2,1)S(1)}, u32[]{:S(2)}, u32[]{:S(2)}) collective-permute-start(bf16[16,2048]{1,0:T(8,128)(2,1)S(1)} %get-tuple-element.46), channel_id=1, source_target_pairs={{1,30},{2,29},{5,2},{6,1},{9,6},{10,5},{13,10},{14,9},{17,14},{18,... | collective-permute-start | bytes 196616 | tf_op jit(solution)/shard_map/ppermute | solution.py:548
  24.4 3.9 %collective-permute-start.6 = (bf16[16,2048]{1,0:T(8,128)(2,1)S(1)}, bf16[16,2048]{1,0:T(8,128)(2,1)S(1)}, u32[]{:S(2)}, u32[]{:S(2)}) collective-permute-start(bf16[16,2048]{1,0:T(8,128)(2,1)S(1)} %get-tuple-element.47), channel_id=1, source_target_pairs={{0,29},{1,28},{2,31},{3,30},{4,1},{5,0},{6,3},{7,2},{8,5},{9,4},{1... | collective-permute-start | bytes 196616 | tf_op jit(solution)/shard_map/ppermute | solution.py:548
  28.3 1.0 %shard_map.213.refs_10_.mine0 = bf16[32,2048]{1,0:T(8,128)(2,1)S(1)} custom-call(bf16[64,2048]{1,0:T(8,128)(2,1)S(1)} %get-tuple-element.42.halo, bf16[128,2048]{1,0:T(8,128)(2,1)S(1)} %get-tuple-element.39.refs_6_.masked, bf16[128,2048]{1,0:T(8,128)(2,1)S(1)} %get-tuple-element.43.inner, f32[1,2048]{1,0:T(1,128)S(1)} %get-tuple-element.44.gain_sum, ...), custom_call_target="tpu_custom_call" | custom-call | tf_op jit(solution)/shard_map/pallas_call | solution.py:503
  29.3 0.7 %collective-permute-start.3 = (bf16[32,2048]{1,0:T(8,128)(2,1)S(1)}, bf16[32,2048]{1,0:T(8,128)(2,1)S(1)}, u32[]{:S(2)}, u32[]{:S(2)}) collective-permute-start(bf16[32,2048]{1,0:T(8,128)(2,1)S(1)} %shard_map.213.refs_10_.mine0), channel_id=1, source_target_pairs={{0,1},{1,0},{2,3},{3,2},{4,5},{5,4},{6,7},{7,6},{8,9},{9,8},{10,11... | collective-permute-start | bytes 393224 | tf_op jit(solution)/shard_map/ppermute | solution.py:625
  30.0 2.8 %collective-permute-done.8.refs_3_ = bf16[64,2048]{1,0:T(8,128)(2,1)S(1)} collective-permute-done((bf16[64,2048]{1,0:T(8,128)(2,1)S(1)}, bf16[64,2048]{1,0:T(8,128)(2,1)S(1)}, u32[]{:S(2)}, u32[]{:S(2)}) %collective-permute-start.8) | collective-permute-done | bytes 262176 | tf_op jit(solution)/shard_map/ppermute | solution.py:548
  32.8 0.8 %collective-permute-done.6.refs_11_.near = bf16[16,2048]{1,0:T(8,128)(2,1)S(1)} collective-permute-done((bf16[16,2048]{1,0:T(8,128)(2,1)S(1)}, bf16[16,2048]{1,0:T(8,128)(2,1)S(1)}, u32[]{:S(2)}, u32[]{:S(2)}) %collective-permute-start.6) | collective-permute-done | bytes 65568 | tf_op jit(solution)/shard_map/ppermute | solution.py:548
  33.6 2.6 %shard_map.214 = (f32[192,2048]{1,0:T(8,128)S(1)}, f32[192,2048]{1,0:T(8,128)S(1)}, f32[160,2048]{1,0:T(8,128)S(1)}, f32[128,2048]{1,0:T(8,128)S(1)}, f32[128,12...) custom-call(s32[8]{0:T(128)S(1)} %copy-done.10, ...), custom_call_target="tpu_custom_call" | custom-call | flops 5000000000 | tf_op jit(solution)/shard_map/pallas_call | solution.py:503
  36.2 1.8 %collective-permute-start.11 = (bf16[96,2048]{1,0:T(8,128)(2,1)S(1)}, bf16[96,2048]{1,0:T(8,128)(2,1)S(1)}, u32[]{:S(2)}, u32[]{:S(2)}) collective-permute-start(bf16[96,2048]{1,0:T(8,128)(2,1)S(1)} %get-tuple-element.56), channel_id=1, source_target_pairs={{0,8},{4,12},{8,16},{12,20},{16,24},{20,28},{24,0},{28,4},{1,9},{5... | collective-permute-start | bytes 1179656 | tf_op jit(solution)/shard_map/ppermute | solution.py:536
  38.0 1.4 %shard_map.215 = (bf16[160,2048]{1,0:T(8,128)(2,1)S(1)}, bf16[32,2048]{1,0:T(8,128)(2,1)S(1)}) custom-call(s32[8]{0:T(128)S(1)} %copy-done.10, bf16[128,2048]{1,0:T(8,128)(2,1)S(1)} %collective-permute-done.4.received, bf16[16,2048]{1,0:T(8,128)(2,1)S(1)} %collective-permute-done.5.refs_12_.far, bf16[16,2048]{1,0:T(8,128)(2,1)S(1)} %collective-permute-done.6.refs_11_.near, ...), custom_call_target="tpu_custom_call" | custom-call | flops 2000000000 | tf_op jit(solution)/shard_map/pallas_call | solution.py:503
  39.4 0.1 collective-permute-start.9
  39.4 2.0 %shard_map.219 = bf16[128,2048]{1,0:T(8,128)(2,1)S(1)} custom-call(s32[8]{0:T(128)S(1)} %copy-done.10, bf16[2,128,2048]{2,1,0:T(8,128)(2,1)S(1)} %bitcast.19, bf16[128,2048]{1,0:T(8,128)(2,1)S(1)} %collective-permute-done.4.received, bf16[2,32,2048]{2,1,0:T(8,128)(2,1)S(1)} %get-tuple-element.38.refs_5_.refs_4_.weights, ...), custom_call_target="tpu_custom_call" | custom-call | flops 6000000000 | tf_op jit(solution)/shard_map/pallas_call | solution.py:503
  41.4 3.8 %collective-permute-start.13 = (bf16[128,2048]{1,0:T(8,128)(2,1)S(1)}, bf16[128,2048]{1,0:T(8,128)(2,1)S(1)}, u32[]{:S(2)}, u32[]{:S(2)}) collective-permute-start(bf16[128,2048]{1,0:T(8,128)(2,1)S(1)} %shard_map.219), channel_id=1, source_target_pairs={{0,28},{4,0},{8,4},{12,8},{16,12},{20,16},{24,20},{28,24},{1,29},{... | collective-permute-start | bytes 1572872 | tf_op jit(solution)/shard_map/ppermute | solution.py:536
  45.2 0.1 shard_map.216.refs_6_.mine
  45.3 1.7 %collective-permute-start.10 = (bf16[64,2048]{1,0:T(8,128)(2,1)S(1)}, bf16[64,2048]{1,0:T(8,128)(2,1)S(1)}, u32[]{:S(2)}, u32[]{:S(2)}) collective-permute-start(bf16[64,2048]{1,0:T(8,128)(2,1)S(1)} %shard_map.216.refs_6_.mine), channel_id=1, source_target_pairs={{0,2},{1,3},{2,0},{3,1},{4,6},{5,7},{6,4},{7,5},{8,10},{9,11},{10,... | collective-permute-start | bytes 786440 | tf_op jit(solution)/shard_map/ppermute | solution.py:625
  47.0 1.1 %collective-permute-done.11.refs_2_ = bf16[96,2048]{1,0:T(8,128)(2,1)S(1)} collective-permute-done((bf16[96,2048]{1,0:T(8,128)(2,1)S(1)}, bf16[96,2048]{1,0:T(8,128)(2,1)S(1)}, u32[]{:S(2)}, u32[]{:S(2)}) %collective-permute-start.11) | collective-permute-done | bytes 393248 | tf_op jit(solution)/shard_map/ppermute | solution.py:536
  48.1 2.8 %shard_map.217.between = bf16[160,2048]{1,0:T(8,128)(2,1)S(1)} custom-call(s32[8]{0:T(128)S(1)} %copy-done.10, bf16[128,2048]{1,0:T(8,128)(2,1)} %collective-permute-done.2.refs_14_.refs_1_, bf16[96,2048]{1,0:T(8,128)(2,1)S(1)} %collective-permute-done.11.refs_2_, bf16[384,192]{1,0:T(8,128)(2,1)S(1)} %copy-done.5, bf16[192,64]{1,0:T(8,128)(2,1)S(1)} %copy-done.16, ...), custom_call_target="tpu_custom_call" | custom-call | flops 10000000000 | tf_op jit(solution)/shard_map/pallas_call | solution.py:503
  50.9 1.9 %shard_map.218.act = bf16[128,2048]{1,0:T(8,128)(2,1)S(1)} custom-call(s32[8]{0:T(128)S(1)} %copy-done.10, bf16[160,2048]{1,0:T(8,128)(2,1)S(1)} %shard_map.217.between, bf16[32,2048]{1,0:T(8,128)(2,1)S(1)} %collective-permute-done.12.layer, bf16[320,160]{1,0:T(8,128)(2,1)S(1)} %copy-done.12, bf16[160,64]{1,0:T(8,128)(2,1)S(1)} %copy-done.17, ...), custom_call_target="tpu_custom_call" | custom-call | flops 10000000000 | tf_op jit(solution)/shard_map/pallas_call | solution.py:503
  52.9 1.4 %collective-permute-done.10.other = bf16[64,2048]{1,0:T(8,128)(2,1)S(1)} collective-permute-done((bf16[64,2048]{1,0:T(8,128)(2,1)S(1)}, bf16[64,2048]{1,0:T(8,128)(2,1)S(1)}, u32[]{:S(2)}, u32[]{:S(2)}) %collective-permute-start.10) | collective-permute-done | bytes 262176 | tf_op jit(solution)/shard_map/ppermute | solution.py:625
  54.3 1.7 %shard_map.220 = (bf16[128,2048]{1,0:T(8,128)(2,1)}, bf16[128,2048]{1,0:T(8,128)(2,1)}, f32[31,2,2048]{2,1,0:T(2,128)}, f32[2,2048]{1,0:T(2,128)}) custom-call(s32[8]{0:T(128)S(1)} %copy-done.10, bf16[64,2048]{1,0:T(8,128)(2,1)S(1)} %shard_map.216.refs_6_.mine, bf16[64,2048]{1,0:T(8,128)(2,1)S(1)} %collective-permute-done.10.other, ...), custom_call_target="tpu_custom_call" | custom-call | tf_op jit(solution)/shard_map/pallas_call | solution.py:503
  (43 shorter events, 0.1 us)
Async XLA Ops:
  0.6 9.9 %copy-start.4 = (bf16[1,2,31,2048]{3,1,2,0:T(2,128)(2,1)S(1)}, bf16[1,2,31,2048]{3,1,2,0:T(2,128)(2,1)}, u32[]{:S(2)}) copy-start(bf16[1,2,31,2048]{3,1,2,0:T(2,128)(2,1)} %param.22) | copy-start | bytes 761860
  0.6 9.9 %copy-start.8 = (bf16[1,2,2048]{2,1,0:T(2,128)(2,1)S(1)}, bf16[1,2,2048]{2,1,0:T(2,128)(2,1)}, u32[]{:S(2)}) copy-start(bf16[1,2,2048]{2,1,0:T(2,128)(2,1)} %param.23) | copy-start | bytes 24580
  0.7 19.3 %collective-permute-start.2 = (bf16[128,2048]{1,0:T(8,128)(2,1)}, bf16[128,2048]{1,0:T(8,128)(2,1)}, u32[]{:S(2)}, u32[]{:S(2)}) collective-permute-start(bf16[128,2048]{1,0:T(8,128)(2,1)} %bitcast.21), channel_id=1, source_target_pairs={{0,8},{4,12},{8,16},{12,20},{16,24},{20,28},{24,0},{28,4},{1,9},{5... | collective-permute-start | bytes 1572872 | tf_op jit(solution)/shard_map/ppermute | solution.py:536
  3.7 16.3 %copy-start.5 = (bf16[384,192]{1,0:T(8,128)(2,1)S(1)}, bf16[384,192]{1,0:T(8,128)(2,1)}, u32[]{:S(2)}) copy-start(bf16[384,192]{1,0:T(8,128)(2,1)} %constant.20.clone.refs_9_.m_table.refs_7_.refs_3_) | copy-start | bytes 442372
  5.6 14.4 %copy-start.10 = (s32[8]{0:T(128)S(1)}, s32[8]{0:T(128)}, u32[]{:S(2)}) copy-start(s32[8]{0:T(128)} %get-tuple-element.35.notes.refs_0_) | copy-start | bytes 100
  5.6 13.1 %collective-permute-start = (bf16[48,2048]{1,0:T(8,128)(2,1)}, bf16[48,2048]{1,0:T(8,128)(2,1)S(1)}, u32[]{:S(2)}, u32[]{:S(2)}) collective-permute-start(bf16[48,2048]{1,0:T(8,128)(2,1)} %get-tuple-element.36), channel_id=1, source_target_pairs={{1,2},{2,1},{5,6},{6,5},{9,10},{10,9},{13,14},{14,13},{17,18},{18,... | collective-permute-start | bytes 589832 | tf_op jit(solution)/shard_map/ppermute | solution.py:548
  6.3 13.7 %collective-permute-start.1 = (bf16[48,2048]{1,0:T(8,128)(2,1)}, bf16[48,2048]{1,0:T(8,128)(2,1)S(1)}, u32[]{:S(2)}, u32[]{:S(2)}) collective-permute-start(bf16[48,2048]{1,0:T(8,128)(2,1)} %get-tuple-element.37), channel_id=1, source_target_pairs={{0,1},{1,0},{2,3},{3,2},{4,5},{5,4},{6,7},{7,6},{8,9},{9,8},{10,11... | collective-permute-start | bytes 589832 | tf_op jit(solution)/shard_map/ppermute | solution.py:548
  10.6 1.2 %copy-start = (bf16[1,2,128,2048]{3,2,1,0:T(8,128)(2,1)S(1)}, bf16[1,2,128,2048]{3,2,1,0:T(8,128)(2,1)}, u32[]{:S(2)}) copy-start(bf16[1,2,128,2048]{3,2,1,0:T(8,128)(2,1)} %param.21) | copy-start | bytes 3145732
  11.8 1.0 %copy-start.3 = (bf16[1,128,2048]{2,1,0:T(8,128)(2,1)S(1)}, bf16[1,128,2048]{2,1,0:T(8,128)(2,1)}, u32[]{:S(2)}) copy-start(bf16[1,128,2048]{2,1,0:T(8,128)(2,1)} %param.19) | copy-start | bytes 1572868
  12.8 0.7 %copy-start.9 = (s32[8]{0:T(128)S(1)}, s32[8]{0:T(128)}, u32[]{:S(2)}) copy-start(s32[8]{0:T(128)} %get-tuple-element.35.notes.refs_0_) | copy-start | bytes 100
  13.5 6.5 %copy-start.2 = (bf16[1,128,2048]{2,1,0:T(8,128)(2,1)S(1)}, bf16[1,128,2048]{2,1,0:T(8,128)(2,1)}, u32[]{:S(2)}) copy-start(bf16[1,128,2048]{2,1,0:T(8,128)(2,1)} %grad.1) | copy-start | bytes 1572868
  13.5 6.5 %copy-start.11 = (bf16[384,160]{1,0:T(8,128)(2,1)S(1)}, bf16[384,160]{1,0:T(8,128)(2,1)}, u32[]{:S(2)}) copy-start(bf16[384,160]{1,0:T(8,128)(2,1)} %constant.23.clone.refs_12_.g_table) | copy-start | bytes 368644
  13.5 6.5 %copy-start.13 = (bf16[320,192]{1,0:T(8,128)(2,1)S(1)}, bf16[320,192]{1,0:T(8,128)(2,1)}, u32[]{:S(2)}) copy-start(bf16[320,192]{1,0:T(8,128)(2,1)} %constant.22.clone.refs_11_.refs_9_.refs_5_) | copy-start | bytes 368644
  13.5 6.5 %copy-start.15 = (bf16[256,192]{1,0:T(8,128)(2,1)S(1)}, bf16[256,192]{1,0:T(8,128)(2,1)}, u32[]{:S(2)}) copy-start(bf16[256,192]{1,0:T(8,128)(2,1)} %constant.24.clone.refs_13_.x_table) | copy-start | bytes 294916
  13.5 6.5 %copy-start.16 = (bf16[192,64]{1,0:T(8,128)(2,1)S(1)}, bf16[192,64]{1,0:T(8,128)(2,1)}, u32[]{:S(2)}) copy-start(bf16[192,64]{1,0:T(8,128)(2,1)} %constant.21.clone.refs_10_.refs_8_.refs_4_) | copy-start | bytes 73732
  15.2 14.1 %collective-permute-start.7 = (bf16[64,2048]{1,0:T(8,128)(2,1)S(1)}, bf16[64,2048]{1,0:T(8,128)(2,1)S(1)}, u32[]{:S(2)}, u32[]{:S(2)}) collective-permute-start(bf16[64,2048]{1,0:T(8,128)(2,1)S(1)} %get-tuple-element.48), channel_id=1, source_target_pairs={{1,2},{2,1},{5,6},{6,5},{9,10},{10,9},{13,14},{14,13},{17,18},{18,... | collective-permute-start | bytes 786440 | tf_op jit(solution)/shard_map/ppermute | solution.py:548
  15.9 16.9 %collective-permute-start.8 = (bf16[64,2048]{1,0:T(8,128)(2,1)S(1)}, bf16[64,2048]{1,0:T(8,128)(2,1)S(1)}, u32[]{:S(2)}, u32[]{:S(2)}) collective-permute-start(bf16[64,2048]{1,0:T(8,128)(2,1)S(1)} %get-tuple-element.49), channel_id=1, source_target_pairs={{0,1},{1,0},{2,3},{3,2},{4,5},{5,4},{6,7},{7,6},{8,9},{9,8},{10,11... | collective-permute-start | bytes 786440 | tf_op jit(solution)/shard_map/ppermute | solution.py:548
  20.1 8.2 %copy-start.6 = (bf16[192,256]{1,0:T(8,128)(2,1)S(1)}, bf16[192,256]{1,0:T(8,128)(2,1)}, u32[]{:S(2)}) copy-start(bf16[192,256]{1,0:T(8,128)(2,1)} %constant.25.clone.go_table) | copy-start | bytes 294916
  20.1 8.2 %copy-start.7 = (bf16[64,192]{1,0:T(8,128)(2,1)S(1)}, bf16[64,192]{1,0:T(8,128)(2,1)}, u32[]{:S(2)}) copy-start(bf16[64,192]{1,0:T(8,128)(2,1)} %constant.26.clone.t_table) | copy-start | bytes 73732
  23.6 10.0 %copy-start.1 = (bf16[1,2,128,2048]{3,2,1,0:T(8,128)(2,1)S(1)}, bf16[1,2,128,2048]{3,2,1,0:T(8,128)(2,1)}, u32[]{:S(2)}) copy-start(bf16[1,2,128,2048]{3,2,1,0:T(8,128)(2,1)} %param.21) | copy-start | bytes 3145732
  23.6 9.2 %collective-permute-start.5 = (bf16[16,2048]{1,0:T(8,128)(2,1)S(1)}, bf16[16,2048]{1,0:T(8,128)(2,1)S(1)}, u32[]{:S(2)}, u32[]{:S(2)}) collective-permute-start(bf16[16,2048]{1,0:T(8,128)(2,1)S(1)} %get-tuple-element.46), channel_id=1, source_target_pairs={{1,30},{2,29},{5,2},{6,1},{9,6},{10,5},{13,10},{14,9},{17,14},{18,... | collective-permute-start | bytes 196616 | tf_op jit(solution)/shard_map/ppermute | solution.py:548
  24.4 9.2 %collective-permute-start.6 = (bf16[16,2048]{1,0:T(8,128)(2,1)S(1)}, bf16[16,2048]{1,0:T(8,128)(2,1)S(1)}, u32[]{:S(2)}, u32[]{:S(2)}) collective-permute-start(bf16[16,2048]{1,0:T(8,128)(2,1)S(1)} %get-tuple-element.47), channel_id=1, source_target_pairs={{0,29},{1,28},{2,31},{3,30},{4,1},{5,0},{6,3},{7,2},{8,5},{9,4},{1... | collective-permute-start | bytes 196616 | tf_op jit(solution)/shard_map/ppermute | solution.py:548
  28.3 9.7 %collective-permute-start.4 = (bf16[128,2048]{1,0:T(8,128)(2,1)S(1)}, bf16[128,2048]{1,0:T(8,128)(2,1)S(1)}, u32[]{:S(2)}, u32[]{:S(2)}) collective-permute-start(bf16[128,2048]{1,0:T(8,128)(2,1)S(1)} %get-tuple-element.45), channel_id=1, source_target_pairs={{0,28},{4,0},{8,4},{12,8},{16,12},{20,16},{24,20},{28,24},{1,29},{... | collective-permute-start | bytes 1572872 | tf_op jit(solution)/shard_map/ppermute | solution.py:536
  29.3 15.9 %collective-permute-start.3 = (bf16[32,2048]{1,0:T(8,128)(2,1)S(1)}, bf16[32,2048]{1,0:T(8,128)(2,1)S(1)}, u32[]{:S(2)}, u32[]{:S(2)}) collective-permute-start(bf16[32,2048]{1,0:T(8,128)(2,1)S(1)} %shard_map.213.refs_10_.mine0), channel_id=1, source_target_pairs={{0,1},{1,0},{2,3},{3,2},{4,5},{5,4},{6,7},{7,6},{8,9},{9,8},{10,11... | collective-permute-start | bytes 393224 | tf_op jit(solution)/shard_map/ppermute | solution.py:625
  36.2 11.9 %collective-permute-start.11 = (bf16[96,2048]{1,0:T(8,128)(2,1)S(1)}, bf16[96,2048]{1,0:T(8,128)(2,1)S(1)}, u32[]{:S(2)}, u32[]{:S(2)}) collective-permute-start(bf16[96,2048]{1,0:T(8,128)(2,1)S(1)} %get-tuple-element.56), channel_id=1, source_target_pairs={{0,8},{4,12},{8,16},{12,20},{16,24},{20,28},{24,0},{28,4},{1,9},{5... | collective-permute-start | bytes 1179656 | tf_op jit(solution)/shard_map/ppermute | solution.py:536
  38.0 12.9 %collective-permute-start.12 = (bf16[32,2048]{1,0:T(8,128)(2,1)S(1)}, bf16[32,2048]{1,0:T(8,128)(2,1)S(1)}, u32[]{:S(2)}, u32[]{:S(2)}) collective-permute-start(bf16[32,2048]{1,0:T(8,128)(2,1)S(1)} %get-tuple-element.57), channel_id=1, source_target_pairs={{0,4},{4,8},{8,12},{12,16},{16,20},{20,24},{24,28},{28,0},{1,5},{5... | collective-permute-start | bytes 393224 | tf_op jit(solution)/shard_map/ppermute | solution.py:536
  39.4 5.8 %collective-permute-start.9 = (bf16[32,2048]{1,0:T(8,128)(2,1)S(1)}, bf16[32,2048]{1,0:T(8,128)(2,1)S(1)}, u32[]{:S(2)}, u32[]{:S(2)}) collective-permute-start(bf16[32,2048]{1,0:T(8,128)(2,1)S(1)} %get-tuple-element.55.mine1), channel_id=1, source_target_pairs={{0,1},{1,0},{2,3},{3,2},{4,5},{5,4},{6,7},{7,6},{8,9},{9,8},{10,11... | collective-permute-start | bytes 393224 | tf_op jit(solution)/shard_map/ppermute | solution.py:625
  41.4 12.9 %collective-permute-start.13 = (bf16[128,2048]{1,0:T(8,128)(2,1)S(1)}, bf16[128,2048]{1,0:T(8,128)(2,1)S(1)}, u32[]{:S(2)}, u32[]{:S(2)}) collective-permute-start(bf16[128,2048]{1,0:T(8,128)(2,1)S(1)} %shard_map.219), channel_id=1, source_target_pairs={{0,28},{4,0},{8,4},{12,8},{16,12},{20,16},{24,20},{28,24},{1,29},{... | collective-permute-start | bytes 1572872 | tf_op jit(solution)/shard_map/ppermute | solution.py:536
  45.3 5.7 %copy-start.12 = (bf16[320,160]{1,0:T(8,128)(2,1)S(1)}, bf16[320,160]{1,0:T(8,128)(2,1)}, u32[]{:S(2)}) copy-start(bf16[320,160]{1,0:T(8,128)(2,1)} %constant.27.clone.m_table) | copy-start | bytes 307204
  45.3 5.7 %copy-start.14 = (bf16[256,160]{1,0:T(8,128)(2,1)S(1)}, bf16[256,160]{1,0:T(8,128)(2,1)}, u32[]{:S(2)}) copy-start(bf16[256,160]{1,0:T(8,128)(2,1)} %constant.29.clone.c_table) | copy-start | bytes 245764
  45.3 5.7 %copy-start.17 = (bf16[160,64]{1,0:T(8,128)(2,1)S(1)}, bf16[160,64]{1,0:T(8,128)(2,1)}, u32[]{:S(2)}) copy-start(bf16[160,64]{1,0:T(8,128)(2,1)} %constant.28.clone.q_table) | copy-start | bytes 61444
  45.3 9.0 %collective-permute-start.10 = (bf16[64,2048]{1,0:T(8,128)(2,1)S(1)}, bf16[64,2048]{1,0:T(8,128)(2,1)S(1)}, u32[]{:S(2)}, u32[]{:S(2)}) collective-permute-start(bf16[64,2048]{1,0:T(8,128)(2,1)S(1)} %shard_map.216.refs_6_.mine), channel_id=1, source_target_pairs={{0,2},{1,3},{2,0},{3,1},{4,6},{5,7},{6,4},{7,5},{8,10},{9,11},{10,... | collective-permute-start | bytes 786440 | tf_op jit(solution)/shard_map/ppermute | solution.py:625

commit v15 on v14

--- a/solution.py
+++ b/solution.py
@@ -308,21 +308,13 @@
     out[...] = added(mine, other)
 
 
-def below_kernel(mine0, other0, mine1, other1, out):
-    count = mine0.shape[0]
-    out[pl.ds(0, count), :] = added(mine0, other0)
-    out[pl.ds(count, count), :] = added(mine1, other1)
-
-
 def second_ready_kernel(
-    reach, notes, saved, far, near, weights, ahead0, ahead1, m_table, q_table, c_table,
-    m_out, q_out, factor, conv_out, mean, inverse, ahead, next_layer, halo, halos, masked,
+    reach, notes, saved, far, near, weights, m_table, q_table, c_table,
+    m_out, q_out, factor, conv_out, mean, inverse, ahead, halo, halos, masked,
 ):
     left, right = sorted_halos(near, far, reach, halos)
     ahead[pl.ds(0, reach), :] = left[...]
     ahead[pl.ds(reach, reach), :] = right[...]
-    ahead[pl.ds(2 * reach, ahead0.shape[0]), :] = ahead0[...]
-    next_layer[...] = ahead1[...]
     own, width = masked.shape
     slot, length, first = looked_up(notes, BACK1)
     gain = slot_row(weights, slot)
@@ -344,10 +336,13 @@
 
 
 def second_taps_kernel(
-    notes, received, far, near, weights, m, factor, conv, go_table, t_table, mixed_out, taps, halos
+    notes, received, far, near, weights, m, factor, conv, taps0, go_table, t_table, mixed_out, taps, halos
 ):
     own, width = conv.shape
     rows = factor.shape[0]
+    count = taps0.shape[0]
+    taps[pl.ds(0, count), :] = taps0[...]
+    taps1 = taps.at[pl.ds(count, count)]
     edge = (rows - own) // 2
     gain = slot_row(weights, notes[BACK1])
     left, right = sorted_halos(near, far, 0, halos)
@@ -358,7 +353,7 @@
         mixed_out[:, columns] = mixed
         inner = mixed[edge : edge + own]
         gain_sum = jnp.sum(inner.astype(F32) * conv[:, columns], axis=0, keepdims=True) / gain(columns)
-        put_taps(taps, tap_term(go_table, t_table, m[:, columns], inner), gain_sum, columns)
+        put_taps(taps1, tap_term(go_table, t_table, m[:, columns], inner), gain_sum, columns)
 
     each_block(width, block)
 
@@ -388,12 +383,11 @@
     return lambda columns: layer[last : last + 1, columns].astype(F32)
 
 
-def first_forward_kernel(reach, notes, act, ahead, m_table, q_table, c_table, out, halo, masked):
+def first_forward_kernel(reach, notes, act, ahead, layer, m_table, q_table, c_table, out, halo, masked):
     own, width = act.shape
     middle = reach // 2
     _, length, first = looked_up(notes, AHEAD0)
     left, right = ahead.at[pl.ds(0, reach)], ahead.at[pl.ds(reach, reach)]
-    layer = ahead.at[pl.ds(2 * reach, ahead.shape[0] - 2 * reach)]
     inner = [(left, middle, middle), (act, 0, own), (right, 0, middle)]
     norm_pieces([(act, 0, own)], row_gain(layer), first, length, masked)
     norm_halo(left, right, own, row_gain(layer), first, length, halo)
@@ -583,6 +577,7 @@
         0,
     )
     near1, far1 = swapped(near1, far1)
+    ahead0, ahead1 = shifted(ahead0, 2), shifted(ahead1, 1)
     g_table, x_table = stacked(to_freq(size, span(one, own))), stacked(from_freq(size, span(0, own)))
     grad_mid, near2, far2, halo0, inner0, gain0 = run(
         functools.partial(first_backward_kernel, two),
@@ -604,33 +599,33 @@
         first_taps_kernel, like(tap_count + 1, width, BF16), [],
         [halo0, layer0[0], inner0, gain0, m_table, go_table, t_table],
         0,
+        near2, far2,
     )
     halo_scratch = [
         pltpu.VMEM((2 * two, width), BF16), pltpu.VMEM((2, two, width), BF16), pltpu.VMEM((own, width), BF16)
     ]
-    m1, q1, factor1, conv1, mean1, inverse1, ahead0, ahead1 = run(
+    m1, q1, factor1, conv1, mean1, inverse1, ahead = run(
         functools.partial(second_ready_kernel, two),
         (
             like(size, width, F32), like(size, width, F32), like(small, width, F32), like(own, width, F32),
-            like(own, LANES, F32), like(own, LANES, F32), like(2 * two + tap_count + 1, width, BF16),
-            like(tap_count + 1, width, BF16),
+            like(own, LANES, F32), like(own, LANES, F32), like(2 * two, width, BF16),
         ),
         halo_scratch,
-        [notes, saved, far1, near1, weights, ahead0, ahead1, m_table, q_table, c_table],
+        [notes, saved, far1, near1, weights, m_table, q_table, c_table],
         5,
-        taps0, near2, far2,
-    )
-    ahead0, ahead1 = shifted(ahead0, 2), shifted(ahead1, 1)
+        taps0,
+    )
+    ahead = shifted(ahead, 2)
     def partner(x, step):
         return lax.ppermute(x, "tm", [(i, i ^ step) for i in range(shards)])
 
-    other0 = partner(taps0, 1)
-    mixed1, taps1 = run(
+    mixed1, sums = run(
         second_taps_kernel,
-        (like(small, width, BF16), like(tap_count + 1, width, BF16)),
+        (like(small, width, BF16), like(2 * (tap_count + 1), width, BF16)),
         [pltpu.VMEM((2, one, width), BF16)],
-        [notes, grad_mid, far2, near2, weights, m1, factor1, conv1, go_table, t_table],
+        [notes, grad_mid, far2, near2, weights, m1, factor1, conv1, taps0, go_table, t_table],
         2,
+        ahead0, ahead1,
     )
     grad_out = run(
         second_backward_kernel,
@@ -643,13 +638,12 @@
         6,
     )
     grad_out = shifted(grad_out, -1)
-    other1 = partner(taps1, 1)
-    mine = call(below_kernel, like(2 * (tap_count + 1), width, BF16), [], (taps0, other0, taps1, other1), 6)
+    mine = call(add_kernel, like(*sums.shape, BF16), [], (sums, partner(sums, 1)), 6)
     between = run(
         functools.partial(first_forward_kernel, two),
         like(small, width, BF16),
         [pltpu.VMEM((2 * two, width), BF16), pltpu.VMEM((own, width), BF16)],
-        [notes, act_ahead, ahead0, m_table, q_table, c_table],
+        [notes, act_ahead, ahead, ahead0, m_table, q_table, c_table],
         10,
         mine,
     )

time: 56.5 us -> 58.6 us (1.037)
  waiting for transfers between devices: 7.41 us -> 13 us
  starting transfers between devices: 24.1 us -> 20.6 us
    ppermute x5 -> x6, waiting for transfers between devices: 1.1 us -> 3.44 us  [shifted(): lax.ppermute(x, 'section', [(i, (i + by) % sections) for i in range(secti...]
    ppermute x5 -> x6, starting transfers between devices: 8.65 us -> 6.49 us  [shifted(): lax.ppermute(x, 'section', [(i, (i + by) % sections) for i in range(secti...]
    ppermute x3 -> x2, waiting for transfers between devices: 1.38 us -> 3.22 us  [partner(): return lax.ppermute(x, 'tm', [(i, i ^ step) for i in range(shards)])]
    ppermute x6, waiting for transfers between devices: 4.92 us -> 6.33 us  [swapped(): results.append(lax.ppermute(x, ('section', 'tm'), pairs))]
    ppermute x3 -> x2, starting transfers between devices: 2.44 us -> 1.02 us  [partner(): return lax.ppermute(x, 'tm', [(i, i ^ step) for i in range(shards)])]
  transfers between devices with their start and end apart: 14 -> 14, of which waited for: 5 -> 5; matrix products, arithmetic and copies ran while one was open for 0% -> 0% of each run, Pallas kernels for 33% -> 32%
where the time goes in v15:
time: 58.6 us; the launch traced here: 58.3 us
  starting transfers between devices  20.6 us (35%)
  Pallas kernels  20.6 us (35%)
  waiting for transfers between devices  13 us (22%)
  local copies, waits for them, and re-layouts  3 us (5%)
  between operations  1.09 us (2%)
    pallas_call x11, Pallas kernels, call(): pl.pallas_call(kernel, out_shape=outs, in_specs=specs, out_specs=jax.tree...  20.6 us
    ppermute x6, starting transfers between devices, swapped(): results.append(lax.ppermute(x, ('section', 'tm'), pairs))  13.1 us
    ppermute x6, starting transfers between devices, shifted(): lax.ppermute(x, 'section', [(i, (i + by) % sections) for i in range(secti...  6.49 us
    ppermute x6, waiting for transfers between devices, swapped(): results.append(lax.ppermute(x, ('section', 'tm'), pairs))  6.33 us
    ppermute x6, waiting for transfers between devices, shifted(): lax.ppermute(x, 'section', [(i, (i + by) % sections) for i in range(secti...  3.44 us
    ppermute x2, waiting for transfers between devices, partner(): return lax.ppermute(x, 'tm', [(i, i ^ step) for i in range(shards)])  3.22 us
    unnamed x36, local copies, waits for them, and re-layouts  3 us
  transfers between devices with their start and end apart: 14, of which 5 were waited for; matrix products, arithmetic and copies ran while one was open for 0% of the time, Pallas kernels for 32%

profile of v15, /device:TPU:0, one launch (start us, length us, event | category | flops | bytes accessed | tf_op | source)
XLA Modules:
  0.0 58.3 jit_solution(418458075704518911)
XLA Ops:
  0.7 3.1 %collective-permute-start.2 = (bf16[128,2048]{1,0:T(8,128)(2,1)}, bf16[128,2048]{1,0:T(8,128)(2,1)}, u32[]{:S(2)}, u32[]{:S(2)}) collective-permute-start(bf16[128,2048]{1,0:T(8,128)(2,1)} %bitcast.21), channel_id=1, source_target_pairs={{0,8},{4,12},{8,16},{12,20},{16,24},{20,28},{24,0},{28,4},{1,9},{5... | collective-permute-start | bytes 1572872 | tf_op jit(solution)/shard_map/ppermute | solution.py:530
  3.7 1.9 %shard_map.210 = (bf16[48,2048]{1,0:T(8,128)(2,1)}, bf16[48,2048]{1,0:T(8,128)(2,1)}, s32[8]{0:T(128)}) custom-call(bf16[2,128,2048]{2,1,0:T(8,128)(2,1)} %bitcast.15, bf16[1,128,2048]{2,1,0:T(8,128)(2,1)} %grad.1, s32[8]{0:T(128)} %back_lengths.1, s32[8]{0:T(128)} %ahead_lengths.1, s32[2,8]{1,0:T(2,128)} %bitcast.25, s32[2,8]{1,0:T(2,128)} %bitcast.26), custom_call_target="tpu_custom_call" | custom-call | tf_op jit(solution)/shard_map/pallas_call | solution.py:497
  5.6 0.7 %collective-permute-start = (bf16[48,2048]{1,0:T(8,128)(2,1)}, bf16[48,2048]{1,0:T(8,128)(2,1)S(1)}, u32[]{:S(2)}, u32[]{:S(2)}) collective-permute-start(bf16[48,2048]{1,0:T(8,128)(2,1)} %get-tuple-element.35), channel_id=1, source_target_pairs={{1,2},{2,1},{5,6},{6,5},{9,10},{10,9},{13,14},{14,13},{17,18},{18,... | collective-permute-start | bytes 589832 | tf_op jit(solution)/shard_map/ppermute | solution.py:542
  6.3 4.3 %collective-permute-start.1 = (bf16[48,2048]{1,0:T(8,128)(2,1)}, bf16[48,2048]{1,0:T(8,128)(2,1)S(1)}, u32[]{:S(2)}, u32[]{:S(2)}) collective-permute-start(bf16[48,2048]{1,0:T(8,128)(2,1)} %get-tuple-element.36), channel_id=1, source_target_pairs={{0,1},{1,0},{2,3},{3,2},{4,5},{5,4},{6,7},{7,6},{8,9},{9,8},{10,11... | collective-permute-start | bytes 589832 | tf_op jit(solution)/shard_map/ppermute | solution.py:542
  10.6 1.2 %copy-done = bf16[1,2,128,2048]{3,2,1,0:T(8,128)(2,1)S(1)} copy-done((bf16[1,2,128,2048]{3,2,1,0:T(8,128)(2,1)S(1)}, bf16[1,2,128,2048]{3,2,1,0:T(8,128)(2,1)}, u32[]{:S(2)}) %copy-start) | copy-done | bytes 1048600
  11.8 1.0 %copy-done.3 = bf16[1,128,2048]{2,1,0:T(8,128)(2,1)S(1)} copy-done((bf16[1,128,2048]{2,1,0:T(8,128)(2,1)S(1)}, bf16[1,128,2048]{2,1,0:T(8,128)(2,1)}, u32[]{:S(2)}) %copy-start.3) | copy-done | bytes 524312
  12.8 0.7 %copy-done.9 = s32[8]{0:T(128)S(1)} copy-done((s32[8]{0:T(128)S(1)}, s32[8]{0:T(128)}, u32[]{:S(2)}) %copy-start.9) | copy-done | bytes 56
  13.5 0.0 copy-start.16
  13.5 1.7 %shard_map.211 = (bf16[2,32,2048]{2,1,0:T(8,128)(2,1)S(1)}, bf16[32,2048]{1,0:T(8,128)(2,1)S(1)}, bf16[32,2048]{1,0:T(8,128)(2,1)S(1)}, bf16[64,2048]{1,0:T(8,12...) custom-call(s32[8]{0:T(128)S(1)} %copy-done.9, ...), custom_call_target="tpu_custom_call" | custom-call | tf_op jit(solution)/shard_map/pallas_call | solution.py:497
  15.2 0.7 %collective-permute-start.6 = (bf16[64,2048]{1,0:T(8,128)(2,1)S(1)}, bf16[64,2048]{1,0:T(8,128)(2,1)S(1)}, u32[]{:S(2)}, u32[]{:S(2)}) collective-permute-start(bf16[64,2048]{1,0:T(8,128)(2,1)S(1)} %get-tuple-element.44), channel_id=1, source_target_pairs={{1,2},{2,1},{5,6},{6,5},{9,10},{10,9},{13,14},{14,13},{17,18},{18,... | collective-permute-start | bytes 786440 | tf_op jit(solution)/shard_map/ppermute | solution.py:542
  15.9 2.8 %collective-permute-start.7 = (bf16[64,2048]{1,0:T(8,128)(2,1)S(1)}, bf16[64,2048]{1,0:T(8,128)(2,1)S(1)}, u32[]{:S(2)}, u32[]{:S(2)}) collective-permute-start(bf16[64,2048]{1,0:T(8,128)(2,1)S(1)} %get-tuple-element.45), channel_id=1, source_target_pairs={{0,1},{1,0},{2,3},{3,2},{4,5},{5,4},{6,7},{7,6},{8,9},{9,8},{10,11... | collective-permute-start | bytes 786440 | tf_op jit(solution)/shard_map/ppermute | solution.py:542
  18.7 1.3 %collective-permute-done.1.refs_3_ = bf16[48,2048]{1,0:T(8,128)(2,1)S(1)} collective-permute-done((bf16[48,2048]{1,0:T(8,128)(2,1)}, bf16[48,2048]{1,0:T(8,128)(2,1)S(1)}, u32[]{:S(2)}, u32[]{:S(2)}) %collective-permute-start.1) | collective-permute-done | bytes 196640 | tf_op jit(solution)/shard_map/ppermute | solution.py:542
  20.0 0.0 copy-start.6
  20.1 3.5 %shard_map.212 = (bf16[128,2048]{1,0:T(8,128)(2,1)S(1)}, bf16[16,2048]{1,0:T(8,128)(2,1)S(1)}, bf16[16,2048]{1,0:T(8,128)(2,1)S(1)}, bf16[64,2048]{1,0:T(8,128)(...) custom-call(s32[8]{0:T(128)S(1)} %copy-done.9, bf16[2,128,2048]{2,1,0:T(8,128)(2,1)S(1)} %bitcast.17, ...), custom_call_target="tpu_custom_call" | custom-call | flops 4000000000 | tf_op jit(solution)/shard_map/pallas_call | solution.py:497
  23.6 0.8 %collective-permute-start.4 = (bf16[16,2048]{1,0:T(8,128)(2,1)S(1)}, bf16[16,2048]{1,0:T(8,128)(2,1)S(1)}, u32[]{:S(2)}, u32[]{:S(2)}) collective-permute-start(bf16[16,2048]{1,0:T(8,128)(2,1)S(1)} %get-tuple-element.42), channel_id=1, source_target_pairs={{1,30},{2,29},{5,2},{6,1},{9,6},{10,5},{13,10},{14,9},{17,14},{18,... | collective-permute-start | bytes 196616 | tf_op jit(solution)/shard_map/ppermute | solution.py:542
  24.4 3.9 %collective-permute-start.5 = (bf16[16,2048]{1,0:T(8,128)(2,1)S(1)}, bf16[16,2048]{1,0:T(8,128)(2,1)S(1)}, u32[]{:S(2)}, u32[]{:S(2)}) collective-permute-start(bf16[16,2048]{1,0:T(8,128)(2,1)S(1)} %get-tuple-element.43), channel_id=1, source_target_pairs={{0,29},{1,28},{2,31},{3,30},{4,1},{5,0},{6,3},{7,2},{8,5},{9,4},{1... | collective-permute-start | bytes 196616 | tf_op jit(solution)/shard_map/ppermute | solution.py:542
  28.3 5.0 %collective-permute-done.5.refs_7_.refs_3_ = bf16[16,2048]{1,0:T(8,128)(2,1)S(1)} collective-permute-done((bf16[16,2048]{1,0:T(8,128)(2,1)S(1)}, bf16[16,2048]{1,0:T(8,128)(2,1)S(1)}, u32[]{:S(2)}, u32[]{:S(2)}) %collective-permute-start.5) | collective-permute-done | bytes 65568 | tf_op jit(solution)/shard_map/ppermute | solution.py:542
  33.3 1.0 %shard_map.213.refs_8_ = bf16[32,2048]{1,0:T(8,128)(2,1)S(1)} custom-call(bf16[64,2048]{1,0:T(8,128)(2,1)S(1)} %get-tuple-element.46.refs_0_, bf16[128,2048]{1,0:T(8,128)(2,1)S(1)} %get-tuple-element.38.refs_6_.refs_1_, bf16[128,2048]{1,0:T(8,128)(2,1)S(1)} %get-tuple-element.47.refs_2_, f32[1,2048]{1,0:T(1,128)S(1)} %get-tuple-element.48.refs_3_, ...), custom_call_target="tpu_custom_call" | custom-call | tf_op jit(solution)/shard_map/pallas_call | solution.py:497
  34.3 2.6 %shard_map.214 = (f32[192,2048]{1,0:T(8,128)S(1)}, f32[192,2048]{1,0:T(8,128)S(1)}, f32[160,2048]{1,0:T(8,128)S(1)}, f32[128,2048]{1,0:T(8,128)S(1)}, f32[128,12...) custom-call(s32[8]{0:T(128)S(1)} %copy-done.9, bf16[2,128,2048]{2,1,0:T(8,128)(2,1)S(1)} %bitcast.18, ...), custom_call_target="tpu_custom_call" | custom-call | flops 5000000000 | tf_op jit(solution)/shard_map/pallas_call | solution.py:497
  36.9 1.6 %collective-permute-start.12 = (bf16[64,2048]{1,0:T(8,128)(2,1)S(1)}, bf16[64,2048]{1,0:T(8,128)(2,1)S(1)}, u32[]{:S(2)}, u32[]{:S(2)}) collective-permute-start(bf16[64,2048]{1,0:T(8,128)(2,1)S(1)} %get-tuple-element.55), channel_id=1, source_target_pairs={{0,8},{4,12},{8,16},{12,20},{16,24},{20,28},{24,0},{28,4},{1,9},{5... | collective-permute-start | bytes 786440 | tf_op jit(solution)/shard_map/ppermute | solution.py:530
  38.6 3.4 %collective-permute-done.8.refs_11_.refs_3_ = bf16[32,2048]{1,0:T(8,128)(2,1)S(1)} collective-permute-done((bf16[32,2048]{1,0:T(8,128)(2,1)S(1)}, bf16[32,2048]{1,0:T(8,128)(2,1)S(1)}, u32[]{:S(2)}, u32[]{:S(2)}) %collective-permute-start.8) | collective-permute-done | bytes 131104 | tf_op jit(solution)/shard_map/ppermute | solution.py:530
  42.0 1.4 %shard_map.215 = (bf16[160,2048]{1,0:T(8,128)(2,1)S(1)}, bf16[64,2048]{1,0:T(8,128)(2,1)S(1)}) custom-call(s32[8]{0:T(128)S(1)} %copy-done.10, bf16[128,2048]{1,0:T(8,128)(2,1)S(1)} %collective-permute-done.3.refs_1_.received, bf16[16,2048]{1,0:T(8,128)(2,1)S(1)} %collective-permute-done.4.refs_8_.refs_2_, ...), custom_call_target="tpu_custom_call" | custom-call | flops 2000000000 | tf_op jit(solution)/shard_map/pallas_call | solution.py:497
  43.4 0.0 collective-permute-start.10
  43.5 2.0 %shard_map.219 = bf16[128,2048]{1,0:T(8,128)(2,1)S(1)} custom-call(s32[8]{0:T(128)S(1)} %copy-done.10, bf16[2,128,2048]{2,1,0:T(8,128)(2,1)S(1)} %bitcast.19, bf16[128,2048]{1,0:T(8,128)(2,1)S(1)} %collective-permute-done.3.refs_1_.received, bf16[2,32,2048]{2,1,0:T(8,128)(2,1)S(1)} %get-tuple-element.37.refs_5_.refs_4_.weights, ...), custom_call_target="tpu_custom_call" | custom-call | flops 6000000000 | tf_op jit(solution)/shard_map/pallas_call | solution.py:497
  45.5 1.8 %collective-permute-start.13 = (bf16[128,2048]{1,0:T(8,128)(2,1)S(1)}, bf16[128,2048]{1,0:T(8,128)(2,1)S(1)}, u32[]{:S(2)}, u32[]{:S(2)}) collective-permute-start(bf16[128,2048]{1,0:T(8,128)(2,1)S(1)} %shard_map.219), channel_id=1, source_target_pairs={{0,28},{4,0},{8,4},{12,8},{16,12},{20,16},{24,20},{28,24},{1,29},{... | collective-permute-start | bytes 1572872 | tf_op jit(solution)/shard_map/ppermute | solution.py:530
  47.2 2.6 %collective-permute-done.10.other = bf16[64,2048]{1,0:T(8,128)(2,1)S(1)} collective-permute-done((bf16[64,2048]{1,0:T(8,128)(2,1)S(1)}, bf16[64,2048]{1,0:T(8,128)(2,1)S(1)}, u32[]{:S(2)}, u32[]{:S(2)}) %collective-permute-start.10) | collective-permute-done | bytes 262176 | tf_op jit(solution)/shard_map/ppermute | solution.py:620
  49.8 0.1 shard_map.216.refs_7_.mine
  49.9 1.0 %collective-permute-start.11 = (bf16[64,2048]{1,0:T(8,128)(2,1)S(1)}, bf16[64,2048]{1,0:T(8,128)(2,1)S(1)}, u32[]{:S(2)}, u32[]{:S(2)}) collective-permute-start(bf16[64,2048]{1,0:T(8,128)(2,1)S(1)} %shard_map.216.refs_7_.mine), channel_id=1, source_target_pairs={{0,2},{1,3},{2,0},{3,1},{4,6},{5,7},{6,4},{7,5},{8,10},{9,11},{10,... | collective-permute-start | bytes 786440 | tf_op jit(solution)/shard_map/ppermute | solution.py:620
  50.9 2.8 %shard_map.217.between = bf16[160,2048]{1,0:T(8,128)(2,1)S(1)} custom-call(s32[8]{0:T(128)S(1)} %copy-done.10, bf16[128,2048]{1,0:T(8,128)(2,1)} %collective-permute-done.2.refs_14_.refs_1_, bf16[64,2048]{1,0:T(8,128)(2,1)S(1)} %collective-permute-done.12.refs_2_, bf16[32,2048]{1,0:T(8,128)(2,1)S(1)} %collective-permute-done.8.refs_11_.refs_3_, ...), custom_call_target="tpu_custom_call" | custom-call | flops 10000000000 | tf_op jit(solution)/shard_map/pallas_call | solution.py:497
  53.8 2.0 %shard_map.218.act = bf16[128,2048]{1,0:T(8,128)(2,1)S(1)} custom-call(s32[8]{0:T(128)S(1)} %copy-done.10, bf16[160,2048]{1,0:T(8,128)(2,1)S(1)} %shard_map.217.between, bf16[32,2048]{1,0:T(8,128)(2,1)S(1)} %collective-permute-done.9.refs_12_.layer, bf16[320,160]{1,0:T(8,128)(2,1)S(1)} %copy-done.13, bf16[160,64]{1,0:T(8,128)(2,1)S(1)} %copy-done.17, ...), custom_call_target="tpu_custom_call" | custom-call | flops 10000000000 | tf_op jit(solution)/shard_map/pallas_call | solution.py:497
  55.8 0.6 %collective-permute-done.11.other = bf16[64,2048]{1,0:T(8,128)(2,1)S(1)} collective-permute-done((bf16[64,2048]{1,0:T(8,128)(2,1)S(1)}, bf16[64,2048]{1,0:T(8,128)(2,1)S(1)}, u32[]{:S(2)}, u32[]{:S(2)}) %collective-permute-start.11) | collective-permute-done | bytes 262176 | tf_op jit(solution)/shard_map/ppermute | solution.py:620
  56.4 1.7 %shard_map.220 = (bf16[128,2048]{1,0:T(8,128)(2,1)}, bf16[128,2048]{1,0:T(8,128)(2,1)}, f32[31,2,2048]{2,1,0:T(2,128)}, f32[2,2048]{1,0:T(2,128)}) custom-call(s32[8]{0:T(128)S(1)} %copy-done.10, bf16[64,2048]{1,0:T(8,128)(2,1)S(1)} %shard_map.216.refs_7_.mine, bf16[64,2048]{1,0:T(8,128)(2,1)S(1)} %collective-permute-done.11.other, ...), custom_call_target="tpu_custom_call" | custom-call | tf_op jit(solution)/shard_map/pallas_call | solution.py:497
  (43 shorter events, 0.1 us)
Async XLA Ops:
  0.6 9.9 %copy-start.8 = (bf16[1,2,2048]{2,1,0:T(2,128)(2,1)S(1)}, bf16[1,2,2048]{2,1,0:T(2,128)(2,1)}, u32[]{:S(2)}) copy-start(bf16[1,2,2048]{2,1,0:T(2,128)(2,1)} %param.23) | copy-start | bytes 24580
  0.6 9.9 %copy-start.4 = (bf16[1,2,31,2048]{3,1,2,0:T(2,128)(2,1)S(1)}, bf16[1,2,31,2048]{3,1,2,0:T(2,128)(2,1)}, u32[]{:S(2)}) copy-start(bf16[1,2,31,2048]{3,1,2,0:T(2,128)(2,1)} %param.22) | copy-start | bytes 761860
  0.7 19.3 %collective-permute-start.2 = (bf16[128,2048]{1,0:T(8,128)(2,1)}, bf16[128,2048]{1,0:T(8,128)(2,1)}, u32[]{:S(2)}, u32[]{:S(2)}) collective-permute-start(bf16[128,2048]{1,0:T(8,128)(2,1)} %bitcast.21), channel_id=1, source_target_pairs={{0,8},{4,12},{8,16},{12,20},{16,24},{20,28},{24,0},{28,4},{1,9},{5... | collective-permute-start | bytes 1572872 | tf_op jit(solution)/shard_map/ppermute | solution.py:530
  3.7 16.3 %copy-start.5 = (bf16[384,192]{1,0:T(8,128)(2,1)S(1)}, bf16[384,192]{1,0:T(8,128)(2,1)}, u32[]{:S(2)}) copy-start(bf16[384,192]{1,0:T(8,128)(2,1)} %constant.20.clone.refs_9_.refs_4_.refs_5_) | copy-start | bytes 442372
  5.6 13.1 %collective-permute-start = (bf16[48,2048]{1,0:T(8,128)(2,1)}, bf16[48,2048]{1,0:T(8,128)(2,1)S(1)}, u32[]{:S(2)}, u32[]{:S(2)}) collective-permute-start(bf16[48,2048]{1,0:T(8,128)(2,1)} %get-tuple-element.35), channel_id=1, source_target_pairs={{1,2},{2,1},{5,6},{6,5},{9,10},{10,9},{13,14},{14,13},{17,18},{18,... | collective-permute-start | bytes 589832 | tf_op jit(solution)/shard_map/ppermute | solution.py:542
  6.3 13.7 %collective-permute-start.1 = (bf16[48,2048]{1,0:T(8,128)(2,1)}, bf16[48,2048]{1,0:T(8,128)(2,1)S(1)}, u32[]{:S(2)}, u32[]{:S(2)}) collective-permute-start(bf16[48,2048]{1,0:T(8,128)(2,1)} %get-tuple-element.36), channel_id=1, source_target_pairs={{0,1},{1,0},{2,3},{3,2},{4,5},{5,4},{6,7},{7,6},{8,9},{9,8},{10,11... | collective-permute-start | bytes 589832 | tf_op jit(solution)/shard_map/ppermute | solution.py:542
  10.6 1.2 %copy-start = (bf16[1,2,128,2048]{3,2,1,0:T(8,128)(2,1)S(1)}, bf16[1,2,128,2048]{3,2,1,0:T(8,128)(2,1)}, u32[]{:S(2)}) copy-start(bf16[1,2,128,2048]{3,2,1,0:T(8,128)(2,1)} %param.21) | copy-start | bytes 3145732
  11.8 1.0 %copy-start.3 = (bf16[1,128,2048]{2,1,0:T(8,128)(2,1)S(1)}, bf16[1,128,2048]{2,1,0:T(8,128)(2,1)}, u32[]{:S(2)}) copy-start(bf16[1,128,2048]{2,1,0:T(8,128)(2,1)} %param.19) | copy-start | bytes 1572868
  12.8 0.7 %copy-start.9 = (s32[8]{0:T(128)S(1)}, s32[8]{0:T(128)}, u32[]{:S(2)}) copy-start(s32[8]{0:T(128)} %get-tuple-element.34.notes.refs_0_) | copy-start | bytes 100
  13.5 6.5 %copy-start.2 = (bf16[1,128,2048]{2,1,0:T(8,128)(2,1)S(1)}, bf16[1,128,2048]{2,1,0:T(8,128)(2,1)}, u32[]{:S(2)}) copy-start(bf16[1,128,2048]{2,1,0:T(8,128)(2,1)} %grad.1) | copy-start | bytes 1572868
  13.5 6.5 %copy-start.11 = (bf16[384,160]{1,0:T(8,128)(2,1)S(1)}, bf16[384,160]{1,0:T(8,128)(2,1)}, u32[]{:S(2)}) copy-start(bf16[384,160]{1,0:T(8,128)(2,1)} %constant.23.clone.refs_12_.g_table) | copy-start | bytes 368644
  13.5 6.5 %copy-start.12 = (bf16[320,192]{1,0:T(8,128)(2,1)S(1)}, bf16[320,192]{1,0:T(8,128)(2,1)}, u32[]{:S(2)}) copy-start(bf16[320,192]{1,0:T(8,128)(2,1)} %constant.22.clone.refs_11_.refs_7_.refs_6_) | copy-start | bytes 368644
  13.5 6.5 %copy-start.15 = (bf16[256,192]{1,0:T(8,128)(2,1)S(1)}, bf16[256,192]{1,0:T(8,128)(2,1)}, u32[]{:S(2)}) copy-start(bf16[256,192]{1,0:T(8,128)(2,1)} %constant.24.clone.refs_13_.x_table) | copy-start | bytes 294916
  13.5 6.5 %copy-start.16 = (bf16[192,64]{1,0:T(8,128)(2,1)S(1)}, bf16[192,64]{1,0:T(8,128)(2,1)}, u32[]{:S(2)}) copy-start(bf16[192,64]{1,0:T(8,128)(2,1)} %constant.21.clone.refs_10_.refs_6_.refs_5_) | copy-start | bytes 73732
  15.2 19.1 %collective-permute-start.6 = (bf16[64,2048]{1,0:T(8,128)(2,1)S(1)}, bf16[64,2048]{1,0:T(8,128)(2,1)S(1)}, u32[]{:S(2)}, u32[]{:S(2)}) collective-permute-start(bf16[64,2048]{1,0:T(8,128)(2,1)S(1)} %get-tuple-element.44), channel_id=1, source_target_pairs={{1,2},{2,1},{5,6},{6,5},{9,10},{10,9},{13,14},{14,13},{17,18},{18,... | collective-permute-start | bytes 786440 | tf_op jit(solution)/shard_map/ppermute | solution.py:542
  15.9 18.4 %collective-permute-start.7 = (bf16[64,2048]{1,0:T(8,128)(2,1)S(1)}, bf16[64,2048]{1,0:T(8,128)(2,1)S(1)}, u32[]{:S(2)}, u32[]{:S(2)}) collective-permute-start(bf16[64,2048]{1,0:T(8,128)(2,1)S(1)} %get-tuple-element.45), channel_id=1, source_target_pairs={{0,1},{1,0},{2,3},{3,2},{4,5},{5,4},{6,7},{7,6},{8,9},{9,8},{10,11... | collective-permute-start | bytes 786440 | tf_op jit(solution)/shard_map/ppermute | solution.py:542
  20.0 13.3 %copy-start.6 = (bf16[192,256]{1,0:T(8,128)(2,1)S(1)}, bf16[192,256]{1,0:T(8,128)(2,1)}, u32[]{:S(2)}) copy-start(bf16[192,256]{1,0:T(8,128)(2,1)} %constant.25.clone.refs_5_.refs_9_) | copy-start | bytes 294916
  20.0 13.2 %copy-start.7 = (bf16[64,192]{1,0:T(8,128)(2,1)S(1)}, bf16[64,192]{1,0:T(8,128)(2,1)}, u32[]{:S(2)}) copy-start(bf16[64,192]{1,0:T(8,128)(2,1)} %constant.26.clone.refs_6_.refs_10_) | copy-start | bytes 73732
  23.6 10.8 %copy-start.1 = (bf16[1,2,128,2048]{3,2,1,0:T(8,128)(2,1)S(1)}, bf16[1,2,128,2048]{3,2,1,0:T(8,128)(2,1)}, u32[]{:S(2)}) copy-start(bf16[1,2,128,2048]{3,2,1,0:T(8,128)(2,1)} %param.21) | copy-start | bytes 3145732
  23.6 4.7 %collective-permute-start.4 = (bf16[16,2048]{1,0:T(8,128)(2,1)S(1)}, bf16[16,2048]{1,0:T(8,128)(2,1)S(1)}, u32[]{:S(2)}, u32[]{:S(2)}) collective-permute-start(bf16[16,2048]{1,0:T(8,128)(2,1)S(1)} %get-tuple-element.42), channel_id=1, source_target_pairs={{1,30},{2,29},{5,2},{6,1},{9,6},{10,5},{13,10},{14,9},{17,14},{18,... | collective-permute-start | bytes 196616 | tf_op jit(solution)/shard_map/ppermute | solution.py:542
  24.4 8.9 %collective-permute-start.5 = (bf16[16,2048]{1,0:T(8,128)(2,1)S(1)}, bf16[16,2048]{1,0:T(8,128)(2,1)S(1)}, u32[]{:S(2)}, u32[]{:S(2)}) collective-permute-start(bf16[16,2048]{1,0:T(8,128)(2,1)S(1)} %get-tuple-element.43), channel_id=1, source_target_pairs={{0,29},{1,28},{2,31},{3,30},{4,1},{5,0},{6,3},{7,2},{8,5},{9,4},{1... | collective-permute-start | bytes 196616 | tf_op jit(solution)/shard_map/ppermute | solution.py:542
  28.3 13.7 %collective-permute-start.3 = (bf16[128,2048]{1,0:T(8,128)(2,1)S(1)}, bf16[128,2048]{1,0:T(8,128)(2,1)S(1)}, u32[]{:S(2)}, u32[]{:S(2)}) collective-permute-start(bf16[128,2048]{1,0:T(8,128)(2,1)S(1)} %get-tuple-element.41), channel_id=1, source_target_pairs={{0,28},{4,0},{8,4},{12,8},{16,12},{20,16},{24,20},{28,24},{1,29},{... | collective-permute-start | bytes 1572872 | tf_op jit(solution)/shard_map/ppermute | solution.py:530
  28.3 13.7 %collective-permute-start.8 = (bf16[32,2048]{1,0:T(8,128)(2,1)S(1)}, bf16[32,2048]{1,0:T(8,128)(2,1)S(1)}, u32[]{:S(2)}, u32[]{:S(2)}) collective-permute-start(bf16[32,2048]{1,0:T(8,128)(2,1)S(1)} %get-tuple-element.52), channel_id=1, source_target_pairs={{0,8},{4,12},{8,16},{12,20},{16,24},{20,28},{24,0},{28,4},{1,9},{5... | collective-permute-start | bytes 393224 | tf_op jit(solution)/shard_map/ppermute | solution.py:530
  33.3 8.7 %collective-permute-start.9 = (bf16[32,2048]{1,0:T(8,128)(2,1)S(1)}, bf16[32,2048]{1,0:T(8,128)(2,1)S(1)}, u32[]{:S(2)}, u32[]{:S(2)}) collective-permute-start(bf16[32,2048]{1,0:T(8,128)(2,1)S(1)} %get-tuple-element.53), channel_id=1, source_target_pairs={{0,4},{4,8},{8,12},{12,16},{16,20},{20,24},{24,28},{28,0},{1,5},{5... | collective-permute-start | bytes 393224 | tf_op jit(solution)/shard_map/ppermute | solution.py:530
  34.3 7.7 %copy-start.10 = (s32[8]{0:T(128)S(1)}, s32[8]{0:T(128)}, u32[]{:S(2)}) copy-start(s32[8]{0:T(128)} %get-tuple-element.34.notes.refs_0_) | copy-start | bytes 100
  36.9 14.0 %collective-permute-start.12 = (bf16[64,2048]{1,0:T(8,128)(2,1)S(1)}, bf16[64,2048]{1,0:T(8,128)(2,1)S(1)}, u32[]{:S(2)}, u32[]{:S(2)}) collective-permute-start(bf16[64,2048]{1,0:T(8,128)(2,1)S(1)} %get-tuple-element.55), channel_id=1, source_target_pairs={{0,8},{4,12},{8,16},{12,20},{16,24},{20,28},{24,0},{28,4},{1,9},{5... | collective-permute-start | bytes 786440 | tf_op jit(solution)/shard_map/ppermute | solution.py:530
  43.4 6.4 %collective-permute-start.10 = (bf16[64,2048]{1,0:T(8,128)(2,1)S(1)}, bf16[64,2048]{1,0:T(8,128)(2,1)S(1)}, u32[]{:S(2)}, u32[]{:S(2)}) collective-permute-start(bf16[64,2048]{1,0:T(8,128)(2,1)S(1)} %get-tuple-element.54.mine), channel_id=1, source_target_pairs={{0,1},{1,0},{2,3},{3,2},{4,5},{5,4},{6,7},{7,6},{8,9},{9,8},{10,11... | collective-permute-start | bytes 786440 | tf_op jit(solution)/shard_map/ppermute | solution.py:620
  45.5 10.3 %collective-permute-start.13 = (bf16[128,2048]{1,0:T(8,128)(2,1)S(1)}, bf16[128,2048]{1,0:T(8,128)(2,1)S(1)}, u32[]{:S(2)}, u32[]{:S(2)}) collective-permute-start(bf16[128,2048]{1,0:T(8,128)(2,1)S(1)} %shard_map.219), channel_id=1, source_target_pairs={{0,28},{4,0},{8,4},{12,8},{16,12},{20,16},{24,20},{28,24},{1,29},{... | collective-permute-start | bytes 1572872 | tf_op jit(solution)/shard_map/ppermute | solution.py:530
  49.9 3.8 %copy-start.13 = (bf16[320,160]{1,0:T(8,128)(2,1)S(1)}, bf16[320,160]{1,0:T(8,128)(2,1)}, u32[]{:S(2)}) copy-start(bf16[320,160]{1,0:T(8,128)(2,1)} %constant.27.clone.m_table) | copy-start | bytes 307204
  49.9 3.8 %copy-start.14 = (bf16[256,160]{1,0:T(8,128)(2,1)S(1)}, bf16[256,160]{1,0:T(8,128)(2,1)}, u32[]{:S(2)}) copy-start(bf16[256,160]{1,0:T(8,128)(2,1)} %constant.29.clone.c_table) | copy-start | bytes 245764
  49.9 3.8 %copy-start.17 = (bf16[160,64]{1,0:T(8,128)(2,1)S(1)}, bf16[160,64]{1,0:T(8,128)(2,1)}, u32[]{:S(2)}) copy-start(bf16[160,64]{1,0:T(8,128)(2,1)} %constant.28.clone.q_table) | copy-start | bytes 61444
  49.9 6.4 %collective-permute-start.11 = (bf16[64,2048]{1,0:T(8,128)(2,1)S(1)}, bf16[64,2048]{1,0:T(8,128)(2,1)S(1)}, u32[]{:S(2)}, u32[]{:S(2)}) collective-permute-start(bf16[64,2048]{1,0:T(8,128)(2,1)S(1)} %shard_map.216.refs_7_.mine), channel_id=1, source_target_pairs={{0,2},{1,3},{2,0},{3,1},{4,6},{5,7},{6,4},{7,5},{8,10},{9,11},{10,... | collective-permute-start | bytes 786440 | tf_op jit(solution)/shard_map/ppermute | solution.py:620

commit v16 on v15

--- a/solution.py
+++ b/solution.py
@@ -308,26 +308,33 @@
     out[...] = added(mine, other)
 
 
+def second_early_kernel(notes, saved, weights, q_table, masked, mean, inverse, q):
+    own = masked.shape[0]
+    slot, length, first = looked_up(notes, BACK1)
+    norm_pieces([(saved.at[1], 0, own)], slot_row(weights, slot), first, length, masked, mean, inverse)
+
+    def block(columns):
+        q[:, columns] = tap_spectrum(q_table[...], weights[slot, :, columns])
+
+    each_block(masked.shape[1], block)
+
+
 def second_ready_kernel(
-    reach, notes, saved, far, near, weights, m_table, q_table, c_table,
-    m_out, q_out, factor, conv_out, mean, inverse, ahead, halo, halos, masked,
+    reach, notes, far, near, weights, ahead0, masked, q, m_table, c_table, m_out, factor, conv_out, ahead, halo, halos
 ):
     left, right = sorted_halos(near, far, reach, halos)
     ahead[pl.ds(0, reach), :] = left[...]
     ahead[pl.ds(reach, reach), :] = right[...]
+    ahead[pl.ds(2 * reach, ahead0.shape[0]), :] = ahead0[...]
     own, width = masked.shape
     slot, length, first = looked_up(notes, BACK1)
-    gain = slot_row(weights, slot)
     left, right = sorted_halos(near, far, 0, halos)
-    norm_pieces([(saved.at[1], 0, own)], gain, first, length, masked, mean, inverse)
-    norm_halo(left, right, own, gain, first, length, halo)
+    norm_halo(left, right, own, slot_row(weights, slot), first, length, halo)
 
     def block(columns):
         m = transform(m_table, joined(halo, masked, columns))
-        q = tap_spectrum(q_table[...], weights[slot, :, columns])
-        conv = transform(c_table, product(m, q))
+        conv = transform(c_table, product(m, q[:, columns]))
         m_out[:, columns] = m
-        q_out[:, columns] = q
         factor[:, columns] = gate_factor(conv)
         edge = (conv.shape[0] - own) // 2
         conv_out[:, columns] = conv[edge : edge + own]
@@ -383,11 +390,12 @@
     return lambda columns: layer[last : last + 1, columns].astype(F32)
 
 
-def first_forward_kernel(reach, notes, act, ahead, layer, m_table, q_table, c_table, out, halo, masked):
+def first_forward_kernel(reach, notes, act, ahead, m_table, q_table, c_table, out, halo, masked):
     own, width = act.shape
     middle = reach // 2
     _, length, first = looked_up(notes, AHEAD0)
     left, right = ahead.at[pl.ds(0, reach)], ahead.at[pl.ds(reach, reach)]
+    layer = ahead.at[pl.ds(2 * reach, ahead.shape[0] - 2 * reach)]
     inner = [(left, middle, middle), (act, 0, own), (right, 0, middle)]
     norm_pieces([(act, 0, own)], row_gain(layer), first, length, masked)
     norm_halo(left, right, own, row_gain(layer), first, length, halo)
@@ -577,7 +585,7 @@
         0,
     )
     near1, far1 = swapped(near1, far1)
-    ahead0, ahead1 = shifted(ahead0, 2), shifted(ahead1, 1)
+    ahead1 = shifted(ahead1, 1)
     g_table, x_table = stacked(to_freq(size, span(one, own))), stacked(from_freq(size, span(0, own)))
     grad_mid, near2, far2, halo0, inner0, gain0 = run(
         functools.partial(first_backward_kernel, two),
@@ -599,23 +607,22 @@
         first_taps_kernel, like(tap_count + 1, width, BF16), [],
         [halo0, layer0[0], inner0, gain0, m_table, go_table, t_table],
         0,
-        near2, far2,
-    )
-    halo_scratch = [
-        pltpu.VMEM((2 * two, width), BF16), pltpu.VMEM((2, two, width), BF16), pltpu.VMEM((own, width), BF16)
-    ]
-    m1, q1, factor1, conv1, mean1, inverse1, ahead = run(
+    )
+    masked1, mean1, inverse1, q1 = run(
+        second_early_kernel, (*layer, like(size, width, F32)), [], [notes, saved, weights, q_table], 1, taps0
+    )
+    m1, factor1, conv1, ahead0 = run(
         functools.partial(second_ready_kernel, two),
         (
-            like(size, width, F32), like(size, width, F32), like(small, width, F32), like(own, width, F32),
-            like(own, LANES, F32), like(own, LANES, F32), like(2 * two, width, BF16),
+            like(size, width, F32), like(small, width, F32), like(own, width, F32),
+            like(2 * two + tap_count + 1, width, BF16),
         ),
-        halo_scratch,
-        [notes, saved, far1, near1, weights, m_table, q_table, c_table],
+        [pltpu.VMEM((2 * two, width), BF16), pltpu.VMEM((2, two, width), BF16)],
+        [notes, far1, near1, weights, ahead0, masked1, q1, m_table, c_table],
         5,
-        taps0,
-    )
-    ahead = shifted(ahead, 2)
+        near2, far2,
+    )
+    ahead0 = shifted(ahead0, 2)
     def partner(x, step):
         return lax.ppermute(x, "tm", [(i, i ^ step) for i in range(shards)])
 
@@ -625,7 +632,6 @@
         [pltpu.VMEM((2, one, width), BF16)],
         [notes, grad_mid, far2, near2, weights, m1, factor1, conv1, taps0, go_table, t_table],
         2,
-        ahead0, ahead1,
     )
     grad_out = run(
         second_backward_kernel,
@@ -643,7 +649,7 @@
         functools.partial(first_forward_kernel, two),
         like(small, width, BF16),
         [pltpu.VMEM((2 * two, width), BF16), pltpu.VMEM((own, width), BF16)],
-        [notes, act_ahead, ahead, ahead0, m_table, q_table, c_table],
+        [notes, act_ahead, ahead0, m_table, q_table, c_table],
         10,
         mine,
     )

time: 58.6 us -> 55.8 us (0.952)
  waiting for transfers between devices: 13 us -> 6.21 us
  starting transfers between devices: 20.6 us -> 23.9 us
  Pallas kernels: 20.6 us -> 21.2 us
    ppermute x2, waiting for transfers between devices: 3.22 us -> 0.43 us  [partner(): return lax.ppermute(x, 'tm', [(i, i ^ step) for i in range(shards)])]
    ppermute x6 -> x5, starting transfers between devices: 6.49 us -> 9.2 us  [shifted(): lax.ppermute(x, 'section', [(i, (i + by) % sections) for i in range(secti...]
    ppermute x6, waiting for transfers between devices: 6.33 us -> 3.64 us  [swapped(): results.append(lax.ppermute(x, ('section', 'tm'), pairs))]
    ppermute x6 -> x5, waiting for transfers between devices: 3.44 us -> 2.14 us  [shifted(): lax.ppermute(x, 'section', [(i, (i + by) % sections) for i in range(secti...]
    ppermute x2, starting transfers between devices: 1.02 us -> 1.69 us  [partner(): return lax.ppermute(x, 'tm', [(i, i ^ step) for i in range(shards)])]
    pallas_call x11 -> x12, Pallas kernels: 20.6 us -> 21.2 us  [call(): pl.pallas_call(kernel, out_shape=outs, in_specs=specs, out_specs=jax.tree...]
  transfers between devices with their start and end apart: 14 -> 13, of which waited for: 5 -> 5; matrix products, arithmetic and copies ran while one was open for 0% -> 0% of each run, Pallas kernels for 32% -> 35%
where the time goes in v16:
time: 55.8 us; the launch traced here: 55.4 us
  starting transfers between devices  23.9 us (43%)
  Pallas kernels  21.2 us (38%)
  waiting for transfers between devices  6.21 us (11%)
  local copies, waits for them, and re-layouts  3 us (5%)
  between operations  1.11 us (2%)
    pallas_call x12, Pallas kernels, call(): pl.pallas_call(kernel, out_shape=outs, in_specs=specs, out_specs=jax.tree...  21.2 us
    ppermute x6, starting transfers between devices, swapped(): results.append(lax.ppermute(x, ('section', 'tm'), pairs))  13.1 us
    ppermute x5, starting transfers between devices, shifted(): lax.ppermute(x, 'section', [(i, (i + by) % sections) for i in range(secti...  9.2 us
    ppermute x6, waiting for transfers between devices, swapped(): results.append(lax.ppermute(x, ('section', 'tm'), pairs))  3.64 us
    unnamed x36, local copies, waits for them, and re-layouts  3 us
    ppermute x5, waiting for transfers between devices, shifted(): lax.ppermute(x, 'section', [(i, (i + by) % sections) for i in range(secti...  2.14 us
    ppermute x2, starting transfers between devices, partner(): return lax.ppermute(x, 'tm', [(i, i ^ step) for i in range(shards)])  1.69 us
  transfers between devices with their start and end apart: 13, of which 5 were waited for; matrix products, arithmetic and copies ran while one was open for 0% of the time, Pallas kernels for 35%

profile of v16, /device:TPU:0, one launch (start us, length us, event | category | flops | bytes accessed | tf_op | source)
XLA Modules:
  0.0 55.4 jit_solution(5261076371037173074)
XLA Ops:
  0.7 3.1 %collective-permute-start.2 = (bf16[128,2048]{1,0:T(8,128)(2,1)}, bf16[128,2048]{1,0:T(8,128)(2,1)}, u32[]{:S(2)}, u32[]{:S(2)}) collective-permute-start(bf16[128,2048]{1,0:T(8,128)(2,1)} %bitcast.21), channel_id=1, source_target_pairs={{0,8},{4,12},{8,16},{12,20},{16,24},{20,28},{24,0},{28,4},{1,9},{5... | collective-permute-start | bytes 1572872 | tf_op jit(solution)/shard_map/ppermute | solution.py:538
  3.7 1.9 %shard_map.210 = (bf16[48,2048]{1,0:T(8,128)(2,1)}, bf16[48,2048]{1,0:T(8,128)(2,1)}, s32[8]{0:T(128)}) custom-call(bf16[2,128,2048]{2,1,0:T(8,128)(2,1)} %bitcast.15, bf16[1,128,2048]{2,1,0:T(8,128)(2,1)} %grad.1, s32[8]{0:T(128)} %back_lengths.1, s32[8]{0:T(128)} %ahead_lengths.1, s32[2,8]{1,0:T(2,128)} %bitcast.25, s32[2,8]{1,0:T(2,128)} %bitcast.26), custom_call_target="tpu_custom_call" | custom-call | tf_op jit(solution)/shard_map/pallas_call | solution.py:505
  5.6 0.7 %collective-permute-start = (bf16[48,2048]{1,0:T(8,128)(2,1)}, bf16[48,2048]{1,0:T(8,128)(2,1)S(1)}, u32[]{:S(2)}, u32[]{:S(2)}) collective-permute-start(bf16[48,2048]{1,0:T(8,128)(2,1)} %get-tuple-element.36), channel_id=1, source_target_pairs={{1,2},{2,1},{5,6},{6,5},{9,10},{10,9},{13,14},{14,13},{17,18},{18,... | collective-permute-start | bytes 589832 | tf_op jit(solution)/shard_map/ppermute | solution.py:550
  6.3 4.3 %collective-permute-start.1 = (bf16[48,2048]{1,0:T(8,128)(2,1)}, bf16[48,2048]{1,0:T(8,128)(2,1)S(1)}, u32[]{:S(2)}, u32[]{:S(2)}) collective-permute-start(bf16[48,2048]{1,0:T(8,128)(2,1)} %get-tuple-element.37), channel_id=1, source_target_pairs={{0,1},{1,0},{2,3},{3,2},{4,5},{5,4},{6,7},{7,6},{8,9},{9,8},{10,11... | collective-permute-start | bytes 589832 | tf_op jit(solution)/shard_map/ppermute | solution.py:550
  10.6 1.2 %copy-done = bf16[1,2,128,2048]{3,2,1,0:T(8,128)(2,1)S(1)} copy-done((bf16[1,2,128,2048]{3,2,1,0:T(8,128)(2,1)S(1)}, bf16[1,2,128,2048]{3,2,1,0:T(8,128)(2,1)}, u32[]{:S(2)}) %copy-start) | copy-done | bytes 1048600
  11.8 1.0 %copy-done.3 = bf16[1,128,2048]{2,1,0:T(8,128)(2,1)S(1)} copy-done((bf16[1,128,2048]{2,1,0:T(8,128)(2,1)S(1)}, bf16[1,128,2048]{2,1,0:T(8,128)(2,1)}, u32[]{:S(2)}) %copy-start.3) | copy-done | bytes 524312
  12.8 0.7 %copy-done.9 = s32[8]{0:T(128)S(1)} copy-done((s32[8]{0:T(128)S(1)}, s32[8]{0:T(128)}, u32[]{:S(2)}) %copy-start.9) | copy-done | bytes 56
  13.5 1.7 %shard_map.211 = (bf16[2,32,2048]{2,1,0:T(8,128)(2,1)S(1)}, bf16[32,2048]{1,0:T(8,128)(2,1)S(1)}, bf16[32,2048]{1,0:T(8,128)(2,1)S(1)}, bf16[64,2048]{1,0:T(8,12...) custom-call(s32[8]{0:T(128)S(1)} %copy-done.9, ...), custom_call_target="tpu_custom_call" | custom-call | tf_op jit(solution)/shard_map/pallas_call | solution.py:505
  15.2 0.7 %collective-permute-start.6 = (bf16[64,2048]{1,0:T(8,128)(2,1)S(1)}, bf16[64,2048]{1,0:T(8,128)(2,1)S(1)}, u32[]{:S(2)}, u32[]{:S(2)}) collective-permute-start(bf16[64,2048]{1,0:T(8,128)(2,1)S(1)} %get-tuple-element.45), channel_id=1, source_target_pairs={{1,2},{2,1},{5,6},{6,5},{9,10},{10,9},{13,14},{14,13},{17,18},{18,... | collective-permute-start | bytes 786440 | tf_op jit(solution)/shard_map/ppermute | solution.py:550
  15.9 2.8 %collective-permute-start.7 = (bf16[64,2048]{1,0:T(8,128)(2,1)S(1)}, bf16[64,2048]{1,0:T(8,128)(2,1)S(1)}, u32[]{:S(2)}, u32[]{:S(2)}) collective-permute-start(bf16[64,2048]{1,0:T(8,128)(2,1)S(1)} %get-tuple-element.46), channel_id=1, source_target_pairs={{0,1},{1,0},{2,3},{3,2},{4,5},{5,4},{6,7},{7,6},{8,9},{9,8},{10,11... | collective-permute-start | bytes 786440 | tf_op jit(solution)/shard_map/ppermute | solution.py:550
  18.7 1.3 %collective-permute-done.1.refs_3_ = bf16[48,2048]{1,0:T(8,128)(2,1)S(1)} collective-permute-done((bf16[48,2048]{1,0:T(8,128)(2,1)}, bf16[48,2048]{1,0:T(8,128)(2,1)S(1)}, u32[]{:S(2)}, u32[]{:S(2)}) %collective-permute-start.1) | collective-permute-done | bytes 196640 | tf_op jit(solution)/shard_map/ppermute | solution.py:550
  20.1 3.5 %shard_map.212 = (bf16[128,2048]{1,0:T(8,128)(2,1)S(1)}, bf16[16,2048]{1,0:T(8,128)(2,1)S(1)}, bf16[16,2048]{1,0:T(8,128)(2,1)S(1)}, bf16[64,2048]{1,0:T(8,128)(...) custom-call(s32[8]{0:T(128)S(1)} %copy-done.10, bf16[2,128,2048]{2,1,0:T(8,128)(2,1)S(1)} %bitcast.17, ...), custom_call_target="tpu_custom_call" | custom-call | flops 4000000000 | tf_op jit(solution)/shard_map/pallas_call | solution.py:505
  23.6 0.8 %collective-permute-start.4 = (bf16[16,2048]{1,0:T(8,128)(2,1)S(1)}, bf16[16,2048]{1,0:T(8,128)(2,1)S(1)}, u32[]{:S(2)}, u32[]{:S(2)}) collective-permute-start(bf16[16,2048]{1,0:T(8,128)(2,1)S(1)} %get-tuple-element.43), channel_id=1, source_target_pairs={{1,30},{2,29},{5,2},{6,1},{9,6},{10,5},{13,10},{14,9},{17,14},{18,... | collective-permute-start | bytes 196616 | tf_op jit(solution)/shard_map/ppermute | solution.py:550
  24.4 3.9 %collective-permute-start.5 = (bf16[16,2048]{1,0:T(8,128)(2,1)S(1)}, bf16[16,2048]{1,0:T(8,128)(2,1)S(1)}, u32[]{:S(2)}, u32[]{:S(2)}) collective-permute-start(bf16[16,2048]{1,0:T(8,128)(2,1)S(1)} %get-tuple-element.44), channel_id=1, source_target_pairs={{0,29},{1,28},{2,31},{3,30},{4,1},{5,0},{6,3},{7,2},{8,5},{9,4},{1... | collective-permute-start | bytes 196616 | tf_op jit(solution)/shard_map/ppermute | solution.py:550
  28.3 1.0 %shard_map.213.refs_4_.taps0 = bf16[32,2048]{1,0:T(8,128)(2,1)S(1)} custom-call(bf16[64,2048]{1,0:T(8,128)(2,1)S(1)} %get-tuple-element.48.halo, bf16[128,2048]{1,0:T(8,128)(2,1)S(1)} %get-tuple-element.39.refs_6_.masked, bf16[128,2048]{1,0:T(8,128)(2,1)S(1)} %get-tuple-element.49.inner, f32[1,2048]{1,0:T(1,128)S(1)} %get-tuple-element.50.gain_sum, ...), custom_call_target="tpu_custom_call" | custom-call | tf_op jit(solution)/shard_map/pallas_call | solution.py:505
  29.3 1.1 %shard_map.214 = (bf16[128,2048]{1,0:T(8,128)(2,1)S(1)}, f32[128,128]{1,0:T(8,128)S(1)}, f32[128,128]{1,0:T(8,128)S(1)}, f32[192,2048]{1,0:T(8,128)S(1)}) custom-call(s32[8]{0:T(128)S(1)} %copy-done.10, bf16[2,128,2048]{2,1,0:T(8,128)(2,1)S(1)} %bitcast.18, bf16[2,32,2048]{2,1,0:T(8,128)(2,1)S(1)} %get-tuple-element.38.refs_5_.refs_2_.refs_3_.weights, ...), custom_call_target="tpu_custom_call" | custom-call | flops 1000000000 | tf_op jit(solution)/shard_map/pallas_call | solution.py:505
  30.4 0.6 %collective-permute-start.11 = (bf16[32,2048]{1,0:T(8,128)(2,1)S(1)}, bf16[32,2048]{1,0:T(8,128)(2,1)S(1)}, u32[]{:S(2)}, u32[]{:S(2)}) collective-permute-start(bf16[32,2048]{1,0:T(8,128)(2,1)S(1)} %get-tuple-element.58), channel_id=1, source_target_pairs={{0,4},{4,8},{8,12},{12,16},{16,20},{20,24},{24,28},{28,0},{1,5},{5... | collective-permute-start | bytes 393224 | tf_op jit(solution)/shard_map/ppermute | solution.py:538
  31.0 1.9 %collective-permute-done.7.refs_2_ = bf16[64,2048]{1,0:T(8,128)(2,1)S(1)} collective-permute-done((bf16[64,2048]{1,0:T(8,128)(2,1)S(1)}, bf16[64,2048]{1,0:T(8,128)(2,1)S(1)}, u32[]{:S(2)}, u32[]{:S(2)}) %collective-permute-start.7) | collective-permute-done | bytes 262176 | tf_op jit(solution)/shard_map/ppermute | solution.py:550
  32.8 0.5 collective-permute-done.5.refs_9_.near
  33.3 2.1 %shard_map.215 = (f32[192,2048]{1,0:T(8,128)S(1)}, f32[160,2048]{1,0:T(8,128)S(1)}, f32[128,2048]{1,0:T(8,128)S(1)}, bf16[96,2048]{1,0:T(8,128)(2,1)S(1)}) custom-call(s32[8]{0:T(128)S(1)} %copy-done.10, bf16[64,2048]{1,0:T(8,128)(2,1)S(1)} %collective-permute-done.6.refs_1_, bf16[64,2048]{1,0:T(8,128)(2,1)S(1)} %collective-permute-done.7.refs_2_, ...), custom_call_target="tpu_custom_call" | custom-call | flops 5000000000 | tf_op jit(solution)/shard_map/pallas_call | solution.py:505
  35.4 1.6 %collective-permute-start.10 = (bf16[96,2048]{1,0:T(8,128)(2,1)S(1)}, bf16[96,2048]{1,0:T(8,128)(2,1)S(1)}, u32[]{:S(2)}, u32[]{:S(2)}) collective-permute-start(bf16[96,2048]{1,0:T(8,128)(2,1)S(1)} %get-tuple-element.57), channel_id=1, source_target_pairs={{0,8},{4,12},{8,16},{12,20},{16,24},{20,28},{24,0},{28,4},{1,9},{5... | collective-permute-start | bytes 1179656 | tf_op jit(solution)/shard_map/ppermute | solution.py:538
  37.0 2.1 %collective-permute-done.3.received = bf16[128,2048]{1,0:T(8,128)(2,1)S(1)} collective-permute-done((bf16[128,2048]{1,0:T(8,128)(2,1)S(1)}, bf16[128,2048]{1,0:T(8,128)(2,1)S(1)}, u32[]{:S(2)}, u32[]{:S(2)}) %collective-permute-start.3) | collective-permute-done | bytes 524320 | tf_op jit(solution)/shard_map/ppermute | solution.py:538
  39.2 1.4 %shard_map.216 = (bf16[160,2048]{1,0:T(8,128)(2,1)S(1)}, bf16[64,2048]{1,0:T(8,128)(2,1)S(1)}) custom-call(s32[8]{0:T(128)S(1)} %copy-done.10, bf16[128,2048]{1,0:T(8,128)(2,1)S(1)} %collective-permute-done.3.received, bf16[16,2048]{1,0:T(8,128)(2,1)S(1)} %collective-permute-done.4.refs_10_.far, bf16[16,2048]{1,0:T(8,128)(2,1)S(1)} %collective-permute-done.5.refs_9_.near, ...), custom_call_target="tpu_custom_call" | custom-call | flops 2000000000 | tf_op jit(solution)/shard_map/pallas_call | solution.py:505
  40.6 0.0 collective-permute-start.8
  40.6 2.0 %shard_map.220 = bf16[128,2048]{1,0:T(8,128)(2,1)S(1)} custom-call(s32[8]{0:T(128)S(1)} %copy-done.10, bf16[2,128,2048]{2,1,0:T(8,128)(2,1)S(1)} %bitcast.19, bf16[128,2048]{1,0:T(8,128)(2,1)S(1)} %collective-permute-done.3.received, bf16[2,32,2048]{2,1,0:T(8,128)(2,1)S(1)} %get-tuple-element.38.refs_5_.refs_2_.refs_3_.weights, ...), custom_call_target="tpu_custom_call" | custom-call | flops 6000000000 | tf_op jit(solution)/shard_map/pallas_call | solution.py:505
  42.6 3.9 %collective-permute-start.12 = (bf16[128,2048]{1,0:T(8,128)(2,1)S(1)}, bf16[128,2048]{1,0:T(8,128)(2,1)S(1)}, u32[]{:S(2)}, u32[]{:S(2)}) collective-permute-start(bf16[128,2048]{1,0:T(8,128)(2,1)S(1)} %shard_map.220), channel_id=1, source_target_pairs={{0,28},{4,0},{8,4},{12,8},{16,12},{20,16},{24,20},{28,24},{1,29},{... | collective-permute-start | bytes 1572872 | tf_op jit(solution)/shard_map/ppermute | solution.py:538
  46.5 0.4 collective-permute-done.8.other
  47.0 0.1 shard_map.217.refs_6_.mine
  47.1 1.6 %collective-permute-start.9 = (bf16[64,2048]{1,0:T(8,128)(2,1)S(1)}, bf16[64,2048]{1,0:T(8,128)(2,1)S(1)}, u32[]{:S(2)}, u32[]{:S(2)}) collective-permute-start(bf16[64,2048]{1,0:T(8,128)(2,1)S(1)} %shard_map.217.refs_6_.mine), channel_id=1, source_target_pairs={{0,2},{1,3},{2,0},{3,1},{4,6},{5,7},{6,4},{7,5},{8,10},{9,11},{10,... | collective-permute-start | bytes 786440 | tf_op jit(solution)/shard_map/ppermute | solution.py:627
  48.7 2.8 %shard_map.218.between = bf16[160,2048]{1,0:T(8,128)(2,1)S(1)} custom-call(s32[8]{0:T(128)S(1)} %copy-done.10, bf16[128,2048]{1,0:T(8,128)(2,1)} %collective-permute-done.2.refs_14_.refs_1_, bf16[96,2048]{1,0:T(8,128)(2,1)S(1)} %collective-permute-done.10.refs_2_, bf16[384,192]{1,0:T(8,128)(2,1)S(1)} %copy-done.5, bf16[192,64]{1,0:T(8,128)(2,1)S(1)} %copy-done.16, ...), custom_call_target="tpu_custom_call" | custom-call | flops 10000000000 | tf_op jit(solution)/shard_map/pallas_call | solution.py:505
  51.6 2.0 %shard_map.219.act = bf16[128,2048]{1,0:T(8,128)(2,1)S(1)} custom-call(s32[8]{0:T(128)S(1)} %copy-done.10, bf16[160,2048]{1,0:T(8,128)(2,1)S(1)} %shard_map.218.between, bf16[32,2048]{1,0:T(8,128)(2,1)S(1)} %collective-permute-done.11.layer, bf16[320,160]{1,0:T(8,128)(2,1)S(1)} %copy-done.12, bf16[160,64]{1,0:T(8,128)(2,1)S(1)} %copy-done.17, ...), custom_call_target="tpu_custom_call" | custom-call | flops 10000000000 | tf_op jit(solution)/shard_map/pallas_call | solution.py:505
  53.6 1.7 %shard_map.221 = (bf16[128,2048]{1,0:T(8,128)(2,1)}, bf16[128,2048]{1,0:T(8,128)(2,1)}, f32[31,2,2048]{2,1,0:T(2,128)}, f32[2,2048]{1,0:T(2,128)}) custom-call(s32[8]{0:T(128)S(1)} %copy-done.10, bf16[64,2048]{1,0:T(8,128)(2,1)S(1)} %shard_map.217.refs_6_.mine, bf16[64,2048]{1,0:T(8,128)(2,1)S(1)} %collective-permute-done.9.other, ...), custom_call_target="tpu_custom_call" | custom-call | tf_op jit(solution)/shard_map/pallas_call | solution.py:505
  (42 shorter events, 0.1 us)
Async XLA Ops:
  0.6 9.9 %copy-start.8 = (bf16[1,2,2048]{2,1,0:T(2,128)(2,1)S(1)}, bf16[1,2,2048]{2,1,0:T(2,128)(2,1)}, u32[]{:S(2)}) copy-start(bf16[1,2,2048]{2,1,0:T(2,128)(2,1)} %param.23) | copy-start | bytes 24580
  0.6 9.9 %copy-start.4 = (bf16[1,2,31,2048]{3,1,2,0:T(2,128)(2,1)S(1)}, bf16[1,2,31,2048]{3,1,2,0:T(2,128)(2,1)}, u32[]{:S(2)}) copy-start(bf16[1,2,31,2048]{3,1,2,0:T(2,128)(2,1)} %param.22) | copy-start | bytes 761860
  0.7 19.3 %collective-permute-start.2 = (bf16[128,2048]{1,0:T(8,128)(2,1)}, bf16[128,2048]{1,0:T(8,128)(2,1)}, u32[]{:S(2)}, u32[]{:S(2)}) collective-permute-start(bf16[128,2048]{1,0:T(8,128)(2,1)} %bitcast.21), channel_id=1, source_target_pairs={{0,8},{4,12},{8,16},{12,20},{16,24},{20,28},{24,0},{28,4},{1,9},{5... | collective-permute-start | bytes 1572872 | tf_op jit(solution)/shard_map/ppermute | solution.py:538
  3.7 16.3 %copy-start.5 = (bf16[384,192]{1,0:T(8,128)(2,1)S(1)}, bf16[384,192]{1,0:T(8,128)(2,1)}, u32[]{:S(2)}) copy-start(bf16[384,192]{1,0:T(8,128)(2,1)} %constant.20.clone.refs_9_.m_table.refs_7_.refs_3_) | copy-start | bytes 442372
  5.6 14.4 %copy-start.10 = (s32[8]{0:T(128)S(1)}, s32[8]{0:T(128)}, u32[]{:S(2)}) copy-start(s32[8]{0:T(128)} %get-tuple-element.35.notes.refs_0_) | copy-start | bytes 100
  5.6 13.1 %collective-permute-start = (bf16[48,2048]{1,0:T(8,128)(2,1)}, bf16[48,2048]{1,0:T(8,128)(2,1)S(1)}, u32[]{:S(2)}, u32[]{:S(2)}) collective-permute-start(bf16[48,2048]{1,0:T(8,128)(2,1)} %get-tuple-element.36), channel_id=1, source_target_pairs={{1,2},{2,1},{5,6},{6,5},{9,10},{10,9},{13,14},{14,13},{17,18},{18,... | collective-permute-start | bytes 589832 | tf_op jit(solution)/shard_map/ppermute | solution.py:550
  6.3 13.7 %collective-permute-start.1 = (bf16[48,2048]{1,0:T(8,128)(2,1)}, bf16[48,2048]{1,0:T(8,128)(2,1)S(1)}, u32[]{:S(2)}, u32[]{:S(2)}) collective-permute-start(bf16[48,2048]{1,0:T(8,128)(2,1)} %get-tuple-element.37), channel_id=1, source_target_pairs={{0,1},{1,0},{2,3},{3,2},{4,5},{5,4},{6,7},{7,6},{8,9},{9,8},{10,11... | collective-permute-start | bytes 589832 | tf_op jit(solution)/shard_map/ppermute | solution.py:550
  10.6 1.2 %copy-start = (bf16[1,2,128,2048]{3,2,1,0:T(8,128)(2,1)S(1)}, bf16[1,2,128,2048]{3,2,1,0:T(8,128)(2,1)}, u32[]{:S(2)}) copy-start(bf16[1,2,128,2048]{3,2,1,0:T(8,128)(2,1)} %param.21) | copy-start | bytes 3145732
  11.8 1.0 %copy-start.3 = (bf16[1,128,2048]{2,1,0:T(8,128)(2,1)S(1)}, bf16[1,128,2048]{2,1,0:T(8,128)(2,1)}, u32[]{:S(2)}) copy-start(bf16[1,128,2048]{2,1,0:T(8,128)(2,1)} %param.19) | copy-start | bytes 1572868
  12.8 0.7 %copy-start.9 = (s32[8]{0:T(128)S(1)}, s32[8]{0:T(128)}, u32[]{:S(2)}) copy-start(s32[8]{0:T(128)} %get-tuple-element.35.notes.refs_0_) | copy-start | bytes 100
  13.5 6.5 %copy-start.2 = (bf16[1,128,2048]{2,1,0:T(8,128)(2,1)S(1)}, bf16[1,128,2048]{2,1,0:T(8,128)(2,1)}, u32[]{:S(2)}) copy-start(bf16[1,128,2048]{2,1,0:T(8,128)(2,1)} %grad.1) | copy-start | bytes 1572868
  13.5 6.5 %copy-start.11 = (bf16[384,160]{1,0:T(8,128)(2,1)S(1)}, bf16[384,160]{1,0:T(8,128)(2,1)}, u32[]{:S(2)}) copy-start(bf16[384,160]{1,0:T(8,128)(2,1)} %constant.23.clone.refs_12_.g_table) | copy-start | bytes 368644
  13.5 6.5 %copy-start.13 = (bf16[320,192]{1,0:T(8,128)(2,1)S(1)}, bf16[320,192]{1,0:T(8,128)(2,1)}, u32[]{:S(2)}) copy-start(bf16[320,192]{1,0:T(8,128)(2,1)} %constant.22.clone.refs_11_.refs_8_.refs_5_) | copy-start | bytes 368644
  13.5 6.5 %copy-start.15 = (bf16[256,192]{1,0:T(8,128)(2,1)S(1)}, bf16[256,192]{1,0:T(8,128)(2,1)}, u32[]{:S(2)}) copy-start(bf16[256,192]{1,0:T(8,128)(2,1)} %constant.24.clone.refs_13_.x_table) | copy-start | bytes 294916
  13.5 6.5 %copy-start.16 = (bf16[192,64]{1,0:T(8,128)(2,1)S(1)}, bf16[192,64]{1,0:T(8,128)(2,1)}, u32[]{:S(2)}) copy-start(bf16[192,64]{1,0:T(8,128)(2,1)} %constant.21.clone.refs_10_.refs_3_.refs_4_) | copy-start | bytes 73732
  15.2 15.2 %collective-permute-start.6 = (bf16[64,2048]{1,0:T(8,128)(2,1)S(1)}, bf16[64,2048]{1,0:T(8,128)(2,1)S(1)}, u32[]{:S(2)}, u32[]{:S(2)}) collective-permute-start(bf16[64,2048]{1,0:T(8,128)(2,1)S(1)} %get-tuple-element.45), channel_id=1, source_target_pairs={{1,2},{2,1},{5,6},{6,5},{9,10},{10,9},{13,14},{14,13},{17,18},{18,... | collective-permute-start | bytes 786440 | tf_op jit(solution)/shard_map/ppermute | solution.py:550
  15.9 16.9 %collective-permute-start.7 = (bf16[64,2048]{1,0:T(8,128)(2,1)S(1)}, bf16[64,2048]{1,0:T(8,128)(2,1)S(1)}, u32[]{:S(2)}, u32[]{:S(2)}) collective-permute-start(bf16[64,2048]{1,0:T(8,128)(2,1)S(1)} %get-tuple-element.46), channel_id=1, source_target_pairs={{0,1},{1,0},{2,3},{3,2},{4,5},{5,4},{6,7},{7,6},{8,9},{9,8},{10,11... | collective-permute-start | bytes 786440 | tf_op jit(solution)/shard_map/ppermute | solution.py:550
  20.1 8.2 %copy-start.6 = (bf16[192,256]{1,0:T(8,128)(2,1)S(1)}, bf16[192,256]{1,0:T(8,128)(2,1)}, u32[]{:S(2)}) copy-start(bf16[192,256]{1,0:T(8,128)(2,1)} %constant.25.clone.go_table) | copy-start | bytes 294916
  20.1 8.2 %copy-start.7 = (bf16[64,192]{1,0:T(8,128)(2,1)S(1)}, bf16[64,192]{1,0:T(8,128)(2,1)}, u32[]{:S(2)}) copy-start(bf16[64,192]{1,0:T(8,128)(2,1)} %constant.26.clone.t_table) | copy-start | bytes 73732
  23.6 5.7 %copy-start.1 = (bf16[1,2,128,2048]{3,2,1,0:T(8,128)(2,1)S(1)}, bf16[1,2,128,2048]{3,2,1,0:T(8,128)(2,1)}, u32[]{:S(2)}) copy-start(bf16[1,2,128,2048]{3,2,1,0:T(8,128)(2,1)} %param.21) | copy-start | bytes 3145732
  23.6 9.2 %collective-permute-start.4 = (bf16[16,2048]{1,0:T(8,128)(2,1)S(1)}, bf16[16,2048]{1,0:T(8,128)(2,1)S(1)}, u32[]{:S(2)}, u32[]{:S(2)}) collective-permute-start(bf16[16,2048]{1,0:T(8,128)(2,1)S(1)} %get-tuple-element.43), channel_id=1, source_target_pairs={{1,30},{2,29},{5,2},{6,1},{9,6},{10,5},{13,10},{14,9},{17,14},{18,... | collective-permute-start | bytes 196616 | tf_op jit(solution)/shard_map/ppermute | solution.py:550
  24.4 8.9 %collective-permute-start.5 = (bf16[16,2048]{1,0:T(8,128)(2,1)S(1)}, bf16[16,2048]{1,0:T(8,128)(2,1)S(1)}, u32[]{:S(2)}, u32[]{:S(2)}) collective-permute-start(bf16[16,2048]{1,0:T(8,128)(2,1)S(1)} %get-tuple-element.44), channel_id=1, source_target_pairs={{0,29},{1,28},{2,31},{3,30},{4,1},{5,0},{6,3},{7,2},{8,5},{9,4},{1... | collective-permute-start | bytes 196616 | tf_op jit(solution)/shard_map/ppermute | solution.py:550
  28.3 10.9 %collective-permute-start.3 = (bf16[128,2048]{1,0:T(8,128)(2,1)S(1)}, bf16[128,2048]{1,0:T(8,128)(2,1)S(1)}, u32[]{:S(2)}, u32[]{:S(2)}) collective-permute-start(bf16[128,2048]{1,0:T(8,128)(2,1)S(1)} %get-tuple-element.42), channel_id=1, source_target_pairs={{0,28},{4,0},{8,4},{12,8},{16,12},{20,16},{24,20},{28,24},{1,29},{... | collective-permute-start | bytes 1572872 | tf_op jit(solution)/shard_map/ppermute | solution.py:538
  30.4 21.1 %collective-permute-start.11 = (bf16[32,2048]{1,0:T(8,128)(2,1)S(1)}, bf16[32,2048]{1,0:T(8,128)(2,1)S(1)}, u32[]{:S(2)}, u32[]{:S(2)}) collective-permute-start(bf16[32,2048]{1,0:T(8,128)(2,1)S(1)} %get-tuple-element.58), channel_id=1, source_target_pairs={{0,4},{4,8},{8,12},{12,16},{16,20},{20,24},{24,28},{28,0},{1,5},{5... | collective-permute-start | bytes 393224 | tf_op jit(solution)/shard_map/ppermute | solution.py:538
  35.4 13.3 %collective-permute-start.10 = (bf16[96,2048]{1,0:T(8,128)(2,1)S(1)}, bf16[96,2048]{1,0:T(8,128)(2,1)S(1)}, u32[]{:S(2)}, u32[]{:S(2)}) collective-permute-start(bf16[96,2048]{1,0:T(8,128)(2,1)S(1)} %get-tuple-element.57), channel_id=1, source_target_pairs={{0,8},{4,12},{8,16},{12,20},{16,24},{20,28},{24,0},{28,4},{1,9},{5... | collective-permute-start | bytes 1179656 | tf_op jit(solution)/shard_map/ppermute | solution.py:538
  40.6 6.4 %collective-permute-start.8 = (bf16[64,2048]{1,0:T(8,128)(2,1)S(1)}, bf16[64,2048]{1,0:T(8,128)(2,1)S(1)}, u32[]{:S(2)}, u32[]{:S(2)}) collective-permute-start(bf16[64,2048]{1,0:T(8,128)(2,1)S(1)} %get-tuple-element.56.mine), channel_id=1, source_target_pairs={{0,1},{1,0},{2,3},{3,2},{4,5},{5,4},{6,7},{7,6},{8,9},{9,8},{10,11... | collective-permute-start | bytes 786440 | tf_op jit(solution)/shard_map/ppermute | solution.py:627
  42.6 10.9 %collective-permute-start.12 = (bf16[128,2048]{1,0:T(8,128)(2,1)S(1)}, bf16[128,2048]{1,0:T(8,128)(2,1)S(1)}, u32[]{:S(2)}, u32[]{:S(2)}) collective-permute-start(bf16[128,2048]{1,0:T(8,128)(2,1)S(1)} %shard_map.220), channel_id=1, source_target_pairs={{0,28},{4,0},{8,4},{12,8},{16,12},{20,16},{24,20},{28,24},{1,29},{... | collective-permute-start | bytes 1572872 | tf_op jit(solution)/shard_map/ppermute | solution.py:538
  47.0 4.5 %copy-start.12 = (bf16[320,160]{1,0:T(8,128)(2,1)S(1)}, bf16[320,160]{1,0:T(8,128)(2,1)}, u32[]{:S(2)}) copy-start(bf16[320,160]{1,0:T(8,128)(2,1)} %constant.27.clone.m_table) | copy-start | bytes 307204
  47.0 4.5 %copy-start.14 = (bf16[256,160]{1,0:T(8,128)(2,1)S(1)}, bf16[256,160]{1,0:T(8,128)(2,1)}, u32[]{:S(2)}) copy-start(bf16[256,160]{1,0:T(8,128)(2,1)} %constant.29.clone.c_table) | copy-start | bytes 245764
  47.1 4.5 %copy-start.17 = (bf16[160,64]{1,0:T(8,128)(2,1)S(1)}, bf16[160,64]{1,0:T(8,128)(2,1)}, u32[]{:S(2)}) copy-start(bf16[160,64]{1,0:T(8,128)(2,1)} %constant.28.clone.q_table) | copy-start | bytes 61444
  47.1 6.5 %collective-permute-start.9 = (bf16[64,2048]{1,0:T(8,128)(2,1)S(1)}, bf16[64,2048]{1,0:T(8,128)(2,1)S(1)}, u32[]{:S(2)}, u32[]{:S(2)}) collective-permute-start(bf16[64,2048]{1,0:T(8,128)(2,1)S(1)} %shard_map.217.refs_6_.mine), channel_id=1, source_target_pairs={{0,2},{1,3},{2,0},{3,1},{4,6},{5,7},{6,4},{7,5},{8,10},{9,11},{10,... | collective-permute-start | bytes 786440 | tf_op jit(solution)/shard_map/ppermute | solution.py:627

commit v17 on v16

--- a/solution.py
+++ b/solution.py
@@ -620,7 +620,6 @@
         [pltpu.VMEM((2 * two, width), BF16), pltpu.VMEM((2, two, width), BF16)],
         [notes, far1, near1, weights, ahead0, masked1, q1, m_table, c_table],
         5,
-        near2, far2,
     )
     ahead0 = shifted(ahead0, 2)
     def partner(x, step):

time: 55.8 us -> 56.2 us (level)
  starting transfers between devices: 23.9 us -> 25.3 us
  waiting for transfers between devices: 6.21 us -> 5.26 us
    ppermute x2, waiting for transfers between devices: 0.43 us -> 3.38 us  [partner(): return lax.ppermute(x, 'tm', [(i, i ^ step) for i in range(shards)])]
    ppermute x6, waiting for transfers between devices: 3.64 us -> 1.12 us  [swapped(): results.append(lax.ppermute(x, ('section', 'tm'), pairs))]
    ppermute x5, starting transfers between devices: 9.2 us -> 10.7 us  [shifted(): lax.ppermute(x, 'section', [(i, (i + by) % sections) for i in range(secti...]
    ppermute x5, waiting for transfers between devices: 2.14 us -> 0.77 us  [shifted(): lax.ppermute(x, 'section', [(i, (i + by) % sections) for i in range(secti...]
    ppermute x6, starting transfers between devices: 13.1 us -> 11.7 us  [swapped(): results.append(lax.ppermute(x, ('section', 'tm'), pairs))]
    ppermute x2, starting transfers between devices: 1.69 us -> 2.9 us  [partner(): return lax.ppermute(x, 'tm', [(i, i ^ step) for i in range(shards)])]
where the time goes in v17:
time: 56.2 us; the launch traced here: 55.8 us
  starting transfers between devices  25.3 us (45%)
  Pallas kernels  21.2 us (38%)
  waiting for transfers between devices  5.26 us (9%)
  local copies, waits for them, and re-layouts  3 us (5%)
  between operations  1.11 us (2%)
    pallas_call x12, Pallas kernels, call(): pl.pallas_call(kernel, out_shape=outs, in_specs=specs, out_specs=jax.tree...  21.2 us
    ppermute x6, starting transfers between devices, swapped(): results.append(lax.ppermute(x, ('section', 'tm'), pairs))  11.7 us
    ppermute x5, starting transfers between devices, shifted(): lax.ppermute(x, 'section', [(i, (i + by) % sections) for i in range(secti...  10.7 us
    ppermute x2, waiting for transfers between devices, partner(): return lax.ppermute(x, 'tm', [(i, i ^ step) for i in range(shards)])  3.38 us
    unnamed x36, local copies, waits for them, and re-layouts  3 us
    ppermute x2, starting transfers between devices, partner(): return lax.ppermute(x, 'tm', [(i, i ^ step) for i in range(shards)])  2.9 us
  transfers between devices with their start and end apart: 13, of which 5 were waited for; matrix products, arithmetic and copies ran while one was open for 0% of the time, Pallas kernels for 35%

profile of v17, /device:TPU:0, one launch (start us, length us, event | category | flops | bytes accessed | tf_op | source)
XLA Modules:
  0.0 55.8 jit_solution(11473342613439138351)
XLA Ops:
  0.7 3.1 %collective-permute-start.2 = (bf16[128,2048]{1,0:T(8,128)(2,1)}, bf16[128,2048]{1,0:T(8,128)(2,1)}, u32[]{:S(2)}, u32[]{:S(2)}) collective-permute-start(bf16[128,2048]{1,0:T(8,128)(2,1)} %bitcast.21), channel_id=1, source_target_pairs={{0,8},{4,12},{8,16},{12,20},{16,24},{20,28},{24,0},{28,4},{1,9},{5... | collective-permute-start | bytes 1572872 | tf_op jit(solution)/shard_map/ppermute | solution.py:538
  3.7 1.9 %shard_map.210 = (bf16[48,2048]{1,0:T(8,128)(2,1)}, bf16[48,2048]{1,0:T(8,128)(2,1)}, s32[8]{0:T(128)}) custom-call(bf16[2,128,2048]{2,1,0:T(8,128)(2,1)} %bitcast.15, bf16[1,128,2048]{2,1,0:T(8,128)(2,1)} %grad.1, s32[8]{0:T(128)} %back_lengths.1, s32[8]{0:T(128)} %ahead_lengths.1, s32[2,8]{1,0:T(2,128)} %bitcast.25, s32[2,8]{1,0:T(2,128)} %bitcast.26), custom_call_target="tpu_custom_call" | custom-call | tf_op jit(solution)/shard_map/pallas_call | solution.py:505
  5.6 0.7 %collective-permute-start = (bf16[48,2048]{1,0:T(8,128)(2,1)}, bf16[48,2048]{1,0:T(8,128)(2,1)S(1)}, u32[]{:S(2)}, u32[]{:S(2)}) collective-permute-start(bf16[48,2048]{1,0:T(8,128)(2,1)} %get-tuple-element.36), channel_id=1, source_target_pairs={{1,2},{2,1},{5,6},{6,5},{9,10},{10,9},{13,14},{14,13},{17,18},{18,... | collective-permute-start | bytes 589832 | tf_op jit(solution)/shard_map/ppermute | solution.py:550
  6.3 4.3 %collective-permute-start.1 = (bf16[48,2048]{1,0:T(8,128)(2,1)}, bf16[48,2048]{1,0:T(8,128)(2,1)S(1)}, u32[]{:S(2)}, u32[]{:S(2)}) collective-permute-start(bf16[48,2048]{1,0:T(8,128)(2,1)} %get-tuple-element.37), channel_id=1, source_target_pairs={{0,1},{1,0},{2,3},{3,2},{4,5},{5,4},{6,7},{7,6},{8,9},{9,8},{10,11... | collective-permute-start | bytes 589832 | tf_op jit(solution)/shard_map/ppermute | solution.py:550
  10.6 1.2 %copy-done = bf16[1,2,128,2048]{3,2,1,0:T(8,128)(2,1)S(1)} copy-done((bf16[1,2,128,2048]{3,2,1,0:T(8,128)(2,1)S(1)}, bf16[1,2,128,2048]{3,2,1,0:T(8,128)(2,1)}, u32[]{:S(2)}) %copy-start) | copy-done | bytes 1048600
  11.8 1.0 %copy-done.3 = bf16[1,128,2048]{2,1,0:T(8,128)(2,1)S(1)} copy-done((bf16[1,128,2048]{2,1,0:T(8,128)(2,1)S(1)}, bf16[1,128,2048]{2,1,0:T(8,128)(2,1)}, u32[]{:S(2)}) %copy-start.3) | copy-done | bytes 524312
  12.8 0.7 %copy-done.9 = s32[8]{0:T(128)S(1)} copy-done((s32[8]{0:T(128)S(1)}, s32[8]{0:T(128)}, u32[]{:S(2)}) %copy-start.9) | copy-done | bytes 56
  13.5 1.7 %shard_map.211 = (bf16[2,32,2048]{2,1,0:T(8,128)(2,1)S(1)}, bf16[32,2048]{1,0:T(8,128)(2,1)S(1)}, bf16[32,2048]{1,0:T(8,128)(2,1)S(1)}, bf16[64,2048]{1,0:T(8,12...) custom-call(s32[8]{0:T(128)S(1)} %copy-done.9, ...), custom_call_target="tpu_custom_call" | custom-call | tf_op jit(solution)/shard_map/pallas_call | solution.py:505
  15.3 0.7 %collective-permute-start.6 = (bf16[64,2048]{1,0:T(8,128)(2,1)S(1)}, bf16[64,2048]{1,0:T(8,128)(2,1)S(1)}, u32[]{:S(2)}, u32[]{:S(2)}) collective-permute-start(bf16[64,2048]{1,0:T(8,128)(2,1)S(1)} %get-tuple-element.45), channel_id=1, source_target_pairs={{1,2},{2,1},{5,6},{6,5},{9,10},{10,9},{13,14},{14,13},{17,18},{18,... | collective-permute-start | bytes 786440 | tf_op jit(solution)/shard_map/ppermute | solution.py:550
  16.0 2.8 %collective-permute-start.7 = (bf16[64,2048]{1,0:T(8,128)(2,1)S(1)}, bf16[64,2048]{1,0:T(8,128)(2,1)S(1)}, u32[]{:S(2)}, u32[]{:S(2)}) collective-permute-start(bf16[64,2048]{1,0:T(8,128)(2,1)S(1)} %get-tuple-element.46), channel_id=1, source_target_pairs={{0,1},{1,0},{2,3},{3,2},{4,5},{5,4},{6,7},{7,6},{8,9},{9,8},{10,11... | collective-permute-start | bytes 786440 | tf_op jit(solution)/shard_map/ppermute | solution.py:550
  18.8 0.5 collective-permute-done.1.refs_3_
  19.3 3.5 %shard_map.212 = (bf16[128,2048]{1,0:T(8,128)(2,1)S(1)}, bf16[16,2048]{1,0:T(8,128)(2,1)S(1)}, bf16[16,2048]{1,0:T(8,128)(2,1)S(1)}, bf16[64,2048]{1,0:T(8,128)(...) custom-call(s32[8]{0:T(128)S(1)} %copy-done.10, bf16[2,128,2048]{2,1,0:T(8,128)(2,1)S(1)} %bitcast.17, ...), custom_call_target="tpu_custom_call" | custom-call | flops 4000000000 | tf_op jit(solution)/shard_map/pallas_call | solution.py:505
  22.9 0.8 %collective-permute-start.4 = (bf16[16,2048]{1,0:T(8,128)(2,1)S(1)}, bf16[16,2048]{1,0:T(8,128)(2,1)S(1)}, u32[]{:S(2)}, u32[]{:S(2)}) collective-permute-start(bf16[16,2048]{1,0:T(8,128)(2,1)S(1)} %get-tuple-element.43), channel_id=1, source_target_pairs={{1,30},{2,29},{5,2},{6,1},{9,6},{10,5},{13,10},{14,9},{17,14},{18,... | collective-permute-start | bytes 196616 | tf_op jit(solution)/shard_map/ppermute | solution.py:550
  23.7 2.5 %collective-permute-start.3 = (bf16[128,2048]{1,0:T(8,128)(2,1)S(1)}, bf16[128,2048]{1,0:T(8,128)(2,1)S(1)}, u32[]{:S(2)}, u32[]{:S(2)}) collective-permute-start(bf16[128,2048]{1,0:T(8,128)(2,1)S(1)} %get-tuple-element.42), channel_id=1, source_target_pairs={{0,28},{4,0},{8,4},{12,8},{16,12},{20,16},{24,20},{28,24},{1,29},{... | collective-permute-start | bytes 1572872 | tf_op jit(solution)/shard_map/ppermute | solution.py:538
  26.2 1.0 %shard_map.213.refs_4_.taps0 = bf16[32,2048]{1,0:T(8,128)(2,1)S(1)} custom-call(bf16[64,2048]{1,0:T(8,128)(2,1)S(1)} %get-tuple-element.48.halo, bf16[128,2048]{1,0:T(8,128)(2,1)S(1)} %get-tuple-element.39.refs_6_.masked, bf16[128,2048]{1,0:T(8,128)(2,1)S(1)} %get-tuple-element.49.inner, f32[1,2048]{1,0:T(1,128)S(1)} %get-tuple-element.50.gain_sum, ...), custom_call_target="tpu_custom_call" | custom-call | tf_op jit(solution)/shard_map/pallas_call | solution.py:505
  27.2 1.1 %shard_map.214 = (bf16[128,2048]{1,0:T(8,128)(2,1)S(1)}, f32[128,128]{1,0:T(8,128)S(1)}, f32[128,128]{1,0:T(8,128)S(1)}, f32[192,2048]{1,0:T(8,128)S(1)}) custom-call(s32[8]{0:T(128)S(1)} %copy-done.10, bf16[2,128,2048]{2,1,0:T(8,128)(2,1)S(1)} %bitcast.18, bf16[2,32,2048]{2,1,0:T(8,128)(2,1)S(1)} %get-tuple-element.38.refs_5_.refs_2_.weights, ...), custom_call_target="tpu_custom_call" | custom-call | flops 1000000000 | tf_op jit(solution)/shard_map/pallas_call | solution.py:505
  28.3 2.5 %collective-permute-start.5 = (bf16[16,2048]{1,0:T(8,128)(2,1)S(1)}, bf16[16,2048]{1,0:T(8,128)(2,1)S(1)}, u32[]{:S(2)}, u32[]{:S(2)}) collective-permute-start(bf16[16,2048]{1,0:T(8,128)(2,1)S(1)} %get-tuple-element.44), channel_id=1, source_target_pairs={{0,29},{1,28},{2,31},{3,30},{4,1},{5,0},{6,3},{7,2},{8,5},{9,4},{1... | collective-permute-start | bytes 196616 | tf_op jit(solution)/shard_map/ppermute | solution.py:550
  30.9 0.6 %collective-permute-done.7.near = bf16[64,2048]{1,0:T(8,128)(2,1)S(1)} collective-permute-done((bf16[64,2048]{1,0:T(8,128)(2,1)S(1)}, bf16[64,2048]{1,0:T(8,128)(2,1)S(1)}, u32[]{:S(2)}, u32[]{:S(2)}) %collective-permute-start.7) | collective-permute-done | bytes 262176 | tf_op jit(solution)/shard_map/ppermute | solution.py:550
  31.5 2.1 %shard_map.215 = (f32[192,2048]{1,0:T(8,128)S(1)}, f32[160,2048]{1,0:T(8,128)S(1)}, f32[128,2048]{1,0:T(8,128)S(1)}, bf16[96,2048]{1,0:T(8,128)(2,1)S(1)}) custom-call(s32[8]{0:T(128)S(1)} %copy-done.10, bf16[64,2048]{1,0:T(8,128)(2,1)S(1)} %collective-permute-done.6.far, bf16[64,2048]{1,0:T(8,128)(2,1)S(1)} %collective-permute-done.7.near, ...), custom_call_target="tpu_custom_call" | custom-call | flops 5000000000 | tf_op jit(solution)/shard_map/pallas_call | solution.py:505
  33.6 1.6 %collective-permute-start.10 = (bf16[96,2048]{1,0:T(8,128)(2,1)S(1)}, bf16[96,2048]{1,0:T(8,128)(2,1)S(1)}, u32[]{:S(2)}, u32[]{:S(2)}) collective-permute-start(bf16[96,2048]{1,0:T(8,128)(2,1)S(1)} %get-tuple-element.57), channel_id=1, source_target_pairs={{0,8},{4,12},{8,16},{12,20},{16,24},{20,28},{24,0},{28,4},{1,9},{5... | collective-permute-start | bytes 1179656 | tf_op jit(solution)/shard_map/ppermute | solution.py:538
  35.2 1.4 %shard_map.216 = (bf16[160,2048]{1,0:T(8,128)(2,1)S(1)}, bf16[64,2048]{1,0:T(8,128)(2,1)S(1)}) custom-call(s32[8]{0:T(128)S(1)} %copy-done.10, bf16[128,2048]{1,0:T(8,128)(2,1)S(1)} %collective-permute-done.3.received, bf16[16,2048]{1,0:T(8,128)(2,1)S(1)} %collective-permute-done.4.far, bf16[16,2048]{1,0:T(8,128)(2,1)S(1)} %collective-permute-done.5.near, ...), custom_call_target="tpu_custom_call" | custom-call | flops 2000000000 | tf_op jit(solution)/shard_map/pallas_call | solution.py:505
  36.6 2.5 %collective-permute-start.8 = (bf16[64,2048]{1,0:T(8,128)(2,1)S(1)}, bf16[64,2048]{1,0:T(8,128)(2,1)S(1)}, u32[]{:S(2)}, u32[]{:S(2)}) collective-permute-start(bf16[64,2048]{1,0:T(8,128)(2,1)S(1)} %get-tuple-element.56.mine), channel_id=1, source_target_pairs={{0,1},{1,0},{2,3},{3,2},{4,5},{5,4},{6,7},{7,6},{8,9},{9,8},{10,11... | collective-permute-start | bytes 786440 | tf_op jit(solution)/shard_map/ppermute | solution.py:626
  39.1 2.0 %shard_map.220 = bf16[128,2048]{1,0:T(8,128)(2,1)S(1)} custom-call(s32[8]{0:T(128)S(1)} %copy-done.10, bf16[2,128,2048]{2,1,0:T(8,128)(2,1)S(1)} %bitcast.19, bf16[128,2048]{1,0:T(8,128)(2,1)S(1)} %collective-permute-done.3.received, bf16[2,32,2048]{2,1,0:T(8,128)(2,1)S(1)} %get-tuple-element.38.refs_5_.refs_2_.weights, ...), custom_call_target="tpu_custom_call" | custom-call | flops 6000000000 | tf_op jit(solution)/shard_map/pallas_call | solution.py:505
  41.1 3.4 %collective-permute-start.12 = (bf16[128,2048]{1,0:T(8,128)(2,1)S(1)}, bf16[128,2048]{1,0:T(8,128)(2,1)S(1)}, u32[]{:S(2)}, u32[]{:S(2)}) collective-permute-start(bf16[128,2048]{1,0:T(8,128)(2,1)S(1)} %shard_map.220), channel_id=1, source_target_pairs={{0,28},{4,0},{8,4},{12,8},{16,12},{20,16},{24,20},{28,24},{1,29},{... | collective-permute-start | bytes 1572872 | tf_op jit(solution)/shard_map/ppermute | solution.py:538
  44.5 1.3 %collective-permute-done.8.other = bf16[64,2048]{1,0:T(8,128)(2,1)S(1)} collective-permute-done((bf16[64,2048]{1,0:T(8,128)(2,1)S(1)}, bf16[64,2048]{1,0:T(8,128)(2,1)S(1)}, u32[]{:S(2)}, u32[]{:S(2)}) %collective-permute-start.8) | collective-permute-done | bytes 262176 | tf_op jit(solution)/shard_map/ppermute | solution.py:626
  45.8 0.1 shard_map.217.refs_6_.mine
  45.9 0.4 collective-permute-start.9
  46.3 0.8 %collective-permute-done.10.refs_2_ = bf16[96,2048]{1,0:T(8,128)(2,1)S(1)} collective-permute-done((bf16[96,2048]{1,0:T(8,128)(2,1)S(1)}, bf16[96,2048]{1,0:T(8,128)(2,1)S(1)}, u32[]{:S(2)}, u32[]{:S(2)}) %collective-permute-start.10) | collective-permute-done | bytes 393248 | tf_op jit(solution)/shard_map/ppermute | solution.py:538
  47.1 2.8 %shard_map.218.between = bf16[160,2048]{1,0:T(8,128)(2,1)S(1)} custom-call(s32[8]{0:T(128)S(1)} %copy-done.10, bf16[128,2048]{1,0:T(8,128)(2,1)} %collective-permute-done.2.refs_14_.refs_1_, bf16[96,2048]{1,0:T(8,128)(2,1)S(1)} %collective-permute-done.10.refs_2_, bf16[384,192]{1,0:T(8,128)(2,1)S(1)} %copy-done.5, bf16[192,64]{1,0:T(8,128)(2,1)S(1)} %copy-done.16, ...), custom_call_target="tpu_custom_call" | custom-call | flops 10000000000 | tf_op jit(solution)/shard_map/pallas_call | solution.py:505
  49.9 2.0 %shard_map.219.act = bf16[128,2048]{1,0:T(8,128)(2,1)S(1)} custom-call(s32[8]{0:T(128)S(1)} %copy-done.10, bf16[160,2048]{1,0:T(8,128)(2,1)S(1)} %shard_map.218.between, bf16[32,2048]{1,0:T(8,128)(2,1)S(1)} %collective-permute-done.11.layer, bf16[320,160]{1,0:T(8,128)(2,1)S(1)} %copy-done.12, bf16[160,64]{1,0:T(8,128)(2,1)S(1)} %copy-done.17, ...), custom_call_target="tpu_custom_call" | custom-call | flops 10000000000 | tf_op jit(solution)/shard_map/pallas_call | solution.py:505
  51.9 2.1 %collective-permute-done.9.other = bf16[64,2048]{1,0:T(8,128)(2,1)S(1)} collective-permute-done((bf16[64,2048]{1,0:T(8,128)(2,1)S(1)}, bf16[64,2048]{1,0:T(8,128)(2,1)S(1)}, u32[]{:S(2)}, u32[]{:S(2)}) %collective-permute-start.9) | collective-permute-done | bytes 262176 | tf_op jit(solution)/shard_map/ppermute | solution.py:626
  54.0 1.7 %shard_map.221 = (bf16[128,2048]{1,0:T(8,128)(2,1)}, bf16[128,2048]{1,0:T(8,128)(2,1)}, f32[31,2,2048]{2,1,0:T(2,128)}, f32[2,2048]{1,0:T(2,128)}) custom-call(s32[8]{0:T(128)S(1)} %copy-done.10, bf16[64,2048]{1,0:T(8,128)(2,1)S(1)} %shard_map.217.refs_6_.mine, bf16[64,2048]{1,0:T(8,128)(2,1)S(1)} %collective-permute-done.9.other, ...), custom_call_target="tpu_custom_call" | custom-call | tf_op jit(solution)/shard_map/pallas_call | solution.py:505
  (42 shorter events, 0.2 us)
Async XLA Ops:
  0.6 9.9 %copy-start.8 = (bf16[1,2,2048]{2,1,0:T(2,128)(2,1)S(1)}, bf16[1,2,2048]{2,1,0:T(2,128)(2,1)}, u32[]{:S(2)}) copy-start(bf16[1,2,2048]{2,1,0:T(2,128)(2,1)} %param.23) | copy-start | bytes 24580
  0.6 9.9 %copy-start.4 = (bf16[1,2,31,2048]{3,1,2,0:T(2,128)(2,1)S(1)}, bf16[1,2,31,2048]{3,1,2,0:T(2,128)(2,1)}, u32[]{:S(2)}) copy-start(bf16[1,2,31,2048]{3,1,2,0:T(2,128)(2,1)} %param.22) | copy-start | bytes 761860
  0.7 18.6 %collective-permute-start.2 = (bf16[128,2048]{1,0:T(8,128)(2,1)}, bf16[128,2048]{1,0:T(8,128)(2,1)}, u32[]{:S(2)}, u32[]{:S(2)}) collective-permute-start(bf16[128,2048]{1,0:T(8,128)(2,1)} %bitcast.21), channel_id=1, source_target_pairs={{0,8},{4,12},{8,16},{12,20},{16,24},{20,28},{24,0},{28,4},{1,9},{5... | collective-permute-start | bytes 1572872 | tf_op jit(solution)/shard_map/ppermute | solution.py:538
  3.7 15.5 %copy-start.5 = (bf16[384,192]{1,0:T(8,128)(2,1)S(1)}, bf16[384,192]{1,0:T(8,128)(2,1)}, u32[]{:S(2)}) copy-start(bf16[384,192]{1,0:T(8,128)(2,1)} %constant.20.clone.refs_9_.m_table.refs_3_) | copy-start | bytes 442372
  5.6 13.7 %copy-start.10 = (s32[8]{0:T(128)S(1)}, s32[8]{0:T(128)}, u32[]{:S(2)}) copy-start(s32[8]{0:T(128)} %get-tuple-element.35.notes.refs_0_) | copy-start | bytes 100
  5.6 10.4 %collective-permute-start = (bf16[48,2048]{1,0:T(8,128)(2,1)}, bf16[48,2048]{1,0:T(8,128)(2,1)S(1)}, u32[]{:S(2)}, u32[]{:S(2)}) collective-permute-start(bf16[48,2048]{1,0:T(8,128)(2,1)} %get-tuple-element.36), channel_id=1, source_target_pairs={{1,2},{2,1},{5,6},{6,5},{9,10},{10,9},{13,14},{14,13},{17,18},{18,... | collective-permute-start | bytes 589832 | tf_op jit(solution)/shard_map/ppermute | solution.py:550
  6.3 13.0 %collective-permute-start.1 = (bf16[48,2048]{1,0:T(8,128)(2,1)}, bf16[48,2048]{1,0:T(8,128)(2,1)S(1)}, u32[]{:S(2)}, u32[]{:S(2)}) collective-permute-start(bf16[48,2048]{1,0:T(8,128)(2,1)} %get-tuple-element.37), channel_id=1, source_target_pairs={{0,1},{1,0},{2,3},{3,2},{4,5},{5,4},{6,7},{7,6},{8,9},{9,8},{10,11... | collective-permute-start | bytes 589832 | tf_op jit(solution)/shard_map/ppermute | solution.py:550
  10.6 1.2 %copy-start = (bf16[1,2,128,2048]{3,2,1,0:T(8,128)(2,1)S(1)}, bf16[1,2,128,2048]{3,2,1,0:T(8,128)(2,1)}, u32[]{:S(2)}) copy-start(bf16[1,2,128,2048]{3,2,1,0:T(8,128)(2,1)} %param.21) | copy-start | bytes 3145732
  11.8 1.0 %copy-start.3 = (bf16[1,128,2048]{2,1,0:T(8,128)(2,1)S(1)}, bf16[1,128,2048]{2,1,0:T(8,128)(2,1)}, u32[]{:S(2)}) copy-start(bf16[1,128,2048]{2,1,0:T(8,128)(2,1)} %param.19) | copy-start | bytes 1572868
  12.8 0.7 %copy-start.9 = (s32[8]{0:T(128)S(1)}, s32[8]{0:T(128)}, u32[]{:S(2)}) copy-start(s32[8]{0:T(128)} %get-tuple-element.35.notes.refs_0_) | copy-start | bytes 100
  13.5 5.8 %copy-start.2 = (bf16[1,128,2048]{2,1,0:T(8,128)(2,1)S(1)}, bf16[1,128,2048]{2,1,0:T(8,128)(2,1)}, u32[]{:S(2)}) copy-start(bf16[1,128,2048]{2,1,0:T(8,128)(2,1)} %grad.1) | copy-start | bytes 1572868
  13.5 5.8 %copy-start.11 = (bf16[384,160]{1,0:T(8,128)(2,1)S(1)}, bf16[384,160]{1,0:T(8,128)(2,1)}, u32[]{:S(2)}) copy-start(bf16[384,160]{1,0:T(8,128)(2,1)} %constant.23.clone.refs_12_.g_table) | copy-start | bytes 368644
  13.5 5.8 %copy-start.13 = (bf16[320,192]{1,0:T(8,128)(2,1)S(1)}, bf16[320,192]{1,0:T(8,128)(2,1)}, u32[]{:S(2)}) copy-start(bf16[320,192]{1,0:T(8,128)(2,1)} %constant.22.clone.refs_11_.c_table.refs_5_) | copy-start | bytes 368644
  13.5 5.8 %copy-start.15 = (bf16[256,192]{1,0:T(8,128)(2,1)S(1)}, bf16[256,192]{1,0:T(8,128)(2,1)}, u32[]{:S(2)}) copy-start(bf16[256,192]{1,0:T(8,128)(2,1)} %constant.24.clone.refs_13_.x_table) | copy-start | bytes 294916
  13.5 5.8 %copy-start.16 = (bf16[192,64]{1,0:T(8,128)(2,1)S(1)}, bf16[192,64]{1,0:T(8,128)(2,1)}, u32[]{:S(2)}) copy-start(bf16[192,64]{1,0:T(8,128)(2,1)} %constant.21.clone.refs_10_.refs_3_.refs_4_) | copy-start | bytes 73732
  15.2 34.7 %collective-permute-start.11 = (bf16[32,2048]{1,0:T(8,128)(2,1)S(1)}, bf16[32,2048]{1,0:T(8,128)(2,1)S(1)}, u32[]{:S(2)}, u32[]{:S(2)}) collective-permute-start(bf16[32,2048]{1,0:T(8,128)(2,1)S(1)} %get-tuple-element.58), channel_id=1, source_target_pairs={{0,4},{4,8},{8,12},{12,16},{16,20},{20,24},{24,28},{28,0},{1,5},{5... | collective-permute-start | bytes 393224 | tf_op jit(solution)/shard_map/ppermute | solution.py:538
  15.3 13.0 %collective-permute-start.6 = (bf16[64,2048]{1,0:T(8,128)(2,1)S(1)}, bf16[64,2048]{1,0:T(8,128)(2,1)S(1)}, u32[]{:S(2)}, u32[]{:S(2)}) collective-permute-start(bf16[64,2048]{1,0:T(8,128)(2,1)S(1)} %get-tuple-element.45), channel_id=1, source_target_pairs={{1,2},{2,1},{5,6},{6,5},{9,10},{10,9},{13,14},{14,13},{17,18},{18,... | collective-permute-start | bytes 786440 | tf_op jit(solution)/shard_map/ppermute | solution.py:550
  16.0 15.5 %collective-permute-start.7 = (bf16[64,2048]{1,0:T(8,128)(2,1)S(1)}, bf16[64,2048]{1,0:T(8,128)(2,1)S(1)}, u32[]{:S(2)}, u32[]{:S(2)}) collective-permute-start(bf16[64,2048]{1,0:T(8,128)(2,1)S(1)} %get-tuple-element.46), channel_id=1, source_target_pairs={{0,1},{1,0},{2,3},{3,2},{4,5},{5,4},{6,7},{7,6},{8,9},{9,8},{10,11... | collective-permute-start | bytes 786440 | tf_op jit(solution)/shard_map/ppermute | solution.py:550
  19.3 6.9 %copy-start.6 = (bf16[192,256]{1,0:T(8,128)(2,1)S(1)}, bf16[192,256]{1,0:T(8,128)(2,1)}, u32[]{:S(2)}) copy-start(bf16[192,256]{1,0:T(8,128)(2,1)} %constant.25.clone.go_table) | copy-start | bytes 294916
  19.3 6.9 %copy-start.7 = (bf16[64,192]{1,0:T(8,128)(2,1)S(1)}, bf16[64,192]{1,0:T(8,128)(2,1)}, u32[]{:S(2)}) copy-start(bf16[64,192]{1,0:T(8,128)(2,1)} %constant.26.clone.t_table) | copy-start | bytes 73732
  22.8 4.4 %copy-start.1 = (bf16[1,2,128,2048]{3,2,1,0:T(8,128)(2,1)S(1)}, bf16[1,2,128,2048]{3,2,1,0:T(8,128)(2,1)}, u32[]{:S(2)}) copy-start(bf16[1,2,128,2048]{3,2,1,0:T(8,128)(2,1)} %param.21) | copy-start | bytes 3145732
  22.9 12.3 %collective-permute-start.4 = (bf16[16,2048]{1,0:T(8,128)(2,1)S(1)}, bf16[16,2048]{1,0:T(8,128)(2,1)S(1)}, u32[]{:S(2)}, u32[]{:S(2)}) collective-permute-start(bf16[16,2048]{1,0:T(8,128)(2,1)S(1)} %get-tuple-element.43), channel_id=1, source_target_pairs={{1,30},{2,29},{5,2},{6,1},{9,6},{10,5},{13,10},{14,9},{17,14},{18,... | collective-permute-start | bytes 196616 | tf_op jit(solution)/shard_map/ppermute | solution.py:550
  23.7 11.6 %collective-permute-start.3 = (bf16[128,2048]{1,0:T(8,128)(2,1)S(1)}, bf16[128,2048]{1,0:T(8,128)(2,1)S(1)}, u32[]{:S(2)}, u32[]{:S(2)}) collective-permute-start(bf16[128,2048]{1,0:T(8,128)(2,1)S(1)} %get-tuple-element.42), channel_id=1, source_target_pairs={{0,28},{4,0},{8,4},{12,8},{16,12},{20,16},{24,20},{28,24},{1,29},{... | collective-permute-start | bytes 1572872 | tf_op jit(solution)/shard_map/ppermute | solution.py:538
  28.3 6.9 %collective-permute-start.5 = (bf16[16,2048]{1,0:T(8,128)(2,1)S(1)}, bf16[16,2048]{1,0:T(8,128)(2,1)S(1)}, u32[]{:S(2)}, u32[]{:S(2)}) collective-permute-start(bf16[16,2048]{1,0:T(8,128)(2,1)S(1)} %get-tuple-element.44), channel_id=1, source_target_pairs={{0,29},{1,28},{2,31},{3,30},{4,1},{5,0},{6,3},{7,2},{8,5},{9,4},{1... | collective-permute-start | bytes 196616 | tf_op jit(solution)/shard_map/ppermute | solution.py:550
  33.6 13.5 %collective-permute-start.10 = (bf16[96,2048]{1,0:T(8,128)(2,1)S(1)}, bf16[96,2048]{1,0:T(8,128)(2,1)S(1)}, u32[]{:S(2)}, u32[]{:S(2)}) collective-permute-start(bf16[96,2048]{1,0:T(8,128)(2,1)S(1)} %get-tuple-element.57), channel_id=1, source_target_pairs={{0,8},{4,12},{8,16},{12,20},{16,24},{20,28},{24,0},{28,4},{1,9},{5... | collective-permute-start | bytes 1179656 | tf_op jit(solution)/shard_map/ppermute | solution.py:538
  36.6 9.2 %collective-permute-start.8 = (bf16[64,2048]{1,0:T(8,128)(2,1)S(1)}, bf16[64,2048]{1,0:T(8,128)(2,1)S(1)}, u32[]{:S(2)}, u32[]{:S(2)}) collective-permute-start(bf16[64,2048]{1,0:T(8,128)(2,1)S(1)} %get-tuple-element.56.mine), channel_id=1, source_target_pairs={{0,1},{1,0},{2,3},{3,2},{4,5},{5,4},{6,7},{7,6},{8,9},{9,8},{10,11... | collective-permute-start | bytes 786440 | tf_op jit(solution)/shard_map/ppermute | solution.py:626
  41.1 10.8 %collective-permute-start.12 = (bf16[128,2048]{1,0:T(8,128)(2,1)S(1)}, bf16[128,2048]{1,0:T(8,128)(2,1)S(1)}, u32[]{:S(2)}, u32[]{:S(2)}) collective-permute-start(bf16[128,2048]{1,0:T(8,128)(2,1)S(1)} %shard_map.220), channel_id=1, source_target_pairs={{0,28},{4,0},{8,4},{12,8},{16,12},{20,16},{24,20},{28,24},{1,29},{... | collective-permute-start | bytes 1572872 | tf_op jit(solution)/shard_map/ppermute | solution.py:538
  45.9 4.0 %copy-start.12 = (bf16[320,160]{1,0:T(8,128)(2,1)S(1)}, bf16[320,160]{1,0:T(8,128)(2,1)}, u32[]{:S(2)}) copy-start(bf16[320,160]{1,0:T(8,128)(2,1)} %constant.27.clone.m_table) | copy-start | bytes 307204
  45.9 4.0 %copy-start.14 = (bf16[256,160]{1,0:T(8,128)(2,1)S(1)}, bf16[256,160]{1,0:T(8,128)(2,1)}, u32[]{:S(2)}) copy-start(bf16[256,160]{1,0:T(8,128)(2,1)} %constant.29.clone.c_table) | copy-start | bytes 245764
  45.9 4.0 %copy-start.17 = (bf16[160,64]{1,0:T(8,128)(2,1)S(1)}, bf16[160,64]{1,0:T(8,128)(2,1)}, u32[]{:S(2)}) copy-start(bf16[160,64]{1,0:T(8,128)(2,1)} %constant.28.clone.q_table) | copy-start | bytes 61444
  45.9 8.0 %collective-permute-start.9 = (bf16[64,2048]{1,0:T(8,128)(2,1)S(1)}, bf16[64,2048]{1,0:T(8,128)(2,1)S(1)}, u32[]{:S(2)}, u32[]{:S(2)}) collective-permute-start(bf16[64,2048]{1,0:T(8,128)(2,1)S(1)} %shard_map.217.refs_6_.mine), channel_id=1, source_target_pairs={{0,2},{1,3},{2,0},{3,1},{4,6},{5,7},{6,4},{7,5},{8,10},{9,11},{10,... | collective-permute-start | bytes 786440 | tf_op jit(solution)/shard_map/ppermute | solution.py:626

commit v18 on v17

--- a/solution.py
+++ b/solution.py
@@ -304,8 +304,9 @@
     return (mine[...].astype(F32) + other[...].astype(F32)).astype(BF16)
 
 
-def add_kernel(mine, other, out):
-    out[...] = added(mine, other)
+def add_kernel(mine0, other0, mine1, other1, out0, out1):
+    out0[...] = added(mine0, other0)
+    out1[...] = added(mine1, other1)
 
 
 def second_early_kernel(notes, saved, weights, q_table, masked, mean, inverse, q):
@@ -343,13 +344,11 @@
 
 
 def second_taps_kernel(
-    notes, received, far, near, weights, m, factor, conv, taps0, go_table, t_table, mixed_out, taps, halos
+    notes, received, far, near, weights, m, factor, conv, taps0, go_table, t_table, mixed_out, taps, taps0_out, halos
 ):
+    taps0_out[...] = taps0[...]
     own, width = conv.shape
     rows = factor.shape[0]
-    count = taps0.shape[0]
-    taps[pl.ds(0, count), :] = taps0[...]
-    taps1 = taps.at[pl.ds(count, count)]
     edge = (rows - own) // 2
     gain = slot_row(weights, notes[BACK1])
     left, right = sorted_halos(near, far, 0, halos)
@@ -360,7 +359,7 @@
         mixed_out[:, columns] = mixed
         inner = mixed[edge : edge + own]
         gain_sum = jnp.sum(inner.astype(F32) * conv[:, columns], axis=0, keepdims=True) / gain(columns)
-        put_taps(taps1, tap_term(go_table, t_table, m[:, columns], inner), gain_sum, columns)
+        put_taps(taps, tap_term(go_table, t_table, m[:, columns], inner), gain_sum, columns)
 
     each_block(width, block)
 
@@ -453,7 +452,7 @@
     notes[AHEAD0 + 1] = ahead_len[lax.rem(section + sections - 2, sections)]
 
 
-def final_kernel(notes, mine, other, act, grad, act_out, grad_out, taps_out, gains_out, taps, gains, sems):
+def final_kernel(notes, mine0, mine1, other0, other1, act, grad, act_out, grad_out, taps_out, gains_out, taps, gains, sems):
     copies = [
         pltpu.make_async_copy(act, act_out, sems.at[0]),
         pltpu.make_async_copy(grad, grad_out, sems.at[1]),
@@ -464,8 +463,8 @@
     step = width // 4
     for begin in range(0, width, step):
         columns = pl.ds(begin, step)
-        total = mine[:, columns].astype(F32) + other[:, columns].astype(F32)
-        ticks = total[: count + 1], total[count + 1 :]
+        pairs = (mine0, other0), (mine1, other1)
+        ticks = [a[:, columns].astype(F32) + b[:, columns].astype(F32) for a, b in pairs]
         for slot in range(slots):
             use = [(notes[layer] == slot).astype(F32) for layer in (BACK0, BACK1)]
             both = use[0] * ticks[0] + use[1] * ticks[1]
@@ -625,9 +624,9 @@
     def partner(x, step):
         return lax.ppermute(x, "tm", [(i, i ^ step) for i in range(shards)])
 
-    mixed1, sums = run(
+    mixed1, taps1, taps0 = run(
         second_taps_kernel,
-        (like(small, width, BF16), like(2 * (tap_count + 1), width, BF16)),
+        (like(small, width, BF16), like(tap_count + 1, width, BF16), like(tap_count + 1, width, BF16)),
         [pltpu.VMEM((2, one, width), BF16)],
         [notes, grad_mid, far2, near2, weights, m1, factor1, conv1, taps0, go_table, t_table],
         2,
@@ -643,14 +642,21 @@
         6,
     )
     grad_out = shifted(grad_out, -1)
-    mine = call(add_kernel, like(*sums.shape, BF16), [], (sums, partner(sums, 1)), 6)
+    steps = [1 << i for i in range(shards.bit_length() - 1)]
+    mine = taps0, taps1
+    other = partner(taps0, steps[0]), partner(taps1, steps[-1])
+    order = list(zip(steps, steps[::-1]))[1:]
+    for count, pair in enumerate(order):
+        operands = (mine[0], other[0], mine[1], other[1])
+        mine = call(add_kernel, (like(*taps0.shape, BF16),) * 2, [], operands, 0 if count else 6)
+        other = tuple(partner(x, step) for x, step in zip(mine, pair))
     between = run(
         functools.partial(first_forward_kernel, two),
         like(small, width, BF16),
         [pltpu.VMEM((2 * two, width), BF16), pltpu.VMEM((own, width), BF16)],
         [notes, act_ahead, ahead0, m_table, q_table, c_table],
         10,
-        mine,
+        mine[0],
     )
     act_out = run(
         second_forward_kernel,
@@ -662,13 +668,6 @@
         ],
         10,
     )
-    step = 2
-    while True:
-        other = partner(mine, step)
-        step *= 2
-        if step >= shards:
-            break
-        mine = call(add_kernel, like(*mine.shape, BF16), [], (mine, other), 0)
     slots = kernels.shape[1]
     act_out, grad_out, taps, gains = call(
         final_kernel,
@@ -680,8 +679,8 @@
             pltpu.VMEM((tap_count, slots, width), F32), pltpu.VMEM((slots, width), F32),
             pltpu.SemaphoreType.DMA((7,)),
         ],
-        (notes, mine, other, act_out, grad_out),
-        0, [SMEM] + [VMEM] * 2 + [ANY] * 2, (ANY,) * 4,
+        (notes, *mine, *other, act_out, grad_out),
+        0, [SMEM] + [VMEM] * 4 + [ANY] * 2, (ANY,) * 4,
     )
     return act_out[None], grad_out[None], taps.transpose(1, 0, 2)[None], gains[None]
 

time: 56.2 us -> 55.2 us (0.982)
  waiting for transfers between devices: 5.26 us -> 1.14 us
  starting transfers between devices: 25.3 us -> 28.5 us
    ppermute x2 -> x4, waiting for transfers between devices: 3.38 us -> 0.01 us  [partner(): return lax.ppermute(x, 'tm', [(i, i ^ step) for i in range(shards)])]
    ppermute x2 -> x4, starting transfers between devices: 2.9 us -> 4.69 us  [partner(): return lax.ppermute(x, 'tm', [(i, i ^ step) for i in range(shards)])]
    ppermute x5, starting transfers between devices: 10.7 us -> 12 us  [shifted(): lax.ppermute(x, 'section', [(i, (i + by) % sections) for i in range(secti...]
    ppermute x5, waiting for transfers between devices: 0.77 us -> 0.01 us  [shifted(): lax.ppermute(x, 'section', [(i, (i + by) % sections) for i in range(secti...]
  transfers between devices with their start and end apart: 13 -> 15, of which waited for: 5 -> 2; matrix products, arithmetic and copies ran while one was open for 0% -> 0% of each run, Pallas kernels for 35% -> 35%
where the time goes in v18:
time: 55.2 us; the launch traced here: 54.9 us
  starting transfers between devices  28.5 us (52%)
  Pallas kernels  21.2 us (38%)
  local copies, waits for them, and re-layouts  2.99 us (5%)
  waiting for transfers between devices  1.14 us (2%)
  between operations  1.1 us (2%)
    pallas_call x12, Pallas kernels, call(): pl.pallas_call(kernel, out_shape=outs, in_specs=specs, out_specs=jax.tree...  21.2 us
    ppermute x5, starting transfers between devices, shifted(): lax.ppermute(x, 'section', [(i, (i + by) % sections) for i in range(secti...  12 us
    ppermute x6, starting transfers between devices, swapped(): results.append(lax.ppermute(x, ('section', 'tm'), pairs))  11.7 us
    ppermute x4, starting transfers between devices, partner(): return lax.ppermute(x, 'tm', [(i, i ^ step) for i in range(shards)])  4.69 us
    unnamed x36, local copies, waits for them, and re-layouts  2.99 us
    ppermute x6, waiting for transfers between devices, swapped(): results.append(lax.ppermute(x, ('section', 'tm'), pairs))  1.12 us
  transfers between devices with their start and end apart: 15, of which 2 were waited for; matrix products, arithmetic and copies ran while one was open for 0% of the time, Pallas kernels for 35%

profile of v18, /device:TPU:0, one launch (start us, length us, event | category | flops | bytes accessed | tf_op | source)
XLA Modules:
  0.0 54.9 jit_solution(14388167502822623710)
XLA Ops:
  0.7 3.1 %collective-permute-start.2 = (bf16[128,2048]{1,0:T(8,128)(2,1)}, bf16[128,2048]{1,0:T(8,128)(2,1)}, u32[]{:S(2)}, u32[]{:S(2)}) collective-permute-start(bf16[128,2048]{1,0:T(8,128)(2,1)} %bitcast.21), channel_id=1, source_target_pairs={{0,8},{4,12},{8,16},{12,20},{16,24},{20,28},{24,0},{28,4},{1,9},{5... | collective-permute-start | bytes 1572872 | tf_op jit(solution)/shard_map/ppermute | solution.py:537
  3.7 1.9 %shard_map.210 = (bf16[48,2048]{1,0:T(8,128)(2,1)}, bf16[48,2048]{1,0:T(8,128)(2,1)}, s32[8]{0:T(128)}) custom-call(bf16[2,128,2048]{2,1,0:T(8,128)(2,1)} %bitcast.15, bf16[1,128,2048]{2,1,0:T(8,128)(2,1)} %grad.1, s32[8]{0:T(128)} %back_lengths.1, s32[8]{0:T(128)} %ahead_lengths.1, s32[2,8]{1,0:T(2,128)} %bitcast.25, s32[2,8]{1,0:T(2,128)} %bitcast.26), custom_call_target="tpu_custom_call" | custom-call | tf_op jit(solution)/shard_map/pallas_call | solution.py:504
  5.6 0.7 %collective-permute-start = (bf16[48,2048]{1,0:T(8,128)(2,1)}, bf16[48,2048]{1,0:T(8,128)(2,1)S(1)}, u32[]{:S(2)}, u32[]{:S(2)}) collective-permute-start(bf16[48,2048]{1,0:T(8,128)(2,1)} %get-tuple-element.39), channel_id=1, source_target_pairs={{1,2},{2,1},{5,6},{6,5},{9,10},{10,9},{13,14},{14,13},{17,18},{18,... | collective-permute-start | bytes 589832 | tf_op jit(solution)/shard_map/ppermute | solution.py:549
  6.3 4.3 %collective-permute-start.1 = (bf16[48,2048]{1,0:T(8,128)(2,1)}, bf16[48,2048]{1,0:T(8,128)(2,1)S(1)}, u32[]{:S(2)}, u32[]{:S(2)}) collective-permute-start(bf16[48,2048]{1,0:T(8,128)(2,1)} %get-tuple-element.40), channel_id=1, source_target_pairs={{0,1},{1,0},{2,3},{3,2},{4,5},{5,4},{6,7},{7,6},{8,9},{9,8},{10,11... | collective-permute-start | bytes 589832 | tf_op jit(solution)/shard_map/ppermute | solution.py:549
  10.6 1.2 %copy-done = bf16[1,2,128,2048]{3,2,1,0:T(8,128)(2,1)S(1)} copy-done((bf16[1,2,128,2048]{3,2,1,0:T(8,128)(2,1)S(1)}, bf16[1,2,128,2048]{3,2,1,0:T(8,128)(2,1)}, u32[]{:S(2)}) %copy-start) | copy-done | bytes 1048600
  11.8 1.0 %copy-done.3 = bf16[1,128,2048]{2,1,0:T(8,128)(2,1)S(1)} copy-done((bf16[1,128,2048]{2,1,0:T(8,128)(2,1)S(1)}, bf16[1,128,2048]{2,1,0:T(8,128)(2,1)}, u32[]{:S(2)}) %copy-start.3) | copy-done | bytes 524312
  12.8 0.7 %copy-done.9 = s32[8]{0:T(128)S(1)} copy-done((s32[8]{0:T(128)S(1)}, s32[8]{0:T(128)}, u32[]{:S(2)}) %copy-start.9) | copy-done | bytes 56
  13.5 0.0 copy-start.16
  13.5 1.7 %shard_map.211 = (bf16[2,32,2048]{2,1,0:T(8,128)(2,1)S(1)}, bf16[32,2048]{1,0:T(8,128)(2,1)S(1)}, bf16[32,2048]{1,0:T(8,128)(2,1)S(1)}, bf16[64,2048]{1,0:T(8,12...) custom-call(s32[8]{0:T(128)S(1)} %copy-done.9, ...), custom_call_target="tpu_custom_call" | custom-call | tf_op jit(solution)/shard_map/pallas_call | solution.py:504
  15.2 0.1 collective-permute-start.13
  15.3 0.7 %collective-permute-start.6 = (bf16[64,2048]{1,0:T(8,128)(2,1)S(1)}, bf16[64,2048]{1,0:T(8,128)(2,1)S(1)}, u32[]{:S(2)}, u32[]{:S(2)}) collective-permute-start(bf16[64,2048]{1,0:T(8,128)(2,1)S(1)} %get-tuple-element.48), channel_id=1, source_target_pairs={{1,2},{2,1},{5,6},{6,5},{9,10},{10,9},{13,14},{14,13},{17,18},{18,... | collective-permute-start | bytes 786440 | tf_op jit(solution)/shard_map/ppermute | solution.py:549
  16.0 2.8 %collective-permute-start.7 = (bf16[64,2048]{1,0:T(8,128)(2,1)S(1)}, bf16[64,2048]{1,0:T(8,128)(2,1)S(1)}, u32[]{:S(2)}, u32[]{:S(2)}) collective-permute-start(bf16[64,2048]{1,0:T(8,128)(2,1)S(1)} %get-tuple-element.49), channel_id=1, source_target_pairs={{0,1},{1,0},{2,3},{3,2},{4,5},{5,4},{6,7},{7,6},{8,9},{9,8},{10,11... | collective-permute-start | bytes 786440 | tf_op jit(solution)/shard_map/ppermute | solution.py:549
  18.8 0.5 collective-permute-done.1.refs_3_
  19.3 3.5 %shard_map.212 = (bf16[128,2048]{1,0:T(8,128)(2,1)S(1)}, bf16[16,2048]{1,0:T(8,128)(2,1)S(1)}, bf16[16,2048]{1,0:T(8,128)(2,1)S(1)}, bf16[64,2048]{1,0:T(8,128)(...) custom-call(s32[8]{0:T(128)S(1)} %copy-done.10, bf16[2,128,2048]{2,1,0:T(8,128)(2,1)S(1)} %bitcast.17, ...), custom_call_target="tpu_custom_call" | custom-call | flops 4000000000 | tf_op jit(solution)/shard_map/pallas_call | solution.py:504
  22.9 0.8 %collective-permute-start.4 = (bf16[16,2048]{1,0:T(8,128)(2,1)S(1)}, bf16[16,2048]{1,0:T(8,128)(2,1)S(1)}, u32[]{:S(2)}, u32[]{:S(2)}) collective-permute-start(bf16[16,2048]{1,0:T(8,128)(2,1)S(1)} %get-tuple-element.46), channel_id=1, source_target_pairs={{1,30},{2,29},{5,2},{6,1},{9,6},{10,5},{13,10},{14,9},{17,14},{18,... | collective-permute-start | bytes 196616 | tf_op jit(solution)/shard_map/ppermute | solution.py:549
  23.7 2.5 %collective-permute-start.3 = (bf16[128,2048]{1,0:T(8,128)(2,1)S(1)}, bf16[128,2048]{1,0:T(8,128)(2,1)S(1)}, u32[]{:S(2)}, u32[]{:S(2)}) collective-permute-start(bf16[128,2048]{1,0:T(8,128)(2,1)S(1)} %get-tuple-element.45), channel_id=1, source_target_pairs={{0,28},{4,0},{8,4},{12,8},{16,12},{20,16},{24,20},{28,24},{1,29},{... | collective-permute-start | bytes 1572872 | tf_op jit(solution)/shard_map/ppermute | solution.py:537
  26.2 1.0 %shard_map.213.refs_4_.taps0 = bf16[32,2048]{1,0:T(8,128)(2,1)S(1)} custom-call(bf16[64,2048]{1,0:T(8,128)(2,1)S(1)} %get-tuple-element.51.halo, bf16[128,2048]{1,0:T(8,128)(2,1)S(1)} %get-tuple-element.42.refs_6_.masked, bf16[128,2048]{1,0:T(8,128)(2,1)S(1)} %get-tuple-element.52.inner, f32[1,2048]{1,0:T(1,128)S(1)} %get-tuple-element.53.gain_sum, ...), custom_call_target="tpu_custom_call" | custom-call | tf_op jit(solution)/shard_map/pallas_call | solution.py:504
  27.2 1.1 %shard_map.214 = (bf16[128,2048]{1,0:T(8,128)(2,1)S(1)}, f32[128,128]{1,0:T(8,128)S(1)}, f32[128,128]{1,0:T(8,128)S(1)}, f32[192,2048]{1,0:T(8,128)S(1)}) custom-call(s32[8]{0:T(128)S(1)} %copy-done.10, bf16[2,128,2048]{2,1,0:T(8,128)(2,1)S(1)} %bitcast.18, bf16[2,32,2048]{2,1,0:T(8,128)(2,1)S(1)} %get-tuple-element.41.refs_5_.refs_2_.weights, ...), custom_call_target="tpu_custom_call" | custom-call | flops 1000000000 | tf_op jit(solution)/shard_map/pallas_call | solution.py:504
  28.3 2.5 %collective-permute-start.5 = (bf16[16,2048]{1,0:T(8,128)(2,1)S(1)}, bf16[16,2048]{1,0:T(8,128)(2,1)S(1)}, u32[]{:S(2)}, u32[]{:S(2)}) collective-permute-start(bf16[16,2048]{1,0:T(8,128)(2,1)S(1)} %get-tuple-element.47), channel_id=1, source_target_pairs={{0,29},{1,28},{2,31},{3,30},{4,1},{5,0},{6,3},{7,2},{8,5},{9,4},{1... | collective-permute-start | bytes 196616 | tf_op jit(solution)/shard_map/ppermute | solution.py:549
  30.9 0.6 %collective-permute-done.7.near = bf16[64,2048]{1,0:T(8,128)(2,1)S(1)} collective-permute-done((bf16[64,2048]{1,0:T(8,128)(2,1)S(1)}, bf16[64,2048]{1,0:T(8,128)(2,1)S(1)}, u32[]{:S(2)}, u32[]{:S(2)}) %collective-permute-start.7) | collective-permute-done | bytes 262176 | tf_op jit(solution)/shard_map/ppermute | solution.py:549
  31.5 2.1 %shard_map.215 = (f32[192,2048]{1,0:T(8,128)S(1)}, f32[160,2048]{1,0:T(8,128)S(1)}, f32[128,2048]{1,0:T(8,128)S(1)}, bf16[96,2048]{1,0:T(8,128)(2,1)S(1)}) custom-call(s32[8]{0:T(128)S(1)} %copy-done.10, bf16[64,2048]{1,0:T(8,128)(2,1)S(1)} %collective-permute-done.6.far, bf16[64,2048]{1,0:T(8,128)(2,1)S(1)} %collective-permute-done.7.near, ...), custom_call_target="tpu_custom_call" | custom-call | flops 5000000000 | tf_op jit(solution)/shard_map/pallas_call | solution.py:504
  33.6 1.6 %collective-permute-start.12 = (bf16[96,2048]{1,0:T(8,128)(2,1)S(1)}, bf16[96,2048]{1,0:T(8,128)(2,1)S(1)}, u32[]{:S(2)}, u32[]{:S(2)}) collective-permute-start(bf16[96,2048]{1,0:T(8,128)(2,1)S(1)} %get-tuple-element.63), channel_id=1, source_target_pairs={{0,8},{4,12},{8,16},{12,20},{16,24},{20,28},{24,0},{28,4},{1,9},{5... | collective-permute-start | bytes 1179656 | tf_op jit(solution)/shard_map/ppermute | solution.py:537
  35.2 1.4 %shard_map.216 = (bf16[160,2048]{1,0:T(8,128)(2,1)S(1)}, bf16[32,2048]{1,0:T(8,128)(2,1)S(1)}, bf16[32,2048]{1,0:T(8,128)(2,1)S(1)}) custom-call(s32[8]{0:T(128)S(1)} %copy-done.10, bf16[128,2048]{1,0:T(8,128)(2,1)S(1)} %collective-permute-done.3.received, bf16[16,2048]{1,0:T(8,128)(2,1)S(1)} %collective-permute-done.4.far, ...), custom_call_target="tpu_custom_call" | custom-call | flops 2000000000 | tf_op jit(solution)/shard_map/pallas_call | solution.py:504
  36.6 2.5 %collective-permute-start.8 = (bf16[32,2048]{1,0:T(8,128)(2,1)S(1)}, bf16[32,2048]{1,0:T(8,128)(2,1)S(1)}, u32[]{:S(2)}, u32[]{:S(2)}) collective-permute-start(bf16[32,2048]{1,0:T(8,128)(2,1)S(1)} %get-tuple-element.59.mine0), channel_id=1, source_target_pairs={{0,1},{1,0},{2,3},{3,2},{4,5},{5,4},{6,7},{7,6},{8,9},{9,8},{10,11... | collective-permute-start | bytes 393224 | tf_op jit(solution)/shard_map/ppermute | solution.py:625
  39.1 2.0 %shard_map.220 = bf16[128,2048]{1,0:T(8,128)(2,1)S(1)} custom-call(s32[8]{0:T(128)S(1)} %copy-done.10, bf16[2,128,2048]{2,1,0:T(8,128)(2,1)S(1)} %bitcast.19, bf16[128,2048]{1,0:T(8,128)(2,1)S(1)} %collective-permute-done.3.received, bf16[2,32,2048]{2,1,0:T(8,128)(2,1)S(1)} %get-tuple-element.41.refs_5_.refs_2_.weights, ...), custom_call_target="tpu_custom_call" | custom-call | flops 6000000000 | tf_op jit(solution)/shard_map/pallas_call | solution.py:504
  41.1 4.8 %collective-permute-start.14 = (bf16[128,2048]{1,0:T(8,128)(2,1)S(1)}, bf16[128,2048]{1,0:T(8,128)(2,1)S(1)}, u32[]{:S(2)}, u32[]{:S(2)}) collective-permute-start(bf16[128,2048]{1,0:T(8,128)(2,1)S(1)} %shard_map.220), channel_id=1, source_target_pairs={{0,28},{4,0},{8,4},{12,8},{16,12},{20,16},{24,20},{28,24},{1,29},{... | collective-permute-start | bytes 1572872 | tf_op jit(solution)/shard_map/ppermute | solution.py:537
  45.9 0.1 shard_map.217
  45.9 0.4 collective-permute-start.11
  46.4 1.7 %collective-permute-start.10 = (bf16[32,2048]{1,0:T(8,128)(2,1)S(1)}, bf16[32,2048]{1,0:T(8,128)(2,1)S(1)}, u32[]{:S(2)}, u32[]{:S(2)}) collective-permute-start(bf16[32,2048]{1,0:T(8,128)(2,1)S(1)} %get-tuple-element.61.refs_6_.mine0), channel_id=1, source_target_pairs={{0,2},{1,3},{2,0},{3,1},{4,6},{5,7},{6,4},{7,5},{8,10},{9,11},{10,... | collective-permute-start | bytes 393224 | tf_op jit(solution)/shard_map/ppermute | solution.py:625
  48.1 2.8 %shard_map.218.between = bf16[160,2048]{1,0:T(8,128)(2,1)S(1)} custom-call(s32[8]{0:T(128)S(1)} %copy-done.10, bf16[128,2048]{1,0:T(8,128)(2,1)} %collective-permute-done.2.refs_14_.refs_1_, bf16[96,2048]{1,0:T(8,128)(2,1)S(1)} %collective-permute-done.12.refs_2_, bf16[384,192]{1,0:T(8,128)(2,1)S(1)} %copy-done.5, bf16[192,64]{1,0:T(8,128)(2,1)S(1)} %copy-done.16, ...), custom_call_target="tpu_custom_call" | custom-call | flops 10000000000 | tf_op jit(solution)/shard_map/pallas_call | solution.py:504
  51.0 1.9 %shard_map.219.act = bf16[128,2048]{1,0:T(8,128)(2,1)S(1)} custom-call(s32[8]{0:T(128)S(1)} %copy-done.10, bf16[160,2048]{1,0:T(8,128)(2,1)S(1)} %shard_map.218.between, bf16[32,2048]{1,0:T(8,128)(2,1)S(1)} %collective-permute-done.13.layer, bf16[320,160]{1,0:T(8,128)(2,1)S(1)} %copy-done.12, bf16[160,64]{1,0:T(8,128)(2,1)S(1)} %copy-done.17, ...), custom_call_target="tpu_custom_call" | custom-call | flops 10000000000 | tf_op jit(solution)/shard_map/pallas_call | solution.py:504
  53.0 1.7 %shard_map.221 = (bf16[128,2048]{1,0:T(8,128)(2,1)}, bf16[128,2048]{1,0:T(8,128)(2,1)}, f32[31,2,2048]{2,1,0:T(2,128)}, f32[2,2048]{1,0:T(2,128)}) custom-call(s32[8]{0:T(128)S(1)} %copy-done.10, bf16[32,2048]{1,0:T(8,128)(2,1)S(1)} %get-tuple-element.61.refs_6_.mine0, bf16[32,2048]{1,0:T(8,128)(2,1)S(1)} %get-tuple-element.62.mine1, ...), custom_call_target="tpu_custom_call" | custom-call | tf_op jit(solution)/shard_map/pallas_call | solution.py:504
  (46 shorter events, 0.1 us)
Async XLA Ops:
  0.6 9.9 %copy-start.8 = (bf16[1,2,2048]{2,1,0:T(2,128)(2,1)S(1)}, bf16[1,2,2048]{2,1,0:T(2,128)(2,1)}, u32[]{:S(2)}) copy-start(bf16[1,2,2048]{2,1,0:T(2,128)(2,1)} %param.23) | copy-start | bytes 24580
  0.6 9.9 %copy-start.4 = (bf16[1,2,31,2048]{3,1,2,0:T(2,128)(2,1)S(1)}, bf16[1,2,31,2048]{3,1,2,0:T(2,128)(2,1)}, u32[]{:S(2)}) copy-start(bf16[1,2,31,2048]{3,1,2,0:T(2,128)(2,1)} %param.22) | copy-start | bytes 761860
  0.7 18.6 %collective-permute-start.2 = (bf16[128,2048]{1,0:T(8,128)(2,1)}, bf16[128,2048]{1,0:T(8,128)(2,1)}, u32[]{:S(2)}, u32[]{:S(2)}) collective-permute-start(bf16[128,2048]{1,0:T(8,128)(2,1)} %bitcast.21), channel_id=1, source_target_pairs={{0,8},{4,12},{8,16},{12,20},{16,24},{20,28},{24,0},{28,4},{1,9},{5... | collective-permute-start | bytes 1572872 | tf_op jit(solution)/shard_map/ppermute | solution.py:537
  3.7 15.5 %copy-start.5 = (bf16[384,192]{1,0:T(8,128)(2,1)S(1)}, bf16[384,192]{1,0:T(8,128)(2,1)}, u32[]{:S(2)}) copy-start(bf16[384,192]{1,0:T(8,128)(2,1)} %constant.20.clone.refs_9_.m_table.refs_3_) | copy-start | bytes 442372
  5.6 13.7 %copy-start.10 = (s32[8]{0:T(128)S(1)}, s32[8]{0:T(128)}, u32[]{:S(2)}) copy-start(s32[8]{0:T(128)} %get-tuple-element.38.notes.refs_0_) | copy-start | bytes 100
  5.6 10.4 %collective-permute-start = (bf16[48,2048]{1,0:T(8,128)(2,1)}, bf16[48,2048]{1,0:T(8,128)(2,1)S(1)}, u32[]{:S(2)}, u32[]{:S(2)}) collective-permute-start(bf16[48,2048]{1,0:T(8,128)(2,1)} %get-tuple-element.39), channel_id=1, source_target_pairs={{1,2},{2,1},{5,6},{6,5},{9,10},{10,9},{13,14},{14,13},{17,18},{18,... | collective-permute-start | bytes 589832 | tf_op jit(solution)/shard_map/ppermute | solution.py:549
  6.3 13.0 %collective-permute-start.1 = (bf16[48,2048]{1,0:T(8,128)(2,1)}, bf16[48,2048]{1,0:T(8,128)(2,1)S(1)}, u32[]{:S(2)}, u32[]{:S(2)}) collective-permute-start(bf16[48,2048]{1,0:T(8,128)(2,1)} %get-tuple-element.40), channel_id=1, source_target_pairs={{0,1},{1,0},{2,3},{3,2},{4,5},{5,4},{6,7},{7,6},{8,9},{9,8},{10,11... | collective-permute-start | bytes 589832 | tf_op jit(solution)/shard_map/ppermute | solution.py:549
  10.6 1.2 %copy-start = (bf16[1,2,128,2048]{3,2,1,0:T(8,128)(2,1)S(1)}, bf16[1,2,128,2048]{3,2,1,0:T(8,128)(2,1)}, u32[]{:S(2)}) copy-start(bf16[1,2,128,2048]{3,2,1,0:T(8,128)(2,1)} %param.21) | copy-start | bytes 3145732
  11.8 1.0 %copy-start.3 = (bf16[1,128,2048]{2,1,0:T(8,128)(2,1)S(1)}, bf16[1,128,2048]{2,1,0:T(8,128)(2,1)}, u32[]{:S(2)}) copy-start(bf16[1,128,2048]{2,1,0:T(8,128)(2,1)} %param.19) | copy-start | bytes 1572868
  13.5 5.8 %copy-start.2 = (bf16[1,128,2048]{2,1,0:T(8,128)(2,1)S(1)}, bf16[1,128,2048]{2,1,0:T(8,128)(2,1)}, u32[]{:S(2)}) copy-start(bf16[1,128,2048]{2,1,0:T(8,128)(2,1)} %grad.1) | copy-start | bytes 1572868
  13.5 5.8 %copy-start.11 = (bf16[384,160]{1,0:T(8,128)(2,1)S(1)}, bf16[384,160]{1,0:T(8,128)(2,1)}, u32[]{:S(2)}) copy-start(bf16[384,160]{1,0:T(8,128)(2,1)} %constant.23.clone.refs_12_.g_table) | copy-start | bytes 368644
  13.5 5.8 %copy-start.13 = (bf16[320,192]{1,0:T(8,128)(2,1)S(1)}, bf16[320,192]{1,0:T(8,128)(2,1)}, u32[]{:S(2)}) copy-start(bf16[320,192]{1,0:T(8,128)(2,1)} %constant.22.clone.refs_11_.c_table.refs_5_) | copy-start | bytes 368644
  13.5 5.8 %copy-start.15 = (bf16[256,192]{1,0:T(8,128)(2,1)S(1)}, bf16[256,192]{1,0:T(8,128)(2,1)}, u32[]{:S(2)}) copy-start(bf16[256,192]{1,0:T(8,128)(2,1)} %constant.24.clone.refs_13_.x_table) | copy-start | bytes 294916
  13.5 5.8 %copy-start.16 = (bf16[192,64]{1,0:T(8,128)(2,1)S(1)}, bf16[192,64]{1,0:T(8,128)(2,1)}, u32[]{:S(2)}) copy-start(bf16[192,64]{1,0:T(8,128)(2,1)} %constant.21.clone.refs_10_.refs_3_.refs_4_) | copy-start | bytes 73732
  15.2 35.7 %collective-permute-start.13 = (bf16[32,2048]{1,0:T(8,128)(2,1)S(1)}, bf16[32,2048]{1,0:T(8,128)(2,1)S(1)}, u32[]{:S(2)}, u32[]{:S(2)}) collective-permute-start(bf16[32,2048]{1,0:T(8,128)(2,1)S(1)} %get-tuple-element.64), channel_id=1, source_target_pairs={{0,4},{4,8},{8,12},{12,16},{16,20},{20,24},{24,28},{28,0},{1,5},{5... | collective-permute-start | bytes 393224 | tf_op jit(solution)/shard_map/ppermute | solution.py:537
  15.3 13.0 %collective-permute-start.6 = (bf16[64,2048]{1,0:T(8,128)(2,1)S(1)}, bf16[64,2048]{1,0:T(8,128)(2,1)S(1)}, u32[]{:S(2)}, u32[]{:S(2)}) collective-permute-start(bf16[64,2048]{1,0:T(8,128)(2,1)S(1)} %get-tuple-element.48), channel_id=1, source_target_pairs={{1,2},{2,1},{5,6},{6,5},{9,10},{10,9},{13,14},{14,13},{17,18},{18,... | collective-permute-start | bytes 786440 | tf_op jit(solution)/shard_map/ppermute | solution.py:549
  16.0 15.5 %collective-permute-start.7 = (bf16[64,2048]{1,0:T(8,128)(2,1)S(1)}, bf16[64,2048]{1,0:T(8,128)(2,1)S(1)}, u32[]{:S(2)}, u32[]{:S(2)}) collective-permute-start(bf16[64,2048]{1,0:T(8,128)(2,1)S(1)} %get-tuple-element.49), channel_id=1, source_target_pairs={{0,1},{1,0},{2,3},{3,2},{4,5},{5,4},{6,7},{7,6},{8,9},{9,8},{10,11... | collective-permute-start | bytes 786440 | tf_op jit(solution)/shard_map/ppermute | solution.py:549
  19.3 6.9 %copy-start.6 = (bf16[192,256]{1,0:T(8,128)(2,1)S(1)}, bf16[192,256]{1,0:T(8,128)(2,1)}, u32[]{:S(2)}) copy-start(bf16[192,256]{1,0:T(8,128)(2,1)} %constant.25.clone.go_table) | copy-start | bytes 294916
  19.3 6.9 %copy-start.7 = (bf16[64,192]{1,0:T(8,128)(2,1)S(1)}, bf16[64,192]{1,0:T(8,128)(2,1)}, u32[]{:S(2)}) copy-start(bf16[64,192]{1,0:T(8,128)(2,1)} %constant.26.clone.t_table) | copy-start | bytes 73732
  22.8 4.4 %copy-start.1 = (bf16[1,2,128,2048]{3,2,1,0:T(8,128)(2,1)S(1)}, bf16[1,2,128,2048]{3,2,1,0:T(8,128)(2,1)}, u32[]{:S(2)}) copy-start(bf16[1,2,128,2048]{3,2,1,0:T(8,128)(2,1)} %param.21) | copy-start | bytes 3145732
  22.9 12.3 %collective-permute-start.4 = (bf16[16,2048]{1,0:T(8,128)(2,1)S(1)}, bf16[16,2048]{1,0:T(8,128)(2,1)S(1)}, u32[]{:S(2)}, u32[]{:S(2)}) collective-permute-start(bf16[16,2048]{1,0:T(8,128)(2,1)S(1)} %get-tuple-element.46), channel_id=1, source_target_pairs={{1,30},{2,29},{5,2},{6,1},{9,6},{10,5},{13,10},{14,9},{17,14},{18,... | collective-permute-start | bytes 196616 | tf_op jit(solution)/shard_map/ppermute | solution.py:549
  23.7 11.6 %collective-permute-start.3 = (bf16[128,2048]{1,0:T(8,128)(2,1)S(1)}, bf16[128,2048]{1,0:T(8,128)(2,1)S(1)}, u32[]{:S(2)}, u32[]{:S(2)}) collective-permute-start(bf16[128,2048]{1,0:T(8,128)(2,1)S(1)} %get-tuple-element.45), channel_id=1, source_target_pairs={{0,28},{4,0},{8,4},{12,8},{16,12},{20,16},{24,20},{28,24},{1,29},{... | collective-permute-start | bytes 1572872 | tf_op jit(solution)/shard_map/ppermute | solution.py:537
  28.3 6.9 %collective-permute-start.5 = (bf16[16,2048]{1,0:T(8,128)(2,1)S(1)}, bf16[16,2048]{1,0:T(8,128)(2,1)S(1)}, u32[]{:S(2)}, u32[]{:S(2)}) collective-permute-start(bf16[16,2048]{1,0:T(8,128)(2,1)S(1)} %get-tuple-element.47), channel_id=1, source_target_pairs={{0,29},{1,28},{2,31},{3,30},{4,1},{5,0},{6,3},{7,2},{8,5},{9,4},{1... | collective-permute-start | bytes 196616 | tf_op jit(solution)/shard_map/ppermute | solution.py:549
  33.6 14.6 %collective-permute-start.12 = (bf16[96,2048]{1,0:T(8,128)(2,1)S(1)}, bf16[96,2048]{1,0:T(8,128)(2,1)S(1)}, u32[]{:S(2)}, u32[]{:S(2)}) collective-permute-start(bf16[96,2048]{1,0:T(8,128)(2,1)S(1)} %get-tuple-element.63), channel_id=1, source_target_pairs={{0,8},{4,12},{8,16},{12,20},{16,24},{20,28},{24,0},{28,4},{1,9},{5... | collective-permute-start | bytes 1179656 | tf_op jit(solution)/shard_map/ppermute | solution.py:537
  36.6 9.3 %collective-permute-start.8 = (bf16[32,2048]{1,0:T(8,128)(2,1)S(1)}, bf16[32,2048]{1,0:T(8,128)(2,1)S(1)}, u32[]{:S(2)}, u32[]{:S(2)}) collective-permute-start(bf16[32,2048]{1,0:T(8,128)(2,1)S(1)} %get-tuple-element.59.mine0), channel_id=1, source_target_pairs={{0,1},{1,0},{2,3},{3,2},{4,5},{5,4},{6,7},{7,6},{8,9},{9,8},{10,11... | collective-permute-start | bytes 393224 | tf_op jit(solution)/shard_map/ppermute | solution.py:625
  39.1 6.7 %collective-permute-start.9 = (bf16[32,2048]{1,0:T(8,128)(2,1)S(1)}, bf16[32,2048]{1,0:T(8,128)(2,1)S(1)}, u32[]{:S(2)}, u32[]{:S(2)}) collective-permute-start(bf16[32,2048]{1,0:T(8,128)(2,1)S(1)} %get-tuple-element.60.mine1), channel_id=1, source_target_pairs={{0,2},{1,3},{2,0},{3,1},{4,6},{5,7},{6,4},{7,5},{8,10},{9,11},{10,... | collective-permute-start | bytes 393224 | tf_op jit(solution)/shard_map/ppermute | solution.py:625
  41.1 11.9 %collective-permute-start.14 = (bf16[128,2048]{1,0:T(8,128)(2,1)S(1)}, bf16[128,2048]{1,0:T(8,128)(2,1)S(1)}, u32[]{:S(2)}, u32[]{:S(2)}) collective-permute-start(bf16[128,2048]{1,0:T(8,128)(2,1)S(1)} %shard_map.220), channel_id=1, source_target_pairs={{0,28},{4,0},{8,4},{12,8},{16,12},{20,16},{24,20},{28,24},{1,29},{... | collective-permute-start | bytes 1572872 | tf_op jit(solution)/shard_map/ppermute | solution.py:537
  45.9 7.0 %collective-permute-start.11 = (bf16[32,2048]{1,0:T(8,128)(2,1)S(1)}, bf16[32,2048]{1,0:T(8,128)(2,1)S(1)}, u32[]{:S(2)}, u32[]{:S(2)}) collective-permute-start(bf16[32,2048]{1,0:T(8,128)(2,1)S(1)} %get-tuple-element.62.mine1), channel_id=1, source_target_pairs={{0,1},{1,0},{2,3},{3,2},{4,5},{5,4},{6,7},{7,6},{8,9},{9,8},{10,11... | collective-permute-start | bytes 393224 | tf_op jit(solution)/shard_map/ppermute | solution.py:625
  46.4 4.6 %copy-start.12 = (bf16[320,160]{1,0:T(8,128)(2,1)S(1)}, bf16[320,160]{1,0:T(8,128)(2,1)}, u32[]{:S(2)}) copy-start(bf16[320,160]{1,0:T(8,128)(2,1)} %constant.27.clone.m_table) | copy-start | bytes 307204
  46.4 4.6 %copy-start.14 = (bf16[256,160]{1,0:T(8,128)(2,1)S(1)}, bf16[256,160]{1,0:T(8,128)(2,1)}, u32[]{:S(2)}) copy-start(bf16[256,160]{1,0:T(8,128)(2,1)} %constant.29.clone.c_table) | copy-start | bytes 245764
  46.4 4.6 %copy-start.17 = (bf16[160,64]{1,0:T(8,128)(2,1)S(1)}, bf16[160,64]{1,0:T(8,128)(2,1)}, u32[]{:S(2)}) copy-start(bf16[160,64]{1,0:T(8,128)(2,1)} %constant.28.clone.q_table) | copy-start | bytes 61444
  46.4 6.6 %collective-permute-start.10 = (bf16[32,2048]{1,0:T(8,128)(2,1)S(1)}, bf16[32,2048]{1,0:T(8,128)(2,1)S(1)}, u32[]{:S(2)}, u32[]{:S(2)}) collective-permute-start(bf16[32,2048]{1,0:T(8,128)(2,1)S(1)} %get-tuple-element.61.refs_6_.mine0), channel_id=1, source_target_pairs={{0,2},{1,3},{2,0},{3,1},{4,6},{5,7},{6,4},{7,5},{8,10},{9,11},{10,... | collective-permute-start | bytes 393224 | tf_op jit(solution)/shard_map/ppermute | solution.py:625
  (1 other events, 0.7 us)

commit v19 on v18

--- a/solution.py
+++ b/solution.py
@@ -56,6 +56,10 @@
 
 def transform(table, values):
     return sum(halves(dot(table[...], values.astype(BF16))))
+
+
+def rounded_transform(table, values):
+    return dot(table[: table.shape[0] // 2], values.astype(BF16))
 
 
 def halves(values):
@@ -401,7 +405,7 @@
 
     def block(columns):
         q = tap_spectrum(q_table[...], layer[:, columns])
-        conv = transform(c_table, product(transform(m_table, joined(halo, masked, columns)), q))
+        conv = rounded_transform(c_table, product(rounded_transform(m_table, joined(halo, masked, columns)), q))
         out[:, columns] = (window(inner, columns).astype(F32) + conv * sigmoid(conv)).astype(BF16)
 
     each_block(width, block)
@@ -416,7 +420,7 @@
 
     def block(columns):
         q = tap_spectrum(q_table[...], layer[:, columns])
-        conv = transform(c_table, product(transform(m_table, masked[:, columns]), q))
+        conv = rounded_transform(c_table, product(rounded_transform(m_table, masked[:, columns]), q))
         out[:, columns] = (between[edge : edge + own, columns].astype(F32) + conv * sigmoid(conv)).astype(BF16)
 
     each_block(width, block)

time: 55.2 us -> 55 us (level)
  no operation moved by 1% of the time
where the time goes in v19:
time: 55 us; the launch traced here: 54.7 us
  starting transfers between devices  28.5 us (52%)
  Pallas kernels  21 us (38%)
  local copies, waits for them, and re-layouts  2.99 us (5%)
  waiting for transfers between devices  1.14 us (2%)
  between operations  1.1 us (2%)
    pallas_call x12, Pallas kernels, call(): pl.pallas_call(kernel, out_shape=outs, in_specs=specs, out_specs=jax.tree...  21 us
    ppermute x5, starting transfers between devices, shifted(): lax.ppermute(x, 'section', [(i, (i + by) % sections) for i in range(secti...  12 us
    ppermute x6, starting transfers between devices, swapped(): results.append(lax.ppermute(x, ('section', 'tm'), pairs))  11.7 us
    ppermute x4, starting transfers between devices, partner(): return lax.ppermute(x, 'tm', [(i, i ^ step) for i in range(shards)])  4.69 us
    unnamed x36, local copies, waits for them, and re-layouts  2.99 us
    ppermute x6, waiting for transfers between devices, swapped(): results.append(lax.ppermute(x, ('section', 'tm'), pairs))  1.12 us
  transfers between devices with their start and end apart: 15, of which 2 were waited for; matrix products, arithmetic and copies ran while one was open for 0% of the time, Pallas kernels for 35%

profile of v19, /device:TPU:0, one launch (start us, length us, event | category | flops | bytes accessed | tf_op | source)
XLA Modules:
  0.0 54.7 jit_solution(1514693357556616050)
XLA Ops:
  0.7 3.1 %collective-permute-start.2 = (bf16[128,2048]{1,0:T(8,128)(2,1)}, bf16[128,2048]{1,0:T(8,128)(2,1)}, u32[]{:S(2)}, u32[]{:S(2)}) collective-permute-start(bf16[128,2048]{1,0:T(8,128)(2,1)} %bitcast.21), channel_id=1, source_target_pairs={{0,8},{4,12},{8,16},{12,20},{16,24},{20,28},{24,0},{28,4},{1,9},{5... | collective-permute-start | bytes 1572872 | tf_op jit(solution)/shard_map/ppermute | solution.py:541
  3.7 1.9 %shard_map.210 = (bf16[48,2048]{1,0:T(8,128)(2,1)}, bf16[48,2048]{1,0:T(8,128)(2,1)}, s32[8]{0:T(128)}) custom-call(bf16[2,128,2048]{2,1,0:T(8,128)(2,1)} %bitcast.15, bf16[1,128,2048]{2,1,0:T(8,128)(2,1)} %grad.1, s32[8]{0:T(128)} %back_lengths.1, s32[8]{0:T(128)} %ahead_lengths.1, s32[2,8]{1,0:T(2,128)} %bitcast.25, s32[2,8]{1,0:T(2,128)} %bitcast.26), custom_call_target="tpu_custom_call" | custom-call | tf_op jit(solution)/shard_map/pallas_call | solution.py:508
  5.6 0.7 %collective-permute-start = (bf16[48,2048]{1,0:T(8,128)(2,1)}, bf16[48,2048]{1,0:T(8,128)(2,1)S(1)}, u32[]{:S(2)}, u32[]{:S(2)}) collective-permute-start(bf16[48,2048]{1,0:T(8,128)(2,1)} %get-tuple-element.39), channel_id=1, source_target_pairs={{1,2},{2,1},{5,6},{6,5},{9,10},{10,9},{13,14},{14,13},{17,18},{18,... | collective-permute-start | bytes 589832 | tf_op jit(solution)/shard_map/ppermute | solution.py:553
  6.3 4.3 %collective-permute-start.1 = (bf16[48,2048]{1,0:T(8,128)(2,1)}, bf16[48,2048]{1,0:T(8,128)(2,1)S(1)}, u32[]{:S(2)}, u32[]{:S(2)}) collective-permute-start(bf16[48,2048]{1,0:T(8,128)(2,1)} %get-tuple-element.40), channel_id=1, source_target_pairs={{0,1},{1,0},{2,3},{3,2},{4,5},{5,4},{6,7},{7,6},{8,9},{9,8},{10,11... | collective-permute-start | bytes 589832 | tf_op jit(solution)/shard_map/ppermute | solution.py:553
  10.6 1.2 %copy-done = bf16[1,2,128,2048]{3,2,1,0:T(8,128)(2,1)S(1)} copy-done((bf16[1,2,128,2048]{3,2,1,0:T(8,128)(2,1)S(1)}, bf16[1,2,128,2048]{3,2,1,0:T(8,128)(2,1)}, u32[]{:S(2)}) %copy-start) | copy-done | bytes 1048600
  11.8 1.0 %copy-done.3 = bf16[1,128,2048]{2,1,0:T(8,128)(2,1)S(1)} copy-done((bf16[1,128,2048]{2,1,0:T(8,128)(2,1)S(1)}, bf16[1,128,2048]{2,1,0:T(8,128)(2,1)}, u32[]{:S(2)}) %copy-start.3) | copy-done | bytes 524312
  12.8 0.7 %copy-done.9 = s32[8]{0:T(128)S(1)} copy-done((s32[8]{0:T(128)S(1)}, s32[8]{0:T(128)}, u32[]{:S(2)}) %copy-start.9) | copy-done | bytes 56
  13.5 0.0 copy-start.16
  13.5 1.7 %shard_map.211 = (bf16[2,32,2048]{2,1,0:T(8,128)(2,1)S(1)}, bf16[32,2048]{1,0:T(8,128)(2,1)S(1)}, bf16[32,2048]{1,0:T(8,128)(2,1)S(1)}, bf16[64,2048]{1,0:T(8,12...) custom-call(s32[8]{0:T(128)S(1)} %copy-done.9, ...), custom_call_target="tpu_custom_call" | custom-call | tf_op jit(solution)/shard_map/pallas_call | solution.py:508
  15.2 0.1 collective-permute-start.13
  15.3 0.7 %collective-permute-start.6 = (bf16[64,2048]{1,0:T(8,128)(2,1)S(1)}, bf16[64,2048]{1,0:T(8,128)(2,1)S(1)}, u32[]{:S(2)}, u32[]{:S(2)}) collective-permute-start(bf16[64,2048]{1,0:T(8,128)(2,1)S(1)} %get-tuple-element.48), channel_id=1, source_target_pairs={{1,2},{2,1},{5,6},{6,5},{9,10},{10,9},{13,14},{14,13},{17,18},{18,... | collective-permute-start | bytes 786440 | tf_op jit(solution)/shard_map/ppermute | solution.py:553
  16.0 2.8 %collective-permute-start.7 = (bf16[64,2048]{1,0:T(8,128)(2,1)S(1)}, bf16[64,2048]{1,0:T(8,128)(2,1)S(1)}, u32[]{:S(2)}, u32[]{:S(2)}) collective-permute-start(bf16[64,2048]{1,0:T(8,128)(2,1)S(1)} %get-tuple-element.49), channel_id=1, source_target_pairs={{0,1},{1,0},{2,3},{3,2},{4,5},{5,4},{6,7},{7,6},{8,9},{9,8},{10,11... | collective-permute-start | bytes 786440 | tf_op jit(solution)/shard_map/ppermute | solution.py:553
  18.8 0.5 collective-permute-done.1.refs_3_
  19.3 3.5 %shard_map.212 = (bf16[128,2048]{1,0:T(8,128)(2,1)S(1)}, bf16[16,2048]{1,0:T(8,128)(2,1)S(1)}, bf16[16,2048]{1,0:T(8,128)(2,1)S(1)}, bf16[64,2048]{1,0:T(8,128)(...) custom-call(s32[8]{0:T(128)S(1)} %copy-done.10, bf16[2,128,2048]{2,1,0:T(8,128)(2,1)S(1)} %bitcast.17, ...), custom_call_target="tpu_custom_call" | custom-call | flops 4000000000 | tf_op jit(solution)/shard_map/pallas_call | solution.py:508
  22.9 0.8 %collective-permute-start.4 = (bf16[16,2048]{1,0:T(8,128)(2,1)S(1)}, bf16[16,2048]{1,0:T(8,128)(2,1)S(1)}, u32[]{:S(2)}, u32[]{:S(2)}) collective-permute-start(bf16[16,2048]{1,0:T(8,128)(2,1)S(1)} %get-tuple-element.46), channel_id=1, source_target_pairs={{1,30},{2,29},{5,2},{6,1},{9,6},{10,5},{13,10},{14,9},{17,14},{18,... | collective-permute-start | bytes 196616 | tf_op jit(solution)/shard_map/ppermute | solution.py:553
  23.7 2.5 %collective-permute-start.3 = (bf16[128,2048]{1,0:T(8,128)(2,1)S(1)}, bf16[128,2048]{1,0:T(8,128)(2,1)S(1)}, u32[]{:S(2)}, u32[]{:S(2)}) collective-permute-start(bf16[128,2048]{1,0:T(8,128)(2,1)S(1)} %get-tuple-element.45), channel_id=1, source_target_pairs={{0,28},{4,0},{8,4},{12,8},{16,12},{20,16},{24,20},{28,24},{1,29},{... | collective-permute-start | bytes 1572872 | tf_op jit(solution)/shard_map/ppermute | solution.py:541
  26.2 1.0 %shard_map.213.refs_4_.taps0 = bf16[32,2048]{1,0:T(8,128)(2,1)S(1)} custom-call(bf16[64,2048]{1,0:T(8,128)(2,1)S(1)} %get-tuple-element.51.halo, bf16[128,2048]{1,0:T(8,128)(2,1)S(1)} %get-tuple-element.42.refs_6_.masked, bf16[128,2048]{1,0:T(8,128)(2,1)S(1)} %get-tuple-element.52.inner, f32[1,2048]{1,0:T(1,128)S(1)} %get-tuple-element.53.gain_sum, ...), custom_call_target="tpu_custom_call" | custom-call | tf_op jit(solution)/shard_map/pallas_call | solution.py:508
  27.2 1.1 %shard_map.214 = (bf16[128,2048]{1,0:T(8,128)(2,1)S(1)}, f32[128,128]{1,0:T(8,128)S(1)}, f32[128,128]{1,0:T(8,128)S(1)}, f32[192,2048]{1,0:T(8,128)S(1)}) custom-call(s32[8]{0:T(128)S(1)} %copy-done.10, bf16[2,128,2048]{2,1,0:T(8,128)(2,1)S(1)} %bitcast.18, bf16[2,32,2048]{2,1,0:T(8,128)(2,1)S(1)} %get-tuple-element.41.refs_5_.refs_2_.weights, ...), custom_call_target="tpu_custom_call" | custom-call | flops 1000000000 | tf_op jit(solution)/shard_map/pallas_call | solution.py:508
  28.3 2.5 %collective-permute-start.5 = (bf16[16,2048]{1,0:T(8,128)(2,1)S(1)}, bf16[16,2048]{1,0:T(8,128)(2,1)S(1)}, u32[]{:S(2)}, u32[]{:S(2)}) collective-permute-start(bf16[16,2048]{1,0:T(8,128)(2,1)S(1)} %get-tuple-element.47), channel_id=1, source_target_pairs={{0,29},{1,28},{2,31},{3,30},{4,1},{5,0},{6,3},{7,2},{8,5},{9,4},{1... | collective-permute-start | bytes 196616 | tf_op jit(solution)/shard_map/ppermute | solution.py:553
  30.9 0.6 %collective-permute-done.7.near = bf16[64,2048]{1,0:T(8,128)(2,1)S(1)} collective-permute-done((bf16[64,2048]{1,0:T(8,128)(2,1)S(1)}, bf16[64,2048]{1,0:T(8,128)(2,1)S(1)}, u32[]{:S(2)}, u32[]{:S(2)}) %collective-permute-start.7) | collective-permute-done | bytes 262176 | tf_op jit(solution)/shard_map/ppermute | solution.py:553
  31.5 2.1 %shard_map.215 = (f32[192,2048]{1,0:T(8,128)S(1)}, f32[160,2048]{1,0:T(8,128)S(1)}, f32[128,2048]{1,0:T(8,128)S(1)}, bf16[96,2048]{1,0:T(8,128)(2,1)S(1)}) custom-call(s32[8]{0:T(128)S(1)} %copy-done.10, bf16[64,2048]{1,0:T(8,128)(2,1)S(1)} %collective-permute-done.6.far, bf16[64,2048]{1,0:T(8,128)(2,1)S(1)} %collective-permute-done.7.near, ...), custom_call_target="tpu_custom_call" | custom-call | flops 5000000000 | tf_op jit(solution)/shard_map/pallas_call | solution.py:508
  33.6 1.6 %collective-permute-start.12 = (bf16[96,2048]{1,0:T(8,128)(2,1)S(1)}, bf16[96,2048]{1,0:T(8,128)(2,1)S(1)}, u32[]{:S(2)}, u32[]{:S(2)}) collective-permute-start(bf16[96,2048]{1,0:T(8,128)(2,1)S(1)} %get-tuple-element.63), channel_id=1, source_target_pairs={{0,8},{4,12},{8,16},{12,20},{16,24},{20,28},{24,0},{28,4},{1,9},{5... | collective-permute-start | bytes 1179656 | tf_op jit(solution)/shard_map/ppermute | solution.py:541
  35.2 1.4 %shard_map.216 = (bf16[160,2048]{1,0:T(8,128)(2,1)S(1)}, bf16[32,2048]{1,0:T(8,128)(2,1)S(1)}, bf16[32,2048]{1,0:T(8,128)(2,1)S(1)}) custom-call(s32[8]{0:T(128)S(1)} %copy-done.10, bf16[128,2048]{1,0:T(8,128)(2,1)S(1)} %collective-permute-done.3.received, bf16[16,2048]{1,0:T(8,128)(2,1)S(1)} %collective-permute-done.4.far, ...), custom_call_target="tpu_custom_call" | custom-call | flops 2000000000 | tf_op jit(solution)/shard_map/pallas_call | solution.py:508
  36.6 2.5 %collective-permute-start.8 = (bf16[32,2048]{1,0:T(8,128)(2,1)S(1)}, bf16[32,2048]{1,0:T(8,128)(2,1)S(1)}, u32[]{:S(2)}, u32[]{:S(2)}) collective-permute-start(bf16[32,2048]{1,0:T(8,128)(2,1)S(1)} %get-tuple-element.59.mine0), channel_id=1, source_target_pairs={{0,1},{1,0},{2,3},{3,2},{4,5},{5,4},{6,7},{7,6},{8,9},{9,8},{10,11... | collective-permute-start | bytes 393224 | tf_op jit(solution)/shard_map/ppermute | solution.py:629
  39.1 2.0 %shard_map.220 = bf16[128,2048]{1,0:T(8,128)(2,1)S(1)} custom-call(s32[8]{0:T(128)S(1)} %copy-done.10, bf16[2,128,2048]{2,1,0:T(8,128)(2,1)S(1)} %bitcast.19, bf16[128,2048]{1,0:T(8,128)(2,1)S(1)} %collective-permute-done.3.received, bf16[2,32,2048]{2,1,0:T(8,128)(2,1)S(1)} %get-tuple-element.41.refs_5_.refs_2_.weights, ...), custom_call_target="tpu_custom_call" | custom-call | flops 6000000000 | tf_op jit(solution)/shard_map/pallas_call | solution.py:508
  41.1 4.8 %collective-permute-start.14 = (bf16[128,2048]{1,0:T(8,128)(2,1)S(1)}, bf16[128,2048]{1,0:T(8,128)(2,1)S(1)}, u32[]{:S(2)}, u32[]{:S(2)}) collective-permute-start(bf16[128,2048]{1,0:T(8,128)(2,1)S(1)} %shard_map.220), channel_id=1, source_target_pairs={{0,28},{4,0},{8,4},{12,8},{16,12},{20,16},{24,20},{28,24},{1,29},{... | collective-permute-start | bytes 1572872 | tf_op jit(solution)/shard_map/ppermute | solution.py:541
  45.9 0.1 shard_map.217
  45.9 0.4 collective-permute-start.11
  46.4 1.7 %collective-permute-start.10 = (bf16[32,2048]{1,0:T(8,128)(2,1)S(1)}, bf16[32,2048]{1,0:T(8,128)(2,1)S(1)}, u32[]{:S(2)}, u32[]{:S(2)}) collective-permute-start(bf16[32,2048]{1,0:T(8,128)(2,1)S(1)} %get-tuple-element.61.refs_6_.mine0), channel_id=1, source_target_pairs={{0,2},{1,3},{2,0},{3,1},{4,6},{5,7},{6,4},{7,5},{8,10},{9,11},{10,... | collective-permute-start | bytes 393224 | tf_op jit(solution)/shard_map/ppermute | solution.py:629
  48.1 2.7 %shard_map.218.between = bf16[160,2048]{1,0:T(8,128)(2,1)S(1)} custom-call(s32[8]{0:T(128)S(1)} %copy-done.10, bf16[128,2048]{1,0:T(8,128)(2,1)} %collective-permute-done.2.refs_14_.refs_1_, bf16[96,2048]{1,0:T(8,128)(2,1)S(1)} %collective-permute-done.12.refs_2_, bf16[384,192]{1,0:T(8,128)(2,1)S(1)} %copy-done.5, bf16[192,64]{1,0:T(8,128)(2,1)S(1)} %copy-done.16, ...), custom_call_target="tpu_custom_call" | custom-call | flops 10000000000 | tf_op jit(solution)/shard_map/pallas_call | solution.py:508
  50.9 1.9 %shard_map.219.act = bf16[128,2048]{1,0:T(8,128)(2,1)S(1)} custom-call(s32[8]{0:T(128)S(1)} %copy-done.10, bf16[160,2048]{1,0:T(8,128)(2,1)S(1)} %shard_map.218.between, bf16[32,2048]{1,0:T(8,128)(2,1)S(1)} %collective-permute-done.13.layer, bf16[320,160]{1,0:T(8,128)(2,1)S(1)} %copy-done.12, bf16[160,64]{1,0:T(8,128)(2,1)S(1)} %copy-done.17, ...), custom_call_target="tpu_custom_call" | custom-call | flops 10000000000 | tf_op jit(solution)/shard_map/pallas_call | solution.py:508
  52.8 1.7 %shard_map.221 = (bf16[128,2048]{1,0:T(8,128)(2,1)}, bf16[128,2048]{1,0:T(8,128)(2,1)}, f32[31,2,2048]{2,1,0:T(2,128)}, f32[2,2048]{1,0:T(2,128)}) custom-call(s32[8]{0:T(128)S(1)} %copy-done.10, bf16[32,2048]{1,0:T(8,128)(2,1)S(1)} %get-tuple-element.61.refs_6_.mine0, bf16[32,2048]{1,0:T(8,128)(2,1)S(1)} %get-tuple-element.62.mine1, ...), custom_call_target="tpu_custom_call" | custom-call | tf_op jit(solution)/shard_map/pallas_call | solution.py:508
  (46 shorter events, 0.1 us)
Async XLA Ops:
  0.6 9.9 %copy-start.8 = (bf16[1,2,2048]{2,1,0:T(2,128)(2,1)S(1)}, bf16[1,2,2048]{2,1,0:T(2,128)(2,1)}, u32[]{:S(2)}) copy-start(bf16[1,2,2048]{2,1,0:T(2,128)(2,1)} %param.23) | copy-start | bytes 24580
  0.6 9.9 %copy-start.4 = (bf16[1,2,31,2048]{3,1,2,0:T(2,128)(2,1)S(1)}, bf16[1,2,31,2048]{3,1,2,0:T(2,128)(2,1)}, u32[]{:S(2)}) copy-start(bf16[1,2,31,2048]{3,1,2,0:T(2,128)(2,1)} %param.22) | copy-start | bytes 761860
  0.7 18.6 %collective-permute-start.2 = (bf16[128,2048]{1,0:T(8,128)(2,1)}, bf16[128,2048]{1,0:T(8,128)(2,1)}, u32[]{:S(2)}, u32[]{:S(2)}) collective-permute-start(bf16[128,2048]{1,0:T(8,128)(2,1)} %bitcast.21), channel_id=1, source_target_pairs={{0,8},{4,12},{8,16},{12,20},{16,24},{20,28},{24,0},{28,4},{1,9},{5... | collective-permute-start | bytes 1572872 | tf_op jit(solution)/shard_map/ppermute | solution.py:541
  3.7 15.5 %copy-start.5 = (bf16[384,192]{1,0:T(8,128)(2,1)S(1)}, bf16[384,192]{1,0:T(8,128)(2,1)}, u32[]{:S(2)}) copy-start(bf16[384,192]{1,0:T(8,128)(2,1)} %constant.20.clone.refs_9_.m_table.refs_3_) | copy-start | bytes 442372
  5.6 13.7 %copy-start.10 = (s32[8]{0:T(128)S(1)}, s32[8]{0:T(128)}, u32[]{:S(2)}) copy-start(s32[8]{0:T(128)} %get-tuple-element.38.notes.refs_0_) | copy-start | bytes 100
  5.6 10.4 %collective-permute-start = (bf16[48,2048]{1,0:T(8,128)(2,1)}, bf16[48,2048]{1,0:T(8,128)(2,1)S(1)}, u32[]{:S(2)}, u32[]{:S(2)}) collective-permute-start(bf16[48,2048]{1,0:T(8,128)(2,1)} %get-tuple-element.39), channel_id=1, source_target_pairs={{1,2},{2,1},{5,6},{6,5},{9,10},{10,9},{13,14},{14,13},{17,18},{18,... | collective-permute-start | bytes 589832 | tf_op jit(solution)/shard_map/ppermute | solution.py:553
  6.3 13.0 %collective-permute-start.1 = (bf16[48,2048]{1,0:T(8,128)(2,1)}, bf16[48,2048]{1,0:T(8,128)(2,1)S(1)}, u32[]{:S(2)}, u32[]{:S(2)}) collective-permute-start(bf16[48,2048]{1,0:T(8,128)(2,1)} %get-tuple-element.40), channel_id=1, source_target_pairs={{0,1},{1,0},{2,3},{3,2},{4,5},{5,4},{6,7},{7,6},{8,9},{9,8},{10,11... | collective-permute-start | bytes 589832 | tf_op jit(solution)/shard_map/ppermute | solution.py:553
  10.6 1.2 %copy-start = (bf16[1,2,128,2048]{3,2,1,0:T(8,128)(2,1)S(1)}, bf16[1,2,128,2048]{3,2,1,0:T(8,128)(2,1)}, u32[]{:S(2)}) copy-start(bf16[1,2,128,2048]{3,2,1,0:T(8,128)(2,1)} %param.21) | copy-start | bytes 3145732
  11.8 1.0 %copy-start.3 = (bf16[1,128,2048]{2,1,0:T(8,128)(2,1)S(1)}, bf16[1,128,2048]{2,1,0:T(8,128)(2,1)}, u32[]{:S(2)}) copy-start(bf16[1,128,2048]{2,1,0:T(8,128)(2,1)} %param.19) | copy-start | bytes 1572868
  13.5 5.8 %copy-start.2 = (bf16[1,128,2048]{2,1,0:T(8,128)(2,1)S(1)}, bf16[1,128,2048]{2,1,0:T(8,128)(2,1)}, u32[]{:S(2)}) copy-start(bf16[1,128,2048]{2,1,0:T(8,128)(2,1)} %grad.1) | copy-start | bytes 1572868
  13.5 5.8 %copy-start.11 = (bf16[384,160]{1,0:T(8,128)(2,1)S(1)}, bf16[384,160]{1,0:T(8,128)(2,1)}, u32[]{:S(2)}) copy-start(bf16[384,160]{1,0:T(8,128)(2,1)} %constant.23.clone.refs_12_.g_table) | copy-start | bytes 368644
  13.5 5.8 %copy-start.13 = (bf16[320,192]{1,0:T(8,128)(2,1)S(1)}, bf16[320,192]{1,0:T(8,128)(2,1)}, u32[]{:S(2)}) copy-start(bf16[320,192]{1,0:T(8,128)(2,1)} %constant.22.clone.refs_11_.c_table.refs_5_) | copy-start | bytes 368644
  13.5 5.8 %copy-start.15 = (bf16[256,192]{1,0:T(8,128)(2,1)S(1)}, bf16[256,192]{1,0:T(8,128)(2,1)}, u32[]{:S(2)}) copy-start(bf16[256,192]{1,0:T(8,128)(2,1)} %constant.24.clone.refs_13_.x_table) | copy-start | bytes 294916
  13.5 5.8 %copy-start.16 = (bf16[192,64]{1,0:T(8,128)(2,1)S(1)}, bf16[192,64]{1,0:T(8,128)(2,1)}, u32[]{:S(2)}) copy-start(bf16[192,64]{1,0:T(8,128)(2,1)} %constant.21.clone.refs_10_.refs_3_.refs_4_) | copy-start | bytes 73732
  15.2 35.6 %collective-permute-start.13 = (bf16[32,2048]{1,0:T(8,128)(2,1)S(1)}, bf16[32,2048]{1,0:T(8,128)(2,1)S(1)}, u32[]{:S(2)}, u32[]{:S(2)}) collective-permute-start(bf16[32,2048]{1,0:T(8,128)(2,1)S(1)} %get-tuple-element.64), channel_id=1, source_target_pairs={{0,4},{4,8},{8,12},{12,16},{16,20},{20,24},{24,28},{28,0},{1,5},{5... | collective-permute-start | bytes 393224 | tf_op jit(solution)/shard_map/ppermute | solution.py:541
  15.3 13.0 %collective-permute-start.6 = (bf16[64,2048]{1,0:T(8,128)(2,1)S(1)}, bf16[64,2048]{1,0:T(8,128)(2,1)S(1)}, u32[]{:S(2)}, u32[]{:S(2)}) collective-permute-start(bf16[64,2048]{1,0:T(8,128)(2,1)S(1)} %get-tuple-element.48), channel_id=1, source_target_pairs={{1,2},{2,1},{5,6},{6,5},{9,10},{10,9},{13,14},{14,13},{17,18},{18,... | collective-permute-start | bytes 786440 | tf_op jit(solution)/shard_map/ppermute | solution.py:553
  16.0 15.5 %collective-permute-start.7 = (bf16[64,2048]{1,0:T(8,128)(2,1)S(1)}, bf16[64,2048]{1,0:T(8,128)(2,1)S(1)}, u32[]{:S(2)}, u32[]{:S(2)}) collective-permute-start(bf16[64,2048]{1,0:T(8,128)(2,1)S(1)} %get-tuple-element.49), channel_id=1, source_target_pairs={{0,1},{1,0},{2,3},{3,2},{4,5},{5,4},{6,7},{7,6},{8,9},{9,8},{10,11... | collective-permute-start | bytes 786440 | tf_op jit(solution)/shard_map/ppermute | solution.py:553
  19.3 6.9 %copy-start.6 = (bf16[192,256]{1,0:T(8,128)(2,1)S(1)}, bf16[192,256]{1,0:T(8,128)(2,1)}, u32[]{:S(2)}) copy-start(bf16[192,256]{1,0:T(8,128)(2,1)} %constant.25.clone.go_table) | copy-start | bytes 294916
  19.3 6.9 %copy-start.7 = (bf16[64,192]{1,0:T(8,128)(2,1)S(1)}, bf16[64,192]{1,0:T(8,128)(2,1)}, u32[]{:S(2)}) copy-start(bf16[64,192]{1,0:T(8,128)(2,1)} %constant.26.clone.t_table) | copy-start | bytes 73732
  22.8 4.4 %copy-start.1 = (bf16[1,2,128,2048]{3,2,1,0:T(8,128)(2,1)S(1)}, bf16[1,2,128,2048]{3,2,1,0:T(8,128)(2,1)}, u32[]{:S(2)}) copy-start(bf16[1,2,128,2048]{3,2,1,0:T(8,128)(2,1)} %param.21) | copy-start | bytes 3145732
  22.9 12.3 %collective-permute-start.4 = (bf16[16,2048]{1,0:T(8,128)(2,1)S(1)}, bf16[16,2048]{1,0:T(8,128)(2,1)S(1)}, u32[]{:S(2)}, u32[]{:S(2)}) collective-permute-start(bf16[16,2048]{1,0:T(8,128)(2,1)S(1)} %get-tuple-element.46), channel_id=1, source_target_pairs={{1,30},{2,29},{5,2},{6,1},{9,6},{10,5},{13,10},{14,9},{17,14},{18,... | collective-permute-start | bytes 196616 | tf_op jit(solution)/shard_map/ppermute | solution.py:553
  23.7 11.6 %collective-permute-start.3 = (bf16[128,2048]{1,0:T(8,128)(2,1)S(1)}, bf16[128,2048]{1,0:T(8,128)(2,1)S(1)}, u32[]{:S(2)}, u32[]{:S(2)}) collective-permute-start(bf16[128,2048]{1,0:T(8,128)(2,1)S(1)} %get-tuple-element.45), channel_id=1, source_target_pairs={{0,28},{4,0},{8,4},{12,8},{16,12},{20,16},{24,20},{28,24},{1,29},{... | collective-permute-start | bytes 1572872 | tf_op jit(solution)/shard_map/ppermute | solution.py:541
  28.3 6.9 %collective-permute-start.5 = (bf16[16,2048]{1,0:T(8,128)(2,1)S(1)}, bf16[16,2048]{1,0:T(8,128)(2,1)S(1)}, u32[]{:S(2)}, u32[]{:S(2)}) collective-permute-start(bf16[16,2048]{1,0:T(8,128)(2,1)S(1)} %get-tuple-element.47), channel_id=1, source_target_pairs={{0,29},{1,28},{2,31},{3,30},{4,1},{5,0},{6,3},{7,2},{8,5},{9,4},{1... | collective-permute-start | bytes 196616 | tf_op jit(solution)/shard_map/ppermute | solution.py:553
  33.6 14.6 %collective-permute-start.12 = (bf16[96,2048]{1,0:T(8,128)(2,1)S(1)}, bf16[96,2048]{1,0:T(8,128)(2,1)S(1)}, u32[]{:S(2)}, u32[]{:S(2)}) collective-permute-start(bf16[96,2048]{1,0:T(8,128)(2,1)S(1)} %get-tuple-element.63), channel_id=1, source_target_pairs={{0,8},{4,12},{8,16},{12,20},{16,24},{20,28},{24,0},{28,4},{1,9},{5... | collective-permute-start | bytes 1179656 | tf_op jit(solution)/shard_map/ppermute | solution.py:541
  36.6 9.3 %collective-permute-start.8 = (bf16[32,2048]{1,0:T(8,128)(2,1)S(1)}, bf16[32,2048]{1,0:T(8,128)(2,1)S(1)}, u32[]{:S(2)}, u32[]{:S(2)}) collective-permute-start(bf16[32,2048]{1,0:T(8,128)(2,1)S(1)} %get-tuple-element.59.mine0), channel_id=1, source_target_pairs={{0,1},{1,0},{2,3},{3,2},{4,5},{5,4},{6,7},{7,6},{8,9},{9,8},{10,11... | collective-permute-start | bytes 393224 | tf_op jit(solution)/shard_map/ppermute | solution.py:629
  39.1 6.7 %collective-permute-start.9 = (bf16[32,2048]{1,0:T(8,128)(2,1)S(1)}, bf16[32,2048]{1,0:T(8,128)(2,1)S(1)}, u32[]{:S(2)}, u32[]{:S(2)}) collective-permute-start(bf16[32,2048]{1,0:T(8,128)(2,1)S(1)} %get-tuple-element.60.mine1), channel_id=1, source_target_pairs={{0,2},{1,3},{2,0},{3,1},{4,6},{5,7},{6,4},{7,5},{8,10},{9,11},{10,... | collective-permute-start | bytes 393224 | tf_op jit(solution)/shard_map/ppermute | solution.py:629
  41.1 11.7 %collective-permute-start.14 = (bf16[128,2048]{1,0:T(8,128)(2,1)S(1)}, bf16[128,2048]{1,0:T(8,128)(2,1)S(1)}, u32[]{:S(2)}, u32[]{:S(2)}) collective-permute-start(bf16[128,2048]{1,0:T(8,128)(2,1)S(1)} %shard_map.220), channel_id=1, source_target_pairs={{0,28},{4,0},{8,4},{12,8},{16,12},{20,16},{24,20},{28,24},{1,29},{... | collective-permute-start | bytes 1572872 | tf_op jit(solution)/shard_map/ppermute | solution.py:541
  45.9 6.8 %collective-permute-start.11 = (bf16[32,2048]{1,0:T(8,128)(2,1)S(1)}, bf16[32,2048]{1,0:T(8,128)(2,1)S(1)}, u32[]{:S(2)}, u32[]{:S(2)}) collective-permute-start(bf16[32,2048]{1,0:T(8,128)(2,1)S(1)} %get-tuple-element.62.mine1), channel_id=1, source_target_pairs={{0,1},{1,0},{2,3},{3,2},{4,5},{5,4},{6,7},{7,6},{8,9},{9,8},{10,11... | collective-permute-start | bytes 393224 | tf_op jit(solution)/shard_map/ppermute | solution.py:629
  46.4 4.5 %copy-start.12 = (bf16[320,160]{1,0:T(8,128)(2,1)S(1)}, bf16[320,160]{1,0:T(8,128)(2,1)}, u32[]{:S(2)}) copy-start(bf16[320,160]{1,0:T(8,128)(2,1)} %constant.27.clone.m_table) | copy-start | bytes 307204
  46.4 4.5 %copy-start.14 = (bf16[256,160]{1,0:T(8,128)(2,1)S(1)}, bf16[256,160]{1,0:T(8,128)(2,1)}, u32[]{:S(2)}) copy-start(bf16[256,160]{1,0:T(8,128)(2,1)} %constant.29.clone.c_table) | copy-start | bytes 245764
  46.4 4.5 %copy-start.17 = (bf16[160,64]{1,0:T(8,128)(2,1)S(1)}, bf16[160,64]{1,0:T(8,128)(2,1)}, u32[]{:S(2)}) copy-start(bf16[160,64]{1,0:T(8,128)(2,1)} %constant.28.clone.q_table) | copy-start | bytes 61444
  46.4 6.4 %collective-permute-start.10 = (bf16[32,2048]{1,0:T(8,128)(2,1)S(1)}, bf16[32,2048]{1,0:T(8,128)(2,1)S(1)}, u32[]{:S(2)}, u32[]{:S(2)}) collective-permute-start(bf16[32,2048]{1,0:T(8,128)(2,1)S(1)} %get-tuple-element.61.refs_6_.mine0), channel_id=1, source_target_pairs={{0,2},{1,3},{2,0},{3,1},{4,6},{5,7},{6,4},{7,5},{8,10},{9,11},{10,... | collective-permute-start | bytes 393224 | tf_op jit(solution)/shard_map/ppermute | solution.py:629
  (1 other events, 0.7 us)

commit v20 on v19

--- a/solution.py
+++ b/solution.py
@@ -171,7 +171,7 @@
 
 def first_pass(pieces, mean, inverse, gain, mask, tables, mixed, q, columns, scaled, sum_a, sum_b):
     g_table, x_table = tables
-    grad_masked = wide(mask, BLOCK) * transform(x_table, product_conj(transform(g_table, mixed), q))
+    grad_masked = wide(mask, BLOCK) * rounded_transform(x_table, product_conj(transform(g_table, mixed), q))
     centered = window(pieces, columns).astype(F32) - wide(mean[...], BLOCK)
     weighted = grad_masked * (centered * wide(inverse[...], BLOCK))
     gain = gain(columns)

time: 55 us -> 55 us (level)
  no operation moved by 1% of the time
where the time goes in v20:
time: 55 us; the launch traced here: 54.6 us
  starting transfers between devices  28.5 us (52%)
  Pallas kernels  20.9 us (38%)
  local copies, waits for them, and re-layouts  2.99 us (5%)
  waiting for transfers between devices  1.16 us (2%)
  between operations  1.1 us (2%)
    pallas_call x12, Pallas kernels, call(): pl.pallas_call(kernel, out_shape=outs, in_specs=specs, out_specs=jax.tree...  20.9 us
    ppermute x5, starting transfers between devices, shifted(): lax.ppermute(x, 'section', [(i, (i + by) % sections) for i in range(secti...  12 us
    ppermute x6, starting transfers between devices, swapped(): results.append(lax.ppermute(x, ('section', 'tm'), pairs))  11.7 us
    ppermute x4, starting transfers between devices, partner(): return lax.ppermute(x, 'tm', [(i, i ^ step) for i in range(shards)])  4.7 us
    unnamed x36, local copies, waits for them, and re-layouts  2.99 us
    ppermute x6, waiting for transfers between devices, swapped(): results.append(lax.ppermute(x, ('section', 'tm'), pairs))  1.13 us
  transfers between devices with their start and end apart: 15, of which 2 were waited for; matrix products, arithmetic and copies ran while one was open for 0% of the time, Pallas kernels for 35%

profile of v20, /device:TPU:0, one launch (start us, length us, event | category | flops | bytes accessed | tf_op | source)
XLA Modules:
  0.0 54.6 jit_solution(7468886158534831478)
XLA Ops:
  0.7 3.1 %collective-permute-start.2 = (bf16[128,2048]{1,0:T(8,128)(2,1)}, bf16[128,2048]{1,0:T(8,128)(2,1)}, u32[]{:S(2)}, u32[]{:S(2)}) collective-permute-start(bf16[128,2048]{1,0:T(8,128)(2,1)} %bitcast.21), channel_id=1, source_target_pairs={{0,8},{4,12},{8,16},{12,20},{16,24},{20,28},{24,0},{28,4},{1,9},{5... | collective-permute-start | bytes 1572872 | tf_op jit(solution)/shard_map/ppermute | solution.py:541
  3.7 1.9 %shard_map.210 = (bf16[48,2048]{1,0:T(8,128)(2,1)}, bf16[48,2048]{1,0:T(8,128)(2,1)}, s32[8]{0:T(128)}) custom-call(bf16[2,128,2048]{2,1,0:T(8,128)(2,1)} %bitcast.15, bf16[1,128,2048]{2,1,0:T(8,128)(2,1)} %grad.1, s32[8]{0:T(128)} %back_lengths.1, s32[8]{0:T(128)} %ahead_lengths.1, s32[2,8]{1,0:T(2,128)} %bitcast.25, s32[2,8]{1,0:T(2,128)} %bitcast.26), custom_call_target="tpu_custom_call" | custom-call | tf_op jit(solution)/shard_map/pallas_call | solution.py:508
  5.6 0.7 %collective-permute-start = (bf16[48,2048]{1,0:T(8,128)(2,1)}, bf16[48,2048]{1,0:T(8,128)(2,1)S(1)}, u32[]{:S(2)}, u32[]{:S(2)}) collective-permute-start(bf16[48,2048]{1,0:T(8,128)(2,1)} %get-tuple-element.39), channel_id=1, source_target_pairs={{1,2},{2,1},{5,6},{6,5},{9,10},{10,9},{13,14},{14,13},{17,18},{18,... | collective-permute-start | bytes 589832 | tf_op jit(solution)/shard_map/ppermute | solution.py:553
  6.3 4.3 %collective-permute-start.1 = (bf16[48,2048]{1,0:T(8,128)(2,1)}, bf16[48,2048]{1,0:T(8,128)(2,1)S(1)}, u32[]{:S(2)}, u32[]{:S(2)}) collective-permute-start(bf16[48,2048]{1,0:T(8,128)(2,1)} %get-tuple-element.40), channel_id=1, source_target_pairs={{0,1},{1,0},{2,3},{3,2},{4,5},{5,4},{6,7},{7,6},{8,9},{9,8},{10,11... | collective-permute-start | bytes 589832 | tf_op jit(solution)/shard_map/ppermute | solution.py:553
  10.6 1.2 %copy-done = bf16[1,2,128,2048]{3,2,1,0:T(8,128)(2,1)S(1)} copy-done((bf16[1,2,128,2048]{3,2,1,0:T(8,128)(2,1)S(1)}, bf16[1,2,128,2048]{3,2,1,0:T(8,128)(2,1)}, u32[]{:S(2)}) %copy-start) | copy-done | bytes 1048600
  11.8 1.0 %copy-done.3 = bf16[1,128,2048]{2,1,0:T(8,128)(2,1)S(1)} copy-done((bf16[1,128,2048]{2,1,0:T(8,128)(2,1)S(1)}, bf16[1,128,2048]{2,1,0:T(8,128)(2,1)}, u32[]{:S(2)}) %copy-start.3) | copy-done | bytes 524312
  12.8 0.7 %copy-done.9 = s32[8]{0:T(128)S(1)} copy-done((s32[8]{0:T(128)S(1)}, s32[8]{0:T(128)}, u32[]{:S(2)}) %copy-start.9) | copy-done | bytes 56
  13.5 0.0 copy-start.16
  13.5 1.7 %shard_map.211 = (bf16[2,32,2048]{2,1,0:T(8,128)(2,1)S(1)}, bf16[32,2048]{1,0:T(8,128)(2,1)S(1)}, bf16[32,2048]{1,0:T(8,128)(2,1)S(1)}, bf16[64,2048]{1,0:T(8,12...) custom-call(s32[8]{0:T(128)S(1)} %copy-done.9, ...), custom_call_target="tpu_custom_call" | custom-call | tf_op jit(solution)/shard_map/pallas_call | solution.py:508
  15.2 0.1 collective-permute-start.13
  15.3 0.7 %collective-permute-start.6 = (bf16[64,2048]{1,0:T(8,128)(2,1)S(1)}, bf16[64,2048]{1,0:T(8,128)(2,1)S(1)}, u32[]{:S(2)}, u32[]{:S(2)}) collective-permute-start(bf16[64,2048]{1,0:T(8,128)(2,1)S(1)} %get-tuple-element.48), channel_id=1, source_target_pairs={{1,2},{2,1},{5,6},{6,5},{9,10},{10,9},{13,14},{14,13},{17,18},{18,... | collective-permute-start | bytes 786440 | tf_op jit(solution)/shard_map/ppermute | solution.py:553
  16.0 2.8 %collective-permute-start.7 = (bf16[64,2048]{1,0:T(8,128)(2,1)S(1)}, bf16[64,2048]{1,0:T(8,128)(2,1)S(1)}, u32[]{:S(2)}, u32[]{:S(2)}) collective-permute-start(bf16[64,2048]{1,0:T(8,128)(2,1)S(1)} %get-tuple-element.49), channel_id=1, source_target_pairs={{0,1},{1,0},{2,3},{3,2},{4,5},{5,4},{6,7},{7,6},{8,9},{9,8},{10,11... | collective-permute-start | bytes 786440 | tf_op jit(solution)/shard_map/ppermute | solution.py:553
  18.8 0.5 collective-permute-done.1.refs_3_
  19.3 3.5 %shard_map.212 = (bf16[128,2048]{1,0:T(8,128)(2,1)S(1)}, bf16[16,2048]{1,0:T(8,128)(2,1)S(1)}, bf16[16,2048]{1,0:T(8,128)(2,1)S(1)}, bf16[64,2048]{1,0:T(8,128)(...) custom-call(s32[8]{0:T(128)S(1)} %copy-done.10, bf16[2,128,2048]{2,1,0:T(8,128)(2,1)S(1)} %bitcast.17, ...), custom_call_target="tpu_custom_call" | custom-call | flops 4000000000 | tf_op jit(solution)/shard_map/pallas_call | solution.py:508
  22.9 0.8 %collective-permute-start.4 = (bf16[16,2048]{1,0:T(8,128)(2,1)S(1)}, bf16[16,2048]{1,0:T(8,128)(2,1)S(1)}, u32[]{:S(2)}, u32[]{:S(2)}) collective-permute-start(bf16[16,2048]{1,0:T(8,128)(2,1)S(1)} %get-tuple-element.46), channel_id=1, source_target_pairs={{1,30},{2,29},{5,2},{6,1},{9,6},{10,5},{13,10},{14,9},{17,14},{18,... | collective-permute-start | bytes 196616 | tf_op jit(solution)/shard_map/ppermute | solution.py:553
  23.7 2.5 %collective-permute-start.3 = (bf16[128,2048]{1,0:T(8,128)(2,1)S(1)}, bf16[128,2048]{1,0:T(8,128)(2,1)S(1)}, u32[]{:S(2)}, u32[]{:S(2)}) collective-permute-start(bf16[128,2048]{1,0:T(8,128)(2,1)S(1)} %get-tuple-element.45), channel_id=1, source_target_pairs={{0,28},{4,0},{8,4},{12,8},{16,12},{20,16},{24,20},{28,24},{1,29},{... | collective-permute-start | bytes 1572872 | tf_op jit(solution)/shard_map/ppermute | solution.py:541
  26.2 1.0 %shard_map.213.refs_4_.taps0 = bf16[32,2048]{1,0:T(8,128)(2,1)S(1)} custom-call(bf16[64,2048]{1,0:T(8,128)(2,1)S(1)} %get-tuple-element.51.halo, bf16[128,2048]{1,0:T(8,128)(2,1)S(1)} %get-tuple-element.42.refs_6_.masked, bf16[128,2048]{1,0:T(8,128)(2,1)S(1)} %get-tuple-element.52.inner, f32[1,2048]{1,0:T(1,128)S(1)} %get-tuple-element.53.gain_sum, ...), custom_call_target="tpu_custom_call" | custom-call | tf_op jit(solution)/shard_map/pallas_call | solution.py:508
  27.2 1.1 %shard_map.214 = (bf16[128,2048]{1,0:T(8,128)(2,1)S(1)}, f32[128,128]{1,0:T(8,128)S(1)}, f32[128,128]{1,0:T(8,128)S(1)}, f32[192,2048]{1,0:T(8,128)S(1)}) custom-call(s32[8]{0:T(128)S(1)} %copy-done.10, bf16[2,128,2048]{2,1,0:T(8,128)(2,1)S(1)} %bitcast.18, bf16[2,32,2048]{2,1,0:T(8,128)(2,1)S(1)} %get-tuple-element.41.refs_5_.refs_2_.weights, ...), custom_call_target="tpu_custom_call" | custom-call | flops 1000000000 | tf_op jit(solution)/shard_map/pallas_call | solution.py:508
  28.3 2.5 %collective-permute-start.5 = (bf16[16,2048]{1,0:T(8,128)(2,1)S(1)}, bf16[16,2048]{1,0:T(8,128)(2,1)S(1)}, u32[]{:S(2)}, u32[]{:S(2)}) collective-permute-start(bf16[16,2048]{1,0:T(8,128)(2,1)S(1)} %get-tuple-element.47), channel_id=1, source_target_pairs={{0,29},{1,28},{2,31},{3,30},{4,1},{5,0},{6,3},{7,2},{8,5},{9,4},{1... | collective-permute-start | bytes 196616 | tf_op jit(solution)/shard_map/ppermute | solution.py:553
  30.8 0.6 %collective-permute-done.7.near = bf16[64,2048]{1,0:T(8,128)(2,1)S(1)} collective-permute-done((bf16[64,2048]{1,0:T(8,128)(2,1)S(1)}, bf16[64,2048]{1,0:T(8,128)(2,1)S(1)}, u32[]{:S(2)}, u32[]{:S(2)}) %collective-permute-start.7) | collective-permute-done | bytes 262176 | tf_op jit(solution)/shard_map/ppermute | solution.py:553
  31.5 2.1 %shard_map.215 = (f32[192,2048]{1,0:T(8,128)S(1)}, f32[160,2048]{1,0:T(8,128)S(1)}, f32[128,2048]{1,0:T(8,128)S(1)}, bf16[96,2048]{1,0:T(8,128)(2,1)S(1)}) custom-call(s32[8]{0:T(128)S(1)} %copy-done.10, bf16[64,2048]{1,0:T(8,128)(2,1)S(1)} %collective-permute-done.6.far, bf16[64,2048]{1,0:T(8,128)(2,1)S(1)} %collective-permute-done.7.near, ...), custom_call_target="tpu_custom_call" | custom-call | flops 5000000000 | tf_op jit(solution)/shard_map/pallas_call | solution.py:508
  33.6 1.6 %collective-permute-start.12 = (bf16[96,2048]{1,0:T(8,128)(2,1)S(1)}, bf16[96,2048]{1,0:T(8,128)(2,1)S(1)}, u32[]{:S(2)}, u32[]{:S(2)}) collective-permute-start(bf16[96,2048]{1,0:T(8,128)(2,1)S(1)} %get-tuple-element.63), channel_id=1, source_target_pairs={{0,8},{4,12},{8,16},{12,20},{16,24},{20,28},{24,0},{28,4},{1,9},{5... | collective-permute-start | bytes 1179656 | tf_op jit(solution)/shard_map/ppermute | solution.py:541
  35.2 1.4 %shard_map.216 = (bf16[160,2048]{1,0:T(8,128)(2,1)S(1)}, bf16[32,2048]{1,0:T(8,128)(2,1)S(1)}, bf16[32,2048]{1,0:T(8,128)(2,1)S(1)}) custom-call(s32[8]{0:T(128)S(1)} %copy-done.10, bf16[128,2048]{1,0:T(8,128)(2,1)S(1)} %collective-permute-done.3.received, bf16[16,2048]{1,0:T(8,128)(2,1)S(1)} %collective-permute-done.4.far, ...), custom_call_target="tpu_custom_call" | custom-call | flops 2000000000 | tf_op jit(solution)/shard_map/pallas_call | solution.py:508
  36.6 2.5 %collective-permute-start.8 = (bf16[32,2048]{1,0:T(8,128)(2,1)S(1)}, bf16[32,2048]{1,0:T(8,128)(2,1)S(1)}, u32[]{:S(2)}, u32[]{:S(2)}) collective-permute-start(bf16[32,2048]{1,0:T(8,128)(2,1)S(1)} %get-tuple-element.59.mine0), channel_id=1, source_target_pairs={{0,1},{1,0},{2,3},{3,2},{4,5},{5,4},{6,7},{7,6},{8,9},{9,8},{10,11... | collective-permute-start | bytes 393224 | tf_op jit(solution)/shard_map/ppermute | solution.py:629
  39.1 1.9 %shard_map.220 = bf16[128,2048]{1,0:T(8,128)(2,1)S(1)} custom-call(s32[8]{0:T(128)S(1)} %copy-done.10, bf16[2,128,2048]{2,1,0:T(8,128)(2,1)S(1)} %bitcast.19, bf16[128,2048]{1,0:T(8,128)(2,1)S(1)} %collective-permute-done.3.received, bf16[2,32,2048]{2,1,0:T(8,128)(2,1)S(1)} %get-tuple-element.41.refs_5_.refs_2_.weights, ...), custom_call_target="tpu_custom_call" | custom-call | flops 6000000000 | tf_op jit(solution)/shard_map/pallas_call | solution.py:508
  41.1 4.8 %collective-permute-start.14 = (bf16[128,2048]{1,0:T(8,128)(2,1)S(1)}, bf16[128,2048]{1,0:T(8,128)(2,1)S(1)}, u32[]{:S(2)}, u32[]{:S(2)}) collective-permute-start(bf16[128,2048]{1,0:T(8,128)(2,1)S(1)} %shard_map.220), channel_id=1, source_target_pairs={{0,28},{4,0},{8,4},{12,8},{16,12},{20,16},{24,20},{28,24},{1,29},{... | collective-permute-start | bytes 1572872 | tf_op jit(solution)/shard_map/ppermute | solution.py:541
  45.8 0.1 shard_map.217
  45.9 0.4 collective-permute-start.11
  46.3 1.7 %collective-permute-start.10 = (bf16[32,2048]{1,0:T(8,128)(2,1)S(1)}, bf16[32,2048]{1,0:T(8,128)(2,1)S(1)}, u32[]{:S(2)}, u32[]{:S(2)}) collective-permute-start(bf16[32,2048]{1,0:T(8,128)(2,1)S(1)} %get-tuple-element.61.refs_6_.mine0), channel_id=1, source_target_pairs={{0,2},{1,3},{2,0},{3,1},{4,6},{5,7},{6,4},{7,5},{8,10},{9,11},{10,... | collective-permute-start | bytes 393224 | tf_op jit(solution)/shard_map/ppermute | solution.py:629
  48.1 2.7 %shard_map.218.between = bf16[160,2048]{1,0:T(8,128)(2,1)S(1)} custom-call(s32[8]{0:T(128)S(1)} %copy-done.10, bf16[128,2048]{1,0:T(8,128)(2,1)} %collective-permute-done.2.refs_14_.refs_1_, bf16[96,2048]{1,0:T(8,128)(2,1)S(1)} %collective-permute-done.12.refs_2_, bf16[384,192]{1,0:T(8,128)(2,1)S(1)} %copy-done.5, bf16[192,64]{1,0:T(8,128)(2,1)S(1)} %copy-done.16, ...), custom_call_target="tpu_custom_call" | custom-call | flops 10000000000 | tf_op jit(solution)/shard_map/pallas_call | solution.py:508
  50.8 1.9 %shard_map.219.act = bf16[128,2048]{1,0:T(8,128)(2,1)S(1)} custom-call(s32[8]{0:T(128)S(1)} %copy-done.10, bf16[160,2048]{1,0:T(8,128)(2,1)S(1)} %shard_map.218.between, bf16[32,2048]{1,0:T(8,128)(2,1)S(1)} %collective-permute-done.13.layer, bf16[320,160]{1,0:T(8,128)(2,1)S(1)} %copy-done.12, bf16[160,64]{1,0:T(8,128)(2,1)S(1)} %copy-done.17, ...), custom_call_target="tpu_custom_call" | custom-call | flops 10000000000 | tf_op jit(solution)/shard_map/pallas_call | solution.py:508
  52.8 1.7 %shard_map.221 = (bf16[128,2048]{1,0:T(8,128)(2,1)}, bf16[128,2048]{1,0:T(8,128)(2,1)}, f32[31,2,2048]{2,1,0:T(2,128)}, f32[2,2048]{1,0:T(2,128)}) custom-call(s32[8]{0:T(128)S(1)} %copy-done.10, bf16[32,2048]{1,0:T(8,128)(2,1)S(1)} %get-tuple-element.61.refs_6_.mine0, bf16[32,2048]{1,0:T(8,128)(2,1)S(1)} %get-tuple-element.62.mine1, ...), custom_call_target="tpu_custom_call" | custom-call | tf_op jit(solution)/shard_map/pallas_call | solution.py:508
  (46 shorter events, 0.1 us)
Async XLA Ops:
  0.6 9.9 %copy-start.8 = (bf16[1,2,2048]{2,1,0:T(2,128)(2,1)S(1)}, bf16[1,2,2048]{2,1,0:T(2,128)(2,1)}, u32[]{:S(2)}) copy-start(bf16[1,2,2048]{2,1,0:T(2,128)(2,1)} %param.23) | copy-start | bytes 24580
  0.6 9.9 %copy-start.4 = (bf16[1,2,31,2048]{3,1,2,0:T(2,128)(2,1)S(1)}, bf16[1,2,31,2048]{3,1,2,0:T(2,128)(2,1)}, u32[]{:S(2)}) copy-start(bf16[1,2,31,2048]{3,1,2,0:T(2,128)(2,1)} %param.22) | copy-start | bytes 761860
  0.7 18.6 %collective-permute-start.2 = (bf16[128,2048]{1,0:T(8,128)(2,1)}, bf16[128,2048]{1,0:T(8,128)(2,1)}, u32[]{:S(2)}, u32[]{:S(2)}) collective-permute-start(bf16[128,2048]{1,0:T(8,128)(2,1)} %bitcast.21), channel_id=1, source_target_pairs={{0,8},{4,12},{8,16},{12,20},{16,24},{20,28},{24,0},{28,4},{1,9},{5... | collective-permute-start | bytes 1572872 | tf_op jit(solution)/shard_map/ppermute | solution.py:541
  3.7 15.5 %copy-start.5 = (bf16[384,192]{1,0:T(8,128)(2,1)S(1)}, bf16[384,192]{1,0:T(8,128)(2,1)}, u32[]{:S(2)}) copy-start(bf16[384,192]{1,0:T(8,128)(2,1)} %constant.20.clone.refs_9_.m_table.refs_3_) | copy-start | bytes 442372
  5.6 13.7 %copy-start.10 = (s32[8]{0:T(128)S(1)}, s32[8]{0:T(128)}, u32[]{:S(2)}) copy-start(s32[8]{0:T(128)} %get-tuple-element.38.notes.refs_0_) | copy-start | bytes 100
  5.6 10.4 %collective-permute-start = (bf16[48,2048]{1,0:T(8,128)(2,1)}, bf16[48,2048]{1,0:T(8,128)(2,1)S(1)}, u32[]{:S(2)}, u32[]{:S(2)}) collective-permute-start(bf16[48,2048]{1,0:T(8,128)(2,1)} %get-tuple-element.39), channel_id=1, source_target_pairs={{1,2},{2,1},{5,6},{6,5},{9,10},{10,9},{13,14},{14,13},{17,18},{18,... | collective-permute-start | bytes 589832 | tf_op jit(solution)/shard_map/ppermute | solution.py:553
  6.3 13.0 %collective-permute-start.1 = (bf16[48,2048]{1,0:T(8,128)(2,1)}, bf16[48,2048]{1,0:T(8,128)(2,1)S(1)}, u32[]{:S(2)}, u32[]{:S(2)}) collective-permute-start(bf16[48,2048]{1,0:T(8,128)(2,1)} %get-tuple-element.40), channel_id=1, source_target_pairs={{0,1},{1,0},{2,3},{3,2},{4,5},{5,4},{6,7},{7,6},{8,9},{9,8},{10,11... | collective-permute-start | bytes 589832 | tf_op jit(solution)/shard_map/ppermute | solution.py:553
  10.6 1.2 %copy-start = (bf16[1,2,128,2048]{3,2,1,0:T(8,128)(2,1)S(1)}, bf16[1,2,128,2048]{3,2,1,0:T(8,128)(2,1)}, u32[]{:S(2)}) copy-start(bf16[1,2,128,2048]{3,2,1,0:T(8,128)(2,1)} %param.21) | copy-start | bytes 3145732
  11.8 1.0 %copy-start.3 = (bf16[1,128,2048]{2,1,0:T(8,128)(2,1)S(1)}, bf16[1,128,2048]{2,1,0:T(8,128)(2,1)}, u32[]{:S(2)}) copy-start(bf16[1,128,2048]{2,1,0:T(8,128)(2,1)} %param.19) | copy-start | bytes 1572868
  13.5 5.8 %copy-start.2 = (bf16[1,128,2048]{2,1,0:T(8,128)(2,1)S(1)}, bf16[1,128,2048]{2,1,0:T(8,128)(2,1)}, u32[]{:S(2)}) copy-start(bf16[1,128,2048]{2,1,0:T(8,128)(2,1)} %grad.1) | copy-start | bytes 1572868
  13.5 5.8 %copy-start.11 = (bf16[384,160]{1,0:T(8,128)(2,1)S(1)}, bf16[384,160]{1,0:T(8,128)(2,1)}, u32[]{:S(2)}) copy-start(bf16[384,160]{1,0:T(8,128)(2,1)} %constant.23.clone.refs_12_.g_table) | copy-start | bytes 368644
  13.5 5.8 %copy-start.13 = (bf16[320,192]{1,0:T(8,128)(2,1)S(1)}, bf16[320,192]{1,0:T(8,128)(2,1)}, u32[]{:S(2)}) copy-start(bf16[320,192]{1,0:T(8,128)(2,1)} %constant.22.clone.refs_11_.c_table.refs_5_) | copy-start | bytes 368644
  13.5 5.8 %copy-start.15 = (bf16[256,192]{1,0:T(8,128)(2,1)S(1)}, bf16[256,192]{1,0:T(8,128)(2,1)}, u32[]{:S(2)}) copy-start(bf16[256,192]{1,0:T(8,128)(2,1)} %constant.24.clone.refs_13_.x_table) | copy-start | bytes 294916
  13.5 5.8 %copy-start.16 = (bf16[192,64]{1,0:T(8,128)(2,1)S(1)}, bf16[192,64]{1,0:T(8,128)(2,1)}, u32[]{:S(2)}) copy-start(bf16[192,64]{1,0:T(8,128)(2,1)} %constant.21.clone.refs_10_.refs_3_.refs_4_) | copy-start | bytes 73732
  15.2 35.6 %collective-permute-start.13 = (bf16[32,2048]{1,0:T(8,128)(2,1)S(1)}, bf16[32,2048]{1,0:T(8,128)(2,1)S(1)}, u32[]{:S(2)}, u32[]{:S(2)}) collective-permute-start(bf16[32,2048]{1,0:T(8,128)(2,1)S(1)} %get-tuple-element.64), channel_id=1, source_target_pairs={{0,4},{4,8},{8,12},{12,16},{16,20},{20,24},{24,28},{28,0},{1,5},{5... | collective-permute-start | bytes 393224 | tf_op jit(solution)/shard_map/ppermute | solution.py:541
  15.3 13.0 %collective-permute-start.6 = (bf16[64,2048]{1,0:T(8,128)(2,1)S(1)}, bf16[64,2048]{1,0:T(8,128)(2,1)S(1)}, u32[]{:S(2)}, u32[]{:S(2)}) collective-permute-start(bf16[64,2048]{1,0:T(8,128)(2,1)S(1)} %get-tuple-element.48), channel_id=1, source_target_pairs={{1,2},{2,1},{5,6},{6,5},{9,10},{10,9},{13,14},{14,13},{17,18},{18,... | collective-permute-start | bytes 786440 | tf_op jit(solution)/shard_map/ppermute | solution.py:553
  16.0 15.5 %collective-permute-start.7 = (bf16[64,2048]{1,0:T(8,128)(2,1)S(1)}, bf16[64,2048]{1,0:T(8,128)(2,1)S(1)}, u32[]{:S(2)}, u32[]{:S(2)}) collective-permute-start(bf16[64,2048]{1,0:T(8,128)(2,1)S(1)} %get-tuple-element.49), channel_id=1, source_target_pairs={{0,1},{1,0},{2,3},{3,2},{4,5},{5,4},{6,7},{7,6},{8,9},{9,8},{10,11... | collective-permute-start | bytes 786440 | tf_op jit(solution)/shard_map/ppermute | solution.py:553
  19.3 6.9 %copy-start.6 = (bf16[192,256]{1,0:T(8,128)(2,1)S(1)}, bf16[192,256]{1,0:T(8,128)(2,1)}, u32[]{:S(2)}) copy-start(bf16[192,256]{1,0:T(8,128)(2,1)} %constant.25.clone.go_table) | copy-start | bytes 294916
  19.3 6.9 %copy-start.7 = (bf16[64,192]{1,0:T(8,128)(2,1)S(1)}, bf16[64,192]{1,0:T(8,128)(2,1)}, u32[]{:S(2)}) copy-start(bf16[64,192]{1,0:T(8,128)(2,1)} %constant.26.clone.t_table) | copy-start | bytes 73732
  22.8 4.4 %copy-start.1 = (bf16[1,2,128,2048]{3,2,1,0:T(8,128)(2,1)S(1)}, bf16[1,2,128,2048]{3,2,1,0:T(8,128)(2,1)}, u32[]{:S(2)}) copy-start(bf16[1,2,128,2048]{3,2,1,0:T(8,128)(2,1)} %param.21) | copy-start | bytes 3145732
  22.9 12.3 %collective-permute-start.4 = (bf16[16,2048]{1,0:T(8,128)(2,1)S(1)}, bf16[16,2048]{1,0:T(8,128)(2,1)S(1)}, u32[]{:S(2)}, u32[]{:S(2)}) collective-permute-start(bf16[16,2048]{1,0:T(8,128)(2,1)S(1)} %get-tuple-element.46), channel_id=1, source_target_pairs={{1,30},{2,29},{5,2},{6,1},{9,6},{10,5},{13,10},{14,9},{17,14},{18,... | collective-permute-start | bytes 196616 | tf_op jit(solution)/shard_map/ppermute | solution.py:553
  23.7 11.5 %collective-permute-start.3 = (bf16[128,2048]{1,0:T(8,128)(2,1)S(1)}, bf16[128,2048]{1,0:T(8,128)(2,1)S(1)}, u32[]{:S(2)}, u32[]{:S(2)}) collective-permute-start(bf16[128,2048]{1,0:T(8,128)(2,1)S(1)} %get-tuple-element.45), channel_id=1, source_target_pairs={{0,28},{4,0},{8,4},{12,8},{16,12},{20,16},{24,20},{28,24},{1,29},{... | collective-permute-start | bytes 1572872 | tf_op jit(solution)/shard_map/ppermute | solution.py:541
  28.3 6.9 %collective-permute-start.5 = (bf16[16,2048]{1,0:T(8,128)(2,1)S(1)}, bf16[16,2048]{1,0:T(8,128)(2,1)S(1)}, u32[]{:S(2)}, u32[]{:S(2)}) collective-permute-start(bf16[16,2048]{1,0:T(8,128)(2,1)S(1)} %get-tuple-element.47), channel_id=1, source_target_pairs={{0,29},{1,28},{2,31},{3,30},{4,1},{5,0},{6,3},{7,2},{8,5},{9,4},{1... | collective-permute-start | bytes 196616 | tf_op jit(solution)/shard_map/ppermute | solution.py:553
  33.6 14.5 %collective-permute-start.12 = (bf16[96,2048]{1,0:T(8,128)(2,1)S(1)}, bf16[96,2048]{1,0:T(8,128)(2,1)S(1)}, u32[]{:S(2)}, u32[]{:S(2)}) collective-permute-start(bf16[96,2048]{1,0:T(8,128)(2,1)S(1)} %get-tuple-element.63), channel_id=1, source_target_pairs={{0,8},{4,12},{8,16},{12,20},{16,24},{20,28},{24,0},{28,4},{1,9},{5... | collective-permute-start | bytes 1179656 | tf_op jit(solution)/shard_map/ppermute | solution.py:541
  36.6 9.2 %collective-permute-start.8 = (bf16[32,2048]{1,0:T(8,128)(2,1)S(1)}, bf16[32,2048]{1,0:T(8,128)(2,1)S(1)}, u32[]{:S(2)}, u32[]{:S(2)}) collective-permute-start(bf16[32,2048]{1,0:T(8,128)(2,1)S(1)} %get-tuple-element.59.mine0), channel_id=1, source_target_pairs={{0,1},{1,0},{2,3},{3,2},{4,5},{5,4},{6,7},{7,6},{8,9},{9,8},{10,11... | collective-permute-start | bytes 393224 | tf_op jit(solution)/shard_map/ppermute | solution.py:629
  39.1 6.7 %collective-permute-start.9 = (bf16[32,2048]{1,0:T(8,128)(2,1)S(1)}, bf16[32,2048]{1,0:T(8,128)(2,1)S(1)}, u32[]{:S(2)}, u32[]{:S(2)}) collective-permute-start(bf16[32,2048]{1,0:T(8,128)(2,1)S(1)} %get-tuple-element.60.mine1), channel_id=1, source_target_pairs={{0,2},{1,3},{2,0},{3,1},{4,6},{5,7},{6,4},{7,5},{8,10},{9,11},{10,... | collective-permute-start | bytes 393224 | tf_op jit(solution)/shard_map/ppermute | solution.py:629
  41.1 11.7 %collective-permute-start.14 = (bf16[128,2048]{1,0:T(8,128)(2,1)S(1)}, bf16[128,2048]{1,0:T(8,128)(2,1)S(1)}, u32[]{:S(2)}, u32[]{:S(2)}) collective-permute-start(bf16[128,2048]{1,0:T(8,128)(2,1)S(1)} %shard_map.220), channel_id=1, source_target_pairs={{0,28},{4,0},{8,4},{12,8},{16,12},{20,16},{24,20},{28,24},{1,29},{... | collective-permute-start | bytes 1572872 | tf_op jit(solution)/shard_map/ppermute | solution.py:541
  45.9 6.8 %collective-permute-start.11 = (bf16[32,2048]{1,0:T(8,128)(2,1)S(1)}, bf16[32,2048]{1,0:T(8,128)(2,1)S(1)}, u32[]{:S(2)}, u32[]{:S(2)}) collective-permute-start(bf16[32,2048]{1,0:T(8,128)(2,1)S(1)} %get-tuple-element.62.mine1), channel_id=1, source_target_pairs={{0,1},{1,0},{2,3},{3,2},{4,5},{5,4},{6,7},{7,6},{8,9},{9,8},{10,11... | collective-permute-start | bytes 393224 | tf_op jit(solution)/shard_map/ppermute | solution.py:629
  46.3 4.5 %copy-start.12 = (bf16[320,160]{1,0:T(8,128)(2,1)S(1)}, bf16[320,160]{1,0:T(8,128)(2,1)}, u32[]{:S(2)}) copy-start(bf16[320,160]{1,0:T(8,128)(2,1)} %constant.27.clone.m_table) | copy-start | bytes 307204
  46.3 4.5 %copy-start.14 = (bf16[256,160]{1,0:T(8,128)(2,1)S(1)}, bf16[256,160]{1,0:T(8,128)(2,1)}, u32[]{:S(2)}) copy-start(bf16[256,160]{1,0:T(8,128)(2,1)} %constant.29.clone.c_table) | copy-start | bytes 245764
  46.3 4.5 %copy-start.17 = (bf16[160,64]{1,0:T(8,128)(2,1)S(1)}, bf16[160,64]{1,0:T(8,128)(2,1)}, u32[]{:S(2)}) copy-start(bf16[160,64]{1,0:T(8,128)(2,1)} %constant.28.clone.q_table) | copy-start | bytes 61444
  46.3 6.4 %collective-permute-start.10 = (bf16[32,2048]{1,0:T(8,128)(2,1)S(1)}, bf16[32,2048]{1,0:T(8,128)(2,1)S(1)}, u32[]{:S(2)}, u32[]{:S(2)}) collective-permute-start(bf16[32,2048]{1,0:T(8,128)(2,1)S(1)} %get-tuple-element.61.refs_6_.mine0), channel_id=1, source_target_pairs={{0,2},{1,3},{2,0},{3,1},{4,6},{5,7},{6,4},{7,5},{8,10},{9,11},{10,... | collective-permute-start | bytes 393224 | tf_op jit(solution)/shard_map/ppermute | solution.py:629
  (1 other events, 0.7 us)
